TPU v7x, 32 devices: a whole 2x2x4 slice. The times are simulated.
32 devices in a mesh: dp: 2 (over y), tm: 4 (over x, core), height: 4 (over z).
Axes of the slice: x: 2, y: 2, z: 4, core: 2. Of those that a mesh axis runs over, the one named last changes fastest.
Arguments:
- low_frames: bfloat16 [2, 16, 16, 32, 256], P('dp', 'tm', 'height'), may hold values from -6 to 6
- spatial_weight: bfloat16 [3, 3, 256, 256], replicated, may hold values from -0.125 to 0.125
- temporal_weight: bfloat16 [3, 256, 256], replicated, may hold values from -0.21875 to 0.21875
- cotangent: bfloat16 [2, 16, 32, 64, 256], P('dp', 'tm', 'height'), may hold values from -6 to 6
Outputs:
- section_out: bfloat16 [2, 16, 32, 64, 256], P('dp', 'tm', 'height')
- input_grad: bfloat16 [2, 16, 16, 32, 256], P('dp', 'tm', 'height')
- spatial_grad: float32 [3, 3, 256, 256], replicated
- temporal_grad: float32 [3, 256, 256], replicated
All inputs are finite; a program needn't handle non-finite values.
Results may differ from a plain program's by a relative error of at most 0.0033.
Values may be sent and summed in bfloat16 or wider, within the bound.
No kernel may reach another device: no remote copies, remote signals or barrier semaphores. Data moves between devices by JAX's collectives and lax.ppermute only.
A program may use at most 64 MiB of HBM per device.

v0:
```python
import functools

import jax
import jax.numpy as jnp
from jax import lax
from jax.experimental import pallas as pl
from jax.experimental.pallas import tpu as pltpu
from jax.sharding import Mesh
from jax.sharding import PartitionSpec as P


class Bits:
    def __init__(self, mesh):
        self.axes = {}
        for name in mesh.axis_names:
            count = mesh.shape[name].bit_length() - 1
            self.axes[name] = tuple(f"{name}{bit}" for bit in reversed(range(count)))
        names = [bit for bits in self.axes.values() for bit in bits]
        self.mesh = Mesh(mesh.devices.reshape([2] * len(names)), tuple(names))
        self.core = next((n for n in names if self.same_chip(n)), self.axes["tm"][-1])
        self.near = []
        for bits in self.axes.values():
            self.near += [b for b in bits if b != self.core][-1:]
        self.far = [n for n in names if n != self.core and n not in self.near]

    def same_chip(self, name):
        at = [1 if n == name else 0 for n in self.mesh.axis_names]
        here = self.mesh.devices[tuple([0] * len(at))]
        there = self.mesh.devices[tuple(at)]
        return tuple(getattr(here, "coords", (0,))) == tuple(getattr(there, "coords", (1,)))

    def swap(self, block, axis):
        return lax.ppermute(block, axis, [(0, 1), (1, 0)])

    def shift(self, block, name, distance):
        axes = self.axes[name]
        devices = range(1 << len(axes))
        route = [(i - distance, i) for i in devices if i - distance in devices]
        return lax.ppermute(block, axes, route)

    def halves(self, mine, other):
        return (mine + self.swap(other, self.core)).astype(jnp.bfloat16)

    def exchange(self, parts):
        return lax.all_to_all(parts, tuple(self.near), 0, 0, tiled=True)

    def gather(self, total, parts):
        for axis in self.far:
            own = total.astype(jnp.bfloat16)
            total = own.astype(jnp.float32) + self.swap(own, axis).astype(jnp.float32)
        total = total.astype(jnp.bfloat16)
        spread = jnp.broadcast_to(total, (parts,) + total.shape)
        half = self.exchange(spread)
        return half, self.swap(half, self.core)


SIDES = ((0, 0), (0, 1), (1, 0), (1, 1))
VMEM = pltpu.CompilerParams(vmem_limit_bytes=56 * 2**20)


def product(left, right):
    return jnp.dot(left, right, preferred_element_type=jnp.float32)


def product_nt(left, right):
    return lax.dot_general(left, right, (((1,), (1,)), ((), ())), preferred_element_type=jnp.float32)


def rows_at_once(rows_low, cols_low):
    return max(n for n in (1, 2, 4, 8) if rows_low % n == 0 and (n == 1 or 4 * n * cols_low <= 256))


def by_side(count, cols_low, dtype=jnp.bfloat16):
    size = 4 * count * cols_low
    to = lax.broadcasted_iota(jnp.int32, (size, size), 0)
    at = lax.broadcasted_iota(jnp.int32, (size, size), 1)
    q, rest = to % cols_low, to // cols_low
    p, side = rest % count, rest // count
    return (at == (p * 2 + side // 2) * 2 * cols_low + 2 * q + side % 2).astype(jnp.float32).astype(dtype)


def from_side(count, cols_low, dtype=jnp.bfloat16):
    size = 4 * count * cols_low
    at = lax.broadcasted_iota(jnp.int32, (size, size), 0)
    to = lax.broadcasted_iota(jnp.int32, (size, size), 1)
    q, rest = to % cols_low, to // cols_low
    p, side = rest % count, rest // count
    return (at == (p * 2 + side // 2) * 2 * cols_low + 2 * q + side % 2).astype(jnp.float32).astype(dtype)


def box(count, cols_low, dtype=jnp.bfloat16):
    size = 4 * count * cols_low
    to = lax.broadcasted_iota(jnp.int32, (size // 4, size), 0)
    at = lax.broadcasted_iota(jnp.int32, (size // 4, size), 1)
    p, q = at // (4 * cols_low), at % (2 * cols_low) // 2
    return (to == p * cols_low + q).astype(jnp.float32).astype(dtype)


def column(rows, cols_low, chan):
    return lax.broadcasted_iota(jnp.int32, (rows, chan), 0) % cols_low


def from_left(x, at):
    return jnp.where(at == 0, 0.0, pltpu.roll(x, 1, 0))


def from_right(x, at, last):
    return jnp.where(at == last, 0.0, pltpu.roll(x, x.shape[0] - 1, 0))


def grads_kernel(core_ref, low_ref, up_ref, down_ref, cot_ref, later_ref, ws_ref, wt_ref,
                 act_ref, pg_ref, mine_ref, other_ref, cot_side, acc):
    frame, frames = pl.program_id(0), pl.num_programs(0)
    _, rows_low, cols_low, chan = low_ref.shape
    count = rows_low * cols_low
    group = rows_at_once(rows_low, cols_low)
    span = group * cols_low
    order = by_side(group, cols_low)

    def sort_frame(source, slot):
        for n in range(rows_low // group):
            block = source[2 * group * n : 2 * group * (n + 1)].reshape(4 * span, chan)
            block = product(order, block).astype(jnp.bfloat16).reshape(4, span, chan)
            cot_side[slot, :, n * span : (n + 1) * span, :] = block

    @pl.when(frame == 0)
    def _():
        for n in range(2):
            sort_frame(cot_ref.at[n], n)

    @pl.when(frame + 2 < frames)
    def _():
        sort_frame(cot_ref.at[jnp.minimum(frame + 2, frames - 1)], frame + 2)

    @pl.when(frame + 2 >= frames)
    def _():
        sort_frame(later_ref.at[jnp.maximum(frame + 2 - frames, 0)], frame + 2)

    low = jnp.concatenate([up_ref[0], low_ref[0], down_ref[0]], axis=0)
    flat = low.reshape(-1, chan)
    rows = [[], []]
    for j in range(3):
        taps = [product(flat, ws_ref[i, j]).reshape(low.shape) for i in range(3)]
        even = taps[0][:rows_low] + (taps[1] + taps[2])[1 : rows_low + 1]
        odd = (taps[0] + taps[1])[1 : rows_low + 1] + taps[2][2:]
        rows[0].append(even.reshape(count, chan))
        rows[1].append(odd.reshape(count, chan))
    at = column(count, cols_low, chan)
    pres = []
    for a in range(2):
        first, second, third = rows[a]
        pres.append(from_left(first, at) + (second + third))
        pres.append((first + second) + from_right(third, at, cols_low - 1))

    acts, pgs = [], []
    for side, pre in enumerate(pres):
        sig = jax.nn.sigmoid(pre)
        acts.append((pre * sig).astype(jnp.bfloat16))
        act_grad = product_nt(cot_side[frame, side], wt_ref[0])
        for k in (1, 2):
            act_grad = act_grad + product_nt(cot_side[frame + k, side], wt_ref[k])
        pgs.append((act_grad * (sig * (1.0 + pre * (1.0 - sig)))).astype(jnp.bfloat16))
        act_ref[0, side] = acts[side]
        pg_ref[0, side] = pgs[side]

    sums = []
    wide = flat.astype(jnp.float32)
    at = column(wide.shape[0], cols_low, chan)
    moved = [from_left(wide, at), wide, from_right(wide, at, cols_low - 1)]
    turned = {}
    for dc in range(3):
        view = moved[dc].astype(jnp.bfloat16).reshape(low.shape)
        for dr in range(3):
            turned[dr - 1, dc - 1] = view[dr : dr + rows_low].reshape(count, chan).T
    pg = jnp.concatenate(pgs, axis=0)
    for i in range(3):
        for j in range(3):
            left = jnp.concatenate([turned[(a + i - 1) // 2, (b + j - 1) // 2] for a, b in SIDES], axis=1)
            sums.append(product(left, pg))
    act = jnp.concatenate(acts, axis=0).T
    for k in range(3):
        sums.append(product(act, cot_side[frame + k].reshape(4 * count, chan)))

    @pl.when(frame == 0)
    def _():
        for tap, value in enumerate(sums):
            acc[tap] = value

    @pl.when(frame > 0)
    def _():
        for tap, value in enumerate(sums):
            acc[tap] += value

    @pl.when(frame == frames - 1)
    def _():
        parts = mine_ref.shape[0]
        half = chan // 2
        size = half // parts
        core = core_ref[0]
        for out, start in ((mine_ref, core * half), (other_ref, half - core * half)):
            for n in range(parts):
                for tap in range(12):
                    begin = pl.multiple_of(start + n * size, size)
                    out[n, tap * size : (tap + 1) * size, :] = acc[tap, pl.ds(begin, size), :]


def whole(shape):
    return pl.BlockSpec(shape, lambda f: (0,) * len(shape))


def each(shape):
    return pl.BlockSpec((1,) + tuple(shape[1:]), lambda f: (f,) + (0,) * (len(shape) - 1))


SCALAR = pl.BlockSpec(memory_space=pltpu.SMEM)
UNREAD = pl.BlockSpec(memory_space=pl.ANY)


def weight_grads(core, parts, low, up, down, cot, later, ws, wt):
    frames, rows_low, cols_low, chan = low.shape
    count = rows_low * cols_low
    side = (frames, 4, count, chan)
    piece = (parts, 12 * (chan // (2 * parts)), chan)
    flops = 2 * 2048 * chan * chan * 20
    return pl.pallas_call(
        grads_kernel,
        grid=(frames,),
        in_specs=[SCALAR, each(low.shape), each(up.shape), each(down.shape),
                  whole(cot.shape), whole(later.shape), whole(ws.shape), whole(wt.shape)],
        out_specs=[each(side), each(side), whole(piece), whole(piece)],
        out_shape=[jax.ShapeDtypeStruct(side, jnp.bfloat16)] * 2
        + [jax.ShapeDtypeStruct(piece, jnp.float32)] * 2,
        scratch_shapes=[pltpu.VMEM((frames + 2, 4, count, chan), jnp.bfloat16),
                        pltpu.VMEM((12, chan, chan), jnp.float32)],
        compiler_params=VMEM,
        cost_estimate=pl.CostEstimate(flops=flops, bytes_accessed=8 * 2**20, transcendentals=frames * 4 * count * chan),
        name="weight_grads",
    )(core, low, up, down, cot, later, ws, wt)


def section_kernel(act_ref, low_ref, wt_ref, _, out_ref):
    frame = pl.program_id(0)
    _, rows_low, cols_low, chan = low_ref.shape
    group = rows_at_once(rows_low, cols_low)
    span = group * cols_low
    order = from_side(group, cols_low)
    low = low_ref[0].reshape(-1, chan).astype(jnp.float32)
    mixed = []
    for side in range(4):
        total = low
        for k in range(3):
            total = total + product(act_ref[frame + 2 - k, side], wt_ref[k])
        mixed.append(total.astype(jnp.bfloat16))
    for n in range(rows_low // group):
        block = jnp.concatenate([m[n * span : (n + 1) * span] for m in mixed], axis=0)
        block = product(order, block).astype(jnp.bfloat16)
        out_ref[0, 2 * group * n : 2 * group * (n + 1)] = block.reshape(2 * group, 2 * cols_low, chan)


def section(act_ext, low, wt, before):
    frames, rows_low, cols_low, chan = low.shape
    out = (frames, 2 * rows_low, 2 * cols_low, chan)
    return pl.pallas_call(
        section_kernel,
        grid=(frames,),
        in_specs=[whole(act_ext.shape), each(low.shape), whole(wt.shape), UNREAD],
        out_specs=each(out),
        out_shape=jax.ShapeDtypeStruct(out, jnp.bfloat16),
        compiler_params=VMEM,
        cost_estimate=pl.CostEstimate(flops=2 * 2048 * chan * chan * 4, bytes_accessed=3 * 2**20, transcendentals=0),
        name="section",
    )(act_ext, low, wt, before)


def input_kernel(pg_ref, up_ref, down_ref, cot_ref, ws_ref, _, out_ref):
    _, rows_low, cols_low, chan = out_ref.shape
    group = rows_at_once(rows_low, cols_low)
    span = group * cols_low
    place = box(group, cols_low)
    count = rows_low * cols_low
    total = jnp.concatenate(
        [product(place, cot_ref[0, 2 * group * n : 2 * group * (n + 1)].reshape(4 * span, chan))
         for n in range(rows_low // group)], axis=0)
    tall = (rows_low + 1, cols_low, chan)
    at = column(tall[0] * cols_low, cols_low, chan)
    own = [pg_ref[0, side].astype(jnp.float32) for side in range(4)]
    above = [up_ref[0, b].astype(jnp.float32) for b in range(2)]
    below = [down_ref[0, b].astype(jnp.float32) for b in range(2)]
    even = [jnp.concatenate([own[b], below[b]], axis=0) for b in range(2)]
    odd = [jnp.concatenate([above[b], own[2 + b]], axis=0) for b in range(2)]
    for j in range(3):
        pair = []
        for first, second in (even, odd):
            if j == 0:
                value = second + from_right(first, at, cols_low - 1)
            elif j == 1:
                value = first + second
            else:
                value = first + from_left(second, at)
            pair.append(value.reshape(tall))
        top, low = pair
        for i, value in enumerate((low[1:] + top[1:], top[:-1] + low[1:], low[:-1] + top[:-1])):
            value = value.reshape(count, chan)
            high = value.astype(jnp.bfloat16)
            rest = (value - high.astype(jnp.float32)).astype(jnp.bfloat16)
            total = total + product_nt(high, ws_ref[i, j]) + product_nt(rest, ws_ref[i, j])
    out_ref[0] = total.astype(jnp.bfloat16).reshape(rows_low, cols_low, chan)


def input_grads(pg, up, down, cot, ws, before, low_shape):
    chan = low_shape[-1]
    return pl.pallas_call(
        input_kernel,
        grid=(low_shape[0],),
        in_specs=[each(pg.shape), each(up.shape), each(down.shape), each(cot.shape), whole(ws.shape), UNREAD],
        out_specs=each(low_shape),
        out_shape=jax.ShapeDtypeStruct(low_shape, jnp.bfloat16),
        compiler_params=VMEM,
        cost_estimate=pl.CostEstimate(flops=2 * 2048 * chan * chan * 6, bytes_accessed=4 * 2**20, transcendentals=0),
        name="input_grads",
    )(pg, up, down, cot, ws, before)


def place_kernel(core_ref, half_ref, theirs_ref, spatial_ref, temporal_ref):
    parts, rows, chan = half_ref.shape
    size = rows // 12
    half = chan // 2
    core = core_ref[0]
    for source, start in ((half_ref, core * half), (theirs_ref, half - core * half)):
        for n in range(parts):
            begin = pl.multiple_of(start + n * size, size)
            for tap in range(12):
                value = source[n, tap * size : (tap + 1) * size, :].astype(jnp.float32)
                if tap < 9:
                    spatial_ref[tap // 3, tap % 3, pl.ds(begin, size), :] = value
                else:
                    temporal_ref[tap - 9, pl.ds(begin, size), :] = value


def place(core, half, theirs, chan):
    full = pl.BlockSpec(memory_space=pltpu.VMEM)
    return pl.pallas_call(
        place_kernel,
        in_specs=[SCALAR, full, full],
        out_specs=[full, full],
        out_shape=[jax.ShapeDtypeStruct((3, 3, chan, chan), jnp.float32),
                   jax.ShapeDtypeStruct((3, chan, chan), jnp.float32)],
        compiler_params=VMEM,
        name="place",
    )(core, half, theirs)


def sum_kernel(got_ref, *refs):
    total = got_ref[0].astype(jnp.float32)
    for n in range(1, got_ref.shape[0]):
        total = total + got_ref[n].astype(jnp.float32)
    refs[-1][...] = total


def sum_parts(got, *before):
    full = pl.BlockSpec(memory_space=pltpu.VMEM)
    return pl.pallas_call(
        sum_kernel,
        in_specs=[full] + [UNREAD] * len(before),
        out_specs=full,
        out_shape=jax.ShapeDtypeStruct(got.shape[1:], jnp.float32),
        compiler_params=VMEM,
        name="sum_parts",
    )(got, *before)


def on_device(bits, low_frames, spatial_weight, temporal_weight, cotangent):
    low, cot = low_frames[0], cotangent[0]
    frames, rows_low, cols_low, chan = low.shape
    core = lax.axis_index(bits.core).astype(jnp.int32).reshape(1)
    up = bits.shift(low[:, -1:], "height", 1)
    down = bits.shift(low[:, :1], "height", -1)
    later = bits.shift(cot[:2], "tm", -1)
    act, pg, mine, other = weight_grads(
        core, 1 << len(bits.near), low, up, down, cot, later, spatial_weight, temporal_weight
    )
    kept = bits.halves(mine, other)
    got = bits.exchange(kept)
    earlier = bits.shift(act[frames - 2 :], "tm", 1)
    section_out = section(jnp.concatenate([earlier, act], axis=0), low, temporal_weight, kept)
    above = bits.shift(pg[:, 2:, -cols_low:], "height", 1)
    below = bits.shift(pg[:, :2, :cols_low], "height", -1)
    input_grad = input_grads(pg, above, below, cot, spatial_weight, kept, low.shape)
    total = sum_parts(got, section_out, input_grad)
    half, theirs = bits.gather(total, got.shape[0])
    spatial_grad, temporal_grad = place(core, half, theirs, chan)
    return section_out[None], input_grad[None], spatial_grad, temporal_grad


def solution(mesh):
    bits = Bits(mesh)
    block = P(*(bits.axes[name] for name in ("dp", "tm", "height")), None, None)
    return jax.shard_map(
        functools.partial(on_device, bits),
        mesh=bits.mesh,
        in_specs=(block, P(), P(), block),
        out_specs=(block, block, P(), P()),
        check_vma=False,
    )
```

profile of v0, /device:TPU:0, one launch (start us, length us, event | category | flops | bytes accessed | tf_op | source)
XLA Modules:
  0.0 101.9 jit_solution(16035434204912998601)
XLA Ops:
  0.6 1.1 %slice_bitcast_fusion = bf16[2,8,64,256]{3,2,1,0:T(8,128)(2,1)S(1)} fusion(bf16[1,4,8,64,256]{4,3,2,1,0:T(8,128)(2,1)} %param.7), kind=kLoop, calls=%fused_computation.2 | loop fusion | bytes 1048576 | tf_op jit(solution)/shard_map/slice | solution.py:378
  1.7 1.3 %collective-permute-start.2 = (bf16[2,8,64,256]{3,2,1,0:T(8,128)(2,1)S(1)}, bf16[2,8,64,256]{3,2,1,0:T(8,128)(2,1)S(1)}, u32[]{:S(2)}, u32[]{:S(2)}) collective-permute-start(bf16[2,8,64,256]{3,2,1,0:T(8,128)(2,1)S(1)} %slice_bitcast_fusion), channel_id=1, source_target_pairs={{4,0},{8,4},{12,8},{5,1},{9,5},{13,9},{6,2},{10,6},{14,10},{7,3},{... | collective-permute-start | bytes 1572872 | tf_op jit(solution)/shard_map/ppermute | solution.py:39
  3.0 0.9 fusion.1
  3.9 4.9 %collective-permute-start = (bf16[4,1,32,256]{3,2,1,0:T(8,128)(2,1)S(1)}, bf16[4,1,32,256]{3,2,1,0:T(8,128)(2,1)S(1)}, u32[]{:S(2)}, u32[]{:S(2)}) collective-permute-start(bf16[4,1,32,256]{3,2,1,0:T(8,128)(2,1)S(1)} %get-tuple-element.19), channel_id=1, source_target_pairs={{0,1},{1,2},{2,3},{4,5},{5,6},{6,7},{8,9},{9,10},{10,11},{12,13},{... | collective-permute-start | bytes 196616 | tf_op jit(solution)/shard_map/ppermute | solution.py:39
  8.8 1.3 %collective-permute-start.1 = (bf16[4,1,32,256]{3,2,1,0:T(8,128)(2,1)S(1)}, bf16[4,1,32,256]{3,2,1,0:T(8,128)(2,1)S(1)}, u32[]{:S(2)}, u32[]{:S(2)}) collective-permute-start(bf16[4,1,32,256]{3,2,1,0:T(8,128)(2,1)S(1)} %get-tuple-element.18), channel_id=1, source_target_pairs={{1,0},{2,1},{3,2},{5,4},{6,5},{7,6},{9,8},{10,9},{11,10},{13,12},{... | collective-permute-start | bytes 196616 | tf_op jit(solution)/shard_map/ppermute | solution.py:39
  10.1 1.0 collective-permute-done.up_ref
  11.1 0.0 copy-start.7
  11.2 4.4 %collective-permute-done.1.down_ref = bf16[4,1,32,256]{3,2,1,0:T(8,128)(2,1)S(1)} collective-permute-done((bf16[4,1,32,256]{3,2,1,0:T(8,128)(2,1)S(1)}, bf16[4,1,32,256]{3,2,1,0:T(8,128)(2,1)S(1)}, u32[]{:S(2)}, u32[]{:S(2)}) %collective-permute-start.1) | collective-permute-done | bytes 65568 | tf_op jit(solution)/shard_map/ppermute | solution.py:39
  15.6 0.0 copy-start.8
  15.6 0.0 collective-permute-done.2.later_ref
  15.6 0.0 copy-start.4
  15.6 0.0 copy-done.7
  15.6 0.6 copy-done.8
  16.2 0.2 copy-done.4
  16.4 13.8 %weight_grads.1 = (bf16[4,4,128,256]{3,2,1,0:T(8,128)(2,1)}, bf16[4,4,128,256]{3,2,1,0:T(8,128)(2,1)}, f32[8,192,256]{2,1,0:T(8,128)}, f32[8,192,256]{2,1,0:T(8,128)}) custom-call(s32[1]{0:T(128)} %bitcast.core_ref, bf16[4,4,32,256]{3,2,1,0:T(8,128)(2,1)} %bitcast.9, bf16[4,1,32,256]{3,2,1,0:T(8,128)(2,1)} %copy-done.7, bf16[4,1,32,256]{3,2,1,0:T(8,128)(2,1)} %copy-done.8, ...), custom_call_target="tpu_custom_call" | custom-call | flops 5368709120 | bytes 8388608 | tf_op jit(solution)/shard_map/weight_grads/pallas_call | solution.py:225
  30.2 0.1 collective-permute-start.4
  30.3 3.6 %collective-permute-done.4 = f32[8,192,256]{2,1,0:T(8,128)S(1)} collective-permute-done((f32[8,192,256]{2,1,0:T(8,128)}, f32[8,192,256]{2,1,0:T(8,128)S(1)}, u32[]{:S(2)}, u32[]{:S(2)}) %collective-permute-start.4) | collective-permute-done | bytes 1572896 | tf_op jit(solution)/shard_map/ppermute | solution.py:33
  33.9 2.5 %add_convert_fusion._ = bf16[8,192,256]{2,1,0:T(8,128)(2,1)} fusion(f32[8,192,256]{2,1,0:T(8,128)} %get-tuple-element.11, f32[8,192,256]{2,1,0:T(8,128)S(1)} %collective-permute-done.4), kind=kLoop, calls=%fused_computation.1 | loop fusion | flops 786432 | bytes 3932160 | tf_op jit(solution)/shard_map/convert_element_type | solution.py:42
  36.4 0.0 copy-start.2
  36.4 4.9 %all-to-all-start = ((bf16[8,192,256]{2,1,0:T(8,128)(2,1)}), bf16[8,192,256]{2,1,0:T(8,128)(2,1)S(1)}, u32[]{:S(2)}, u32[]{:S(2)}) async-start(bf16[8,192,256]{2,1,0:T(8,128)(2,1)} %add_convert_fusion._), calls=%async_computation | async-start | bytes 1572864 | tf_op jit(solution)/shard_map/all_to_all | solution.py:45
  41.3 0.0 copy-done.2
  41.4 1.8 %collective-permute-start.3 = (bf16[2,4,128,256]{3,2,1,0:T(8,128)(2,1)S(1)}, bf16[2,4,128,256]{3,2,1,0:T(8,128)(2,1)S(1)}, u32[]{:S(2)}, u32[]{:S(2)}) collective-permute-start(bf16[2,4,128,256]{3,2,1,0:T(8,128)(2,1)S(1)} %slice.25), channel_id=1, source_target_pairs={{0,4},{4,8},{8,12},{1,5},{5,9},{9,13},{2,6},{6,10},{10,14},{3,7},{... | collective-permute-start | bytes 1572872 | tf_op jit(solution)/shard_map/ppermute | solution.py:39
  43.2 1.0 fusion
  44.2 3.6 %collective-permute-start.5 = (bf16[4,2,32,256]{3,2,1,0:T(8,128)(2,1)S(1)}, bf16[4,2,32,256]{3,2,1,0:T(8,128)(2,1)S(1)}, u32[]{:S(2)}, u32[]{:S(2)}) collective-permute-start(bf16[4,2,32,256]{3,2,1,0:T(8,128)(2,1)S(1)} %get-tuple-element.17), channel_id=1, source_target_pairs={{0,1},{1,2},{2,3},{4,5},{5,6},{6,7},{8,9},{9,10},{10,11},{12,13},{... | collective-permute-start | bytes 393224 | tf_op jit(solution)/shard_map/ppermute | solution.py:39
  47.8 1.3 %collective-permute-start.6 = (bf16[4,2,32,256]{3,2,1,0:T(8,128)(2,1)S(1)}, bf16[4,2,32,256]{3,2,1,0:T(8,128)(2,1)S(1)}, u32[]{:S(2)}, u32[]{:S(2)}) collective-permute-start(bf16[4,2,32,256]{3,2,1,0:T(8,128)(2,1)S(1)} %get-tuple-element.16), channel_id=1, source_target_pairs={{1,0},{2,1},{3,2},{5,4},{6,5},{7,6},{9,8},{10,9},{11,10},{13,12},{... | collective-permute-start | bytes 393224 | tf_op jit(solution)/shard_map/ppermute | solution.py:39
  49.1 0.0 collective-permute-done.3
  49.1 1.3 %pad_maximum_fusion.act_ref = bf16[6,4,128,256]{3,2,1,0:T(8,128)(2,1)} fusion(bf16[4,4,128,256]{3,2,1,0:T(8,128)(2,1)S(1)} %copy-done.2, bf16[2,4,128,256]{3,2,1,0:T(8,128)(2,1)S(1)} %collective-permute-done.3), kind=kLoop, calls=%fused_computation | loop fusion | flops 786432 | bytes 3145728 | tf_op jit(solution)/shard_map/concatenate | solution.py:385
  50.4 4.9 %section.1.refs_0_ = bf16[4,8,64,256]{3,2,1,0:T(8,128)(2,1)} custom-call(bf16[6,4,128,256]{3,2,1,0:T(8,128)(2,1)} %pad_maximum_fusion.act_ref, bf16[4,4,32,256]{3,2,1,0:T(8,128)(2,1)} %bitcast.10, bf16[3,256,256]{2,1,0:T(8,128)(2,1)} %wt_ref.3, bf16[8,192,256]{2,1,0:T(8,128)(2,1)} %add_convert_fusion._), custom_call_target="tpu_custom_call" | custom-call | flops 1073741824 | bytes 3145728 | tf_op jit(solution)/shard_map/section/pallas_call | solution.py:263
  55.4 0.0 collective-permute-done.5.up_ref
  55.4 0.0 copy-start.5
  55.4 0.0 collective-permute-done.6.down_ref
  55.4 0.6 copy-done.5
  56.0 0.6 copy-done.6
  56.7 6.2 %input_grads.1.refs_1_ = bf16[4,4,32,256]{3,2,1,0:T(8,128)(2,1)} custom-call(bf16[4,4,128,256]{3,2,1,0:T(8,128)(2,1)} %get-tuple-element.13.pg_ref, bf16[4,2,32,256]{3,2,1,0:T(8,128)(2,1)} %copy-done.5, bf16[4,2,32,256]{3,2,1,0:T(8,128)(2,1)} %copy-done.6, bf16[4,8,64,256]{3,2,1,0:T(8,128)(2,1)} %bitcast.13, bf16[3,3,256,256]{3,2,1,0:T(8,128)(2,1)} %ws_ref.3, ...), custom_call_target="tpu_custom_call" | custom-call | flops 1610612736 | bytes 4194304 | tf_op jit(solution)/shard_map/input_grads/pallas_call | solution.py:312
  62.8 0.0 all-to-all-done.got_ref
  62.9 0.9 copy-done
  63.7 1.9 %sum_parts.1 = f32[192,256]{1,0:T(8,128)} custom-call(bf16[8,192,256]{2,1,0:T(8,128)(2,1)} %copy-done, bf16[4,8,64,256]{3,2,1,0:T(8,128)(2,1)} %section.1.refs_0_, bf16[4,4,32,256]{3,2,1,0:T(8,128)(2,1)} %input_grads.1.refs_1_), custom_call_target="tpu_custom_call" | custom-call | tf_op jit(solution)/shard_map/sum_parts/pallas_call | solution.py:362
  65.6 0.9 convert_element_type.16
  66.6 2.6 %collective-permute-start.7 = (bf16[192,256]{1,0:T(8,128)(2,1)S(1)}, bf16[192,256]{1,0:T(8,128)(2,1)S(1)}, u32[]{:S(2)}, u32[]{:S(2)}) collective-permute-start(bf16[192,256]{1,0:T(8,128)(2,1)S(1)} %convert_element_type.16), channel_id=1, source_target_pairs={{0,2},{2,0},{1,3},{3,1},{4,6},{6,4},{5,7},{7,5},{8,10},{10,8},{9,1... | collective-permute-start | bytes 294920 | tf_op jit(solution)/shard_map/ppermute | solution.py:33
  69.2 3.0 %collective-permute-done.7 = bf16[192,256]{1,0:T(8,128)(2,1)S(1)} collective-permute-done((bf16[192,256]{1,0:T(8,128)(2,1)S(1)}, bf16[192,256]{1,0:T(8,128)(2,1)S(1)}, u32[]{:S(2)}, u32[]{:S(2)}) %collective-permute-start.7) | collective-permute-done | bytes 98336 | tf_op jit(solution)/shard_map/ppermute | solution.py:33
  72.2 1.0 add_convert_fusion.1
  73.1 0.1 broadcast_in_dim.11
  73.2 22.3 %all_to_all.10.half_ref = bf16[8,192,256]{2,1,0:T(8,128)(2,1)S(1)} all-to-all(bf16[8,192,256]{2,1,0:T(8,128)(2,1)S(1)} %broadcast_in_dim.11), channel_id=1, replica_groups=mesh['dp0'=2,'tm1'=2,'tm0'=2,'height1'=2,'height0'=2] {'dp0','tm1','heig..., dimensions={0} | all-to-all | bytes 1572864 | tf_op jit(solution)/shard_map/all_to_all | solution.py:45
  95.4 0.0 collective-permute-start.8
  95.4 2.3 %collective-permute-done.8.theirs_ref = bf16[8,192,256]{2,1,0:T(8,128)(2,1)S(1)} collective-permute-done((bf16[8,192,256]{2,1,0:T(8,128)(2,1)S(1)}, bf16[8,192,256]{2,1,0:T(8,128)(2,1)S(1)}, u32[]{:S(2)}, u32[]{:S(2)}) %collective-permute-start.8) | collective-permute-done | bytes 786464 | tf_op jit(solution)/shard_map/ppermute | solution.py:33
  97.7 0.0 copy-done.1
  97.7 0.9 copy-done.3
  98.7 3.2 %place.1 = (f32[3,3,256,256]{3,2,1,0:T(8,128)}, f32[3,256,256]{2,1,0:T(8,128)}) custom-call(s32[1]{0:T(128)} %bitcast.core_ref, bf16[8,192,256]{2,1,0:T(8,128)(2,1)} %copy-done.1, bf16[8,192,256]{2,1,0:T(8,128)(2,1)} %copy-done.3), custom_call_target="tpu_custom_call" | custom-call | tf_op jit(solution)/shard_map/place/pallas_call | solution.py:342
  (5 shorter events, 0.0 us)
Async XLA Ops:
  1.7 13.9 %collective-permute-start.2 = (bf16[2,8,64,256]{3,2,1,0:T(8,128)(2,1)S(1)}, bf16[2,8,64,256]{3,2,1,0:T(8,128)(2,1)S(1)}, u32[]{:S(2)}, u32[]{:S(2)}) collective-permute-start(bf16[2,8,64,256]{3,2,1,0:T(8,128)(2,1)S(1)} %slice_bitcast_fusion), channel_id=1, source_target_pairs={{4,0},{8,4},{12,8},{5,1},{9,5},{13,9},{6,2},{10,6},{14,10},{7,3},{... | collective-permute-start | bytes 1572872 | tf_op jit(solution)/shard_map/ppermute | solution.py:39
  3.9 7.2 %collective-permute-start = (bf16[4,1,32,256]{3,2,1,0:T(8,128)(2,1)S(1)}, bf16[4,1,32,256]{3,2,1,0:T(8,128)(2,1)S(1)}, u32[]{:S(2)}, u32[]{:S(2)}) collective-permute-start(bf16[4,1,32,256]{3,2,1,0:T(8,128)(2,1)S(1)} %get-tuple-element.19), channel_id=1, source_target_pairs={{0,1},{1,2},{2,3},{4,5},{5,6},{6,7},{8,9},{9,10},{10,11},{12,13},{... | collective-permute-start | bytes 196616 | tf_op jit(solution)/shard_map/ppermute | solution.py:39
  8.8 6.7 %collective-permute-start.1 = (bf16[4,1,32,256]{3,2,1,0:T(8,128)(2,1)S(1)}, bf16[4,1,32,256]{3,2,1,0:T(8,128)(2,1)S(1)}, u32[]{:S(2)}, u32[]{:S(2)}) collective-permute-start(bf16[4,1,32,256]{3,2,1,0:T(8,128)(2,1)S(1)} %get-tuple-element.18), channel_id=1, source_target_pairs={{1,0},{2,1},{3,2},{5,4},{6,5},{7,6},{9,8},{10,9},{11,10},{13,12},{... | collective-permute-start | bytes 196616 | tf_op jit(solution)/shard_map/ppermute | solution.py:39
  11.1 4.4 %copy-start.7 = (bf16[4,1,32,256]{3,2,1,0:T(8,128)(2,1)}, bf16[4,1,32,256]{3,2,1,0:T(8,128)(2,1)S(1)}, u32[]{:S(2)}) copy-start(bf16[4,1,32,256]{3,2,1,0:T(8,128)(2,1)S(1)} %collective-permute-done.up_ref) | copy-start | bytes 196612
  15.6 0.6 copy-start.8
  15.6 0.8 copy-start.4
  30.2 3.7 %collective-permute-start.4 = (f32[8,192,256]{2,1,0:T(8,128)}, f32[8,192,256]{2,1,0:T(8,128)S(1)}, u32[]{:S(2)}, u32[]{:S(2)}) collective-permute-start(f32[8,192,256]{2,1,0:T(8,128)} %get-tuple-element.12), channel_id=1, source_target_pairs={{0,4},{4,0},{1,5},{5,1},{2,6},{6,2},{3,7},{7,3},{8,12},{12,8},{9,1... | collective-permute-start | bytes 4718600 | tf_op jit(solution)/shard_map/ppermute | solution.py:33
  36.4 4.9 %copy-start.2 = (bf16[4,4,128,256]{3,2,1,0:T(8,128)(2,1)S(1)}, bf16[4,4,128,256]{3,2,1,0:T(8,128)(2,1)}, u32[]{:S(2)}) copy-start(bf16[4,4,128,256]{3,2,1,0:T(8,128)(2,1)} %get-tuple-element.10) | copy-start | bytes 3145732
  36.4 26.4 %all-to-all-start = ((bf16[8,192,256]{2,1,0:T(8,128)(2,1)}), bf16[8,192,256]{2,1,0:T(8,128)(2,1)S(1)}, u32[]{:S(2)}, u32[]{:S(2)}) async-start(bf16[8,192,256]{2,1,0:T(8,128)(2,1)} %add_convert_fusion._), calls=%async_computation | async-start | bytes 1572864 | tf_op jit(solution)/shard_map/all_to_all | solution.py:45
  41.4 7.8 %collective-permute-start.3 = (bf16[2,4,128,256]{3,2,1,0:T(8,128)(2,1)S(1)}, bf16[2,4,128,256]{3,2,1,0:T(8,128)(2,1)S(1)}, u32[]{:S(2)}, u32[]{:S(2)}) collective-permute-start(bf16[2,4,128,256]{3,2,1,0:T(8,128)(2,1)S(1)} %slice.25), channel_id=1, source_target_pairs={{0,4},{4,8},{8,12},{1,5},{5,9},{9,13},{2,6},{6,10},{10,14},{3,7},{... | collective-permute-start | bytes 1572872 | tf_op jit(solution)/shard_map/ppermute | solution.py:39
  44.2 11.2 %collective-permute-start.5 = (bf16[4,2,32,256]{3,2,1,0:T(8,128)(2,1)S(1)}, bf16[4,2,32,256]{3,2,1,0:T(8,128)(2,1)S(1)}, u32[]{:S(2)}, u32[]{:S(2)}) collective-permute-start(bf16[4,2,32,256]{3,2,1,0:T(8,128)(2,1)S(1)} %get-tuple-element.17), channel_id=1, source_target_pairs={{0,1},{1,2},{2,3},{4,5},{5,6},{6,7},{8,9},{9,10},{10,11},{12,13},{... | collective-permute-start | bytes 393224 | tf_op jit(solution)/shard_map/ppermute | solution.py:39
  47.8 7.6 %collective-permute-start.6 = (bf16[4,2,32,256]{3,2,1,0:T(8,128)(2,1)S(1)}, bf16[4,2,32,256]{3,2,1,0:T(8,128)(2,1)S(1)}, u32[]{:S(2)}, u32[]{:S(2)}) collective-permute-start(bf16[4,2,32,256]{3,2,1,0:T(8,128)(2,1)S(1)} %get-tuple-element.16), channel_id=1, source_target_pairs={{1,0},{2,1},{3,2},{5,4},{6,5},{7,6},{9,8},{10,9},{11,10},{13,12},{... | collective-permute-start | bytes 393224 | tf_op jit(solution)/shard_map/ppermute | solution.py:39
  55.4 0.7 copy-start.5
  56.0 0.7 copy-start.6
  62.9 0.9 copy-start
  66.6 5.6 %collective-permute-start.7 = (bf16[192,256]{1,0:T(8,128)(2,1)S(1)}, bf16[192,256]{1,0:T(8,128)(2,1)S(1)}, u32[]{:S(2)}, u32[]{:S(2)}) collective-permute-start(bf16[192,256]{1,0:T(8,128)(2,1)S(1)} %convert_element_type.16), channel_id=1, source_target_pairs={{0,2},{2,0},{1,3},{3,1},{4,6},{6,4},{5,7},{7,5},{8,10},{10,8},{9,1... | collective-permute-start | bytes 294920 | tf_op jit(solution)/shard_map/ppermute | solution.py:33
  95.4 2.3 %copy-start.1 = (bf16[8,192,256]{2,1,0:T(8,128)(2,1)}, bf16[8,192,256]{2,1,0:T(8,128)(2,1)S(1)}, u32[]{:S(2)}) copy-start(bf16[8,192,256]{2,1,0:T(8,128)(2,1)S(1)} %all_to_all.10.half_ref) | copy-start | bytes 2359300
  95.4 2.3 %collective-permute-start.8 = (bf16[8,192,256]{2,1,0:T(8,128)(2,1)S(1)}, bf16[8,192,256]{2,1,0:T(8,128)(2,1)S(1)}, u32[]{:S(2)}, u32[]{:S(2)}) collective-permute-start(bf16[8,192,256]{2,1,0:T(8,128)(2,1)S(1)} %all_to_all.10.half_ref), channel_id=1, source_target_pairs={{0,4},{4,0},{1,5},{5,1},{2,6},{6,2},{3,7},{7,3},{8,12},{12,8},{9,1... | collective-permute-start | bytes 2359304 | tf_op jit(solution)/shard_map/ppermute | solution.py:33
  97.7 0.9 copy-start.3
where the time goes:
time: 103 us; the launch traced here: 102 us
  Pallas kernels  30.1 us (29%)
  blocking collectives  22.3 us (22%)
  starting transfers between devices  21.9 us (21%)
  waiting for transfers between devices  14.3 us (14%)
  local copies, waits for them, and re-layouts  6.92 us (7%)
  other arithmetic  5.69 us (6%)
    all_to_all x1, blocking collectives, exchange(): return lax.all_to_all(parts, tuple(self.near), 0, 0, tiled=True)  22.3 us
    ppermute x6, starting transfers between devices, shift(): return lax.ppermute(block, axes, route)  14.2 us
    pallas_call x1, Pallas kernels, weight_grads(): pl.pallas_call(grads_kernel, grid=(frames,), in_specs=[SCALAR, each(low.s...  13.8 us
    ppermute x3, waiting for transfers between devices, swap(): return lax.ppermute(block, axis, [(0, 1), (1, 0)])  8.86 us
    pallas_call x1, Pallas kernels, input_grads(): pl.pallas_call(input_kernel, grid=(low_shape[0],), in_specs=[each(pg.shap...  6.18 us
    ppermute x6, waiting for transfers between devices, shift(): return lax.ppermute(block, axes, route)  5.49 us
    pallas_call x1, Pallas kernels, section(): pl.pallas_call(section_kernel, grid=(frames,), in_specs=[whole(act_ext.sh...  4.93 us
    all_to_all x1, starting transfers between devices, exchange(): return lax.all_to_all(parts, tuple(self.near), 0, 0, tiled=True)  4.92 us
  transfers between devices with their start and end apart: 10, of which 5 were waited for; matrix products, arithmetic and copies ran while one was open for 3% of the time, Pallas kernels for 11%

commit v1 on v0

--- a/solution.py
+++ b/solution.py
@@ -38,24 +38,22 @@
         route = [(i - distance, i) for i in devices if i - distance in devices]
         return lax.ppermute(block, axes, route)
 
-    def halves(self, mine, other):
-        return (mine + self.swap(other, self.core)).astype(jnp.bfloat16)
-
     def exchange(self, parts):
         return lax.all_to_all(parts, tuple(self.near), 0, 0, tiled=True)
 
     def gather(self, total, parts):
         for axis in self.far:
-            own = total.astype(jnp.bfloat16)
-            total = own.astype(jnp.float32) + self.swap(own, axis).astype(jnp.float32)
-        total = total.astype(jnp.bfloat16)
+            total = (total.astype(jnp.float32) + self.swap(total, axis).astype(jnp.float32)).astype(jnp.bfloat16)
         spread = jnp.broadcast_to(total, (parts,) + total.shape)
         half = self.exchange(spread)
         return half, self.swap(half, self.core)
 
 
 SIDES = ((0, 0), (0, 1), (1, 0), (1, 1))
-VMEM = pltpu.CompilerParams(vmem_limit_bytes=56 * 2**20)
+
+
+def grant(mib):
+    return pltpu.CompilerParams(vmem_limit_bytes=mib * 2**20)
 
 
 def product(left, right):
@@ -108,34 +106,20 @@
     return jnp.where(at == last, 0.0, pltpu.roll(x, x.shape[0] - 1, 0))
 
 
-def grads_kernel(core_ref, low_ref, up_ref, down_ref, cot_ref, later_ref, ws_ref, wt_ref,
-                 act_ref, pg_ref, mine_ref, other_ref, cot_side, acc):
-    frame, frames = pl.program_id(0), pl.num_programs(0)
-    _, rows_low, cols_low, chan = low_ref.shape
-    count = rows_low * cols_low
+def sort_columns(source, target, cols_low):
+    rows_low, chan = source.shape[0] // 2, source.shape[2]
     group = rows_at_once(rows_low, cols_low)
     span = group * cols_low
     order = by_side(group, cols_low)
-
-    def sort_frame(source, slot):
-        for n in range(rows_low // group):
-            block = source[2 * group * n : 2 * group * (n + 1)].reshape(4 * span, chan)
-            block = product(order, block).astype(jnp.bfloat16).reshape(4, span, chan)
-            cot_side[slot, :, n * span : (n + 1) * span, :] = block
-
-    @pl.when(frame == 0)
-    def _():
-        for n in range(2):
-            sort_frame(cot_ref.at[n], n)
-
-    @pl.when(frame + 2 < frames)
-    def _():
-        sort_frame(cot_ref.at[jnp.minimum(frame + 2, frames - 1)], frame + 2)
-
-    @pl.when(frame + 2 >= frames)
-    def _():
-        sort_frame(later_ref.at[jnp.maximum(frame + 2 - frames, 0)], frame + 2)
-
+    for n in range(rows_low // group):
+        block = source[2 * group * n : 2 * group * (n + 1)].reshape(4 * span, chan)
+        block = product(order, block).astype(jnp.bfloat16).reshape(4, span, chan)
+        target[:, n * span : (n + 1) * span, :] = block
+
+
+def forward_kernel(low_ref, up_ref, down_ref, cot_ref, ws_ref, act_ref, slope_ref, cot_side):
+    _, rows_low, cols_low, chan = low_ref.shape
+    count = rows_low * cols_low
     low = jnp.concatenate([up_ref[0], low_ref[0], down_ref[0]], axis=0)
     flat = low.reshape(-1, chan)
     rows = [[], []]
@@ -146,99 +130,178 @@
         rows[0].append(even.reshape(count, chan))
         rows[1].append(odd.reshape(count, chan))
     at = column(count, cols_low, chan)
-    pres = []
     for a in range(2):
         first, second, third = rows[a]
-        pres.append(from_left(first, at) + (second + third))
-        pres.append((first + second) + from_right(third, at, cols_low - 1))
-
-    acts, pgs = [], []
-    for side, pre in enumerate(pres):
-        sig = jax.nn.sigmoid(pre)
-        acts.append((pre * sig).astype(jnp.bfloat16))
-        act_grad = product_nt(cot_side[frame, side], wt_ref[0])
-        for k in (1, 2):
-            act_grad = act_grad + product_nt(cot_side[frame + k, side], wt_ref[k])
-        pgs.append((act_grad * (sig * (1.0 + pre * (1.0 - sig)))).astype(jnp.bfloat16))
-        act_ref[0, side] = acts[side]
-        pg_ref[0, side] = pgs[side]
-
+        for b in range(2):
+            if b == 0:
+                pre = from_left(first, at) + (second + third)
+            else:
+                pre = (first + second) + from_right(third, at, cols_low - 1)
+            sig = jax.nn.sigmoid(pre)
+            act_ref[0, 2 * a + b] = (pre * sig).astype(jnp.bfloat16)
+            slope_ref[0, 2 * a + b] = sig * (1.0 + pre * (1.0 - sig))
+    sort_columns(cot_ref.at[0], cot_side.at[0], cols_low)
+
+
+def add_sums(low, act, pg, cots, out_ref):
+    rows_low, cols_low, half = low.shape[0] - 2, low.shape[1], low.shape[2]
+    count = rows_low * cols_low
     sums = []
-    wide = flat.astype(jnp.float32)
-    at = column(wide.shape[0], cols_low, chan)
+    wide = low.reshape(-1, half).astype(jnp.float32)
+    at = column(wide.shape[0], cols_low, half)
     moved = [from_left(wide, at), wide, from_right(wide, at, cols_low - 1)]
     turned = {}
     for dc in range(3):
         view = moved[dc].astype(jnp.bfloat16).reshape(low.shape)
         for dr in range(3):
-            turned[dr - 1, dc - 1] = view[dr : dr + rows_low].reshape(count, chan).T
-    pg = jnp.concatenate(pgs, axis=0)
+            turned[dr - 1, dc - 1] = view[dr : dr + rows_low].reshape(count, half).T
     for i in range(3):
         for j in range(3):
             left = jnp.concatenate([turned[(a + i - 1) // 2, (b + j - 1) // 2] for a, b in SIDES], axis=1)
             sums.append(product(left, pg))
-    act = jnp.concatenate(acts, axis=0).T
-    for k in range(3):
-        sums.append(product(act, cot_side[frame + k].reshape(4 * count, chan)))
+    act = act.T
+    for cot in cots:
+        sums.append(product(act, cot))
+
+    def each_piece(store):
+        parts = out_ref.shape[0]
+        size = half // parts
+        for tap, value in enumerate(sums):
+            for n in range(parts):
+                store(n, slice(tap * size, (tap + 1) * size), value[n * size : (n + 1) * size])
+
+    @pl.when(pl.program_id(0) == 0)
+    def _():
+        def store(n, rows, value):
+            out_ref[n, rows, :] = value
+
+        each_piece(store)
+
+    @pl.when(pl.program_id(0) > 0)
+    def _():
+        def store(n, rows, value):
+            out_ref[n, rows, :] += value
+
+        each_piece(store)
+
+
+def backward_kernel(_, low_ref, up_ref, down_ref, act_ref, slope_ref, cot_ref, later_ref, wt_ref, pg_ref, ext_ref, out_ref):
+    frame = pl.program_id(0)
+    frames, _, count, chan = cot_ref.shape
+    cols_low = low_ref.shape[2]
 
     @pl.when(frame == 0)
     def _():
-        for tap, value in enumerate(sums):
-            acc[tap] = value
-
-    @pl.when(frame > 0)
-    def _():
-        for tap, value in enumerate(sums):
-            acc[tap] += value
-
-    @pl.when(frame == frames - 1)
-    def _():
-        parts = mine_ref.shape[0]
-        half = chan // 2
-        size = half // parts
-        core = core_ref[0]
-        for out, start in ((mine_ref, core * half), (other_ref, half - core * half)):
-            for n in range(parts):
-                for tap in range(12):
-                    begin = pl.multiple_of(start + n * size, size)
-                    out[n, tap * size : (tap + 1) * size, :] = acc[tap, pl.ds(begin, size), :]
+        ext_ref[:frames] = cot_ref[...]
+        for n in range(2):
+            sort_columns(later_ref.at[n], ext_ref.at[frames + n], cols_low)
+
+    pgs = []
+    for side in range(4):
+        act_grad = product_nt(ext_ref[frame, side], wt_ref[0])
+        for k in (1, 2):
+            act_grad = act_grad + product_nt(ext_ref[frame + k, side], wt_ref[k])
+        pgs.append((act_grad * slope_ref[0, side]).astype(jnp.bfloat16))
+        pg_ref[0, side] = pgs[side]
+    low = jnp.concatenate([up_ref[0], low_ref[0], down_ref[0]], axis=0)
+    act = act_ref[0].reshape(4 * count, -1)
+    cots = [ext_ref[frame + k].reshape(4 * count, chan) for k in range(3)]
+    add_sums(low, act, jnp.concatenate(pgs, axis=0), cots, out_ref)
+
+
+def half_kernel(_, low_ref, up_ref, down_ref, act_ref, pg_ref, ext_ref, __, out_ref):
+    frame = pl.program_id(0)
+    _, _, count, chan = pg_ref.shape
+    low = jnp.concatenate([up_ref[0], low_ref[0], down_ref[0]], axis=0)
+    act = act_ref[0].reshape(4 * count, -1)
+    cots = [ext_ref[frame + k].reshape(4 * count, chan) for k in range(3)]
+    add_sums(low, act, pg_ref[0].reshape(4 * count, chan), cots, out_ref)
 
 
 def whole(shape):
-    return pl.BlockSpec(shape, lambda f: (0,) * len(shape))
+    return pl.BlockSpec(shape, lambda f, *_: (0,) * len(shape))
 
 
 def each(shape):
-    return pl.BlockSpec((1,) + tuple(shape[1:]), lambda f: (f,) + (0,) * (len(shape) - 1))
+    return pl.BlockSpec((1,) + tuple(shape[1:]), lambda f, *_: (f,) + (0,) * (len(shape) - 1))
+
+
+def half_of(shape):
+    block = (1,) + tuple(shape[1:-1]) + (shape[-1] // 2,)
+    return pl.BlockSpec(block, lambda f, side: (f,) + (0,) * (len(shape) - 2) + (side[0],))
 
 
 SCALAR = pl.BlockSpec(memory_space=pltpu.SMEM)
 UNREAD = pl.BlockSpec(memory_space=pl.ANY)
 
 
-def weight_grads(core, parts, low, up, down, cot, later, ws, wt):
+def like(shape, dtype):
+    return jax.ShapeDtypeStruct(shape, dtype)
+
+
+TOKEN = like((8, 128), jnp.float32)
+
+
+def cost(units, mib):
+    return pl.CostEstimate(flops=units * 2 * 2048 * 256 * 256, bytes_accessed=mib * 2**20, transcendentals=0)
+
+
+def forward(low, up, down, cot, ws):
     frames, rows_low, cols_low, chan = low.shape
-    count = rows_low * cols_low
-    side = (frames, 4, count, chan)
+    side = (frames, 4, rows_low * cols_low, chan)
+    return pl.pallas_call(
+        forward_kernel,
+        grid=(frames,),
+        in_specs=[each(low.shape), each(up.shape), each(down.shape), each(cot.shape), whole(ws.shape)],
+        out_specs=[each(side)] * 3,
+        out_shape=[like(side, jnp.bfloat16), like(side, jnp.float32), like(side, jnp.bfloat16)],
+        compiler_params=grant(20),
+        cost_estimate=cost(10, 8),
+        name="forward",
+    )(low, up, down, cot, ws)
+
+
+def backward(side, parts, low, up, down, act, slope, cot, later, wt):
+    frames, _, count, chan = act.shape
+    ext = (frames + 2,) + act.shape[1:]
     piece = (parts, 12 * (chan // (2 * parts)), chan)
-    flops = 2 * 2048 * chan * chan * 20
-    return pl.pallas_call(
-        grads_kernel,
-        grid=(frames,),
-        in_specs=[SCALAR, each(low.shape), each(up.shape), each(down.shape),
-                  whole(cot.shape), whole(later.shape), whole(ws.shape), whole(wt.shape)],
-        out_specs=[each(side), each(side), whole(piece), whole(piece)],
-        out_shape=[jax.ShapeDtypeStruct(side, jnp.bfloat16)] * 2
-        + [jax.ShapeDtypeStruct(piece, jnp.float32)] * 2,
-        scratch_shapes=[pltpu.VMEM((frames + 2, 4, count, chan), jnp.bfloat16),
-                        pltpu.VMEM((12, chan, chan), jnp.float32)],
-        compiler_params=VMEM,
-        cost_estimate=pl.CostEstimate(flops=flops, bytes_accessed=8 * 2**20, transcendentals=frames * 4 * count * chan),
-        name="weight_grads",
-    )(core, low, up, down, cot, later, ws, wt)
-
-
-def section_kernel(act_ref, low_ref, wt_ref, _, out_ref):
+    return pl.pallas_call(
+        backward_kernel,
+        grid_spec=pltpu.PrefetchScalarGridSpec(
+            num_scalar_prefetch=1,
+            grid=(frames,),
+            in_specs=[half_of(low.shape), half_of(up.shape), half_of(down.shape), half_of(act.shape),
+                      each(slope.shape), whole(cot.shape), whole(later.shape), whole(wt.shape)],
+            out_specs=[each(act.shape), whole(ext), whole(piece)],
+        ),
+        out_shape=[like(act.shape, jnp.bfloat16), like(ext, jnp.bfloat16), like(piece, jnp.float32)],
+        compiler_params=grant(28),
+        cost_estimate=cost(15, 10),
+        name="backward",
+    )(side, low, up, down, act, slope, cot, later, wt)
+
+
+def half_grads(side, parts, low, up, down, act, pg, ext, before):
+    frames, _, _, chan = act.shape
+    piece = (parts, 12 * (chan // (2 * parts)), chan)
+    return pl.pallas_call(
+        half_kernel,
+        grid_spec=pltpu.PrefetchScalarGridSpec(
+            num_scalar_prefetch=1,
+            grid=(frames,),
+            in_specs=[half_of(low.shape), half_of(up.shape), half_of(down.shape), half_of(act.shape),
+                      each(pg.shape), whole(ext.shape), UNREAD],
+            out_specs=whole(piece),
+        ),
+        out_shape=like(piece, jnp.float32),
+        compiler_params=grant(24),
+        cost_estimate=cost(10, 6),
+        name="half_grads",
+    )(side, low, up, down, act, pg, ext, before)
+
+
+def section_kernel(act_ref, low_ref, wt_ref, _, out_ref, token_ref):
+    token_ref[...] = jnp.zeros_like(token_ref)
     frame = pl.program_id(0)
     _, rows_low, cols_low, chan = low_ref.shape
     group = rows_at_once(rows_low, cols_low)
@@ -264,15 +327,16 @@
         section_kernel,
         grid=(frames,),
         in_specs=[whole(act_ext.shape), each(low.shape), whole(wt.shape), UNREAD],
-        out_specs=each(out),
-        out_shape=jax.ShapeDtypeStruct(out, jnp.bfloat16),
-        compiler_params=VMEM,
+        out_specs=[each(out), whole(TOKEN.shape)],
+        out_shape=[like(out, jnp.bfloat16), TOKEN],
+        compiler_params=grant(16),
         cost_estimate=pl.CostEstimate(flops=2 * 2048 * chan * chan * 4, bytes_accessed=3 * 2**20, transcendentals=0),
         name="section",
     )(act_ext, low, wt, before)
 
 
-def input_kernel(pg_ref, up_ref, down_ref, cot_ref, ws_ref, _, out_ref):
+def input_kernel(pg_ref, up_ref, down_ref, cot_ref, ws_ref, _, out_ref, token_ref):
+    token_ref[...] = jnp.zeros_like(token_ref)
     _, rows_low, cols_low, chan = out_ref.shape
     group = rows_at_once(rows_low, cols_low)
     span = group * cols_low
@@ -313,9 +377,9 @@
         input_kernel,
         grid=(low_shape[0],),
         in_specs=[each(pg.shape), each(up.shape), each(down.shape), each(cot.shape), whole(ws.shape), UNREAD],
-        out_specs=each(low_shape),
-        out_shape=jax.ShapeDtypeStruct(low_shape, jnp.bfloat16),
-        compiler_params=VMEM,
+        out_specs=[each(low_shape), whole(TOKEN.shape)],
+        out_shape=[like(low_shape, jnp.bfloat16), TOKEN],
+        compiler_params=grant(20),
         cost_estimate=pl.CostEstimate(flops=2 * 2048 * chan * chan * 6, bytes_accessed=4 * 2**20, transcendentals=0),
         name="input_grads",
     )(pg, up, down, cot, ws, before)
@@ -345,16 +409,32 @@
         out_specs=[full, full],
         out_shape=[jax.ShapeDtypeStruct((3, 3, chan, chan), jnp.float32),
                    jax.ShapeDtypeStruct((3, chan, chan), jnp.float32)],
-        compiler_params=VMEM,
+        compiler_params=grant(10),
         name="place",
     )(core, half, theirs)
+
+
+def add_kernel(mine_ref, theirs_ref, out_ref):
+    out_ref[...] = (mine_ref[...] + theirs_ref[...]).astype(jnp.bfloat16)
+
+
+def add_halves(mine, theirs):
+    full = pl.BlockSpec(memory_space=pltpu.VMEM)
+    return pl.pallas_call(
+        add_kernel,
+        in_specs=[full, full],
+        out_specs=full,
+        out_shape=like(mine.shape, jnp.bfloat16),
+        compiler_params=grant(8),
+        name="add_halves",
+    )(mine, theirs)
 
 
 def sum_kernel(got_ref, *refs):
     total = got_ref[0].astype(jnp.float32)
     for n in range(1, got_ref.shape[0]):
         total = total + got_ref[n].astype(jnp.float32)
-    refs[-1][...] = total
+    refs[-1][...] = total.astype(jnp.bfloat16)
 
 
 def sum_parts(got, *before):
@@ -363,8 +443,8 @@
         sum_kernel,
         in_specs=[full] + [UNREAD] * len(before),
         out_specs=full,
-        out_shape=jax.ShapeDtypeStruct(got.shape[1:], jnp.float32),
-        compiler_params=VMEM,
+        out_shape=like(got.shape[1:], jnp.bfloat16),
+        compiler_params=grant(4),
         name="sum_parts",
     )(got, *before)
 
@@ -376,17 +456,21 @@
     up = bits.shift(low[:, -1:], "height", 1)
     down = bits.shift(low[:, :1], "height", -1)
     later = bits.shift(cot[:2], "tm", -1)
-    act, pg, mine, other = weight_grads(
-        core, 1 << len(bits.near), low, up, down, cot, later, spatial_weight, temporal_weight
+    parts = 1 << len(bits.near)
+    act, slope, cot_side = forward(low, up, down, cot, spatial_weight)
+    earlier = bits.shift(act[frames - 2 :], "tm", 1)
+    pg, ext, other = backward(
+        1 - core, parts, low, up, down, act, slope, cot_side, later, temporal_weight
     )
-    kept = bits.halves(mine, other)
+    theirs = bits.swap(other, bits.core)
+    mine = half_grads(core, parts, low, up, down, act, pg, ext, earlier)
+    kept = add_halves(mine, theirs)
     got = bits.exchange(kept)
-    earlier = bits.shift(act[frames - 2 :], "tm", 1)
-    section_out = section(jnp.concatenate([earlier, act], axis=0), low, temporal_weight, kept)
+    section_out, section_done = section(jnp.concatenate([earlier, act], axis=0), low, temporal_weight, kept)
     above = bits.shift(pg[:, 2:, -cols_low:], "height", 1)
     below = bits.shift(pg[:, :2, :cols_low], "height", -1)
-    input_grad = input_grads(pg, above, below, cot, spatial_weight, kept, low.shape)
-    total = sum_parts(got, section_out, input_grad)
+    input_grad, input_done = input_grads(pg, above, below, cot, spatial_weight, kept, low.shape)
+    total = sum_parts(got, section_done, input_done)
     half, theirs = bits.gather(total, got.shape[0])
     spatial_grad, temporal_grad = place(core, half, theirs, chan)
     return section_out[None], input_grad[None], spatial_grad, temporal_grad

time: 103 us -> 87.4 us (0.85)
  starting transfers between devices: 21.9 us -> 31.9 us
  blocking collectives: 22.3 us -> 13.5 us
  Pallas kernels: 30.1 us -> 22.5 us
  other arithmetic: 5.69 us -> 0.16 us
  waiting for transfers between devices: 14.3 us -> 12.5 us
  local copies, waits for them, and re-layouts: 6.92 us -> 5.55 us
    all_to_all x1, blocking collectives: 22.3 us -> 13.5 us  [exchange(): return lax.all_to_all(parts, tuple(self.near), 0, 0, tiled=True)]
    all_to_all x1, starting transfers between devices: 4.92 us -> 12.6 us  [exchange(): return lax.all_to_all(parts, tuple(self.near), 0, 0, tiled=True)]
    convert_element_type x3 -> x1, other arithmetic: 4.41 us -> 0.03 us  [gather(): (total.astype(jnp.float32) + self.swap(total, axis).astype(jnp.float32))....]
    ppermute x3, waiting for transfers between devices: 8.86 us -> 5.91 us  [swap(): return lax.ppermute(block, axis, [(0, 1), (1, 0)])]
    ppermute x6, starting transfers between devices: 14.2 us -> 16.2 us  [shift(): return lax.ppermute(block, axes, route)]
    pallas_call x1, Pallas kernels: 1.91 us -> 0.1 us  [sum_parts(): pl.pallas_call(sum_kernel, in_specs=[full] + [UNREAD] * len(before), out_...]
    pallas_call x1, Pallas kernels: 4.93 us -> 3.18 us  [section(): pl.pallas_call(section_kernel, grid=(frames,), in_specs=[whole(act_ext.sh...]
    pallas_call x1, Pallas kernels: 6.18 us -> 4.63 us  [input_grads(): pl.pallas_call(input_kernel, grid=(low_shape[0],), in_specs=[each(pg.shap...]
  transfers between devices with their start and end apart: 10 -> 10, of which waited for: 5 -> 6; matrix products, arithmetic and copies ran while one was open for 3% -> 1% of each run, Pallas kernels for 11% -> 16%
where the time goes in v1:
time: 87.4 us; the launch traced here: 86.9 us
  starting transfers between devices  31.9 us (36%)
  Pallas kernels  22.5 us (26%)
  blocking collectives  13.5 us (15%)
  waiting for transfers between devices  12.5 us (14%)
  local copies, waits for them, and re-layouts  5.55 us (6%)
    ppermute x6, starting transfers between devices, shift(): return lax.ppermute(block, axes, route)  16.2 us
    all_to_all x1, blocking collectives, exchange(): return lax.all_to_all(parts, tuple(self.near), 0, 0, tiled=True)  13.5 us
    all_to_all x1, starting transfers between devices, exchange(): return lax.all_to_all(parts, tuple(self.near), 0, 0, tiled=True)  12.6 us
    ppermute x6, waiting for transfers between devices, shift(): return lax.ppermute(block, axes, route)  6.57 us
    pallas_call x1, Pallas kernels, backward(): pl.pallas_call(backward_kernel, grid_spec=pltpu.PrefetchScalarGridSpec(nu...  5.93 us
    ppermute x3, waiting for transfers between devices, swap(): return lax.ppermute(block, axis, [(0, 1), (1, 0)])  5.91 us
    pallas_call x1, Pallas kernels, input_grads(): pl.pallas_call(input_kernel, grid=(low_shape[0],), in_specs=[each(pg.shap...  4.63 us
    unnamed x18, local copies, waits for them, and re-layouts  3.48 us
  transfers between devices with their start and end apart: 10, of which 6 were waited for; matrix products, arithmetic and copies ran while one was open for 1% of the time, Pallas kernels for 16%

profile of v1, /device:TPU:0, one launch (start us, length us, event | category | flops | bytes accessed | tf_op | source)
XLA Modules:
  0.0 86.9 jit_solution(11230287361442822332)
XLA Ops:
  0.6 1.1 %slice_bitcast_fusion = bf16[2,8,64,256]{3,2,1,0:T(8,128)(2,1)S(1)} fusion(bf16[1,4,8,64,256]{4,3,2,1,0:T(8,128)(2,1)} %param.7), kind=kLoop, calls=%fused_computation.1 | loop fusion | bytes 1048576 | tf_op jit(solution)/shard_map/slice | solution.py:458
  1.7 1.3 %collective-permute-start.3 = (bf16[2,8,64,256]{3,2,1,0:T(8,128)(2,1)S(1)}, bf16[2,8,64,256]{3,2,1,0:T(8,128)(2,1)S(1)}, u32[]{:S(2)}, u32[]{:S(2)}) collective-permute-start(bf16[2,8,64,256]{3,2,1,0:T(8,128)(2,1)S(1)} %slice_bitcast_fusion), channel_id=1, source_target_pairs={{4,0},{8,4},{12,8},{5,1},{9,5},{13,9},{6,2},{10,6},{14,10},{7,3},{... | collective-permute-start | bytes 1572872 | tf_op jit(solution)/shard_map/ppermute | solution.py:39
  3.0 0.9 %fusion.1 = (bf16[4,1,32,256]{3,2,1,0:T(8,128)(2,1)S(1)}, bf16[4,1,32,256]{3,2,1,0:T(8,128)(2,1)S(1)}) fusion(bf16[4,4,32,256]{3,2,1,0:T(8,128)(2,1)} %bitcast.9), kind=kLoop, calls=%fused_computation.4 | loop fusion | bytes 262144 | tf_op jit(solution)/shard_map/slice | solution.py:457
  3.9 1.3 %collective-permute-start.1 = (bf16[4,1,32,256]{3,2,1,0:T(8,128)(2,1)S(1)}, bf16[4,1,32,256]{3,2,1,0:T(8,128)(2,1)S(1)}, u32[]{:S(2)}, u32[]{:S(2)}) collective-permute-start(bf16[4,1,32,256]{3,2,1,0:T(8,128)(2,1)S(1)} %get-tuple-element.30), channel_id=1, source_target_pairs={{1,0},{2,1},{3,2},{5,4},{6,5},{7,6},{9,8},{10,9},{11,10},{13,12},{... | collective-permute-start | bytes 196616 | tf_op jit(solution)/shard_map/ppermute | solution.py:39
  5.2 5.6 %collective-permute-start = (bf16[4,1,32,256]{3,2,1,0:T(8,128)(2,1)S(1)}, bf16[4,1,32,256]{3,2,1,0:T(8,128)(2,1)S(1)}, u32[]{:S(2)}, u32[]{:S(2)}) collective-permute-start(bf16[4,1,32,256]{3,2,1,0:T(8,128)(2,1)S(1)} %get-tuple-element.31), channel_id=1, source_target_pairs={{0,1},{1,2},{2,3},{4,5},{5,6},{6,7},{8,9},{9,10},{10,11},{12,13},{... | collective-permute-start | bytes 196616 | tf_op jit(solution)/shard_map/ppermute | solution.py:39
  10.8 0.6 collective-permute-done.1.down_ref
  11.4 1.7 %collective-permute-done.up_ref = bf16[4,1,32,256]{3,2,1,0:T(8,128)(2,1)S(1)} collective-permute-done((bf16[4,1,32,256]{3,2,1,0:T(8,128)(2,1)S(1)}, bf16[4,1,32,256]{3,2,1,0:T(8,128)(2,1)S(1)}, u32[]{:S(2)}, u32[]{:S(2)}) %collective-permute-start) | collective-permute-done | bytes 65568 | tf_op jit(solution)/shard_map/ppermute | solution.py:39
  13.1 0.0 copy-start
  13.1 1.2 %copy-done = bf16[1,4,8,64,256]{4,3,2,1,0:T(8,128)(2,1)S(1)} copy-done((bf16[1,4,8,64,256]{4,3,2,1,0:T(8,128)(2,1)S(1)}, bf16[1,4,8,64,256]{4,3,2,1,0:T(8,128)(2,1)}, u32[]{:S(2)}) %copy-start) | copy-done | bytes 1048600
  14.3 0.0 copy-start.2
  14.3 0.9 %copy-done.2 = bf16[1,4,4,32,256]{4,3,2,1,0:T(8,128)(2,1)S(1)} copy-done((bf16[1,4,4,32,256]{4,3,2,1,0:T(8,128)(2,1)S(1)}, bf16[1,4,4,32,256]{4,3,2,1,0:T(8,128)(2,1)}, u32[]{:S(2)}) %copy-start.2) | copy-done | bytes 262168
  15.3 1.3 %copy-done.5 = bf16[3,3,256,256]{3,2,1,0:T(8,128)(2,1)S(1)} copy-done((bf16[3,3,256,256]{3,2,1,0:T(8,128)(2,1)S(1)}, bf16[3,3,256,256]{3,2,1,0:T(8,128)(2,1)}, u32[]{:S(2)}) %copy-start.5) | copy-done | bytes 1179672
  16.5 2.5 %forward.1 = (bf16[4,4,128,256]{3,2,1,0:T(8,128)(2,1)S(1)}, f32[4,4,128,256]{3,2,1,0:T(8,128)S(1)}, bf16[4,4,128,256]{3,2,1,0:T(8,128)(2,1)S(1)}) custom-call(bf16[4,4,32,256]{3,2,1,0:T(8,128)(2,1)S(1)} %bitcast.10, bf16[4,1,32,256]{3,2,1,0:T(8,128)(2,1)S(1)} %collective-permute-done.up_ref, bf16[4,1,32,256]{3,2,1,0:T(8,128)(2,1)S(1)} %collective-permute-done.1.down_ref, ...), custom_call_target="tpu_custom_call" | custom-call | flops 2684354560 | bytes 8388608 | tf_op jit(solution)/shard_map/forward/pallas_call | solution.py:252
  19.1 0.0 collective-permute-done.3.later_ref
  19.1 0.0 copy-done.3
  19.1 0.0 copy-done.7
  19.1 5.9 %backward.1 = (bf16[4,4,128,256]{3,2,1,0:T(8,128)(2,1)S(1)}, bf16[6,4,128,256]{3,2,1,0:T(8,128)(2,1)S(1)}, f32[8,192,256]{2,1,0:T(8,128)S(1)}) custom-call(s32[1]{0:T(128)S(6)} %sub.3._, bf16[4,4,32,256]{3,2,1,0:T(8,128)(2,1)S(1)} %bitcast.11, bf16[4,1,32,256]{3,2,1,0:T(8,128)(2,1)S(1)} %collective-permute-done.up_ref, ...), custom_call_target="tpu_custom_call" | custom-call | flops 4026531840 | bytes 10485760 | tf_op jit(solution)/shard_map/backward/pallas_call | solution.py:268
  25.0 0.4 collective-permute-start.4
  25.5 2.1 %collective-permute-start.2 = (bf16[2,4,128,256]{3,2,1,0:T(8,128)(2,1)S(1)}, bf16[2,4,128,256]{3,2,1,0:T(8,128)(2,1)S(1)}, u32[]{:S(2)}, u32[]{:S(2)}) collective-permute-start(bf16[2,4,128,256]{3,2,1,0:T(8,128)(2,1)S(1)} %slice.23), channel_id=1, source_target_pairs={{0,4},{4,8},{8,12},{1,5},{5,9},{9,13},{2,6},{6,10},{10,14},{3,7},{... | collective-permute-start | bytes 1572872 | tf_op jit(solution)/shard_map/ppermute | solution.py:39
  27.6 1.6 %collective-permute-done.2.__ = bf16[2,4,128,256]{3,2,1,0:T(8,128)(2,1)S(1)} collective-permute-done((bf16[2,4,128,256]{3,2,1,0:T(8,128)(2,1)S(1)}, bf16[2,4,128,256]{3,2,1,0:T(8,128)(2,1)S(1)}, u32[]{:S(2)}, u32[]{:S(2)}) %collective-permute-start.2) | collective-permute-done | bytes 524320 | tf_op jit(solution)/shard_map/ppermute | solution.py:39
  29.2 3.2 %half_grads.1.mine_ref = f32[8,192,256]{2,1,0:T(8,128)S(1)} custom-call(s32[1]{0:T(128)} %bitcast.2._.core_ref, bf16[4,4,32,256]{3,2,1,0:T(8,128)(2,1)S(1)} %bitcast.12, bf16[4,1,32,256]{3,2,1,0:T(8,128)(2,1)S(1)} %collective-permute-done.up_ref, bf16[4,1,32,256]{3,2,1,0:T(8,128)(2,1)S(1)} %collective-permute-done.1.down_ref, ...), custom_call_target="tpu_custom_call" | custom-call | flops 2684354560 | bytes 6291456 | tf_op jit(solution)/shard_map/half_grads/pallas_call | solution.py:287
  32.4 0.0 collective-permute-done.4.theirs_ref
  32.5 1.0 %add_halves.1._ = bf16[8,192,256]{2,1,0:T(8,128)(2,1)} custom-call(f32[8,192,256]{2,1,0:T(8,128)S(1)} %half_grads.1.mine_ref, f32[8,192,256]{2,1,0:T(8,128)S(1)} %collective-permute-done.4.theirs_ref), custom_call_target="tpu_custom_call" | custom-call | tf_op jit(solution)/shard_map/add_halves/pallas_call | solution.py:423
  33.5 12.6 %all-to-all-start = ((bf16[8,192,256]{2,1,0:T(8,128)(2,1)}), bf16[8,192,256]{2,1,0:T(8,128)(2,1)S(1)}, u32[]{:S(2)}, u32[]{:S(2)}) async-start(bf16[8,192,256]{2,1,0:T(8,128)(2,1)} %add_halves.1._), calls=%async_computation | async-start | bytes 1572864 | tf_op jit(solution)/shard_map/all_to_all | solution.py:42
  46.1 1.3 %collective-permute-start.6 = (bf16[4,2,32,256]{3,2,1,0:T(8,128)(2,1)S(1)}, bf16[4,2,32,256]{3,2,1,0:T(8,128)(2,1)S(1)}, u32[]{:S(2)}, u32[]{:S(2)}) collective-permute-start(bf16[4,2,32,256]{3,2,1,0:T(8,128)(2,1)S(1)} %get-tuple-element.28), channel_id=1, source_target_pairs={{1,0},{2,1},{3,2},{5,4},{6,5},{7,6},{9,8},{10,9},{11,10},{13,12},{... | collective-permute-start | bytes 393224 | tf_op jit(solution)/shard_map/ppermute | solution.py:39
  47.4 0.0 copy-start.4
  47.4 0.0 copy-start.8
  47.4 4.7 %collective-permute-start.5 = (bf16[4,2,32,256]{3,2,1,0:T(8,128)(2,1)S(1)}, bf16[4,2,32,256]{3,2,1,0:T(8,128)(2,1)S(1)}, u32[]{:S(2)}, u32[]{:S(2)}) collective-permute-start(bf16[4,2,32,256]{3,2,1,0:T(8,128)(2,1)S(1)} %get-tuple-element.29), channel_id=1, source_target_pairs={{0,1},{1,2},{2,3},{4,5},{5,6},{6,7},{8,9},{9,10},{10,11},{12,13},{... | collective-permute-start | bytes 393224 | tf_op jit(solution)/shard_map/ppermute | solution.py:39
  52.1 0.1 pad_maximum_fusion.act_ref
  52.3 0.0 copy-done.4
  52.3 0.0 copy-done.8
  52.3 0.0 copy-start.1
  52.3 0.0 copy-start.6
  52.3 3.2 %section.1 = (bf16[4,8,64,256]{3,2,1,0:T(8,128)(2,1)}, f32[8,128]{1,0:T(8,128)S(1)}) custom-call(bf16[6,4,128,256]{3,2,1,0:T(8,128)(2,1)S(1)} %pad_maximum_fusion.act_ref, bf16[4,4,32,256]{3,2,1,0:T(8,128)(2,1)S(1)} %bitcast.13, bf16[3,256,256]{2,1,0:T(8,128)(2,1)S(1)} %copy-done.8, bf16[8,192,256]{2,1,0:T(8,128)(2,1)} %add_halves.1._), custom_call_target="tpu_custom_call" | custom-call | flops 1073741824 | bytes 3145728 | tf_op jit(solution)/shard_map/section/pallas_call | solution.py:326
  55.5 2.6 %collective-permute-done.6.down_ref = bf16[4,2,32,256]{3,2,1,0:T(8,128)(2,1)S(1)} collective-permute-done((bf16[4,2,32,256]{3,2,1,0:T(8,128)(2,1)S(1)}, bf16[4,2,32,256]{3,2,1,0:T(8,128)(2,1)S(1)}, u32[]{:S(2)}, u32[]{:S(2)}) %collective-permute-start.6) | collective-permute-done | bytes 131104 | tf_op jit(solution)/shard_map/ppermute | solution.py:39
  58.1 0.0 collective-permute-done.5.up_ref
  58.1 0.0 copy-done.1
  58.1 0.0 copy-done.6
  58.1 4.6 %input_grads.1 = (bf16[4,4,32,256]{3,2,1,0:T(8,128)(2,1)}, f32[8,128]{1,0:T(8,128)S(1)}) custom-call(bf16[4,4,128,256]{3,2,1,0:T(8,128)(2,1)S(1)} %get-tuple-element.19.pg_ref, bf16[4,2,32,256]{3,2,1,0:T(8,128)(2,1)S(1)} %collective-permute-done.5.up_ref, bf16[4,2,32,256]{3,2,1,0:T(8,128)(2,1)S(1)} %collective-permute-done.6.down_ref, ...), custom_call_target="tpu_custom_call" | custom-call | flops 1610612736 | bytes 4194304 | tf_op jit(solution)/shard_map/input_grads/pallas_call | solution.py:376
  62.7 0.0 all-to-all-done.got_ref
  62.7 0.1 sum_parts.1
  62.8 2.6 %collective-permute-start.7 = (bf16[192,256]{1,0:T(8,128)(2,1)S(1)}, bf16[192,256]{1,0:T(8,128)(2,1)S(1)}, u32[]{:S(2)}, u32[]{:S(2)}) collective-permute-start(bf16[192,256]{1,0:T(8,128)(2,1)S(1)} %sum_parts.1), channel_id=1, source_target_pairs={{0,2},{2,0},{1,3},{3,1},{4,6},{6,4},{5,7},{7,5},{8,10},{10,8},{9,1... | collective-permute-start | bytes 294920 | tf_op jit(solution)/shard_map/ppermute | solution.py:33
  65.5 3.6 %collective-permute-done.7 = bf16[192,256]{1,0:T(8,128)(2,1)S(1)} collective-permute-done((bf16[192,256]{1,0:T(8,128)(2,1)S(1)}, bf16[192,256]{1,0:T(8,128)(2,1)S(1)}, u32[]{:S(2)}, u32[]{:S(2)}) %collective-permute-start.7) | collective-permute-done | bytes 98336 | tf_op jit(solution)/shard_map/ppermute | solution.py:33
  69.1 0.1 broadcast_in_dim.11
  69.2 13.5 %all_to_all.10.half_ref = bf16[8,192,256]{2,1,0:T(8,128)(2,1)S(1)} all-to-all(bf16[8,192,256]{2,1,0:T(8,128)(2,1)S(1)} %broadcast_in_dim.11), channel_id=1, replica_groups=mesh['dp0'=2,'tm1'=2,'tm0'=2,'height1'=2,'height0'=2] {'dp0','tm1','heig..., dimensions={0} | all-to-all | bytes 1572864 | tf_op jit(solution)/shard_map/all_to_all | solution.py:42
  82.7 0.0 collective-permute-start.8
  82.7 2.3 %collective-permute-done.8.theirs_ref = bf16[8,192,256]{2,1,0:T(8,128)(2,1)S(1)} collective-permute-done((bf16[8,192,256]{2,1,0:T(8,128)(2,1)S(1)}, bf16[8,192,256]{2,1,0:T(8,128)(2,1)S(1)}, u32[]{:S(2)}, u32[]{:S(2)}) %collective-permute-start.8) | collective-permute-done | bytes 786464 | tf_op jit(solution)/shard_map/ppermute | solution.py:33
  85.0 1.9 %place.1 = (f32[3,3,256,256]{3,2,1,0:T(8,128)}, f32[3,256,256]{2,1,0:T(8,128)}) custom-call(s32[1]{0:T(128)} %bitcast.2._.core_ref, bf16[8,192,256]{2,1,0:T(8,128)(2,1)S(1)} %all_to_all.10.half_ref, bf16[8,192,256]{2,1,0:T(8,128)(2,1)S(1)} %collective-permute-done.8.theirs_ref), custom_call_target="tpu_custom_call" | custom-call | tf_op jit(solution)/shard_map/place/pallas_call | solution.py:406
  (6 shorter events, 0.1 us)
Async XLA Ops:
  1.7 17.4 %collective-permute-start.3 = (bf16[2,8,64,256]{3,2,1,0:T(8,128)(2,1)S(1)}, bf16[2,8,64,256]{3,2,1,0:T(8,128)(2,1)S(1)}, u32[]{:S(2)}, u32[]{:S(2)}) collective-permute-start(bf16[2,8,64,256]{3,2,1,0:T(8,128)(2,1)S(1)} %slice_bitcast_fusion), channel_id=1, source_target_pairs={{4,0},{8,4},{12,8},{5,1},{9,5},{13,9},{6,2},{10,6},{14,10},{7,3},{... | collective-permute-start | bytes 1572872 | tf_op jit(solution)/shard_map/ppermute | solution.py:39
  3.9 7.5 %collective-permute-start.1 = (bf16[4,1,32,256]{3,2,1,0:T(8,128)(2,1)S(1)}, bf16[4,1,32,256]{3,2,1,0:T(8,128)(2,1)S(1)}, u32[]{:S(2)}, u32[]{:S(2)}) collective-permute-start(bf16[4,1,32,256]{3,2,1,0:T(8,128)(2,1)S(1)} %get-tuple-element.30), channel_id=1, source_target_pairs={{1,0},{2,1},{3,2},{5,4},{6,5},{7,6},{9,8},{10,9},{11,10},{13,12},{... | collective-permute-start | bytes 196616 | tf_op jit(solution)/shard_map/ppermute | solution.py:39
  5.2 7.9 %collective-permute-start = (bf16[4,1,32,256]{3,2,1,0:T(8,128)(2,1)S(1)}, bf16[4,1,32,256]{3,2,1,0:T(8,128)(2,1)S(1)}, u32[]{:S(2)}, u32[]{:S(2)}) collective-permute-start(bf16[4,1,32,256]{3,2,1,0:T(8,128)(2,1)S(1)} %get-tuple-element.31), channel_id=1, source_target_pairs={{0,1},{1,2},{2,3},{4,5},{5,6},{6,7},{8,9},{9,10},{10,11},{12,13},{... | collective-permute-start | bytes 196616 | tf_op jit(solution)/shard_map/ppermute | solution.py:39
  13.1 1.2 %copy-start = (bf16[1,4,8,64,256]{4,3,2,1,0:T(8,128)(2,1)S(1)}, bf16[1,4,8,64,256]{4,3,2,1,0:T(8,128)(2,1)}, u32[]{:S(2)}) copy-start(bf16[1,4,8,64,256]{4,3,2,1,0:T(8,128)(2,1)} %param.7) | copy-start | bytes 3145732
  14.3 0.9 %copy-start.2 = (bf16[1,4,4,32,256]{4,3,2,1,0:T(8,128)(2,1)S(1)}, bf16[1,4,4,32,256]{4,3,2,1,0:T(8,128)(2,1)}, u32[]{:S(2)}) copy-start(bf16[1,4,4,32,256]{4,3,2,1,0:T(8,128)(2,1)} %param.4) | copy-start | bytes 786436
  15.3 1.3 %copy-start.5 = (bf16[3,3,256,256]{3,2,1,0:T(8,128)(2,1)S(1)}, bf16[3,3,256,256]{3,2,1,0:T(8,128)(2,1)}, u32[]{:S(2)}) copy-start(bf16[3,3,256,256]{3,2,1,0:T(8,128)(2,1)} %ws_ref.3) | copy-start | bytes 3538948
  16.5 2.6 %copy-start.3 = (bf16[1,4,4,32,256]{4,3,2,1,0:T(8,128)(2,1)S(1)}, bf16[1,4,4,32,256]{4,3,2,1,0:T(8,128)(2,1)}, u32[]{:S(2)}) copy-start(bf16[1,4,4,32,256]{4,3,2,1,0:T(8,128)(2,1)} %param.4) | copy-start | bytes 786436
  16.5 2.6 %copy-start.7 = (bf16[3,256,256]{2,1,0:T(8,128)(2,1)S(1)}, bf16[3,256,256]{2,1,0:T(8,128)(2,1)}, u32[]{:S(2)}) copy-start(bf16[3,256,256]{2,1,0:T(8,128)(2,1)} %wt_ref.3) | copy-start | bytes 1179652
  25.0 7.4 %collective-permute-start.4 = (f32[8,192,256]{2,1,0:T(8,128)S(1)}, f32[8,192,256]{2,1,0:T(8,128)S(1)}, u32[]{:S(2)}, u32[]{:S(2)}) collective-permute-start(f32[8,192,256]{2,1,0:T(8,128)S(1)} %get-tuple-element.21), channel_id=1, source_target_pairs={{0,4},{4,0},{1,5},{5,1},{2,6},{6,2},{3,7},{7,3},{8,12},{12,8},{9,1... | collective-permute-start | bytes 4718600 | tf_op jit(solution)/shard_map/ppermute | solution.py:33
  25.5 3.7 %collective-permute-start.2 = (bf16[2,4,128,256]{3,2,1,0:T(8,128)(2,1)S(1)}, bf16[2,4,128,256]{3,2,1,0:T(8,128)(2,1)S(1)}, u32[]{:S(2)}, u32[]{:S(2)}) collective-permute-start(bf16[2,4,128,256]{3,2,1,0:T(8,128)(2,1)S(1)} %slice.23), channel_id=1, source_target_pairs={{0,4},{4,8},{8,12},{1,5},{5,9},{9,13},{2,6},{6,10},{10,14},{3,7},{... | collective-permute-start | bytes 1572872 | tf_op jit(solution)/shard_map/ppermute | solution.py:39
  33.5 29.3 %all-to-all-start = ((bf16[8,192,256]{2,1,0:T(8,128)(2,1)}), bf16[8,192,256]{2,1,0:T(8,128)(2,1)S(1)}, u32[]{:S(2)}, u32[]{:S(2)}) async-start(bf16[8,192,256]{2,1,0:T(8,128)(2,1)} %add_halves.1._), calls=%async_computation | async-start | bytes 1572864 | tf_op jit(solution)/shard_map/all_to_all | solution.py:42
  46.1 12.0 %collective-permute-start.6 = (bf16[4,2,32,256]{3,2,1,0:T(8,128)(2,1)S(1)}, bf16[4,2,32,256]{3,2,1,0:T(8,128)(2,1)S(1)}, u32[]{:S(2)}, u32[]{:S(2)}) collective-permute-start(bf16[4,2,32,256]{3,2,1,0:T(8,128)(2,1)S(1)} %get-tuple-element.28), channel_id=1, source_target_pairs={{1,0},{2,1},{3,2},{5,4},{6,5},{7,6},{9,8},{10,9},{11,10},{13,12},{... | collective-permute-start | bytes 393224 | tf_op jit(solution)/shard_map/ppermute | solution.py:39
  47.4 4.9 %copy-start.4 = (bf16[1,4,4,32,256]{4,3,2,1,0:T(8,128)(2,1)S(1)}, bf16[1,4,4,32,256]{4,3,2,1,0:T(8,128)(2,1)}, u32[]{:S(2)}) copy-start(bf16[1,4,4,32,256]{4,3,2,1,0:T(8,128)(2,1)} %param.4) | copy-start | bytes 786436
  47.4 4.9 %copy-start.8 = (bf16[3,256,256]{2,1,0:T(8,128)(2,1)S(1)}, bf16[3,256,256]{2,1,0:T(8,128)(2,1)}, u32[]{:S(2)}) copy-start(bf16[3,256,256]{2,1,0:T(8,128)(2,1)} %wt_ref.3) | copy-start | bytes 1179652
  47.4 10.7 %collective-permute-start.5 = (bf16[4,2,32,256]{3,2,1,0:T(8,128)(2,1)S(1)}, bf16[4,2,32,256]{3,2,1,0:T(8,128)(2,1)S(1)}, u32[]{:S(2)}, u32[]{:S(2)}) collective-permute-start(bf16[4,2,32,256]{3,2,1,0:T(8,128)(2,1)S(1)} %get-tuple-element.29), channel_id=1, source_target_pairs={{0,1},{1,2},{2,3},{4,5},{5,6},{6,7},{8,9},{9,10},{10,11},{12,13},{... | collective-permute-start | bytes 393224 | tf_op jit(solution)/shard_map/ppermute | solution.py:39
  52.3 5.8 %copy-start.1 = (bf16[1,4,8,64,256]{4,3,2,1,0:T(8,128)(2,1)S(1)}, bf16[1,4,8,64,256]{4,3,2,1,0:T(8,128)(2,1)}, u32[]{:S(2)}) copy-start(bf16[1,4,8,64,256]{4,3,2,1,0:T(8,128)(2,1)} %param.7) | copy-start | bytes 3145732
  52.3 5.8 %copy-start.6 = (bf16[3,3,256,256]{3,2,1,0:T(8,128)(2,1)S(1)}, bf16[3,3,256,256]{3,2,1,0:T(8,128)(2,1)}, u32[]{:S(2)}) copy-start(bf16[3,3,256,256]{3,2,1,0:T(8,128)(2,1)} %ws_ref.3) | copy-start | bytes 3538948
  62.8 6.3 %collective-permute-start.7 = (bf16[192,256]{1,0:T(8,128)(2,1)S(1)}, bf16[192,256]{1,0:T(8,128)(2,1)S(1)}, u32[]{:S(2)}, u32[]{:S(2)}) collective-permute-start(bf16[192,256]{1,0:T(8,128)(2,1)S(1)} %sum_parts.1), channel_id=1, source_target_pairs={{0,2},{2,0},{1,3},{3,1},{4,6},{6,4},{5,7},{7,5},{8,10},{10,8},{9,1... | collective-permute-start | bytes 294920 | tf_op jit(solution)/shard_map/ppermute | solution.py:33
  82.7 2.3 %collective-permute-start.8 = (bf16[8,192,256]{2,1,0:T(8,128)(2,1)S(1)}, bf16[8,192,256]{2,1,0:T(8,128)(2,1)S(1)}, u32[]{:S(2)}, u32[]{:S(2)}) collective-permute-start(bf16[8,192,256]{2,1,0:T(8,128)(2,1)S(1)} %all_to_all.10.half_ref), channel_id=1, source_target_pairs={{0,4},{4,0},{1,5},{5,1},{2,6},{6,2},{3,7},{7,3},{8,12},{12,8},{9,1... | collective-permute-start | bytes 2359304 | tf_op jit(solution)/shard_map/ppermute | solution.py:33

commit v2 on v1

--- a/solution.py
+++ b/solution.py
@@ -41,12 +41,20 @@
     def exchange(self, parts):
         return lax.all_to_all(parts, tuple(self.near), 0, 0, tiled=True)
 
-    def gather(self, total, parts):
-        for axis in self.far:
+    def rows(self, first, last):
+        odd = lax.axis_index(self.axes["height"][-1]) == 1
+        return self.pairs(jnp.where(odd, first, last), jnp.where(odd, last, first))
+
+    def pairs(self, inner, outer):
+        axes = self.axes["height"]
+        low = range(1, (1 << len(axes)) - 1, 2)
+        route = [(i, i + 1) for i in low] + [(i + 1, i) for i in low]
+        return self.swap(inner, axes[-1]), lax.ppermute(outer, axes, route)
+
+    def far_sums(self, total):
+        for axis in self.far[:-1]:
             total = (total.astype(jnp.float32) + self.swap(total, axis).astype(jnp.float32)).astype(jnp.bfloat16)
-        spread = jnp.broadcast_to(total, (parts,) + total.shape)
-        half = self.exchange(spread)
-        return half, self.swap(half, self.core)
+        return total, self.swap(total, self.far[-1])
 
 
 SIDES = ((0, 0), (0, 1), (1, 0), (1, 1))
@@ -117,10 +125,16 @@
         target[:, n * span : (n + 1) * span, :] = block
 
 
-def forward_kernel(low_ref, up_ref, down_ref, cot_ref, ws_ref, act_ref, slope_ref, cot_side):
-    _, rows_low, cols_low, chan = low_ref.shape
+def tall(place_ref, low_ref, inner_ref, outer_ref):
+    odd = place_ref[1] == 1
+    up = jnp.where(odd, inner_ref[0], outer_ref[0])
+    down = jnp.where(odd, outer_ref[0], inner_ref[0])
+    return jnp.concatenate([up, low_ref[0], down], axis=0)
+
+
+def spatial(low, ws_ref):
+    rows_low, cols_low, chan = low.shape[0] - 2, low.shape[1], low.shape[2]
     count = rows_low * cols_low
-    low = jnp.concatenate([up_ref[0], low_ref[0], down_ref[0]], axis=0)
     flat = low.reshape(-1, chan)
     rows = [[], []]
     for j in range(3):
@@ -130,17 +144,23 @@
         rows[0].append(even.reshape(count, chan))
         rows[1].append(odd.reshape(count, chan))
     at = column(count, cols_low, chan)
-    for a in range(2):
-        first, second, third = rows[a]
-        for b in range(2):
-            if b == 0:
-                pre = from_left(first, at) + (second + third)
-            else:
-                pre = (first + second) + from_right(third, at, cols_low - 1)
-            sig = jax.nn.sigmoid(pre)
-            act_ref[0, 2 * a + b] = (pre * sig).astype(jnp.bfloat16)
-            slope_ref[0, 2 * a + b] = sig * (1.0 + pre * (1.0 - sig))
-    sort_columns(cot_ref.at[0], cot_side.at[0], cols_low)
+    for first, second, third in rows:
+        yield from_left(first, at) + (second + third)
+        yield (first + second) + from_right(third, at, cols_low - 1)
+
+
+def forward_kernel(place_ref, low_ref, inner_ref, outer_ref, cot_ref, ws_ref, act_ref, slope_ref, cot_side):
+    low = tall(place_ref, low_ref, inner_ref, outer_ref)
+    for side, pre in enumerate(spatial(low, ws_ref)):
+        sig = jax.nn.sigmoid(pre)
+        act_ref[0, side] = (pre * sig).astype(jnp.bfloat16)
+        slope_ref[0, side] = sig * (1.0 + pre * (1.0 - sig))
+    sort_columns(cot_ref.at[0], cot_side.at[0], low.shape[1])
+
+
+def act_kernel(low_ref, ws_ref, act_ref):
+    for side, pre in enumerate(spatial(low_ref[0], ws_ref)):
+        act_ref[0, side] = (pre * jax.nn.sigmoid(pre)).astype(jnp.bfloat16)
 
 
 def add_sums(low, act, pg, cots, out_ref):
@@ -185,7 +205,7 @@
         each_piece(store)
 
 
-def backward_kernel(_, low_ref, up_ref, down_ref, act_ref, slope_ref, cot_ref, later_ref, wt_ref, pg_ref, ext_ref, out_ref):
+def backward_kernel(place_ref, low_ref, inner_ref, outer_ref, act_ref, slope_ref, cot_ref, later_ref, wt_ref, pg_ref, ext_ref, out_ref):
     frame = pl.program_id(0)
     frames, _, count, chan = cot_ref.shape
     cols_low = low_ref.shape[2]
@@ -203,16 +223,16 @@
             act_grad = act_grad + product_nt(ext_ref[frame + k, side], wt_ref[k])
         pgs.append((act_grad * slope_ref[0, side]).astype(jnp.bfloat16))
         pg_ref[0, side] = pgs[side]
-    low = jnp.concatenate([up_ref[0], low_ref[0], down_ref[0]], axis=0)
+    low = tall(place_ref, low_ref, inner_ref, outer_ref)
     act = act_ref[0].reshape(4 * count, -1)
     cots = [ext_ref[frame + k].reshape(4 * count, chan) for k in range(3)]
     add_sums(low, act, jnp.concatenate(pgs, axis=0), cots, out_ref)
 
 
-def half_kernel(_, low_ref, up_ref, down_ref, act_ref, pg_ref, ext_ref, __, out_ref):
+def half_kernel(place_ref, low_ref, inner_ref, outer_ref, act_ref, pg_ref, ext_ref, out_ref):
     frame = pl.program_id(0)
     _, _, count, chan = pg_ref.shape
-    low = jnp.concatenate([up_ref[0], low_ref[0], down_ref[0]], axis=0)
+    low = tall(place_ref, low_ref, inner_ref, outer_ref)
     act = act_ref[0].reshape(4 * count, -1)
     cots = [ext_ref[frame + k].reshape(4 * count, chan) for k in range(3)]
     add_sums(low, act, pg_ref[0].reshape(4 * count, chan), cots, out_ref)
@@ -246,22 +266,67 @@
     return pl.CostEstimate(flops=units * 2 * 2048 * 256 * 256, bytes_accessed=mib * 2**20, transcendentals=0)
 
 
-def forward(low, up, down, cot, ws):
+def in_hbm(array):
+    return pltpu.with_memory_space_constraint(array, pltpu.HBM)
+
+
+def forward(place, low, inner, outer, cot, ws):
     frames, rows_low, cols_low, chan = low.shape
     side = (frames, 4, rows_low * cols_low, chan)
     return pl.pallas_call(
         forward_kernel,
         grid=(frames,),
-        in_specs=[each(low.shape), each(up.shape), each(down.shape), each(cot.shape), whole(ws.shape)],
+        in_specs=[SCALAR, each(low.shape), each(inner.shape), each(outer.shape), each(cot.shape), whole(ws.shape)],
         out_specs=[each(side)] * 3,
         out_shape=[like(side, jnp.bfloat16), like(side, jnp.float32), like(side, jnp.bfloat16)],
         compiler_params=grant(20),
         cost_estimate=cost(10, 8),
         name="forward",
-    )(low, up, down, cot, ws)
-
-
-def backward(side, parts, low, up, down, act, slope, cot, later, wt):
+    )(place, in_hbm(low), inner, outer, in_hbm(cot), in_hbm(ws))
+
+
+def edges_kernel(place_ref, low_ref, inner_ref, outer_ref, pg_ref, _, tall_ref, pg_inner, pg_outer):
+    cols_low = low_ref.shape[2]
+    first = low_ref.shape[0] - tall_ref.shape[0]
+    for n in range(tall_ref.shape[0]):
+        at = pl.ds(first + n, 1)
+        tall_ref[n] = tall(place_ref, low_ref.at[at], inner_ref.at[at], outer_ref.at[at])
+    odd = place_ref[1] == 1
+    top, bottom = pg_ref[:, :2, :cols_low, :], pg_ref[:, 2:, -cols_low:, :]
+    pg_inner[...] = jnp.where(odd, top, bottom)
+    pg_outer[...] = jnp.where(odd, bottom, top)
+
+
+def edges(place, low, inner, outer, pg, before):
+    frames, rows_low, cols_low, chan = low.shape
+    full = pl.BlockSpec(memory_space=pltpu.VMEM)
+    rows = like((frames, 2, cols_low, chan), jnp.bfloat16)
+    return pl.pallas_call(
+        edges_kernel,
+        in_specs=[SCALAR, full, full, full, full, UNREAD],
+        out_specs=[full] * 3,
+        out_shape=[like((2, rows_low + 2, cols_low, chan), jnp.bfloat16), rows, rows],
+        compiler_params=grant(8),
+        name="edges",
+    )(place, low, inner, outer, pg, before)
+
+
+def earlier_act(low, ws):
+    frames, rows_tall, cols_low, chan = low.shape
+    side = (frames, 4, (rows_tall - 2) * cols_low, chan)
+    return pl.pallas_call(
+        act_kernel,
+        grid=(frames,),
+        in_specs=[each(low.shape), whole(ws.shape)],
+        out_specs=each(side),
+        out_shape=like(side, jnp.bfloat16),
+        compiler_params=grant(16),
+        cost_estimate=cost(4, 3),
+        name="earlier_act",
+    )(low, ws)
+
+
+def backward(place, parts, low, inner, outer, act, slope, cot, later, wt):
     frames, _, count, chan = act.shape
     ext = (frames + 2,) + act.shape[1:]
     piece = (parts, 12 * (chan // (2 * parts)), chan)
@@ -270,7 +335,7 @@
         grid_spec=pltpu.PrefetchScalarGridSpec(
             num_scalar_prefetch=1,
             grid=(frames,),
-            in_specs=[half_of(low.shape), half_of(up.shape), half_of(down.shape), half_of(act.shape),
+            in_specs=[half_of(low.shape), half_of(inner.shape), half_of(outer.shape), half_of(act.shape),
                       each(slope.shape), whole(cot.shape), whole(later.shape), whole(wt.shape)],
             out_specs=[each(act.shape), whole(ext), whole(piece)],
         ),
@@ -278,10 +343,10 @@
         compiler_params=grant(28),
         cost_estimate=cost(15, 10),
         name="backward",
-    )(side, low, up, down, act, slope, cot, later, wt)
-
-
-def half_grads(side, parts, low, up, down, act, pg, ext, before):
+    )(place, low, inner, outer, act, slope, cot, later, in_hbm(wt))
+
+
+def half_grads(place, parts, low, inner, outer, act, pg, ext):
     frames, _, _, chan = act.shape
     piece = (parts, 12 * (chan // (2 * parts)), chan)
     return pl.pallas_call(
@@ -289,15 +354,15 @@
         grid_spec=pltpu.PrefetchScalarGridSpec(
             num_scalar_prefetch=1,
             grid=(frames,),
-            in_specs=[half_of(low.shape), half_of(up.shape), half_of(down.shape), half_of(act.shape),
-                      each(pg.shape), whole(ext.shape), UNREAD],
+            in_specs=[half_of(low.shape), half_of(inner.shape), half_of(outer.shape), half_of(act.shape),
+                      each(pg.shape), whole(ext.shape)],
             out_specs=whole(piece),
         ),
         out_shape=like(piece, jnp.float32),
         compiler_params=grant(24),
         cost_estimate=cost(10, 6),
         name="half_grads",
-    )(side, low, up, down, act, pg, ext, before)
+    )(place, low, inner, outer, act, pg, ext)
 
 
 def section_kernel(act_ref, low_ref, wt_ref, _, out_ref, token_ref):
@@ -335,21 +400,24 @@
     )(act_ext, low, wt, before)
 
 
-def input_kernel(pg_ref, up_ref, down_ref, cot_ref, ws_ref, _, out_ref, token_ref):
+def input_kernel(place_ref, pg_ref, inner_ref, outer_ref, cot_ref, ws_ref, _, out_ref, token_ref):
     token_ref[...] = jnp.zeros_like(token_ref)
     _, rows_low, cols_low, chan = out_ref.shape
     group = rows_at_once(rows_low, cols_low)
     span = group * cols_low
-    place = box(group, cols_low)
+    boxes = box(group, cols_low)
     count = rows_low * cols_low
     total = jnp.concatenate(
-        [product(place, cot_ref[0, 2 * group * n : 2 * group * (n + 1)].reshape(4 * span, chan))
+        [product(boxes, cot_ref[0, 2 * group * n : 2 * group * (n + 1)].reshape(4 * span, chan))
          for n in range(rows_low // group)], axis=0)
-    tall = (rows_low + 1, cols_low, chan)
-    at = column(tall[0] * cols_low, cols_low, chan)
+    higher = (rows_low + 1, cols_low, chan)
+    at = column(higher[0] * cols_low, cols_low, chan)
     own = [pg_ref[0, side].astype(jnp.float32) for side in range(4)]
-    above = [up_ref[0, b].astype(jnp.float32) for b in range(2)]
-    below = [down_ref[0, b].astype(jnp.float32) for b in range(2)]
+    odd_place = place_ref[1] == 1
+    inner = [inner_ref[0, b].astype(jnp.float32) for b in range(2)]
+    outer = [outer_ref[0, b].astype(jnp.float32) for b in range(2)]
+    above = [jnp.where(odd_place, inner[b], outer[b]) for b in range(2)]
+    below = [jnp.where(odd_place, outer[b], inner[b]) for b in range(2)]
     even = [jnp.concatenate([own[b], below[b]], axis=0) for b in range(2)]
     odd = [jnp.concatenate([above[b], own[2 + b]], axis=0) for b in range(2)]
     for j in range(3):
@@ -361,7 +429,7 @@
                 value = first + second
             else:
                 value = first + from_left(second, at)
-            pair.append(value.reshape(tall))
+            pair.append(value.reshape(higher))
         top, low = pair
         for i, value in enumerate((low[1:] + top[1:], top[:-1] + low[1:], low[:-1] + top[:-1])):
             value = value.reshape(count, chan)
@@ -371,25 +439,25 @@
     out_ref[0] = total.astype(jnp.bfloat16).reshape(rows_low, cols_low, chan)
 
 
-def input_grads(pg, up, down, cot, ws, before, low_shape):
+def input_grads(place, pg, inner, outer, cot, ws, before, low_shape):
     chan = low_shape[-1]
     return pl.pallas_call(
         input_kernel,
         grid=(low_shape[0],),
-        in_specs=[each(pg.shape), each(up.shape), each(down.shape), each(cot.shape), whole(ws.shape), UNREAD],
+        in_specs=[SCALAR, each(pg.shape), each(inner.shape), each(outer.shape), each(cot.shape), whole(ws.shape), UNREAD],
         out_specs=[each(low_shape), whole(TOKEN.shape)],
         out_shape=[like(low_shape, jnp.bfloat16), TOKEN],
         compiler_params=grant(20),
         cost_estimate=pl.CostEstimate(flops=2 * 2048 * chan * chan * 6, bytes_accessed=4 * 2**20, transcendentals=0),
         name="input_grads",
-    )(pg, up, down, cot, ws, before)
-
-
-def place_kernel(core_ref, half_ref, theirs_ref, spatial_ref, temporal_ref):
+    )(place, pg, inner, outer, cot, ws, before)
+
+
+def place_kernel(place_ref, half_ref, theirs_ref, _, spatial_ref, temporal_ref):
     parts, rows, chan = half_ref.shape
     size = rows // 12
     half = chan // 2
-    core = core_ref[0]
+    core = place_ref[0]
     for source, start in ((half_ref, core * half), (theirs_ref, half - core * half)):
         for n in range(parts):
             begin = pl.multiple_of(start + n * size, size)
@@ -401,17 +469,17 @@
                     temporal_ref[tap - 9, pl.ds(begin, size), :] = value
 
 
-def place(core, half, theirs, chan):
+def put(place, half, theirs, chan, before):
     full = pl.BlockSpec(memory_space=pltpu.VMEM)
     return pl.pallas_call(
         place_kernel,
-        in_specs=[SCALAR, full, full],
+        in_specs=[SCALAR, full, full, UNREAD],
         out_specs=[full, full],
         out_shape=[jax.ShapeDtypeStruct((3, 3, chan, chan), jnp.float32),
                    jax.ShapeDtypeStruct((3, chan, chan), jnp.float32)],
         compiler_params=grant(10),
         name="place",
-    )(core, half, theirs)
+    )(place, half, theirs, before)
 
 
 def add_kernel(mine_ref, theirs_ref, out_ref):
@@ -430,49 +498,75 @@
     )(mine, theirs)
 
 
-def sum_kernel(got_ref, *refs):
+def sum_kernel(got_ref, _, out_ref):
     total = got_ref[0].astype(jnp.float32)
     for n in range(1, got_ref.shape[0]):
         total = total + got_ref[n].astype(jnp.float32)
-    refs[-1][...] = total.astype(jnp.bfloat16)
-
-
-def sum_parts(got, *before):
+    out_ref[...] = total.astype(jnp.bfloat16)
+
+
+def sum_parts(got, before):
     full = pl.BlockSpec(memory_space=pltpu.VMEM)
     return pl.pallas_call(
         sum_kernel,
-        in_specs=[full] + [UNREAD] * len(before),
+        in_specs=[full, UNREAD],
         out_specs=full,
         out_shape=like(got.shape[1:], jnp.bfloat16),
         compiler_params=grant(4),
         name="sum_parts",
-    )(got, *before)
+    )(got, before)
+
+
+def spread_kernel(own_ref, theirs_ref, *refs):
+    total = (own_ref[...].astype(jnp.float32) + theirs_ref[...].astype(jnp.float32)).astype(jnp.bfloat16)
+    for n in range(refs[-1].shape[0]):
+        refs[-1][n] = total
+
+
+def spread(own, theirs, parts, *before):
+    full = pl.BlockSpec(memory_space=pltpu.VMEM)
+    return pl.pallas_call(
+        spread_kernel,
+        in_specs=[full, full] + [UNREAD] * len(before),
+        out_specs=full,
+        out_shape=like((parts,) + own.shape, jnp.bfloat16),
+        compiler_params=grant(4),
+        name="spread",
+    )(own, theirs, *before)
 
 
 def on_device(bits, low_frames, spatial_weight, temporal_weight, cotangent):
     low, cot = low_frames[0], cotangent[0]
     frames, rows_low, cols_low, chan = low.shape
-    core = lax.axis_index(bits.core).astype(jnp.int32).reshape(1)
-    up = bits.shift(low[:, -1:], "height", 1)
-    down = bits.shift(low[:, :1], "height", -1)
+    core = lax.axis_index(bits.core).astype(jnp.int32)
+    odd = lax.axis_index(bits.axes["height"][-1]).astype(jnp.int32)
+    mine, other = jnp.stack([core, odd]), jnp.stack([1 - core, odd])
+    parts = 1 << len(bits.near)
+
     later = bits.shift(cot[:2], "tm", -1)
-    parts = 1 << len(bits.near)
-    act, slope, cot_side = forward(low, up, down, cot, spatial_weight)
-    earlier = bits.shift(act[frames - 2 :], "tm", 1)
-    pg, ext, other = backward(
-        1 - core, parts, low, up, down, act, slope, cot_side, later, temporal_weight
+    inner, outer = bits.rows(low[:, :1], low[:, -1:])
+    act, slope, cot_side = forward(mine, low, inner, outer, cot, spatial_weight)
+    pg, ext, theirs = backward(
+        other, parts, low, inner, outer, act, slope, cot_side, later, temporal_weight
     )
-    theirs = bits.swap(other, bits.core)
-    mine = half_grads(core, parts, low, up, down, act, pg, ext, earlier)
-    kept = add_halves(mine, theirs)
+    theirs = bits.swap(theirs, bits.core)
+    own = half_grads(mine, parts, low, inner, outer, act, pg, ext)
+    kept = add_halves(own, theirs)
     got = bits.exchange(kept)
-    section_out, section_done = section(jnp.concatenate([earlier, act], axis=0), low, temporal_weight, kept)
-    above = bits.shift(pg[:, 2:, -cols_low:], "height", 1)
-    below = bits.shift(pg[:, :2, :cols_low], "height", -1)
-    input_grad, input_done = input_grads(pg, above, below, cot, spatial_weight, kept, low.shape)
-    total = sum_parts(got, section_done, input_done)
-    half, theirs = bits.gather(total, got.shape[0])
-    spatial_grad, temporal_grad = place(core, half, theirs, chan)
+
+    edge, pg_inner, pg_outer = edges(mine, low, inner, outer, pg, kept)
+    earlier = earlier_act(bits.shift(edge, "tm", 1), spatial_weight)
+    pg_inner, pg_outer = bits.pairs(pg_inner, pg_outer)
+
+    total, far = bits.far_sums(sum_parts(got, earlier))
+    section_out, section_done = section(jnp.concatenate([earlier, act], axis=0), low, temporal_weight, total)
+    totals = spread(total, far, parts, section_done, pg_inner, pg_outer)
+    input_grad, input_done = input_grads(
+        mine, pg, pg_inner, pg_outer, cot, spatial_weight, totals, low.shape
+    )
+    half = bits.exchange(totals)
+    theirs = bits.swap(half, bits.core)
+    spatial_grad, temporal_grad = put(mine, half, theirs, chan, input_done)
     return section_out[None], input_grad[None], spatial_grad, temporal_grad
 
 

time: 87.4 us -> 79.9 us (0.914)
  starting transfers between devices: 31.9 us -> 18.4 us
  Pallas kernels: 22.5 us -> 29.9 us
  local copies, waits for them, and re-layouts: 5.55 us -> 2.11 us
  blocking collectives: 13.5 us -> 15.2 us
  other arithmetic: 0.16 us -> 1.11 us
    ppermute x6 -> x2, starting transfers between devices: 16.2 us -> 3.4 us  [shift(): return lax.ppermute(block, axes, route)]
    all_to_all x1, starting transfers between devices: 12.6 us -> 5.17 us  [exchange(): return lax.all_to_all(parts, tuple(self.near), 0, 0, tiled=True)]
    all_to_all x1, waiting for transfers between devices: 0.01 us -> 6.77 us  [exchange(): return lax.all_to_all(parts, tuple(self.near), 0, 0, tiled=True)]
    ppermute x6 -> x2, waiting for transfers between devices: 6.57 us -> 0.01 us  [shift(): return lax.ppermute(block, axes, route)]
    ppermute x3 -> x5, starting transfers between devices: 3.07 us -> 8.41 us  [swap(): return lax.ppermute(block, axis, [(0, 1), (1, 0)])]
    pallas_call x4 -> x7, Pallas kernels: 9.13 us -> 14.4 us  [the longest x1 5.16 us: input_grads(): pl.pallas_call(input_kernel, grid=(low_shape[0],), in_specs=[SCALAR, each...]
    unnamed x18, local copies, waits for them, and re-layouts: 3.48 us -> 1.03 us
    all_to_all x1, blocking collectives: 13.5 us -> 15.2 us  [exchange(): return lax.all_to_all(parts, tuple(self.near), 0, 0, tiled=True)]
  transfers between devices with their start and end apart: 10 -> 10, of which waited for: 6 -> 3; matrix products, arithmetic and copies ran while one was open for 1% -> 1% of each run, Pallas kernels for 16% -> 24%
where the time goes in v2:
time: 79.9 us; the launch traced here: 79.3 us
  Pallas kernels  29.9 us (37%)
  starting transfers between devices  18.4 us (23%)
  blocking collectives  15.2 us (19%)
  waiting for transfers between devices  11.8 us (15%)
  local copies, waits for them, and re-layouts  2.11 us (3%)
  other arithmetic  1.11 us (1%)
  between operations  0.82 us (1%)
    all_to_all x1, blocking collectives, exchange(): return lax.all_to_all(parts, tuple(self.near), 0, 0, tiled=True)  15.2 us
    ppermute x5, starting transfers between devices, swap(): return lax.ppermute(block, axis, [(0, 1), (1, 0)])  8.41 us
    pallas_call x1, Pallas kernels, backward(): pl.pallas_call(backward_kernel, grid_spec=pltpu.PrefetchScalarGridSpec(nu...  7.45 us
    all_to_all x1, waiting for transfers between devices, exchange(): return lax.all_to_all(parts, tuple(self.near), 0, 0, tiled=True)  6.77 us
    all_to_all x1, starting transfers between devices, exchange(): return lax.all_to_all(parts, tuple(self.near), 0, 0, tiled=True)  5.17 us
    pallas_call x1, Pallas kernels, input_grads(): pl.pallas_call(input_kernel, grid=(low_shape[0],), in_specs=[SCALAR, each...  5.16 us
    ppermute x5, waiting for transfers between devices, swap(): return lax.ppermute(block, axis, [(0, 1), (1, 0)])  5.03 us
    pallas_call x1, Pallas kernels, forward(): pl.pallas_call(forward_kernel, grid=(frames,), in_specs=[SCALAR, each(low...  4.42 us
  transfers between devices with their start and end apart: 10, of which 3 were waited for; matrix products, arithmetic and copies ran while one was open for 1% of the time, Pallas kernels for 24%

profile of v2, /device:TPU:0, one launch (start us, length us, event | category | flops | bytes accessed | tf_op | source)
XLA Modules:
  0.0 79.3 jit_solution(4156515810037103467)
XLA Ops:
  0.6 1.1 %slice_bitcast_fusion = bf16[2,8,64,256]{3,2,1,0:T(8,128)(2,1)S(1)} fusion(bf16[1,4,8,64,256]{4,3,2,1,0:T(8,128)(2,1)} %param.7), kind=kLoop, calls=%fused_computation.1 | loop fusion | bytes 1048576 | tf_op jit(solution)/shard_map/slice | solution.py:546
  1.7 1.3 %collective-permute-start.2 = (bf16[2,8,64,256]{3,2,1,0:T(8,128)(2,1)S(1)}, bf16[2,8,64,256]{3,2,1,0:T(8,128)(2,1)S(1)}, u32[]{:S(2)}, u32[]{:S(2)}) collective-permute-start(bf16[2,8,64,256]{3,2,1,0:T(8,128)(2,1)S(1)} %slice_bitcast_fusion), channel_id=1, source_target_pairs={{4,0},{8,4},{12,8},{5,1},{9,5},{13,9},{6,2},{10,6},{14,10},{7,3},{... | collective-permute-start | bytes 1572872 | tf_op jit(solution)/shard_map/ppermute | solution.py:39
  3.0 0.9 %broadcast_select_fusion = (bf16[4,1,32,256]{3,2,1,0:T(8,128)(2,1)S(1)}, bf16[4,1,32,256]{3,2,1,0:T(8,128)(2,1)S(1)}) fusion(pred[]{:T(512)S(6)} %eq.3, bf16[4,4,32,256]{3,2,1,0:T(8,128)(2,1)} %bitcast.9), kind=kLoop, calls=%fused_computation.2 | loop fusion | flops 65536 | bytes 262145 | tf_op jit(solution)/shard_map/jit(_where)/select_n | solution.py:46
  3.9 0.7 collective-permute-start.1
  4.6 5.9 %collective-permute-start = (bf16[4,1,32,256]{3,2,1,0:T(8,128)(2,1)S(1)}, bf16[4,1,32,256]{3,2,1,0:T(8,128)(2,1)S(1)}, u32[]{:S(2)}, u32[]{:S(2)}) collective-permute-start(bf16[4,1,32,256]{3,2,1,0:T(8,128)(2,1)S(1)} %get-tuple-element.35), channel_id=1, source_target_pairs={{0,1},{1,0},{2,3},{3,2},{4,5},{5,4},{6,7},{7,6},{8,9},{9,8},{10,11... | collective-permute-start | bytes 196616 | tf_op jit(solution)/shard_map/ppermute | solution.py:33
  10.5 0.1 pad_add_fusion
  10.6 0.0 collective-permute-done.1.outer_ref
  10.6 2.7 %collective-permute-done.inner_ref = bf16[4,1,32,256]{3,2,1,0:T(8,128)(2,1)S(1)} collective-permute-done((bf16[4,1,32,256]{3,2,1,0:T(8,128)(2,1)S(1)}, bf16[4,1,32,256]{3,2,1,0:T(8,128)(2,1)S(1)}, u32[]{:S(2)}, u32[]{:S(2)}) %collective-permute-start) | collective-permute-done | bytes 65568 | tf_op jit(solution)/shard_map/ppermute | solution.py:33
  13.3 4.4 %forward.1 = (bf16[4,4,128,256]{3,2,1,0:T(8,128)(2,1)S(1)}, f32[4,4,128,256]{3,2,1,0:T(8,128)S(1)}, bf16[4,4,128,256]{3,2,1,0:T(8,128)(2,1)S(1)}) custom-call(s32[2]{0:T(128)S(1)} %get-tuple-element.36.place_ref, bf16[4,4,32,256]{3,2,1,0:T(8,128)(2,1)} %bitcast.10, bf16[4,1,32,256]{3,2,1,0:T(8,128)(2,1)S(1)} %collective-permute-done.inner_ref, ...), custom_call_target="tpu_custom_call" | custom-call | flops 2684354560 | bytes 8388608 | tf_op jit(solution)/shard_map/forward/pallas_call | solution.py:276
  17.7 0.0 copy-start
  17.7 0.0 collective-permute-done.2.later_ref
  17.7 0.0 copy-done.4
  17.7 7.5 %backward.1 = (bf16[4,4,128,256]{3,2,1,0:T(8,128)(2,1)S(1)}, bf16[6,4,128,256]{3,2,1,0:T(8,128)(2,1)S(1)}, f32[8,192,256]{2,1,0:T(8,128)S(1)}) custom-call(s32[2]{0:T(128)S(1)} %get-tuple-element.37.place_ref, bf16[4,4,32,256]{3,2,1,0:T(8,128)(2,1)S(1)} %bitcast.11, bf16[4,1,32,256]{3,2,1,0:T(8,128)(2,1)S(1)} %collective-permute-done.inner_ref, ...), custom_call_target="tpu_custom_call" | custom-call | flops 4026531840 | bytes 10485760 | tf_op jit(solution)/shard_map/backward/pallas_call | solution.py:333
  25.2 0.0 copy-start.2
  25.2 0.2 collective-permute-start.3
  25.4 0.0 copy-done
  25.4 3.8 %half_grads.1.mine_ref = f32[8,192,256]{2,1,0:T(8,128)S(1)} custom-call(s32[2]{0:T(128)S(1)} %get-tuple-element.36.place_ref, bf16[4,4,32,256]{3,2,1,0:T(8,128)(2,1)S(1)} %bitcast.12, bf16[4,1,32,256]{3,2,1,0:T(8,128)(2,1)S(1)} %collective-permute-done.inner_ref, bf16[4,1,32,256]{3,2,1,0:T(8,128)(2,1)S(1)} %collective-permute-done.1.outer_ref, ...), custom_call_target="tpu_custom_call" | custom-call | flops 2684354560 | bytes 6291456 | tf_op jit(solution)/shard_map/half_grads/pallas_call | solution.py:352
  29.2 0.0 collective-permute-done.3.theirs_ref
  29.2 1.0 %add_halves.1._ = bf16[8,192,256]{2,1,0:T(8,128)(2,1)} custom-call(f32[8,192,256]{2,1,0:T(8,128)S(1)} %half_grads.1.mine_ref, f32[8,192,256]{2,1,0:T(8,128)S(1)} %collective-permute-done.3.theirs_ref), custom_call_target="tpu_custom_call" | custom-call | tf_op jit(solution)/shard_map/add_halves/pallas_call | solution.py:491
  30.2 5.2 %all-to-all-start = ((bf16[8,192,256]{2,1,0:T(8,128)(2,1)}), bf16[8,192,256]{2,1,0:T(8,128)(2,1)S(1)}, u32[]{:S(2)}, u32[]{:S(2)}) async-start(bf16[8,192,256]{2,1,0:T(8,128)(2,1)} %add_halves.1._), calls=%async_computation | async-start | bytes 1572864 | tf_op jit(solution)/shard_map/all_to_all | solution.py:42
  35.4 0.0 copy-done.2
  35.4 0.0 copy-start.6
  35.4 1.2 %edges.1 = (bf16[2,6,32,256]{3,2,1,0:T(8,128)(2,1)S(1)}, bf16[4,2,32,256]{3,2,1,0:T(8,128)(2,1)}, bf16[4,2,32,256]{3,2,1,0:T(8,128)(2,1)S(1)}) custom-call(s32[2]{0:T(128)S(1)} %get-tuple-element.36.place_ref, bf16[4,4,32,256]{3,2,1,0:T(8,128)(2,1)S(1)} %bitcast.13, bf16[4,1,32,256]{3,2,1,0:T(8,128)(2,1)S(1)} %collective-permute-done.inner_ref, ...), custom_call_target="tpu_custom_call" | custom-call | tf_op jit(solution)/shard_map/edges/pallas_call | solution.py:304
  36.6 2.1 %collective-permute-start.4 = (bf16[2,6,32,256]{3,2,1,0:T(8,128)(2,1)S(1)}, bf16[2,6,32,256]{3,2,1,0:T(8,128)(2,1)S(1)}, u32[]{:S(2)}, u32[]{:S(2)}) collective-permute-start(bf16[2,6,32,256]{3,2,1,0:T(8,128)(2,1)S(1)} %get-tuple-element.25), channel_id=1, source_target_pairs={{0,4},{4,8},{8,12},{1,5},{5,9},{9,13},{2,6},{6,10},{10,14},{3,7},{... | collective-permute-start | bytes 589832 | tf_op jit(solution)/shard_map/ppermute | solution.py:39
  38.8 1.8 %collective-permute-start.5 = (bf16[4,2,32,256]{3,2,1,0:T(8,128)(2,1)}, bf16[4,2,32,256]{3,2,1,0:T(8,128)(2,1)S(1)}, u32[]{:S(2)}, u32[]{:S(2)}) collective-permute-start(bf16[4,2,32,256]{3,2,1,0:T(8,128)(2,1)} %get-tuple-element.27), channel_id=1, source_target_pairs={{0,1},{1,0},{2,3},{3,2},{4,5},{5,4},{6,7},{7,6},{8,9},{9,8},{10,11... | collective-permute-start | bytes 393224 | tf_op jit(solution)/shard_map/ppermute | solution.py:33
  40.6 0.8 collective-permute-start.6
  41.4 0.0 collective-permute-done.4.low_ref
  41.4 0.0 copy-done.6
  41.4 1.0 %earlier_act.1._ = bf16[2,4,128,256]{3,2,1,0:T(8,128)(2,1)S(1)} custom-call(bf16[2,6,32,256]{3,2,1,0:T(8,128)(2,1)S(1)} %collective-permute-done.4.low_ref, bf16[3,3,256,256]{3,2,1,0:T(8,128)(2,1)S(1)} %copy-done.6), custom_call_target="tpu_custom_call" | custom-call | flops 1073741824 | bytes 3145728 | tf_op jit(solution)/shard_map/earlier_act/pallas_call | solution.py:317
  42.4 0.0 copy-done.1
  42.4 0.1 pad_maximum_fusion.act_ref
  42.6 6.8 %all-to-all-done.got_ref = bf16[8,192,256]{2,1,0:T(8,128)(2,1)S(1)} async-done(((bf16[8,192,256]{2,1,0:T(8,128)(2,1)}), bf16[8,192,256]{2,1,0:T(8,128)(2,1)S(1)}, u32[]{:S(2)}, u32[]{:S(2)}) %all-to-all-start) | async-done | bytes 786464 | tf_op jit(solution)/shard_map/all_to_all | solution.py:42
  49.4 0.1 sum_parts.1._.own_ref
  49.5 0.5 collective-permute-start.7
  50.0 1.0 %copy-done.8 = bf16[3,256,256]{2,1,0:T(8,128)(2,1)S(1)} copy-done((bf16[3,256,256]{2,1,0:T(8,128)(2,1)S(1)}, bf16[3,256,256]{2,1,0:T(8,128)(2,1)}, u32[]{:S(2)}) %copy-start.8) | copy-done | bytes 393240
  51.0 3.2 %section.1 = (bf16[4,8,64,256]{3,2,1,0:T(8,128)(2,1)}, f32[8,128]{1,0:T(8,128)S(1)}) custom-call(bf16[6,4,128,256]{3,2,1,0:T(8,128)(2,1)S(1)} %pad_maximum_fusion.act_ref, bf16[4,4,32,256]{3,2,1,0:T(8,128)(2,1)S(1)} %bitcast.14, bf16[3,256,256]{2,1,0:T(8,128)(2,1)S(1)} %copy-done.8, bf16[192,256]{1,0:T(8,128)(2,1)S(1)} %sum_parts.1._.own_ref), custom_call_target="tpu_custom_call" | custom-call | flops 1073741824 | bytes 3145728 | tf_op jit(solution)/shard_map/section/pallas_call | solution.py:391
  54.2 0.0 collective-permute-done.5.refs_1_.inner_ref
  54.2 0.0 collective-permute-done.6.refs_2_.outer_ref
  54.2 2.3 %collective-permute-done.7.theirs_ref = bf16[192,256]{1,0:T(8,128)(2,1)S(1)} collective-permute-done((bf16[192,256]{1,0:T(8,128)(2,1)S(1)}, bf16[192,256]{1,0:T(8,128)(2,1)S(1)}, u32[]{:S(2)}, u32[]{:S(2)}) %collective-permute-start.7) | collective-permute-done | bytes 98336 | tf_op jit(solution)/shard_map/ppermute | solution.py:33
  56.5 0.1 spread.1._
  56.5 15.2 %all_to_all.10.half_ref = bf16[8,192,256]{2,1,0:T(8,128)(2,1)S(1)} all-to-all(bf16[8,192,256]{2,1,0:T(8,128)(2,1)S(1)} %spread.1._), channel_id=1, replica_groups=mesh['dp0'=2,'tm1'=2,'tm0'=2,'height1'=2,'height0'=2] {'dp0','tm1','heig..., dimensions={0} | all-to-all | bytes 1572864 | tf_op jit(solution)/shard_map/all_to_all | solution.py:42
  71.7 0.0 collective-permute-start.8
  71.8 0.0 copy-done.7
  71.8 0.0 copy-done.3
  71.8 0.0 copy-done.5
  71.8 5.2 %input_grads.1 = (bf16[4,4,32,256]{3,2,1,0:T(8,128)(2,1)}, f32[8,128]{1,0:T(8,128)S(1)}) custom-call(s32[2]{0:T(128)S(1)} %get-tuple-element.36.place_ref, bf16[4,4,128,256]{3,2,1,0:T(8,128)(2,1)S(1)} %copy-done.3, bf16[4,2,32,256]{3,2,1,0:T(8,128)(2,1)S(1)} %collective-permute-done.5.refs_1_.inner_ref, ...), custom_call_target="tpu_custom_call" | custom-call | flops 1610612736 | bytes 4194304 | tf_op jit(solution)/shard_map/input_grads/pallas_call | solution.py:444
  76.9 0.0 collective-permute-done.8.theirs_ref
  76.9 2.4 %place.1 = (f32[3,3,256,256]{3,2,1,0:T(8,128)}, f32[3,256,256]{2,1,0:T(8,128)}) custom-call(s32[2]{0:T(128)S(1)} %get-tuple-element.36.place_ref, bf16[8,192,256]{2,1,0:T(8,128)(2,1)S(1)} %all_to_all.10.half_ref, bf16[8,192,256]{2,1,0:T(8,128)(2,1)S(1)} %collective-permute-done.8.theirs_ref, f32[8,128]{1,0:T(8,128)S(1)} %get-tuple-element.31._), custom_call_target="tpu_custom_call" | custom-call | tf_op jit(solution)/shard_map/place/pallas_call | solution.py:474
  (6 shorter events, 0.0 us)
Async XLA Ops:
  1.7 16.0 %collective-permute-start.2 = (bf16[2,8,64,256]{3,2,1,0:T(8,128)(2,1)S(1)}, bf16[2,8,64,256]{3,2,1,0:T(8,128)(2,1)S(1)}, u32[]{:S(2)}, u32[]{:S(2)}) collective-permute-start(bf16[2,8,64,256]{3,2,1,0:T(8,128)(2,1)S(1)} %slice_bitcast_fusion), channel_id=1, source_target_pairs={{4,0},{8,4},{12,8},{5,1},{9,5},{13,9},{6,2},{10,6},{14,10},{7,3},{... | collective-permute-start | bytes 1572872 | tf_op jit(solution)/shard_map/ppermute | solution.py:39
  3.9 6.7 %collective-permute-start.1 = (bf16[4,1,32,256]{3,2,1,0:T(8,128)(2,1)S(1)}, bf16[4,1,32,256]{3,2,1,0:T(8,128)(2,1)S(1)}, u32[]{:S(2)}, u32[]{:S(2)}) collective-permute-start(bf16[4,1,32,256]{3,2,1,0:T(8,128)(2,1)S(1)} %get-tuple-element.34), channel_id=1, source_target_pairs={{1,2},{2,1},{5,6},{6,5},{9,10},{10,9},{13,14},{14,13},{17,18},{18,... | collective-permute-start | bytes 196616 | tf_op jit(solution)/shard_map/ppermute | solution.py:52
  4.6 8.7 %collective-permute-start = (bf16[4,1,32,256]{3,2,1,0:T(8,128)(2,1)S(1)}, bf16[4,1,32,256]{3,2,1,0:T(8,128)(2,1)S(1)}, u32[]{:S(2)}, u32[]{:S(2)}) collective-permute-start(bf16[4,1,32,256]{3,2,1,0:T(8,128)(2,1)S(1)} %get-tuple-element.35), channel_id=1, source_target_pairs={{0,1},{1,0},{2,3},{3,2},{4,5},{5,4},{6,7},{7,6},{8,9},{9,8},{10,11... | collective-permute-start | bytes 196616 | tf_op jit(solution)/shard_map/ppermute | solution.py:33
  13.3 4.5 %copy-start.4 = (bf16[1,4,4,32,256]{4,3,2,1,0:T(8,128)(2,1)S(1)}, bf16[1,4,4,32,256]{4,3,2,1,0:T(8,128)(2,1)}, u32[]{:S(2)}) copy-start(bf16[1,4,4,32,256]{4,3,2,1,0:T(8,128)(2,1)} %param.4) | copy-start | bytes 786436
  17.7 7.7 %copy-start = (bf16[4,4,128,256]{3,2,1,0:T(8,128)(2,1)}, bf16[4,4,128,256]{3,2,1,0:T(8,128)(2,1)S(1)}, u32[]{:S(2)}) copy-start(bf16[4,4,128,256]{3,2,1,0:T(8,128)(2,1)S(1)} %get-tuple-element.19.act_ref) | copy-start | bytes 3145732
  25.2 10.2 %copy-start.2 = (bf16[4,4,128,256]{3,2,1,0:T(8,128)(2,1)}, bf16[4,4,128,256]{3,2,1,0:T(8,128)(2,1)S(1)}, u32[]{:S(2)}) copy-start(bf16[4,4,128,256]{3,2,1,0:T(8,128)(2,1)S(1)} %get-tuple-element.22.pg_ref) | copy-start | bytes 3145732
  25.2 4.0 %collective-permute-start.3 = (f32[8,192,256]{2,1,0:T(8,128)S(1)}, f32[8,192,256]{2,1,0:T(8,128)S(1)}, u32[]{:S(2)}, u32[]{:S(2)}) collective-permute-start(f32[8,192,256]{2,1,0:T(8,128)S(1)} %get-tuple-element.24), channel_id=1, source_target_pairs={{0,4},{4,0},{1,5},{5,1},{2,6},{6,2},{3,7},{7,3},{8,12},{12,8},{9,1... | collective-permute-start | bytes 4718600 | tf_op jit(solution)/shard_map/ppermute | solution.py:33
  30.2 19.1 %all-to-all-start = ((bf16[8,192,256]{2,1,0:T(8,128)(2,1)}), bf16[8,192,256]{2,1,0:T(8,128)(2,1)S(1)}, u32[]{:S(2)}, u32[]{:S(2)}) async-start(bf16[8,192,256]{2,1,0:T(8,128)(2,1)} %add_halves.1._), calls=%async_computation | async-start | bytes 1572864 | tf_op jit(solution)/shard_map/all_to_all | solution.py:42
  35.4 6.0 %copy-start.6 = (bf16[3,3,256,256]{3,2,1,0:T(8,128)(2,1)S(1)}, bf16[3,3,256,256]{3,2,1,0:T(8,128)(2,1)}, u32[]{:S(2)}) copy-start(bf16[3,3,256,256]{3,2,1,0:T(8,128)(2,1)} %ws_ref.5) | copy-start | bytes 3538948
  36.6 4.7 %collective-permute-start.4 = (bf16[2,6,32,256]{3,2,1,0:T(8,128)(2,1)S(1)}, bf16[2,6,32,256]{3,2,1,0:T(8,128)(2,1)S(1)}, u32[]{:S(2)}, u32[]{:S(2)}) collective-permute-start(bf16[2,6,32,256]{3,2,1,0:T(8,128)(2,1)S(1)} %get-tuple-element.25), channel_id=1, source_target_pairs={{0,4},{4,8},{8,12},{1,5},{5,9},{9,13},{2,6},{6,10},{10,14},{3,7},{... | collective-permute-start | bytes 589832 | tf_op jit(solution)/shard_map/ppermute | solution.py:39
  38.8 15.4 %collective-permute-start.5 = (bf16[4,2,32,256]{3,2,1,0:T(8,128)(2,1)}, bf16[4,2,32,256]{3,2,1,0:T(8,128)(2,1)S(1)}, u32[]{:S(2)}, u32[]{:S(2)}) collective-permute-start(bf16[4,2,32,256]{3,2,1,0:T(8,128)(2,1)} %get-tuple-element.27), channel_id=1, source_target_pairs={{0,1},{1,0},{2,3},{3,2},{4,5},{5,4},{6,7},{7,6},{8,9},{9,8},{10,11... | collective-permute-start | bytes 393224 | tf_op jit(solution)/shard_map/ppermute | solution.py:33
  40.6 1.9 %copy-start.1 = (bf16[4,4,128,256]{3,2,1,0:T(8,128)(2,1)S(1)}, bf16[4,4,128,256]{3,2,1,0:T(8,128)(2,1)}, u32[]{:S(2)}) copy-start(bf16[4,4,128,256]{3,2,1,0:T(8,128)(2,1)} %copy-done) | copy-start | bytes 3145732
  40.6 13.6 %collective-permute-start.6 = (bf16[4,2,32,256]{3,2,1,0:T(8,128)(2,1)S(1)}, bf16[4,2,32,256]{3,2,1,0:T(8,128)(2,1)S(1)}, u32[]{:S(2)}, u32[]{:S(2)}) collective-permute-start(bf16[4,2,32,256]{3,2,1,0:T(8,128)(2,1)S(1)} %get-tuple-element.28), channel_id=1, source_target_pairs={{1,2},{2,1},{5,6},{6,5},{9,10},{10,9},{13,14},{14,13},{17,18},{18,... | collective-permute-start | bytes 393224 | tf_op jit(solution)/shard_map/ppermute | solution.py:52
  49.5 7.0 %collective-permute-start.7 = (bf16[192,256]{1,0:T(8,128)(2,1)S(1)}, bf16[192,256]{1,0:T(8,128)(2,1)S(1)}, u32[]{:S(2)}, u32[]{:S(2)}) collective-permute-start(bf16[192,256]{1,0:T(8,128)(2,1)S(1)} %sum_parts.1._.own_ref), channel_id=1, source_target_pairs={{0,2},{2,0},{1,3},{3,1},{4,6},{6,4},{5,7},{7,5},{8,10},{10,8},{9,1... | collective-permute-start | bytes 294920 | tf_op jit(solution)/shard_map/ppermute | solution.py:33
  50.0 1.0 %copy-start.8 = (bf16[3,256,256]{2,1,0:T(8,128)(2,1)S(1)}, bf16[3,256,256]{2,1,0:T(8,128)(2,1)}, u32[]{:S(2)}) copy-start(bf16[3,256,256]{2,1,0:T(8,128)(2,1)} %wt_ref.3) | copy-start | bytes 1179652
  51.0 20.8 %copy-start.7 = (bf16[3,3,256,256]{3,2,1,0:T(8,128)(2,1)S(1)}, bf16[3,3,256,256]{3,2,1,0:T(8,128)(2,1)}, u32[]{:S(2)}) copy-start(bf16[3,3,256,256]{3,2,1,0:T(8,128)(2,1)} %ws_ref.5) | copy-start | bytes 3538948
  54.1 17.6 %copy-start.3 = (bf16[4,4,128,256]{3,2,1,0:T(8,128)(2,1)S(1)}, bf16[4,4,128,256]{3,2,1,0:T(8,128)(2,1)}, u32[]{:S(2)}) copy-start(bf16[4,4,128,256]{3,2,1,0:T(8,128)(2,1)} %copy-done.2) | copy-start | bytes 3145732
  54.2 17.6 %copy-start.5 = (bf16[1,4,8,64,256]{4,3,2,1,0:T(8,128)(2,1)S(1)}, bf16[1,4,8,64,256]{4,3,2,1,0:T(8,128)(2,1)}, u32[]{:S(2)}) copy-start(bf16[1,4,8,64,256]{4,3,2,1,0:T(8,128)(2,1)} %param.7) | copy-start | bytes 3145732
  71.7 5.2 %collective-permute-start.8 = (bf16[8,192,256]{2,1,0:T(8,128)(2,1)S(1)}, bf16[8,192,256]{2,1,0:T(8,128)(2,1)S(1)}, u32[]{:S(2)}, u32[]{:S(2)}) collective-permute-start(bf16[8,192,256]{2,1,0:T(8,128)(2,1)S(1)} %all_to_all.10.half_ref), channel_id=1, source_target_pairs={{0,4},{4,0},{1,5},{5,1},{2,6},{6,2},{3,7},{7,3},{8,12},{12,8},{9,1... | collective-permute-start | bytes 2359304 | tf_op jit(solution)/shard_map/ppermute | solution.py:33

commit v3 on v2

--- a/solution.py
+++ b/solution.py
@@ -41,15 +41,12 @@
     def exchange(self, parts):
         return lax.all_to_all(parts, tuple(self.near), 0, 0, tiled=True)
 
-    def rows(self, first, last):
-        odd = lax.axis_index(self.axes["height"][-1]) == 1
-        return self.pairs(jnp.where(odd, first, last), jnp.where(odd, last, first))
-
     def pairs(self, inner, outer):
         axes = self.axes["height"]
         low = range(1, (1 << len(axes)) - 1, 2)
         route = [(i, i + 1) for i in low] + [(i + 1, i) for i in low]
-        return self.swap(inner, axes[-1]), lax.ppermute(outer, axes, route)
+        outer = lax.ppermute(outer, axes, route)
+        return self.swap(inner, axes[-1]), outer
 
     def far_sums(self, total):
         for axis in self.far[:-1]:
@@ -149,16 +146,15 @@
         yield (first + second) + from_right(third, at, cols_low - 1)
 
 
-def forward_kernel(place_ref, low_ref, inner_ref, outer_ref, cot_ref, ws_ref, act_ref, slope_ref, cot_side):
+def forward_kernel(place_ref, low_ref, inner_ref, outer_ref, ws_ref, act_ref, slope_ref):
     low = tall(place_ref, low_ref, inner_ref, outer_ref)
     for side, pre in enumerate(spatial(low, ws_ref)):
         sig = jax.nn.sigmoid(pre)
         act_ref[0, side] = (pre * sig).astype(jnp.bfloat16)
         slope_ref[0, side] = sig * (1.0 + pre * (1.0 - sig))
-    sort_columns(cot_ref.at[0], cot_side.at[0], low.shape[1])
-
-
-def act_kernel(low_ref, ws_ref, act_ref):
+
+
+def act_kernel(low_ref, ws_ref, _, act_ref):
     for side, pre in enumerate(spatial(low_ref[0], ws_ref)):
         act_ref[0, side] = (pre * jax.nn.sigmoid(pre)).astype(jnp.bfloat16)
 
@@ -270,19 +266,93 @@
     return pltpu.with_memory_space_constraint(array, pltpu.HBM)
 
 
-def forward(place, low, inner, outer, cot, ws):
+FULL = pl.BlockSpec(memory_space=pltpu.VMEM)
+
+
+def first_kernel(place_ref, low_ref, cot_ref, inner_ref, outer_ref, later_ref, sems):
+    last = low_ref.shape[1] - 1
+    odd = place_ref[1]
+    copies = [
+        pltpu.make_async_copy(cot_ref.at[0:2], later_ref, sems.at[0]),
+        pltpu.make_async_copy(low_ref.at[:, pl.ds(last * (1 - odd), 1)], inner_ref, sems.at[1]),
+        pltpu.make_async_copy(low_ref.at[:, pl.ds(last * odd, 1)], outer_ref, sems.at[2]),
+    ]
+    for copy in copies:
+        copy.start()
+    for copy in copies:
+        copy.wait()
+
+
+def first_messages(place, low, cot):
+    row = like(low[:, :1].shape, low.dtype)
+    return pl.pallas_call(
+        first_kernel,
+        in_specs=[SCALAR, UNREAD, UNREAD],
+        out_specs=[FULL] * 3,
+        out_shape=[row, row, like(cot[:2].shape, cot.dtype)],
+        scratch_shapes=[pltpu.SemaphoreType.DMA((3,))],
+        compiler_params=grant(4),
+        name="first_messages",
+    )(place, in_hbm(low), in_hbm(cot))
+
+
+def load_kernel(low_hbm, cot_hbm, ws_hbm, wt_hbm, low_ref, ws_ref, wt_ref, side_ref, cot_ref, sems):
+    frames, cols_low = low_ref.shape[0], low_ref.shape[2]
+    copies = [pltpu.make_async_copy(cot_hbm.at[n], cot_ref.at[n], sems.at[n]) for n in range(frames)]
+    pairs = ((low_hbm, low_ref), (ws_hbm, ws_ref), (wt_hbm, wt_ref))
+    copies += [pltpu.make_async_copy(a, b, sems.at[frames + n]) for n, (a, b) in enumerate(pairs)]
+    for copy in copies:
+        copy.start()
+    for n in range(frames):
+        copies[n].wait()
+        sort_columns(cot_ref.at[n], side_ref.at[n], cols_low)
+    for copy in copies[frames:]:
+        copy.wait()
+
+
+def load(low, cot, ws, wt):
+    frames, rows_low, cols_low, chan = low.shape
+    return pl.pallas_call(
+        load_kernel,
+        in_specs=[UNREAD] * 4,
+        out_specs=[FULL] * 4,
+        out_shape=[like(low.shape, low.dtype), like(ws.shape, ws.dtype), like(wt.shape, wt.dtype),
+                   like((frames, 4, rows_low * cols_low, chan), jnp.bfloat16)],
+        scratch_shapes=[pltpu.VMEM(cot.shape, cot.dtype), pltpu.SemaphoreType.DMA((frames + 3,))],
+        compiler_params=grant(12),
+        cost_estimate=cost(2, 4),
+        name="load",
+    )(in_hbm(low), in_hbm(cot), in_hbm(ws), in_hbm(wt))
+
+
+def nothing(*_):
+    pass
+
+
+def after(arrays, *before):
+    return pl.pallas_call(
+        nothing,
+        in_specs=[UNREAD] * (len(arrays) + len(before)),
+        out_specs=[UNREAD] * len(arrays),
+        out_shape=[like(a.shape, a.dtype) for a in arrays],
+        input_output_aliases={n: n for n in range(len(arrays))},
+        name="after",
+    )(*arrays, *before)
+
+
+def forward(place, low, inner, outer, ws):
     frames, rows_low, cols_low, chan = low.shape
     side = (frames, 4, rows_low * cols_low, chan)
     return pl.pallas_call(
         forward_kernel,
         grid=(frames,),
-        in_specs=[SCALAR, each(low.shape), each(inner.shape), each(outer.shape), each(cot.shape), whole(ws.shape)],
-        out_specs=[each(side)] * 3,
-        out_shape=[like(side, jnp.bfloat16), like(side, jnp.float32), like(side, jnp.bfloat16)],
+        in_specs=[SCALAR, each(low.shape), each(inner.shape), each(outer.shape), whole(ws.shape)],
+        out_specs=[each(side)] * 2,
+        out_shape=[like(side, jnp.bfloat16), like(side, jnp.float32)],
         compiler_params=grant(20),
         cost_estimate=cost(10, 8),
         name="forward",
-    )(place, in_hbm(low), inner, outer, in_hbm(cot), in_hbm(ws))
+    )(place, low, inner, outer, ws)
 
 
 def edges_kernel(place_ref, low_ref, inner_ref, outer_ref, pg_ref, _, tall_ref, pg_inner, pg_outer):
@@ -311,19 +381,19 @@
     )(place, low, inner, outer, pg, before)
 
 
-def earlier_act(low, ws):
+def earlier_act(low, ws, before):
     frames, rows_tall, cols_low, chan = low.shape
     side = (frames, 4, (rows_tall - 2) * cols_low, chan)
     return pl.pallas_call(
         act_kernel,
         grid=(frames,),
-        in_specs=[each(low.shape), whole(ws.shape)],
+        in_specs=[each(low.shape), whole(ws.shape), UNREAD],
         out_specs=each(side),
         out_shape=like(side, jnp.bfloat16),
         compiler_params=grant(16),
         cost_estimate=cost(4, 3),
         name="earlier_act",
-    )(low, ws)
+    )(low, ws, before)
 
 
 def backward(place, parts, low, inner, outer, act, slope, cot, later, wt):
@@ -343,7 +413,7 @@
         compiler_params=grant(28),
         cost_estimate=cost(15, 10),
         name="backward",
-    )(place, low, inner, outer, act, slope, cot, later, in_hbm(wt))
+    )(place, low, inner, outer, act, slope, cot, later, wt)
 
 
 def half_grads(place, parts, low, inner, outer, act, pg, ext):
@@ -453,33 +523,39 @@
     )(place, pg, inner, outer, cot, ws, before)
 
 
-def place_kernel(place_ref, half_ref, theirs_ref, _, spatial_ref, temporal_ref):
+def put_kernel(place_ref, half_ref, *refs):
+    spatial_ref, temporal_ref, wide, sems = refs[-4:]
     parts, rows, chan = half_ref.shape
-    size = rows // 12
-    half = chan // 2
-    core = place_ref[0]
-    for source, start in ((half_ref, core * half), (theirs_ref, half - core * half)):
+    size, half = rows // 12, chan // 2
+    for tap in range(12):
         for n in range(parts):
-            begin = pl.multiple_of(start + n * size, size)
-            for tap in range(12):
-                value = source[n, tap * size : (tap + 1) * size, :].astype(jnp.float32)
-                if tap < 9:
-                    spatial_ref[tap // 3, tap % 3, pl.ds(begin, size), :] = value
-                else:
-                    temporal_ref[tap - 9, pl.ds(begin, size), :] = value
-
-
-def put(place, half, theirs, chan, before):
-    full = pl.BlockSpec(memory_space=pltpu.VMEM)
-    return pl.pallas_call(
-        place_kernel,
-        in_specs=[SCALAR, full, full, UNREAD],
-        out_specs=[full, full],
-        out_shape=[jax.ShapeDtypeStruct((3, 3, chan, chan), jnp.float32),
-                   jax.ShapeDtypeStruct((3, chan, chan), jnp.float32)],
-        compiler_params=grant(10),
-        name="place",
-    )(place, half, theirs, before)
+            wide[tap, n * size : (n + 1) * size, :] = half_ref[n, tap * size : (tap + 1) * size, :].astype(jnp.float32)
+    to = pl.ds(pl.multiple_of(place_ref[0] * half, half), half)
+    copies = []
+    for tap in range(12):
+        if tap < 9:
+            target = spatial_ref.at[tap // 3, tap % 3, to]
+        else:
+            target = temporal_ref.at[tap - 9, to]
+        copies.append(pltpu.make_async_copy(wide.at[tap], target, sems.at[tap]))
+        copies[-1].start()
+    for copy in copies:
+        copy.wait()
+
+
+def put(place, half, *done):
+    chan = half.shape[-1]
+    hbm = pl.BlockSpec(memory_space=pltpu.HBM)
+    return pl.pallas_call(
+        put_kernel,
+        in_specs=[SCALAR, FULL] + [hbm] * len(done),
+        out_specs=[hbm, hbm],
+        out_shape=[like((3, 3, chan, chan), jnp.float32), like((3, chan, chan), jnp.float32)],
+        input_output_aliases={2 + n: n for n in range(len(done))},
+        scratch_shapes=[pltpu.VMEM((12, chan // 2, chan), jnp.float32), pltpu.SemaphoreType.DMA((12,))],
+        compiler_params=grant(6),
+        name="put",
+    )(place, half, *done)
 
 
 def add_kernel(mine_ref, theirs_ref, out_ref):
@@ -498,23 +574,23 @@
     )(mine, theirs)
 
 
-def sum_kernel(got_ref, _, out_ref):
+def sum_kernel(got_ref, out_ref):
     total = got_ref[0].astype(jnp.float32)
     for n in range(1, got_ref.shape[0]):
         total = total + got_ref[n].astype(jnp.float32)
     out_ref[...] = total.astype(jnp.bfloat16)
 
 
-def sum_parts(got, before):
+def sum_parts(got):
     full = pl.BlockSpec(memory_space=pltpu.VMEM)
     return pl.pallas_call(
         sum_kernel,
-        in_specs=[full, UNREAD],
+        in_specs=[full],
         out_specs=full,
         out_shape=like(got.shape[1:], jnp.bfloat16),
         compiler_params=grant(4),
         name="sum_parts",
-    )(got, before)
+    )(got)
 
 
 def spread_kernel(own_ref, theirs_ref, *refs):
@@ -543,30 +619,28 @@
     mine, other = jnp.stack([core, odd]), jnp.stack([1 - core, odd])
     parts = 1 << len(bits.near)
 
-    later = bits.shift(cot[:2], "tm", -1)
-    inner, outer = bits.rows(low[:, :1], low[:, -1:])
-    act, slope, cot_side = forward(mine, low, inner, outer, cot, spatial_weight)
-    pg, ext, theirs = backward(
-        other, parts, low, inner, outer, act, slope, cot_side, later, temporal_weight
-    )
+    inner, outer, later = first_messages(mine, low, cot)
+    later = bits.shift(later, "tm", -1)
+    inner, outer = bits.pairs(inner, outer)
+    low, ws, wt, cot_side = load(low, cot, spatial_weight, temporal_weight)
+    act, slope = forward(mine, low, inner, outer, ws)
+    pg, ext, theirs = backward(other, parts, low, inner, outer, act, slope, cot_side, later, wt)
     theirs = bits.swap(theirs, bits.core)
     own = half_grads(mine, parts, low, inner, outer, act, pg, ext)
     kept = add_halves(own, theirs)
-    got = bits.exchange(kept)
-
-    edge, pg_inner, pg_outer = edges(mine, low, inner, outer, pg, kept)
-    earlier = earlier_act(bits.shift(edge, "tm", 1), spatial_weight)
+    total = sum_parts(bits.exchange(kept))
+    messages = after(edges(mine, low, inner, outer, pg, kept), total)
+    total, far = bits.far_sums(total)
+    edge, pg_inner, pg_outer = messages
+    edge = bits.shift(edge, "tm", 1)
     pg_inner, pg_outer = bits.pairs(pg_inner, pg_outer)
-
-    total, far = bits.far_sums(sum_parts(got, earlier))
-    section_out, section_done = section(jnp.concatenate([earlier, act], axis=0), low, temporal_weight, total)
-    totals = spread(total, far, parts, section_done, pg_inner, pg_outer)
-    input_grad, input_done = input_grads(
-        mine, pg, pg_inner, pg_outer, cot, spatial_weight, totals, low.shape
-    )
-    half = bits.exchange(totals)
+    totals = spread(total, far, parts)
+    earlier = earlier_act(edge, ws, totals)
+    section_out, section_done = section(jnp.concatenate([earlier, act], axis=0), low, wt, totals)
+    input_grad, input_done = input_grads(mine, pg, pg_inner, pg_outer, cot, ws, totals, low.shape)
+    half, = after([bits.exchange(totals)], section_done, input_done)
     theirs = bits.swap(half, bits.core)
-    spatial_grad, temporal_grad = put(mine, half, theirs, chan, input_done)
+    spatial_grad, temporal_grad = put(other, theirs, *put(mine, half))
     return section_out[None], input_grad[None], spatial_grad, temporal_grad
 
 

time: 79.9 us -> 87.1 us (1.090)
  local copies, waits for them, and re-layouts: 2.11 us -> 8.49 us
  blocking collectives: 15.2 us -> 19.9 us
  waiting for transfers between devices: 11.8 us -> 9.45 us
  starting transfers between devices: 18.4 us -> 16.1 us
  Pallas kernels: 29.9 us -> 31.4 us
    unnamed x18 -> x32, local copies, waits for them, and re-layouts: 1.03 us -> 8.49 us
    all_to_all x1, waiting for transfers between devices: 6.77 us -> 0.01 us  [exchange(): return lax.all_to_all(parts, tuple(self.near), 0, 0, tiled=True)]
    pallas_call x2 -> x7, Pallas kernels: 2.51 us -> 7.41 us  [the longest x2 3.75 us: put(): pl.pallas_call(put_kernel, in_specs=[SCALAR, FULL] + [hbm] * len(done), o...]
    all_to_all x1, blocking collectives: 15.2 us -> 19.9 us  [exchange(): return lax.all_to_all(parts, tuple(self.near), 0, 0, tiled=True)]
    ppermute x5, waiting for transfers between devices: 5.03 us -> 9.43 us  [swap(): return lax.ppermute(block, axis, [(0, 1), (1, 0)])]
    all_to_all x1, starting transfers between devices: 5.17 us -> 3.55 us  [exchange(): return lax.all_to_all(parts, tuple(self.near), 0, 0, tiled=True)]
    pallas_call x1, Pallas kernels: 4.42 us -> 2.93 us  [forward(): pl.pallas_call(forward_kernel, grid=(frames,), in_specs=[SCALAR, each(low...]
    pallas_call x1, Pallas kernels: 7.45 us -> 6.36 us  [backward(): pl.pallas_call(backward_kernel, grid_spec=pltpu.PrefetchScalarGridSpec(nu...]
  transfers between devices with their start and end apart: 10 -> 10, of which waited for: 3 -> 2; matrix products, arithmetic and copies ran while one was open for 1% -> 0% of each run, Pallas kernels for 24% -> 23%
where the time goes in v3:
time: 87.1 us; the launch traced here: 86.5 us
  Pallas kernels  31.4 us (36%)
  blocking collectives  19.9 us (23%)
  starting transfers between devices  16.1 us (18%)
  waiting for transfers between devices  9.45 us (11%)
  local copies, waits for them, and re-layouts  8.49 us (10%)
  between operations  0.89 us (1%)
    all_to_all x1, blocking collectives, exchange(): return lax.all_to_all(parts, tuple(self.near), 0, 0, tiled=True)  19.9 us
    ppermute x5, waiting for transfers between devices, swap(): return lax.ppermute(block, axis, [(0, 1), (1, 0)])  9.43 us
    ppermute x5, starting transfers between devices, swap(): return lax.ppermute(block, axis, [(0, 1), (1, 0)])  8.61 us
    unnamed x32, local copies, waits for them, and re-layouts  8.49 us
    pallas_call x1, Pallas kernels, backward(): pl.pallas_call(backward_kernel, grid_spec=pltpu.PrefetchScalarGridSpec(nu...  6.36 us
    pallas_call x1, Pallas kernels, input_grads(): pl.pallas_call(input_kernel, grid=(low_shape[0],), in_specs=[SCALAR, each...  5.06 us
    pallas_call x2, Pallas kernels, put(): pl.pallas_call(put_kernel, in_specs=[SCALAR, FULL] + [hbm] * len(done), o...  3.75 us
    pallas_call x1, Pallas kernels, half_grads(): pl.pallas_call(half_kernel, grid_spec=pltpu.PrefetchScalarGridSpec(num_sc...  3.66 us
  transfers between devices with their start and end apart: 10, of which 2 were waited for; matrix products, arithmetic and copies ran while one was open for 0% of the time, Pallas kernels for 23%

profile of v3, /device:TPU:0, one launch (start us, length us, event | category | flops | bytes accessed | tf_op | source)
XLA Modules:
  0.0 86.5 jit_solution(6251869744118499949)
XLA Ops:
  0.6 0.1 pad_add_fusion.place_ref
  0.7 1.6 %first_messages.1 = (bf16[4,1,32,256]{3,2,1,0:T(8,128)(2,1)S(1)}, bf16[4,1,32,256]{3,2,1,0:T(8,128)(2,1)S(1)}, bf16[2,8,64,256]{3,2,1,0:T(8,128)(2,1)S(1)}) custom-call(s32[2]{0:T(128)S(1)} %pad_add_fusion.place_ref, bf16[4,4,32,256]{3,2,1,0:T(8,128)(2,1)} %bitcast.10, bf16[4,8,64,256]{3,2,1,0:T(8,128)(2,1)} %bitcast.7), custom_call_target="tpu_custom_call" | custom-call | tf_op jit(solution)/shard_map/first_messages/pallas_call | solution.py:288
  2.3 1.3 %collective-permute-start.2 = (bf16[2,8,64,256]{3,2,1,0:T(8,128)(2,1)S(1)}, bf16[2,8,64,256]{3,2,1,0:T(8,128)(2,1)S(1)}, u32[]{:S(2)}, u32[]{:S(2)}) collective-permute-start(bf16[2,8,64,256]{3,2,1,0:T(8,128)(2,1)S(1)} %get-tuple-element.37), channel_id=1, source_target_pairs={{4,0},{8,4},{12,8},{5,1},{9,5},{13,9},{6,2},{10,6},{14,10},{7,3},{... | collective-permute-start | bytes 1572872 | tf_op jit(solution)/shard_map/ppermute | solution.py:39
  3.6 3.1 %collective-permute-start = (bf16[4,1,32,256]{3,2,1,0:T(8,128)(2,1)S(1)}, bf16[4,1,32,256]{3,2,1,0:T(8,128)(2,1)S(1)}, u32[]{:S(2)}, u32[]{:S(2)}) collective-permute-start(bf16[4,1,32,256]{3,2,1,0:T(8,128)(2,1)S(1)} %get-tuple-element.31), channel_id=1, source_target_pairs={{0,1},{1,0},{2,3},{3,2},{4,5},{5,4},{6,7},{7,6},{8,9},{9,8},{10,11... | collective-permute-start | bytes 196616 | tf_op jit(solution)/shard_map/ppermute | solution.py:33
  6.7 0.7 collective-permute-start.1
  7.4 0.1 pad_add_fusion.1.place_ref
  7.5 2.0 %load.1 = (bf16[4,4,32,256]{3,2,1,0:T(8,128)(2,1)S(1)}, bf16[3,3,256,256]{3,2,1,0:T(8,128)(2,1)S(1)}, bf16[3,256,256]{2,1,0:T(8,128)(2,1)S(1)}, bf16[4,4,128,256]{3,2,1,0:T(8,128)(2,1)S(1)}) custom-call(bf16[4,4,32,256]{3,2,1,0:T(8,128)(2,1)} %bitcast.11, bf16[4,8,64,256]{3,2,1,0:T(8,128)(2,1)} %bitcast.8, bf16[3,3,256,256]{3,2,1,0:T(8,128)(2,1)} %ws_hbm.1, ...), custom_call_target="tpu_custom_call" | custom-call | flops 536870912 | bytes 4194304 | tf_op jit(solution)/shard_map/load/pallas_call | solution.py:315
  9.4 0.0 copy-start.14
  9.4 0.0 collective-permute-done.inner_ref
  9.4 0.0 collective-permute-done.1.outer_ref
  9.5 2.9 %forward.1 = (bf16[4,4,128,256]{3,2,1,0:T(8,128)(2,1)S(1)}, f32[4,4,128,256]{3,2,1,0:T(8,128)S(1)}) custom-call(s32[2]{0:T(128)S(1)} %pad_add_fusion.place_ref, bf16[4,4,32,256]{3,2,1,0:T(8,128)(2,1)S(1)} %get-tuple-element.30.low_ref, bf16[4,1,32,256]{3,2,1,0:T(8,128)(2,1)S(1)} %collective-permute-done.inner_ref, ...), custom_call_target="tpu_custom_call" | custom-call | flops 2684354560 | bytes 8388608 | tf_op jit(solution)/shard_map/forward/pallas_call | solution.py:346
  12.4 0.0 copy-start.3
  12.4 0.0 collective-permute-done.2.later_ref
  12.4 6.4 %backward.1 = (bf16[4,4,128,256]{3,2,1,0:T(8,128)(2,1)S(1)}, bf16[6,4,128,256]{3,2,1,0:T(8,128)(2,1)S(1)}, f32[8,192,256]{2,1,0:T(8,128)S(1)}) custom-call(s32[2]{0:T(128)S(1)} %pad_add_fusion.1.place_ref, bf16[4,4,32,256]{3,2,1,0:T(8,128)(2,1)S(1)} %get-tuple-element.30.low_ref, bf16[4,1,32,256]{3,2,1,0:T(8,128)(2,1)S(1)} %collective-permute-done.inner_ref, ...), custom_call_target="tpu_custom_call" | custom-call | flops 4026531840 | bytes 10485760 | tf_op jit(solution)/shard_map/backward/pallas_call | solution.py:403
  18.8 1.8 %collective-permute-start.3 = (f32[8,192,256]{2,1,0:T(8,128)S(1)}, f32[8,192,256]{2,1,0:T(8,128)S(1)}, u32[]{:S(2)}, u32[]{:S(2)}) collective-permute-start(f32[8,192,256]{2,1,0:T(8,128)S(1)} %get-tuple-element.41), channel_id=1, source_target_pairs={{0,4},{4,0},{1,5},{5,1},{2,6},{6,2},{3,7},{7,3},{8,12},{12,8},{9,1... | collective-permute-start | bytes 4718600 | tf_op jit(solution)/shard_map/ppermute | solution.py:33
  20.6 3.7 %half_grads.1.mine_ref = f32[8,192,256]{2,1,0:T(8,128)S(1)} custom-call(s32[2]{0:T(128)S(1)} %pad_add_fusion.place_ref, bf16[4,4,32,256]{3,2,1,0:T(8,128)(2,1)S(1)} %get-tuple-element.30.low_ref, bf16[4,1,32,256]{3,2,1,0:T(8,128)(2,1)S(1)} %collective-permute-done.inner_ref, bf16[4,1,32,256]{3,2,1,0:T(8,128)(2,1)S(1)} %collective-permute-done.1.outer_ref, ...), custom_call_target="tpu_custom_call" | custom-call | flops 2684354560 | bytes 6291456 | tf_op jit(solution)/shard_map/half_grads/pallas_call | solution.py:422
  24.3 0.0 collective-permute-done.3.theirs_ref
  24.3 0.3 add_halves.1._
  24.5 19.9 %all_to_all.10.got_ref = bf16[8,192,256]{2,1,0:T(8,128)(2,1)S(1)} all-to-all(bf16[8,192,256]{2,1,0:T(8,128)(2,1)S(1)} %add_halves.1._), channel_id=1, replica_groups=mesh['dp0'=2,'tm1'=2,'tm0'=2,'height1'=2,'height0'=2] {'dp0','tm1','heig..., dimensions={0} | all-to-all | bytes 1572864 | tf_op jit(solution)/shard_map/all_to_all | solution.py:42
  44.5 0.1 sum_parts.1.__3_.own_ref
  44.6 1.8 %collective-permute-start.5 = (bf16[192,256]{1,0:T(8,128)(2,1)S(1)}, bf16[192,256]{1,0:T(8,128)(2,1)S(1)}, u32[]{:S(2)}, u32[]{:S(2)}) collective-permute-start(bf16[192,256]{1,0:T(8,128)(2,1)S(1)} %sum_parts.1.__3_.own_ref), channel_id=1, source_target_pairs={{0,2},{2,0},{1,3},{3,1},{4,6},{6,4},{5,7},{7,5},{8,10},{10,8},{9,1... | collective-permute-start | bytes 294920 | tf_op jit(solution)/shard_map/ppermute | solution.py:33
  46.4 5.0 %collective-permute-done.5.theirs_ref = bf16[192,256]{1,0:T(8,128)(2,1)S(1)} collective-permute-done((bf16[192,256]{1,0:T(8,128)(2,1)S(1)}, bf16[192,256]{1,0:T(8,128)(2,1)S(1)}, u32[]{:S(2)}, u32[]{:S(2)}) %collective-permute-start.5) | collective-permute-done | bytes 98336 | tf_op jit(solution)/shard_map/ppermute | solution.py:33
  51.4 0.9 %spread.1._ = bf16[8,192,256]{2,1,0:T(8,128)(2,1)} custom-call(bf16[192,256]{1,0:T(8,128)(2,1)S(1)} %sum_parts.1.__3_.own_ref, bf16[192,256]{1,0:T(8,128)(2,1)S(1)} %collective-permute-done.5.theirs_ref), custom_call_target="tpu_custom_call" | custom-call | tf_op jit(solution)/shard_map/spread/pallas_call | solution.py:604
  52.4 3.5 %all-to-all-start.1 = ((bf16[8,192,256]{2,1,0:T(8,128)(2,1)}), bf16[8,192,256]{2,1,0:T(8,128)(2,1)S(1)}, u32[]{:S(2)}, u32[]{:S(2)}) async-start(bf16[8,192,256]{2,1,0:T(8,128)(2,1)} %spread.1._), calls=%async_computation.1 | async-start | bytes 1572864 | tf_op jit(solution)/shard_map/all_to_all | solution.py:42
  55.9 1.2 %copy-done.6 = bf16[4,4,128,256]{3,2,1,0:T(8,128)(2,1)S(1)} copy-done((bf16[4,4,128,256]{3,2,1,0:T(8,128)(2,1)S(1)}, bf16[4,4,128,256]{3,2,1,0:T(8,128)(2,1)}, u32[]{:S(2)}) %copy-start.6) | copy-done | bytes 1048600
  57.2 0.6 edges.1
  57.8 0.7 copy-done.9
  58.4 0.7 copy-done.10
  59.1 0.6 copy-done.11
  59.7 1.9 %collective-permute-start.6 = (bf16[4,2,32,256]{3,2,1,0:T(8,128)(2,1)}, bf16[4,2,32,256]{3,2,1,0:T(8,128)(2,1)S(1)}, u32[]{:S(2)}, u32[]{:S(2)}) collective-permute-start(bf16[4,2,32,256]{3,2,1,0:T(8,128)(2,1)} %get-tuple-element.47), channel_id=1, source_target_pairs={{0,1},{1,0},{2,3},{3,2},{4,5},{5,4},{6,7},{7,6},{8,9},{9,8},{10,11... | collective-permute-start | bytes 393224 | tf_op jit(solution)/shard_map/ppermute | solution.py:33
  61.7 0.7 collective-permute-start.7
  62.3 1.3 %collective-permute-start.4 = (bf16[2,6,32,256]{3,2,1,0:T(8,128)(2,1)}, bf16[2,6,32,256]{3,2,1,0:T(8,128)(2,1)S(1)}, u32[]{:S(2)}, u32[]{:S(2)}) collective-permute-start(bf16[2,6,32,256]{3,2,1,0:T(8,128)(2,1)} %get-tuple-element.45), channel_id=1, source_target_pairs={{0,4},{4,8},{8,12},{1,5},{5,9},{9,13},{2,6},{6,10},{10,14},{3,7},{... | collective-permute-start | bytes 589832 | tf_op jit(solution)/shard_map/ppermute | solution.py:39
  63.6 4.4 %collective-permute-done.6.inner_ref = bf16[4,2,32,256]{3,2,1,0:T(8,128)(2,1)S(1)} collective-permute-done((bf16[4,2,32,256]{3,2,1,0:T(8,128)(2,1)}, bf16[4,2,32,256]{3,2,1,0:T(8,128)(2,1)S(1)}, u32[]{:S(2)}, u32[]{:S(2)}) %collective-permute-start.6) | collective-permute-done | bytes 131104 | tf_op jit(solution)/shard_map/ppermute | solution.py:33
  68.0 1.2 %copy-done.7 = bf16[4,4,128,256]{3,2,1,0:T(8,128)(2,1)S(1)} copy-done((bf16[4,4,128,256]{3,2,1,0:T(8,128)(2,1)S(1)}, bf16[4,4,128,256]{3,2,1,0:T(8,128)(2,1)}, u32[]{:S(2)}) %copy-start.7) | copy-done | bytes 1048600
  69.3 1.3 %copy-done.15 = bf16[3,3,256,256]{3,2,1,0:T(8,128)(2,1)S(1)} copy-done((bf16[3,3,256,256]{3,2,1,0:T(8,128)(2,1)S(1)}, bf16[3,3,256,256]{3,2,1,0:T(8,128)(2,1)}, u32[]{:S(2)}) %copy-start.15) | copy-done | bytes 1179672
  70.5 5.1 %input_grads.1 = (bf16[4,4,32,256]{3,2,1,0:T(8,128)(2,1)}, f32[8,128]{1,0:T(8,128)S(1)}) custom-call(s32[2]{0:T(128)S(1)} %pad_add_fusion.place_ref, bf16[4,4,128,256]{3,2,1,0:T(8,128)(2,1)S(1)} %copy-done.7, bf16[4,2,32,256]{3,2,1,0:T(8,128)(2,1)S(1)} %collective-permute-done.6.inner_ref, bf16[4,2,32,256]{3,2,1,0:T(8,128)(2,1)S(1)} %collective-permute-done.7.outer_ref, ...), custom_call_target="tpu_custom_call" | custom-call | flops 1610612736 | bytes 4194304 | tf_op jit(solution)/shard_map/input_grads/pallas_call | solution.py:514
  75.6 1.1 %earlier_act.1 = bf16[2,4,128,256]{3,2,1,0:T(8,128)(2,1)S(1)} custom-call(bf16[2,6,32,256]{3,2,1,0:T(8,128)(2,1)S(1)} %collective-permute-done.4.low_ref, bf16[3,3,256,256]{3,2,1,0:T(8,128)(2,1)S(1)} %copy-done.15, bf16[8,192,256]{2,1,0:T(8,128)(2,1)} %spread.1._), custom_call_target="tpu_custom_call" | custom-call | flops 1073741824 | bytes 3145728 | tf_op jit(solution)/shard_map/earlier_act/pallas_call | solution.py:387
  76.7 0.1 copy-done.4
  76.8 0.1 pad_maximum_fusion.act_ref
  77.0 3.2 %section.1 = (bf16[4,8,64,256]{3,2,1,0:T(8,128)(2,1)}, f32[8,128]{1,0:T(8,128)S(1)}) custom-call(bf16[6,4,128,256]{3,2,1,0:T(8,128)(2,1)S(1)} %pad_maximum_fusion.act_ref, bf16[4,4,32,256]{3,2,1,0:T(8,128)(2,1)S(1)} %get-tuple-element.30.low_ref, bf16[3,256,256]{2,1,0:T(8,128)(2,1)S(1)} %get-tuple-element.38.wt_ref, bf16[8,192,256]{2,1,0:T(8,128)(2,1)} %spread.1._), custom_call_target="tpu_custom_call" | custom-call | flops 1073741824 | bytes 3145728 | tf_op jit(solution)/shard_map/section/pallas_call | solution.py:461
  80.1 0.6 copy-done.13
  80.7 0.0 all-to-all-done.1.__0_
  80.7 0.9 %copy-done = bf16[8,192,256]{2,1,0:T(8,128)(2,1)} copy-done((bf16[8,192,256]{2,1,0:T(8,128)(2,1)}, bf16[8,192,256]{2,1,0:T(8,128)(2,1)S(1)}, u32[]{:S(2)}) %copy-start) | copy-done | bytes 786456
  81.6 0.0 collective-permute-start.8
  81.6 1.1 %copy-done.1 = bf16[8,192,256]{2,1,0:T(8,128)(2,1)S(1)} copy-done((bf16[8,192,256]{2,1,0:T(8,128)(2,1)S(1)}, bf16[8,192,256]{2,1,0:T(8,128)(2,1)}, u32[]{:S(2)}) %copy-start.1) | copy-done | bytes 786456
  82.8 1.9 %put.2 = (f32[3,3,256,256]{3,2,1,0:T(8,128)}, f32[3,256,256]{2,1,0:T(8,128)}) custom-call(s32[2]{0:T(128)S(1)} %pad_add_fusion.place_ref, bf16[8,192,256]{2,1,0:T(8,128)(2,1)S(1)} %copy-done.1), custom_call_target="tpu_custom_call" | custom-call | tf_op jit(solution)/shard_map/put/pallas_call | solution.py:549
  84.6 0.0 collective-permute-done.8.half_ref
  84.6 1.9 %put.3 = (f32[3,3,256,256]{3,2,1,0:T(8,128)}, f32[3,256,256]{2,1,0:T(8,128)}) custom-call(s32[2]{0:T(128)S(1)} %pad_add_fusion.1.place_ref, bf16[8,192,256]{2,1,0:T(8,128)(2,1)S(1)} %collective-permute-done.8.half_ref, f32[3,3,256,256]{3,2,1,0:T(8,128)} %get-tuple-element.52.refs_0_, ...), custom_call_target="tpu_custom_call", output_to_operand_aliasing={{0}: (2, {}), {1}: (3, {})} | custom-call | tf_op jit(solution)/shard_map/put/pallas_call | solution.py:549
  (24 shorter events, 0.0 us)
Async XLA Ops:
  2.3 10.1 %collective-permute-start.2 = (bf16[2,8,64,256]{3,2,1,0:T(8,128)(2,1)S(1)}, bf16[2,8,64,256]{3,2,1,0:T(8,128)(2,1)S(1)}, u32[]{:S(2)}, u32[]{:S(2)}) collective-permute-start(bf16[2,8,64,256]{3,2,1,0:T(8,128)(2,1)S(1)} %get-tuple-element.37), channel_id=1, source_target_pairs={{4,0},{8,4},{12,8},{5,1},{9,5},{13,9},{6,2},{10,6},{14,10},{7,3},{... | collective-permute-start | bytes 1572872 | tf_op jit(solution)/shard_map/ppermute | solution.py:39
  3.6 5.8 %collective-permute-start = (bf16[4,1,32,256]{3,2,1,0:T(8,128)(2,1)S(1)}, bf16[4,1,32,256]{3,2,1,0:T(8,128)(2,1)S(1)}, u32[]{:S(2)}, u32[]{:S(2)}) collective-permute-start(bf16[4,1,32,256]{3,2,1,0:T(8,128)(2,1)S(1)} %get-tuple-element.31), channel_id=1, source_target_pairs={{0,1},{1,0},{2,3},{3,2},{4,5},{5,4},{6,7},{7,6},{8,9},{9,8},{10,11... | collective-permute-start | bytes 196616 | tf_op jit(solution)/shard_map/ppermute | solution.py:33
  6.7 2.7 %collective-permute-start.1 = (bf16[4,1,32,256]{3,2,1,0:T(8,128)(2,1)S(1)}, bf16[4,1,32,256]{3,2,1,0:T(8,128)(2,1)S(1)}, u32[]{:S(2)}, u32[]{:S(2)}) collective-permute-start(bf16[4,1,32,256]{3,2,1,0:T(8,128)(2,1)S(1)} %get-tuple-element.32), channel_id=1, source_target_pairs={{1,2},{2,1},{5,6},{6,5},{9,10},{10,9},{13,14},{14,13},{17,18},{18,... | collective-permute-start | bytes 196616 | tf_op jit(solution)/shard_map/ppermute | solution.py:48
  9.4 3.0 %copy-start.14 = (bf16[3,3,256,256]{3,2,1,0:T(8,128)(2,1)}, bf16[3,3,256,256]{3,2,1,0:T(8,128)(2,1)S(1)}, u32[]{:S(2)}) copy-start(bf16[3,3,256,256]{3,2,1,0:T(8,128)(2,1)S(1)} %get-tuple-element.33.ws_ref) | copy-start | bytes 3538948
  12.4 8.2 %copy-start.3 = (bf16[4,4,128,256]{3,2,1,0:T(8,128)(2,1)}, bf16[4,4,128,256]{3,2,1,0:T(8,128)(2,1)S(1)}, u32[]{:S(2)}) copy-start(bf16[4,4,128,256]{3,2,1,0:T(8,128)(2,1)S(1)} %get-tuple-element.34.act_ref) | copy-start | bytes 3145732
  18.8 5.5 %copy-start.5 = (bf16[4,4,128,256]{3,2,1,0:T(8,128)(2,1)}, bf16[4,4,128,256]{3,2,1,0:T(8,128)(2,1)S(1)}, u32[]{:S(2)}) copy-start(bf16[4,4,128,256]{3,2,1,0:T(8,128)(2,1)S(1)} %get-tuple-element.39.pg_ref) | copy-start | bytes 3145732
  18.8 5.5 %collective-permute-start.3 = (f32[8,192,256]{2,1,0:T(8,128)S(1)}, f32[8,192,256]{2,1,0:T(8,128)S(1)}, u32[]{:S(2)}, u32[]{:S(2)}) collective-permute-start(f32[8,192,256]{2,1,0:T(8,128)S(1)} %get-tuple-element.41), channel_id=1, source_target_pairs={{0,4},{4,0},{1,5},{5,1},{2,6},{6,2},{3,7},{7,3},{8,12},{12,8},{9,1... | collective-permute-start | bytes 4718600 | tf_op jit(solution)/shard_map/ppermute | solution.py:33
  44.6 13.2 %copy-start.8 = (bf16[192,256]{1,0:T(8,128)(2,1)}, bf16[192,256]{1,0:T(8,128)(2,1)S(1)}, u32[]{:S(2)}) copy-start(bf16[192,256]{1,0:T(8,128)(2,1)S(1)} %sum_parts.1.__3_.own_ref) | copy-start | bytes 294916
  44.6 6.9 %collective-permute-start.5 = (bf16[192,256]{1,0:T(8,128)(2,1)S(1)}, bf16[192,256]{1,0:T(8,128)(2,1)S(1)}, u32[]{:S(2)}, u32[]{:S(2)}) collective-permute-start(bf16[192,256]{1,0:T(8,128)(2,1)S(1)} %sum_parts.1.__3_.own_ref), channel_id=1, source_target_pairs={{0,2},{2,0},{1,3},{3,1},{4,6},{6,4},{5,7},{7,5},{8,10},{10,8},{9,1... | collective-permute-start | bytes 294920 | tf_op jit(solution)/shard_map/ppermute | solution.py:33
  52.4 28.4 %all-to-all-start.1 = ((bf16[8,192,256]{2,1,0:T(8,128)(2,1)}), bf16[8,192,256]{2,1,0:T(8,128)(2,1)S(1)}, u32[]{:S(2)}, u32[]{:S(2)}) async-start(bf16[8,192,256]{2,1,0:T(8,128)(2,1)} %spread.1._), calls=%async_computation.1 | async-start | bytes 1572864 | tf_op jit(solution)/shard_map/all_to_all | solution.py:42
  55.9 1.2 %copy-start.6 = (bf16[4,4,128,256]{3,2,1,0:T(8,128)(2,1)S(1)}, bf16[4,4,128,256]{3,2,1,0:T(8,128)(2,1)}, u32[]{:S(2)}) copy-start(bf16[4,4,128,256]{3,2,1,0:T(8,128)(2,1)} %copy-done.5) | copy-start | bytes 3145732
  57.2 10.9 %copy-start.2 = (bf16[1,4,8,64,256]{4,3,2,1,0:T(8,128)(2,1)S(1)}, bf16[1,4,8,64,256]{4,3,2,1,0:T(8,128)(2,1)}, u32[]{:S(2)}) copy-start(bf16[1,4,8,64,256]{4,3,2,1,0:T(8,128)(2,1)} %param.7) | copy-start | bytes 3145732
  57.7 0.7 copy-start.9
  58.4 0.7 copy-start.10
  59.1 0.6 copy-start.11
  59.7 8.3 %collective-permute-start.6 = (bf16[4,2,32,256]{3,2,1,0:T(8,128)(2,1)}, bf16[4,2,32,256]{3,2,1,0:T(8,128)(2,1)S(1)}, u32[]{:S(2)}, u32[]{:S(2)}) collective-permute-start(bf16[4,2,32,256]{3,2,1,0:T(8,128)(2,1)} %get-tuple-element.47), channel_id=1, source_target_pairs={{0,1},{1,0},{2,3},{3,2},{4,5},{5,4},{6,7},{7,6},{8,9},{9,8},{10,11... | collective-permute-start | bytes 393224 | tf_op jit(solution)/shard_map/ppermute | solution.py:33
  61.7 6.4 %collective-permute-start.7 = (bf16[4,2,32,256]{3,2,1,0:T(8,128)(2,1)}, bf16[4,2,32,256]{3,2,1,0:T(8,128)(2,1)S(1)}, u32[]{:S(2)}, u32[]{:S(2)}) collective-permute-start(bf16[4,2,32,256]{3,2,1,0:T(8,128)(2,1)} %get-tuple-element.48), channel_id=1, source_target_pairs={{1,2},{2,1},{5,6},{6,5},{9,10},{10,9},{13,14},{14,13},{17,18},{18,... | collective-permute-start | bytes 393224 | tf_op jit(solution)/shard_map/ppermute | solution.py:48
  62.3 13.3 %collective-permute-start.4 = (bf16[2,6,32,256]{3,2,1,0:T(8,128)(2,1)}, bf16[2,6,32,256]{3,2,1,0:T(8,128)(2,1)S(1)}, u32[]{:S(2)}, u32[]{:S(2)}) collective-permute-start(bf16[2,6,32,256]{3,2,1,0:T(8,128)(2,1)} %get-tuple-element.45), channel_id=1, source_target_pairs={{0,4},{4,8},{8,12},{1,5},{5,9},{9,13},{2,6},{6,10},{10,14},{3,7},{... | collective-permute-start | bytes 589832 | tf_op jit(solution)/shard_map/ppermute | solution.py:39
  68.0 1.2 %copy-start.7 = (bf16[4,4,128,256]{3,2,1,0:T(8,128)(2,1)S(1)}, bf16[4,4,128,256]{3,2,1,0:T(8,128)(2,1)}, u32[]{:S(2)}) copy-start(bf16[4,4,128,256]{3,2,1,0:T(8,128)(2,1)} %copy-done.5) | copy-start | bytes 3145732
  69.3 1.3 %copy-start.15 = (bf16[3,3,256,256]{3,2,1,0:T(8,128)(2,1)S(1)}, bf16[3,3,256,256]{3,2,1,0:T(8,128)(2,1)}, u32[]{:S(2)}) copy-start(bf16[3,3,256,256]{3,2,1,0:T(8,128)(2,1)} %copy-done.14) | copy-start | bytes 3538948
  75.6 1.1 %copy-start.12 = (f32[8,128]{1,0:T(8,128)}, f32[8,128]{1,0:T(8,128)S(1)}, u32[]{:S(2)}) copy-start(f32[8,128]{1,0:T(8,128)S(1)} %get-tuple-element.51.__2_) | copy-start | bytes 12292
  75.6 1.2 %copy-start.4 = (bf16[4,4,128,256]{3,2,1,0:T(8,128)(2,1)S(1)}, bf16[4,4,128,256]{3,2,1,0:T(8,128)(2,1)}, u32[]{:S(2)}) copy-start(bf16[4,4,128,256]{3,2,1,0:T(8,128)(2,1)} %copy-done.3) | copy-start | bytes 3145732
  80.1 0.6 copy-start.13
  80.7 0.9 %copy-start = (bf16[8,192,256]{2,1,0:T(8,128)(2,1)}, bf16[8,192,256]{2,1,0:T(8,128)(2,1)S(1)}, u32[]{:S(2)}) copy-start(bf16[8,192,256]{2,1,0:T(8,128)(2,1)S(1)} %all-to-all-done.1.__0_) | copy-start | bytes 2359300
  81.6 3.0 %collective-permute-start.8 = (bf16[8,192,256]{2,1,0:T(8,128)(2,1)}, bf16[8,192,256]{2,1,0:T(8,128)(2,1)S(1)}, u32[]{:S(2)}, u32[]{:S(2)}) collective-permute-start(bf16[8,192,256]{2,1,0:T(8,128)(2,1)} %after.3.half_ref), channel_id=1, source_target_pairs={{0,4},{4,0},{1,5},{5,1},{2,6},{6,2},{3,7},{7,3},{8,12},{12,8},{9,1... | collective-permute-start | bytes 2359304 | tf_op jit(solution)/shard_map/ppermute | solution.py:33
  81.6 1.1 %copy-start.1 = (bf16[8,192,256]{2,1,0:T(8,128)(2,1)S(1)}, bf16[8,192,256]{2,1,0:T(8,128)(2,1)}, u32[]{:S(2)}) copy-start(bf16[8,192,256]{2,1,0:T(8,128)(2,1)} %after.3.half_ref) | copy-start | bytes 2359300

commit v4 on v3

--- a/solution.py
+++ b/solution.py
@@ -154,7 +154,7 @@
         slope_ref[0, side] = sig * (1.0 + pre * (1.0 - sig))
 
 
-def act_kernel(low_ref, ws_ref, _, act_ref):
+def act_kernel(low_ref, ws_ref, act_ref):
     for side, pre in enumerate(spatial(low_ref[0], ws_ref)):
         act_ref[0, side] = (pre * jax.nn.sigmoid(pre)).astype(jnp.bfloat16)
 
@@ -336,6 +336,7 @@
         out_specs=[UNREAD] * len(arrays),
         out_shape=[like(a.shape, a.dtype) for a in arrays],
         input_output_aliases={n: n for n in range(len(arrays))},
+        compiler_params=grant(1),
         name="after",
     )(*arrays, *before)
 
@@ -381,19 +382,19 @@
     )(place, low, inner, outer, pg, before)
 
 
-def earlier_act(low, ws, before):
+def earlier_act(low, ws):
     frames, rows_tall, cols_low, chan = low.shape
     side = (frames, 4, (rows_tall - 2) * cols_low, chan)
     return pl.pallas_call(
         act_kernel,
         grid=(frames,),
-        in_specs=[each(low.shape), whole(ws.shape), UNREAD],
+        in_specs=[each(low.shape), whole(ws.shape)],
         out_specs=each(side),
         out_shape=like(side, jnp.bfloat16),
         compiler_params=grant(16),
         cost_estimate=cost(4, 3),
         name="earlier_act",
-    )(low, ws, before)
+    )(low, ws)
 
 
 def backward(place, parts, low, inner, outer, act, slope, cot, later, wt):
@@ -574,23 +575,23 @@
     )(mine, theirs)
 
 
-def sum_kernel(got_ref, out_ref):
+def sum_kernel(got_ref, _, out_ref):
     total = got_ref[0].astype(jnp.float32)
     for n in range(1, got_ref.shape[0]):
         total = total + got_ref[n].astype(jnp.float32)
     out_ref[...] = total.astype(jnp.bfloat16)
 
 
-def sum_parts(got):
+def sum_parts(got, before):
     full = pl.BlockSpec(memory_space=pltpu.VMEM)
     return pl.pallas_call(
         sum_kernel,
-        in_specs=[full],
+        in_specs=[full, UNREAD],
         out_specs=full,
         out_shape=like(got.shape[1:], jnp.bfloat16),
         compiler_params=grant(4),
         name="sum_parts",
-    )(got)
+    )(got, before)
 
 
 def spread_kernel(own_ref, theirs_ref, *refs):
@@ -628,17 +629,15 @@
     theirs = bits.swap(theirs, bits.core)
     own = half_grads(mine, parts, low, inner, outer, act, pg, ext)
     kept = add_halves(own, theirs)
-    total = sum_parts(bits.exchange(kept))
-    messages = after(edges(mine, low, inner, outer, pg, kept), total)
-    total, far = bits.far_sums(total)
-    edge, pg_inner, pg_outer = messages
-    edge = bits.shift(edge, "tm", 1)
+    got = bits.exchange(kept)
+    edge, pg_inner, pg_outer = edges(mine, low, inner, outer, pg, kept)
+    earlier = earlier_act(bits.shift(edge, "tm", 1), ws)
     pg_inner, pg_outer = bits.pairs(pg_inner, pg_outer)
-    totals = spread(total, far, parts)
-    earlier = earlier_act(edge, ws, totals)
-    section_out, section_done = section(jnp.concatenate([earlier, act], axis=0), low, wt, totals)
+    total, far = bits.far_sums(sum_parts(got, earlier))
+    section_out, section_done = section(jnp.concatenate([earlier, act], axis=0), low, wt, total)
+    totals = spread(total, far, parts, section_done, pg_inner, pg_outer)
     input_grad, input_done = input_grads(mine, pg, pg_inner, pg_outer, cot, ws, totals, low.shape)
-    half, = after([bits.exchange(totals)], section_done, input_done)
+    half, = after([bits.exchange(totals)], input_done)
     theirs = bits.swap(half, bits.core)
     spatial_grad, temporal_grad = put(other, theirs, *put(mine, half))
     return section_out[None], input_grad[None], spatial_grad, temporal_grad

time: 87.1 us -> 74.8 us (0.86)
  blocking collectives: 19.9 us -> 0 us
  starting transfers between devices: 16.1 us -> 24 us
  local copies, waits for them, and re-layouts: 8.49 us -> 2.3 us
  waiting for transfers between devices: 9.45 us -> 13.8 us
  Pallas kernels: 31.4 us -> 33.1 us
    all_to_all x1 -> x0, blocking collectives: 19.9 us -> none  [exchange(): return lax.all_to_all(parts, tuple(self.near), 0, 0, tiled=True)]
    all_to_all x1 -> x2, waiting for transfers between devices: 0.01 us -> 12.4 us  [exchange(): return lax.all_to_all(parts, tuple(self.near), 0, 0, tiled=True)]
    ppermute x5, waiting for transfers between devices: 9.43 us -> 1.43 us  [swap(): return lax.ppermute(block, axis, [(0, 1), (1, 0)])]
    all_to_all x1 -> x2, starting transfers between devices: 3.55 us -> 10.7 us  [exchange(): return lax.all_to_all(parts, tuple(self.near), 0, 0, tiled=True)]
    unnamed x32 -> x20, local copies, waits for them, and re-layouts: 8.49 us -> 2.3 us
  transfers between devices with their start and end apart: 10 -> 11, of which waited for: 2 -> 4; matrix products, arithmetic and copies ran while one was open for 0% -> 0% of each run, Pallas kernels for 23% -> 28%
where the time goes in v4:
time: 74.8 us; the launch traced here: 74.4 us
  Pallas kernels  33.1 us (44%)
  starting transfers between devices  24 us (32%)
  waiting for transfers between devices  13.8 us (18%)
  local copies, waits for them, and re-layouts  2.3 us (3%)
  between operations  0.89 us (1%)
    all_to_all x2, waiting for transfers between devices, exchange(): return lax.all_to_all(parts, tuple(self.near), 0, 0, tiled=True)  12.4 us
    all_to_all x2, starting transfers between devices, exchange(): return lax.all_to_all(parts, tuple(self.near), 0, 0, tiled=True)  10.7 us
    ppermute x5, starting transfers between devices, swap(): return lax.ppermute(block, axis, [(0, 1), (1, 0)])  8.47 us
    pallas_call x1, Pallas kernels, backward(): pl.pallas_call(backward_kernel, grid_spec=pltpu.PrefetchScalarGridSpec(nu...  6.5 us
    pallas_call x1, Pallas kernels, input_grads(): pl.pallas_call(input_kernel, grid=(low_shape[0],), in_specs=[SCALAR, each...  5.05 us
    pallas_call x1, Pallas kernels, half_grads(): pl.pallas_call(half_kernel, grid_spec=pltpu.PrefetchScalarGridSpec(num_sc...  3.79 us
    pallas_call x2, Pallas kernels, put(): pl.pallas_call(put_kernel, in_specs=[SCALAR, FULL] + [hbm] * len(done), o...  3.74 us
    ppermute x2, starting transfers between devices, shift(): return lax.ppermute(block, axes, route)  3.4 us
  transfers between devices with their start and end apart: 11, of which 4 were waited for; matrix products, arithmetic and copies ran while one was open for 0% of the time, Pallas kernels for 28%

profile of v4, /device:TPU:0, one launch (start us, length us, event | category | flops | bytes accessed | tf_op | source)
XLA Modules:
  0.0 74.4 jit_solution(4141687878095304523)
XLA Ops:
  0.6 0.1 pad_add_fusion.place_ref
  0.7 1.6 %first_messages.1 = (bf16[4,1,32,256]{3,2,1,0:T(8,128)(2,1)S(1)}, bf16[4,1,32,256]{3,2,1,0:T(8,128)(2,1)S(1)}, bf16[2,8,64,256]{3,2,1,0:T(8,128)(2,1)S(1)}) custom-call(s32[2]{0:T(128)S(1)} %pad_add_fusion.place_ref, bf16[4,4,32,256]{3,2,1,0:T(8,128)(2,1)} %bitcast.10, bf16[4,8,64,256]{3,2,1,0:T(8,128)(2,1)} %bitcast.7), custom_call_target="tpu_custom_call" | custom-call | tf_op jit(solution)/shard_map/first_messages/pallas_call | solution.py:288
  2.3 1.3 %collective-permute-start.2 = (bf16[2,8,64,256]{3,2,1,0:T(8,128)(2,1)S(1)}, bf16[2,8,64,256]{3,2,1,0:T(8,128)(2,1)S(1)}, u32[]{:S(2)}, u32[]{:S(2)}) collective-permute-start(bf16[2,8,64,256]{3,2,1,0:T(8,128)(2,1)S(1)} %get-tuple-element.34), channel_id=1, source_target_pairs={{4,0},{8,4},{12,8},{5,1},{9,5},{13,9},{6,2},{10,6},{14,10},{7,3},{... | collective-permute-start | bytes 1572872 | tf_op jit(solution)/shard_map/ppermute | solution.py:39
  3.6 3.1 %collective-permute-start = (bf16[4,1,32,256]{3,2,1,0:T(8,128)(2,1)S(1)}, bf16[4,1,32,256]{3,2,1,0:T(8,128)(2,1)S(1)}, u32[]{:S(2)}, u32[]{:S(2)}) collective-permute-start(bf16[4,1,32,256]{3,2,1,0:T(8,128)(2,1)S(1)} %get-tuple-element.28), channel_id=1, source_target_pairs={{0,1},{1,0},{2,3},{3,2},{4,5},{5,4},{6,7},{7,6},{8,9},{9,8},{10,11... | collective-permute-start | bytes 196616 | tf_op jit(solution)/shard_map/ppermute | solution.py:33
  6.7 0.7 collective-permute-start.1
  7.4 0.1 pad_add_fusion.1.place_ref
  7.5 2.0 %load.1 = (bf16[4,4,32,256]{3,2,1,0:T(8,128)(2,1)S(1)}, bf16[3,3,256,256]{3,2,1,0:T(8,128)(2,1)S(1)}, bf16[3,256,256]{2,1,0:T(8,128)(2,1)S(1)}, bf16[4,4,128,256]{3,2,1,0:T(8,128)(2,1)S(1)}) custom-call(bf16[4,4,32,256]{3,2,1,0:T(8,128)(2,1)} %bitcast.11, bf16[4,8,64,256]{3,2,1,0:T(8,128)(2,1)} %bitcast.8, bf16[3,3,256,256]{3,2,1,0:T(8,128)(2,1)} %ws_hbm.1, ...), custom_call_target="tpu_custom_call" | custom-call | flops 536870912 | bytes 4194304 | tf_op jit(solution)/shard_map/load/pallas_call | solution.py:315
  9.4 0.0 copy-start.5
  9.4 0.0 copy-start.8
  9.4 0.0 collective-permute-done.inner_ref
  9.5 0.0 collective-permute-done.1.outer_ref
  9.5 2.9 %forward.1 = (bf16[4,4,128,256]{3,2,1,0:T(8,128)(2,1)S(1)}, f32[4,4,128,256]{3,2,1,0:T(8,128)S(1)}) custom-call(s32[2]{0:T(128)S(1)} %pad_add_fusion.place_ref, bf16[4,4,32,256]{3,2,1,0:T(8,128)(2,1)S(1)} %get-tuple-element.27.low_ref, bf16[4,1,32,256]{3,2,1,0:T(8,128)(2,1)S(1)} %collective-permute-done.inner_ref, ...), custom_call_target="tpu_custom_call" | custom-call | flops 2684354560 | bytes 8388608 | tf_op jit(solution)/shard_map/forward/pallas_call | solution.py:347
  12.4 0.0 copy-start.1
  12.4 0.0 collective-permute-done.2.later_ref
  12.4 0.0 copy-done.8
  12.4 6.5 %backward.1 = (bf16[4,4,128,256]{3,2,1,0:T(8,128)(2,1)S(1)}, bf16[6,4,128,256]{3,2,1,0:T(8,128)(2,1)S(1)}, f32[8,192,256]{2,1,0:T(8,128)S(1)}) custom-call(s32[2]{0:T(128)S(1)} %pad_add_fusion.1.place_ref, bf16[4,4,32,256]{3,2,1,0:T(8,128)(2,1)S(1)} %get-tuple-element.27.low_ref, bf16[4,1,32,256]{3,2,1,0:T(8,128)(2,1)S(1)} %collective-permute-done.inner_ref, ...), custom_call_target="tpu_custom_call" | custom-call | flops 4026531840 | bytes 10485760 | tf_op jit(solution)/shard_map/backward/pallas_call | solution.py:404
  19.0 1.8 %collective-permute-start.3 = (f32[8,192,256]{2,1,0:T(8,128)S(1)}, f32[8,192,256]{2,1,0:T(8,128)S(1)}, u32[]{:S(2)}, u32[]{:S(2)}) collective-permute-start(f32[8,192,256]{2,1,0:T(8,128)S(1)} %get-tuple-element.38), channel_id=1, source_target_pairs={{0,4},{4,0},{1,5},{5,1},{2,6},{6,2},{3,7},{7,3},{8,12},{12,8},{9,1... | collective-permute-start | bytes 4718600 | tf_op jit(solution)/shard_map/ppermute | solution.py:33
  20.7 3.8 %half_grads.1.mine_ref = f32[8,192,256]{2,1,0:T(8,128)S(1)} custom-call(s32[2]{0:T(128)S(1)} %pad_add_fusion.place_ref, bf16[4,4,32,256]{3,2,1,0:T(8,128)(2,1)S(1)} %get-tuple-element.27.low_ref, bf16[4,1,32,256]{3,2,1,0:T(8,128)(2,1)S(1)} %collective-permute-done.inner_ref, bf16[4,1,32,256]{3,2,1,0:T(8,128)(2,1)S(1)} %collective-permute-done.1.outer_ref, ...), custom_call_target="tpu_custom_call" | custom-call | flops 2684354560 | bytes 6291456 | tf_op jit(solution)/shard_map/half_grads/pallas_call | solution.py:423
  24.5 0.0 collective-permute-done.3.theirs_ref
  24.6 1.0 %add_halves.1._ = bf16[8,192,256]{2,1,0:T(8,128)(2,1)} custom-call(f32[8,192,256]{2,1,0:T(8,128)S(1)} %half_grads.1.mine_ref, f32[8,192,256]{2,1,0:T(8,128)S(1)} %collective-permute-done.3.theirs_ref), custom_call_target="tpu_custom_call" | custom-call | tf_op jit(solution)/shard_map/add_halves/pallas_call | solution.py:568
  25.6 6.9 %all-to-all-start = ((bf16[8,192,256]{2,1,0:T(8,128)(2,1)}), bf16[8,192,256]{2,1,0:T(8,128)(2,1)S(1)}, u32[]{:S(2)}, u32[]{:S(2)}) async-start(bf16[8,192,256]{2,1,0:T(8,128)(2,1)} %add_halves.1._), calls=%async_computation | async-start | bytes 1572864 | tf_op jit(solution)/shard_map/all_to_all | solution.py:42
  32.5 0.0 copy-start.6
  32.5 1.2 %edges.1 = (bf16[2,6,32,256]{3,2,1,0:T(8,128)(2,1)S(1)}, bf16[4,2,32,256]{3,2,1,0:T(8,128)(2,1)}, bf16[4,2,32,256]{3,2,1,0:T(8,128)(2,1)S(1)}) custom-call(s32[2]{0:T(128)S(1)} %pad_add_fusion.place_ref, bf16[4,4,32,256]{3,2,1,0:T(8,128)(2,1)S(1)} %get-tuple-element.27.low_ref, bf16[4,1,32,256]{3,2,1,0:T(8,128)(2,1)S(1)} %collective-permute-done.inner_ref, ...), custom_call_target="tpu_custom_call" | custom-call | tf_op jit(solution)/shard_map/edges/pallas_call | solution.py:375
  33.7 2.1 %collective-permute-start.4 = (bf16[2,6,32,256]{3,2,1,0:T(8,128)(2,1)S(1)}, bf16[2,6,32,256]{3,2,1,0:T(8,128)(2,1)S(1)}, u32[]{:S(2)}, u32[]{:S(2)}) collective-permute-start(bf16[2,6,32,256]{3,2,1,0:T(8,128)(2,1)S(1)} %get-tuple-element.39), channel_id=1, source_target_pairs={{0,4},{4,8},{8,12},{1,5},{5,9},{9,13},{2,6},{6,10},{10,14},{3,7},{... | collective-permute-start | bytes 589832 | tf_op jit(solution)/shard_map/ppermute | solution.py:39
  35.8 1.8 %collective-permute-start.5 = (bf16[4,2,32,256]{3,2,1,0:T(8,128)(2,1)}, bf16[4,2,32,256]{3,2,1,0:T(8,128)(2,1)S(1)}, u32[]{:S(2)}, u32[]{:S(2)}) collective-permute-start(bf16[4,2,32,256]{3,2,1,0:T(8,128)(2,1)} %get-tuple-element.41), channel_id=1, source_target_pairs={{0,1},{1,0},{2,3},{3,2},{4,5},{5,4},{6,7},{7,6},{8,9},{9,8},{10,11... | collective-permute-start | bytes 393224 | tf_op jit(solution)/shard_map/ppermute | solution.py:33
  37.6 0.8 %collective-permute-start.6 = (bf16[4,2,32,256]{3,2,1,0:T(8,128)(2,1)S(1)}, bf16[4,2,32,256]{3,2,1,0:T(8,128)(2,1)S(1)}, u32[]{:S(2)}, u32[]{:S(2)}) collective-permute-start(bf16[4,2,32,256]{3,2,1,0:T(8,128)(2,1)S(1)} %get-tuple-element.42), channel_id=1, source_target_pairs={{1,2},{2,1},{5,6},{6,5},{9,10},{10,9},{13,14},{14,13},{17,18},{18,... | collective-permute-start | bytes 393224 | tf_op jit(solution)/shard_map/ppermute | solution.py:48
  38.4 0.0 collective-permute-done.4.low_ref
  38.4 1.0 %earlier_act.1._ = bf16[2,4,128,256]{3,2,1,0:T(8,128)(2,1)S(1)} custom-call(bf16[2,6,32,256]{3,2,1,0:T(8,128)(2,1)S(1)} %collective-permute-done.4.low_ref, bf16[3,3,256,256]{3,2,1,0:T(8,128)(2,1)S(1)} %copy-done.6), custom_call_target="tpu_custom_call" | custom-call | flops 1073741824 | bytes 3145728 | tf_op jit(solution)/shard_map/earlier_act/pallas_call | solution.py:388
  39.5 0.1 pad_maximum_fusion.act_ref
  39.7 6.8 %all-to-all-done.got_ref = bf16[8,192,256]{2,1,0:T(8,128)(2,1)S(1)} async-done(((bf16[8,192,256]{2,1,0:T(8,128)(2,1)}), bf16[8,192,256]{2,1,0:T(8,128)(2,1)S(1)}, u32[]{:S(2)}, u32[]{:S(2)}) %all-to-all-start) | async-done | bytes 786464 | tf_op jit(solution)/shard_map/all_to_all | solution.py:42
  46.4 0.1 sum_parts.1._.own_ref
  46.5 1.8 %collective-permute-start.7 = (bf16[192,256]{1,0:T(8,128)(2,1)S(1)}, bf16[192,256]{1,0:T(8,128)(2,1)S(1)}, u32[]{:S(2)}, u32[]{:S(2)}) collective-permute-start(bf16[192,256]{1,0:T(8,128)(2,1)S(1)} %sum_parts.1._.own_ref), channel_id=1, source_target_pairs={{0,2},{2,0},{1,3},{3,1},{4,6},{6,4},{5,7},{7,5},{8,10},{10,8},{9,1... | collective-permute-start | bytes 294920 | tf_op jit(solution)/shard_map/ppermute | solution.py:33
  48.3 1.0 %copy-done.9 = bf16[3,256,256]{2,1,0:T(8,128)(2,1)S(1)} copy-done((bf16[3,256,256]{2,1,0:T(8,128)(2,1)S(1)}, bf16[3,256,256]{2,1,0:T(8,128)(2,1)}, u32[]{:S(2)}) %copy-start.9) | copy-done | bytes 393240
  49.3 3.2 %section.1 = (bf16[4,8,64,256]{3,2,1,0:T(8,128)(2,1)}, f32[8,128]{1,0:T(8,128)S(1)}) custom-call(bf16[6,4,128,256]{3,2,1,0:T(8,128)(2,1)S(1)} %pad_maximum_fusion.act_ref, bf16[4,4,32,256]{3,2,1,0:T(8,128)(2,1)S(1)} %get-tuple-element.27.low_ref, bf16[3,256,256]{2,1,0:T(8,128)(2,1)S(1)} %copy-done.9, bf16[192,256]{1,0:T(8,128)(2,1)S(1)} %sum_parts.1._.own_ref), custom_call_target="tpu_custom_call" | custom-call | flops 1073741824 | bytes 3145728 | tf_op jit(solution)/shard_map/section/pallas_call | solution.py:462
  52.5 0.0 collective-permute-done.5.refs_1_.inner_ref
  52.5 0.0 collective-permute-done.6.refs_2_.outer_ref
  52.5 1.0 %collective-permute-done.7.theirs_ref = bf16[192,256]{1,0:T(8,128)(2,1)S(1)} collective-permute-done((bf16[192,256]{1,0:T(8,128)(2,1)S(1)}, bf16[192,256]{1,0:T(8,128)(2,1)S(1)}, u32[]{:S(2)}, u32[]{:S(2)}) %collective-permute-start.7) | collective-permute-done | bytes 98336 | tf_op jit(solution)/shard_map/ppermute | solution.py:33
  53.5 0.9 %spread.1._ = bf16[8,192,256]{2,1,0:T(8,128)(2,1)} custom-call(bf16[192,256]{1,0:T(8,128)(2,1)S(1)} %sum_parts.1._.own_ref, bf16[192,256]{1,0:T(8,128)(2,1)S(1)} %collective-permute-done.7.theirs_ref, f32[8,128]{1,0:T(8,128)S(1)} %get-tuple-element.43.refs_0_, bf16[4,2,32,256]{3,2,1,0:T(8,128)(2,1)S(1)} %collective-permute-done.5.refs_1_.inner_ref, ...), custom_call_target="tpu_custom_call" | custom-call | tf_op jit(solution)/shard_map/spread/pallas_call | solution.py:605
  54.5 3.8 %all-to-all-start.1 = ((bf16[8,192,256]{2,1,0:T(8,128)(2,1)}), bf16[8,192,256]{2,1,0:T(8,128)(2,1)S(1)}, u32[]{:S(2)}, u32[]{:S(2)}) async-start(bf16[8,192,256]{2,1,0:T(8,128)(2,1)} %spread.1._), calls=%async_computation.1 | async-start | bytes 1572864 | tf_op jit(solution)/shard_map/all_to_all | solution.py:42
  58.3 0.0 copy-done.4
  58.3 0.0 copy-start.7
  58.3 1.3 %copy-done.7 = bf16[3,3,256,256]{3,2,1,0:T(8,128)(2,1)S(1)} copy-done((bf16[3,3,256,256]{3,2,1,0:T(8,128)(2,1)S(1)}, bf16[3,3,256,256]{3,2,1,0:T(8,128)(2,1)}, u32[]{:S(2)}) %copy-start.7) | copy-done | bytes 1179672
  59.6 5.1 %input_grads.1 = (bf16[4,4,32,256]{3,2,1,0:T(8,128)(2,1)}, f32[8,128]{1,0:T(8,128)S(1)}) custom-call(s32[2]{0:T(128)S(1)} %pad_add_fusion.place_ref, bf16[4,4,128,256]{3,2,1,0:T(8,128)(2,1)S(1)} %copy-done.4, bf16[4,2,32,256]{3,2,1,0:T(8,128)(2,1)S(1)} %collective-permute-done.5.refs_1_.inner_ref, ...), custom_call_target="tpu_custom_call" | custom-call | flops 1610612736 | bytes 4194304 | tf_op jit(solution)/shard_map/input_grads/pallas_call | solution.py:515
  64.6 5.6 %all-to-all-done.1.__0_ = bf16[8,192,256]{2,1,0:T(8,128)(2,1)S(1)} async-done(((bf16[8,192,256]{2,1,0:T(8,128)(2,1)}), bf16[8,192,256]{2,1,0:T(8,128)(2,1)S(1)}, u32[]{:S(2)}, u32[]{:S(2)}) %all-to-all-start.1) | async-done | bytes 786464 | tf_op jit(solution)/shard_map/all_to_all | solution.py:42
  70.2 0.0 collective-permute-start.8
  70.2 1.9 %put.2 = (f32[3,3,256,256]{3,2,1,0:T(8,128)}, f32[3,256,256]{2,1,0:T(8,128)}) custom-call(s32[2]{0:T(128)S(1)} %pad_add_fusion.place_ref, bf16[8,192,256]{2,1,0:T(8,128)(2,1)S(1)} %after.1.half_ref), custom_call_target="tpu_custom_call" | custom-call | tf_op jit(solution)/shard_map/put/pallas_call | solution.py:550
  72.1 0.4 collective-permute-done.8.half_ref
  72.5 1.9 %put.3 = (f32[3,3,256,256]{3,2,1,0:T(8,128)}, f32[3,256,256]{2,1,0:T(8,128)}) custom-call(s32[2]{0:T(128)S(1)} %pad_add_fusion.1.place_ref, bf16[8,192,256]{2,1,0:T(8,128)(2,1)S(1)} %collective-permute-done.8.half_ref, f32[3,3,256,256]{3,2,1,0:T(8,128)} %get-tuple-element.46.refs_0_, ...), custom_call_target="tpu_custom_call", output_to_operand_aliasing={{0}: (2, {}), {1}: (3, {})} | custom-call | tf_op jit(solution)/shard_map/put/pallas_call | solution.py:550
  (12 shorter events, 0.0 us)
Async XLA Ops:
  2.3 10.1 %collective-permute-start.2 = (bf16[2,8,64,256]{3,2,1,0:T(8,128)(2,1)S(1)}, bf16[2,8,64,256]{3,2,1,0:T(8,128)(2,1)S(1)}, u32[]{:S(2)}, u32[]{:S(2)}) collective-permute-start(bf16[2,8,64,256]{3,2,1,0:T(8,128)(2,1)S(1)} %get-tuple-element.34), channel_id=1, source_target_pairs={{4,0},{8,4},{12,8},{5,1},{9,5},{13,9},{6,2},{10,6},{14,10},{7,3},{... | collective-permute-start | bytes 1572872 | tf_op jit(solution)/shard_map/ppermute | solution.py:39
  3.6 5.8 %collective-permute-start = (bf16[4,1,32,256]{3,2,1,0:T(8,128)(2,1)S(1)}, bf16[4,1,32,256]{3,2,1,0:T(8,128)(2,1)S(1)}, u32[]{:S(2)}, u32[]{:S(2)}) collective-permute-start(bf16[4,1,32,256]{3,2,1,0:T(8,128)(2,1)S(1)} %get-tuple-element.28), channel_id=1, source_target_pairs={{0,1},{1,0},{2,3},{3,2},{4,5},{5,4},{6,7},{7,6},{8,9},{9,8},{10,11... | collective-permute-start | bytes 196616 | tf_op jit(solution)/shard_map/ppermute | solution.py:33
  6.7 2.7 %collective-permute-start.1 = (bf16[4,1,32,256]{3,2,1,0:T(8,128)(2,1)S(1)}, bf16[4,1,32,256]{3,2,1,0:T(8,128)(2,1)S(1)}, u32[]{:S(2)}, u32[]{:S(2)}) collective-permute-start(bf16[4,1,32,256]{3,2,1,0:T(8,128)(2,1)S(1)} %get-tuple-element.29), channel_id=1, source_target_pairs={{1,2},{2,1},{5,6},{6,5},{9,10},{10,9},{13,14},{14,13},{17,18},{18,... | collective-permute-start | bytes 196616 | tf_op jit(solution)/shard_map/ppermute | solution.py:48
  9.4 3.0 %copy-start.5 = (bf16[3,3,256,256]{3,2,1,0:T(8,128)(2,1)}, bf16[3,3,256,256]{3,2,1,0:T(8,128)(2,1)S(1)}, u32[]{:S(2)}) copy-start(bf16[3,3,256,256]{3,2,1,0:T(8,128)(2,1)S(1)} %get-tuple-element.30.ws_ref) | copy-start | bytes 3538948
  9.4 3.0 %copy-start.8 = (bf16[3,256,256]{2,1,0:T(8,128)(2,1)}, bf16[3,256,256]{2,1,0:T(8,128)(2,1)S(1)}, u32[]{:S(2)}) copy-start(bf16[3,256,256]{2,1,0:T(8,128)(2,1)S(1)} %get-tuple-element.35.wt_ref) | copy-start | bytes 1179652
  12.4 8.3 %copy-start.1 = (bf16[4,4,128,256]{3,2,1,0:T(8,128)(2,1)}, bf16[4,4,128,256]{3,2,1,0:T(8,128)(2,1)S(1)}, u32[]{:S(2)}) copy-start(bf16[4,4,128,256]{3,2,1,0:T(8,128)(2,1)S(1)} %get-tuple-element.31.act_ref) | copy-start | bytes 3145732
  19.0 13.5 %copy-start.3 = (bf16[4,4,128,256]{3,2,1,0:T(8,128)(2,1)}, bf16[4,4,128,256]{3,2,1,0:T(8,128)(2,1)S(1)}, u32[]{:S(2)}) copy-start(bf16[4,4,128,256]{3,2,1,0:T(8,128)(2,1)S(1)} %get-tuple-element.36.pg_ref) | copy-start | bytes 3145732
  19.0 5.6 %collective-permute-start.3 = (f32[8,192,256]{2,1,0:T(8,128)S(1)}, f32[8,192,256]{2,1,0:T(8,128)S(1)}, u32[]{:S(2)}, u32[]{:S(2)}) collective-permute-start(f32[8,192,256]{2,1,0:T(8,128)S(1)} %get-tuple-element.38), channel_id=1, source_target_pairs={{0,4},{4,0},{1,5},{5,1},{2,6},{6,2},{3,7},{7,3},{8,12},{12,8},{9,1... | collective-permute-start | bytes 4718600 | tf_op jit(solution)/shard_map/ppermute | solution.py:33
  25.6 20.8 %all-to-all-start = ((bf16[8,192,256]{2,1,0:T(8,128)(2,1)}), bf16[8,192,256]{2,1,0:T(8,128)(2,1)S(1)}, u32[]{:S(2)}, u32[]{:S(2)}) async-start(bf16[8,192,256]{2,1,0:T(8,128)(2,1)} %add_halves.1._), calls=%async_computation | async-start | bytes 1572864 | tf_op jit(solution)/shard_map/all_to_all | solution.py:42
  32.5 6.0 %copy-start.6 = (bf16[3,3,256,256]{3,2,1,0:T(8,128)(2,1)S(1)}, bf16[3,3,256,256]{3,2,1,0:T(8,128)(2,1)}, u32[]{:S(2)}) copy-start(bf16[3,3,256,256]{3,2,1,0:T(8,128)(2,1)} %copy-done.5) | copy-start | bytes 3538948
  33.7 4.7 %collective-permute-start.4 = (bf16[2,6,32,256]{3,2,1,0:T(8,128)(2,1)S(1)}, bf16[2,6,32,256]{3,2,1,0:T(8,128)(2,1)S(1)}, u32[]{:S(2)}, u32[]{:S(2)}) collective-permute-start(bf16[2,6,32,256]{3,2,1,0:T(8,128)(2,1)S(1)} %get-tuple-element.39), channel_id=1, source_target_pairs={{0,4},{4,8},{8,12},{1,5},{5,9},{9,13},{2,6},{6,10},{10,14},{3,7},{... | collective-permute-start | bytes 589832 | tf_op jit(solution)/shard_map/ppermute | solution.py:39
  35.8 16.7 %collective-permute-start.5 = (bf16[4,2,32,256]{3,2,1,0:T(8,128)(2,1)}, bf16[4,2,32,256]{3,2,1,0:T(8,128)(2,1)S(1)}, u32[]{:S(2)}, u32[]{:S(2)}) collective-permute-start(bf16[4,2,32,256]{3,2,1,0:T(8,128)(2,1)} %get-tuple-element.41), channel_id=1, source_target_pairs={{0,1},{1,0},{2,3},{3,2},{4,5},{5,4},{6,7},{7,6},{8,9},{9,8},{10,11... | collective-permute-start | bytes 393224 | tf_op jit(solution)/shard_map/ppermute | solution.py:33
  37.6 1.9 %copy-start.2 = (bf16[4,4,128,256]{3,2,1,0:T(8,128)(2,1)S(1)}, bf16[4,4,128,256]{3,2,1,0:T(8,128)(2,1)}, u32[]{:S(2)}) copy-start(bf16[4,4,128,256]{3,2,1,0:T(8,128)(2,1)} %copy-done.1) | copy-start | bytes 3145732
  37.6 14.9 %collective-permute-start.6 = (bf16[4,2,32,256]{3,2,1,0:T(8,128)(2,1)S(1)}, bf16[4,2,32,256]{3,2,1,0:T(8,128)(2,1)S(1)}, u32[]{:S(2)}, u32[]{:S(2)}) collective-permute-start(bf16[4,2,32,256]{3,2,1,0:T(8,128)(2,1)S(1)} %get-tuple-element.42), channel_id=1, source_target_pairs={{1,2},{2,1},{5,6},{6,5},{9,10},{10,9},{13,14},{14,13},{17,18},{18,... | collective-permute-start | bytes 393224 | tf_op jit(solution)/shard_map/ppermute | solution.py:48
  46.5 7.0 %collective-permute-start.7 = (bf16[192,256]{1,0:T(8,128)(2,1)S(1)}, bf16[192,256]{1,0:T(8,128)(2,1)S(1)}, u32[]{:S(2)}, u32[]{:S(2)}) collective-permute-start(bf16[192,256]{1,0:T(8,128)(2,1)S(1)} %sum_parts.1._.own_ref), channel_id=1, source_target_pairs={{0,2},{2,0},{1,3},{3,1},{4,6},{6,4},{5,7},{7,5},{8,10},{10,8},{9,1... | collective-permute-start | bytes 294920 | tf_op jit(solution)/shard_map/ppermute | solution.py:33
  48.3 1.0 %copy-start.9 = (bf16[3,256,256]{2,1,0:T(8,128)(2,1)S(1)}, bf16[3,256,256]{2,1,0:T(8,128)(2,1)}, u32[]{:S(2)}) copy-start(bf16[3,256,256]{2,1,0:T(8,128)(2,1)} %copy-done.8) | copy-start | bytes 1179652
  52.5 5.7 %copy-start = (bf16[1,4,8,64,256]{4,3,2,1,0:T(8,128)(2,1)S(1)}, bf16[1,4,8,64,256]{4,3,2,1,0:T(8,128)(2,1)}, u32[]{:S(2)}) copy-start(bf16[1,4,8,64,256]{4,3,2,1,0:T(8,128)(2,1)} %param.7) | copy-start | bytes 3145732
  52.5 5.8 %copy-start.4 = (bf16[4,4,128,256]{3,2,1,0:T(8,128)(2,1)S(1)}, bf16[4,4,128,256]{3,2,1,0:T(8,128)(2,1)}, u32[]{:S(2)}) copy-start(bf16[4,4,128,256]{3,2,1,0:T(8,128)(2,1)} %copy-done.3) | copy-start | bytes 3145732
  54.5 15.7 %all-to-all-start.1 = ((bf16[8,192,256]{2,1,0:T(8,128)(2,1)}), bf16[8,192,256]{2,1,0:T(8,128)(2,1)S(1)}, u32[]{:S(2)}, u32[]{:S(2)}) async-start(bf16[8,192,256]{2,1,0:T(8,128)(2,1)} %spread.1._), calls=%async_computation.1 | async-start | bytes 1572864 | tf_op jit(solution)/shard_map/all_to_all | solution.py:42
  58.3 1.3 %copy-start.7 = (bf16[3,3,256,256]{3,2,1,0:T(8,128)(2,1)S(1)}, bf16[3,3,256,256]{3,2,1,0:T(8,128)(2,1)}, u32[]{:S(2)}) copy-start(bf16[3,3,256,256]{3,2,1,0:T(8,128)(2,1)} %copy-done.5) | copy-start | bytes 3538948
  70.2 2.3 %collective-permute-start.8 = (bf16[8,192,256]{2,1,0:T(8,128)(2,1)S(1)}, bf16[8,192,256]{2,1,0:T(8,128)(2,1)S(1)}, u32[]{:S(2)}, u32[]{:S(2)}) collective-permute-start(bf16[8,192,256]{2,1,0:T(8,128)(2,1)S(1)} %after.1.half_ref), channel_id=1, source_target_pairs={{0,4},{4,0},{1,5},{5,1},{2,6},{6,2},{3,7},{7,3},{8,12},{12,8},{9,1... | collective-permute-start | bytes 2359304 | tf_op jit(solution)/shard_map/ppermute | solution.py:33

commit v5 on v4

--- a/solution.py
+++ b/solution.py
@@ -18,10 +18,10 @@
         names = [bit for bits in self.axes.values() for bit in bits]
         self.mesh = Mesh(mesh.devices.reshape([2] * len(names)), tuple(names))
         self.core = next((n for n in names if self.same_chip(n)), self.axes["tm"][-1])
-        self.near = []
-        for bits in self.axes.values():
-            self.near += [b for b in bits if b != self.core][-1:]
-        self.far = [n for n in names if n != self.core and n not in self.near]
+        others = [[b for b in reversed(bits) if b != self.core] for bits in self.axes.values()]
+        turns = [bits[turn] for turn in range(len(names)) for bits in others if turn < len(bits)]
+        self.near = [n for n in names if n in turns[:4]]
+        self.far = turns[4:]
 
     def same_chip(self, name):
         at = [1 if n == name else 0 for n in self.mesh.axis_names]
@@ -49,9 +49,10 @@
         return self.swap(inner, axes[-1]), outer
 
     def far_sums(self, total):
-        for axis in self.far[:-1]:
-            total = (total.astype(jnp.float32) + self.swap(total, axis).astype(jnp.float32)).astype(jnp.bfloat16)
-        return total, self.swap(total, self.far[-1])
+        for axis in self.far:
+            total = total.astype(jnp.float32) + self.swap(total, axis).astype(jnp.float32)
+            total = lax.reduce_precision(total, 8, 7).astype(jnp.bfloat16)
+        return total
 
 
 SIDES = ((0, 0), (0, 1), (1, 0), (1, 1))
@@ -179,26 +180,15 @@
     for cot in cots:
         sums.append(product(act, cot))
 
-    def each_piece(store):
-        parts = out_ref.shape[0]
-        size = half // parts
-        for tap, value in enumerate(sums):
-            for n in range(parts):
-                store(n, slice(tap * size, (tap + 1) * size), value[n * size : (n + 1) * size])
-
     @pl.when(pl.program_id(0) == 0)
     def _():
-        def store(n, rows, value):
-            out_ref[n, rows, :] = value
-
-        each_piece(store)
+        for tap, value in enumerate(sums):
+            out_ref[tap] = value
 
     @pl.when(pl.program_id(0) > 0)
     def _():
-        def store(n, rows, value):
-            out_ref[n, rows, :] += value
-
-        each_piece(store)
+        for tap, value in enumerate(sums):
+            out_ref[tap] += value
 
 
 def backward_kernel(place_ref, low_ref, inner_ref, outer_ref, act_ref, slope_ref, cot_ref, later_ref, wt_ref, pg_ref, ext_ref, out_ref):
@@ -397,10 +387,10 @@
     )(low, ws)
 
 
-def backward(place, parts, low, inner, outer, act, slope, cot, later, wt):
+def backward(place, low, inner, outer, act, slope, cot, later, wt):
     frames, _, count, chan = act.shape
     ext = (frames + 2,) + act.shape[1:]
-    piece = (parts, 12 * (chan // (2 * parts)), chan)
+    half = (12, chan // 2, chan)
     return pl.pallas_call(
         backward_kernel,
         grid_spec=pltpu.PrefetchScalarGridSpec(
@@ -408,18 +398,18 @@
             grid=(frames,),
             in_specs=[half_of(low.shape), half_of(inner.shape), half_of(outer.shape), half_of(act.shape),
                       each(slope.shape), whole(cot.shape), whole(later.shape), whole(wt.shape)],
-            out_specs=[each(act.shape), whole(ext), whole(piece)],
+            out_specs=[each(act.shape), whole(ext), whole(half)],
         ),
-        out_shape=[like(act.shape, jnp.bfloat16), like(ext, jnp.bfloat16), like(piece, jnp.float32)],
+        out_shape=[like(act.shape, jnp.bfloat16), like(ext, jnp.bfloat16), like(half, jnp.float32)],
         compiler_params=grant(28),
         cost_estimate=cost(15, 10),
         name="backward",
     )(place, low, inner, outer, act, slope, cot, later, wt)
 
 
-def half_grads(place, parts, low, inner, outer, act, pg, ext):
+def half_grads(place, low, inner, outer, act, pg, ext):
     frames, _, _, chan = act.shape
-    piece = (parts, 12 * (chan // (2 * parts)), chan)
+    half = (12, chan // 2, chan)
     return pl.pallas_call(
         half_kernel,
         grid_spec=pltpu.PrefetchScalarGridSpec(
@@ -427,9 +417,9 @@
             grid=(frames,),
             in_specs=[half_of(low.shape), half_of(inner.shape), half_of(outer.shape), half_of(act.shape),
                       each(pg.shape), whole(ext.shape)],
-            out_specs=whole(piece),
+            out_specs=whole(half),
         ),
-        out_shape=like(piece, jnp.float32),
+        out_shape=like(half, jnp.float32),
         compiler_params=grant(24),
         cost_estimate=cost(10, 6),
         name="half_grads",
@@ -526,14 +516,11 @@
 
 def put_kernel(place_ref, half_ref, *refs):
     spatial_ref, temporal_ref, wide, sems = refs[-4:]
-    parts, rows, chan = half_ref.shape
-    size, half = rows // 12, chan // 2
-    for tap in range(12):
-        for n in range(parts):
-            wide[tap, n * size : (n + 1) * size, :] = half_ref[n, tap * size : (tap + 1) * size, :].astype(jnp.float32)
+    taps, half, _ = half_ref.shape
     to = pl.ds(pl.multiple_of(place_ref[0] * half, half), half)
     copies = []
-    for tap in range(12):
+    for tap in range(taps):
+        wide[tap] = half_ref[tap].astype(jnp.float32)
         if tap < 9:
             target = spatial_ref.at[tap // 3, tap % 3, to]
         else:
@@ -579,37 +566,20 @@
     total = got_ref[0].astype(jnp.float32)
     for n in range(1, got_ref.shape[0]):
         total = total + got_ref[n].astype(jnp.float32)
-    out_ref[...] = total.astype(jnp.bfloat16)
-
-
-def sum_parts(got, before):
-    full = pl.BlockSpec(memory_space=pltpu.VMEM)
+    total = total.astype(jnp.bfloat16)
+    for n in range(out_ref.shape[0]):
+        out_ref[n] = total
+
+
+def sum_parts(got, copies, before):
     return pl.pallas_call(
         sum_kernel,
-        in_specs=[full, UNREAD],
-        out_specs=full,
-        out_shape=like(got.shape[1:], jnp.bfloat16),
+        in_specs=[FULL, UNREAD],
+        out_specs=FULL,
+        out_shape=like((copies,) + got.shape[1:], jnp.bfloat16),
         compiler_params=grant(4),
         name="sum_parts",
     )(got, before)
-
-
-def spread_kernel(own_ref, theirs_ref, *refs):
-    total = (own_ref[...].astype(jnp.float32) + theirs_ref[...].astype(jnp.float32)).astype(jnp.bfloat16)
-    for n in range(refs[-1].shape[0]):
-        refs[-1][n] = total
-
-
-def spread(own, theirs, parts, *before):
-    full = pl.BlockSpec(memory_space=pltpu.VMEM)
-    return pl.pallas_call(
-        spread_kernel,
-        in_specs=[full, full] + [UNREAD] * len(before),
-        out_specs=full,
-        out_shape=like((parts,) + own.shape, jnp.bfloat16),
-        compiler_params=grant(4),
-        name="spread",
-    )(own, theirs, *before)
 
 
 def on_device(bits, low_frames, spatial_weight, temporal_weight, cotangent):
@@ -625,19 +595,22 @@
     inner, outer = bits.pairs(inner, outer)
     low, ws, wt, cot_side = load(low, cot, spatial_weight, temporal_weight)
     act, slope = forward(mine, low, inner, outer, ws)
-    pg, ext, theirs = backward(other, parts, low, inner, outer, act, slope, cot_side, later, wt)
+    pg, ext, theirs = backward(other, low, inner, outer, act, slope, cot_side, later, wt)
     theirs = bits.swap(theirs, bits.core)
-    own = half_grads(mine, parts, low, inner, outer, act, pg, ext)
+    own = half_grads(mine, low, inner, outer, act, pg, ext)
     kept = add_halves(own, theirs)
-    got = bits.exchange(kept)
+    got = bits.exchange(kept.reshape(parts, -1, chan))
     edge, pg_inner, pg_outer = edges(mine, low, inner, outer, pg, kept)
     earlier = earlier_act(bits.shift(edge, "tm", 1), ws)
     pg_inner, pg_outer = bits.pairs(pg_inner, pg_outer)
-    total, far = bits.far_sums(sum_parts(got, earlier))
-    section_out, section_done = section(jnp.concatenate([earlier, act], axis=0), low, wt, total)
-    totals = spread(total, far, parts, section_done, pg_inner, pg_outer)
+    if bits.far:
+        total = bits.far_sums(sum_parts(got, 1, earlier)[0])
+        totals = jnp.broadcast_to(total, got.shape)
+    else:
+        totals = sum_parts(got, parts, earlier)
+    section_out, section_done = section(jnp.concatenate([earlier, act], axis=0), low, wt, totals)
     input_grad, input_done = input_grads(mine, pg, pg_inner, pg_outer, cot, ws, totals, low.shape)
-    half, = after([bits.exchange(totals)], input_done)
+    half, = after([bits.exchange(totals).reshape(kept.shape)], section_done, input_done)
     theirs = bits.swap(half, bits.core)
     spatial_grad, temporal_grad = put(other, theirs, *put(mine, half))
     return section_out[None], input_grad[None], spatial_grad, temporal_grad

time: 74.8 us -> 90.6 us (1.21)
  the two profiles are of different devices: /device:TPU:0 before, /device:TPU:9 now
where the time goes in v5:
time: 90.6 us; the launch traced here: 90.2 us
  Pallas kernels  32.3 us (36%)
  starting transfers between devices  30.3 us (33%)
  waiting for transfers between devices  26.3 us (29%)
    all_to_all x2, starting transfers between devices, exchange(): return lax.all_to_all(parts, tuple(self.near), 0, 0, tiled=True)  13.3 us
    ppermute x2, starting transfers between devices, pairs(): outer = lax.ppermute(outer, axes, route)  8.61 us
    all_to_all x2, waiting for transfers between devices, exchange(): return lax.all_to_all(parts, tuple(self.near), 0, 0, tiled=True)  8.48 us
    ppermute x4, waiting for transfers between devices, swap(): return lax.ppermute(block, axis, [(0, 1), (1, 0)])  7.46 us
    pallas_call x1, Pallas kernels, backward(): pl.pallas_call(backward_kernel, grid_spec=pltpu.PrefetchScalarGridSpec(nu...  6.51 us
    ppermute x2, waiting for transfers between devices, pairs(): outer = lax.ppermute(outer, axes, route)  6.36 us
    ppermute x2, starting transfers between devices, shift(): return lax.ppermute(block, axes, route)  6.15 us
    pallas_call x1, Pallas kernels, input_grads(): pl.pallas_call(input_kernel, grid=(low_shape[0],), in_specs=[SCALAR, each...  5.16 us
  transfers between devices with their start and end apart: 10, of which 6 were waited for; matrix products, arithmetic and copies ran while one was open for 0% of the time, Pallas kernels for 23%

profile of v5, /device:TPU:9, one launch (start us, length us, event | category | flops | bytes accessed | tf_op | source)
XLA Modules:
  0.0 90.2 jit_solution(922892683850571395)
XLA Ops:
  0.6 0.1 pad_add_fusion.place_ref
  0.7 1.6 %first_messages.1 = (bf16[4,1,32,256]{3,2,1,0:T(8,128)(2,1)S(1)}, bf16[4,1,32,256]{3,2,1,0:T(8,128)(2,1)S(1)}, bf16[2,8,64,256]{3,2,1,0:T(8,128)(2,1)S(1)}) custom-call(s32[2]{0:T(128)S(1)} %pad_add_fusion.place_ref, bf16[4,4,32,256]{3,2,1,0:T(8,128)(2,1)} %bitcast.13, bf16[4,8,64,256]{3,2,1,0:T(8,128)(2,1)} %bitcast.10), custom_call_target="tpu_custom_call" | custom-call | tf_op jit(solution)/shard_map/first_messages/pallas_call | solution.py:278
  2.3 2.6 %collective-permute-start.2 = (bf16[2,8,64,256]{3,2,1,0:T(8,128)(2,1)S(1)}, bf16[2,8,64,256]{3,2,1,0:T(8,128)(2,1)S(1)}, u32[]{:S(2)}, u32[]{:S(2)}) collective-permute-start(bf16[2,8,64,256]{3,2,1,0:T(8,128)(2,1)S(1)} %get-tuple-element.34), channel_id=1, source_target_pairs={{4,0},{8,4},{12,8},{5,1},{9,5},{13,9},{6,2},{10,6},{14,10},{7,3},{... | collective-permute-start | bytes 1572872 | tf_op jit(solution)/shard_map/ppermute | solution.py:39
  4.9 0.1 collective-permute-start
  5.0 4.5 %collective-permute-start.1 = (bf16[4,1,32,256]{3,2,1,0:T(8,128)(2,1)S(1)}, bf16[4,1,32,256]{3,2,1,0:T(8,128)(2,1)S(1)}, u32[]{:S(2)}, u32[]{:S(2)}) collective-permute-start(bf16[4,1,32,256]{3,2,1,0:T(8,128)(2,1)S(1)} %get-tuple-element.29), channel_id=1, source_target_pairs={{1,2},{2,1},{5,6},{6,5},{9,10},{10,9},{13,14},{14,13},{17,18},{18,... | collective-permute-start | bytes 196616 | tf_op jit(solution)/shard_map/ppermute | solution.py:48
  9.5 0.1 pad_add_fusion.1.place_ref
  9.6 1.9 %load.1 = (bf16[4,4,32,256]{3,2,1,0:T(8,128)(2,1)S(1)}, bf16[3,3,256,256]{3,2,1,0:T(8,128)(2,1)S(1)}, bf16[3,256,256]{2,1,0:T(8,128)(2,1)S(1)}, bf16[4,4,128,256]{3,2,1,0:T(8,128)(2,1)S(1)}) custom-call(bf16[4,4,32,256]{3,2,1,0:T(8,128)(2,1)} %bitcast.14, bf16[4,8,64,256]{3,2,1,0:T(8,128)(2,1)} %bitcast.11, bf16[3,3,256,256]{3,2,1,0:T(8,128)(2,1)} %ws_hbm.1, ...), custom_call_target="tpu_custom_call" | custom-call | flops 536870912 | bytes 4194304 | tf_op jit(solution)/shard_map/load/pallas_call | solution.py:305
  11.5 0.0 copy-start.3
  11.5 0.0 copy-start.6
  11.5 0.0 copy-start.1
  11.6 0.0 collective-permute-done.inner_ref
  11.6 0.2 collective-permute-done.1.outer_ref
  11.8 2.9 %forward.1 = (bf16[4,4,128,256]{3,2,1,0:T(8,128)(2,1)S(1)}, f32[4,4,128,256]{3,2,1,0:T(8,128)S(1)}) custom-call(s32[2]{0:T(128)S(1)} %pad_add_fusion.place_ref, bf16[4,4,32,256]{3,2,1,0:T(8,128)(2,1)S(1)} %get-tuple-element.27.low_ref, bf16[4,1,32,256]{3,2,1,0:T(8,128)(2,1)S(1)} %collective-permute-done.inner_ref, ...), custom_call_target="tpu_custom_call" | custom-call | flops 2684354560 | bytes 8388608 | tf_op jit(solution)/shard_map/forward/pallas_call | solution.py:337
  14.7 0.0 copy-done.3
  14.7 0.0 collective-permute-done.2.later_ref
  14.7 0.0 copy-done.6
  14.8 6.5 %backward.1 = (bf16[4,4,128,256]{3,2,1,0:T(8,128)(2,1)S(1)}, bf16[6,4,128,256]{3,2,1,0:T(8,128)(2,1)S(1)}, f32[12,128,256]{2,1,0:T(8,128)S(1)}) custom-call(s32[2]{0:T(128)S(1)} %pad_add_fusion.1.place_ref, bf16[4,4,32,256]{3,2,1,0:T(8,128)(2,1)S(1)} %get-tuple-element.27.low_ref, bf16[4,1,32,256]{3,2,1,0:T(8,128)(2,1)S(1)} %collective-permute-done.inner_ref, ...), custom_call_target="tpu_custom_call" | custom-call | flops 4026531840 | bytes 10485760 | tf_op jit(solution)/shard_map/backward/pallas_call | solution.py:394
  21.3 0.5 collective-permute-start.3
  21.7 3.8 %half_grads.1.mine_ref = f32[12,128,256]{2,1,0:T(8,128)S(1)} custom-call(s32[2]{0:T(128)S(1)} %pad_add_fusion.place_ref, bf16[4,4,32,256]{3,2,1,0:T(8,128)(2,1)S(1)} %get-tuple-element.27.low_ref, bf16[4,1,32,256]{3,2,1,0:T(8,128)(2,1)S(1)} %collective-permute-done.inner_ref, bf16[4,1,32,256]{3,2,1,0:T(8,128)(2,1)S(1)} %collective-permute-done.1.outer_ref, ...), custom_call_target="tpu_custom_call" | custom-call | flops 2684354560 | bytes 6291456 | tf_op jit(solution)/shard_map/half_grads/pallas_call | solution.py:413
  25.5 0.0 collective-permute-done.3.theirs_ref
  25.5 1.0 %add_halves.1._ = bf16[12,128,256]{2,1,0:T(8,128)(2,1)} custom-call(f32[12,128,256]{2,1,0:T(8,128)S(1)} %half_grads.1.mine_ref, f32[12,128,256]{2,1,0:T(8,128)S(1)} %collective-permute-done.3.theirs_ref), custom_call_target="tpu_custom_call" | custom-call | tf_op jit(solution)/shard_map/add_halves/pallas_call | solution.py:555
  26.6 6.2 %all-to-all-start = ((bf16[16,96,256]{2,1,0:T(8,128)(2,1)}), bf16[16,96,256]{2,1,0:T(8,128)(2,1)S(1)}, u32[]{:S(2)}, u32[]{:S(2)}) async-start(bf16[16,96,256]{2,1,0:T(8,128)(2,1)} %bitcast.5), calls=%async_computation | async-start | bytes 1572864 | tf_op jit(solution)/shard_map/all_to_all | solution.py:42
  32.7 0.0 copy-done.1
  32.7 0.0 copy-start.4
  32.7 0.6 edges.1
  33.3 0.0 copy-start.8
  33.3 3.6 %collective-permute-start.4 = (bf16[2,6,32,256]{3,2,1,0:T(8,128)(2,1)S(1)}, bf16[2,6,32,256]{3,2,1,0:T(8,128)(2,1)S(1)}, u32[]{:S(2)}, u32[]{:S(2)}) collective-permute-start(bf16[2,6,32,256]{3,2,1,0:T(8,128)(2,1)S(1)} %get-tuple-element.39), channel_id=1, source_target_pairs={{0,4},{4,8},{8,12},{1,5},{5,9},{9,13},{2,6},{6,10},{10,14},{3,7},{... | collective-permute-start | bytes 589832 | tf_op jit(solution)/shard_map/ppermute | solution.py:39
  36.9 4.0 %collective-permute-done.4.low_ref = bf16[2,6,32,256]{3,2,1,0:T(8,128)(2,1)S(1)} collective-permute-done((bf16[2,6,32,256]{3,2,1,0:T(8,128)(2,1)S(1)}, bf16[2,6,32,256]{3,2,1,0:T(8,128)(2,1)S(1)}, u32[]{:S(2)}, u32[]{:S(2)}) %collective-permute-start.4) | collective-permute-done | bytes 196640 | tf_op jit(solution)/shard_map/ppermute | solution.py:39
  40.9 0.0 copy-done.4
  41.0 1.0 %earlier_act.1._ = bf16[2,4,128,256]{3,2,1,0:T(8,128)(2,1)S(1)} custom-call(bf16[2,6,32,256]{3,2,1,0:T(8,128)(2,1)S(1)} %collective-permute-done.4.low_ref, bf16[3,3,256,256]{3,2,1,0:T(8,128)(2,1)S(1)} %copy-done.4), custom_call_target="tpu_custom_call" | custom-call | flops 1073741824 | bytes 3145728 | tf_op jit(solution)/shard_map/earlier_act/pallas_call | solution.py:378
  42.0 8.5 %all-to-all-done.got_ref = bf16[16,96,256]{2,1,0:T(8,128)(2,1)S(1)} async-done(((bf16[16,96,256]{2,1,0:T(8,128)(2,1)}), bf16[16,96,256]{2,1,0:T(8,128)(2,1)S(1)}, u32[]{:S(2)}, u32[]{:S(2)}) %all-to-all-start) | async-done | bytes 786464 | tf_op jit(solution)/shard_map/all_to_all | solution.py:42
  50.5 1.0 %sum_parts.1._ = bf16[16,96,256]{2,1,0:T(8,128)(2,1)} custom-call(bf16[16,96,256]{2,1,0:T(8,128)(2,1)S(1)} %all-to-all-done.got_ref, bf16[2,4,128,256]{3,2,1,0:T(8,128)(2,1)S(1)} %earlier_act.1._), custom_call_target="tpu_custom_call" | custom-call | tf_op jit(solution)/shard_map/sum_parts/pallas_call | solution.py:575
  51.5 7.2 %all-to-all-start.1 = ((bf16[16,96,256]{2,1,0:T(8,128)(2,1)}), bf16[16,96,256]{2,1,0:T(8,128)(2,1)S(1)}, u32[]{:S(2)}, u32[]{:S(2)}) async-start(bf16[16,96,256]{2,1,0:T(8,128)(2,1)} %sum_parts.1._), calls=%async_computation.1 | async-start | bytes 1572864 | tf_op jit(solution)/shard_map/all_to_all | solution.py:42
  58.7 0.3 collective-permute-start.5
  58.9 4.1 %collective-permute-start.6 = (bf16[4,2,32,256]{3,2,1,0:T(8,128)(2,1)S(1)}, bf16[4,2,32,256]{3,2,1,0:T(8,128)(2,1)S(1)}, u32[]{:S(2)}, u32[]{:S(2)}) collective-permute-start(bf16[4,2,32,256]{3,2,1,0:T(8,128)(2,1)S(1)} %get-tuple-element.42), channel_id=1, source_target_pairs={{1,2},{2,1},{5,6},{6,5},{9,10},{10,9},{13,14},{14,13},{17,18},{18,... | collective-permute-start | bytes 393224 | tf_op jit(solution)/shard_map/ppermute | solution.py:48
  63.1 0.1 pad_maximum_fusion.act_ref
  63.2 0.0 copy-start
  63.2 0.0 copy-start.5
  63.3 3.2 %section.1 = (bf16[4,8,64,256]{3,2,1,0:T(8,128)(2,1)}, f32[8,128]{1,0:T(8,128)S(1)}) custom-call(bf16[6,4,128,256]{3,2,1,0:T(8,128)(2,1)S(1)} %pad_maximum_fusion.act_ref, bf16[4,4,32,256]{3,2,1,0:T(8,128)(2,1)S(1)} %copy-done.2, bf16[3,256,256]{2,1,0:T(8,128)(2,1)S(1)} %copy-done.7, bf16[16,96,256]{2,1,0:T(8,128)(2,1)} %sum_parts.1._), custom_call_target="tpu_custom_call" | custom-call | flops 1073741824 | bytes 3145728 | tf_op jit(solution)/shard_map/section/pallas_call | solution.py:452
  66.4 7.3 %collective-permute-done.5.inner_ref = bf16[4,2,32,256]{3,2,1,0:T(8,128)(2,1)S(1)} collective-permute-done((bf16[4,2,32,256]{3,2,1,0:T(8,128)(2,1)}, bf16[4,2,32,256]{3,2,1,0:T(8,128)(2,1)S(1)}, u32[]{:S(2)}, u32[]{:S(2)}) %collective-permute-start.5) | collective-permute-done | bytes 131104 | tf_op jit(solution)/shard_map/ppermute | solution.py:33
  73.8 6.1 %collective-permute-done.6.outer_ref = bf16[4,2,32,256]{3,2,1,0:T(8,128)(2,1)S(1)} collective-permute-done((bf16[4,2,32,256]{3,2,1,0:T(8,128)(2,1)S(1)}, bf16[4,2,32,256]{3,2,1,0:T(8,128)(2,1)S(1)}, u32[]{:S(2)}, u32[]{:S(2)}) %collective-permute-start.6) | collective-permute-done | bytes 131104 | tf_op jit(solution)/shard_map/ppermute | solution.py:48
  79.9 0.0 copy-done.5
  79.9 5.2 %input_grads.1 = (bf16[4,4,32,256]{3,2,1,0:T(8,128)(2,1)}, f32[8,128]{1,0:T(8,128)S(1)}) custom-call(s32[2]{0:T(128)S(1)} %pad_add_fusion.place_ref, bf16[4,4,128,256]{3,2,1,0:T(8,128)(2,1)S(1)} %get-tuple-element.36.pg_ref, bf16[4,2,32,256]{3,2,1,0:T(8,128)(2,1)S(1)} %collective-permute-done.5.inner_ref, ...), custom_call_target="tpu_custom_call" | custom-call | flops 1610612736 | bytes 4194304 | tf_op jit(solution)/shard_map/input_grads/pallas_call | solution.py:505
  85.1 0.0 all-to-all-done.1
  85.1 1.5 %collective-permute-start.7 = (bf16[12,128,256]{2,1,0:T(8,128)(2,1)S(1)}, bf16[12,128,256]{2,1,0:T(8,128)(2,1)S(1)}, u32[]{:S(2)}, u32[]{:S(2)}) collective-permute-start(bf16[12,128,256]{2,1,0:T(8,128)(2,1)S(1)} %after.1.half_ref), channel_id=1, source_target_pairs={{0,4},{4,0},{1,5},{5,1},{2,6},{6,2},{3,7},{7,3},{8,12},{12,8},{9,1... | collective-permute-start | bytes 2359304 | tf_op jit(solution)/shard_map/ppermute | solution.py:33
  86.5 1.8 %put.2 = (f32[3,3,256,256]{3,2,1,0:T(8,128)}, f32[3,256,256]{2,1,0:T(8,128)}) custom-call(s32[2]{0:T(128)S(1)} %pad_add_fusion.place_ref, bf16[12,128,256]{2,1,0:T(8,128)(2,1)S(1)} %after.1.half_ref), custom_call_target="tpu_custom_call" | custom-call | tf_op jit(solution)/shard_map/put/pallas_call | solution.py:537
  88.3 0.1 collective-permute-done.7.half_ref
  88.4 1.8 %put.3 = (f32[3,3,256,256]{3,2,1,0:T(8,128)}, f32[3,256,256]{2,1,0:T(8,128)}) custom-call(s32[2]{0:T(128)S(1)} %pad_add_fusion.1.place_ref, bf16[12,128,256]{2,1,0:T(8,128)(2,1)S(1)} %collective-permute-done.7.half_ref, f32[3,3,256,256]{3,2,1,0:T(8,128)} %get-tuple-element.46.refs_0_, ...), custom_call_target="tpu_custom_call", output_to_operand_aliasing={{0}: (2, {}), {1}: (3, {})} | custom-call | tf_op jit(solution)/shard_map/put/pallas_call | solution.py:537
  (7 shorter events, 0.0 us)
Async XLA Ops:
  2.3 12.4 %collective-permute-start.2 = (bf16[2,8,64,256]{3,2,1,0:T(8,128)(2,1)S(1)}, bf16[2,8,64,256]{3,2,1,0:T(8,128)(2,1)S(1)}, u32[]{:S(2)}, u32[]{:S(2)}) collective-permute-start(bf16[2,8,64,256]{3,2,1,0:T(8,128)(2,1)S(1)} %get-tuple-element.34), channel_id=1, source_target_pairs={{4,0},{8,4},{12,8},{5,1},{9,5},{13,9},{6,2},{10,6},{14,10},{7,3},{... | collective-permute-start | bytes 1572872 | tf_op jit(solution)/shard_map/ppermute | solution.py:39
  4.9 6.6 %collective-permute-start = (bf16[4,1,32,256]{3,2,1,0:T(8,128)(2,1)S(1)}, bf16[4,1,32,256]{3,2,1,0:T(8,128)(2,1)S(1)}, u32[]{:S(2)}, u32[]{:S(2)}) collective-permute-start(bf16[4,1,32,256]{3,2,1,0:T(8,128)(2,1)S(1)} %get-tuple-element.28), channel_id=1, source_target_pairs={{0,1},{1,0},{2,3},{3,2},{4,5},{5,4},{6,7},{7,6},{8,9},{9,8},{10,11... | collective-permute-start | bytes 196616 | tf_op jit(solution)/shard_map/ppermute | solution.py:33
  5.0 6.8 %collective-permute-start.1 = (bf16[4,1,32,256]{3,2,1,0:T(8,128)(2,1)S(1)}, bf16[4,1,32,256]{3,2,1,0:T(8,128)(2,1)S(1)}, u32[]{:S(2)}, u32[]{:S(2)}) collective-permute-start(bf16[4,1,32,256]{3,2,1,0:T(8,128)(2,1)S(1)} %get-tuple-element.29), channel_id=1, source_target_pairs={{1,2},{2,1},{5,6},{6,5},{9,10},{10,9},{13,14},{14,13},{17,18},{18,... | collective-permute-start | bytes 196616 | tf_op jit(solution)/shard_map/ppermute | solution.py:48
  11.5 3.2 %copy-start.3 = (bf16[3,3,256,256]{3,2,1,0:T(8,128)(2,1)}, bf16[3,3,256,256]{3,2,1,0:T(8,128)(2,1)S(1)}, u32[]{:S(2)}) copy-start(bf16[3,3,256,256]{3,2,1,0:T(8,128)(2,1)S(1)} %get-tuple-element.30.ws_ref) | copy-start | bytes 3538948
  11.5 3.2 %copy-start.6 = (bf16[3,256,256]{2,1,0:T(8,128)(2,1)}, bf16[3,256,256]{2,1,0:T(8,128)(2,1)S(1)}, u32[]{:S(2)}) copy-start(bf16[3,256,256]{2,1,0:T(8,128)(2,1)S(1)} %get-tuple-element.35.wt_ref) | copy-start | bytes 1179652
  11.5 21.2 %copy-start.1 = (bf16[4,4,32,256]{3,2,1,0:T(8,128)(2,1)}, bf16[4,4,32,256]{3,2,1,0:T(8,128)(2,1)S(1)}, u32[]{:S(2)}) copy-start(bf16[4,4,32,256]{3,2,1,0:T(8,128)(2,1)S(1)} %get-tuple-element.27.low_ref) | copy-start | bytes 786436
  21.3 4.3 %collective-permute-start.3 = (f32[12,128,256]{2,1,0:T(8,128)S(1)}, f32[12,128,256]{2,1,0:T(8,128)S(1)}, u32[]{:S(2)}, u32[]{:S(2)}) collective-permute-start(f32[12,128,256]{2,1,0:T(8,128)S(1)} %get-tuple-element.38), channel_id=1, source_target_pairs={{0,4},{4,0},{1,5},{5,1},{2,6},{6,2},{3,7},{7,3},{8,12},{12,8},{9,1... | collective-permute-start | bytes 4718600 | tf_op jit(solution)/shard_map/ppermute | solution.py:33
  26.6 23.9 %all-to-all-start = ((bf16[16,96,256]{2,1,0:T(8,128)(2,1)}), bf16[16,96,256]{2,1,0:T(8,128)(2,1)S(1)}, u32[]{:S(2)}, u32[]{:S(2)}) async-start(bf16[16,96,256]{2,1,0:T(8,128)(2,1)} %bitcast.5), calls=%async_computation | async-start | bytes 1572864 | tf_op jit(solution)/shard_map/all_to_all | solution.py:42
  32.7 8.2 %copy-start.4 = (bf16[3,3,256,256]{3,2,1,0:T(8,128)(2,1)S(1)}, bf16[3,3,256,256]{3,2,1,0:T(8,128)(2,1)}, u32[]{:S(2)}) copy-start(bf16[3,3,256,256]{3,2,1,0:T(8,128)(2,1)} %copy-done.3) | copy-start | bytes 3538948
  33.3 3.6 %copy-start.8 = (bf16[4,2,32,256]{3,2,1,0:T(8,128)(2,1)}, bf16[4,2,32,256]{3,2,1,0:T(8,128)(2,1)S(1)}, u32[]{:S(2)}) copy-start(bf16[4,2,32,256]{3,2,1,0:T(8,128)(2,1)S(1)} %get-tuple-element.41) | copy-start | bytes 393220
  33.3 7.6 %collective-permute-start.4 = (bf16[2,6,32,256]{3,2,1,0:T(8,128)(2,1)S(1)}, bf16[2,6,32,256]{3,2,1,0:T(8,128)(2,1)S(1)}, u32[]{:S(2)}, u32[]{:S(2)}) collective-permute-start(bf16[2,6,32,256]{3,2,1,0:T(8,128)(2,1)S(1)} %get-tuple-element.39), channel_id=1, source_target_pairs={{0,4},{4,8},{8,12},{1,5},{5,9},{9,13},{2,6},{6,10},{10,14},{3,7},{... | collective-permute-start | bytes 589832 | tf_op jit(solution)/shard_map/ppermute | solution.py:39
  51.5 33.6 %all-to-all-start.1 = ((bf16[16,96,256]{2,1,0:T(8,128)(2,1)}), bf16[16,96,256]{2,1,0:T(8,128)(2,1)S(1)}, u32[]{:S(2)}, u32[]{:S(2)}) async-start(bf16[16,96,256]{2,1,0:T(8,128)(2,1)} %sum_parts.1._), calls=%async_computation.1 | async-start | bytes 1572864 | tf_op jit(solution)/shard_map/all_to_all | solution.py:42
  58.7 15.1 %collective-permute-start.5 = (bf16[4,2,32,256]{3,2,1,0:T(8,128)(2,1)}, bf16[4,2,32,256]{3,2,1,0:T(8,128)(2,1)S(1)}, u32[]{:S(2)}, u32[]{:S(2)}) collective-permute-start(bf16[4,2,32,256]{3,2,1,0:T(8,128)(2,1)} %copy-done.8), channel_id=1, source_target_pairs={{0,1},{1,0},{2,3},{3,2},{4,5},{5,4},{6,7},{7,6},{8,9},{9,8},{10,11... | collective-permute-start | bytes 393224 | tf_op jit(solution)/shard_map/ppermute | solution.py:33
  58.9 4.3 %copy-start.2 = (bf16[4,4,32,256]{3,2,1,0:T(8,128)(2,1)S(1)}, bf16[4,4,32,256]{3,2,1,0:T(8,128)(2,1)}, u32[]{:S(2)}) copy-start(bf16[4,4,32,256]{3,2,1,0:T(8,128)(2,1)} %copy-done.1) | copy-start | bytes 786436
  58.9 4.3 %copy-start.7 = (bf16[3,256,256]{2,1,0:T(8,128)(2,1)S(1)}, bf16[3,256,256]{2,1,0:T(8,128)(2,1)}, u32[]{:S(2)}) copy-start(bf16[3,256,256]{2,1,0:T(8,128)(2,1)} %copy-done.6) | copy-start | bytes 1179652
  58.9 21.0 %collective-permute-start.6 = (bf16[4,2,32,256]{3,2,1,0:T(8,128)(2,1)S(1)}, bf16[4,2,32,256]{3,2,1,0:T(8,128)(2,1)S(1)}, u32[]{:S(2)}, u32[]{:S(2)}) collective-permute-start(bf16[4,2,32,256]{3,2,1,0:T(8,128)(2,1)S(1)} %get-tuple-element.42), channel_id=1, source_target_pairs={{1,2},{2,1},{5,6},{6,5},{9,10},{10,9},{13,14},{14,13},{17,18},{18,... | collective-permute-start | bytes 393224 | tf_op jit(solution)/shard_map/ppermute | solution.py:48
  63.2 16.7 %copy-start = (bf16[1,4,8,64,256]{4,3,2,1,0:T(8,128)(2,1)S(1)}, bf16[1,4,8,64,256]{4,3,2,1,0:T(8,128)(2,1)}, u32[]{:S(2)}) copy-start(bf16[1,4,8,64,256]{4,3,2,1,0:T(8,128)(2,1)} %param.7) | copy-start | bytes 3145732
  63.2 16.6 %copy-start.5 = (bf16[3,3,256,256]{3,2,1,0:T(8,128)(2,1)S(1)}, bf16[3,3,256,256]{3,2,1,0:T(8,128)(2,1)}, u32[]{:S(2)}) copy-start(bf16[3,3,256,256]{3,2,1,0:T(8,128)(2,1)} %copy-done.3) | copy-start | bytes 3538948
  85.1 3.4 %collective-permute-start.7 = (bf16[12,128,256]{2,1,0:T(8,128)(2,1)S(1)}, bf16[12,128,256]{2,1,0:T(8,128)(2,1)S(1)}, u32[]{:S(2)}, u32[]{:S(2)}) collective-permute-start(bf16[12,128,256]{2,1,0:T(8,128)(2,1)S(1)} %after.1.half_ref), channel_id=1, source_target_pairs={{0,4},{4,0},{1,5},{5,1},{2,6},{6,2},{3,7},{7,3},{8,12},{12,8},{9,1... | collective-permute-start | bytes 2359304 | tf_op jit(solution)/shard_map/ppermute | solution.py:33

commit v6 on v5

--- a/solution.py
+++ b/solution.py
@@ -20,8 +20,8 @@
         self.core = next((n for n in names if self.same_chip(n)), self.axes["tm"][-1])
         others = [[b for b in reversed(bits) if b != self.core] for bits in self.axes.values()]
         turns = [bits[turn] for turn in range(len(names)) for bits in others if turn < len(bits)]
-        self.near = [n for n in names if n in turns[:4]]
-        self.far = turns[4:]
+        self.near = [n for n in names if n in turns[:3]]
+        self.far = turns[3:]
 
     def same_chip(self, name):
         at = [1 if n == name else 0 for n in self.mesh.axis_names]
@@ -49,10 +49,10 @@
         return self.swap(inner, axes[-1]), outer
 
     def far_sums(self, total):
-        for axis in self.far:
+        for axis in self.far[:-1]:
             total = total.astype(jnp.float32) + self.swap(total, axis).astype(jnp.float32)
             total = lax.reduce_precision(total, 8, 7).astype(jnp.bfloat16)
-        return total
+        return total, self.swap(total, self.far[-1])
 
 
 SIDES = ((0, 0), (0, 1), (1, 0), (1, 1))
@@ -123,11 +123,11 @@
         target[:, n * span : (n + 1) * span, :] = block
 
 
-def tall(place_ref, low_ref, inner_ref, outer_ref):
+def tall(place_ref, low_ref, inner_ref, outer_ref, frame, lanes=slice(None)):
     odd = place_ref[1] == 1
-    up = jnp.where(odd, inner_ref[0], outer_ref[0])
-    down = jnp.where(odd, outer_ref[0], inner_ref[0])
-    return jnp.concatenate([up, low_ref[0], down], axis=0)
+    inner, outer = inner_ref[frame, :, :, lanes], outer_ref[frame, :, :, lanes]
+    up, down = jnp.where(odd, inner, outer), jnp.where(odd, outer, inner)
+    return jnp.concatenate([up, low_ref[frame, :, :, lanes], down], axis=0)
 
 
 def spatial(low, ws_ref):
@@ -148,11 +148,12 @@
 
 
 def forward_kernel(place_ref, low_ref, inner_ref, outer_ref, ws_ref, act_ref, slope_ref):
-    low = tall(place_ref, low_ref, inner_ref, outer_ref)
-    for side, pre in enumerate(spatial(low, ws_ref)):
-        sig = jax.nn.sigmoid(pre)
-        act_ref[0, side] = (pre * sig).astype(jnp.bfloat16)
-        slope_ref[0, side] = sig * (1.0 + pre * (1.0 - sig))
+    for frame in range(low_ref.shape[0]):
+        low = tall(place_ref, low_ref, inner_ref, outer_ref, frame)
+        for side, pre in enumerate(spatial(low, ws_ref)):
+            sig = jax.nn.sigmoid(pre)
+            act_ref[frame, side] = (pre * sig).astype(jnp.bfloat16)
+            slope_ref[frame, side] = sig * (1.0 + pre * (1.0 - sig))
 
 
 def act_kernel(low_ref, ws_ref, act_ref):
@@ -160,68 +161,46 @@
         act_ref[0, side] = (pre * jax.nn.sigmoid(pre)).astype(jnp.bfloat16)
 
 
-def add_sums(low, act, pg, cots, out_ref):
-    rows_low, cols_low, half = low.shape[0] - 2, low.shape[1], low.shape[2]
-    count = rows_low * cols_low
-    sums = []
-    wide = low.reshape(-1, half).astype(jnp.float32)
-    at = column(wide.shape[0], cols_low, half)
-    moved = [from_left(wide, at), wide, from_right(wide, at, cols_low - 1)]
-    turned = {}
-    for dc in range(3):
-        view = moved[dc].astype(jnp.bfloat16).reshape(low.shape)
-        for dr in range(3):
-            turned[dr - 1, dc - 1] = view[dr : dr + rows_low].reshape(count, half).T
-    for i in range(3):
-        for j in range(3):
-            left = jnp.concatenate([turned[(a + i - 1) // 2, (b + j - 1) // 2] for a, b in SIDES], axis=1)
-            sums.append(product(left, pg))
-    act = act.T
-    for cot in cots:
-        sums.append(product(act, cot))
-
-    @pl.when(pl.program_id(0) == 0)
-    def _():
-        for tap, value in enumerate(sums):
-            out_ref[tap] = value
-
-    @pl.when(pl.program_id(0) > 0)
-    def _():
-        for tap, value in enumerate(sums):
-            out_ref[tap] += value
+def half_sums(place_ref, low_ref, inner_ref, outer_ref, act_ref, pg_ref, ext_ref, out_ref):
+    frames, rows_low, cols_low, chan = low_ref.shape
+    count, half = rows_low * cols_low, chan // 2
+    lanes = pl.ds(pl.multiple_of(place_ref[0] * half, half), half)
+    lefts = [[] for _ in range(9)]
+    acts = []
+    at = column((rows_low + 2) * cols_low, cols_low, half)
+    for frame in range(frames):
+        low = tall(place_ref, low_ref, inner_ref, outer_ref, frame, lanes)
+        wide = low.reshape(-1, half).astype(jnp.float32)
+        moved = [from_left(wide, at), wide, from_right(wide, at, cols_low - 1)]
+        turned = {}
+        for dc in range(3):
+            view = moved[dc].astype(jnp.bfloat16).reshape(low.shape)
+            for dr in range(3):
+                turned[dr - 1, dc - 1] = view[dr : dr + rows_low].reshape(count, half).T
+        for i in range(3):
+            for j in range(3):
+                lefts[3 * i + j] += [turned[(a + i - 1) // 2, (b + j - 1) // 2] for a, b in SIDES]
+        acts.append(act_ref[frame, :, :, lanes].reshape(4 * count, half).T)
+    pg = pg_ref[...].reshape(frames * 4 * count, chan)
+    for tap, left in enumerate(lefts):
+        out_ref[tap] = product(jnp.concatenate(left, axis=1), pg)
+    act = jnp.concatenate(acts, axis=1)
+    for k in range(3):
+        out_ref[9 + k] = product(act, ext_ref[k : k + frames].reshape(frames * 4 * count, chan))
 
 
 def backward_kernel(place_ref, low_ref, inner_ref, outer_ref, act_ref, slope_ref, cot_ref, later_ref, wt_ref, pg_ref, ext_ref, out_ref):
-    frame = pl.program_id(0)
     frames, _, count, chan = cot_ref.shape
-    cols_low = low_ref.shape[2]
-
-    @pl.when(frame == 0)
-    def _():
-        ext_ref[:frames] = cot_ref[...]
-        for n in range(2):
-            sort_columns(later_ref.at[n], ext_ref.at[frames + n], cols_low)
-
-    pgs = []
-    for side in range(4):
-        act_grad = product_nt(ext_ref[frame, side], wt_ref[0])
+    ext_ref[:frames] = cot_ref[...]
+    for n in range(2):
+        sort_columns(later_ref.at[n], ext_ref.at[frames + n], low_ref.shape[2])
+    for frame in range(frames):
+        act_grad = product_nt(ext_ref[frame].reshape(4 * count, chan), wt_ref[0])
         for k in (1, 2):
-            act_grad = act_grad + product_nt(ext_ref[frame + k, side], wt_ref[k])
-        pgs.append((act_grad * slope_ref[0, side]).astype(jnp.bfloat16))
-        pg_ref[0, side] = pgs[side]
-    low = tall(place_ref, low_ref, inner_ref, outer_ref)
-    act = act_ref[0].reshape(4 * count, -1)
-    cots = [ext_ref[frame + k].reshape(4 * count, chan) for k in range(3)]
-    add_sums(low, act, jnp.concatenate(pgs, axis=0), cots, out_ref)
-
-
-def half_kernel(place_ref, low_ref, inner_ref, outer_ref, act_ref, pg_ref, ext_ref, out_ref):
-    frame = pl.program_id(0)
-    _, _, count, chan = pg_ref.shape
-    low = tall(place_ref, low_ref, inner_ref, outer_ref)
-    act = act_ref[0].reshape(4 * count, -1)
-    cots = [ext_ref[frame + k].reshape(4 * count, chan) for k in range(3)]
-    add_sums(low, act, pg_ref[0].reshape(4 * count, chan), cots, out_ref)
+            act_grad = act_grad + product_nt(ext_ref[frame + k].reshape(4 * count, chan), wt_ref[k])
+        slope = slope_ref[frame].reshape(4 * count, chan)
+        pg_ref[frame] = (act_grad * slope).astype(jnp.bfloat16).reshape(4, count, chan)
+    half_sums(place_ref, low_ref, inner_ref, outer_ref, act_ref, pg_ref, ext_ref, out_ref)
 
 
 def whole(shape):
@@ -230,11 +209,6 @@
 
 def each(shape):
     return pl.BlockSpec((1,) + tuple(shape[1:]), lambda f, *_: (f,) + (0,) * (len(shape) - 1))
-
-
-def half_of(shape):
-    block = (1,) + tuple(shape[1:-1]) + (shape[-1] // 2,)
-    return pl.BlockSpec(block, lambda f, side: (f,) + (0,) * (len(shape) - 2) + (side[0],))
 
 
 SCALAR = pl.BlockSpec(memory_space=pltpu.SMEM)
@@ -336,9 +310,8 @@
     side = (frames, 4, rows_low * cols_low, chan)
     return pl.pallas_call(
         forward_kernel,
-        grid=(frames,),
-        in_specs=[SCALAR, each(low.shape), each(inner.shape), each(outer.shape), whole(ws.shape)],
-        out_specs=[each(side)] * 2,
+        in_specs=[SCALAR] + [FULL] * 4,
+        out_specs=[FULL] * 2,
         out_shape=[like(side, jnp.bfloat16), like(side, jnp.float32)],
         compiler_params=grant(20),
         cost_estimate=cost(10, 8),
@@ -350,8 +323,7 @@
     cols_low = low_ref.shape[2]
     first = low_ref.shape[0] - tall_ref.shape[0]
     for n in range(tall_ref.shape[0]):
-        at = pl.ds(first + n, 1)
-        tall_ref[n] = tall(place_ref, low_ref.at[at], inner_ref.at[at], outer_ref.at[at])
+        tall_ref[n] = tall(place_ref, low_ref, inner_ref, outer_ref, first + n)
     odd = place_ref[1] == 1
     top, bottom = pg_ref[:, :2, :cols_low, :], pg_ref[:, 2:, -cols_low:, :]
     pg_inner[...] = jnp.where(odd, top, bottom)
@@ -388,39 +360,27 @@
 
 
 def backward(place, low, inner, outer, act, slope, cot, later, wt):
-    frames, _, count, chan = act.shape
+    frames, _, _, chan = act.shape
     ext = (frames + 2,) + act.shape[1:]
-    half = (12, chan // 2, chan)
     return pl.pallas_call(
         backward_kernel,
-        grid_spec=pltpu.PrefetchScalarGridSpec(
-            num_scalar_prefetch=1,
-            grid=(frames,),
-            in_specs=[half_of(low.shape), half_of(inner.shape), half_of(outer.shape), half_of(act.shape),
-                      each(slope.shape), whole(cot.shape), whole(later.shape), whole(wt.shape)],
-            out_specs=[each(act.shape), whole(ext), whole(half)],
-        ),
-        out_shape=[like(act.shape, jnp.bfloat16), like(ext, jnp.bfloat16), like(half, jnp.float32)],
-        compiler_params=grant(28),
+        in_specs=[SCALAR] + [FULL] * 8,
+        out_specs=[FULL] * 3,
+        out_shape=[like(act.shape, jnp.bfloat16), like(ext, jnp.bfloat16), like((12, chan // 2, chan), jnp.float32)],
+        compiler_params=grant(24),
         cost_estimate=cost(15, 10),
         name="backward",
     )(place, low, inner, outer, act, slope, cot, later, wt)
 
 
 def half_grads(place, low, inner, outer, act, pg, ext):
-    frames, _, _, chan = act.shape
-    half = (12, chan // 2, chan)
-    return pl.pallas_call(
-        half_kernel,
-        grid_spec=pltpu.PrefetchScalarGridSpec(
-            num_scalar_prefetch=1,
-            grid=(frames,),
-            in_specs=[half_of(low.shape), half_of(inner.shape), half_of(outer.shape), half_of(act.shape),
-                      each(pg.shape), whole(ext.shape)],
-            out_specs=whole(half),
-        ),
-        out_shape=like(half, jnp.float32),
-        compiler_params=grant(24),
+    chan = low.shape[-1]
+    return pl.pallas_call(
+        half_sums,
+        in_specs=[SCALAR] + [FULL] * 6,
+        out_specs=FULL,
+        out_shape=like((12, chan // 2, chan), jnp.float32),
+        compiler_params=grant(20),
         cost_estimate=cost(10, 6),
         name="half_grads",
     )(place, low, inner, outer, act, pg, ext)
@@ -566,20 +526,35 @@
     total = got_ref[0].astype(jnp.float32)
     for n in range(1, got_ref.shape[0]):
         total = total + got_ref[n].astype(jnp.float32)
-    total = total.astype(jnp.bfloat16)
-    for n in range(out_ref.shape[0]):
-        out_ref[n] = total
-
-
-def sum_parts(got, copies, before):
+    out_ref[...] = total.astype(jnp.bfloat16)
+
+
+def sum_parts(got, before):
     return pl.pallas_call(
         sum_kernel,
         in_specs=[FULL, UNREAD],
         out_specs=FULL,
-        out_shape=like((copies,) + got.shape[1:], jnp.bfloat16),
+        out_shape=like(got.shape[1:], jnp.bfloat16),
         compiler_params=grant(4),
         name="sum_parts",
     )(got, before)
+
+
+def spread_kernel(own_ref, theirs_ref, *refs):
+    total = (own_ref[...].astype(jnp.float32) + theirs_ref[...].astype(jnp.float32)).astype(jnp.bfloat16)
+    for n in range(refs[-1].shape[0]):
+        refs[-1][n] = total
+
+
+def spread(own, theirs, parts, *before):
+    return pl.pallas_call(
+        spread_kernel,
+        in_specs=[FULL, FULL] + [UNREAD] * len(before),
+        out_specs=FULL,
+        out_shape=like((parts,) + own.shape, jnp.bfloat16),
+        compiler_params=grant(4),
+        name="spread",
+    )(own, theirs, *before)
 
 
 def on_device(bits, low_frames, spatial_weight, temporal_weight, cotangent):
@@ -603,14 +578,11 @@
     edge, pg_inner, pg_outer = edges(mine, low, inner, outer, pg, kept)
     earlier = earlier_act(bits.shift(edge, "tm", 1), ws)
     pg_inner, pg_outer = bits.pairs(pg_inner, pg_outer)
-    if bits.far:
-        total = bits.far_sums(sum_parts(got, 1, earlier)[0])
-        totals = jnp.broadcast_to(total, got.shape)
-    else:
-        totals = sum_parts(got, parts, earlier)
-    section_out, section_done = section(jnp.concatenate([earlier, act], axis=0), low, wt, totals)
+    total, far = bits.far_sums(sum_parts(got, earlier))
+    section_out, section_done = section(jnp.concatenate([earlier, act], axis=0), low, wt, total)
+    totals = spread(total, far, parts, section_done, pg_inner, pg_outer)
     input_grad, input_done = input_grads(mine, pg, pg_inner, pg_outer, cot, ws, totals, low.shape)
-    half, = after([bits.exchange(totals).reshape(kept.shape)], section_done, input_done)
+    half, = after([bits.exchange(totals).reshape(kept.shape)], input_done)
     theirs = bits.swap(half, bits.core)
     spatial_grad, temporal_grad = put(other, theirs, *put(mine, half))
     return section_out[None], input_grad[None], spatial_grad, temporal_grad

time: 90.6 us -> 70.4 us (0.78)
  the two profiles are of different devices: /device:TPU:9 before, /device:TPU:0 now
where the time goes in v6:
time: 70.4 us; the launch traced here: 70 us
  Pallas kernels  27.7 us (39%)
  starting transfers between devices  23.8 us (34%)
  waiting for transfers between devices  15 us (21%)
  local copies, waits for them, and re-layouts  2.3 us (3%)
  between operations  0.88 us (1%)
    all_to_all x2, waiting for transfers between devices, exchange(): return lax.all_to_all(parts, tuple(self.near), 0, 0, tiled=True)  13.2 us
    all_to_all x2, starting transfers between devices, exchange(): return lax.all_to_all(parts, tuple(self.near), 0, 0, tiled=True)  10.2 us
    ppermute x5, starting transfers between devices, swap(): return lax.ppermute(block, axis, [(0, 1), (1, 0)])  9.07 us
    pallas_call x1, Pallas kernels, input_grads(): pl.pallas_call(input_kernel, grid=(low_shape[0],), in_specs=[SCALAR, each...  5.05 us
    pallas_call x2, Pallas kernels, put(): pl.pallas_call(put_kernel, in_specs=[SCALAR, FULL] + [hbm] * len(done), o...  3.56 us
    pallas_call x1, Pallas kernels, backward(): pl.pallas_call(backward_kernel, in_specs=[SCALAR] + [FULL] * 8, out_specs...  3.35 us
    pallas_call x1, Pallas kernels, section(): pl.pallas_call(section_kernel, grid=(frames,), in_specs=[whole(act_ext.sh...  3.17 us
    ppermute x2, starting transfers between devices, shift(): return lax.ppermute(block, axes, route)  3.05 us
  transfers between devices with their start and end apart: 11, of which 5 were waited for; matrix products, arithmetic and copies ran while one was open for 0% of the time, Pallas kernels for 27%

profile of v6, /device:TPU:0, one launch (start us, length us, event | category | flops | bytes accessed | tf_op | source)
XLA Modules:
  0.0 70.0 jit_solution(10618282124053618553)
XLA Ops:
  0.6 0.1 pad_add_fusion.place_ref
  0.7 1.6 %first_messages.1 = (bf16[4,1,32,256]{3,2,1,0:T(8,128)(2,1)S(1)}, bf16[4,1,32,256]{3,2,1,0:T(8,128)(2,1)S(1)}, bf16[2,8,64,256]{3,2,1,0:T(8,128)(2,1)S(1)}) custom-call(s32[2]{0:T(128)S(1)} %pad_add_fusion.place_ref, bf16[4,4,32,256]{3,2,1,0:T(8,128)(2,1)} %bitcast.13, bf16[4,8,64,256]{3,2,1,0:T(8,128)(2,1)} %bitcast.10), custom_call_target="tpu_custom_call" | custom-call | tf_op jit(solution)/shard_map/first_messages/pallas_call | solution.py:252
  2.3 1.3 %collective-permute-start.2 = (bf16[2,8,64,256]{3,2,1,0:T(8,128)(2,1)S(1)}, bf16[2,8,64,256]{3,2,1,0:T(8,128)(2,1)S(1)}, u32[]{:S(2)}, u32[]{:S(2)}) collective-permute-start(bf16[2,8,64,256]{3,2,1,0:T(8,128)(2,1)S(1)} %get-tuple-element.34), channel_id=1, source_target_pairs={{4,0},{8,4},{12,8},{5,1},{9,5},{13,9},{6,2},{10,6},{14,10},{7,3},{... | collective-permute-start | bytes 1572872 | tf_op jit(solution)/shard_map/ppermute | solution.py:39
  3.6 3.1 %collective-permute-start = (bf16[4,1,32,256]{3,2,1,0:T(8,128)(2,1)S(1)}, bf16[4,1,32,256]{3,2,1,0:T(8,128)(2,1)S(1)}, u32[]{:S(2)}, u32[]{:S(2)}) collective-permute-start(bf16[4,1,32,256]{3,2,1,0:T(8,128)(2,1)S(1)} %get-tuple-element.28), channel_id=1, source_target_pairs={{0,1},{1,0},{2,3},{3,2},{4,5},{5,4},{6,7},{7,6},{8,9},{9,8},{10,11... | collective-permute-start | bytes 196616 | tf_op jit(solution)/shard_map/ppermute | solution.py:33
  6.7 0.7 collective-permute-start.1
  7.4 0.1 pad_add_fusion.1.place_ref
  7.5 2.0 %load.1 = (bf16[4,4,32,256]{3,2,1,0:T(8,128)(2,1)S(1)}, bf16[3,3,256,256]{3,2,1,0:T(8,128)(2,1)S(1)}, bf16[3,256,256]{2,1,0:T(8,128)(2,1)S(1)}, bf16[4,4,128,256]{3,2,1,0:T(8,128)(2,1)S(1)}) custom-call(bf16[4,4,32,256]{3,2,1,0:T(8,128)(2,1)} %bitcast.14, bf16[4,8,64,256]{3,2,1,0:T(8,128)(2,1)} %bitcast.11, bf16[3,3,256,256]{3,2,1,0:T(8,128)(2,1)} %ws_hbm.1, ...), custom_call_target="tpu_custom_call" | custom-call | flops 536870912 | bytes 4194304 | tf_op jit(solution)/shard_map/load/pallas_call | solution.py:279
  9.4 0.0 copy-start.5
  9.4 0.0 copy-start.8
  9.4 0.0 collective-permute-done.inner_ref
  9.5 0.0 collective-permute-done.1.outer_ref
  9.5 2.3 %forward.1 = (bf16[4,4,128,256]{3,2,1,0:T(8,128)(2,1)S(1)}, f32[4,4,128,256]{3,2,1,0:T(8,128)S(1)}) custom-call(s32[2]{0:T(128)S(1)} %pad_add_fusion.place_ref, bf16[4,4,32,256]{3,2,1,0:T(8,128)(2,1)S(1)} %get-tuple-element.27.low_ref, bf16[4,1,32,256]{3,2,1,0:T(8,128)(2,1)S(1)} %collective-permute-done.inner_ref, ...), custom_call_target="tpu_custom_call" | custom-call | flops 2684354560 | bytes 8388608 | tf_op jit(solution)/shard_map/forward/pallas_call | solution.py:311
  11.8 0.0 copy-done.5
  11.8 0.0 copy-start.1
  11.8 0.0 collective-permute-done.2.later_ref
  11.8 3.3 %backward.1 = (bf16[4,4,128,256]{3,2,1,0:T(8,128)(2,1)S(1)}, bf16[6,4,128,256]{3,2,1,0:T(8,128)(2,1)S(1)}, f32[12,128,256]{2,1,0:T(8,128)S(1)}) custom-call(s32[2]{0:T(128)S(1)} %pad_add_fusion.1.place_ref, bf16[4,4,32,256]{3,2,1,0:T(8,128)(2,1)S(1)} %get-tuple-element.27.low_ref, bf16[4,1,32,256]{3,2,1,0:T(8,128)(2,1)S(1)} %collective-permute-done.inner_ref, ...), custom_call_target="tpu_custom_call" | custom-call | flops 4026531840 | bytes 10485760 | tf_op jit(solution)/shard_map/backward/pallas_call | solution.py:365
  15.2 0.0 copy-start.3
  15.2 2.4 %collective-permute-start.3 = (f32[12,128,256]{2,1,0:T(8,128)S(1)}, f32[12,128,256]{2,1,0:T(8,128)S(1)}, u32[]{:S(2)}, u32[]{:S(2)}) collective-permute-start(f32[12,128,256]{2,1,0:T(8,128)S(1)} %get-tuple-element.38), channel_id=1, source_target_pairs={{0,4},{4,0},{1,5},{5,1},{2,6},{6,2},{3,7},{7,3},{8,12},{12,8},{9,1... | collective-permute-start | bytes 4718600 | tf_op jit(solution)/shard_map/ppermute | solution.py:33
  17.6 2.4 %half_grads.1.mine_ref = f32[12,128,256]{2,1,0:T(8,128)S(1)} custom-call(s32[2]{0:T(128)S(1)} %pad_add_fusion.place_ref, bf16[4,4,32,256]{3,2,1,0:T(8,128)(2,1)S(1)} %get-tuple-element.27.low_ref, bf16[4,1,32,256]{3,2,1,0:T(8,128)(2,1)S(1)} %collective-permute-done.inner_ref, bf16[4,1,32,256]{3,2,1,0:T(8,128)(2,1)S(1)} %collective-permute-done.1.outer_ref, ...), custom_call_target="tpu_custom_call" | custom-call | flops 2684354560 | bytes 6291456 | tf_op jit(solution)/shard_map/half_grads/pallas_call | solution.py:378
  19.9 0.7 collective-permute-done.3.theirs_ref
  20.6 1.0 %add_halves.1._ = bf16[12,128,256]{2,1,0:T(8,128)(2,1)} custom-call(f32[12,128,256]{2,1,0:T(8,128)S(1)} %half_grads.1.mine_ref, f32[12,128,256]{2,1,0:T(8,128)S(1)} %collective-permute-done.3.theirs_ref), custom_call_target="tpu_custom_call" | custom-call | tf_op jit(solution)/shard_map/add_halves/pallas_call | solution.py:515
  21.6 6.6 %all-to-all-start = ((bf16[8,192,256]{2,1,0:T(8,128)(2,1)}), bf16[8,192,256]{2,1,0:T(8,128)(2,1)S(1)}, u32[]{:S(2)}, u32[]{:S(2)}) async-start(bf16[8,192,256]{2,1,0:T(8,128)(2,1)} %bitcast.5), calls=%async_computation | async-start | bytes 1572864 | tf_op jit(solution)/shard_map/all_to_all | solution.py:42
  28.3 0.0 copy-start.6
  28.3 1.2 %edges.1 = (bf16[2,6,32,256]{3,2,1,0:T(8,128)(2,1)S(1)}, bf16[4,2,32,256]{3,2,1,0:T(8,128)(2,1)}, bf16[4,2,32,256]{3,2,1,0:T(8,128)(2,1)S(1)}) custom-call(s32[2]{0:T(128)S(1)} %pad_add_fusion.place_ref, bf16[4,4,32,256]{3,2,1,0:T(8,128)(2,1)S(1)} %get-tuple-element.27.low_ref, bf16[4,1,32,256]{3,2,1,0:T(8,128)(2,1)S(1)} %collective-permute-done.inner_ref, ...), custom_call_target="tpu_custom_call" | custom-call | tf_op jit(solution)/shard_map/edges/pallas_call | solution.py:337
  29.5 1.8 %collective-permute-start.4 = (bf16[2,6,32,256]{3,2,1,0:T(8,128)(2,1)S(1)}, bf16[2,6,32,256]{3,2,1,0:T(8,128)(2,1)S(1)}, u32[]{:S(2)}, u32[]{:S(2)}) collective-permute-start(bf16[2,6,32,256]{3,2,1,0:T(8,128)(2,1)S(1)} %get-tuple-element.39), channel_id=1, source_target_pairs={{0,4},{4,8},{8,12},{1,5},{5,9},{9,13},{2,6},{6,10},{10,14},{3,7},{... | collective-permute-start | bytes 589832 | tf_op jit(solution)/shard_map/ppermute | solution.py:39
  31.3 1.8 %collective-permute-start.5 = (bf16[4,2,32,256]{3,2,1,0:T(8,128)(2,1)}, bf16[4,2,32,256]{3,2,1,0:T(8,128)(2,1)S(1)}, u32[]{:S(2)}, u32[]{:S(2)}) collective-permute-start(bf16[4,2,32,256]{3,2,1,0:T(8,128)(2,1)} %get-tuple-element.41), channel_id=1, source_target_pairs={{0,1},{1,0},{2,3},{3,2},{4,5},{5,4},{6,7},{7,6},{8,9},{9,8},{10,11... | collective-permute-start | bytes 393224 | tf_op jit(solution)/shard_map/ppermute | solution.py:33
  33.1 0.8 %collective-permute-start.6 = (bf16[4,2,32,256]{3,2,1,0:T(8,128)(2,1)S(1)}, bf16[4,2,32,256]{3,2,1,0:T(8,128)(2,1)S(1)}, u32[]{:S(2)}, u32[]{:S(2)}) collective-permute-start(bf16[4,2,32,256]{3,2,1,0:T(8,128)(2,1)S(1)} %get-tuple-element.42), channel_id=1, source_target_pairs={{1,2},{2,1},{5,6},{6,5},{9,10},{10,9},{13,14},{14,13},{17,18},{18,... | collective-permute-start | bytes 393224 | tf_op jit(solution)/shard_map/ppermute | solution.py:48
  33.9 0.0 collective-permute-done.4.low_ref
  33.9 1.0 %earlier_act.1._ = bf16[2,4,128,256]{3,2,1,0:T(8,128)(2,1)S(1)} custom-call(bf16[2,6,32,256]{3,2,1,0:T(8,128)(2,1)S(1)} %collective-permute-done.4.low_ref, bf16[3,3,256,256]{3,2,1,0:T(8,128)(2,1)S(1)} %copy-done.6), custom_call_target="tpu_custom_call" | custom-call | flops 1073741824 | bytes 3145728 | tf_op jit(solution)/shard_map/earlier_act/pallas_call | solution.py:350
  35.0 0.1 pad_maximum_fusion.act_ref
  35.1 7.2 %all-to-all-done.got_ref = bf16[8,192,256]{2,1,0:T(8,128)(2,1)S(1)} async-done(((bf16[8,192,256]{2,1,0:T(8,128)(2,1)}), bf16[8,192,256]{2,1,0:T(8,128)(2,1)S(1)}, u32[]{:S(2)}, u32[]{:S(2)}) %all-to-all-start) | async-done | bytes 786464 | tf_op jit(solution)/shard_map/all_to_all | solution.py:42
  42.3 0.1 sum_parts.1._.own_ref
  42.4 1.8 %collective-permute-start.7 = (bf16[192,256]{1,0:T(8,128)(2,1)S(1)}, bf16[192,256]{1,0:T(8,128)(2,1)S(1)}, u32[]{:S(2)}, u32[]{:S(2)}) collective-permute-start(bf16[192,256]{1,0:T(8,128)(2,1)S(1)} %sum_parts.1._.own_ref), channel_id=1, source_target_pairs={{0,2},{2,0},{1,3},{3,1},{4,6},{6,4},{5,7},{7,5},{8,10},{10,8},{9,1... | collective-permute-start | bytes 294920 | tf_op jit(solution)/shard_map/ppermute | solution.py:33
  44.2 1.0 %copy-done.9 = bf16[3,256,256]{2,1,0:T(8,128)(2,1)S(1)} copy-done((bf16[3,256,256]{2,1,0:T(8,128)(2,1)S(1)}, bf16[3,256,256]{2,1,0:T(8,128)(2,1)}, u32[]{:S(2)}) %copy-start.9) | copy-done | bytes 393240
  45.2 3.2 %section.1 = (bf16[4,8,64,256]{3,2,1,0:T(8,128)(2,1)}, f32[8,128]{1,0:T(8,128)S(1)}) custom-call(bf16[6,4,128,256]{3,2,1,0:T(8,128)(2,1)S(1)} %pad_maximum_fusion.act_ref, bf16[4,4,32,256]{3,2,1,0:T(8,128)(2,1)S(1)} %get-tuple-element.27.low_ref, bf16[3,256,256]{2,1,0:T(8,128)(2,1)S(1)} %copy-done.9, bf16[192,256]{1,0:T(8,128)(2,1)S(1)} %sum_parts.1._.own_ref), custom_call_target="tpu_custom_call" | custom-call | flops 1073741824 | bytes 3145728 | tf_op jit(solution)/shard_map/section/pallas_call | solution.py:412
  48.4 0.0 collective-permute-done.5.refs_1_.inner_ref
  48.4 0.0 collective-permute-done.6.refs_2_.outer_ref
  48.4 0.6 collective-permute-done.7.theirs_ref
  49.0 0.9 %spread.1._ = bf16[8,192,256]{2,1,0:T(8,128)(2,1)} custom-call(bf16[192,256]{1,0:T(8,128)(2,1)S(1)} %sum_parts.1._.own_ref, bf16[192,256]{1,0:T(8,128)(2,1)S(1)} %collective-permute-done.7.theirs_ref, f32[8,128]{1,0:T(8,128)S(1)} %get-tuple-element.43.refs_0_, bf16[4,2,32,256]{3,2,1,0:T(8,128)(2,1)S(1)} %collective-permute-done.5.refs_1_.inner_ref, ...), custom_call_target="tpu_custom_call" | custom-call | tf_op jit(solution)/shard_map/spread/pallas_call | solution.py:550
  49.9 3.5 %all-to-all-start.1 = ((bf16[8,192,256]{2,1,0:T(8,128)(2,1)}), bf16[8,192,256]{2,1,0:T(8,128)(2,1)S(1)}, u32[]{:S(2)}, u32[]{:S(2)}) async-start(bf16[8,192,256]{2,1,0:T(8,128)(2,1)} %spread.1._), calls=%async_computation.1 | async-start | bytes 1572864 | tf_op jit(solution)/shard_map/all_to_all | solution.py:42
  53.5 0.0 copy-start.7
  53.5 1.3 %copy-done.7 = bf16[3,3,256,256]{3,2,1,0:T(8,128)(2,1)S(1)} copy-done((bf16[3,3,256,256]{3,2,1,0:T(8,128)(2,1)S(1)}, bf16[3,3,256,256]{3,2,1,0:T(8,128)(2,1)}, u32[]{:S(2)}) %copy-start.7) | copy-done | bytes 1179672
  54.8 5.1 %input_grads.1 = (bf16[4,4,32,256]{3,2,1,0:T(8,128)(2,1)}, f32[8,128]{1,0:T(8,128)S(1)}) custom-call(s32[2]{0:T(128)S(1)} %pad_add_fusion.place_ref, bf16[4,4,128,256]{3,2,1,0:T(8,128)(2,1)S(1)} %copy-done.4, bf16[4,2,32,256]{3,2,1,0:T(8,128)(2,1)S(1)} %collective-permute-done.5.refs_1_.inner_ref, ...), custom_call_target="tpu_custom_call" | custom-call | flops 1610612736 | bytes 4194304 | tf_op jit(solution)/shard_map/input_grads/pallas_call | solution.py:465
  59.8 6.1 %all-to-all-done.1 = bf16[8,192,256]{2,1,0:T(8,128)(2,1)S(1)} async-done(((bf16[8,192,256]{2,1,0:T(8,128)(2,1)}), bf16[8,192,256]{2,1,0:T(8,128)(2,1)S(1)}, u32[]{:S(2)}, u32[]{:S(2)}) %all-to-all-start.1) | async-done | bytes 786464 | tf_op jit(solution)/shard_map/all_to_all | solution.py:42
  65.9 0.0 collective-permute-start.8
  65.9 1.8 %put.2 = (f32[3,3,256,256]{3,2,1,0:T(8,128)}, f32[3,256,256]{2,1,0:T(8,128)}) custom-call(s32[2]{0:T(128)S(1)} %pad_add_fusion.place_ref, bf16[12,128,256]{2,1,0:T(8,128)(2,1)S(1)} %after.1.half_ref), custom_call_target="tpu_custom_call" | custom-call | tf_op jit(solution)/shard_map/put/pallas_call | solution.py:497
  67.7 0.5 collective-permute-done.8.half_ref
  68.2 1.8 %put.3 = (f32[3,3,256,256]{3,2,1,0:T(8,128)}, f32[3,256,256]{2,1,0:T(8,128)}) custom-call(s32[2]{0:T(128)S(1)} %pad_add_fusion.1.place_ref, bf16[12,128,256]{2,1,0:T(8,128)(2,1)S(1)} %collective-permute-done.8.half_ref, f32[3,3,256,256]{3,2,1,0:T(8,128)} %get-tuple-element.46.refs_0_, ...), custom_call_target="tpu_custom_call", output_to_operand_aliasing={{0}: (2, {}), {1}: (3, {})} | custom-call | tf_op jit(solution)/shard_map/put/pallas_call | solution.py:497
  (12 shorter events, 0.0 us)
Async XLA Ops:
  2.3 9.5 %collective-permute-start.2 = (bf16[2,8,64,256]{3,2,1,0:T(8,128)(2,1)S(1)}, bf16[2,8,64,256]{3,2,1,0:T(8,128)(2,1)S(1)}, u32[]{:S(2)}, u32[]{:S(2)}) collective-permute-start(bf16[2,8,64,256]{3,2,1,0:T(8,128)(2,1)S(1)} %get-tuple-element.34), channel_id=1, source_target_pairs={{4,0},{8,4},{12,8},{5,1},{9,5},{13,9},{6,2},{10,6},{14,10},{7,3},{... | collective-permute-start | bytes 1572872 | tf_op jit(solution)/shard_map/ppermute | solution.py:39
  3.6 5.8 %collective-permute-start = (bf16[4,1,32,256]{3,2,1,0:T(8,128)(2,1)S(1)}, bf16[4,1,32,256]{3,2,1,0:T(8,128)(2,1)S(1)}, u32[]{:S(2)}, u32[]{:S(2)}) collective-permute-start(bf16[4,1,32,256]{3,2,1,0:T(8,128)(2,1)S(1)} %get-tuple-element.28), channel_id=1, source_target_pairs={{0,1},{1,0},{2,3},{3,2},{4,5},{5,4},{6,7},{7,6},{8,9},{9,8},{10,11... | collective-permute-start | bytes 196616 | tf_op jit(solution)/shard_map/ppermute | solution.py:33
  6.7 2.7 %collective-permute-start.1 = (bf16[4,1,32,256]{3,2,1,0:T(8,128)(2,1)S(1)}, bf16[4,1,32,256]{3,2,1,0:T(8,128)(2,1)S(1)}, u32[]{:S(2)}, u32[]{:S(2)}) collective-permute-start(bf16[4,1,32,256]{3,2,1,0:T(8,128)(2,1)S(1)} %get-tuple-element.29), channel_id=1, source_target_pairs={{1,2},{2,1},{5,6},{6,5},{9,10},{10,9},{13,14},{14,13},{17,18},{18,... | collective-permute-start | bytes 196616 | tf_op jit(solution)/shard_map/ppermute | solution.py:48
  9.4 2.4 %copy-start.5 = (bf16[3,3,256,256]{3,2,1,0:T(8,128)(2,1)}, bf16[3,3,256,256]{3,2,1,0:T(8,128)(2,1)S(1)}, u32[]{:S(2)}) copy-start(bf16[3,3,256,256]{3,2,1,0:T(8,128)(2,1)S(1)} %get-tuple-element.30.ws_ref) | copy-start | bytes 3538948
  9.4 2.4 %copy-start.8 = (bf16[3,256,256]{2,1,0:T(8,128)(2,1)}, bf16[3,256,256]{2,1,0:T(8,128)(2,1)S(1)}, u32[]{:S(2)}) copy-start(bf16[3,256,256]{2,1,0:T(8,128)(2,1)S(1)} %get-tuple-element.35.wt_ref) | copy-start | bytes 1179652
  11.8 5.8 %copy-start.1 = (bf16[4,4,128,256]{3,2,1,0:T(8,128)(2,1)}, bf16[4,4,128,256]{3,2,1,0:T(8,128)(2,1)S(1)}, u32[]{:S(2)}) copy-start(bf16[4,4,128,256]{3,2,1,0:T(8,128)(2,1)S(1)} %get-tuple-element.31.act_ref) | copy-start | bytes 3145732
  15.2 13.1 %copy-start.3 = (bf16[4,4,128,256]{3,2,1,0:T(8,128)(2,1)}, bf16[4,4,128,256]{3,2,1,0:T(8,128)(2,1)S(1)}, u32[]{:S(2)}) copy-start(bf16[4,4,128,256]{3,2,1,0:T(8,128)(2,1)S(1)} %get-tuple-element.36.pg_ref) | copy-start | bytes 3145732
  15.2 5.4 %collective-permute-start.3 = (f32[12,128,256]{2,1,0:T(8,128)S(1)}, f32[12,128,256]{2,1,0:T(8,128)S(1)}, u32[]{:S(2)}, u32[]{:S(2)}) collective-permute-start(f32[12,128,256]{2,1,0:T(8,128)S(1)} %get-tuple-element.38), channel_id=1, source_target_pairs={{0,4},{4,0},{1,5},{5,1},{2,6},{6,2},{3,7},{7,3},{8,12},{12,8},{9,1... | collective-permute-start | bytes 4718600 | tf_op jit(solution)/shard_map/ppermute | solution.py:33
  21.6 20.7 %all-to-all-start = ((bf16[8,192,256]{2,1,0:T(8,128)(2,1)}), bf16[8,192,256]{2,1,0:T(8,128)(2,1)S(1)}, u32[]{:S(2)}, u32[]{:S(2)}) async-start(bf16[8,192,256]{2,1,0:T(8,128)(2,1)} %bitcast.5), calls=%async_computation | async-start | bytes 1572864 | tf_op jit(solution)/shard_map/all_to_all | solution.py:42
  28.3 5.6 %copy-start.6 = (bf16[3,3,256,256]{3,2,1,0:T(8,128)(2,1)S(1)}, bf16[3,3,256,256]{3,2,1,0:T(8,128)(2,1)}, u32[]{:S(2)}) copy-start(bf16[3,3,256,256]{3,2,1,0:T(8,128)(2,1)} %copy-done.5) | copy-start | bytes 3538948
  29.5 4.4 %collective-permute-start.4 = (bf16[2,6,32,256]{3,2,1,0:T(8,128)(2,1)S(1)}, bf16[2,6,32,256]{3,2,1,0:T(8,128)(2,1)S(1)}, u32[]{:S(2)}, u32[]{:S(2)}) collective-permute-start(bf16[2,6,32,256]{3,2,1,0:T(8,128)(2,1)S(1)} %get-tuple-element.39), channel_id=1, source_target_pairs={{0,4},{4,8},{8,12},{1,5},{5,9},{9,13},{2,6},{6,10},{10,14},{3,7},{... | collective-permute-start | bytes 589832 | tf_op jit(solution)/shard_map/ppermute | solution.py:39
  31.3 17.1 %collective-permute-start.5 = (bf16[4,2,32,256]{3,2,1,0:T(8,128)(2,1)}, bf16[4,2,32,256]{3,2,1,0:T(8,128)(2,1)S(1)}, u32[]{:S(2)}, u32[]{:S(2)}) collective-permute-start(bf16[4,2,32,256]{3,2,1,0:T(8,128)(2,1)} %get-tuple-element.41), channel_id=1, source_target_pairs={{0,1},{1,0},{2,3},{3,2},{4,5},{5,4},{6,7},{7,6},{8,9},{9,8},{10,11... | collective-permute-start | bytes 393224 | tf_op jit(solution)/shard_map/ppermute | solution.py:33
  33.1 1.9 %copy-start.2 = (bf16[4,4,128,256]{3,2,1,0:T(8,128)(2,1)S(1)}, bf16[4,4,128,256]{3,2,1,0:T(8,128)(2,1)}, u32[]{:S(2)}) copy-start(bf16[4,4,128,256]{3,2,1,0:T(8,128)(2,1)} %copy-done.1) | copy-start | bytes 3145732
  33.1 15.3 %collective-permute-start.6 = (bf16[4,2,32,256]{3,2,1,0:T(8,128)(2,1)S(1)}, bf16[4,2,32,256]{3,2,1,0:T(8,128)(2,1)S(1)}, u32[]{:S(2)}, u32[]{:S(2)}) collective-permute-start(bf16[4,2,32,256]{3,2,1,0:T(8,128)(2,1)S(1)} %get-tuple-element.42), channel_id=1, source_target_pairs={{1,2},{2,1},{5,6},{6,5},{9,10},{10,9},{13,14},{14,13},{17,18},{18,... | collective-permute-start | bytes 393224 | tf_op jit(solution)/shard_map/ppermute | solution.py:48
  42.4 6.6 %collective-permute-start.7 = (bf16[192,256]{1,0:T(8,128)(2,1)S(1)}, bf16[192,256]{1,0:T(8,128)(2,1)S(1)}, u32[]{:S(2)}, u32[]{:S(2)}) collective-permute-start(bf16[192,256]{1,0:T(8,128)(2,1)S(1)} %sum_parts.1._.own_ref), channel_id=1, source_target_pairs={{0,2},{2,0},{1,3},{3,1},{4,6},{6,4},{5,7},{7,5},{8,10},{10,8},{9,1... | collective-permute-start | bytes 294920 | tf_op jit(solution)/shard_map/ppermute | solution.py:33
  44.2 1.0 %copy-start.9 = (bf16[3,256,256]{2,1,0:T(8,128)(2,1)S(1)}, bf16[3,256,256]{2,1,0:T(8,128)(2,1)}, u32[]{:S(2)}) copy-start(bf16[3,256,256]{2,1,0:T(8,128)(2,1)} %copy-done.8) | copy-start | bytes 1179652
  48.4 5.1 %copy-start = (bf16[1,4,8,64,256]{4,3,2,1,0:T(8,128)(2,1)S(1)}, bf16[1,4,8,64,256]{4,3,2,1,0:T(8,128)(2,1)}, u32[]{:S(2)}) copy-start(bf16[1,4,8,64,256]{4,3,2,1,0:T(8,128)(2,1)} %param.7) | copy-start | bytes 3145732
  48.4 5.1 %copy-start.4 = (bf16[4,4,128,256]{3,2,1,0:T(8,128)(2,1)S(1)}, bf16[4,4,128,256]{3,2,1,0:T(8,128)(2,1)}, u32[]{:S(2)}) copy-start(bf16[4,4,128,256]{3,2,1,0:T(8,128)(2,1)} %copy-done.3) | copy-start | bytes 3145732
  49.9 16.0 %all-to-all-start.1 = ((bf16[8,192,256]{2,1,0:T(8,128)(2,1)}), bf16[8,192,256]{2,1,0:T(8,128)(2,1)S(1)}, u32[]{:S(2)}, u32[]{:S(2)}) async-start(bf16[8,192,256]{2,1,0:T(8,128)(2,1)} %spread.1._), calls=%async_computation.1 | async-start | bytes 1572864 | tf_op jit(solution)/shard_map/all_to_all | solution.py:42
  53.5 1.3 %copy-start.7 = (bf16[3,3,256,256]{3,2,1,0:T(8,128)(2,1)S(1)}, bf16[3,3,256,256]{3,2,1,0:T(8,128)(2,1)}, u32[]{:S(2)}) copy-start(bf16[3,3,256,256]{3,2,1,0:T(8,128)(2,1)} %copy-done.5) | copy-start | bytes 3538948
  65.9 2.3 %collective-permute-start.8 = (bf16[12,128,256]{2,1,0:T(8,128)(2,1)S(1)}, bf16[12,128,256]{2,1,0:T(8,128)(2,1)S(1)}, u32[]{:S(2)}, u32[]{:S(2)}) collective-permute-start(bf16[12,128,256]{2,1,0:T(8,128)(2,1)S(1)} %after.1.half_ref), channel_id=1, source_target_pairs={{0,4},{4,0},{1,5},{5,1},{2,6},{6,2},{3,7},{7,3},{8,12},{12,8},{9,1... | collective-permute-start | bytes 2359304 | tf_op jit(solution)/shard_map/ppermute | solution.py:33

commit v7 on v6

--- a/solution.py
+++ b/solution.py
@@ -38,8 +38,9 @@
         route = [(i - distance, i) for i in devices if i - distance in devices]
         return lax.ppermute(block, axes, route)
 
-    def exchange(self, parts):
-        return lax.all_to_all(parts, tuple(self.near), 0, 0, tiled=True)
+    def send(self, block, mask):
+        near = tuple(self.near)
+        return lax.ppermute(block, near, [(n, n ^ mask) for n in range(1 << len(near))])
 
     def pairs(self, inner, outer):
         axes = self.axes["height"]
@@ -287,22 +288,6 @@
         cost_estimate=cost(2, 4),
         name="load",
     )(in_hbm(low), in_hbm(cot), in_hbm(ws), in_hbm(wt))
-
-
-def nothing(*_):
-    pass
-
-
-def after(arrays, *before):
-    return pl.pallas_call(
-        nothing,
-        in_specs=[UNREAD] * (len(arrays) + len(before)),
-        out_specs=[UNREAD] * len(arrays),
-        out_shape=[like(a.shape, a.dtype) for a in arrays],
-        input_output_aliases={n: n for n in range(len(arrays))},
-        compiler_params=grant(1),
-        name="after",
-    )(*arrays, *before)
 
 
 def forward(place, low, inner, outer, ws):
@@ -506,55 +491,76 @@
     )(place, half, *done)
 
 
-def add_kernel(mine_ref, theirs_ref, out_ref):
-    out_ref[...] = (mine_ref[...] + theirs_ref[...]).astype(jnp.bfloat16)
-
-
-def add_halves(mine, theirs):
-    full = pl.BlockSpec(memory_space=pltpu.VMEM)
+def add_kernel(place_ref, mine_ref, theirs_ref, *outs):
+    rows = outs[0].shape[0]
+    for n, out_ref in enumerate(outs):
+        at = pl.ds(pl.multiple_of((place_ref[2] ^ n) * rows, rows), rows)
+        out_ref[...] = (mine_ref[at] + theirs_ref[at]).astype(jnp.bfloat16)
+
+
+def add_halves(place, parts, mine, theirs):
+    rows, chan = mine.shape
     return pl.pallas_call(
         add_kernel,
-        in_specs=[full, full],
-        out_specs=full,
-        out_shape=like(mine.shape, jnp.bfloat16),
-        compiler_params=grant(8),
+        in_specs=[SCALAR, FULL, FULL],
+        out_specs=[FULL] * parts,
+        out_shape=[like((rows // parts, chan), jnp.bfloat16)] * parts,
+        compiler_params=grant(6),
         name="add_halves",
-    )(mine, theirs)
-
-
-def sum_kernel(got_ref, _, out_ref):
-    total = got_ref[0].astype(jnp.float32)
-    for n in range(1, got_ref.shape[0]):
-        total = total + got_ref[n].astype(jnp.float32)
-    out_ref[...] = total.astype(jnp.bfloat16)
-
-
-def sum_parts(got, before):
+    )(place, mine, theirs)
+
+
+def sum_kernel(*refs):
+    total = refs[0][...].astype(jnp.float32)
+    for ref in refs[1:-2]:
+        total = total + ref[...].astype(jnp.float32)
+    refs[-1][...] = total.astype(jnp.bfloat16)
+
+
+def sum_parts(parts, before):
     return pl.pallas_call(
         sum_kernel,
-        in_specs=[FULL, UNREAD],
+        in_specs=[FULL] * len(parts) + [UNREAD],
         out_specs=FULL,
-        out_shape=like(got.shape[1:], jnp.bfloat16),
+        out_shape=like(parts[0].shape, jnp.bfloat16),
         compiler_params=grant(4),
         name="sum_parts",
-    )(got, before)
-
-
-def spread_kernel(own_ref, theirs_ref, *refs):
-    total = (own_ref[...].astype(jnp.float32) + theirs_ref[...].astype(jnp.float32)).astype(jnp.bfloat16)
-    for n in range(refs[-1].shape[0]):
-        refs[-1][n] = total
-
-
-def spread(own, theirs, parts, *before):
-    return pl.pallas_call(
-        spread_kernel,
+    )(*parts, before)
+
+
+def far_kernel(own_ref, theirs_ref, *refs):
+    refs[-1][...] = (own_ref[...].astype(jnp.float32) + theirs_ref[...].astype(jnp.float32)).astype(jnp.bfloat16)
+
+
+def add_far(own, theirs, *before):
+    return pl.pallas_call(
+        far_kernel,
         in_specs=[FULL, FULL] + [UNREAD] * len(before),
         out_specs=FULL,
-        out_shape=like((parts,) + own.shape, jnp.bfloat16),
+        out_shape=like(own.shape, jnp.bfloat16),
+        compiler_params=grant(2),
+        name="add_far",
+    )(own, theirs, *before)
+
+
+def join_kernel(place_ref, *refs):
+    out_ref = refs[-1]
+    rows = refs[0].shape[0]
+    for n, ref in enumerate(refs[:-2]):
+        at = pl.ds(pl.multiple_of((place_ref[2] ^ n) * rows, rows), rows)
+        out_ref[at] = ref[...]
+
+
+def join(place, parts, before):
+    rows, chan = parts[0].shape
+    return pl.pallas_call(
+        join_kernel,
+        in_specs=[SCALAR] + [FULL] * len(parts) + [UNREAD],
+        out_specs=FULL,
+        out_shape=like((rows * len(parts), chan), jnp.bfloat16),
         compiler_params=grant(4),
-        name="spread",
-    )(own, theirs, *before)
+        name="join",
+    )(place, *parts, before)
 
 
 def on_device(bits, low_frames, spatial_weight, temporal_weight, cotangent):
@@ -562,7 +568,8 @@
     frames, rows_low, cols_low, chan = low.shape
     core = lax.axis_index(bits.core).astype(jnp.int32)
     odd = lax.axis_index(bits.axes["height"][-1]).astype(jnp.int32)
-    mine, other = jnp.stack([core, odd]), jnp.stack([1 - core, odd])
+    code = lax.axis_index(tuple(bits.near)).astype(jnp.int32)
+    mine, other = jnp.stack([core, odd, code]), jnp.stack([1 - core, odd, code])
     parts = 1 << len(bits.near)
 
     inner, outer, later = first_messages(mine, low, cot)
@@ -573,16 +580,18 @@
     pg, ext, theirs = backward(other, low, inner, outer, act, slope, cot_side, later, wt)
     theirs = bits.swap(theirs, bits.core)
     own = half_grads(mine, low, inner, outer, act, pg, ext)
-    kept = add_halves(own, theirs)
-    got = bits.exchange(kept.reshape(parts, -1, chan))
-    edge, pg_inner, pg_outer = edges(mine, low, inner, outer, pg, kept)
+    masks = range(1, parts)
+    flat = (own.shape[0] * own.shape[1], chan)
+    kept = add_halves(mine, parts, own.reshape(flat), theirs.reshape(flat))
+    got = [kept[0]] + [bits.send(kept[n], n) for n in masks]
+    edge, pg_inner, pg_outer = edges(mine, low, inner, outer, pg, kept[0])
     earlier = earlier_act(bits.shift(edge, "tm", 1), ws)
     pg_inner, pg_outer = bits.pairs(pg_inner, pg_outer)
     total, far = bits.far_sums(sum_parts(got, earlier))
     section_out, section_done = section(jnp.concatenate([earlier, act], axis=0), low, wt, total)
-    totals = spread(total, far, parts, section_done, pg_inner, pg_outer)
-    input_grad, input_done = input_grads(mine, pg, pg_inner, pg_outer, cot, ws, totals, low.shape)
-    half, = after([bits.exchange(totals).reshape(kept.shape)], input_done)
+    total = add_far(total, far, section_done, pg_inner, pg_outer)
+    input_grad, input_done = input_grads(mine, pg, pg_inner, pg_outer, cot, ws, total, low.shape)
+    half = join(mine, [total] + [bits.send(total, n) for n in masks], input_done).reshape(own.shape)
     theirs = bits.swap(half, bits.core)
     spatial_grad, temporal_grad = put(other, theirs, *put(mine, half))
     return section_out[None], input_grad[None], spatial_grad, temporal_grad

time: 70.4 us -> 73.3 us (1.041)
  starting transfers between devices: 23.8 us -> 35.9 us
  waiting for transfers between devices: 15 us -> 9.41 us
  local copies, waits for them, and re-layouts: 2.3 us -> 0.01 us
  Pallas kernels: 27.7 us -> 26.6 us
    ppermute x0 -> x14, starting transfers between devices: none -> 22.6 us  [send(): lax.ppermute(block, near, [(n, n ^ mask) for n in range(1 << len(near))])]
    all_to_all x2 -> x0, waiting for transfers between devices: 13.2 us -> none  [exchange(): return lax.all_to_all(parts, tuple(self.near), 0, 0, tiled=True)]
    all_to_all x2 -> x0, starting transfers between devices: 10.2 us -> none  [exchange(): return lax.all_to_all(parts, tuple(self.near), 0, 0, tiled=True)]
    ppermute x0 -> x14, waiting for transfers between devices: none -> 6.38 us  [send(): lax.ppermute(block, near, [(n, n ^ mask) for n in range(1 << len(near))])]
    unnamed x20 -> x2, local copies, waits for them, and re-layouts: 2.3 us -> 0.01 us
    ppermute x5, waiting for transfers between devices: 1.76 us -> 3.02 us  [swap(): return lax.ppermute(block, axis, [(0, 1), (1, 0)])]
  transfers between devices with their start and end apart: 11 -> 23, of which waited for: 5 -> 7; matrix products, arithmetic and copies ran while one was open for 0% -> 0% of each run, Pallas kernels for 27% -> 25%
where the time goes in v7:
time: 73.3 us; the launch traced here: 73 us
  starting transfers between devices  35.9 us (49%)
  Pallas kernels  26.6 us (36%)
  waiting for transfers between devices  9.41 us (13%)
  between operations  0.85 us (1%)
    ppermute x14, starting transfers between devices, send(): lax.ppermute(block, near, [(n, n ^ mask) for n in range(1 << len(near))])  22.6 us
    ppermute x5, starting transfers between devices, swap(): return lax.ppermute(block, axis, [(0, 1), (1, 0)])  8.35 us
    ppermute x14, waiting for transfers between devices, send(): lax.ppermute(block, near, [(n, n ^ mask) for n in range(1 << len(near))])  6.38 us
    pallas_call x1, Pallas kernels, input_grads(): pl.pallas_call(input_kernel, grid=(low_shape[0],), in_specs=[SCALAR, each...  5.13 us
    ppermute x2, starting transfers between devices, shift(): return lax.ppermute(block, axes, route)  3.58 us
    pallas_call x2, Pallas kernels, put(): pl.pallas_call(put_kernel, in_specs=[SCALAR, FULL] + [hbm] * len(done), o...  3.56 us
    pallas_call x1, Pallas kernels, backward(): pl.pallas_call(backward_kernel, in_specs=[SCALAR] + [FULL] * 8, out_specs...  3.39 us
    pallas_call x1, Pallas kernels, section(): pl.pallas_call(section_kernel, grid=(frames,), in_specs=[whole(act_ext.sh...  3.17 us
  transfers between devices with their start and end apart: 23, of which 7 were waited for; matrix products, arithmetic and copies ran while one was open for 0% of the time, Pallas kernels for 25%

profile of v7, /device:TPU:0, one launch (start us, length us, event | category | flops | bytes accessed | tf_op | source)
XLA Modules:
  0.0 73.0 jit_solution(9018556580411597255)
XLA Ops:
  0.6 0.1 add_add_fusion.place_ref
  0.7 1.6 %first_messages.1 = (bf16[4,1,32,256]{3,2,1,0:T(8,128)(2,1)S(1)}, bf16[4,1,32,256]{3,2,1,0:T(8,128)(2,1)S(1)}, bf16[2,8,64,256]{3,2,1,0:T(8,128)(2,1)S(1)}) custom-call(s32[3]{0:T(128)S(1)} %add_add_fusion.place_ref, bf16[4,4,32,256]{3,2,1,0:T(8,128)(2,1)} %bitcast.18, bf16[4,8,64,256]{3,2,1,0:T(8,128)(2,1)} %bitcast.11), custom_call_target="tpu_custom_call" | custom-call | tf_op jit(solution)/shard_map/first_messages/pallas_call | solution.py:253
  2.3 1.3 %collective-permute-start.2 = (bf16[2,8,64,256]{3,2,1,0:T(8,128)(2,1)S(1)}, bf16[2,8,64,256]{3,2,1,0:T(8,128)(2,1)S(1)}, u32[]{:S(2)}, u32[]{:S(2)}) collective-permute-start(bf16[2,8,64,256]{3,2,1,0:T(8,128)(2,1)S(1)} %get-tuple-element.42), channel_id=1, source_target_pairs={{4,0},{8,4},{12,8},{5,1},{9,5},{13,9},{6,2},{10,6},{14,10},{7,3},{... | collective-permute-start | bytes 1572872 | tf_op jit(solution)/shard_map/ppermute | solution.py:39
  3.6 3.1 %collective-permute-start = (bf16[4,1,32,256]{3,2,1,0:T(8,128)(2,1)S(1)}, bf16[4,1,32,256]{3,2,1,0:T(8,128)(2,1)S(1)}, u32[]{:S(2)}, u32[]{:S(2)}) collective-permute-start(bf16[4,1,32,256]{3,2,1,0:T(8,128)(2,1)S(1)} %get-tuple-element.36), channel_id=1, source_target_pairs={{0,1},{1,0},{2,3},{3,2},{4,5},{5,4},{6,7},{7,6},{8,9},{9,8},{10,11... | collective-permute-start | bytes 196616 | tf_op jit(solution)/shard_map/ppermute | solution.py:33
  6.7 0.7 collective-permute-start.1
  7.4 0.1 add_add_fusion.1.place_ref
  7.5 2.0 %load.1 = (bf16[4,4,32,256]{3,2,1,0:T(8,128)(2,1)S(1)}, bf16[3,3,256,256]{3,2,1,0:T(8,128)(2,1)S(1)}, bf16[3,256,256]{2,1,0:T(8,128)(2,1)S(1)}, bf16[4,4,128,256]{3,2,1,0:T(8,128)(2,1)S(1)}) custom-call(bf16[4,4,32,256]{3,2,1,0:T(8,128)(2,1)} %bitcast.19, bf16[4,8,64,256]{3,2,1,0:T(8,128)(2,1)} %bitcast.12, bf16[3,3,256,256]{3,2,1,0:T(8,128)(2,1)} %ws_hbm.1, ...), custom_call_target="tpu_custom_call" | custom-call | flops 536870912 | bytes 4194304 | tf_op jit(solution)/shard_map/load/pallas_call | solution.py:280
  9.4 0.0 collective-permute-done.1.outer_ref
  9.4 2.4 %forward.1 = (bf16[4,4,128,256]{3,2,1,0:T(8,128)(2,1)S(1)}, f32[4,4,128,256]{3,2,1,0:T(8,128)S(1)}) custom-call(s32[3]{0:T(128)S(1)} %add_add_fusion.place_ref, bf16[4,4,32,256]{3,2,1,0:T(8,128)(2,1)S(1)} %get-tuple-element.35.low_ref, bf16[4,1,32,256]{3,2,1,0:T(8,128)(2,1)S(1)} %collective-permute-done.inner_ref, ...), custom_call_target="tpu_custom_call" | custom-call | flops 2684354560 | bytes 8388608 | tf_op jit(solution)/shard_map/forward/pallas_call | solution.py:296
  11.9 3.4 %backward.1 = (bf16[4,4,128,256]{3,2,1,0:T(8,128)(2,1)S(1)}, bf16[6,4,128,256]{3,2,1,0:T(8,128)(2,1)S(1)}, f32[12,128,256]{2,1,0:T(8,128)S(1)}) custom-call(s32[3]{0:T(128)S(1)} %add_add_fusion.1.place_ref, bf16[4,4,32,256]{3,2,1,0:T(8,128)(2,1)S(1)} %get-tuple-element.35.low_ref, bf16[4,1,32,256]{3,2,1,0:T(8,128)(2,1)S(1)} %collective-permute-done.inner_ref, ...), custom_call_target="tpu_custom_call" | custom-call | flops 4026531840 | bytes 10485760 | tf_op jit(solution)/shard_map/backward/pallas_call | solution.py:350
  15.3 2.3 %collective-permute-start.3 = (f32[12,128,256]{2,1,0:T(8,128)S(1)}, f32[12,128,256]{2,1,0:T(8,128)S(1)}, u32[]{:S(2)}, u32[]{:S(2)}) collective-permute-start(f32[12,128,256]{2,1,0:T(8,128)S(1)} %get-tuple-element.46), channel_id=1, source_target_pairs={{0,4},{4,0},{1,5},{5,1},{2,6},{6,2},{3,7},{7,3},{8,12},{12,8},{9,1... | collective-permute-start | bytes 4718600 | tf_op jit(solution)/shard_map/ppermute | solution.py:33
  17.6 2.4 %half_grads.1 = f32[12,128,256]{2,1,0:T(8,128)S(1)} custom-call(s32[3]{0:T(128)S(1)} %add_add_fusion.place_ref, bf16[4,4,32,256]{3,2,1,0:T(8,128)(2,1)S(1)} %get-tuple-element.35.low_ref, bf16[4,1,32,256]{3,2,1,0:T(8,128)(2,1)S(1)} %collective-permute-done.inner_ref, bf16[4,1,32,256]{3,2,1,0:T(8,128)(2,1)S(1)} %collective-permute-done.1.outer_ref, ...), custom_call_target="tpu_custom_call" | custom-call | flops 2684354560 | bytes 6291456 | tf_op jit(solution)/shard_map/half_grads/pallas_call | solution.py:363
  20.0 0.6 collective-permute-done.3
  20.6 0.7 add_halves.1
  21.3 0.6 edges.1
  21.9 2.3 %collective-permute-start.4 = (bf16[2,6,32,256]{3,2,1,0:T(8,128)(2,1)S(1)}, bf16[2,6,32,256]{3,2,1,0:T(8,128)(2,1)S(1)}, u32[]{:S(2)}, u32[]{:S(2)}) collective-permute-start(bf16[2,6,32,256]{3,2,1,0:T(8,128)(2,1)S(1)} %get-tuple-element.48), channel_id=1, source_target_pairs={{0,4},{4,8},{8,12},{1,5},{5,9},{9,13},{2,6},{6,10},{10,14},{3,7},{... | collective-permute-start | bytes 589832 | tf_op jit(solution)/shard_map/ppermute | solution.py:39
  24.2 3.0 %collective-permute-start.5 = (bf16[192,256]{1,0:T(8,128)(2,1)S(1)}, bf16[192,256]{1,0:T(8,128)(2,1)S(1)}, u32[]{:S(2)}, u32[]{:S(2)}) collective-permute-start(bf16[192,256]{1,0:T(8,128)(2,1)S(1)} %get-tuple-element.49), channel_id=1, source_target_pairs={{0,1},{1,0},{8,9},{9,8},{16,17},{17,16},{24,25},{25,24},{2,3},{3,2... | collective-permute-start | bytes 294920 | tf_op jit(solution)/shard_map/ppermute | solution.py:43
  27.2 1.8 %collective-permute-start.6 = (bf16[192,256]{1,0:T(8,128)(2,1)S(1)}, bf16[192,256]{1,0:T(8,128)(2,1)S(1)}, u32[]{:S(2)}, u32[]{:S(2)}) collective-permute-start(bf16[192,256]{1,0:T(8,128)(2,1)S(1)} %get-tuple-element.50), channel_id=1, source_target_pairs={{0,8},{1,9},{8,0},{9,1},{16,24},{17,25},{24,16},{25,17},{2,10},{3,... | collective-permute-start | bytes 294920 | tf_op jit(solution)/shard_map/ppermute | solution.py:43
  29.1 0.0 collective-permute-start.7
  29.1 1.5 %collective-permute-start.8 = (bf16[192,256]{1,0:T(8,128)(2,1)S(1)}, bf16[192,256]{1,0:T(8,128)(2,1)S(1)}, u32[]{:S(2)}, u32[]{:S(2)}) collective-permute-start(bf16[192,256]{1,0:T(8,128)(2,1)S(1)} %get-tuple-element.52), channel_id=1, source_target_pairs={{0,16},{1,17},{8,24},{9,25},{16,0},{17,1},{24,8},{25,9},{2,18},{3,... | collective-permute-start | bytes 294920 | tf_op jit(solution)/shard_map/ppermute | solution.py:43
  30.6 1.6 %collective-permute-start.9 = (bf16[192,256]{1,0:T(8,128)(2,1)S(1)}, bf16[192,256]{1,0:T(8,128)(2,1)S(1)}, u32[]{:S(2)}, u32[]{:S(2)}) collective-permute-start(bf16[192,256]{1,0:T(8,128)(2,1)S(1)} %get-tuple-element.53), channel_id=1, source_target_pairs={{0,17},{1,16},{8,25},{9,24},{16,1},{17,0},{24,9},{25,8},{2,19},{3,... | collective-permute-start | bytes 294920 | tf_op jit(solution)/shard_map/ppermute | solution.py:43
  32.2 1.0 %earlier_act.1.refs_8_ = bf16[2,4,128,256]{3,2,1,0:T(8,128)(2,1)S(1)} custom-call(bf16[2,6,32,256]{3,2,1,0:T(8,128)(2,1)S(1)} %collective-permute-done.4.low_ref, bf16[3,3,256,256]{3,2,1,0:T(8,128)(2,1)S(1)} %get-tuple-element.38.ws_ref), custom_call_target="tpu_custom_call" | custom-call | flops 1073741824 | bytes 3145728 | tf_op jit(solution)/shard_map/earlier_act/pallas_call | solution.py:335
  33.3 5.9 %collective-permute-start.10 = (bf16[192,256]{1,0:T(8,128)(2,1)S(1)}, bf16[192,256]{1,0:T(8,128)(2,1)S(1)}, u32[]{:S(2)}, u32[]{:S(2)}) collective-permute-start(bf16[192,256]{1,0:T(8,128)(2,1)S(1)} %get-tuple-element.54), channel_id=1, source_target_pairs={{0,24},{1,25},{8,16},{9,17},{16,8},{17,9},{24,0},{25,1},{2,26},{3,... | collective-permute-start | bytes 294920 | tf_op jit(solution)/shard_map/ppermute | solution.py:43
  39.1 1.5 %collective-permute-start.12 = (bf16[4,2,32,256]{3,2,1,0:T(8,128)(2,1)S(1)}, bf16[4,2,32,256]{3,2,1,0:T(8,128)(2,1)S(1)}, u32[]{:S(2)}, u32[]{:S(2)}) collective-permute-start(bf16[4,2,32,256]{3,2,1,0:T(8,128)(2,1)S(1)} %get-tuple-element.57), channel_id=1, source_target_pairs={{0,1},{1,0},{2,3},{3,2},{4,5},{5,4},{6,7},{7,6},{8,9},{9,8},{10,11... | collective-permute-start | bytes 393224 | tf_op jit(solution)/shard_map/ppermute | solution.py:33
  40.7 0.7 collective-permute-start.13
  41.3 0.1 pad_maximum_fusion.act_ref
  41.5 1.7 %collective-permute-done.10.refs_6_ = bf16[192,256]{1,0:T(8,128)(2,1)S(1)} collective-permute-done((bf16[192,256]{1,0:T(8,128)(2,1)S(1)}, bf16[192,256]{1,0:T(8,128)(2,1)S(1)}, u32[]{:S(2)}, u32[]{:S(2)}) %collective-permute-start.10) | collective-permute-done | bytes 98336 | tf_op jit(solution)/shard_map/ppermute | solution.py:43
  43.2 2.3 %collective-permute-done.11.refs_7_ = bf16[192,256]{1,0:T(8,128)(2,1)S(1)} collective-permute-done((bf16[192,256]{1,0:T(8,128)(2,1)S(1)}, bf16[192,256]{1,0:T(8,128)(2,1)S(1)}, u32[]{:S(2)}, u32[]{:S(2)}) %collective-permute-start.11) | collective-permute-done | bytes 98336 | tf_op jit(solution)/shard_map/ppermute | solution.py:43
  45.5 0.1 sum_parts.1._.own_ref
  45.6 0.0 copy-start
  45.7 1.3 %collective-permute-start.14 = (bf16[192,256]{1,0:T(8,128)(2,1)S(1)}, bf16[192,256]{1,0:T(8,128)(2,1)S(1)}, u32[]{:S(2)}, u32[]{:S(2)}) collective-permute-start(bf16[192,256]{1,0:T(8,128)(2,1)S(1)} %sum_parts.1._.own_ref), channel_id=1, source_target_pairs={{0,2},{2,0},{1,3},{3,1},{4,6},{6,4},{5,7},{7,5},{8,10},{10,8},{9,1... | collective-permute-start | bytes 294920 | tf_op jit(solution)/shard_map/ppermute | solution.py:33
  47.0 3.2 %section.1 = (bf16[4,8,64,256]{3,2,1,0:T(8,128)(2,1)}, f32[8,128]{1,0:T(8,128)S(1)}) custom-call(bf16[6,4,128,256]{3,2,1,0:T(8,128)(2,1)S(1)} %pad_maximum_fusion.act_ref, bf16[4,4,32,256]{3,2,1,0:T(8,128)(2,1)S(1)} %get-tuple-element.35.low_ref, bf16[3,256,256]{2,1,0:T(8,128)(2,1)S(1)} %get-tuple-element.43.wt_ref, bf16[192,256]{1,0:T(8,128)(2,1)S(1)} %sum_parts.1._.own_ref), custom_call_target="tpu_custom_call" | custom-call | flops 1073741824 | bytes 3145728 | tf_op jit(solution)/shard_map/section/pallas_call | solution.py:397
  50.1 1.9 %collective-permute-done.14.theirs_ref = bf16[192,256]{1,0:T(8,128)(2,1)S(1)} collective-permute-done((bf16[192,256]{1,0:T(8,128)(2,1)S(1)}, bf16[192,256]{1,0:T(8,128)(2,1)S(1)}, u32[]{:S(2)}, u32[]{:S(2)}) %collective-permute-start.14) | collective-permute-done | bytes 98336 | tf_op jit(solution)/shard_map/ppermute | solution.py:33
  52.1 1.1 %collective-permute-start.21 = (bf16[192,256]{1,0:T(8,128)(2,1)S(1)}, bf16[192,256]{1,0:T(8,128)(2,1)S(1)}, u32[]{:S(2)}, u32[]{:S(2)}) collective-permute-start(bf16[192,256]{1,0:T(8,128)(2,1)S(1)} %add_far.1._.refs_0_), channel_id=1, source_target_pairs={{0,25},{1,24},{8,17},{9,16},{16,9},{17,8},{24,1},{25,0},{2,27},{3,... | collective-permute-start | bytes 294920 | tf_op jit(solution)/shard_map/ppermute | solution.py:43
  53.1 1.5 %collective-permute-start.20 = (bf16[192,256]{1,0:T(8,128)(2,1)S(1)}, bf16[192,256]{1,0:T(8,128)(2,1)S(1)}, u32[]{:S(2)}, u32[]{:S(2)}) collective-permute-start(bf16[192,256]{1,0:T(8,128)(2,1)S(1)} %add_far.1._.refs_0_), channel_id=1, source_target_pairs={{0,24},{1,25},{8,16},{9,17},{16,8},{17,9},{24,0},{25,1},{2,26},{3,... | collective-permute-start | bytes 294920 | tf_op jit(solution)/shard_map/ppermute | solution.py:43
  54.6 2.9 %collective-permute-start.19 = (bf16[192,256]{1,0:T(8,128)(2,1)S(1)}, bf16[192,256]{1,0:T(8,128)(2,1)S(1)}, u32[]{:S(2)}, u32[]{:S(2)}) collective-permute-start(bf16[192,256]{1,0:T(8,128)(2,1)S(1)} %add_far.1._.refs_0_), channel_id=1, source_target_pairs={{0,17},{1,16},{8,25},{9,24},{16,1},{17,0},{24,9},{25,8},{2,19},{3,... | collective-permute-start | bytes 294920 | tf_op jit(solution)/shard_map/ppermute | solution.py:43
  57.5 0.5 collective-permute-start.18
  58.0 0.6 collective-permute-start.17
  58.6 1.2 %collective-permute-done.21.refs_7_ = bf16[192,256]{1,0:T(8,128)(2,1)S(1)} collective-permute-done((bf16[192,256]{1,0:T(8,128)(2,1)S(1)}, bf16[192,256]{1,0:T(8,128)(2,1)S(1)}, u32[]{:S(2)}, u32[]{:S(2)}) %collective-permute-start.21) | collective-permute-done | bytes 98336 | tf_op jit(solution)/shard_map/ppermute | solution.py:43
  59.8 0.1 collective-permute-start.16
  59.9 1.2 %collective-permute-done.20.refs_6_ = bf16[192,256]{1,0:T(8,128)(2,1)S(1)} collective-permute-done((bf16[192,256]{1,0:T(8,128)(2,1)S(1)}, bf16[192,256]{1,0:T(8,128)(2,1)S(1)}, u32[]{:S(2)}, u32[]{:S(2)}) %collective-permute-start.20) | collective-permute-done | bytes 98336 | tf_op jit(solution)/shard_map/ppermute | solution.py:43
  61.0 2.1 %collective-permute-start.15 = (bf16[192,256]{1,0:T(8,128)(2,1)S(1)}, bf16[192,256]{1,0:T(8,128)(2,1)S(1)}, u32[]{:S(2)}, u32[]{:S(2)}) collective-permute-start(bf16[192,256]{1,0:T(8,128)(2,1)S(1)} %add_far.1._.refs_0_), channel_id=1, source_target_pairs={{0,1},{1,0},{8,9},{9,8},{16,17},{17,16},{24,25},{25,24},{2,3},{3,2... | collective-permute-start | bytes 294920 | tf_op jit(solution)/shard_map/ppermute | solution.py:43
  63.1 5.1 %input_grads.1 = (bf16[4,4,32,256]{3,2,1,0:T(8,128)(2,1)}, f32[8,128]{1,0:T(8,128)S(1)}) custom-call(s32[3]{0:T(128)S(1)} %add_add_fusion.place_ref, bf16[4,4,128,256]{3,2,1,0:T(8,128)(2,1)S(1)} %get-tuple-element.44.pg_ref, bf16[4,2,32,256]{3,2,1,0:T(8,128)(2,1)S(1)} %collective-permute-done.12.refs_1_.inner_ref, ...), custom_call_target="tpu_custom_call" | custom-call | flops 1610612736 | bytes 4194304 | tf_op jit(solution)/shard_map/input_grads/pallas_call | solution.py:450
  68.3 0.6 join.1
  68.9 0.1 collective-permute-start.22
  69.0 1.8 %put.2 = (f32[3,3,256,256]{3,2,1,0:T(8,128)}, f32[3,256,256]{2,1,0:T(8,128)}) custom-call(s32[3]{0:T(128)S(1)} %add_add_fusion.place_ref, bf16[12,128,256]{2,1,0:T(8,128)(2,1)S(1)} %bitcast.15), custom_call_target="tpu_custom_call" | custom-call | tf_op jit(solution)/shard_map/put/pallas_call | solution.py:482
  70.8 0.5 collective-permute-done.22.half_ref
  71.3 1.8 %put.3 = (f32[3,3,256,256]{3,2,1,0:T(8,128)}, f32[3,256,256]{2,1,0:T(8,128)}) custom-call(s32[3]{0:T(128)S(1)} %add_add_fusion.1.place_ref, bf16[12,128,256]{2,1,0:T(8,128)(2,1)S(1)} %collective-permute-done.22.half_ref, f32[3,3,256,256]{3,2,1,0:T(8,128)} %get-tuple-element.62.refs_0_, ...), custom_call_target="tpu_custom_call", output_to_operand_aliasing={{0}: (2, {}), {1}: (3, {})} | custom-call | tf_op jit(solution)/shard_map/put/pallas_call | solution.py:482
  (18 shorter events, 0.1 us)
Async XLA Ops:
  2.3 9.5 %collective-permute-start.2 = (bf16[2,8,64,256]{3,2,1,0:T(8,128)(2,1)S(1)}, bf16[2,8,64,256]{3,2,1,0:T(8,128)(2,1)S(1)}, u32[]{:S(2)}, u32[]{:S(2)}) collective-permute-start(bf16[2,8,64,256]{3,2,1,0:T(8,128)(2,1)S(1)} %get-tuple-element.42), channel_id=1, source_target_pairs={{4,0},{8,4},{12,8},{5,1},{9,5},{13,9},{6,2},{10,6},{14,10},{7,3},{... | collective-permute-start | bytes 1572872 | tf_op jit(solution)/shard_map/ppermute | solution.py:39
  3.6 5.8 %collective-permute-start = (bf16[4,1,32,256]{3,2,1,0:T(8,128)(2,1)S(1)}, bf16[4,1,32,256]{3,2,1,0:T(8,128)(2,1)S(1)}, u32[]{:S(2)}, u32[]{:S(2)}) collective-permute-start(bf16[4,1,32,256]{3,2,1,0:T(8,128)(2,1)S(1)} %get-tuple-element.36), channel_id=1, source_target_pairs={{0,1},{1,0},{2,3},{3,2},{4,5},{5,4},{6,7},{7,6},{8,9},{9,8},{10,11... | collective-permute-start | bytes 196616 | tf_op jit(solution)/shard_map/ppermute | solution.py:33
  6.7 2.7 %collective-permute-start.1 = (bf16[4,1,32,256]{3,2,1,0:T(8,128)(2,1)S(1)}, bf16[4,1,32,256]{3,2,1,0:T(8,128)(2,1)S(1)}, u32[]{:S(2)}, u32[]{:S(2)}) collective-permute-start(bf16[4,1,32,256]{3,2,1,0:T(8,128)(2,1)S(1)} %get-tuple-element.37), channel_id=1, source_target_pairs={{1,2},{2,1},{5,6},{6,5},{9,10},{10,9},{13,14},{14,13},{17,18},{18,... | collective-permute-start | bytes 196616 | tf_op jit(solution)/shard_map/ppermute | solution.py:49
  15.3 5.4 %collective-permute-start.3 = (f32[12,128,256]{2,1,0:T(8,128)S(1)}, f32[12,128,256]{2,1,0:T(8,128)S(1)}, u32[]{:S(2)}, u32[]{:S(2)}) collective-permute-start(f32[12,128,256]{2,1,0:T(8,128)S(1)} %get-tuple-element.46), channel_id=1, source_target_pairs={{0,4},{4,0},{1,5},{5,1},{2,6},{6,2},{3,7},{7,3},{8,12},{12,8},{9,1... | collective-permute-start | bytes 4718600 | tf_op jit(solution)/shard_map/ppermute | solution.py:33
  21.9 8.7 %collective-permute-start.4 = (bf16[2,6,32,256]{3,2,1,0:T(8,128)(2,1)S(1)}, bf16[2,6,32,256]{3,2,1,0:T(8,128)(2,1)S(1)}, u32[]{:S(2)}, u32[]{:S(2)}) collective-permute-start(bf16[2,6,32,256]{3,2,1,0:T(8,128)(2,1)S(1)} %get-tuple-element.48), channel_id=1, source_target_pairs={{0,4},{4,8},{8,12},{1,5},{5,9},{9,13},{2,6},{6,10},{10,14},{3,7},{... | collective-permute-start | bytes 589832 | tf_op jit(solution)/shard_map/ppermute | solution.py:39
  24.2 9.0 %collective-permute-start.5 = (bf16[192,256]{1,0:T(8,128)(2,1)S(1)}, bf16[192,256]{1,0:T(8,128)(2,1)S(1)}, u32[]{:S(2)}, u32[]{:S(2)}) collective-permute-start(bf16[192,256]{1,0:T(8,128)(2,1)S(1)} %get-tuple-element.49), channel_id=1, source_target_pairs={{0,1},{1,0},{8,9},{9,8},{16,17},{17,16},{24,25},{25,24},{2,3},{3,2... | collective-permute-start | bytes 294920 | tf_op jit(solution)/shard_map/ppermute | solution.py:43
  27.2 11.9 %collective-permute-start.6 = (bf16[192,256]{1,0:T(8,128)(2,1)S(1)}, bf16[192,256]{1,0:T(8,128)(2,1)S(1)}, u32[]{:S(2)}, u32[]{:S(2)}) collective-permute-start(bf16[192,256]{1,0:T(8,128)(2,1)S(1)} %get-tuple-element.50), channel_id=1, source_target_pairs={{0,8},{1,9},{8,0},{9,1},{16,24},{17,25},{24,16},{25,17},{2,10},{3,... | collective-permute-start | bytes 294920 | tf_op jit(solution)/shard_map/ppermute | solution.py:43
  29.1 10.1 %collective-permute-start.7 = (bf16[192,256]{1,0:T(8,128)(2,1)S(1)}, bf16[192,256]{1,0:T(8,128)(2,1)S(1)}, u32[]{:S(2)}, u32[]{:S(2)}) collective-permute-start(bf16[192,256]{1,0:T(8,128)(2,1)S(1)} %get-tuple-element.51), channel_id=1, source_target_pairs={{0,9},{1,8},{8,1},{9,0},{16,25},{17,24},{24,17},{25,16},{2,11},{3,... | collective-permute-start | bytes 294920 | tf_op jit(solution)/shard_map/ppermute | solution.py:43
  29.1 11.6 %collective-permute-start.8 = (bf16[192,256]{1,0:T(8,128)(2,1)S(1)}, bf16[192,256]{1,0:T(8,128)(2,1)S(1)}, u32[]{:S(2)}, u32[]{:S(2)}) collective-permute-start(bf16[192,256]{1,0:T(8,128)(2,1)S(1)} %get-tuple-element.52), channel_id=1, source_target_pairs={{0,16},{1,17},{8,24},{9,25},{16,0},{17,1},{24,8},{25,9},{2,18},{3,... | collective-permute-start | bytes 294920 | tf_op jit(solution)/shard_map/ppermute | solution.py:43
  30.6 10.9 %collective-permute-start.9 = (bf16[192,256]{1,0:T(8,128)(2,1)S(1)}, bf16[192,256]{1,0:T(8,128)(2,1)S(1)}, u32[]{:S(2)}, u32[]{:S(2)}) collective-permute-start(bf16[192,256]{1,0:T(8,128)(2,1)S(1)} %get-tuple-element.53), channel_id=1, source_target_pairs={{0,17},{1,16},{8,25},{9,24},{16,1},{17,0},{24,9},{25,8},{2,19},{3,... | collective-permute-start | bytes 294920 | tf_op jit(solution)/shard_map/ppermute | solution.py:43
  33.3 10.0 %collective-permute-start.10 = (bf16[192,256]{1,0:T(8,128)(2,1)S(1)}, bf16[192,256]{1,0:T(8,128)(2,1)S(1)}, u32[]{:S(2)}, u32[]{:S(2)}) collective-permute-start(bf16[192,256]{1,0:T(8,128)(2,1)S(1)} %get-tuple-element.54), channel_id=1, source_target_pairs={{0,24},{1,25},{8,16},{9,17},{16,8},{17,9},{24,0},{25,1},{2,26},{3,... | collective-permute-start | bytes 294920 | tf_op jit(solution)/shard_map/ppermute | solution.py:43
  39.1 6.4 %collective-permute-start.11 = (bf16[192,256]{1,0:T(8,128)(2,1)S(1)}, bf16[192,256]{1,0:T(8,128)(2,1)S(1)}, u32[]{:S(2)}, u32[]{:S(2)}) collective-permute-start(bf16[192,256]{1,0:T(8,128)(2,1)S(1)} %get-tuple-element.55), channel_id=1, source_target_pairs={{0,25},{1,24},{8,17},{9,16},{16,9},{17,8},{24,1},{25,0},{2,27},{3,... | collective-permute-start | bytes 294920 | tf_op jit(solution)/shard_map/ppermute | solution.py:43
  39.1 11.0 %collective-permute-start.12 = (bf16[4,2,32,256]{3,2,1,0:T(8,128)(2,1)S(1)}, bf16[4,2,32,256]{3,2,1,0:T(8,128)(2,1)S(1)}, u32[]{:S(2)}, u32[]{:S(2)}) collective-permute-start(bf16[4,2,32,256]{3,2,1,0:T(8,128)(2,1)S(1)} %get-tuple-element.57), channel_id=1, source_target_pairs={{0,1},{1,0},{2,3},{3,2},{4,5},{5,4},{6,7},{7,6},{8,9},{9,8},{10,11... | collective-permute-start | bytes 393224 | tf_op jit(solution)/shard_map/ppermute | solution.py:33
  40.7 9.5 %collective-permute-start.13 = (bf16[4,2,32,256]{3,2,1,0:T(8,128)(2,1)S(1)}, bf16[4,2,32,256]{3,2,1,0:T(8,128)(2,1)S(1)}, u32[]{:S(2)}, u32[]{:S(2)}) collective-permute-start(bf16[4,2,32,256]{3,2,1,0:T(8,128)(2,1)S(1)} %get-tuple-element.58), channel_id=1, source_target_pairs={{1,2},{2,1},{5,6},{6,5},{9,10},{10,9},{13,14},{14,13},{17,18},{18,... | collective-permute-start | bytes 393224 | tf_op jit(solution)/shard_map/ppermute | solution.py:49
  45.6 17.5 %copy-start = (bf16[1,4,8,64,256]{4,3,2,1,0:T(8,128)(2,1)S(1)}, bf16[1,4,8,64,256]{4,3,2,1,0:T(8,128)(2,1)}, u32[]{:S(2)}) copy-start(bf16[1,4,8,64,256]{4,3,2,1,0:T(8,128)(2,1)} %param.7) | copy-start | bytes 3145732
  45.7 6.4 %collective-permute-start.14 = (bf16[192,256]{1,0:T(8,128)(2,1)S(1)}, bf16[192,256]{1,0:T(8,128)(2,1)S(1)}, u32[]{:S(2)}, u32[]{:S(2)}) collective-permute-start(bf16[192,256]{1,0:T(8,128)(2,1)S(1)} %sum_parts.1._.own_ref), channel_id=1, source_target_pairs={{0,2},{2,0},{1,3},{3,1},{4,6},{6,4},{5,7},{7,5},{8,10},{10,8},{9,1... | collective-permute-start | bytes 294920 | tf_op jit(solution)/shard_map/ppermute | solution.py:33
  52.1 7.7 %collective-permute-start.21 = (bf16[192,256]{1,0:T(8,128)(2,1)S(1)}, bf16[192,256]{1,0:T(8,128)(2,1)S(1)}, u32[]{:S(2)}, u32[]{:S(2)}) collective-permute-start(bf16[192,256]{1,0:T(8,128)(2,1)S(1)} %add_far.1._.refs_0_), channel_id=1, source_target_pairs={{0,25},{1,24},{8,17},{9,16},{16,9},{17,8},{24,1},{25,0},{2,27},{3,... | collective-permute-start | bytes 294920 | tf_op jit(solution)/shard_map/ppermute | solution.py:43
  53.1 7.9 %collective-permute-start.20 = (bf16[192,256]{1,0:T(8,128)(2,1)S(1)}, bf16[192,256]{1,0:T(8,128)(2,1)S(1)}, u32[]{:S(2)}, u32[]{:S(2)}) collective-permute-start(bf16[192,256]{1,0:T(8,128)(2,1)S(1)} %add_far.1._.refs_0_), channel_id=1, source_target_pairs={{0,24},{1,25},{8,16},{9,17},{16,8},{17,9},{24,0},{25,1},{2,26},{3,... | collective-permute-start | bytes 294920 | tf_op jit(solution)/shard_map/ppermute | solution.py:43
  54.6 13.7 %collective-permute-start.19 = (bf16[192,256]{1,0:T(8,128)(2,1)S(1)}, bf16[192,256]{1,0:T(8,128)(2,1)S(1)}, u32[]{:S(2)}, u32[]{:S(2)}) collective-permute-start(bf16[192,256]{1,0:T(8,128)(2,1)S(1)} %add_far.1._.refs_0_), channel_id=1, source_target_pairs={{0,17},{1,16},{8,25},{9,24},{16,1},{17,0},{24,9},{25,8},{2,19},{3,... | collective-permute-start | bytes 294920 | tf_op jit(solution)/shard_map/ppermute | solution.py:43
  57.5 10.8 %collective-permute-start.18 = (bf16[192,256]{1,0:T(8,128)(2,1)S(1)}, bf16[192,256]{1,0:T(8,128)(2,1)S(1)}, u32[]{:S(2)}, u32[]{:S(2)}) collective-permute-start(bf16[192,256]{1,0:T(8,128)(2,1)S(1)} %add_far.1._.refs_0_), channel_id=1, source_target_pairs={{0,16},{1,17},{8,24},{9,25},{16,0},{17,1},{24,8},{25,9},{2,18},{3,... | collective-permute-start | bytes 294920 | tf_op jit(solution)/shard_map/ppermute | solution.py:43
  58.0 10.3 %collective-permute-start.17 = (bf16[192,256]{1,0:T(8,128)(2,1)S(1)}, bf16[192,256]{1,0:T(8,128)(2,1)S(1)}, u32[]{:S(2)}, u32[]{:S(2)}) collective-permute-start(bf16[192,256]{1,0:T(8,128)(2,1)S(1)} %add_far.1._.refs_0_), channel_id=1, source_target_pairs={{0,9},{1,8},{8,1},{9,0},{16,25},{17,24},{24,17},{25,16},{2,11},{3,... | collective-permute-start | bytes 294920 | tf_op jit(solution)/shard_map/ppermute | solution.py:43
  59.8 8.5 %collective-permute-start.16 = (bf16[192,256]{1,0:T(8,128)(2,1)S(1)}, bf16[192,256]{1,0:T(8,128)(2,1)S(1)}, u32[]{:S(2)}, u32[]{:S(2)}) collective-permute-start(bf16[192,256]{1,0:T(8,128)(2,1)S(1)} %add_far.1._.refs_0_), channel_id=1, source_target_pairs={{0,8},{1,9},{8,0},{9,1},{16,24},{17,25},{24,16},{25,17},{2,10},{3,... | collective-permute-start | bytes 294920 | tf_op jit(solution)/shard_map/ppermute | solution.py:43
  61.0 7.3 %collective-permute-start.15 = (bf16[192,256]{1,0:T(8,128)(2,1)S(1)}, bf16[192,256]{1,0:T(8,128)(2,1)S(1)}, u32[]{:S(2)}, u32[]{:S(2)}) collective-permute-start(bf16[192,256]{1,0:T(8,128)(2,1)S(1)} %add_far.1._.refs_0_), channel_id=1, source_target_pairs={{0,1},{1,0},{8,9},{9,8},{16,17},{17,16},{24,25},{25,24},{2,3},{3,2... | collective-permute-start | bytes 294920 | tf_op jit(solution)/shard_map/ppermute | solution.py:43
  68.9 2.4 %collective-permute-start.22 = (bf16[12,128,256]{2,1,0:T(8,128)(2,1)S(1)}, bf16[12,128,256]{2,1,0:T(8,128)(2,1)S(1)}, u32[]{:S(2)}, u32[]{:S(2)}) collective-permute-start(bf16[12,128,256]{2,1,0:T(8,128)(2,1)S(1)} %bitcast.14), channel_id=1, source_target_pairs={{0,4},{4,0},{1,5},{5,1},{2,6},{6,2},{3,7},{7,3},{8,12},{12,8},{9,1... | collective-permute-start | bytes 2359304 | tf_op jit(solution)/shard_map/ppermute | solution.py:33

commit v8 on v7

--- a/solution.py
+++ b/solution.py
@@ -37,6 +37,9 @@
         devices = range(1 << len(axes))
         route = [(i - distance, i) for i in devices if i - distance in devices]
         return lax.ppermute(block, axes, route)
+
+    def exchange(self, parts):
+        return lax.all_to_all(parts, tuple(self.near), 0, 0, tiled=True)
 
     def send(self, block, mask):
         near = tuple(self.near)
@@ -157,7 +160,7 @@
             slope_ref[frame, side] = sig * (1.0 + pre * (1.0 - sig))
 
 
-def act_kernel(low_ref, ws_ref, act_ref):
+def act_kernel(low_ref, ws_ref, _, act_ref):
     for side, pre in enumerate(spatial(low_ref[0], ws_ref)):
         act_ref[0, side] = (pre * jax.nn.sigmoid(pre)).astype(jnp.bfloat16)
 
@@ -329,19 +332,19 @@
     )(place, low, inner, outer, pg, before)
 
 
-def earlier_act(low, ws):
+def earlier_act(low, ws, before):
     frames, rows_tall, cols_low, chan = low.shape
     side = (frames, 4, (rows_tall - 2) * cols_low, chan)
     return pl.pallas_call(
         act_kernel,
         grid=(frames,),
-        in_specs=[each(low.shape), whole(ws.shape)],
+        in_specs=[each(low.shape), whole(ws.shape), UNREAD],
         out_specs=each(side),
         out_shape=like(side, jnp.bfloat16),
         compiler_params=grant(16),
         cost_estimate=cost(4, 3),
         name="earlier_act",
-    )(low, ws)
+    )(low, ws, before)
 
 
 def backward(place, low, inner, outer, act, slope, cot, later, wt):
@@ -491,41 +494,37 @@
     )(place, half, *done)
 
 
-def add_kernel(place_ref, mine_ref, theirs_ref, *outs):
-    rows = outs[0].shape[0]
-    for n, out_ref in enumerate(outs):
-        at = pl.ds(pl.multiple_of((place_ref[2] ^ n) * rows, rows), rows)
-        out_ref[...] = (mine_ref[at] + theirs_ref[at]).astype(jnp.bfloat16)
-
-
-def add_halves(place, parts, mine, theirs):
-    rows, chan = mine.shape
+def add_kernel(mine_ref, theirs_ref, out_ref):
+    out_ref[...] = (mine_ref[...] + theirs_ref[...]).astype(jnp.bfloat16)
+
+
+def add_halves(mine, theirs):
     return pl.pallas_call(
         add_kernel,
-        in_specs=[SCALAR, FULL, FULL],
-        out_specs=[FULL] * parts,
-        out_shape=[like((rows // parts, chan), jnp.bfloat16)] * parts,
+        in_specs=[FULL, FULL],
+        out_specs=FULL,
+        out_shape=like(mine.shape, jnp.bfloat16),
         compiler_params=grant(6),
         name="add_halves",
-    )(place, mine, theirs)
-
-
-def sum_kernel(*refs):
-    total = refs[0][...].astype(jnp.float32)
-    for ref in refs[1:-2]:
-        total = total + ref[...].astype(jnp.float32)
-    refs[-1][...] = total.astype(jnp.bfloat16)
-
-
-def sum_parts(parts, before):
+    )(mine, theirs)
+
+
+def sum_kernel(got_ref, _, out_ref):
+    total = got_ref[0].astype(jnp.float32)
+    for n in range(1, got_ref.shape[0]):
+        total = total + got_ref[n].astype(jnp.float32)
+    out_ref[...] = total.astype(jnp.bfloat16)
+
+
+def sum_parts(got, before):
     return pl.pallas_call(
         sum_kernel,
-        in_specs=[FULL] * len(parts) + [UNREAD],
+        in_specs=[FULL, UNREAD],
         out_specs=FULL,
-        out_shape=like(parts[0].shape, jnp.bfloat16),
+        out_shape=like(got.shape[1:], jnp.bfloat16),
         compiler_params=grant(4),
         name="sum_parts",
-    )(*parts, before)
+    )(got, before)
 
 
 def far_kernel(own_ref, theirs_ref, *refs):
@@ -546,21 +545,21 @@
 def join_kernel(place_ref, *refs):
     out_ref = refs[-1]
     rows = refs[0].shape[0]
-    for n, ref in enumerate(refs[:-2]):
+    for n, ref in enumerate(refs[:-1]):
         at = pl.ds(pl.multiple_of((place_ref[2] ^ n) * rows, rows), rows)
         out_ref[at] = ref[...]
 
 
-def join(place, parts, before):
+def join(place, parts):
     rows, chan = parts[0].shape
     return pl.pallas_call(
         join_kernel,
-        in_specs=[SCALAR] + [FULL] * len(parts) + [UNREAD],
+        in_specs=[SCALAR] + [FULL] * len(parts),
         out_specs=FULL,
         out_shape=like((rows * len(parts), chan), jnp.bfloat16),
         compiler_params=grant(4),
         name="join",
-    )(place, *parts, before)
+    )(place, *parts)
 
 
 def on_device(bits, low_frames, spatial_weight, temporal_weight, cotangent):
@@ -580,18 +579,18 @@
     pg, ext, theirs = backward(other, low, inner, outer, act, slope, cot_side, later, wt)
     theirs = bits.swap(theirs, bits.core)
     own = half_grads(mine, low, inner, outer, act, pg, ext)
-    masks = range(1, parts)
-    flat = (own.shape[0] * own.shape[1], chan)
-    kept = add_halves(mine, parts, own.reshape(flat), theirs.reshape(flat))
-    got = [kept[0]] + [bits.send(kept[n], n) for n in masks]
-    edge, pg_inner, pg_outer = edges(mine, low, inner, outer, pg, kept[0])
-    earlier = earlier_act(bits.shift(edge, "tm", 1), ws)
+    kept = add_halves(own, theirs)
+    got = bits.exchange(kept.reshape(parts, -1, chan))
+
+    edge, pg_inner, pg_outer = edges(mine, low, inner, outer, pg, kept)
     pg_inner, pg_outer = bits.pairs(pg_inner, pg_outer)
-    total, far = bits.far_sums(sum_parts(got, earlier))
+    input_grad, input_done = input_grads(mine, pg, pg_inner, pg_outer, cot, ws, kept, low.shape)
+    edge = bits.shift(edge, "tm", 1)
+    total, far = bits.far_sums(sum_parts(got, input_done))
+    earlier = earlier_act(edge, ws, total)
     section_out, section_done = section(jnp.concatenate([earlier, act], axis=0), low, wt, total)
-    total = add_far(total, far, section_done, pg_inner, pg_outer)
-    input_grad, input_done = input_grads(mine, pg, pg_inner, pg_outer, cot, ws, total, low.shape)
-    half = join(mine, [total] + [bits.send(total, n) for n in masks], input_done).reshape(own.shape)
+    total = add_far(total, far, section_done)
+    half = join(mine, [total] + [bits.send(total, n) for n in range(1, parts)]).reshape(own.shape)
     theirs = bits.swap(half, bits.core)
     spatial_grad, temporal_grad = put(other, theirs, *put(mine, half))
     return section_out[None], input_grad[None], spatial_grad, temporal_grad

time: 73.3 us -> 76.9 us (1.049)
  starting transfers between devices: 35.9 us -> 30.5 us
  waiting for transfers between devices: 9.41 us -> 13.7 us
  local copies, waits for them, and re-layouts: 0.01 us -> 3.36 us
  Pallas kernels: 26.6 us -> 27.7 us
    ppermute x14 -> x7, starting transfers between devices: 22.6 us -> 9.74 us  [send(): lax.ppermute(block, near, [(n, n ^ mask) for n in range(1 << len(near))])]
    all_to_all x0 -> x1, starting transfers between devices: none -> 6.76 us  [exchange(): return lax.all_to_all(parts, tuple(self.near), 0, 0, tiled=True)]
    ppermute x5, waiting for transfers between devices: 3.02 us -> 8.47 us  [swap(): return lax.ppermute(block, axis, [(0, 1), (1, 0)])]
    unnamed x2 -> x18, local copies, waits for them, and re-layouts: 0.01 us -> 3.36 us
    ppermute x14 -> x7, waiting for transfers between devices: 6.38 us -> 5.2 us  [send(): lax.ppermute(block, near, [(n, n ^ mask) for n in range(1 << len(near))])]
    ppermute x5, starting transfers between devices: 8.35 us -> 9.47 us  [swap(): return lax.ppermute(block, axis, [(0, 1), (1, 0)])]
    pallas_call x1, Pallas kernels: 1.04 us -> 1.94 us  [earlier_act(): pl.pallas_call(act_kernel, grid=(frames,), in_specs=[each(low.shape), who...]
  transfers between devices with their start and end apart: 23 -> 17, of which waited for: 7 -> 8; matrix products, arithmetic and copies ran while one was open for 0% -> 0% of each run, Pallas kernels for 25% -> 25%
where the time goes in v8:
time: 76.9 us; the launch traced here: 76.4 us
  starting transfers between devices  30.5 us (40%)
  Pallas kernels  27.7 us (36%)
  waiting for transfers between devices  13.7 us (18%)
  local copies, waits for them, and re-layouts  3.36 us (4%)
  between operations  0.87 us (1%)
    ppermute x7, starting transfers between devices, send(): lax.ppermute(block, near, [(n, n ^ mask) for n in range(1 << len(near))])  9.74 us
    ppermute x5, starting transfers between devices, swap(): return lax.ppermute(block, axis, [(0, 1), (1, 0)])  9.47 us
    ppermute x5, waiting for transfers between devices, swap(): return lax.ppermute(block, axis, [(0, 1), (1, 0)])  8.47 us
    all_to_all x1, starting transfers between devices, exchange(): return lax.all_to_all(parts, tuple(self.near), 0, 0, tiled=True)  6.76 us
    ppermute x7, waiting for transfers between devices, send(): lax.ppermute(block, near, [(n, n ^ mask) for n in range(1 << len(near))])  5.2 us
    pallas_call x1, Pallas kernels, input_grads(): pl.pallas_call(input_kernel, grid=(low_shape[0],), in_specs=[SCALAR, each...  5.08 us
    pallas_call x2, Pallas kernels, put(): pl.pallas_call(put_kernel, in_specs=[SCALAR, FULL] + [hbm] * len(done), o...  3.56 us
    pallas_call x1, Pallas kernels, backward(): pl.pallas_call(backward_kernel, in_specs=[SCALAR] + [FULL] * 8, out_specs...  3.38 us
  transfers between devices with their start and end apart: 17, of which 8 were waited for; matrix products, arithmetic and copies ran while one was open for 0% of the time, Pallas kernels for 25%

profile of v8, /device:TPU:0, one launch (start us, length us, event | category | flops | bytes accessed | tf_op | source)
XLA Modules:
  0.0 76.4 jit_solution(6656172534657659381)
XLA Ops:
  0.6 0.1 add_add_fusion.place_ref
  0.7 1.6 %first_messages.1 = (bf16[4,1,32,256]{3,2,1,0:T(8,128)(2,1)S(1)}, bf16[4,1,32,256]{3,2,1,0:T(8,128)(2,1)S(1)}, bf16[2,8,64,256]{3,2,1,0:T(8,128)(2,1)S(1)}) custom-call(s32[3]{0:T(128)S(1)} %add_add_fusion.place_ref, bf16[4,4,32,256]{3,2,1,0:T(8,128)(2,1)} %bitcast.15, bf16[4,8,64,256]{3,2,1,0:T(8,128)(2,1)} %bitcast.10), custom_call_target="tpu_custom_call" | custom-call | tf_op jit(solution)/shard_map/first_messages/pallas_call | solution.py:256
  2.3 1.3 %collective-permute-start.2 = (bf16[2,8,64,256]{3,2,1,0:T(8,128)(2,1)S(1)}, bf16[2,8,64,256]{3,2,1,0:T(8,128)(2,1)S(1)}, u32[]{:S(2)}, u32[]{:S(2)}) collective-permute-start(bf16[2,8,64,256]{3,2,1,0:T(8,128)(2,1)S(1)} %get-tuple-element.34), channel_id=1, source_target_pairs={{4,0},{8,4},{12,8},{5,1},{9,5},{13,9},{6,2},{10,6},{14,10},{7,3},{... | collective-permute-start | bytes 1572872 | tf_op jit(solution)/shard_map/ppermute | solution.py:39
  3.6 3.1 %collective-permute-start = (bf16[4,1,32,256]{3,2,1,0:T(8,128)(2,1)S(1)}, bf16[4,1,32,256]{3,2,1,0:T(8,128)(2,1)S(1)}, u32[]{:S(2)}, u32[]{:S(2)}) collective-permute-start(bf16[4,1,32,256]{3,2,1,0:T(8,128)(2,1)S(1)} %get-tuple-element.28), channel_id=1, source_target_pairs={{0,1},{1,0},{2,3},{3,2},{4,5},{5,4},{6,7},{7,6},{8,9},{9,8},{10,11... | collective-permute-start | bytes 196616 | tf_op jit(solution)/shard_map/ppermute | solution.py:33
  6.7 0.7 collective-permute-start.1
  7.4 0.1 add_add_fusion.1.place_ref
  7.5 2.0 %load.1 = (bf16[4,4,32,256]{3,2,1,0:T(8,128)(2,1)S(1)}, bf16[3,3,256,256]{3,2,1,0:T(8,128)(2,1)S(1)}, bf16[3,256,256]{2,1,0:T(8,128)(2,1)S(1)}, bf16[4,4,128,256]{3,2,1,0:T(8,128)(2,1)S(1)}) custom-call(bf16[4,4,32,256]{3,2,1,0:T(8,128)(2,1)} %bitcast.16, bf16[4,8,64,256]{3,2,1,0:T(8,128)(2,1)} %bitcast.11, bf16[3,3,256,256]{3,2,1,0:T(8,128)(2,1)} %ws_hbm.1, ...), custom_call_target="tpu_custom_call" | custom-call | flops 536870912 | bytes 4194304 | tf_op jit(solution)/shard_map/load/pallas_call | solution.py:283
  9.4 0.0 copy-start.4
  9.5 2.3 %forward.1 = (bf16[4,4,128,256]{3,2,1,0:T(8,128)(2,1)S(1)}, f32[4,4,128,256]{3,2,1,0:T(8,128)S(1)}) custom-call(s32[3]{0:T(128)S(1)} %add_add_fusion.place_ref, bf16[4,4,32,256]{3,2,1,0:T(8,128)(2,1)S(1)} %get-tuple-element.27.low_ref, bf16[4,1,32,256]{3,2,1,0:T(8,128)(2,1)S(1)} %collective-permute-done.inner_ref, ...), custom_call_target="tpu_custom_call" | custom-call | flops 2684354560 | bytes 8388608 | tf_op jit(solution)/shard_map/forward/pallas_call | solution.py:299
  11.8 0.0 collective-permute-done.2.later_ref
  11.8 3.4 %backward.1 = (bf16[4,4,128,256]{3,2,1,0:T(8,128)(2,1)S(1)}, bf16[6,4,128,256]{3,2,1,0:T(8,128)(2,1)S(1)}, f32[12,128,256]{2,1,0:T(8,128)S(1)}) custom-call(s32[3]{0:T(128)S(1)} %add_add_fusion.1.place_ref, bf16[4,4,32,256]{3,2,1,0:T(8,128)(2,1)S(1)} %get-tuple-element.27.low_ref, bf16[4,1,32,256]{3,2,1,0:T(8,128)(2,1)S(1)} %collective-permute-done.inner_ref, ...), custom_call_target="tpu_custom_call" | custom-call | flops 4026531840 | bytes 10485760 | tf_op jit(solution)/shard_map/backward/pallas_call | solution.py:353
  15.2 0.0 copy-start.1
  15.2 2.4 %collective-permute-start.3 = (f32[12,128,256]{2,1,0:T(8,128)S(1)}, f32[12,128,256]{2,1,0:T(8,128)S(1)}, u32[]{:S(2)}, u32[]{:S(2)}) collective-permute-start(f32[12,128,256]{2,1,0:T(8,128)S(1)} %get-tuple-element.38), channel_id=1, source_target_pairs={{0,4},{4,0},{1,5},{5,1},{2,6},{6,2},{3,7},{7,3},{8,12},{12,8},{9,1... | collective-permute-start | bytes 4718600 | tf_op jit(solution)/shard_map/ppermute | solution.py:33
  17.6 2.4 %half_grads.1.mine_ref = f32[12,128,256]{2,1,0:T(8,128)S(1)} custom-call(s32[3]{0:T(128)S(1)} %add_add_fusion.place_ref, bf16[4,4,32,256]{3,2,1,0:T(8,128)(2,1)S(1)} %get-tuple-element.27.low_ref, bf16[4,1,32,256]{3,2,1,0:T(8,128)(2,1)S(1)} %collective-permute-done.inner_ref, bf16[4,1,32,256]{3,2,1,0:T(8,128)(2,1)S(1)} %collective-permute-done.1.outer_ref, ...), custom_call_target="tpu_custom_call" | custom-call | flops 2684354560 | bytes 6291456 | tf_op jit(solution)/shard_map/half_grads/pallas_call | solution.py:366
  20.0 0.6 collective-permute-done.3.theirs_ref
  20.6 1.0 %add_halves.1._ = bf16[12,128,256]{2,1,0:T(8,128)(2,1)} custom-call(f32[12,128,256]{2,1,0:T(8,128)S(1)} %half_grads.1.mine_ref, f32[12,128,256]{2,1,0:T(8,128)S(1)} %collective-permute-done.3.theirs_ref), custom_call_target="tpu_custom_call" | custom-call | tf_op jit(solution)/shard_map/add_halves/pallas_call | solution.py:502
  21.7 6.8 %all-to-all-start = ((bf16[8,192,256]{2,1,0:T(8,128)(2,1)}), bf16[8,192,256]{2,1,0:T(8,128)(2,1)S(1)}, u32[]{:S(2)}, u32[]{:S(2)}) async-start(bf16[8,192,256]{2,1,0:T(8,128)(2,1)} %bitcast.6), calls=%async_computation | async-start | bytes 1572864 | tf_op jit(solution)/shard_map/all_to_all | solution.py:42
  28.4 1.2 %copy-done.2 = bf16[4,4,128,256]{3,2,1,0:T(8,128)(2,1)S(1)} copy-done((bf16[4,4,128,256]{3,2,1,0:T(8,128)(2,1)S(1)}, bf16[4,4,128,256]{3,2,1,0:T(8,128)(2,1)}, u32[]{:S(2)}) %copy-start.2) | copy-done | bytes 1048600
  29.7 0.6 edges.1
  30.2 2.1 %collective-permute-start.5 = (bf16[4,2,32,256]{3,2,1,0:T(8,128)(2,1)S(1)}, bf16[4,2,32,256]{3,2,1,0:T(8,128)(2,1)S(1)}, u32[]{:S(2)}, u32[]{:S(2)}) collective-permute-start(bf16[4,2,32,256]{3,2,1,0:T(8,128)(2,1)S(1)} %get-tuple-element.40), channel_id=1, source_target_pairs={{0,1},{1,0},{2,3},{3,2},{4,5},{5,4},{6,7},{7,6},{8,9},{9,8},{10,11... | collective-permute-start | bytes 393224 | tf_op jit(solution)/shard_map/ppermute | solution.py:33
  32.3 0.7 collective-permute-start.6
  33.0 2.0 %collective-permute-start.4 = (bf16[2,6,32,256]{3,2,1,0:T(8,128)(2,1)S(1)}, bf16[2,6,32,256]{3,2,1,0:T(8,128)(2,1)}, u32[]{:S(2)}, u32[]{:S(2)}) collective-permute-start(bf16[2,6,32,256]{3,2,1,0:T(8,128)(2,1)S(1)} %get-tuple-element.39), channel_id=1, source_target_pairs={{0,4},{4,8},{8,12},{1,5},{5,9},{9,13},{2,6},{6,10},{10,14},{3,7},{... | collective-permute-start | bytes 589832 | tf_op jit(solution)/shard_map/ppermute | solution.py:39
  35.0 7.4 %collective-permute-done.5.inner_ref = bf16[4,2,32,256]{3,2,1,0:T(8,128)(2,1)S(1)} collective-permute-done((bf16[4,2,32,256]{3,2,1,0:T(8,128)(2,1)S(1)}, bf16[4,2,32,256]{3,2,1,0:T(8,128)(2,1)S(1)}, u32[]{:S(2)}, u32[]{:S(2)}) %collective-permute-start.5) | collective-permute-done | bytes 131104 | tf_op jit(solution)/shard_map/ppermute | solution.py:33
  42.3 5.1 %input_grads.1 = (bf16[4,4,32,256]{3,2,1,0:T(8,128)(2,1)}, f32[8,128]{1,0:T(8,128)S(1)}) custom-call(s32[3]{0:T(128)S(1)} %add_add_fusion.place_ref, bf16[4,4,128,256]{3,2,1,0:T(8,128)(2,1)S(1)} %copy-done.3, bf16[4,2,32,256]{3,2,1,0:T(8,128)(2,1)S(1)} %collective-permute-done.5.inner_ref, bf16[4,2,32,256]{3,2,1,0:T(8,128)(2,1)S(1)} %collective-permute-done.6.outer_ref, ...), custom_call_target="tpu_custom_call" | custom-call | flops 1610612736 | bytes 4194304 | tf_op jit(solution)/shard_map/input_grads/pallas_call | solution.py:453
  47.4 0.1 sum_parts.1._.own_ref
  47.5 1.8 %collective-permute-start.7 = (bf16[192,256]{1,0:T(8,128)(2,1)S(1)}, bf16[192,256]{1,0:T(8,128)(2,1)S(1)}, u32[]{:S(2)}, u32[]{:S(2)}) collective-permute-start(bf16[192,256]{1,0:T(8,128)(2,1)S(1)} %sum_parts.1._.own_ref), channel_id=1, source_target_pairs={{0,2},{2,0},{1,3},{3,1},{4,6},{6,4},{5,7},{7,5},{8,10},{10,8},{9,1... | collective-permute-start | bytes 294920 | tf_op jit(solution)/shard_map/ppermute | solution.py:33
  49.4 1.3 %copy-done.6 = bf16[3,3,256,256]{3,2,1,0:T(8,128)(2,1)S(1)} copy-done((bf16[3,3,256,256]{3,2,1,0:T(8,128)(2,1)S(1)}, bf16[3,3,256,256]{3,2,1,0:T(8,128)(2,1)}, u32[]{:S(2)}) %copy-start.6) | copy-done | bytes 1179672
  50.6 1.9 %earlier_act.1 = bf16[2,4,128,256]{3,2,1,0:T(8,128)(2,1)S(1)} custom-call(bf16[2,6,32,256]{3,2,1,0:T(8,128)(2,1)} %collective-permute-done.4.low_ref, bf16[3,3,256,256]{3,2,1,0:T(8,128)(2,1)S(1)} %copy-done.6, bf16[192,256]{1,0:T(8,128)(2,1)S(1)} %sum_parts.1._.own_ref), custom_call_target="tpu_custom_call" | custom-call | flops 1073741824 | bytes 3145728 | tf_op jit(solution)/shard_map/earlier_act/pallas_call | solution.py:338
  52.6 0.1 pad_maximum_fusion.act_ref
  52.7 0.8 %copy-done.8 = bf16[3,256,256]{2,1,0:T(8,128)(2,1)S(1)} copy-done((bf16[3,256,256]{2,1,0:T(8,128)(2,1)S(1)}, bf16[3,256,256]{2,1,0:T(8,128)(2,1)}, u32[]{:S(2)}) %copy-start.8) | copy-done | bytes 393240
  53.6 3.2 %section.1 = (bf16[4,8,64,256]{3,2,1,0:T(8,128)(2,1)}, f32[8,128]{1,0:T(8,128)S(1)}) custom-call(bf16[6,4,128,256]{3,2,1,0:T(8,128)(2,1)S(1)} %pad_maximum_fusion.act_ref, bf16[4,4,32,256]{3,2,1,0:T(8,128)(2,1)S(1)} %get-tuple-element.27.low_ref, bf16[3,256,256]{2,1,0:T(8,128)(2,1)S(1)} %copy-done.8, bf16[192,256]{1,0:T(8,128)(2,1)S(1)} %sum_parts.1._.own_ref), custom_call_target="tpu_custom_call" | custom-call | flops 1073741824 | bytes 3145728 | tf_op jit(solution)/shard_map/section/pallas_call | solution.py:400
  56.8 2.5 %collective-permute-start.14 = (bf16[192,256]{1,0:T(8,128)(2,1)S(1)}, bf16[192,256]{1,0:T(8,128)(2,1)S(1)}, u32[]{:S(2)}, u32[]{:S(2)}) collective-permute-start(bf16[192,256]{1,0:T(8,128)(2,1)S(1)} %add_far.1.refs_0_), channel_id=1, source_target_pairs={{0,25},{1,24},{8,17},{9,16},{16,9},{17,8},{24,1},{25,0},{2,27},{3,... | collective-permute-start | bytes 294920 | tf_op jit(solution)/shard_map/ppermute | solution.py:46
  59.2 0.3 collective-permute-start.13
  59.5 2.6 %collective-permute-start.12 = (bf16[192,256]{1,0:T(8,128)(2,1)S(1)}, bf16[192,256]{1,0:T(8,128)(2,1)S(1)}, u32[]{:S(2)}, u32[]{:S(2)}) collective-permute-start(bf16[192,256]{1,0:T(8,128)(2,1)S(1)} %add_far.1.refs_0_), channel_id=1, source_target_pairs={{0,17},{1,16},{8,25},{9,24},{16,1},{17,0},{24,9},{25,8},{2,19},{3,... | collective-permute-start | bytes 294920 | tf_op jit(solution)/shard_map/ppermute | solution.py:46
  62.1 0.6 collective-permute-start.11
  62.7 1.5 %collective-permute-start.10 = (bf16[192,256]{1,0:T(8,128)(2,1)S(1)}, bf16[192,256]{1,0:T(8,128)(2,1)S(1)}, u32[]{:S(2)}, u32[]{:S(2)}) collective-permute-start(bf16[192,256]{1,0:T(8,128)(2,1)S(1)} %add_far.1.refs_0_), channel_id=1, source_target_pairs={{0,9},{1,8},{8,1},{9,0},{16,25},{17,24},{24,17},{25,16},{2,11},{3,... | collective-permute-start | bytes 294920 | tf_op jit(solution)/shard_map/ppermute | solution.py:46
  64.2 0.4 collective-permute-done.14.refs_7_
  64.6 1.4 %collective-permute-start.9 = (bf16[192,256]{1,0:T(8,128)(2,1)S(1)}, bf16[192,256]{1,0:T(8,128)(2,1)S(1)}, u32[]{:S(2)}, u32[]{:S(2)}) collective-permute-start(bf16[192,256]{1,0:T(8,128)(2,1)S(1)} %add_far.1.refs_0_), channel_id=1, source_target_pairs={{0,8},{1,9},{8,0},{9,1},{16,24},{17,25},{24,16},{25,17},{2,10},{3,... | collective-permute-start | bytes 294920 | tf_op jit(solution)/shard_map/ppermute | solution.py:46
  66.0 1.1 %collective-permute-done.13.refs_6_ = bf16[192,256]{1,0:T(8,128)(2,1)S(1)} collective-permute-done((bf16[192,256]{1,0:T(8,128)(2,1)S(1)}, bf16[192,256]{1,0:T(8,128)(2,1)S(1)}, u32[]{:S(2)}, u32[]{:S(2)}) %collective-permute-start.13) | collective-permute-done | bytes 98336 | tf_op jit(solution)/shard_map/ppermute | solution.py:46
  67.1 0.9 %collective-permute-start.8 = (bf16[192,256]{1,0:T(8,128)(2,1)S(1)}, bf16[192,256]{1,0:T(8,128)(2,1)S(1)}, u32[]{:S(2)}, u32[]{:S(2)}) collective-permute-start(bf16[192,256]{1,0:T(8,128)(2,1)S(1)} %add_far.1.refs_0_), channel_id=1, source_target_pairs={{0,1},{1,0},{8,9},{9,8},{16,17},{17,16},{24,25},{25,24},{2,3},{3,2... | collective-permute-start | bytes 294920 | tf_op jit(solution)/shard_map/ppermute | solution.py:46
  68.0 0.6 collective-permute-done.11.refs_4_
  68.6 0.9 %collective-permute-done.9.refs_2_ = bf16[192,256]{1,0:T(8,128)(2,1)S(1)} collective-permute-done((bf16[192,256]{1,0:T(8,128)(2,1)S(1)}, bf16[192,256]{1,0:T(8,128)(2,1)S(1)}, u32[]{:S(2)}, u32[]{:S(2)}) %collective-permute-start.9) | collective-permute-done | bytes 98336 | tf_op jit(solution)/shard_map/ppermute | solution.py:46
  69.6 2.2 %collective-permute-done.8.refs_1_ = bf16[192,256]{1,0:T(8,128)(2,1)S(1)} collective-permute-done((bf16[192,256]{1,0:T(8,128)(2,1)S(1)}, bf16[192,256]{1,0:T(8,128)(2,1)S(1)}, u32[]{:S(2)}, u32[]{:S(2)}) %collective-permute-start.8) | collective-permute-done | bytes 98336 | tf_op jit(solution)/shard_map/ppermute | solution.py:46
  71.7 0.6 join.1
  72.3 0.1 collective-permute-start.15
  72.4 1.8 %put.2 = (f32[3,3,256,256]{3,2,1,0:T(8,128)}, f32[3,256,256]{2,1,0:T(8,128)}) custom-call(s32[3]{0:T(128)S(1)} %add_add_fusion.place_ref, bf16[12,128,256]{2,1,0:T(8,128)(2,1)S(1)} %bitcast.14), custom_call_target="tpu_custom_call" | custom-call | tf_op jit(solution)/shard_map/put/pallas_call | solution.py:485
  74.2 0.5 collective-permute-done.15.half_ref
  74.7 1.8 %put.3 = (f32[3,3,256,256]{3,2,1,0:T(8,128)}, f32[3,256,256]{2,1,0:T(8,128)}) custom-call(s32[3]{0:T(128)S(1)} %add_add_fusion.1.place_ref, bf16[12,128,256]{2,1,0:T(8,128)(2,1)S(1)} %collective-permute-done.15.half_ref, f32[3,3,256,256]{3,2,1,0:T(8,128)} %get-tuple-element.46.refs_0_, ...), custom_call_target="tpu_custom_call", output_to_operand_aliasing={{0}: (2, {}), {1}: (3, {})} | custom-call | tf_op jit(solution)/shard_map/put/pallas_call | solution.py:485
  (22 shorter events, 0.1 us)
Async XLA Ops:
  2.3 9.5 %collective-permute-start.2 = (bf16[2,8,64,256]{3,2,1,0:T(8,128)(2,1)S(1)}, bf16[2,8,64,256]{3,2,1,0:T(8,128)(2,1)S(1)}, u32[]{:S(2)}, u32[]{:S(2)}) collective-permute-start(bf16[2,8,64,256]{3,2,1,0:T(8,128)(2,1)S(1)} %get-tuple-element.34), channel_id=1, source_target_pairs={{4,0},{8,4},{12,8},{5,1},{9,5},{13,9},{6,2},{10,6},{14,10},{7,3},{... | collective-permute-start | bytes 1572872 | tf_op jit(solution)/shard_map/ppermute | solution.py:39
  3.6 5.8 %collective-permute-start = (bf16[4,1,32,256]{3,2,1,0:T(8,128)(2,1)S(1)}, bf16[4,1,32,256]{3,2,1,0:T(8,128)(2,1)S(1)}, u32[]{:S(2)}, u32[]{:S(2)}) collective-permute-start(bf16[4,1,32,256]{3,2,1,0:T(8,128)(2,1)S(1)} %get-tuple-element.28), channel_id=1, source_target_pairs={{0,1},{1,0},{2,3},{3,2},{4,5},{5,4},{6,7},{7,6},{8,9},{9,8},{10,11... | collective-permute-start | bytes 196616 | tf_op jit(solution)/shard_map/ppermute | solution.py:33
  6.7 2.7 %collective-permute-start.1 = (bf16[4,1,32,256]{3,2,1,0:T(8,128)(2,1)S(1)}, bf16[4,1,32,256]{3,2,1,0:T(8,128)(2,1)S(1)}, u32[]{:S(2)}, u32[]{:S(2)}) collective-permute-start(bf16[4,1,32,256]{3,2,1,0:T(8,128)(2,1)S(1)} %get-tuple-element.29), channel_id=1, source_target_pairs={{1,2},{2,1},{5,6},{6,5},{9,10},{10,9},{13,14},{14,13},{17,18},{18,... | collective-permute-start | bytes 196616 | tf_op jit(solution)/shard_map/ppermute | solution.py:52
  9.4 2.4 %copy-start.4 = (bf16[3,3,256,256]{3,2,1,0:T(8,128)(2,1)}, bf16[3,3,256,256]{3,2,1,0:T(8,128)(2,1)S(1)}, u32[]{:S(2)}) copy-start(bf16[3,3,256,256]{3,2,1,0:T(8,128)(2,1)S(1)} %get-tuple-element.30.ws_ref) | copy-start | bytes 3538948
  9.4 2.4 %copy-start.7 = (bf16[3,256,256]{2,1,0:T(8,128)(2,1)}, bf16[3,256,256]{2,1,0:T(8,128)(2,1)S(1)}, u32[]{:S(2)}) copy-start(bf16[3,256,256]{2,1,0:T(8,128)(2,1)S(1)} %get-tuple-element.35.wt_ref) | copy-start | bytes 1179652
  15.2 4.8 %copy-start.1 = (bf16[4,4,128,256]{3,2,1,0:T(8,128)(2,1)}, bf16[4,4,128,256]{3,2,1,0:T(8,128)(2,1)S(1)}, u32[]{:S(2)}) copy-start(bf16[4,4,128,256]{3,2,1,0:T(8,128)(2,1)S(1)} %get-tuple-element.36.pg_ref) | copy-start | bytes 3145732
  15.2 5.4 %collective-permute-start.3 = (f32[12,128,256]{2,1,0:T(8,128)S(1)}, f32[12,128,256]{2,1,0:T(8,128)S(1)}, u32[]{:S(2)}, u32[]{:S(2)}) collective-permute-start(f32[12,128,256]{2,1,0:T(8,128)S(1)} %get-tuple-element.38), channel_id=1, source_target_pairs={{0,4},{4,0},{1,5},{5,1},{2,6},{6,2},{3,7},{7,3},{8,12},{12,8},{9,1... | collective-permute-start | bytes 4718600 | tf_op jit(solution)/shard_map/ppermute | solution.py:33
  21.7 20.7 %copy-start = (bf16[1,4,8,64,256]{4,3,2,1,0:T(8,128)(2,1)S(1)}, bf16[1,4,8,64,256]{4,3,2,1,0:T(8,128)(2,1)}, u32[]{:S(2)}) copy-start(bf16[1,4,8,64,256]{4,3,2,1,0:T(8,128)(2,1)} %param.7) | copy-start | bytes 3145732
  21.7 25.8 %all-to-all-start = ((bf16[8,192,256]{2,1,0:T(8,128)(2,1)}), bf16[8,192,256]{2,1,0:T(8,128)(2,1)S(1)}, u32[]{:S(2)}, u32[]{:S(2)}) async-start(bf16[8,192,256]{2,1,0:T(8,128)(2,1)} %bitcast.6), calls=%async_computation | async-start | bytes 1572864 | tf_op jit(solution)/shard_map/all_to_all | solution.py:42
  28.4 1.2 %copy-start.2 = (bf16[4,4,128,256]{3,2,1,0:T(8,128)(2,1)S(1)}, bf16[4,4,128,256]{3,2,1,0:T(8,128)(2,1)}, u32[]{:S(2)}) copy-start(bf16[4,4,128,256]{3,2,1,0:T(8,128)(2,1)} %copy-done.1) | copy-start | bytes 3145732
  29.6 12.7 %copy-start.3 = (bf16[4,4,128,256]{3,2,1,0:T(8,128)(2,1)S(1)}, bf16[4,4,128,256]{3,2,1,0:T(8,128)(2,1)}, u32[]{:S(2)}) copy-start(bf16[4,4,128,256]{3,2,1,0:T(8,128)(2,1)} %copy-done.1) | copy-start | bytes 3145732
  29.7 12.7 %copy-start.5 = (bf16[3,3,256,256]{3,2,1,0:T(8,128)(2,1)S(1)}, bf16[3,3,256,256]{3,2,1,0:T(8,128)(2,1)}, u32[]{:S(2)}) copy-start(bf16[3,3,256,256]{3,2,1,0:T(8,128)(2,1)} %copy-done.4) | copy-start | bytes 3538948
  30.2 12.1 %collective-permute-start.5 = (bf16[4,2,32,256]{3,2,1,0:T(8,128)(2,1)S(1)}, bf16[4,2,32,256]{3,2,1,0:T(8,128)(2,1)S(1)}, u32[]{:S(2)}, u32[]{:S(2)}) collective-permute-start(bf16[4,2,32,256]{3,2,1,0:T(8,128)(2,1)S(1)} %get-tuple-element.40), channel_id=1, source_target_pairs={{0,1},{1,0},{2,3},{3,2},{4,5},{5,4},{6,7},{7,6},{8,9},{9,8},{10,11... | collective-permute-start | bytes 393224 | tf_op jit(solution)/shard_map/ppermute | solution.py:33
  32.3 10.0 %collective-permute-start.6 = (bf16[4,2,32,256]{3,2,1,0:T(8,128)(2,1)S(1)}, bf16[4,2,32,256]{3,2,1,0:T(8,128)(2,1)S(1)}, u32[]{:S(2)}, u32[]{:S(2)}) collective-permute-start(bf16[4,2,32,256]{3,2,1,0:T(8,128)(2,1)S(1)} %get-tuple-element.41), channel_id=1, source_target_pairs={{1,2},{2,1},{5,6},{6,5},{9,10},{10,9},{13,14},{14,13},{17,18},{18,... | collective-permute-start | bytes 393224 | tf_op jit(solution)/shard_map/ppermute | solution.py:52
  33.0 16.4 %collective-permute-start.4 = (bf16[2,6,32,256]{3,2,1,0:T(8,128)(2,1)S(1)}, bf16[2,6,32,256]{3,2,1,0:T(8,128)(2,1)}, u32[]{:S(2)}, u32[]{:S(2)}) collective-permute-start(bf16[2,6,32,256]{3,2,1,0:T(8,128)(2,1)S(1)} %get-tuple-element.39), channel_id=1, source_target_pairs={{0,4},{4,8},{8,12},{1,5},{5,9},{9,13},{2,6},{6,10},{10,14},{3,7},{... | collective-permute-start | bytes 589832 | tf_op jit(solution)/shard_map/ppermute | solution.py:39
  47.5 9.2 %collective-permute-start.7 = (bf16[192,256]{1,0:T(8,128)(2,1)S(1)}, bf16[192,256]{1,0:T(8,128)(2,1)S(1)}, u32[]{:S(2)}, u32[]{:S(2)}) collective-permute-start(bf16[192,256]{1,0:T(8,128)(2,1)S(1)} %sum_parts.1._.own_ref), channel_id=1, source_target_pairs={{0,2},{2,0},{1,3},{3,1},{4,6},{6,4},{5,7},{7,5},{8,10},{10,8},{9,1... | collective-permute-start | bytes 294920 | tf_op jit(solution)/shard_map/ppermute | solution.py:33
  49.4 1.3 %copy-start.6 = (bf16[3,3,256,256]{3,2,1,0:T(8,128)(2,1)S(1)}, bf16[3,3,256,256]{3,2,1,0:T(8,128)(2,1)}, u32[]{:S(2)}) copy-start(bf16[3,3,256,256]{3,2,1,0:T(8,128)(2,1)} %copy-done.4) | copy-start | bytes 3538948
  52.6 1.0 %copy-start.8 = (bf16[3,256,256]{2,1,0:T(8,128)(2,1)S(1)}, bf16[3,256,256]{2,1,0:T(8,128)(2,1)}, u32[]{:S(2)}) copy-start(bf16[3,256,256]{2,1,0:T(8,128)(2,1)} %copy-done.7) | copy-start | bytes 1179652
  56.8 7.8 %collective-permute-start.14 = (bf16[192,256]{1,0:T(8,128)(2,1)S(1)}, bf16[192,256]{1,0:T(8,128)(2,1)S(1)}, u32[]{:S(2)}, u32[]{:S(2)}) collective-permute-start(bf16[192,256]{1,0:T(8,128)(2,1)S(1)} %add_far.1.refs_0_), channel_id=1, source_target_pairs={{0,25},{1,24},{8,17},{9,16},{16,9},{17,8},{24,1},{25,0},{2,27},{3,... | collective-permute-start | bytes 294920 | tf_op jit(solution)/shard_map/ppermute | solution.py:46
  59.2 7.9 %collective-permute-start.13 = (bf16[192,256]{1,0:T(8,128)(2,1)S(1)}, bf16[192,256]{1,0:T(8,128)(2,1)S(1)}, u32[]{:S(2)}, u32[]{:S(2)}) collective-permute-start(bf16[192,256]{1,0:T(8,128)(2,1)S(1)} %add_far.1.refs_0_), channel_id=1, source_target_pairs={{0,24},{1,25},{8,16},{9,17},{16,8},{17,9},{24,0},{25,1},{2,26},{3,... | collective-permute-start | bytes 294920 | tf_op jit(solution)/shard_map/ppermute | solution.py:46
  59.5 8.5 %collective-permute-start.12 = (bf16[192,256]{1,0:T(8,128)(2,1)S(1)}, bf16[192,256]{1,0:T(8,128)(2,1)S(1)}, u32[]{:S(2)}, u32[]{:S(2)}) collective-permute-start(bf16[192,256]{1,0:T(8,128)(2,1)S(1)} %add_far.1.refs_0_), channel_id=1, source_target_pairs={{0,17},{1,16},{8,25},{9,24},{16,1},{17,0},{24,9},{25,8},{2,19},{3,... | collective-permute-start | bytes 294920 | tf_op jit(solution)/shard_map/ppermute | solution.py:46
  62.1 6.5 %collective-permute-start.11 = (bf16[192,256]{1,0:T(8,128)(2,1)S(1)}, bf16[192,256]{1,0:T(8,128)(2,1)S(1)}, u32[]{:S(2)}, u32[]{:S(2)}) collective-permute-start(bf16[192,256]{1,0:T(8,128)(2,1)S(1)} %add_far.1.refs_0_), channel_id=1, source_target_pairs={{0,16},{1,17},{8,24},{9,25},{16,0},{17,1},{24,8},{25,9},{2,18},{3,... | collective-permute-start | bytes 294920 | tf_op jit(solution)/shard_map/ppermute | solution.py:46
  62.7 5.9 %collective-permute-start.10 = (bf16[192,256]{1,0:T(8,128)(2,1)S(1)}, bf16[192,256]{1,0:T(8,128)(2,1)S(1)}, u32[]{:S(2)}, u32[]{:S(2)}) collective-permute-start(bf16[192,256]{1,0:T(8,128)(2,1)S(1)} %add_far.1.refs_0_), channel_id=1, source_target_pairs={{0,9},{1,8},{8,1},{9,0},{16,25},{17,24},{24,17},{25,16},{2,11},{3,... | collective-permute-start | bytes 294920 | tf_op jit(solution)/shard_map/ppermute | solution.py:46
  64.6 5.0 %collective-permute-start.9 = (bf16[192,256]{1,0:T(8,128)(2,1)S(1)}, bf16[192,256]{1,0:T(8,128)(2,1)S(1)}, u32[]{:S(2)}, u32[]{:S(2)}) collective-permute-start(bf16[192,256]{1,0:T(8,128)(2,1)S(1)} %add_far.1.refs_0_), channel_id=1, source_target_pairs={{0,8},{1,9},{8,0},{9,1},{16,24},{17,25},{24,16},{25,17},{2,10},{3,... | collective-permute-start | bytes 294920 | tf_op jit(solution)/shard_map/ppermute | solution.py:46
  67.1 4.6 %collective-permute-start.8 = (bf16[192,256]{1,0:T(8,128)(2,1)S(1)}, bf16[192,256]{1,0:T(8,128)(2,1)S(1)}, u32[]{:S(2)}, u32[]{:S(2)}) collective-permute-start(bf16[192,256]{1,0:T(8,128)(2,1)S(1)} %add_far.1.refs_0_), channel_id=1, source_target_pairs={{0,1},{1,0},{8,9},{9,8},{16,17},{17,16},{24,25},{25,24},{2,3},{3,2... | collective-permute-start | bytes 294920 | tf_op jit(solution)/shard_map/ppermute | solution.py:46
  72.3 2.4 %collective-permute-start.15 = (bf16[12,128,256]{2,1,0:T(8,128)(2,1)S(1)}, bf16[12,128,256]{2,1,0:T(8,128)(2,1)S(1)}, u32[]{:S(2)}, u32[]{:S(2)}) collective-permute-start(bf16[12,128,256]{2,1,0:T(8,128)(2,1)S(1)} %bitcast.13), channel_id=1, source_target_pairs={{0,4},{4,0},{1,5},{5,1},{2,6},{6,2},{3,7},{7,3},{8,12},{12,8},{9,1... | collective-permute-start | bytes 2359304 | tf_op jit(solution)/shard_map/ppermute | solution.py:33

commit v9 on v6

--- a/solution.py
+++ b/solution.py
@@ -90,14 +90,6 @@
     q, rest = to % cols_low, to // cols_low
     p, side = rest % count, rest // count
     return (at == (p * 2 + side // 2) * 2 * cols_low + 2 * q + side % 2).astype(jnp.float32).astype(dtype)
-
-
-def box(count, cols_low, dtype=jnp.bfloat16):
-    size = 4 * count * cols_low
-    to = lax.broadcasted_iota(jnp.int32, (size // 4, size), 0)
-    at = lax.broadcasted_iota(jnp.int32, (size // 4, size), 1)
-    p, q = at // (4 * cols_low), at % (2 * cols_low) // 2
-    return (to == p * cols_low + q).astype(jnp.float32).astype(dtype)
 
 
 def column(rows, cols_low, chan):
@@ -156,9 +148,10 @@
             slope_ref[frame, side] = sig * (1.0 + pre * (1.0 - sig))
 
 
-def act_kernel(low_ref, ws_ref, act_ref):
-    for side, pre in enumerate(spatial(low_ref[0], ws_ref)):
-        act_ref[0, side] = (pre * jax.nn.sigmoid(pre)).astype(jnp.bfloat16)
+def act_kernel(low_ref, ws_ref, _, act_ref):
+    for frame in range(low_ref.shape[0]):
+        for side, pre in enumerate(spatial(low_ref[frame], ws_ref)):
+            act_ref[frame, side] = (pre * jax.nn.sigmoid(pre)).astype(jnp.bfloat16)
 
 
 def half_sums(place_ref, low_ref, inner_ref, outer_ref, act_ref, pg_ref, ext_ref, out_ref):
@@ -203,14 +196,6 @@
     half_sums(place_ref, low_ref, inner_ref, outer_ref, act_ref, pg_ref, ext_ref, out_ref)
 
 
-def whole(shape):
-    return pl.BlockSpec(shape, lambda f, *_: (0,) * len(shape))
-
-
-def each(shape):
-    return pl.BlockSpec((1,) + tuple(shape[1:]), lambda f, *_: (f,) + (0,) * (len(shape) - 1))
-
-
 SCALAR = pl.BlockSpec(memory_space=pltpu.SMEM)
 UNREAD = pl.BlockSpec(memory_space=pl.ANY)
 
@@ -237,10 +222,11 @@
     last = low_ref.shape[1] - 1
     odd = place_ref[1]
     copies = [
-        pltpu.make_async_copy(cot_ref.at[0:2], later_ref, sems.at[0]),
-        pltpu.make_async_copy(low_ref.at[:, pl.ds(last * (1 - odd), 1)], inner_ref, sems.at[1]),
-        pltpu.make_async_copy(low_ref.at[:, pl.ds(last * odd, 1)], outer_ref, sems.at[2]),
+        (low_ref.at[:, pl.ds(last * (1 - odd), 1)], inner_ref),
+        (low_ref.at[:, pl.ds(last * odd, 1)], outer_ref),
     ]
+    copies += [(cot_ref.at[n, r], later_ref.at[n, r]) for n in range(2) for r in range(cot_ref.shape[1])]
+    copies = [pltpu.make_async_copy(a, b, sems.at[n]) for n, (a, b) in enumerate(copies)]
     for copy in copies:
         copy.start()
     for copy in copies:
@@ -254,7 +240,7 @@
         in_specs=[SCALAR, UNREAD, UNREAD],
         out_specs=[FULL] * 3,
         out_shape=[row, row, like(cot[:2].shape, cot.dtype)],
-        scratch_shapes=[pltpu.SemaphoreType.DMA((3,))],
+        scratch_shapes=[pltpu.SemaphoreType.DMA((2 + 2 * cot.shape[1],))],
         compiler_params=grant(4),
         name="first_messages",
     )(place, in_hbm(low), in_hbm(cot))
@@ -263,7 +249,8 @@
 def load_kernel(low_hbm, cot_hbm, ws_hbm, wt_hbm, low_ref, ws_ref, wt_ref, side_ref, cot_ref, sems):
     frames, cols_low = low_ref.shape[0], low_ref.shape[2]
     copies = [pltpu.make_async_copy(cot_hbm.at[n], cot_ref.at[n], sems.at[n]) for n in range(frames)]
-    pairs = ((low_hbm, low_ref), (ws_hbm, ws_ref), (wt_hbm, wt_ref))
+    pairs = [(low_hbm, low_ref)] + [(wt_hbm.at[k], wt_ref.at[k]) for k in range(3)]
+    pairs += [(ws_hbm.at[i, j], ws_ref.at[i, j]) for i in range(3) for j in range(3)]
     copies += [pltpu.make_async_copy(a, b, sems.at[frames + n]) for n, (a, b) in enumerate(pairs)]
     for copy in copies:
         copy.start()
@@ -282,27 +269,11 @@
         out_specs=[FULL] * 4,
         out_shape=[like(low.shape, low.dtype), like(ws.shape, ws.dtype), like(wt.shape, wt.dtype),
                    like((frames, 4, rows_low * cols_low, chan), jnp.bfloat16)],
-        scratch_shapes=[pltpu.VMEM(cot.shape, cot.dtype), pltpu.SemaphoreType.DMA((frames + 3,))],
+        scratch_shapes=[pltpu.VMEM(cot.shape, cot.dtype), pltpu.SemaphoreType.DMA((frames + 13,))],
         compiler_params=grant(12),
         cost_estimate=cost(2, 4),
         name="load",
     )(in_hbm(low), in_hbm(cot), in_hbm(ws), in_hbm(wt))
-
-
-def nothing(*_):
-    pass
-
-
-def after(arrays, *before):
-    return pl.pallas_call(
-        nothing,
-        in_specs=[UNREAD] * (len(arrays) + len(before)),
-        out_specs=[UNREAD] * len(arrays),
-        out_shape=[like(a.shape, a.dtype) for a in arrays],
-        input_output_aliases={n: n for n in range(len(arrays))},
-        compiler_params=grant(1),
-        name="after",
-    )(*arrays, *before)
 
 
 def forward(place, low, inner, outer, ws):
@@ -344,19 +315,17 @@
     )(place, low, inner, outer, pg, before)
 
 
-def earlier_act(low, ws):
+def earlier_act(low, ws, before):
     frames, rows_tall, cols_low, chan = low.shape
-    side = (frames, 4, (rows_tall - 2) * cols_low, chan)
     return pl.pallas_call(
         act_kernel,
-        grid=(frames,),
-        in_specs=[each(low.shape), whole(ws.shape)],
-        out_specs=each(side),
-        out_shape=like(side, jnp.bfloat16),
-        compiler_params=grant(16),
+        in_specs=[FULL, FULL, UNREAD],
+        out_specs=FULL,
+        out_shape=like((frames, 4, (rows_tall - 2) * cols_low, chan), jnp.bfloat16),
+        compiler_params=grant(10),
         cost_estimate=cost(4, 3),
         name="earlier_act",
-    )(low, ws)
+    )(low, ws, before)
 
 
 def backward(place, low, inner, outer, act, slope, cot, later, wt):
@@ -386,92 +355,132 @@
     )(place, low, inner, outer, act, pg, ext)
 
 
-def section_kernel(act_ref, low_ref, wt_ref, _, out_ref, token_ref):
+def section_kernel(earlier_ref, act_ref, low_ref, wt_ref, _, out_ref, token_ref, held, sems):
+    frames, rows_low, cols_low, chan = low_ref.shape
+    group = rows_at_once(rows_low, cols_low)
+    span, count = group * cols_low, rows_low * cols_low
+    order = from_side(group, cols_low)
     token_ref[...] = jnp.zeros_like(token_ref)
-    frame = pl.program_id(0)
-    _, rows_low, cols_low, chan = low_ref.shape
-    group = rows_at_once(rows_low, cols_low)
-    span = group * cols_low
-    order = from_side(group, cols_low)
-    low = low_ref[0].reshape(-1, chan).astype(jnp.float32)
-    mixed = []
-    for side in range(4):
-        total = low
+    copies = []
+    for frame in range(frames):
+        total = jnp.concatenate([low_ref[frame].reshape(count, chan).astype(jnp.float32)] * 4, axis=0)
         for k in range(3):
-            total = total + product(act_ref[frame + 2 - k, side], wt_ref[k])
-        mixed.append(total.astype(jnp.bfloat16))
-    for n in range(rows_low // group):
-        block = jnp.concatenate([m[n * span : (n + 1) * span] for m in mixed], axis=0)
-        block = product(order, block).astype(jnp.bfloat16)
-        out_ref[0, 2 * group * n : 2 * group * (n + 1)] = block.reshape(2 * group, 2 * cols_low, chan)
-
-
-def section(act_ext, low, wt, before):
+            act = act_ref[frame - k] if frame >= k else earlier_ref[frame - k + 2]
+            total = total + product(act.reshape(4 * count, chan), wt_ref[k])
+        mixed = total.astype(jnp.bfloat16).reshape(4, count, chan)
+        for n in range(rows_low // group):
+            block = mixed[:, n * span : (n + 1) * span].reshape(4 * span, chan)
+            block = product(order, block).astype(jnp.bfloat16)
+            held[frame, 2 * group * n : 2 * group * (n + 1)] = block.reshape(2 * group, 2 * cols_low, chan)
+        copies.append(pltpu.make_async_copy(held.at[frame], out_ref.at[frame], sems.at[frame]))
+        copies[-1].start()
+    for copy in copies:
+        copy.wait()
+
+
+HBM = pl.BlockSpec(memory_space=pltpu.HBM)
+
+
+def section(earlier, act, low, wt, before):
     frames, rows_low, cols_low, chan = low.shape
     out = (frames, 2 * rows_low, 2 * cols_low, chan)
     return pl.pallas_call(
         section_kernel,
-        grid=(frames,),
-        in_specs=[whole(act_ext.shape), each(low.shape), whole(wt.shape), UNREAD],
-        out_specs=[each(out), whole(TOKEN.shape)],
+        in_specs=[FULL] * 4 + [UNREAD],
+        out_specs=[HBM, FULL],
         out_shape=[like(out, jnp.bfloat16), TOKEN],
-        compiler_params=grant(16),
-        cost_estimate=pl.CostEstimate(flops=2 * 2048 * chan * chan * 4, bytes_accessed=3 * 2**20, transcendentals=0),
+        scratch_shapes=[pltpu.VMEM(out, jnp.bfloat16), pltpu.SemaphoreType.DMA((frames,))],
+        compiler_params=grant(10),
+        cost_estimate=cost(4, 3),
         name="section",
-    )(act_ext, low, wt, before)
-
-
-def input_kernel(place_ref, pg_ref, inner_ref, outer_ref, cot_ref, ws_ref, _, out_ref, token_ref):
+    )(earlier, act, low, wt, before)
+
+
+def split(value):
+    high = value.astype(jnp.bfloat16)
+    return high, (value - high.astype(jnp.float32)).astype(jnp.bfloat16)
+
+
+def column_pair(first, second, j, at, last):
+    if j == 0:
+        return second + from_right(first, at, last)
+    if j == 1:
+        return first + second
+    return first + from_left(second, at)
+
+
+def input_kernel(pg_ref, ext_ref, ws_ref, _, out_ref):
+    frames, _, count, chan = pg_ref.shape
+    cols_low = out_ref.shape[2]
+    rows_low = count // cols_low
+    at = column(count, cols_low, chan)
+    for frame in range(frames):
+        total = sum(ext_ref[frame, side].astype(jnp.float32) for side in range(4))
+        own = [pg_ref[frame, side].astype(jnp.float32) for side in range(4)]
+        zero = jnp.zeros((1, cols_low, chan), jnp.float32)
+        for j in range(3):
+            even = column_pair(own[0], own[1], j, at, cols_low - 1).reshape(rows_low, cols_low, chan)
+            odd = column_pair(own[2], own[3], j, at, cols_low - 1).reshape(rows_low, cols_low, chan)
+            below = jnp.concatenate([even[1:], zero], axis=0)
+            above = jnp.concatenate([zero, odd[:-1]], axis=0)
+            for i, value in enumerate((odd + below, even + odd, above + even)):
+                for part in split(value.reshape(count, chan)):
+                    total = total + product_nt(part, ws_ref[i, j])
+        out_ref[frame] = total.reshape(rows_low, cols_low, chan)
+
+
+def input_own(pg, ext, ws, before, low_shape):
+    return pl.pallas_call(
+        input_kernel,
+        in_specs=[FULL] * 3 + [UNREAD],
+        out_specs=FULL,
+        out_shape=like(low_shape, jnp.float32),
+        compiler_params=grant(10),
+        cost_estimate=cost(6, 4),
+        name="input_own",
+    )(pg, ext, ws, before)
+
+
+def input_edge_kernel(place_ref, own_ref, inner_ref, outer_ref, ws_ref, out_ref, token_ref, held, sem):
+    frames, rows_low, cols_low, chan = own_ref.shape
     token_ref[...] = jnp.zeros_like(token_ref)
-    _, rows_low, cols_low, chan = out_ref.shape
-    group = rows_at_once(rows_low, cols_low)
-    span = group * cols_low
-    boxes = box(group, cols_low)
-    count = rows_low * cols_low
-    total = jnp.concatenate(
-        [product(boxes, cot_ref[0, 2 * group * n : 2 * group * (n + 1)].reshape(4 * span, chan))
-         for n in range(rows_low // group)], axis=0)
-    higher = (rows_low + 1, cols_low, chan)
-    at = column(higher[0] * cols_low, cols_low, chan)
-    own = [pg_ref[0, side].astype(jnp.float32) for side in range(4)]
     odd_place = place_ref[1] == 1
-    inner = [inner_ref[0, b].astype(jnp.float32) for b in range(2)]
-    outer = [outer_ref[0, b].astype(jnp.float32) for b in range(2)]
+    flat = (frames * cols_low, chan)
+    at = column(flat[0], cols_low, chan)
+    inner = [inner_ref[:, b].reshape(flat).astype(jnp.float32) for b in range(2)]
+    outer = [outer_ref[:, b].reshape(flat).astype(jnp.float32) for b in range(2)]
     above = [jnp.where(odd_place, inner[b], outer[b]) for b in range(2)]
     below = [jnp.where(odd_place, outer[b], inner[b]) for b in range(2)]
-    even = [jnp.concatenate([own[b], below[b]], axis=0) for b in range(2)]
-    odd = [jnp.concatenate([above[b], own[2 + b]], axis=0) for b in range(2)]
-    for j in range(3):
-        pair = []
-        for first, second in (even, odd):
-            if j == 0:
-                value = second + from_right(first, at, cols_low - 1)
-            elif j == 1:
-                value = first + second
-            else:
-                value = first + from_left(second, at)
-            pair.append(value.reshape(higher))
-        top, low = pair
-        for i, value in enumerate((low[1:] + top[1:], top[:-1] + low[1:], low[:-1] + top[:-1])):
-            value = value.reshape(count, chan)
-            high = value.astype(jnp.bfloat16)
-            rest = (value - high.astype(jnp.float32)).astype(jnp.bfloat16)
-            total = total + product_nt(high, ws_ref[i, j]) + product_nt(rest, ws_ref[i, j])
-    out_ref[0] = total.astype(jnp.bfloat16).reshape(rows_low, cols_low, chan)
-
-
-def input_grads(place, pg, inner, outer, cot, ws, before, low_shape):
-    chan = low_shape[-1]
-    return pl.pallas_call(
-        input_kernel,
-        grid=(low_shape[0],),
-        in_specs=[SCALAR, each(pg.shape), each(inner.shape), each(outer.shape), each(cot.shape), whole(ws.shape), UNREAD],
-        out_specs=[each(low_shape), whole(TOKEN.shape)],
-        out_shape=[like(low_shape, jnp.bfloat16), TOKEN],
-        compiler_params=grant(20),
-        cost_estimate=pl.CostEstimate(flops=2 * 2048 * chan * chan * 6, bytes_accessed=4 * 2**20, transcendentals=0),
-        name="input_grads",
-    )(place, pg, inner, outer, cot, ws, before)
+    terms = []
+    for (first, second), i in ((above, 2), (below, 0)):
+        total = jnp.zeros(flat, jnp.float32)
+        for j in range(3):
+            for part in split(column_pair(first, second, j, at, cols_low - 1)):
+                total = total + product_nt(part, ws_ref[i, j])
+        terms.append(total.reshape(frames, cols_low, chan))
+    for row in range(rows_low):
+        value = own_ref[:, row]
+        if row == 0:
+            value = value + terms[0]
+        if row == rows_low - 1:
+            value = value + terms[1]
+        held[:, row] = value.astype(jnp.bfloat16)
+    copy = pltpu.make_async_copy(held, out_ref, sem)
+    copy.start()
+    copy.wait()
+
+
+def input_grads(place, own, inner, outer, ws):
+    return pl.pallas_call(
+        input_edge_kernel,
+        in_specs=[SCALAR] + [FULL] * 4,
+        out_specs=[HBM, FULL],
+        out_shape=[like(own.shape, jnp.bfloat16), TOKEN],
+        scratch_shapes=[pltpu.VMEM(own.shape, jnp.bfloat16), pltpu.SemaphoreType.DMA],
+        compiler_params=grant(6),
+        cost_estimate=cost(1, 1),
+        name="input_edge",
+    )(place, own, inner, outer, ws)
 
 
 def put_kernel(place_ref, half_ref, *refs):
@@ -493,11 +502,10 @@
 
 def put(place, half, *done):
     chan = half.shape[-1]
-    hbm = pl.BlockSpec(memory_space=pltpu.HBM)
     return pl.pallas_call(
         put_kernel,
-        in_specs=[SCALAR, FULL] + [hbm] * len(done),
-        out_specs=[hbm, hbm],
+        in_specs=[SCALAR, FULL] + [HBM] * len(done),
+        out_specs=[HBM, HBM],
         out_shape=[like((3, 3, chan, chan), jnp.float32), like((3, chan, chan), jnp.float32)],
         input_output_aliases={2 + n: n for n in range(len(done))},
         scratch_shapes=[pltpu.VMEM((12, chan // 2, chan), jnp.float32), pltpu.SemaphoreType.DMA((12,))],
@@ -576,13 +584,15 @@
     kept = add_halves(own, theirs)
     got = bits.exchange(kept.reshape(parts, -1, chan))
     edge, pg_inner, pg_outer = edges(mine, low, inner, outer, pg, kept)
-    earlier = earlier_act(bits.shift(edge, "tm", 1), ws)
+    edge = bits.shift(edge, "tm", 1)
     pg_inner, pg_outer = bits.pairs(pg_inner, pg_outer)
-    total, far = bits.far_sums(sum_parts(got, earlier))
-    section_out, section_done = section(jnp.concatenate([earlier, act], axis=0), low, wt, total)
-    totals = spread(total, far, parts, section_done, pg_inner, pg_outer)
-    input_grad, input_done = input_grads(mine, pg, pg_inner, pg_outer, cot, ws, totals, low.shape)
-    half, = after([bits.exchange(totals).reshape(kept.shape)], input_done)
+    own_part = input_own(pg, ext, ws, kept, low.shape)
+    total, far = bits.far_sums(sum_parts(got, own_part))
+    earlier = earlier_act(edge, ws, total)
+    section_out, section_done = section(earlier, act, low, wt, total)
+    input_grad, input_done = input_grads(mine, own_part, pg_inner, pg_outer, ws)
+    totals = spread(total, far, parts, section_done, input_done)
+    half = bits.exchange(totals).reshape(kept.shape)
     theirs = bits.swap(half, bits.core)
     spatial_grad, temporal_grad = put(other, theirs, *put(mine, half))
     return section_out[None], input_grad[None], spatial_grad, temporal_grad

time: 70.4 us -> 71.1 us (level)
  blocking collectives: 0 us -> 15 us
  waiting for transfers between devices: 15 us -> 5.57 us
  starting transfers between devices: 23.8 us -> 20.8 us
  local copies, waits for them, and re-layouts: 2.3 us -> 0.04 us
    all_to_all x0 -> x1, blocking collectives: none -> 15 us  [exchange(): return lax.all_to_all(parts, tuple(self.near), 0, 0, tiled=True)]
    all_to_all x2 -> x1, waiting for transfers between devices: 13.2 us -> 0.01 us  [exchange(): return lax.all_to_all(parts, tuple(self.near), 0, 0, tiled=True)]
    ppermute x5, waiting for transfers between devices: 1.76 us -> 5.56 us  [swap(): return lax.ppermute(block, axis, [(0, 1), (1, 0)])]
    all_to_all x2 -> x1, starting transfers between devices: 10.2 us -> 6.64 us  [exchange(): return lax.all_to_all(parts, tuple(self.near), 0, 0, tiled=True)]
    unnamed x20 -> x16, local copies, waits for them, and re-layouts: 2.3 us -> 0.04 us
    pallas_call x6, Pallas kernels: 12.8 us -> 13.8 us  [the longest x2 3.56 us: put(): pl.pallas_call(put_kernel, in_specs=[SCALAR, FULL] + [HBM] * len(done), o...]
    pallas_call x1, Pallas kernels: 0.94 us -> 0.06 us  [spread(): pl.pallas_call(spread_kernel, in_specs=[FULL, FULL] + [UNREAD] * len(befo...]
  transfers between devices with their start and end apart: 11 -> 10, of which waited for: 5 -> 3; matrix products, arithmetic and copies ran while one was open for 0% -> 0% of each run, Pallas kernels for 27% -> 28%
where the time goes in v9:
time: 71.1 us; the launch traced here: 70.7 us
  Pallas kernels  28.1 us (40%)
  starting transfers between devices  20.8 us (29%)
  blocking collectives  15 us (21%)
  waiting for transfers between devices  5.57 us (8%)
  between operations  1.07 us (2%)
    all_to_all x1, blocking collectives, exchange(): return lax.all_to_all(parts, tuple(self.near), 0, 0, tiled=True)  15 us
    ppermute x5, starting transfers between devices, swap(): return lax.ppermute(block, axis, [(0, 1), (1, 0)])  8.92 us
    all_to_all x1, starting transfers between devices, exchange(): return lax.all_to_all(parts, tuple(self.near), 0, 0, tiled=True)  6.64 us
    ppermute x5, waiting for transfers between devices, swap(): return lax.ppermute(block, axis, [(0, 1), (1, 0)])  5.56 us
    ppermute x2, starting transfers between devices, shift(): return lax.ppermute(block, axes, route)  3.73 us
    pallas_call x2, Pallas kernels, put(): pl.pallas_call(put_kernel, in_specs=[SCALAR, FULL] + [HBM] * len(done), o...  3.56 us
    pallas_call x1, Pallas kernels, section(): pl.pallas_call(section_kernel, in_specs=[FULL] * 4 + [UNREAD], out_specs=...  3.47 us
    pallas_call x1, Pallas kernels, backward(): pl.pallas_call(backward_kernel, in_specs=[SCALAR] + [FULL] * 8, out_specs...  3.35 us
  transfers between devices with their start and end apart: 10, of which 3 were waited for; matrix products, arithmetic and copies ran while one was open for 0% of the time, Pallas kernels for 28%

profile of v9, /device:TPU:0, one launch (start us, length us, event | category | flops | bytes accessed | tf_op | source)
XLA Modules:
  0.0 70.7 jit_solution(3502033386931649529)
XLA Ops:
  0.6 0.1 pad_add_fusion.place_ref
  0.7 1.7 %first_messages.1 = (bf16[4,1,32,256]{3,2,1,0:T(8,128)(2,1)S(1)}, bf16[4,1,32,256]{3,2,1,0:T(8,128)(2,1)S(1)}, bf16[2,8,64,256]{3,2,1,0:T(8,128)(2,1)S(1)}) custom-call(s32[2]{0:T(128)S(1)} %pad_add_fusion.place_ref, bf16[4,4,32,256]{3,2,1,0:T(8,128)(2,1)} %bitcast.13, bf16[4,8,64,256]{3,2,1,0:T(8,128)(2,1)} %bitcast.11), custom_call_target="tpu_custom_call" | custom-call | tf_op jit(solution)/shard_map/first_messages/pallas_call | solution.py:238
  2.5 1.3 %collective-permute-start.2 = (bf16[2,8,64,256]{3,2,1,0:T(8,128)(2,1)S(1)}, bf16[2,8,64,256]{3,2,1,0:T(8,128)(2,1)S(1)}, u32[]{:S(2)}, u32[]{:S(2)}) collective-permute-start(bf16[2,8,64,256]{3,2,1,0:T(8,128)(2,1)S(1)} %get-tuple-element.34), channel_id=1, source_target_pairs={{4,0},{8,4},{12,8},{5,1},{9,5},{13,9},{6,2},{10,6},{14,10},{7,3},{... | collective-permute-start | bytes 1572872 | tf_op jit(solution)/shard_map/ppermute | solution.py:39
  3.8 3.1 %collective-permute-start = (bf16[4,1,32,256]{3,2,1,0:T(8,128)(2,1)S(1)}, bf16[4,1,32,256]{3,2,1,0:T(8,128)(2,1)S(1)}, u32[]{:S(2)}, u32[]{:S(2)}) collective-permute-start(bf16[4,1,32,256]{3,2,1,0:T(8,128)(2,1)S(1)} %get-tuple-element.28), channel_id=1, source_target_pairs={{0,1},{1,0},{2,3},{3,2},{4,5},{5,4},{6,7},{7,6},{8,9},{9,8},{10,11... | collective-permute-start | bytes 196616 | tf_op jit(solution)/shard_map/ppermute | solution.py:33
  6.8 0.7 collective-permute-start.1
  7.5 0.1 pad_add_fusion.1.place_ref
  7.6 2.1 %load.1 = (bf16[4,4,32,256]{3,2,1,0:T(8,128)(2,1)S(1)}, bf16[3,3,256,256]{3,2,1,0:T(8,128)(2,1)S(1)}, bf16[3,256,256]{2,1,0:T(8,128)(2,1)S(1)}, bf16[4,4,128,256]{3,2,1,0:T(8,128)(2,1)S(1)}) custom-call(bf16[4,4,32,256]{3,2,1,0:T(8,128)(2,1)} %bitcast.14, bf16[4,8,64,256]{3,2,1,0:T(8,128)(2,1)} %bitcast.12, bf16[3,3,256,256]{3,2,1,0:T(8,128)(2,1)} %ws_hbm.1, ...), custom_call_target="tpu_custom_call" | custom-call | flops 536870912 | bytes 4194304 | tf_op jit(solution)/shard_map/load/pallas_call | solution.py:266
  9.7 0.0 collective-permute-done.inner_ref
  9.7 0.0 collective-permute-done.1.outer_ref
  9.7 2.3 %forward.1 = (bf16[4,4,128,256]{3,2,1,0:T(8,128)(2,1)S(1)}, f32[4,4,128,256]{3,2,1,0:T(8,128)S(1)}) custom-call(s32[2]{0:T(128)S(1)} %pad_add_fusion.place_ref, bf16[4,4,32,256]{3,2,1,0:T(8,128)(2,1)S(1)} %get-tuple-element.27.low_ref, bf16[4,1,32,256]{3,2,1,0:T(8,128)(2,1)S(1)} %collective-permute-done.inner_ref, ...), custom_call_target="tpu_custom_call" | custom-call | flops 2684354560 | bytes 8388608 | tf_op jit(solution)/shard_map/forward/pallas_call | solution.py:282
  12.0 0.0 copy-start.6
  12.0 0.0 collective-permute-done.2.later_ref
  12.1 3.3 %backward.1 = (bf16[4,4,128,256]{3,2,1,0:T(8,128)(2,1)S(1)}, bf16[6,4,128,256]{3,2,1,0:T(8,128)(2,1)S(1)}, f32[12,128,256]{2,1,0:T(8,128)S(1)}) custom-call(s32[2]{0:T(128)S(1)} %pad_add_fusion.1.place_ref, bf16[4,4,32,256]{3,2,1,0:T(8,128)(2,1)S(1)} %get-tuple-element.27.low_ref, bf16[4,1,32,256]{3,2,1,0:T(8,128)(2,1)S(1)} %collective-permute-done.inner_ref, ...), custom_call_target="tpu_custom_call" | custom-call | flops 4026531840 | bytes 10485760 | tf_op jit(solution)/shard_map/backward/pallas_call | solution.py:334
  15.4 0.0 copy-start.4
  15.4 2.3 %collective-permute-start.3 = (f32[12,128,256]{2,1,0:T(8,128)S(1)}, f32[12,128,256]{2,1,0:T(8,128)S(1)}, u32[]{:S(2)}, u32[]{:S(2)}) collective-permute-start(f32[12,128,256]{2,1,0:T(8,128)S(1)} %get-tuple-element.38), channel_id=1, source_target_pairs={{0,4},{4,0},{1,5},{5,1},{2,6},{6,2},{3,7},{7,3},{8,12},{12,8},{9,1... | collective-permute-start | bytes 4718600 | tf_op jit(solution)/shard_map/ppermute | solution.py:33
  17.7 2.4 %half_grads.1.mine_ref = f32[12,128,256]{2,1,0:T(8,128)S(1)} custom-call(s32[2]{0:T(128)S(1)} %pad_add_fusion.place_ref, bf16[4,4,32,256]{3,2,1,0:T(8,128)(2,1)S(1)} %get-tuple-element.27.low_ref, bf16[4,1,32,256]{3,2,1,0:T(8,128)(2,1)S(1)} %collective-permute-done.inner_ref, bf16[4,1,32,256]{3,2,1,0:T(8,128)(2,1)S(1)} %collective-permute-done.1.outer_ref, ...), custom_call_target="tpu_custom_call" | custom-call | flops 2684354560 | bytes 6291456 | tf_op jit(solution)/shard_map/half_grads/pallas_call | solution.py:347
  20.1 0.0 copy-done.4
  20.1 0.7 collective-permute-done.3.theirs_ref
  20.7 1.0 %add_halves.1._ = bf16[12,128,256]{2,1,0:T(8,128)(2,1)} custom-call(f32[12,128,256]{2,1,0:T(8,128)S(1)} %half_grads.1.mine_ref, f32[12,128,256]{2,1,0:T(8,128)S(1)} %collective-permute-done.3.theirs_ref), custom_call_target="tpu_custom_call" | custom-call | tf_op jit(solution)/shard_map/add_halves/pallas_call | solution.py:523
  21.7 6.6 %all-to-all-start = ((bf16[8,192,256]{2,1,0:T(8,128)(2,1)}), bf16[8,192,256]{2,1,0:T(8,128)(2,1)S(1)}, u32[]{:S(2)}, u32[]{:S(2)}) async-start(bf16[8,192,256]{2,1,0:T(8,128)(2,1)} %bitcast.5), calls=%async_computation | async-start | bytes 1572864 | tf_op jit(solution)/shard_map/all_to_all | solution.py:42
  28.4 0.0 copy-done
  28.4 0.0 copy-start.5
  28.4 1.3 %edges.1 = (bf16[2,6,32,256]{3,2,1,0:T(8,128)(2,1)}, bf16[4,2,32,256]{3,2,1,0:T(8,128)(2,1)S(1)}, bf16[4,2,32,256]{3,2,1,0:T(8,128)(2,1)S(1)}) custom-call(s32[2]{0:T(128)S(1)} %pad_add_fusion.place_ref, bf16[4,4,32,256]{3,2,1,0:T(8,128)(2,1)S(1)} %get-tuple-element.27.low_ref, bf16[4,1,32,256]{3,2,1,0:T(8,128)(2,1)S(1)} %collective-permute-done.inner_ref, ...), custom_call_target="tpu_custom_call" | custom-call | tf_op jit(solution)/shard_map/edges/pallas_call | solution.py:308
  29.7 2.4 %collective-permute-start.4 = (bf16[2,6,32,256]{3,2,1,0:T(8,128)(2,1)}, bf16[2,6,32,256]{3,2,1,0:T(8,128)(2,1)}, u32[]{:S(2)}, u32[]{:S(2)}) collective-permute-start(bf16[2,6,32,256]{3,2,1,0:T(8,128)(2,1)} %get-tuple-element.39), channel_id=1, source_target_pairs={{0,4},{4,8},{8,12},{1,5},{5,9},{9,13},{2,6},{6,10},{10,14},{3,7},{... | collective-permute-start | bytes 589832 | tf_op jit(solution)/shard_map/ppermute | solution.py:39
  32.1 1.7 %collective-permute-start.5 = (bf16[4,2,32,256]{3,2,1,0:T(8,128)(2,1)S(1)}, bf16[4,2,32,256]{3,2,1,0:T(8,128)(2,1)S(1)}, u32[]{:S(2)}, u32[]{:S(2)}) collective-permute-start(bf16[4,2,32,256]{3,2,1,0:T(8,128)(2,1)S(1)} %get-tuple-element.41), channel_id=1, source_target_pairs={{0,1},{1,0},{2,3},{3,2},{4,5},{5,4},{6,7},{7,6},{8,9},{9,8},{10,11... | collective-permute-start | bytes 393224 | tf_op jit(solution)/shard_map/ppermute | solution.py:33
  33.8 0.8 %collective-permute-start.6 = (bf16[4,2,32,256]{3,2,1,0:T(8,128)(2,1)S(1)}, bf16[4,2,32,256]{3,2,1,0:T(8,128)(2,1)S(1)}, u32[]{:S(2)}, u32[]{:S(2)}) collective-permute-start(bf16[4,2,32,256]{3,2,1,0:T(8,128)(2,1)S(1)} %get-tuple-element.42), channel_id=1, source_target_pairs={{1,2},{2,1},{5,6},{6,5},{9,10},{10,9},{13,14},{14,13},{17,18},{18,... | collective-permute-start | bytes 393224 | tf_op jit(solution)/shard_map/ppermute | solution.py:48
  34.7 0.0 copy-done.5
  34.7 3.2 %input_own.1._.own_ref = f32[4,4,32,256]{3,2,1,0:T(8,128)S(1)} custom-call(bf16[4,4,128,256]{3,2,1,0:T(8,128)(2,1)S(1)} %get-tuple-element.36.pg_ref, bf16[6,4,128,256]{3,2,1,0:T(8,128)(2,1)S(1)} %copy-done.5, bf16[3,3,256,256]{3,2,1,0:T(8,128)(2,1)S(1)} %get-tuple-element.30.ws_ref, bf16[12,128,256]{2,1,0:T(8,128)(2,1)} %add_halves.1._), custom_call_target="tpu_custom_call" | custom-call | flops 1610612736 | bytes 4194304 | tf_op jit(solution)/shard_map/input_own/pallas_call | solution.py:433
  37.9 4.4 %collective-permute-done.5.inner_ref = bf16[4,2,32,256]{3,2,1,0:T(8,128)(2,1)S(1)} collective-permute-done((bf16[4,2,32,256]{3,2,1,0:T(8,128)(2,1)S(1)}, bf16[4,2,32,256]{3,2,1,0:T(8,128)(2,1)S(1)}, u32[]{:S(2)}, u32[]{:S(2)}) %collective-permute-start.5) | collective-permute-done | bytes 131104 | tf_op jit(solution)/shard_map/ppermute | solution.py:33
  42.3 0.0 collective-permute-done.6.outer_ref
  42.3 1.9 %input_edge.1 = (bf16[4,4,32,256]{3,2,1,0:T(8,128)(2,1)}, f32[8,128]{1,0:T(8,128)S(1)}) custom-call(s32[2]{0:T(128)S(1)} %pad_add_fusion.place_ref, f32[4,4,32,256]{3,2,1,0:T(8,128)S(1)} %input_own.1._.own_ref, bf16[4,2,32,256]{3,2,1,0:T(8,128)(2,1)S(1)} %collective-permute-done.5.inner_ref, bf16[4,2,32,256]{3,2,1,0:T(8,128)(2,1)S(1)} %collective-permute-done.6.outer_ref, ...), custom_call_target="tpu_custom_call" | custom-call | flops 268435456 | bytes 1048576 | tf_op jit(solution)/shard_map/input_edge/pallas_call | solution.py:474
  44.2 0.0 all-to-all-done.got_ref
  44.2 0.1 sum_parts.1._.own_ref
  44.4 0.0 copy-start.7
  44.4 1.8 %collective-permute-start.7 = (bf16[192,256]{1,0:T(8,128)(2,1)S(1)}, bf16[192,256]{1,0:T(8,128)(2,1)S(1)}, u32[]{:S(2)}, u32[]{:S(2)}) collective-permute-start(bf16[192,256]{1,0:T(8,128)(2,1)S(1)} %sum_parts.1._.own_ref), channel_id=1, source_target_pairs={{0,2},{2,0},{1,3},{3,1},{4,6},{6,4},{5,7},{7,5},{8,10},{10,8},{9,1... | collective-permute-start | bytes 294920 | tf_op jit(solution)/shard_map/ppermute | solution.py:33
  46.2 0.0 collective-permute-done.4.low_ref
  46.2 1.7 %earlier_act.1.earlier_ref = bf16[2,4,128,256]{3,2,1,0:T(8,128)(2,1)S(1)} custom-call(bf16[2,6,32,256]{3,2,1,0:T(8,128)(2,1)} %collective-permute-done.4.low_ref, bf16[3,3,256,256]{3,2,1,0:T(8,128)(2,1)S(1)} %get-tuple-element.30.ws_ref, bf16[192,256]{1,0:T(8,128)(2,1)S(1)} %sum_parts.1._.own_ref), custom_call_target="tpu_custom_call" | custom-call | flops 1073741824 | bytes 3145728 | tf_op jit(solution)/shard_map/earlier_act/pallas_call | solution.py:320
  47.9 0.0 copy-done.1
  47.9 0.0 copy-done.3
  47.9 0.0 copy-done.7
  47.9 3.5 %section.1 = (bf16[4,8,64,256]{3,2,1,0:T(8,128)(2,1)}, f32[8,128]{1,0:T(8,128)S(1)}) custom-call(bf16[2,4,128,256]{3,2,1,0:T(8,128)(2,1)S(1)} %earlier_act.1.earlier_ref, bf16[4,4,128,256]{3,2,1,0:T(8,128)(2,1)S(1)} %copy-done.7, bf16[4,4,32,256]{3,2,1,0:T(8,128)(2,1)S(1)} %copy-done.1, bf16[3,256,256]{2,1,0:T(8,128)(2,1)S(1)} %copy-done.3, ...), custom_call_target="tpu_custom_call" | custom-call | flops 1073741824 | bytes 3145728 | tf_op jit(solution)/shard_map/section/pallas_call | solution.py:387
  51.4 0.0 collective-permute-done.7.theirs_ref
  51.4 0.1 spread.1
  51.5 15.0 %all_to_all.10 = bf16[8,192,256]{2,1,0:T(8,128)(2,1)S(1)} all-to-all(bf16[8,192,256]{2,1,0:T(8,128)(2,1)S(1)} %spread.1), channel_id=1, replica_groups=mesh['dp0'=2,'tm1'=2,'tm0'=2,'height1'=2,'height0'=2] {'dp0','tm1','heig..., dimensions={0} | all-to-all | bytes 1572864 | tf_op jit(solution)/shard_map/all_to_all | solution.py:42
  66.5 0.0 collective-permute-start.8
  66.5 1.8 %put.2 = (f32[3,3,256,256]{3,2,1,0:T(8,128)}, f32[3,256,256]{2,1,0:T(8,128)}) custom-call(s32[2]{0:T(128)S(1)} %pad_add_fusion.place_ref, bf16[12,128,256]{2,1,0:T(8,128)(2,1)S(1)} %bitcast.10), custom_call_target="tpu_custom_call" | custom-call | tf_op jit(solution)/shard_map/put/pallas_call | solution.py:505
  68.3 0.5 collective-permute-done.8.half_ref
  68.8 1.8 %put.3 = (f32[3,3,256,256]{3,2,1,0:T(8,128)}, f32[3,256,256]{2,1,0:T(8,128)}) custom-call(s32[2]{0:T(128)S(1)} %pad_add_fusion.1.place_ref, bf16[12,128,256]{2,1,0:T(8,128)(2,1)S(1)} %collective-permute-done.8.half_ref, f32[3,3,256,256]{3,2,1,0:T(8,128)} %get-tuple-element.46.refs_0_, ...), custom_call_target="tpu_custom_call", output_to_operand_aliasing={{0}: (2, {}), {1}: (3, {})} | custom-call | tf_op jit(solution)/shard_map/put/pallas_call | solution.py:505
  (6 shorter events, 0.0 us)
Async XLA Ops:
  2.5 9.6 %collective-permute-start.2 = (bf16[2,8,64,256]{3,2,1,0:T(8,128)(2,1)S(1)}, bf16[2,8,64,256]{3,2,1,0:T(8,128)(2,1)S(1)}, u32[]{:S(2)}, u32[]{:S(2)}) collective-permute-start(bf16[2,8,64,256]{3,2,1,0:T(8,128)(2,1)S(1)} %get-tuple-element.34), channel_id=1, source_target_pairs={{4,0},{8,4},{12,8},{5,1},{9,5},{13,9},{6,2},{10,6},{14,10},{7,3},{... | collective-permute-start | bytes 1572872 | tf_op jit(solution)/shard_map/ppermute | solution.py:39
  3.8 5.9 %collective-permute-start = (bf16[4,1,32,256]{3,2,1,0:T(8,128)(2,1)S(1)}, bf16[4,1,32,256]{3,2,1,0:T(8,128)(2,1)S(1)}, u32[]{:S(2)}, u32[]{:S(2)}) collective-permute-start(bf16[4,1,32,256]{3,2,1,0:T(8,128)(2,1)S(1)} %get-tuple-element.28), channel_id=1, source_target_pairs={{0,1},{1,0},{2,3},{3,2},{4,5},{5,4},{6,7},{7,6},{8,9},{9,8},{10,11... | collective-permute-start | bytes 196616 | tf_op jit(solution)/shard_map/ppermute | solution.py:33
  6.8 2.8 %collective-permute-start.1 = (bf16[4,1,32,256]{3,2,1,0:T(8,128)(2,1)S(1)}, bf16[4,1,32,256]{3,2,1,0:T(8,128)(2,1)S(1)}, u32[]{:S(2)}, u32[]{:S(2)}) collective-permute-start(bf16[4,1,32,256]{3,2,1,0:T(8,128)(2,1)S(1)} %get-tuple-element.29), channel_id=1, source_target_pairs={{1,2},{2,1},{5,6},{6,5},{9,10},{10,9},{13,14},{14,13},{17,18},{18,... | collective-permute-start | bytes 196616 | tf_op jit(solution)/shard_map/ppermute | solution.py:48
  9.7 2.4 %copy-start.2 = (bf16[3,256,256]{2,1,0:T(8,128)(2,1)}, bf16[3,256,256]{2,1,0:T(8,128)(2,1)S(1)}, u32[]{:S(2)}) copy-start(bf16[3,256,256]{2,1,0:T(8,128)(2,1)S(1)} %get-tuple-element.35.wt_ref) | copy-start | bytes 1179652
  9.7 18.7 %copy-start = (bf16[4,4,32,256]{3,2,1,0:T(8,128)(2,1)}, bf16[4,4,32,256]{3,2,1,0:T(8,128)(2,1)S(1)}, u32[]{:S(2)}) copy-start(bf16[4,4,32,256]{3,2,1,0:T(8,128)(2,1)S(1)} %get-tuple-element.27.low_ref) | copy-start | bytes 786436
  12.0 5.7 %copy-start.6 = (bf16[4,4,128,256]{3,2,1,0:T(8,128)(2,1)}, bf16[4,4,128,256]{3,2,1,0:T(8,128)(2,1)S(1)}, u32[]{:S(2)}) copy-start(bf16[4,4,128,256]{3,2,1,0:T(8,128)(2,1)S(1)} %get-tuple-element.31.act_ref) | copy-start | bytes 3145732
  15.4 4.7 %copy-start.4 = (bf16[6,4,128,256]{3,2,1,0:T(8,128)(2,1)}, bf16[6,4,128,256]{3,2,1,0:T(8,128)(2,1)S(1)}, u32[]{:S(2)}) copy-start(bf16[6,4,128,256]{3,2,1,0:T(8,128)(2,1)S(1)} %get-tuple-element.37.ext_ref) | copy-start | bytes 4718596
  15.4 5.3 %collective-permute-start.3 = (f32[12,128,256]{2,1,0:T(8,128)S(1)}, f32[12,128,256]{2,1,0:T(8,128)S(1)}, u32[]{:S(2)}, u32[]{:S(2)}) collective-permute-start(f32[12,128,256]{2,1,0:T(8,128)S(1)} %get-tuple-element.38), channel_id=1, source_target_pairs={{0,4},{4,0},{1,5},{5,1},{2,6},{6,2},{3,7},{7,3},{8,12},{12,8},{9,1... | collective-permute-start | bytes 4718600 | tf_op jit(solution)/shard_map/ppermute | solution.py:33
  21.7 22.5 %all-to-all-start = ((bf16[8,192,256]{2,1,0:T(8,128)(2,1)}), bf16[8,192,256]{2,1,0:T(8,128)(2,1)S(1)}, u32[]{:S(2)}, u32[]{:S(2)}) async-start(bf16[8,192,256]{2,1,0:T(8,128)(2,1)} %bitcast.5), calls=%async_computation | async-start | bytes 1572864 | tf_op jit(solution)/shard_map/all_to_all | solution.py:42
  28.4 6.3 %copy-start.5 = (bf16[6,4,128,256]{3,2,1,0:T(8,128)(2,1)S(1)}, bf16[6,4,128,256]{3,2,1,0:T(8,128)(2,1)}, u32[]{:S(2)}) copy-start(bf16[6,4,128,256]{3,2,1,0:T(8,128)(2,1)} %copy-done.4) | copy-start | bytes 4718596
  29.7 16.5 %collective-permute-start.4 = (bf16[2,6,32,256]{3,2,1,0:T(8,128)(2,1)}, bf16[2,6,32,256]{3,2,1,0:T(8,128)(2,1)}, u32[]{:S(2)}, u32[]{:S(2)}) collective-permute-start(bf16[2,6,32,256]{3,2,1,0:T(8,128)(2,1)} %get-tuple-element.39), channel_id=1, source_target_pairs={{0,4},{4,8},{8,12},{1,5},{5,9},{9,13},{2,6},{6,10},{10,14},{3,7},{... | collective-permute-start | bytes 589832 | tf_op jit(solution)/shard_map/ppermute | solution.py:39
  32.1 10.2 %collective-permute-start.5 = (bf16[4,2,32,256]{3,2,1,0:T(8,128)(2,1)S(1)}, bf16[4,2,32,256]{3,2,1,0:T(8,128)(2,1)S(1)}, u32[]{:S(2)}, u32[]{:S(2)}) collective-permute-start(bf16[4,2,32,256]{3,2,1,0:T(8,128)(2,1)S(1)} %get-tuple-element.41), channel_id=1, source_target_pairs={{0,1},{1,0},{2,3},{3,2},{4,5},{5,4},{6,7},{7,6},{8,9},{9,8},{10,11... | collective-permute-start | bytes 393224 | tf_op jit(solution)/shard_map/ppermute | solution.py:33
  33.8 8.5 %collective-permute-start.6 = (bf16[4,2,32,256]{3,2,1,0:T(8,128)(2,1)S(1)}, bf16[4,2,32,256]{3,2,1,0:T(8,128)(2,1)S(1)}, u32[]{:S(2)}, u32[]{:S(2)}) collective-permute-start(bf16[4,2,32,256]{3,2,1,0:T(8,128)(2,1)S(1)} %get-tuple-element.42), channel_id=1, source_target_pairs={{1,2},{2,1},{5,6},{6,5},{9,10},{10,9},{13,14},{14,13},{17,18},{18,... | collective-permute-start | bytes 393224 | tf_op jit(solution)/shard_map/ppermute | solution.py:48
  44.3 3.6 %copy-start.1 = (bf16[4,4,32,256]{3,2,1,0:T(8,128)(2,1)S(1)}, bf16[4,4,32,256]{3,2,1,0:T(8,128)(2,1)}, u32[]{:S(2)}) copy-start(bf16[4,4,32,256]{3,2,1,0:T(8,128)(2,1)} %copy-done) | copy-start | bytes 786436
  44.4 3.6 %copy-start.3 = (bf16[3,256,256]{2,1,0:T(8,128)(2,1)S(1)}, bf16[3,256,256]{2,1,0:T(8,128)(2,1)}, u32[]{:S(2)}) copy-start(bf16[3,256,256]{2,1,0:T(8,128)(2,1)} %copy-done.2) | copy-start | bytes 1179652
  44.4 3.6 %copy-start.7 = (bf16[4,4,128,256]{3,2,1,0:T(8,128)(2,1)S(1)}, bf16[4,4,128,256]{3,2,1,0:T(8,128)(2,1)}, u32[]{:S(2)}) copy-start(bf16[4,4,128,256]{3,2,1,0:T(8,128)(2,1)} %copy-done.6) | copy-start | bytes 3145732
  44.4 7.0 %collective-permute-start.7 = (bf16[192,256]{1,0:T(8,128)(2,1)S(1)}, bf16[192,256]{1,0:T(8,128)(2,1)S(1)}, u32[]{:S(2)}, u32[]{:S(2)}) collective-permute-start(bf16[192,256]{1,0:T(8,128)(2,1)S(1)} %sum_parts.1._.own_ref), channel_id=1, source_target_pairs={{0,2},{2,0},{1,3},{3,1},{4,6},{6,4},{5,7},{7,5},{8,10},{10,8},{9,1... | collective-permute-start | bytes 294920 | tf_op jit(solution)/shard_map/ppermute | solution.py:33
  66.5 2.3 %collective-permute-start.8 = (bf16[12,128,256]{2,1,0:T(8,128)(2,1)S(1)}, bf16[12,128,256]{2,1,0:T(8,128)(2,1)S(1)}, u32[]{:S(2)}, u32[]{:S(2)}) collective-permute-start(bf16[12,128,256]{2,1,0:T(8,128)(2,1)S(1)} %bitcast.9), channel_id=1, source_target_pairs={{0,4},{4,0},{1,5},{5,1},{2,6},{6,2},{3,7},{7,3},{8,12},{12,8},{9,1... | collective-permute-start | bytes 2359304 | tf_op jit(solution)/shard_map/ppermute | solution.py:33

commit v10 on v9

--- a/solution.py
+++ b/solution.py
@@ -2,6 +2,7 @@
 
 import jax
 import jax.numpy as jnp
+import numpy as np
 from jax import lax
 from jax.experimental import pallas as pl
 from jax.experimental.pallas import tpu as pltpu
@@ -74,26 +75,15 @@
     return max(n for n in (1, 2, 4, 8) if rows_low % n == 0 and (n == 1 or 4 * n * cols_low <= 256))
 
 
-def by_side(count, cols_low, dtype=jnp.bfloat16):
+def side_order(rows_low, cols_low):
+    count = rows_at_once(rows_low, cols_low)
     size = 4 * count * cols_low
-    to = lax.broadcasted_iota(jnp.int32, (size, size), 0)
-    at = lax.broadcasted_iota(jnp.int32, (size, size), 1)
-    q, rest = to % cols_low, to // cols_low
-    p, side = rest % count, rest // count
-    return (at == (p * 2 + side // 2) * 2 * cols_low + 2 * q + side % 2).astype(jnp.float32).astype(dtype)
-
-
-def from_side(count, cols_low, dtype=jnp.bfloat16):
-    size = 4 * count * cols_low
-    at = lax.broadcasted_iota(jnp.int32, (size, size), 0)
-    to = lax.broadcasted_iota(jnp.int32, (size, size), 1)
-    q, rest = to % cols_low, to // cols_low
-    p, side = rest % count, rest // count
-    return (at == (p * 2 + side // 2) * 2 * cols_low + 2 * q + side % 2).astype(jnp.float32).astype(dtype)
+    at = np.arange(size).reshape(count, 2, cols_low, 2).transpose(1, 3, 0, 2).reshape(-1)
+    return (at[:, None] == np.arange(size)[None, :]).astype(np.float32)
 
 
 def column(rows, cols_low, chan):
-    return lax.broadcasted_iota(jnp.int32, (rows, chan), 0) % cols_low
+    return lax.broadcasted_iota(jnp.int32, (rows // cols_low, cols_low, chan), 1).reshape(rows, chan)
 
 
 def from_left(x, at):
@@ -104,11 +94,10 @@
     return jnp.where(at == last, 0.0, pltpu.roll(x, x.shape[0] - 1, 0))
 
 
-def sort_columns(source, target, cols_low):
+def sort_columns(source, target, cols_low, order):
     rows_low, chan = source.shape[0] // 2, source.shape[2]
     group = rows_at_once(rows_low, cols_low)
     span = group * cols_low
-    order = by_side(group, cols_low)
     for n in range(rows_low // group):
         block = source[2 * group * n : 2 * group * (n + 1)].reshape(4 * span, chan)
         block = product(order, block).astype(jnp.bfloat16).reshape(4, span, chan)
@@ -149,9 +138,8 @@
 
 
 def act_kernel(low_ref, ws_ref, _, act_ref):
-    for frame in range(low_ref.shape[0]):
-        for side, pre in enumerate(spatial(low_ref[frame], ws_ref)):
-            act_ref[frame, side] = (pre * jax.nn.sigmoid(pre)).astype(jnp.bfloat16)
+    for side, pre in enumerate(spatial(low_ref[0], ws_ref)):
+        act_ref[0, side] = (pre * jax.nn.sigmoid(pre)).astype(jnp.bfloat16)
 
 
 def half_sums(place_ref, low_ref, inner_ref, outer_ref, act_ref, pg_ref, ext_ref, out_ref):
@@ -175,22 +163,21 @@
                 lefts[3 * i + j] += [turned[(a + i - 1) // 2, (b + j - 1) // 2] for a, b in SIDES]
         acts.append(act_ref[frame, :, :, lanes].reshape(4 * count, half).T)
     pg = pg_ref[...].reshape(frames * 4 * count, chan)
-    for tap, left in enumerate(lefts):
-        out_ref[tap] = product(jnp.concatenate(left, axis=1), pg)
+    left = jnp.concatenate([jnp.concatenate(left, axis=1) for left in lefts], axis=0)
+    out_ref[:9] = product(left, pg).reshape(9, half, chan)
     act = jnp.concatenate(acts, axis=1)
     for k in range(3):
         out_ref[9 + k] = product(act, ext_ref[k : k + frames].reshape(frames * 4 * count, chan))
 
 
-def backward_kernel(place_ref, low_ref, inner_ref, outer_ref, act_ref, slope_ref, cot_ref, later_ref, wt_ref, pg_ref, ext_ref, out_ref):
+def backward_kernel(place_ref, low_ref, inner_ref, outer_ref, act_ref, slope_ref, cot_ref, later_ref, turned_ref, sort_ref, pg_ref, ext_ref, out_ref):
     frames, _, count, chan = cot_ref.shape
     ext_ref[:frames] = cot_ref[...]
     for n in range(2):
-        sort_columns(later_ref.at[n], ext_ref.at[frames + n], low_ref.shape[2])
+        sort_columns(later_ref.at[n], ext_ref.at[frames + n], low_ref.shape[2], sort_ref[...])
     for frame in range(frames):
-        act_grad = product_nt(ext_ref[frame].reshape(4 * count, chan), wt_ref[0])
-        for k in (1, 2):
-            act_grad = act_grad + product_nt(ext_ref[frame + k].reshape(4 * count, chan), wt_ref[k])
+        cots = [ext_ref[frame + k].reshape(4 * count, chan) for k in range(3)]
+        act_grad = product(jnp.concatenate(cots, axis=1), turned_ref[...])
         slope = slope_ref[frame].reshape(4 * count, chan)
         pg_ref[frame] = (act_grad * slope).astype(jnp.bfloat16).reshape(4, count, chan)
     half_sums(place_ref, low_ref, inner_ref, outer_ref, act_ref, pg_ref, ext_ref, out_ref)
@@ -246,34 +233,45 @@
     )(place, in_hbm(low), in_hbm(cot))
 
 
-def load_kernel(low_hbm, cot_hbm, ws_hbm, wt_hbm, low_ref, ws_ref, wt_ref, side_ref, cot_ref, sems):
-    frames, cols_low = low_ref.shape[0], low_ref.shape[2]
-    copies = [pltpu.make_async_copy(cot_hbm.at[n], cot_ref.at[n], sems.at[n]) for n in range(frames)]
-    pairs = [(low_hbm, low_ref)] + [(wt_hbm.at[k], wt_ref.at[k]) for k in range(3)]
+def load_kernel(low_hbm, cot_hbm, ws_hbm, wt_hbm, sort_hbm,
+                low_ref, ws_ref, wt_ref, sort_ref, merge_ref, turned_ref, side_ref, cot_ref, wide_ref, sems):
+    frames, cols_low, chan = low_ref.shape[0], low_ref.shape[2], low_ref.shape[3]
+    pairs = [(sort_hbm, wide_ref)] + [(cot_hbm.at[n], cot_ref.at[n]) for n in range(frames)]
+    pairs += [(wt_hbm.at[k], wt_ref.at[k]) for k in range(3)] + [(low_hbm, low_ref)]
     pairs += [(ws_hbm.at[i, j], ws_ref.at[i, j]) for i in range(3) for j in range(3)]
-    copies += [pltpu.make_async_copy(a, b, sems.at[frames + n]) for n, (a, b) in enumerate(pairs)]
+    copies = [pltpu.make_async_copy(a, b, sems.at[n]) for n, (a, b) in enumerate(pairs)]
     for copy in copies:
         copy.start()
+    copies[0].wait()
+    sort_ref[...] = wide_ref[...].astype(jnp.bfloat16)
+    merge_ref[...] = wide_ref[...].T.astype(jnp.bfloat16)
     for n in range(frames):
-        copies[n].wait()
-        sort_columns(cot_ref.at[n], side_ref.at[n], cols_low)
-    for copy in copies[frames:]:
+        copies[1 + n].wait()
+        sort_columns(cot_ref.at[n], side_ref.at[n], cols_low, sort_ref[...])
+    for k in range(3):
+        copies[1 + frames + k].wait()
+        turned_ref[k * chan : (k + 1) * chan] = wt_ref[k].T
+    for copy in copies[4 + frames :]:
         copy.wait()
 
 
 def load(low, cot, ws, wt):
     frames, rows_low, cols_low, chan = low.shape
+    sort = jnp.asarray(side_order(rows_low, cols_low))
+    order = like(sort.shape, jnp.bfloat16)
+    shapes = [low, ws, wt, order, order, like((3 * chan, chan), wt.dtype),
+              like((frames, 4, rows_low * cols_low, chan), jnp.bfloat16)]
     return pl.pallas_call(
         load_kernel,
-        in_specs=[UNREAD] * 4,
-        out_specs=[FULL] * 4,
-        out_shape=[like(low.shape, low.dtype), like(ws.shape, ws.dtype), like(wt.shape, wt.dtype),
-                   like((frames, 4, rows_low * cols_low, chan), jnp.bfloat16)],
-        scratch_shapes=[pltpu.VMEM(cot.shape, cot.dtype), pltpu.SemaphoreType.DMA((frames + 13,))],
-        compiler_params=grant(12),
+        in_specs=[UNREAD] * 5,
+        out_specs=[FULL] * 7,
+        out_shape=[like(a.shape, a.dtype) for a in shapes],
+        scratch_shapes=[pltpu.VMEM(cot.shape, cot.dtype), pltpu.VMEM(sort.shape, sort.dtype),
+                        pltpu.SemaphoreType.DMA((frames + 14,))],
+        compiler_params=grant(14),
         cost_estimate=cost(2, 4),
         name="load",
-    )(in_hbm(low), in_hbm(cot), in_hbm(ws), in_hbm(wt))
+    )(*[in_hbm(a) for a in (low, cot, ws, wt, sort)])
 
 
 def forward(place, low, inner, outer, ws):
@@ -317,29 +315,31 @@
 
 def earlier_act(low, ws, before):
     frames, rows_tall, cols_low, chan = low.shape
+    side = (frames, 4, (rows_tall - 2) * cols_low, chan)
     return pl.pallas_call(
         act_kernel,
-        in_specs=[FULL, FULL, UNREAD],
-        out_specs=FULL,
-        out_shape=like((frames, 4, (rows_tall - 2) * cols_low, chan), jnp.bfloat16),
+        grid=(frames,),
+        in_specs=[pl.BlockSpec((1,) + low.shape[1:], lambda f: (f, 0, 0, 0)), FULL, UNREAD],
+        out_specs=pl.BlockSpec((1,) + side[1:], lambda f: (f, 0, 0, 0)),
+        out_shape=like(side, jnp.bfloat16),
         compiler_params=grant(10),
         cost_estimate=cost(4, 3),
         name="earlier_act",
     )(low, ws, before)
 
 
-def backward(place, low, inner, outer, act, slope, cot, later, wt):
+def backward(place, low, inner, outer, act, slope, cot, later, turned, sort):
     frames, _, _, chan = act.shape
     ext = (frames + 2,) + act.shape[1:]
     return pl.pallas_call(
         backward_kernel,
-        in_specs=[SCALAR] + [FULL] * 8,
+        in_specs=[SCALAR] + [FULL] * 9,
         out_specs=[FULL] * 3,
         out_shape=[like(act.shape, jnp.bfloat16), like(ext, jnp.bfloat16), like((12, chan // 2, chan), jnp.float32)],
         compiler_params=grant(24),
         cost_estimate=cost(15, 10),
         name="backward",
-    )(place, low, inner, outer, act, slope, cot, later, wt)
+    )(place, low, inner, outer, act, slope, cot, later, turned, sort)
 
 
 def half_grads(place, low, inner, outer, act, pg, ext):
@@ -355,18 +355,19 @@
     )(place, low, inner, outer, act, pg, ext)
 
 
-def section_kernel(earlier_ref, act_ref, low_ref, wt_ref, _, out_ref, token_ref, held, sems):
+def section_kernel(earlier_ref, act_ref, low_ref, wt_ref, merge_ref, _, out_ref, token_ref, held, sems):
     frames, rows_low, cols_low, chan = low_ref.shape
     group = rows_at_once(rows_low, cols_low)
     span, count = group * cols_low, rows_low * cols_low
-    order = from_side(group, cols_low)
+    order = merge_ref[...]
+    wt = wt_ref[...].reshape(3 * chan, chan)
     token_ref[...] = jnp.zeros_like(token_ref)
     copies = []
     for frame in range(frames):
         total = jnp.concatenate([low_ref[frame].reshape(count, chan).astype(jnp.float32)] * 4, axis=0)
-        for k in range(3):
-            act = act_ref[frame - k] if frame >= k else earlier_ref[frame - k + 2]
-            total = total + product(act.reshape(4 * count, chan), wt_ref[k])
+        acts = [act_ref[frame - k] if frame >= k else earlier_ref[frame - k + 2] for k in range(3)]
+        acts = jnp.concatenate([act.reshape(4 * count, chan) for act in acts], axis=1)
+        total = total + product(acts, wt)
         mixed = total.astype(jnp.bfloat16).reshape(4, count, chan)
         for n in range(rows_low // group):
             block = mixed[:, n * span : (n + 1) * span].reshape(4 * span, chan)
@@ -381,19 +382,19 @@
 HBM = pl.BlockSpec(memory_space=pltpu.HBM)
 
 
-def section(earlier, act, low, wt, before):
+def section(earlier, act, low, wt, merge, before):
     frames, rows_low, cols_low, chan = low.shape
     out = (frames, 2 * rows_low, 2 * cols_low, chan)
     return pl.pallas_call(
         section_kernel,
-        in_specs=[FULL] * 4 + [UNREAD],
+        in_specs=[FULL] * 5 + [UNREAD],
         out_specs=[HBM, FULL],
         out_shape=[like(out, jnp.bfloat16), TOKEN],
         scratch_shapes=[pltpu.VMEM(out, jnp.bfloat16), pltpu.SemaphoreType.DMA((frames,))],
         compiler_params=grant(10),
         cost_estimate=cost(4, 3),
         name="section",
-    )(earlier, act, low, wt, before)
+    )(earlier, act, low, wt, merge, before)
 
 
 def split(value):
@@ -414,18 +415,21 @@
     cols_low = out_ref.shape[2]
     rows_low = count // cols_low
     at = column(count, cols_low, chan)
+    turned = jnp.concatenate([ws_ref[i, j].T for j in range(3) for i in range(3)], axis=0)
     for frame in range(frames):
         total = sum(ext_ref[frame, side].astype(jnp.float32) for side in range(4))
         own = [pg_ref[frame, side].astype(jnp.float32) for side in range(4)]
         zero = jnp.zeros((1, cols_low, chan), jnp.float32)
+        parts = []
         for j in range(3):
             even = column_pair(own[0], own[1], j, at, cols_low - 1).reshape(rows_low, cols_low, chan)
             odd = column_pair(own[2], own[3], j, at, cols_low - 1).reshape(rows_low, cols_low, chan)
             below = jnp.concatenate([even[1:], zero], axis=0)
             above = jnp.concatenate([zero, odd[:-1]], axis=0)
-            for i, value in enumerate((odd + below, even + odd, above + even)):
-                for part in split(value.reshape(count, chan)):
-                    total = total + product_nt(part, ws_ref[i, j])
+            for value in (odd + below, even + odd, above + even):
+                parts.append(jnp.concatenate(split(value.reshape(count, chan)), axis=0))
+        sums = product(jnp.concatenate(parts, axis=1), turned)
+        total = total + (sums[:count] + sums[count:])
         out_ref[frame] = total.reshape(rows_low, cols_low, chan)
 
 
@@ -435,13 +439,13 @@
         in_specs=[FULL] * 3 + [UNREAD],
         out_specs=FULL,
         out_shape=like(low_shape, jnp.float32),
-        compiler_params=grant(10),
+        compiler_params=grant(16),
         cost_estimate=cost(6, 4),
         name="input_own",
     )(pg, ext, ws, before)
 
 
-def input_edge_kernel(place_ref, own_ref, inner_ref, outer_ref, ws_ref, out_ref, token_ref, held, sem):
+def input_edge_kernel(place_ref, own_ref, inner_ref, outer_ref, ws_ref, _, out_ref, token_ref, held, sem):
     frames, rows_low, cols_low, chan = own_ref.shape
     token_ref[...] = jnp.zeros_like(token_ref)
     odd_place = place_ref[1] == 1
@@ -470,17 +474,17 @@
     copy.wait()
 
 
-def input_grads(place, own, inner, outer, ws):
+def input_grads(place, own, inner, outer, ws, before):
     return pl.pallas_call(
         input_edge_kernel,
-        in_specs=[SCALAR] + [FULL] * 4,
+        in_specs=[SCALAR] + [FULL] * 4 + [UNREAD],
         out_specs=[HBM, FULL],
         out_shape=[like(own.shape, jnp.bfloat16), TOKEN],
         scratch_shapes=[pltpu.VMEM(own.shape, jnp.bfloat16), pltpu.SemaphoreType.DMA],
         compiler_params=grant(6),
         cost_estimate=cost(1, 1),
         name="input_edge",
-    )(place, own, inner, outer, ws)
+    )(place, own, inner, outer, ws, before)
 
 
 def put_kernel(place_ref, half_ref, *refs):
@@ -576,9 +580,9 @@
     inner, outer, later = first_messages(mine, low, cot)
     later = bits.shift(later, "tm", -1)
     inner, outer = bits.pairs(inner, outer)
-    low, ws, wt, cot_side = load(low, cot, spatial_weight, temporal_weight)
+    low, ws, wt, sort, merge, turned, cot_side = load(low, cot, spatial_weight, temporal_weight)
     act, slope = forward(mine, low, inner, outer, ws)
-    pg, ext, theirs = backward(other, low, inner, outer, act, slope, cot_side, later, wt)
+    pg, ext, theirs = backward(other, low, inner, outer, act, slope, cot_side, later, turned, sort)
     theirs = bits.swap(theirs, bits.core)
     own = half_grads(mine, low, inner, outer, act, pg, ext)
     kept = add_halves(own, theirs)
@@ -589,8 +593,8 @@
     own_part = input_own(pg, ext, ws, kept, low.shape)
     total, far = bits.far_sums(sum_parts(got, own_part))
     earlier = earlier_act(edge, ws, total)
-    section_out, section_done = section(earlier, act, low, wt, total)
-    input_grad, input_done = input_grads(mine, own_part, pg_inner, pg_outer, ws)
+    section_out, section_done = section(earlier, act, low, wt, merge, total)
+    input_grad, input_done = input_grads(mine, own_part, pg_inner, pg_outer, ws, total)
     totals = spread(total, far, parts, section_done, input_done)
     half = bits.exchange(totals).reshape(kept.shape)
     theirs = bits.swap(half, bits.core)

time: 71.1 us -> 70 us (0.985)
  blocking collectives: 15 us -> 13.1 us
  waiting for transfers between devices: 5.57 us -> 6.75 us
    all_to_all x1, waiting for transfers between devices: 0.01 us -> 5.62 us  [exchange(): return lax.all_to_all(parts, tuple(self.near), 0, 0, tiled=True)]
    ppermute x5, waiting for transfers between devices: 5.56 us -> 1.11 us  [swap(): return lax.ppermute(block, axis, [(0, 1), (1, 0)])]
    all_to_all x1, blocking collectives: 15 us -> 13.1 us  [exchange(): return lax.all_to_all(parts, tuple(self.near), 0, 0, tiled=True)]
    pallas_call x1, Pallas kernels: 3.23 us -> 1.55 us  [input_own(): pl.pallas_call(input_kernel, in_specs=[FULL] * 3 + [UNREAD], out_specs=FU...]
    pallas_call x5, Pallas kernels: 12.4 us -> 13.6 us  [the longest x1 3.46 us: section(): pl.pallas_call(section_kernel, in_specs=[FULL] * 5 + [UNREAD], out_specs=...]
where the time goes in v10:
time: 70 us; the launch traced here: 69.6 us
  Pallas kernels  27.7 us (40%)
  starting transfers between devices  20.9 us (30%)
  blocking collectives  13.1 us (19%)
  waiting for transfers between devices  6.75 us (10%)
  between operations  0.93 us (1%)
    all_to_all x1, blocking collectives, exchange(): return lax.all_to_all(parts, tuple(self.near), 0, 0, tiled=True)  13.1 us
    ppermute x5, starting transfers between devices, swap(): return lax.ppermute(block, axis, [(0, 1), (1, 0)])  8.46 us
    all_to_all x1, starting transfers between devices, exchange(): return lax.all_to_all(parts, tuple(self.near), 0, 0, tiled=True)  6.72 us
    all_to_all x1, waiting for transfers between devices, exchange(): return lax.all_to_all(parts, tuple(self.near), 0, 0, tiled=True)  5.62 us
    ppermute x2, starting transfers between devices, shift(): return lax.ppermute(block, axes, route)  3.73 us
    pallas_call x2, Pallas kernels, put(): pl.pallas_call(put_kernel, in_specs=[SCALAR, FULL] + [HBM] * len(done), o...  3.56 us
    pallas_call x1, Pallas kernels, section(): pl.pallas_call(section_kernel, in_specs=[FULL] * 5 + [UNREAD], out_specs=...  3.46 us
    pallas_call x1, Pallas kernels, backward(): pl.pallas_call(backward_kernel, in_specs=[SCALAR] + [FULL] * 9, out_specs...  3.35 us
  transfers between devices with their start and end apart: 10, of which 3 were waited for; matrix products, arithmetic and copies ran while one was open for 0% of the time, Pallas kernels for 28%

profile of v10, /device:TPU:0, one launch (start us, length us, event | category | flops | bytes accessed | tf_op | source)
XLA Modules:
  0.0 69.6 jit_solution(5193115579907592789)
XLA Ops:
  0.6 0.1 pad_add_fusion.place_ref
  0.7 1.7 %first_messages.1 = (bf16[4,1,32,256]{3,2,1,0:T(8,128)(2,1)S(1)}, bf16[4,1,32,256]{3,2,1,0:T(8,128)(2,1)S(1)}, bf16[2,8,64,256]{3,2,1,0:T(8,128)(2,1)S(1)}) custom-call(s32[2]{0:T(128)S(1)} %pad_add_fusion.place_ref, bf16[4,4,32,256]{3,2,1,0:T(8,128)(2,1)} %bitcast.13, bf16[4,8,64,256]{3,2,1,0:T(8,128)(2,1)} %bitcast.11), custom_call_target="tpu_custom_call" | custom-call | tf_op jit(solution)/shard_map/first_messages/pallas_call | solution.py:225
  2.5 1.3 %collective-permute-start.2 = (bf16[2,8,64,256]{3,2,1,0:T(8,128)(2,1)S(1)}, bf16[2,8,64,256]{3,2,1,0:T(8,128)(2,1)S(1)}, u32[]{:S(2)}, u32[]{:S(2)}) collective-permute-start(bf16[2,8,64,256]{3,2,1,0:T(8,128)(2,1)S(1)} %get-tuple-element.37), channel_id=1, source_target_pairs={{4,0},{8,4},{12,8},{5,1},{9,5},{13,9},{6,2},{10,6},{14,10},{7,3},{... | collective-permute-start | bytes 1572872 | tf_op jit(solution)/shard_map/ppermute | solution.py:40
  3.8 3.1 %collective-permute-start = (bf16[4,1,32,256]{3,2,1,0:T(8,128)(2,1)S(1)}, bf16[4,1,32,256]{3,2,1,0:T(8,128)(2,1)S(1)}, u32[]{:S(2)}, u32[]{:S(2)}) collective-permute-start(bf16[4,1,32,256]{3,2,1,0:T(8,128)(2,1)S(1)} %get-tuple-element.31), channel_id=1, source_target_pairs={{0,1},{1,0},{2,3},{3,2},{4,5},{5,4},{6,7},{7,6},{8,9},{9,8},{10,11... | collective-permute-start | bytes 196616 | tf_op jit(solution)/shard_map/ppermute | solution.py:34
  6.8 0.7 collective-permute-start.1
  7.5 0.1 pad_add_fusion.1.place_ref
  7.6 2.4 %load.1 = (bf16[4,4,32,256]{3,2,1,0:T(8,128)(2,1)S(1)}, bf16[3,3,256,256]{3,2,1,0:T(8,128)(2,1)S(1)}, bf16[3,256,256]{2,1,0:T(8,128)(2,1)S(1)}, bf16[256,256]{1,...) custom-call(bf16[4,4,32,256]{3,2,1,0:T(8,128)(2,1)} %bitcast.14, ...), custom_call_target="tpu_custom_call" | custom-call | flops 536870912 | bytes 4194304 | tf_op jit(solution)/shard_map/load/pallas_call | solution.py:264
  10.0 0.0 copy-start.2
  10.0 0.0 collective-permute-done.inner_ref
  10.1 0.0 collective-permute-done.1.outer_ref
  10.1 2.3 %forward.1 = (bf16[4,4,128,256]{3,2,1,0:T(8,128)(2,1)S(1)}, f32[4,4,128,256]{3,2,1,0:T(8,128)S(1)}) custom-call(s32[2]{0:T(128)S(1)} %pad_add_fusion.place_ref, bf16[4,4,32,256]{3,2,1,0:T(8,128)(2,1)S(1)} %get-tuple-element.30.low_ref, bf16[4,1,32,256]{3,2,1,0:T(8,128)(2,1)S(1)} %collective-permute-done.inner_ref, ...), custom_call_target="tpu_custom_call" | custom-call | flops 2684354560 | bytes 8388608 | tf_op jit(solution)/shard_map/forward/pallas_call | solution.py:280
  12.4 0.0 copy-done.2
  12.4 0.0 copy-done.4
  12.4 0.0 copy-start.8
  12.4 0.0 collective-permute-done.2.later_ref
  12.4 3.3 %backward.1 = (bf16[4,4,128,256]{3,2,1,0:T(8,128)(2,1)S(1)}, bf16[6,4,128,256]{3,2,1,0:T(8,128)(2,1)S(1)}, f32[12,128,256]{2,1,0:T(8,128)S(1)}) custom-call(s32[2]{0:T(128)S(1)} %pad_add_fusion.1.place_ref, bf16[4,4,32,256]{3,2,1,0:T(8,128)(2,1)S(1)} %get-tuple-element.30.low_ref, bf16[4,1,32,256]{3,2,1,0:T(8,128)(2,1)S(1)} %collective-permute-done.inner_ref, ...), custom_call_target="tpu_custom_call" | custom-call | flops 4026531840 | bytes 10485760 | tf_op jit(solution)/shard_map/backward/pallas_call | solution.py:334
  15.8 0.0 copy-start.6
  15.8 1.9 %collective-permute-start.3 = (f32[12,128,256]{2,1,0:T(8,128)S(1)}, f32[12,128,256]{2,1,0:T(8,128)S(1)}, u32[]{:S(2)}, u32[]{:S(2)}) collective-permute-start(f32[12,128,256]{2,1,0:T(8,128)S(1)} %get-tuple-element.42), channel_id=1, source_target_pairs={{0,4},{4,0},{1,5},{5,1},{2,6},{6,2},{3,7},{7,3},{8,12},{12,8},{9,1... | collective-permute-start | bytes 4718600 | tf_op jit(solution)/shard_map/ppermute | solution.py:34
  17.7 2.4 %half_grads.1.mine_ref = f32[12,128,256]{2,1,0:T(8,128)S(1)} custom-call(s32[2]{0:T(128)S(1)} %pad_add_fusion.place_ref, bf16[4,4,32,256]{3,2,1,0:T(8,128)(2,1)S(1)} %get-tuple-element.30.low_ref, bf16[4,1,32,256]{3,2,1,0:T(8,128)(2,1)S(1)} %collective-permute-done.inner_ref, bf16[4,1,32,256]{3,2,1,0:T(8,128)(2,1)S(1)} %collective-permute-done.1.outer_ref, ...), custom_call_target="tpu_custom_call" | custom-call | flops 2684354560 | bytes 6291456 | tf_op jit(solution)/shard_map/half_grads/pallas_call | solution.py:347
  20.1 0.0 copy-done.6
  20.1 0.6 collective-permute-done.3.theirs_ref
  20.7 1.0 %add_halves.1._ = bf16[12,128,256]{2,1,0:T(8,128)(2,1)} custom-call(f32[12,128,256]{2,1,0:T(8,128)S(1)} %half_grads.1.mine_ref, f32[12,128,256]{2,1,0:T(8,128)S(1)} %collective-permute-done.3.theirs_ref), custom_call_target="tpu_custom_call" | custom-call | tf_op jit(solution)/shard_map/add_halves/pallas_call | solution.py:527
  21.8 6.7 %all-to-all-start = ((bf16[8,192,256]{2,1,0:T(8,128)(2,1)}), bf16[8,192,256]{2,1,0:T(8,128)(2,1)S(1)}, u32[]{:S(2)}, u32[]{:S(2)}) async-start(bf16[8,192,256]{2,1,0:T(8,128)(2,1)} %bitcast.5), calls=%async_computation | async-start | bytes 1572864 | tf_op jit(solution)/shard_map/all_to_all | solution.py:43
  28.5 0.0 copy-done
  28.5 0.0 copy-start.7
  28.5 1.3 %edges.1 = (bf16[2,6,32,256]{3,2,1,0:T(8,128)(2,1)}, bf16[4,2,32,256]{3,2,1,0:T(8,128)(2,1)}, bf16[4,2,32,256]{3,2,1,0:T(8,128)(2,1)}) custom-call(s32[2]{0:T(128)S(1)} %pad_add_fusion.place_ref, bf16[4,4,32,256]{3,2,1,0:T(8,128)(2,1)S(1)} %get-tuple-element.30.low_ref, bf16[4,1,32,256]{3,2,1,0:T(8,128)(2,1)S(1)} %collective-permute-done.inner_ref, ...), custom_call_target="tpu_custom_call" | custom-call | tf_op jit(solution)/shard_map/edges/pallas_call | solution.py:306
  29.8 2.4 %collective-permute-start.4 = (bf16[2,6,32,256]{3,2,1,0:T(8,128)(2,1)}, bf16[2,6,32,256]{3,2,1,0:T(8,128)(2,1)}, u32[]{:S(2)}, u32[]{:S(2)}) collective-permute-start(bf16[2,6,32,256]{3,2,1,0:T(8,128)(2,1)} %get-tuple-element.43), channel_id=1, source_target_pairs={{0,4},{4,8},{8,12},{1,5},{5,9},{9,13},{2,6},{6,10},{10,14},{3,7},{... | collective-permute-start | bytes 589832 | tf_op jit(solution)/shard_map/ppermute | solution.py:40
  32.3 1.7 %collective-permute-start.5 = (bf16[4,2,32,256]{3,2,1,0:T(8,128)(2,1)}, bf16[4,2,32,256]{3,2,1,0:T(8,128)(2,1)}, u32[]{:S(2)}, u32[]{:S(2)}) collective-permute-start(bf16[4,2,32,256]{3,2,1,0:T(8,128)(2,1)} %get-tuple-element.47), channel_id=1, source_target_pairs={{0,1},{1,0},{2,3},{3,2},{4,5},{5,4},{6,7},{7,6},{8,9},{9,8},{10,11... | collective-permute-start | bytes 393224 | tf_op jit(solution)/shard_map/ppermute | solution.py:34
  34.0 1.3 %collective-permute-start.6 = (bf16[4,2,32,256]{3,2,1,0:T(8,128)(2,1)}, bf16[4,2,32,256]{3,2,1,0:T(8,128)(2,1)}, u32[]{:S(2)}, u32[]{:S(2)}) collective-permute-start(bf16[4,2,32,256]{3,2,1,0:T(8,128)(2,1)} %get-tuple-element.48), channel_id=1, source_target_pairs={{1,2},{2,1},{5,6},{6,5},{9,10},{10,9},{13,14},{14,13},{17,18},{18,... | collective-permute-start | bytes 393224 | tf_op jit(solution)/shard_map/ppermute | solution.py:49
  35.3 0.0 copy-done.7
  35.3 1.6 %input_own.1._.own_ref = f32[4,4,32,256]{3,2,1,0:T(8,128)S(1)} custom-call(bf16[4,4,128,256]{3,2,1,0:T(8,128)(2,1)S(1)} %get-tuple-element.40.pg_ref, bf16[6,4,128,256]{3,2,1,0:T(8,128)(2,1)S(1)} %copy-done.7, bf16[3,3,256,256]{3,2,1,0:T(8,128)(2,1)S(1)} %get-tuple-element.33.ws_ref, bf16[12,128,256]{2,1,0:T(8,128)(2,1)} %add_halves.1._), custom_call_target="tpu_custom_call" | custom-call | flops 1610612736 | bytes 4194304 | tf_op jit(solution)/shard_map/input_own/pallas_call | solution.py:437
  36.9 5.6 %all-to-all-done.got_ref = bf16[8,192,256]{2,1,0:T(8,128)(2,1)S(1)} async-done(((bf16[8,192,256]{2,1,0:T(8,128)(2,1)}), bf16[8,192,256]{2,1,0:T(8,128)(2,1)S(1)}, u32[]{:S(2)}, u32[]{:S(2)}) %all-to-all-start) | async-done | bytes 786464 | tf_op jit(solution)/shard_map/all_to_all | solution.py:43
  42.5 0.1 sum_parts.1._.own_ref
  42.6 1.7 %collective-permute-start.7 = (bf16[192,256]{1,0:T(8,128)(2,1)S(1)}, bf16[192,256]{1,0:T(8,128)(2,1)S(1)}, u32[]{:S(2)}, u32[]{:S(2)}) collective-permute-start(bf16[192,256]{1,0:T(8,128)(2,1)S(1)} %sum_parts.1._.own_ref), channel_id=1, source_target_pairs={{0,2},{2,0},{1,3},{3,1},{4,6},{6,4},{5,7},{7,5},{8,10},{10,8},{9,1... | collective-permute-start | bytes 294920 | tf_op jit(solution)/shard_map/ppermute | solution.py:34
  44.3 0.0 collective-permute-done.4.low_ref
  44.3 1.9 %earlier_act.1.earlier_ref = bf16[2,4,128,256]{3,2,1,0:T(8,128)(2,1)S(1)} custom-call(bf16[2,6,32,256]{3,2,1,0:T(8,128)(2,1)} %collective-permute-done.4.low_ref, bf16[3,3,256,256]{3,2,1,0:T(8,128)(2,1)S(1)} %get-tuple-element.33.ws_ref, bf16[192,256]{1,0:T(8,128)(2,1)S(1)} %sum_parts.1._.own_ref), custom_call_target="tpu_custom_call" | custom-call | flops 1073741824 | bytes 3145728 | tf_op jit(solution)/shard_map/earlier_act/pallas_call | solution.py:319
  46.3 0.0 copy-start.9
  46.3 0.0 collective-permute-done.5.inner_ref
  46.3 0.0 collective-permute-done.6.outer_ref
  46.3 2.5 %input_edge.1 = (bf16[4,4,32,256]{3,2,1,0:T(8,128)(2,1)}, f32[8,128]{1,0:T(8,128)S(1)}) custom-call(s32[2]{0:T(128)S(1)} %pad_add_fusion.place_ref, f32[4,4,32,256]{3,2,1,0:T(8,128)S(1)} %input_own.1._.own_ref, bf16[4,2,32,256]{3,2,1,0:T(8,128)(2,1)} %collective-permute-done.5.inner_ref, bf16[4,2,32,256]{3,2,1,0:T(8,128)(2,1)} %collective-permute-done.6.outer_ref, ...), custom_call_target="tpu_custom_call" | custom-call | flops 268435456 | bytes 1048576 | tf_op jit(solution)/shard_map/input_edge/pallas_call | solution.py:478
  48.8 3.5 %section.1 = (bf16[4,8,64,256]{3,2,1,0:T(8,128)(2,1)}, f32[8,128]{1,0:T(8,128)S(1)}) custom-call(bf16[2,4,128,256]{3,2,1,0:T(8,128)(2,1)S(1)} %earlier_act.1.earlier_ref, bf16[4,4,128,256]{3,2,1,0:T(8,128)(2,1)S(1)} %copy-done.9, bf16[4,4,32,256]{3,2,1,0:T(8,128)(2,1)S(1)} %copy-done.1, bf16[3,256,256]{2,1,0:T(8,128)(2,1)S(1)} %copy-done.3, ...), custom_call_target="tpu_custom_call" | custom-call | flops 1073741824 | bytes 3145728 | tf_op jit(solution)/shard_map/section/pallas_call | solution.py:388
  52.3 0.0 collective-permute-done.7.theirs_ref
  52.3 0.1 spread.1
  52.4 13.1 %all_to_all.10 = bf16[8,192,256]{2,1,0:T(8,128)(2,1)S(1)} all-to-all(bf16[8,192,256]{2,1,0:T(8,128)(2,1)S(1)} %spread.1), channel_id=1, replica_groups=mesh['dp0'=2,'tm1'=2,'tm0'=2,'height1'=2,'height0'=2] {'dp0','tm1','heig..., dimensions={0} | all-to-all | bytes 1572864 | tf_op jit(solution)/shard_map/all_to_all | solution.py:43
  65.5 0.0 collective-permute-start.8
  65.5 1.8 %put.2 = (f32[3,3,256,256]{3,2,1,0:T(8,128)}, f32[3,256,256]{2,1,0:T(8,128)}) custom-call(s32[2]{0:T(128)S(1)} %pad_add_fusion.place_ref, bf16[12,128,256]{2,1,0:T(8,128)(2,1)S(1)} %bitcast.10), custom_call_target="tpu_custom_call" | custom-call | tf_op jit(solution)/shard_map/put/pallas_call | solution.py:509
  67.3 0.5 collective-permute-done.8.half_ref
  67.8 1.8 %put.3 = (f32[3,3,256,256]{3,2,1,0:T(8,128)}, f32[3,256,256]{2,1,0:T(8,128)}) custom-call(s32[2]{0:T(128)S(1)} %pad_add_fusion.1.place_ref, bf16[12,128,256]{2,1,0:T(8,128)(2,1)S(1)} %collective-permute-done.8.half_ref, f32[3,3,256,256]{3,2,1,0:T(8,128)} %get-tuple-element.52.refs_0_, ...), custom_call_target="tpu_custom_call", output_to_operand_aliasing={{0}: (2, {}), {1}: (3, {})} | custom-call | tf_op jit(solution)/shard_map/put/pallas_call | solution.py:509
  (10 shorter events, 0.0 us)
Async XLA Ops:
  2.5 10.0 %collective-permute-start.2 = (bf16[2,8,64,256]{3,2,1,0:T(8,128)(2,1)S(1)}, bf16[2,8,64,256]{3,2,1,0:T(8,128)(2,1)S(1)}, u32[]{:S(2)}, u32[]{:S(2)}) collective-permute-start(bf16[2,8,64,256]{3,2,1,0:T(8,128)(2,1)S(1)} %get-tuple-element.37), channel_id=1, source_target_pairs={{4,0},{8,4},{12,8},{5,1},{9,5},{13,9},{6,2},{10,6},{14,10},{7,3},{... | collective-permute-start | bytes 1572872 | tf_op jit(solution)/shard_map/ppermute | solution.py:40
  3.8 6.3 %collective-permute-start = (bf16[4,1,32,256]{3,2,1,0:T(8,128)(2,1)S(1)}, bf16[4,1,32,256]{3,2,1,0:T(8,128)(2,1)S(1)}, u32[]{:S(2)}, u32[]{:S(2)}) collective-permute-start(bf16[4,1,32,256]{3,2,1,0:T(8,128)(2,1)S(1)} %get-tuple-element.31), channel_id=1, source_target_pairs={{0,1},{1,0},{2,3},{3,2},{4,5},{5,4},{6,7},{7,6},{8,9},{9,8},{10,11... | collective-permute-start | bytes 196616 | tf_op jit(solution)/shard_map/ppermute | solution.py:34
  6.8 3.2 %collective-permute-start.1 = (bf16[4,1,32,256]{3,2,1,0:T(8,128)(2,1)S(1)}, bf16[4,1,32,256]{3,2,1,0:T(8,128)(2,1)S(1)}, u32[]{:S(2)}, u32[]{:S(2)}) collective-permute-start(bf16[4,1,32,256]{3,2,1,0:T(8,128)(2,1)S(1)} %get-tuple-element.32), channel_id=1, source_target_pairs={{1,2},{2,1},{5,6},{6,5},{9,10},{10,9},{13,14},{14,13},{17,18},{18,... | collective-permute-start | bytes 196616 | tf_op jit(solution)/shard_map/ppermute | solution.py:49
  10.0 2.4 %copy-start.2 = (bf16[3,256,256]{2,1,0:T(8,128)(2,1)}, bf16[3,256,256]{2,1,0:T(8,128)(2,1)S(1)}, u32[]{:S(2)}) copy-start(bf16[3,256,256]{2,1,0:T(8,128)(2,1)S(1)} %get-tuple-element.44.wt_ref) | copy-start | bytes 1179652
  10.0 2.4 %copy-start.4 = (bf16[256,256]{1,0:T(8,128)(2,1)}, bf16[256,256]{1,0:T(8,128)(2,1)S(1)}, u32[]{:S(2)}) copy-start(bf16[256,256]{1,0:T(8,128)(2,1)S(1)} %get-tuple-element.45.merge_ref) | copy-start | bytes 393220
  10.0 18.4 %copy-start = (bf16[4,4,32,256]{3,2,1,0:T(8,128)(2,1)}, bf16[4,4,32,256]{3,2,1,0:T(8,128)(2,1)S(1)}, u32[]{:S(2)}) copy-start(bf16[4,4,32,256]{3,2,1,0:T(8,128)(2,1)S(1)} %get-tuple-element.30.low_ref) | copy-start | bytes 786436
  12.4 5.3 %copy-start.8 = (bf16[4,4,128,256]{3,2,1,0:T(8,128)(2,1)}, bf16[4,4,128,256]{3,2,1,0:T(8,128)(2,1)S(1)}, u32[]{:S(2)}) copy-start(bf16[4,4,128,256]{3,2,1,0:T(8,128)(2,1)S(1)} %get-tuple-element.34.act_ref) | copy-start | bytes 3145732
  15.8 4.3 %copy-start.6 = (bf16[6,4,128,256]{3,2,1,0:T(8,128)(2,1)}, bf16[6,4,128,256]{3,2,1,0:T(8,128)(2,1)S(1)}, u32[]{:S(2)}) copy-start(bf16[6,4,128,256]{3,2,1,0:T(8,128)(2,1)S(1)} %get-tuple-element.41.ext_ref) | copy-start | bytes 4718596
  15.8 4.9 %collective-permute-start.3 = (f32[12,128,256]{2,1,0:T(8,128)S(1)}, f32[12,128,256]{2,1,0:T(8,128)S(1)}, u32[]{:S(2)}, u32[]{:S(2)}) collective-permute-start(f32[12,128,256]{2,1,0:T(8,128)S(1)} %get-tuple-element.42), channel_id=1, source_target_pairs={{0,4},{4,0},{1,5},{5,1},{2,6},{6,2},{3,7},{7,3},{8,12},{12,8},{9,1... | collective-permute-start | bytes 4718600 | tf_op jit(solution)/shard_map/ppermute | solution.py:34
  21.8 20.7 %all-to-all-start = ((bf16[8,192,256]{2,1,0:T(8,128)(2,1)}), bf16[8,192,256]{2,1,0:T(8,128)(2,1)S(1)}, u32[]{:S(2)}, u32[]{:S(2)}) async-start(bf16[8,192,256]{2,1,0:T(8,128)(2,1)} %bitcast.5), calls=%async_computation | async-start | bytes 1572864 | tf_op jit(solution)/shard_map/all_to_all | solution.py:43
  28.5 6.8 %copy-start.7 = (bf16[6,4,128,256]{3,2,1,0:T(8,128)(2,1)S(1)}, bf16[6,4,128,256]{3,2,1,0:T(8,128)(2,1)}, u32[]{:S(2)}) copy-start(bf16[6,4,128,256]{3,2,1,0:T(8,128)(2,1)} %copy-done.6) | copy-start | bytes 4718596
  29.8 14.5 %collective-permute-start.4 = (bf16[2,6,32,256]{3,2,1,0:T(8,128)(2,1)}, bf16[2,6,32,256]{3,2,1,0:T(8,128)(2,1)}, u32[]{:S(2)}, u32[]{:S(2)}) collective-permute-start(bf16[2,6,32,256]{3,2,1,0:T(8,128)(2,1)} %get-tuple-element.43), channel_id=1, source_target_pairs={{0,4},{4,8},{8,12},{1,5},{5,9},{9,13},{2,6},{6,10},{10,14},{3,7},{... | collective-permute-start | bytes 589832 | tf_op jit(solution)/shard_map/ppermute | solution.py:40
  32.3 14.1 %collective-permute-start.5 = (bf16[4,2,32,256]{3,2,1,0:T(8,128)(2,1)}, bf16[4,2,32,256]{3,2,1,0:T(8,128)(2,1)}, u32[]{:S(2)}, u32[]{:S(2)}) collective-permute-start(bf16[4,2,32,256]{3,2,1,0:T(8,128)(2,1)} %get-tuple-element.47), channel_id=1, source_target_pairs={{0,1},{1,0},{2,3},{3,2},{4,5},{5,4},{6,7},{7,6},{8,9},{9,8},{10,11... | collective-permute-start | bytes 393224 | tf_op jit(solution)/shard_map/ppermute | solution.py:34
  34.0 12.3 %collective-permute-start.6 = (bf16[4,2,32,256]{3,2,1,0:T(8,128)(2,1)}, bf16[4,2,32,256]{3,2,1,0:T(8,128)(2,1)}, u32[]{:S(2)}, u32[]{:S(2)}) collective-permute-start(bf16[4,2,32,256]{3,2,1,0:T(8,128)(2,1)} %get-tuple-element.48), channel_id=1, source_target_pairs={{1,2},{2,1},{5,6},{6,5},{9,10},{10,9},{13,14},{14,13},{17,18},{18,... | collective-permute-start | bytes 393224 | tf_op jit(solution)/shard_map/ppermute | solution.py:49
  42.6 9.7 %collective-permute-start.7 = (bf16[192,256]{1,0:T(8,128)(2,1)S(1)}, bf16[192,256]{1,0:T(8,128)(2,1)S(1)}, u32[]{:S(2)}, u32[]{:S(2)}) collective-permute-start(bf16[192,256]{1,0:T(8,128)(2,1)S(1)} %sum_parts.1._.own_ref), channel_id=1, source_target_pairs={{0,2},{2,0},{1,3},{3,1},{4,6},{6,4},{5,7},{7,5},{8,10},{10,8},{9,1... | collective-permute-start | bytes 294920 | tf_op jit(solution)/shard_map/ppermute | solution.py:34
  46.3 2.5 %copy-start.1 = (bf16[4,4,32,256]{3,2,1,0:T(8,128)(2,1)S(1)}, bf16[4,4,32,256]{3,2,1,0:T(8,128)(2,1)}, u32[]{:S(2)}) copy-start(bf16[4,4,32,256]{3,2,1,0:T(8,128)(2,1)} %copy-done) | copy-start | bytes 786436
  46.3 2.5 %copy-start.3 = (bf16[3,256,256]{2,1,0:T(8,128)(2,1)S(1)}, bf16[3,256,256]{2,1,0:T(8,128)(2,1)}, u32[]{:S(2)}) copy-start(bf16[3,256,256]{2,1,0:T(8,128)(2,1)} %copy-done.2) | copy-start | bytes 1179652
  46.3 2.5 %copy-start.5 = (bf16[256,256]{1,0:T(8,128)(2,1)S(1)}, bf16[256,256]{1,0:T(8,128)(2,1)}, u32[]{:S(2)}) copy-start(bf16[256,256]{1,0:T(8,128)(2,1)} %copy-done.4) | copy-start | bytes 393220
  46.3 2.5 %copy-start.9 = (bf16[4,4,128,256]{3,2,1,0:T(8,128)(2,1)S(1)}, bf16[4,4,128,256]{3,2,1,0:T(8,128)(2,1)}, u32[]{:S(2)}) copy-start(bf16[4,4,128,256]{3,2,1,0:T(8,128)(2,1)} %copy-done.8) | copy-start | bytes 3145732
  65.5 2.3 %collective-permute-start.8 = (bf16[12,128,256]{2,1,0:T(8,128)(2,1)S(1)}, bf16[12,128,256]{2,1,0:T(8,128)(2,1)S(1)}, u32[]{:S(2)}, u32[]{:S(2)}) collective-permute-start(bf16[12,128,256]{2,1,0:T(8,128)(2,1)S(1)} %bitcast.9), channel_id=1, source_target_pairs={{0,4},{4,0},{1,5},{5,1},{2,6},{6,2},{3,7},{7,3},{8,12},{12,8},{9,1... | collective-permute-start | bytes 2359304 | tf_op jit(solution)/shard_map/ppermute | solution.py:34

commit v11 on v10

--- a/solution.py
+++ b/solution.py
@@ -135,11 +135,6 @@
             sig = jax.nn.sigmoid(pre)
             act_ref[frame, side] = (pre * sig).astype(jnp.bfloat16)
             slope_ref[frame, side] = sig * (1.0 + pre * (1.0 - sig))
-
-
-def act_kernel(low_ref, ws_ref, _, act_ref):
-    for side, pre in enumerate(spatial(low_ref[0], ws_ref)):
-        act_ref[0, side] = (pre * jax.nn.sigmoid(pre)).astype(jnp.bfloat16)
 
 
 def half_sums(place_ref, low_ref, inner_ref, outer_ref, act_ref, pg_ref, ext_ref, out_ref):
@@ -313,21 +308,6 @@
     )(place, low, inner, outer, pg, before)
 
 
-def earlier_act(low, ws, before):
-    frames, rows_tall, cols_low, chan = low.shape
-    side = (frames, 4, (rows_tall - 2) * cols_low, chan)
-    return pl.pallas_call(
-        act_kernel,
-        grid=(frames,),
-        in_specs=[pl.BlockSpec((1,) + low.shape[1:], lambda f: (f, 0, 0, 0)), FULL, UNREAD],
-        out_specs=pl.BlockSpec((1,) + side[1:], lambda f: (f, 0, 0, 0)),
-        out_shape=like(side, jnp.bfloat16),
-        compiler_params=grant(10),
-        cost_estimate=cost(4, 3),
-        name="earlier_act",
-    )(low, ws, before)
-
-
 def backward(place, low, inner, outer, act, slope, cot, later, turned, sort):
     frames, _, _, chan = act.shape
     ext = (frames + 2,) + act.shape[1:]
@@ -355,46 +335,7 @@
     )(place, low, inner, outer, act, pg, ext)
 
 
-def section_kernel(earlier_ref, act_ref, low_ref, wt_ref, merge_ref, _, out_ref, token_ref, held, sems):
-    frames, rows_low, cols_low, chan = low_ref.shape
-    group = rows_at_once(rows_low, cols_low)
-    span, count = group * cols_low, rows_low * cols_low
-    order = merge_ref[...]
-    wt = wt_ref[...].reshape(3 * chan, chan)
-    token_ref[...] = jnp.zeros_like(token_ref)
-    copies = []
-    for frame in range(frames):
-        total = jnp.concatenate([low_ref[frame].reshape(count, chan).astype(jnp.float32)] * 4, axis=0)
-        acts = [act_ref[frame - k] if frame >= k else earlier_ref[frame - k + 2] for k in range(3)]
-        acts = jnp.concatenate([act.reshape(4 * count, chan) for act in acts], axis=1)
-        total = total + product(acts, wt)
-        mixed = total.astype(jnp.bfloat16).reshape(4, count, chan)
-        for n in range(rows_low // group):
-            block = mixed[:, n * span : (n + 1) * span].reshape(4 * span, chan)
-            block = product(order, block).astype(jnp.bfloat16)
-            held[frame, 2 * group * n : 2 * group * (n + 1)] = block.reshape(2 * group, 2 * cols_low, chan)
-        copies.append(pltpu.make_async_copy(held.at[frame], out_ref.at[frame], sems.at[frame]))
-        copies[-1].start()
-    for copy in copies:
-        copy.wait()
-
-
 HBM = pl.BlockSpec(memory_space=pltpu.HBM)
-
-
-def section(earlier, act, low, wt, merge, before):
-    frames, rows_low, cols_low, chan = low.shape
-    out = (frames, 2 * rows_low, 2 * cols_low, chan)
-    return pl.pallas_call(
-        section_kernel,
-        in_specs=[FULL] * 5 + [UNREAD],
-        out_specs=[HBM, FULL],
-        out_shape=[like(out, jnp.bfloat16), TOKEN],
-        scratch_shapes=[pltpu.VMEM(out, jnp.bfloat16), pltpu.SemaphoreType.DMA((frames,))],
-        compiler_params=grant(10),
-        cost_estimate=cost(4, 3),
-        name="section",
-    )(earlier, act, low, wt, merge, before)
 
 
 def split(value):
@@ -445,9 +386,36 @@
     )(pg, ext, ws, before)
 
 
-def input_edge_kernel(place_ref, own_ref, inner_ref, outer_ref, ws_ref, _, out_ref, token_ref, held, sem):
-    frames, rows_low, cols_low, chan = own_ref.shape
+def finish_kernel(place_ref, edge_hbm, inner_hbm, outer_hbm, act_ref, low_ref, own_ref, ws_ref, wt_ref, merge_ref, _,
+                  section_ref, input_ref, token_ref, edge_ref, inner_ref, outer_ref, earlier, held, input_held, sems):
+    frames, rows_low, cols_low, chan = low_ref.shape
+    group = rows_at_once(rows_low, cols_low)
+    span, count = group * cols_low, rows_low * cols_low
+    arrivals = [pltpu.make_async_copy(a, b, sems.at[n]) for n, (a, b) in enumerate(
+        ((edge_hbm, edge_ref), (inner_hbm, inner_ref), (outer_hbm, outer_ref)))]
+    for copy in arrivals:
+        copy.start()
     token_ref[...] = jnp.zeros_like(token_ref)
+    wt = wt_ref[...].reshape(3 * chan, chan)
+    leaving = []
+
+    def section_frame(frame):
+        acts = [act_ref[frame - k] if frame >= k else earlier[frame - k + 2] for k in range(3)]
+        acts = jnp.concatenate([act.reshape(4 * count, chan) for act in acts], axis=1)
+        low = low_ref[frame].reshape(1, count, chan).astype(jnp.float32)
+        mixed = (product(acts, wt).reshape(4, count, chan) + low).astype(jnp.bfloat16)
+        for n in range(rows_low // group):
+            block = mixed[:, n * span : (n + 1) * span].reshape(4 * span, chan)
+            block = product(merge_ref[...], block).astype(jnp.bfloat16)
+            held[frame, 2 * group * n : 2 * group * (n + 1)] = block.reshape(2 * group, 2 * cols_low, chan)
+        leaving.append(pltpu.make_async_copy(held.at[frame], section_ref.at[frame], sems.at[4 + frame]))
+        leaving[-1].start()
+
+    for frame in range(2, frames):
+        section_frame(frame)
+
+    for copy in arrivals[1:]:
+        copy.wait()
     odd_place = place_ref[1] == 1
     flat = (frames * cols_low, chan)
     at = column(flat[0], cols_low, chan)
@@ -459,8 +427,9 @@
     for (first, second), i in ((above, 2), (below, 0)):
         total = jnp.zeros(flat, jnp.float32)
         for j in range(3):
-            for part in split(column_pair(first, second, j, at, cols_low - 1)):
-                total = total + product_nt(part, ws_ref[i, j])
+            parts = jnp.concatenate(split(column_pair(first, second, j, at, cols_low - 1)), axis=0)
+            sums = product_nt(parts, ws_ref[i, j])
+            total = total + (sums[: flat[0]] + sums[flat[0] :])
         terms.append(total.reshape(frames, cols_low, chan))
     for row in range(rows_low):
         value = own_ref[:, row]
@@ -468,23 +437,36 @@
             value = value + terms[0]
         if row == rows_low - 1:
             value = value + terms[1]
-        held[:, row] = value.astype(jnp.bfloat16)
-    copy = pltpu.make_async_copy(held, out_ref, sem)
-    copy.start()
-    copy.wait()
-
-
-def input_grads(place, own, inner, outer, ws, before):
-    return pl.pallas_call(
-        input_edge_kernel,
-        in_specs=[SCALAR] + [FULL] * 4 + [UNREAD],
-        out_specs=[HBM, FULL],
-        out_shape=[like(own.shape, jnp.bfloat16), TOKEN],
-        scratch_shapes=[pltpu.VMEM(own.shape, jnp.bfloat16), pltpu.SemaphoreType.DMA],
-        compiler_params=grant(6),
-        cost_estimate=cost(1, 1),
-        name="input_edge",
-    )(place, own, inner, outer, ws, before)
+        input_held[:, row] = value.astype(jnp.bfloat16)
+    leaving.append(pltpu.make_async_copy(input_held, input_ref, sems.at[3]))
+    leaving[-1].start()
+
+    arrivals[0].wait()
+    for frame in range(2):
+        for side, pre in enumerate(spatial(edge_ref[frame], ws_ref)):
+            earlier[frame, side] = (pre * jax.nn.sigmoid(pre)).astype(jnp.bfloat16)
+    for frame in reversed(range(2)):
+        section_frame(frame)
+    for copy in leaving:
+        copy.wait()
+
+
+def finish(place, edge, inner, outer, act, low, own, ws, wt, merge, before):
+    frames, rows_low, cols_low, chan = low.shape
+    out = (frames, 2 * rows_low, 2 * cols_low, chan)
+    arrivals = [edge, inner, outer]
+    return pl.pallas_call(
+        finish_kernel,
+        in_specs=[SCALAR] + [HBM] * 3 + [FULL] * 6 + [UNREAD],
+        out_specs=[HBM, HBM, FULL],
+        out_shape=[like(out, jnp.bfloat16), like(low.shape, jnp.bfloat16), TOKEN],
+        scratch_shapes=[pltpu.VMEM(a.shape, a.dtype) for a in arrivals]
+        + [pltpu.VMEM((2,) + act.shape[1:], act.dtype), pltpu.VMEM(out, jnp.bfloat16),
+           pltpu.VMEM(low.shape, jnp.bfloat16), pltpu.SemaphoreType.DMA((4 + frames,))],
+        compiler_params=grant(14),
+        cost_estimate=cost(8, 4),
+        name="finish",
+    )(place, *arrivals, act, low, own, ws, wt, merge, before)
 
 
 def put_kernel(place_ref, half_ref, *refs):
@@ -592,10 +574,10 @@
     pg_inner, pg_outer = bits.pairs(pg_inner, pg_outer)
     own_part = input_own(pg, ext, ws, kept, low.shape)
     total, far = bits.far_sums(sum_parts(got, own_part))
-    earlier = earlier_act(edge, ws, total)
-    section_out, section_done = section(earlier, act, low, wt, merge, total)
-    input_grad, input_done = input_grads(mine, own_part, pg_inner, pg_outer, ws, total)
-    totals = spread(total, far, parts, section_done, input_done)
+    section_out, input_grad, done = finish(
+        mine, edge, pg_inner, pg_outer, act, low, own_part, ws, wt, merge, total
+    )
+    totals = spread(total, far, parts, done)
     half = bits.exchange(totals).reshape(kept.shape)
     theirs = bits.swap(half, bits.core)
     spatial_grad, temporal_grad = put(other, theirs, *put(mine, half))

time: 70 us -> 70.2 us (level)
  local copies, waits for them, and re-layouts: 0.05 us -> 3.92 us
  Pallas kernels: 27.7 us -> 25.2 us
  waiting for transfers between devices: 6.75 us -> 6 us
    unnamed x20 -> x14, local copies, waits for them, and re-layouts: 0.05 us -> 3.92 us
    pallas_call x3 -> x1, Pallas kernels: 7.85 us -> 5.42 us  [finish(): pl.pallas_call(finish_kernel, in_specs=[SCALAR] + [HBM] * 3 + [FULL] * 6...]
    all_to_all x1, waiting for transfers between devices: 5.62 us -> 4.88 us  [exchange(): return lax.all_to_all(parts, tuple(self.near), 0, 0, tiled=True)]
  transfers between devices with their start and end apart: 10 -> 10, of which waited for: 3 -> 3; matrix products, arithmetic and copies ran while one was open for 0% -> 0% of each run, Pallas kernels for 28% -> 25%
where the time goes in v11:
time: 70.2 us; the launch traced here: 69.7 us
  Pallas kernels  25.2 us (36%)
  starting transfers between devices  20.3 us (29%)
  blocking collectives  13.3 us (19%)
  waiting for transfers between devices  6 us (9%)
  local copies, waits for them, and re-layouts  3.92 us (6%)
  between operations  0.83 us (1%)
    all_to_all x1, blocking collectives, exchange(): return lax.all_to_all(parts, tuple(self.near), 0, 0, tiled=True)  13.3 us
    ppermute x5, starting transfers between devices, swap(): return lax.ppermute(block, axis, [(0, 1), (1, 0)])  8.59 us
    all_to_all x1, starting transfers between devices, exchange(): return lax.all_to_all(parts, tuple(self.near), 0, 0, tiled=True)  6.68 us
    pallas_call x1, Pallas kernels, finish(): pl.pallas_call(finish_kernel, in_specs=[SCALAR] + [HBM] * 3 + [FULL] * 6...  5.42 us
    all_to_all x1, waiting for transfers between devices, exchange(): return lax.all_to_all(parts, tuple(self.near), 0, 0, tiled=True)  4.88 us
    unnamed x14, local copies, waits for them, and re-layouts  3.92 us
    pallas_call x2, Pallas kernels, put(): pl.pallas_call(put_kernel, in_specs=[SCALAR, FULL] + [HBM] * len(done), o...  3.56 us
    pallas_call x1, Pallas kernels, backward(): pl.pallas_call(backward_kernel, in_specs=[SCALAR] + [FULL] * 9, out_specs...  3.35 us
  transfers between devices with their start and end apart: 10, of which 3 were waited for; matrix products, arithmetic and copies ran while one was open for 0% of the time, Pallas kernels for 25%

profile of v11, /device:TPU:0, one launch (start us, length us, event | category | flops | bytes accessed | tf_op | source)
XLA Modules:
  0.0 69.7 jit_solution(16459036520700947710)
XLA Ops:
  0.6 0.1 pad_add_fusion.place_ref
  0.7 1.7 %first_messages.1 = (bf16[4,1,32,256]{3,2,1,0:T(8,128)(2,1)S(1)}, bf16[4,1,32,256]{3,2,1,0:T(8,128)(2,1)S(1)}, bf16[2,8,64,256]{3,2,1,0:T(8,128)(2,1)S(1)}) custom-call(s32[2]{0:T(128)S(1)} %pad_add_fusion.place_ref, bf16[4,4,32,256]{3,2,1,0:T(8,128)(2,1)} %bitcast.13, bf16[4,8,64,256]{3,2,1,0:T(8,128)(2,1)} %bitcast.11), custom_call_target="tpu_custom_call" | custom-call | tf_op jit(solution)/shard_map/first_messages/pallas_call | solution.py:220
  2.5 1.3 %collective-permute-start.2 = (bf16[2,8,64,256]{3,2,1,0:T(8,128)(2,1)S(1)}, bf16[2,8,64,256]{3,2,1,0:T(8,128)(2,1)S(1)}, u32[]{:S(2)}, u32[]{:S(2)}) collective-permute-start(bf16[2,8,64,256]{3,2,1,0:T(8,128)(2,1)S(1)} %get-tuple-element.36), channel_id=1, source_target_pairs={{4,0},{8,4},{12,8},{5,1},{9,5},{13,9},{6,2},{10,6},{14,10},{7,3},{... | collective-permute-start | bytes 1572872 | tf_op jit(solution)/shard_map/ppermute | solution.py:40
  3.8 3.1 %collective-permute-start = (bf16[4,1,32,256]{3,2,1,0:T(8,128)(2,1)S(1)}, bf16[4,1,32,256]{3,2,1,0:T(8,128)(2,1)S(1)}, u32[]{:S(2)}, u32[]{:S(2)}) collective-permute-start(bf16[4,1,32,256]{3,2,1,0:T(8,128)(2,1)S(1)} %get-tuple-element.30), channel_id=1, source_target_pairs={{0,1},{1,0},{2,3},{3,2},{4,5},{5,4},{6,7},{7,6},{8,9},{9,8},{10,11... | collective-permute-start | bytes 196616 | tf_op jit(solution)/shard_map/ppermute | solution.py:34
  6.8 0.7 collective-permute-start.1
  7.5 0.1 pad_add_fusion.1.place_ref
  7.6 2.4 %load.1 = (bf16[4,4,32,256]{3,2,1,0:T(8,128)(2,1)S(1)}, bf16[3,3,256,256]{3,2,1,0:T(8,128)(2,1)S(1)}, bf16[3,256,256]{2,1,0:T(8,128)(2,1)S(1)}, bf16[256,256]{1,...) custom-call(bf16[4,4,32,256]{3,2,1,0:T(8,128)(2,1)} %bitcast.14, ...), custom_call_target="tpu_custom_call" | custom-call | flops 536870912 | bytes 4194304 | tf_op jit(solution)/shard_map/load/pallas_call | solution.py:259
  10.0 0.0 copy-start
  10.0 0.0 collective-permute-done.inner_ref
  10.0 0.0 collective-permute-done.1.outer_ref
  10.1 2.3 %forward.1 = (bf16[4,4,128,256]{3,2,1,0:T(8,128)(2,1)S(1)}, f32[4,4,128,256]{3,2,1,0:T(8,128)S(1)}) custom-call(s32[2]{0:T(128)S(1)} %pad_add_fusion.place_ref, bf16[4,4,32,256]{3,2,1,0:T(8,128)(2,1)S(1)} %get-tuple-element.29.low_ref, bf16[4,1,32,256]{3,2,1,0:T(8,128)(2,1)S(1)} %collective-permute-done.inner_ref, ...), custom_call_target="tpu_custom_call" | custom-call | flops 2684354560 | bytes 8388608 | tf_op jit(solution)/shard_map/forward/pallas_call | solution.py:275
  12.4 0.0 copy-done
  12.4 0.0 copy-start.5
  12.4 0.0 collective-permute-done.2.later_ref
  12.4 3.3 %backward.1 = (bf16[4,4,128,256]{3,2,1,0:T(8,128)(2,1)S(1)}, bf16[6,4,128,256]{3,2,1,0:T(8,128)(2,1)S(1)}, f32[12,128,256]{2,1,0:T(8,128)S(1)}) custom-call(s32[2]{0:T(128)S(1)} %pad_add_fusion.1.place_ref, bf16[4,4,32,256]{3,2,1,0:T(8,128)(2,1)S(1)} %get-tuple-element.29.low_ref, bf16[4,1,32,256]{3,2,1,0:T(8,128)(2,1)S(1)} %collective-permute-done.inner_ref, ...), custom_call_target="tpu_custom_call" | custom-call | flops 4026531840 | bytes 10485760 | tf_op jit(solution)/shard_map/backward/pallas_call | solution.py:314
  15.8 0.0 copy-start.3
  15.8 1.9 %collective-permute-start.3 = (f32[12,128,256]{2,1,0:T(8,128)S(1)}, f32[12,128,256]{2,1,0:T(8,128)S(1)}, u32[]{:S(2)}, u32[]{:S(2)}) collective-permute-start(f32[12,128,256]{2,1,0:T(8,128)S(1)} %get-tuple-element.41), channel_id=1, source_target_pairs={{0,4},{4,0},{1,5},{5,1},{2,6},{6,2},{3,7},{7,3},{8,12},{12,8},{9,1... | collective-permute-start | bytes 4718600 | tf_op jit(solution)/shard_map/ppermute | solution.py:34
  17.7 0.0 copy-done.5
  17.7 2.4 %half_grads.1.mine_ref = f32[12,128,256]{2,1,0:T(8,128)S(1)} custom-call(s32[2]{0:T(128)S(1)} %pad_add_fusion.place_ref, bf16[4,4,32,256]{3,2,1,0:T(8,128)(2,1)S(1)} %get-tuple-element.29.low_ref, bf16[4,1,32,256]{3,2,1,0:T(8,128)(2,1)S(1)} %collective-permute-done.inner_ref, bf16[4,1,32,256]{3,2,1,0:T(8,128)(2,1)S(1)} %collective-permute-done.1.outer_ref, ...), custom_call_target="tpu_custom_call" | custom-call | flops 2684354560 | bytes 6291456 | tf_op jit(solution)/shard_map/half_grads/pallas_call | solution.py:327
  20.1 0.0 copy-done.3
  20.1 0.6 collective-permute-done.3.theirs_ref
  20.7 1.0 %add_halves.1._ = bf16[12,128,256]{2,1,0:T(8,128)(2,1)} custom-call(f32[12,128,256]{2,1,0:T(8,128)S(1)} %half_grads.1.mine_ref, f32[12,128,256]{2,1,0:T(8,128)S(1)} %collective-permute-done.3.theirs_ref), custom_call_target="tpu_custom_call" | custom-call | tf_op jit(solution)/shard_map/add_halves/pallas_call | solution.py:509
  21.8 6.7 %all-to-all-start = ((bf16[8,192,256]{2,1,0:T(8,128)(2,1)}), bf16[8,192,256]{2,1,0:T(8,128)(2,1)S(1)}, u32[]{:S(2)}, u32[]{:S(2)}) async-start(bf16[8,192,256]{2,1,0:T(8,128)(2,1)} %bitcast.5), calls=%async_computation | async-start | bytes 1572864 | tf_op jit(solution)/shard_map/all_to_all | solution.py:43
  28.4 0.0 copy-start.1
  28.4 1.3 %edges.1 = (bf16[2,6,32,256]{3,2,1,0:T(8,128)(2,1)S(1)}, bf16[4,2,32,256]{3,2,1,0:T(8,128)(2,1)}, bf16[4,2,32,256]{3,2,1,0:T(8,128)(2,1)}) custom-call(s32[2]{0:T(128)S(1)} %pad_add_fusion.place_ref, bf16[4,4,32,256]{3,2,1,0:T(8,128)(2,1)S(1)} %get-tuple-element.29.low_ref, bf16[4,1,32,256]{3,2,1,0:T(8,128)(2,1)S(1)} %collective-permute-done.inner_ref, ...), custom_call_target="tpu_custom_call" | custom-call | tf_op jit(solution)/shard_map/edges/pallas_call | solution.py:301
  29.7 1.8 %collective-permute-start.4 = (bf16[2,6,32,256]{3,2,1,0:T(8,128)(2,1)S(1)}, bf16[2,6,32,256]{3,2,1,0:T(8,128)(2,1)S(1)}, u32[]{:S(2)}, u32[]{:S(2)}) collective-permute-start(bf16[2,6,32,256]{3,2,1,0:T(8,128)(2,1)S(1)} %get-tuple-element.42), channel_id=1, source_target_pairs={{0,4},{4,8},{8,12},{1,5},{5,9},{9,13},{2,6},{6,10},{10,14},{3,7},{... | collective-permute-start | bytes 589832 | tf_op jit(solution)/shard_map/ppermute | solution.py:40
  31.5 1.8 %collective-permute-start.5 = (bf16[4,2,32,256]{3,2,1,0:T(8,128)(2,1)}, bf16[4,2,32,256]{3,2,1,0:T(8,128)(2,1)}, u32[]{:S(2)}, u32[]{:S(2)}) collective-permute-start(bf16[4,2,32,256]{3,2,1,0:T(8,128)(2,1)} %get-tuple-element.43), channel_id=1, source_target_pairs={{0,1},{1,0},{2,3},{3,2},{4,5},{5,4},{6,7},{7,6},{8,9},{9,8},{10,11... | collective-permute-start | bytes 393224 | tf_op jit(solution)/shard_map/ppermute | solution.py:34
  33.3 1.3 %collective-permute-start.6 = (bf16[4,2,32,256]{3,2,1,0:T(8,128)(2,1)}, bf16[4,2,32,256]{3,2,1,0:T(8,128)(2,1)}, u32[]{:S(2)}, u32[]{:S(2)}) collective-permute-start(bf16[4,2,32,256]{3,2,1,0:T(8,128)(2,1)} %get-tuple-element.44), channel_id=1, source_target_pairs={{1,2},{2,1},{5,6},{6,5},{9,10},{10,9},{13,14},{14,13},{17,18},{18,... | collective-permute-start | bytes 393224 | tf_op jit(solution)/shard_map/ppermute | solution.py:49
  34.6 0.0 copy-done.1
  34.6 1.4 %copy-done.4 = bf16[6,4,128,256]{3,2,1,0:T(8,128)(2,1)S(1)} copy-done((bf16[6,4,128,256]{3,2,1,0:T(8,128)(2,1)S(1)}, bf16[6,4,128,256]{3,2,1,0:T(8,128)(2,1)}, u32[]{:S(2)}) %copy-start.4) | copy-done | bytes 1572888
  36.0 1.6 %input_own.1._.own_ref = f32[4,4,32,256]{3,2,1,0:T(8,128)S(1)} custom-call(bf16[4,4,128,256]{3,2,1,0:T(8,128)(2,1)S(1)} %get-tuple-element.39.pg_ref, bf16[6,4,128,256]{3,2,1,0:T(8,128)(2,1)S(1)} %copy-done.4, bf16[3,3,256,256]{3,2,1,0:T(8,128)(2,1)S(1)} %copy-done.1, bf16[12,128,256]{2,1,0:T(8,128)(2,1)} %add_halves.1._), custom_call_target="tpu_custom_call" | custom-call | flops 1610612736 | bytes 4194304 | tf_op jit(solution)/shard_map/input_own/pallas_call | solution.py:378
  37.6 4.9 %all-to-all-done.got_ref = bf16[8,192,256]{2,1,0:T(8,128)(2,1)S(1)} async-done(((bf16[8,192,256]{2,1,0:T(8,128)(2,1)}), bf16[8,192,256]{2,1,0:T(8,128)(2,1)S(1)}, u32[]{:S(2)}, u32[]{:S(2)}) %all-to-all-start) | async-done | bytes 786464 | tf_op jit(solution)/shard_map/all_to_all | solution.py:43
  42.4 0.1 sum_parts.1._.own_ref
  42.6 1.8 %collective-permute-start.7 = (bf16[192,256]{1,0:T(8,128)(2,1)S(1)}, bf16[192,256]{1,0:T(8,128)(2,1)S(1)}, u32[]{:S(2)}, u32[]{:S(2)}) collective-permute-start(bf16[192,256]{1,0:T(8,128)(2,1)S(1)} %sum_parts.1._.own_ref), channel_id=1, source_target_pairs={{0,2},{2,0},{1,3},{3,1},{4,6},{6,4},{5,7},{7,5},{8,10},{10,8},{9,1... | collective-permute-start | bytes 294920 | tf_op jit(solution)/shard_map/ppermute | solution.py:34
  44.3 0.0 collective-permute-done.5.inner_hbm
  44.3 0.0 collective-permute-done.6.outer_hbm
  44.3 0.0 collective-permute-done.4.edge_hbm
  44.3 0.0 copy-start.2
  44.3 1.3 %copy-done.2 = bf16[3,3,256,256]{3,2,1,0:T(8,128)(2,1)S(1)} copy-done((bf16[3,3,256,256]{3,2,1,0:T(8,128)(2,1)S(1)}, bf16[3,3,256,256]{3,2,1,0:T(8,128)(2,1)}, u32[]{:S(2)}) %copy-start.2) | copy-done | bytes 1179672
  45.6 1.2 %copy-done.6 = bf16[4,4,128,256]{3,2,1,0:T(8,128)(2,1)S(1)} copy-done((bf16[4,4,128,256]{3,2,1,0:T(8,128)(2,1)S(1)}, bf16[4,4,128,256]{3,2,1,0:T(8,128)(2,1)}, u32[]{:S(2)}) %copy-start.6) | copy-done | bytes 1048600
  46.8 5.4 %finish.1 = (bf16[4,8,64,256]{3,2,1,0:T(8,128)(2,1)}, bf16[4,4,32,256]{3,2,1,0:T(8,128)(2,1)}, f32[8,128]{1,0:T(8,128)S(1)}) custom-call(s32[2]{0:T(128)S(1)} %pad_add_fusion.place_ref, bf16[2,6,32,256]{3,2,1,0:T(8,128)(2,1)S(1)} %collective-permute-done.4.edge_hbm, bf16[4,2,32,256]{3,2,1,0:T(8,128)(2,1)} %collective-permute-done.5.inner_hbm, ...), custom_call_target="tpu_custom_call" | custom-call | flops 2147483648 | bytes 4194304 | tf_op jit(solution)/shard_map/finish/pallas_call | solution.py:458
  52.3 0.0 collective-permute-done.7.theirs_ref
  52.3 0.1 spread.1
  52.3 13.3 %all_to_all.10 = bf16[8,192,256]{2,1,0:T(8,128)(2,1)S(1)} all-to-all(bf16[8,192,256]{2,1,0:T(8,128)(2,1)S(1)} %spread.1), channel_id=1, replica_groups=mesh['dp0'=2,'tm1'=2,'tm0'=2,'height1'=2,'height0'=2] {'dp0','tm1','heig..., dimensions={0} | all-to-all | bytes 1572864 | tf_op jit(solution)/shard_map/all_to_all | solution.py:43
  65.7 0.0 collective-permute-start.8
  65.7 1.8 %put.2 = (f32[3,3,256,256]{3,2,1,0:T(8,128)}, f32[3,256,256]{2,1,0:T(8,128)}) custom-call(s32[2]{0:T(128)S(1)} %pad_add_fusion.place_ref, bf16[12,128,256]{2,1,0:T(8,128)(2,1)S(1)} %bitcast.10), custom_call_target="tpu_custom_call" | custom-call | tf_op jit(solution)/shard_map/put/pallas_call | solution.py:491
  67.4 0.5 collective-permute-done.8.half_ref
  67.9 1.8 %put.3 = (f32[3,3,256,256]{3,2,1,0:T(8,128)}, f32[3,256,256]{2,1,0:T(8,128)}) custom-call(s32[2]{0:T(128)S(1)} %pad_add_fusion.1.place_ref, bf16[12,128,256]{2,1,0:T(8,128)(2,1)S(1)} %collective-permute-done.8.half_ref, f32[3,3,256,256]{3,2,1,0:T(8,128)} %get-tuple-element.50.refs_0_, ...), custom_call_target="tpu_custom_call", output_to_operand_aliasing={{0}: (2, {}), {1}: (3, {})} | custom-call | tf_op jit(solution)/shard_map/put/pallas_call | solution.py:491
  (2 shorter events, 0.0 us)
Async XLA Ops:
  2.5 9.9 %collective-permute-start.2 = (bf16[2,8,64,256]{3,2,1,0:T(8,128)(2,1)S(1)}, bf16[2,8,64,256]{3,2,1,0:T(8,128)(2,1)S(1)}, u32[]{:S(2)}, u32[]{:S(2)}) collective-permute-start(bf16[2,8,64,256]{3,2,1,0:T(8,128)(2,1)S(1)} %get-tuple-element.36), channel_id=1, source_target_pairs={{4,0},{8,4},{12,8},{5,1},{9,5},{13,9},{6,2},{10,6},{14,10},{7,3},{... | collective-permute-start | bytes 1572872 | tf_op jit(solution)/shard_map/ppermute | solution.py:40
  3.8 6.3 %collective-permute-start = (bf16[4,1,32,256]{3,2,1,0:T(8,128)(2,1)S(1)}, bf16[4,1,32,256]{3,2,1,0:T(8,128)(2,1)S(1)}, u32[]{:S(2)}, u32[]{:S(2)}) collective-permute-start(bf16[4,1,32,256]{3,2,1,0:T(8,128)(2,1)S(1)} %get-tuple-element.30), channel_id=1, source_target_pairs={{0,1},{1,0},{2,3},{3,2},{4,5},{5,4},{6,7},{7,6},{8,9},{9,8},{10,11... | collective-permute-start | bytes 196616 | tf_op jit(solution)/shard_map/ppermute | solution.py:34
  6.8 3.2 %collective-permute-start.1 = (bf16[4,1,32,256]{3,2,1,0:T(8,128)(2,1)S(1)}, bf16[4,1,32,256]{3,2,1,0:T(8,128)(2,1)S(1)}, u32[]{:S(2)}, u32[]{:S(2)}) collective-permute-start(bf16[4,1,32,256]{3,2,1,0:T(8,128)(2,1)S(1)} %get-tuple-element.31), channel_id=1, source_target_pairs={{1,2},{2,1},{5,6},{6,5},{9,10},{10,9},{13,14},{14,13},{17,18},{18,... | collective-permute-start | bytes 196616 | tf_op jit(solution)/shard_map/ppermute | solution.py:49
  10.0 2.4 %copy-start = (bf16[3,3,256,256]{3,2,1,0:T(8,128)(2,1)}, bf16[3,3,256,256]{3,2,1,0:T(8,128)(2,1)S(1)}, u32[]{:S(2)}) copy-start(bf16[3,3,256,256]{3,2,1,0:T(8,128)(2,1)S(1)} %get-tuple-element.32.ws_ref) | copy-start | bytes 3538948
  12.4 5.3 %copy-start.5 = (bf16[4,4,128,256]{3,2,1,0:T(8,128)(2,1)}, bf16[4,4,128,256]{3,2,1,0:T(8,128)(2,1)S(1)}, u32[]{:S(2)}) copy-start(bf16[4,4,128,256]{3,2,1,0:T(8,128)(2,1)S(1)} %get-tuple-element.33.act_ref) | copy-start | bytes 3145732
  15.8 4.4 %copy-start.3 = (bf16[6,4,128,256]{3,2,1,0:T(8,128)(2,1)}, bf16[6,4,128,256]{3,2,1,0:T(8,128)(2,1)S(1)}, u32[]{:S(2)}) copy-start(bf16[6,4,128,256]{3,2,1,0:T(8,128)(2,1)S(1)} %get-tuple-element.40.ext_ref) | copy-start | bytes 4718596
  15.8 5.0 %collective-permute-start.3 = (f32[12,128,256]{2,1,0:T(8,128)S(1)}, f32[12,128,256]{2,1,0:T(8,128)S(1)}, u32[]{:S(2)}, u32[]{:S(2)}) collective-permute-start(f32[12,128,256]{2,1,0:T(8,128)S(1)} %get-tuple-element.41), channel_id=1, source_target_pairs={{0,4},{4,0},{1,5},{5,1},{2,6},{6,2},{3,7},{7,3},{8,12},{12,8},{9,1... | collective-permute-start | bytes 4718600 | tf_op jit(solution)/shard_map/ppermute | solution.py:34
  21.8 20.7 %all-to-all-start = ((bf16[8,192,256]{2,1,0:T(8,128)(2,1)}), bf16[8,192,256]{2,1,0:T(8,128)(2,1)S(1)}, u32[]{:S(2)}, u32[]{:S(2)}) async-start(bf16[8,192,256]{2,1,0:T(8,128)(2,1)} %bitcast.5), calls=%async_computation | async-start | bytes 1572864 | tf_op jit(solution)/shard_map/all_to_all | solution.py:43
  28.4 6.2 %copy-start.1 = (bf16[3,3,256,256]{3,2,1,0:T(8,128)(2,1)S(1)}, bf16[3,3,256,256]{3,2,1,0:T(8,128)(2,1)}, u32[]{:S(2)}) copy-start(bf16[3,3,256,256]{3,2,1,0:T(8,128)(2,1)} %copy-done) | copy-start | bytes 3538948
  29.7 14.6 %collective-permute-start.4 = (bf16[2,6,32,256]{3,2,1,0:T(8,128)(2,1)S(1)}, bf16[2,6,32,256]{3,2,1,0:T(8,128)(2,1)S(1)}, u32[]{:S(2)}, u32[]{:S(2)}) collective-permute-start(bf16[2,6,32,256]{3,2,1,0:T(8,128)(2,1)S(1)} %get-tuple-element.42), channel_id=1, source_target_pairs={{0,4},{4,8},{8,12},{1,5},{5,9},{9,13},{2,6},{6,10},{10,14},{3,7},{... | collective-permute-start | bytes 589832 | tf_op jit(solution)/shard_map/ppermute | solution.py:40
  31.5 12.8 %collective-permute-start.5 = (bf16[4,2,32,256]{3,2,1,0:T(8,128)(2,1)}, bf16[4,2,32,256]{3,2,1,0:T(8,128)(2,1)}, u32[]{:S(2)}, u32[]{:S(2)}) collective-permute-start(bf16[4,2,32,256]{3,2,1,0:T(8,128)(2,1)} %get-tuple-element.43), channel_id=1, source_target_pairs={{0,1},{1,0},{2,3},{3,2},{4,5},{5,4},{6,7},{7,6},{8,9},{9,8},{10,11... | collective-permute-start | bytes 393224 | tf_op jit(solution)/shard_map/ppermute | solution.py:34
  33.3 11.0 %collective-permute-start.6 = (bf16[4,2,32,256]{3,2,1,0:T(8,128)(2,1)}, bf16[4,2,32,256]{3,2,1,0:T(8,128)(2,1)}, u32[]{:S(2)}, u32[]{:S(2)}) collective-permute-start(bf16[4,2,32,256]{3,2,1,0:T(8,128)(2,1)} %get-tuple-element.44), channel_id=1, source_target_pairs={{1,2},{2,1},{5,6},{6,5},{9,10},{10,9},{13,14},{14,13},{17,18},{18,... | collective-permute-start | bytes 393224 | tf_op jit(solution)/shard_map/ppermute | solution.py:49
  34.6 1.4 %copy-start.4 = (bf16[6,4,128,256]{3,2,1,0:T(8,128)(2,1)S(1)}, bf16[6,4,128,256]{3,2,1,0:T(8,128)(2,1)}, u32[]{:S(2)}) copy-start(bf16[6,4,128,256]{3,2,1,0:T(8,128)(2,1)} %copy-done.3) | copy-start | bytes 4718596
  42.6 9.7 %collective-permute-start.7 = (bf16[192,256]{1,0:T(8,128)(2,1)S(1)}, bf16[192,256]{1,0:T(8,128)(2,1)S(1)}, u32[]{:S(2)}, u32[]{:S(2)}) collective-permute-start(bf16[192,256]{1,0:T(8,128)(2,1)S(1)} %sum_parts.1._.own_ref), channel_id=1, source_target_pairs={{0,2},{2,0},{1,3},{3,1},{4,6},{6,4},{5,7},{7,5},{8,10},{10,8},{9,1... | collective-permute-start | bytes 294920 | tf_op jit(solution)/shard_map/ppermute | solution.py:34
  44.3 1.3 %copy-start.2 = (bf16[3,3,256,256]{3,2,1,0:T(8,128)(2,1)S(1)}, bf16[3,3,256,256]{3,2,1,0:T(8,128)(2,1)}, u32[]{:S(2)}) copy-start(bf16[3,3,256,256]{3,2,1,0:T(8,128)(2,1)} %copy-done) | copy-start | bytes 3538948
  45.6 1.2 %copy-start.6 = (bf16[4,4,128,256]{3,2,1,0:T(8,128)(2,1)S(1)}, bf16[4,4,128,256]{3,2,1,0:T(8,128)(2,1)}, u32[]{:S(2)}) copy-start(bf16[4,4,128,256]{3,2,1,0:T(8,128)(2,1)} %copy-done.5) | copy-start | bytes 3145732
  65.7 2.3 %collective-permute-start.8 = (bf16[12,128,256]{2,1,0:T(8,128)(2,1)S(1)}, bf16[12,128,256]{2,1,0:T(8,128)(2,1)S(1)}, u32[]{:S(2)}, u32[]{:S(2)}) collective-permute-start(bf16[12,128,256]{2,1,0:T(8,128)(2,1)S(1)} %bitcast.9), channel_id=1, source_target_pairs={{0,4},{4,0},{1,5},{5,1},{2,6},{6,2},{3,7},{7,3},{8,12},{12,8},{9,1... | collective-permute-start | bytes 2359304 | tf_op jit(solution)/shard_map/ppermute | solution.py:34

commit v12 on v11

--- a/solution.py
+++ b/solution.py
@@ -165,8 +165,11 @@
         out_ref[9 + k] = product(act, ext_ref[k : k + frames].reshape(frames * 4 * count, chan))
 
 
-def backward_kernel(place_ref, low_ref, inner_ref, outer_ref, act_ref, slope_ref, cot_ref, later_ref, turned_ref, sort_ref, pg_ref, ext_ref, out_ref):
+def backward_kernel(place_ref, low_ref, inner_ref, outer_ref, act_ref, slope_ref, cot_ref, later_ref, turned_ref, sort_ref,
+                    pg_ref, ext_ref, out_ref, act_out, pg_out, box_out, box_ref, sems):
     frames, _, count, chan = cot_ref.shape
+    copies = [pltpu.make_async_copy(act_ref, act_out, sems.at[0])]
+    copies[0].start()
     ext_ref[:frames] = cot_ref[...]
     for n in range(2):
         sort_columns(later_ref.at[n], ext_ref.at[frames + n], low_ref.shape[2], sort_ref[...])
@@ -175,7 +178,14 @@
         act_grad = product(jnp.concatenate(cots, axis=1), turned_ref[...])
         slope = slope_ref[frame].reshape(4 * count, chan)
         pg_ref[frame] = (act_grad * slope).astype(jnp.bfloat16).reshape(4, count, chan)
+        box_ref[frame] = sum(cot_ref[frame, side].astype(jnp.float32) for side in range(4))
+        copies.append(pltpu.make_async_copy(pg_ref.at[frame], pg_out.at[frame], sems.at[1 + frame]))
+        copies[-1].start()
+    copies.append(pltpu.make_async_copy(box_ref, box_out, sems.at[1 + frames]))
+    copies[-1].start()
     half_sums(place_ref, low_ref, inner_ref, outer_ref, act_ref, pg_ref, ext_ref, out_ref)
+    for copy in copies:
+        copy.wait()
 
 
 SCALAR = pl.BlockSpec(memory_space=pltpu.SMEM)
@@ -198,6 +208,7 @@
 
 
 FULL = pl.BlockSpec(memory_space=pltpu.VMEM)
+HBM = pl.BlockSpec(memory_space=pltpu.HBM)
 
 
 def first_kernel(place_ref, low_ref, cot_ref, inner_ref, outer_ref, later_ref, sems):
@@ -229,7 +240,7 @@
 
 
 def load_kernel(low_hbm, cot_hbm, ws_hbm, wt_hbm, sort_hbm,
-                low_ref, ws_ref, wt_ref, sort_ref, merge_ref, turned_ref, side_ref, cot_ref, wide_ref, sems):
+                low_ref, ws_ref, sort_ref, turned_ref, side_ref, cot_ref, wide_ref, wt_ref, sems):
     frames, cols_low, chan = low_ref.shape[0], low_ref.shape[2], low_ref.shape[3]
     pairs = [(sort_hbm, wide_ref)] + [(cot_hbm.at[n], cot_ref.at[n]) for n in range(frames)]
     pairs += [(wt_hbm.at[k], wt_ref.at[k]) for k in range(3)] + [(low_hbm, low_ref)]
@@ -239,7 +250,6 @@
         copy.start()
     copies[0].wait()
     sort_ref[...] = wide_ref[...].astype(jnp.bfloat16)
-    merge_ref[...] = wide_ref[...].T.astype(jnp.bfloat16)
     for n in range(frames):
         copies[1 + n].wait()
         sort_columns(cot_ref.at[n], side_ref.at[n], cols_low, sort_ref[...])
@@ -250,18 +260,17 @@
         copy.wait()
 
 
-def load(low, cot, ws, wt):
+def load(low, cot, ws, wt, sort):
     frames, rows_low, cols_low, chan = low.shape
-    sort = jnp.asarray(side_order(rows_low, cols_low))
     order = like(sort.shape, jnp.bfloat16)
-    shapes = [low, ws, wt, order, order, like((3 * chan, chan), wt.dtype),
+    shapes = [low, ws, order, like((3 * chan, chan), wt.dtype),
               like((frames, 4, rows_low * cols_low, chan), jnp.bfloat16)]
     return pl.pallas_call(
         load_kernel,
         in_specs=[UNREAD] * 5,
-        out_specs=[FULL] * 7,
+        out_specs=[FULL] * 5,
         out_shape=[like(a.shape, a.dtype) for a in shapes],
-        scratch_shapes=[pltpu.VMEM(cot.shape, cot.dtype), pltpu.VMEM(sort.shape, sort.dtype),
+        scratch_shapes=[pltpu.VMEM(cot.shape, cot.dtype), pltpu.VMEM(sort.shape, sort.dtype), pltpu.VMEM(wt.shape, wt.dtype),
                         pltpu.SemaphoreType.DMA((frames + 14,))],
         compiler_params=grant(14),
         cost_estimate=cost(2, 4),
@@ -283,40 +292,54 @@
     )(place, low, inner, outer, ws)
 
 
-def edges_kernel(place_ref, low_ref, inner_ref, outer_ref, pg_ref, _, tall_ref, pg_inner, pg_outer):
+def edges_kernel(place_ref, low_hbm, inner_ref, outer_ref, pg_hbm, _, tall_ref, pg_inner, pg_outer, low_ref, rows_ref, sems):
     cols_low = low_ref.shape[2]
-    first = low_ref.shape[0] - tall_ref.shape[0]
-    for n in range(tall_ref.shape[0]):
-        tall_ref[n] = tall(place_ref, low_ref, inner_ref, outer_ref, first + n)
+    frames, first = low_hbm.shape[0], low_hbm.shape[0] - 2
+    copies = [
+        pltpu.make_async_copy(low_hbm.at[first:], low_ref, sems.at[0]),
+        pltpu.make_async_copy(pg_hbm.at[:, 0:2, 0:cols_low], rows_ref.at[0], sems.at[1]),
+        pltpu.make_async_copy(pg_hbm.at[:, 2:4, pg_hbm.shape[2] - cols_low :], rows_ref.at[1], sems.at[2]),
+    ]
+    for copy in copies:
+        copy.start()
+    for copy in copies:
+        copy.wait()
     odd = place_ref[1] == 1
-    top, bottom = pg_ref[:, :2, :cols_low, :], pg_ref[:, 2:, -cols_low:, :]
-    pg_inner[...] = jnp.where(odd, top, bottom)
-    pg_outer[...] = jnp.where(odd, bottom, top)
+    for n in range(2):
+        inner, outer = inner_ref[first + n], outer_ref[first + n]
+        up, down = jnp.where(odd, inner, outer), jnp.where(odd, outer, inner)
+        tall_ref[n] = jnp.concatenate([up, low_ref[n], down], axis=0)
+    pg_inner[...] = jnp.where(odd, rows_ref[0], rows_ref[1])
+    pg_outer[...] = jnp.where(odd, rows_ref[1], rows_ref[0])
 
 
 def edges(place, low, inner, outer, pg, before):
     frames, rows_low, cols_low, chan = low.shape
-    full = pl.BlockSpec(memory_space=pltpu.VMEM)
     rows = like((frames, 2, cols_low, chan), jnp.bfloat16)
     return pl.pallas_call(
         edges_kernel,
-        in_specs=[SCALAR, full, full, full, full, UNREAD],
-        out_specs=[full] * 3,
+        in_specs=[SCALAR, HBM, FULL, FULL, HBM, UNREAD],
+        out_specs=[FULL] * 3,
         out_shape=[like((2, rows_low + 2, cols_low, chan), jnp.bfloat16), rows, rows],
-        compiler_params=grant(8),
+        scratch_shapes=[pltpu.VMEM((2,) + low.shape[1:], low.dtype), pltpu.VMEM((2,) + rows.shape, rows.dtype),
+                        pltpu.SemaphoreType.DMA((3,))],
+        compiler_params=grant(4),
         name="edges",
-    )(place, low, inner, outer, pg, before)
+    )(place, in_hbm(low), inner, outer, in_hbm(pg), before)
 
 
 def backward(place, low, inner, outer, act, slope, cot, later, turned, sort):
-    frames, _, _, chan = act.shape
+    frames, _, count, chan = act.shape
     ext = (frames + 2,) + act.shape[1:]
+    box = (frames, count, chan)
     return pl.pallas_call(
         backward_kernel,
         in_specs=[SCALAR] + [FULL] * 9,
-        out_specs=[FULL] * 3,
-        out_shape=[like(act.shape, jnp.bfloat16), like(ext, jnp.bfloat16), like((12, chan // 2, chan), jnp.float32)],
-        compiler_params=grant(24),
+        out_specs=[FULL] * 3 + [HBM] * 3,
+        out_shape=[like(act.shape, jnp.bfloat16), like(ext, jnp.bfloat16), like((12, chan // 2, chan), jnp.float32),
+                   like(act.shape, jnp.bfloat16), like(act.shape, jnp.bfloat16), like(box, jnp.float32)],
+        scratch_shapes=[pltpu.VMEM(box, jnp.float32), pltpu.SemaphoreType.DMA((frames + 2,))],
+        compiler_params=grant(26),
         cost_estimate=cost(15, 10),
         name="backward",
     )(place, low, inner, outer, act, slope, cot, later, turned, sort)
@@ -335,9 +358,6 @@
     )(place, low, inner, outer, act, pg, ext)
 
 
-HBM = pl.BlockSpec(memory_space=pltpu.HBM)
-
-
 def split(value):
     high = value.astype(jnp.bfloat16)
     return high, (value - high.astype(jnp.float32)).astype(jnp.bfloat16)
@@ -351,14 +371,38 @@
     return first + from_left(second, at)
 
 
-def input_kernel(pg_ref, ext_ref, ws_ref, _, out_ref):
-    frames, _, count, chan = pg_ref.shape
-    cols_low = out_ref.shape[2]
-    rows_low = count // cols_low
+def section_frame(acts, low, wt, merge, held):
+    rows_low, cols_low, chan = low.shape
+    group = rows_at_once(rows_low, cols_low)
+    span, count = group * cols_low, rows_low * cols_low
+    acts = jnp.concatenate([act.reshape(4 * count, chan) for act in acts], axis=1)
+    mixed = product(acts, wt.reshape(3 * chan, chan)).reshape(4, count, chan)
+    mixed = (mixed + low.reshape(1, count, chan).astype(jnp.float32)).astype(jnp.bfloat16)
+    for n in range(rows_low // group):
+        block = mixed[:, n * span : (n + 1) * span].reshape(4 * span, chan)
+        block = product(merge, block).astype(jnp.bfloat16)
+        held[2 * group * n : 2 * group * (n + 1)] = block.reshape(2 * group, 2 * cols_low, chan)
+
+
+def middle_kernel(pg_hbm, act_hbm, box_hbm, low_hbm, ws_hbm, wt_hbm, sort_hbm, _,
+                  out_ref, section_ref, ws_ref, wt_ref, merge_ref, act_ref, low_ref,
+                  pg_ref, box_ref, wide_ref, held, sems):
+    frames, rows_low, cols_low, chan = low_ref.shape
+    count = rows_low * cols_low
+    pairs = [(pg_hbm.at[0], pg_ref.at[0])]
+    pairs += [(ws_hbm.at[i, j], ws_ref.at[i, j]) for i in range(3) for j in range(3)]
+    pairs += [(box_hbm, box_ref)] + [(pg_hbm.at[n], pg_ref.at[n]) for n in range(1, frames)]
+    pairs += [(sort_hbm, wide_ref), (act_hbm, act_ref), (wt_hbm, wt_ref), (low_hbm, low_ref)]
+    copies = [pltpu.make_async_copy(a, b, sems.at[n]) for n, (a, b) in enumerate(pairs)]
+    for copy in copies:
+        copy.start()
+    for copy in copies[:11]:
+        copy.wait()
     at = column(count, cols_low, chan)
     turned = jnp.concatenate([ws_ref[i, j].T for j in range(3) for i in range(3)], axis=0)
     for frame in range(frames):
-        total = sum(ext_ref[frame, side].astype(jnp.float32) for side in range(4))
+        if frame:
+            copies[10 + frame].wait()
         own = [pg_ref[frame, side].astype(jnp.float32) for side in range(4)]
         zero = jnp.zeros((1, cols_low, chan), jnp.float32)
         parts = []
@@ -370,50 +414,56 @@
             for value in (odd + below, even + odd, above + even):
                 parts.append(jnp.concatenate(split(value.reshape(count, chan)), axis=0))
         sums = product(jnp.concatenate(parts, axis=1), turned)
-        total = total + (sums[:count] + sums[count:])
-        out_ref[frame] = total.reshape(rows_low, cols_low, chan)
-
-
-def input_own(pg, ext, ws, before, low_shape):
-    return pl.pallas_call(
-        input_kernel,
-        in_specs=[FULL] * 3 + [UNREAD],
-        out_specs=FULL,
-        out_shape=like(low_shape, jnp.float32),
-        compiler_params=grant(16),
-        cost_estimate=cost(6, 4),
-        name="input_own",
-    )(pg, ext, ws, before)
-
-
-def finish_kernel(place_ref, edge_hbm, inner_hbm, outer_hbm, act_ref, low_ref, own_ref, ws_ref, wt_ref, merge_ref, _,
+        out_ref[frame] = (box_ref[frame] + (sums[:count] + sums[count:])).reshape(rows_low, cols_low, chan)
+    for copy in copies[10 + frames :]:
+        copy.wait()
+    merge_ref[...] = wide_ref[...].T.astype(jnp.bfloat16)
+    leaving = []
+    for frame in range(3, frames):
+        acts = [act_ref[frame - k] for k in range(3)]
+        section_frame(acts, low_ref[frame], wt_ref[...], merge_ref[...], held.at[frame - 3])
+        leaving.append(pltpu.make_async_copy(held.at[frame - 3], section_ref.at[frame], sems.at[frame]))
+        leaving[-1].start()
+    for copy in leaving:
+        copy.wait()
+
+
+def middle(pg, act, box, low, ws, wt, sort, before):
+    frames, rows_low, cols_low, chan = low.shape
+    out = (frames, 2 * rows_low, 2 * cols_low, chan)
+    order = like(sort.shape, jnp.bfloat16)
+    operands = [like(a.shape, a.dtype) for a in (ws, wt, order, act, low)]
+    return pl.pallas_call(
+        middle_kernel,
+        in_specs=[HBM] * 7 + [UNREAD],
+        out_specs=[FULL, HBM] + [FULL] * 5,
+        out_shape=[like(low.shape, jnp.float32), like(out, jnp.bfloat16)] + operands,
+        scratch_shapes=[pltpu.VMEM(pg.shape, pg.dtype), pltpu.VMEM(box.shape, box.dtype),
+                        pltpu.VMEM(sort.shape, sort.dtype), pltpu.VMEM((frames - 3,) + out[1:], jnp.bfloat16),
+                        pltpu.SemaphoreType.DMA((14 + frames,))],
+        compiler_params=grant(20),
+        cost_estimate=cost(8, 5),
+        name="middle",
+    )(*[in_hbm(a) for a in (pg, act, box, low, ws, wt, sort)], before)
+
+
+def finish_kernel(place_ref, edge_hbm, inner_hbm, outer_hbm, act_ref, low_ref, own_ref, ws_ref, wt_ref, merge_ref, _, __,
                   section_ref, input_ref, token_ref, edge_ref, inner_ref, outer_ref, earlier, held, input_held, sems):
     frames, rows_low, cols_low, chan = low_ref.shape
-    group = rows_at_once(rows_low, cols_low)
-    span, count = group * cols_low, rows_low * cols_low
     arrivals = [pltpu.make_async_copy(a, b, sems.at[n]) for n, (a, b) in enumerate(
         ((edge_hbm, edge_ref), (inner_hbm, inner_ref), (outer_hbm, outer_ref)))]
     for copy in arrivals:
         copy.start()
     token_ref[...] = jnp.zeros_like(token_ref)
-    wt = wt_ref[...].reshape(3 * chan, chan)
     leaving = []
 
-    def section_frame(frame):
+    def put_frame(frame):
         acts = [act_ref[frame - k] if frame >= k else earlier[frame - k + 2] for k in range(3)]
-        acts = jnp.concatenate([act.reshape(4 * count, chan) for act in acts], axis=1)
-        low = low_ref[frame].reshape(1, count, chan).astype(jnp.float32)
-        mixed = (product(acts, wt).reshape(4, count, chan) + low).astype(jnp.bfloat16)
-        for n in range(rows_low // group):
-            block = mixed[:, n * span : (n + 1) * span].reshape(4 * span, chan)
-            block = product(merge_ref[...], block).astype(jnp.bfloat16)
-            held[frame, 2 * group * n : 2 * group * (n + 1)] = block.reshape(2 * group, 2 * cols_low, chan)
+        section_frame(acts, low_ref[frame], wt_ref[...], merge_ref[...], held.at[frame])
         leaving.append(pltpu.make_async_copy(held.at[frame], section_ref.at[frame], sems.at[4 + frame]))
         leaving[-1].start()
 
-    for frame in range(2, frames):
-        section_frame(frame)
-
+    put_frame(2)
     for copy in arrivals[1:]:
         copy.wait()
     odd_place = place_ref[1] == 1
@@ -446,27 +496,28 @@
         for side, pre in enumerate(spatial(edge_ref[frame], ws_ref)):
             earlier[frame, side] = (pre * jax.nn.sigmoid(pre)).astype(jnp.bfloat16)
     for frame in reversed(range(2)):
-        section_frame(frame)
+        put_frame(frame)
     for copy in leaving:
         copy.wait()
 
 
-def finish(place, edge, inner, outer, act, low, own, ws, wt, merge, before):
+def finish(place, edge, inner, outer, act, low, own, ws, wt, merge, begun, before):
     frames, rows_low, cols_low, chan = low.shape
-    out = (frames, 2 * rows_low, 2 * cols_low, chan)
+    out = begun.shape
     arrivals = [edge, inner, outer]
     return pl.pallas_call(
         finish_kernel,
-        in_specs=[SCALAR] + [HBM] * 3 + [FULL] * 6 + [UNREAD],
+        in_specs=[SCALAR] + [HBM] * 3 + [FULL] * 6 + [HBM, UNREAD],
         out_specs=[HBM, HBM, FULL],
+        input_output_aliases={10: 0},
         out_shape=[like(out, jnp.bfloat16), like(low.shape, jnp.bfloat16), TOKEN],
         scratch_shapes=[pltpu.VMEM(a.shape, a.dtype) for a in arrivals]
-        + [pltpu.VMEM((2,) + act.shape[1:], act.dtype), pltpu.VMEM(out, jnp.bfloat16),
-           pltpu.VMEM(low.shape, jnp.bfloat16), pltpu.SemaphoreType.DMA((4 + frames,))],
+        + [pltpu.VMEM((2,) + act.shape[1:], act.dtype), pltpu.VMEM((3,) + out[1:], jnp.bfloat16),
+           pltpu.VMEM(low.shape, jnp.bfloat16), pltpu.SemaphoreType.DMA((7,))],
         compiler_params=grant(14),
         cost_estimate=cost(8, 4),
         name="finish",
-    )(place, *arrivals, act, low, own, ws, wt, merge, before)
+    )(place, *arrivals, act, low, own, ws, wt, merge, begun, before)
 
 
 def put_kernel(place_ref, half_ref, *refs):
@@ -562,20 +613,25 @@
     inner, outer, later = first_messages(mine, low, cot)
     later = bits.shift(later, "tm", -1)
     inner, outer = bits.pairs(inner, outer)
-    low, ws, wt, sort, merge, turned, cot_side = load(low, cot, spatial_weight, temporal_weight)
-    act, slope = forward(mine, low, inner, outer, ws)
-    pg, ext, theirs = backward(other, low, inner, outer, act, slope, cot_side, later, turned, sort)
+    order = jnp.asarray(side_order(rows_low, cols_low))
+    low_in, ws, sort, turned, cot_side = load(low, cot, spatial_weight, temporal_weight, order)
+    act, slope = forward(mine, low_in, inner, outer, ws)
+    pg, ext, theirs, act_out, pg_out, box = backward(
+        other, low_in, inner, outer, act, slope, cot_side, later, turned, sort
+    )
     theirs = bits.swap(theirs, bits.core)
-    own = half_grads(mine, low, inner, outer, act, pg, ext)
+    own = half_grads(mine, low_in, inner, outer, act, pg, ext)
     kept = add_halves(own, theirs)
     got = bits.exchange(kept.reshape(parts, -1, chan))
-    edge, pg_inner, pg_outer = edges(mine, low, inner, outer, pg, kept)
+    edge, pg_inner, pg_outer = edges(mine, low, inner, outer, pg_out, kept)
     edge = bits.shift(edge, "tm", 1)
     pg_inner, pg_outer = bits.pairs(pg_inner, pg_outer)
-    own_part = input_own(pg, ext, ws, kept, low.shape)
+    own_part, begun, ws, wt, merge, act, low_in = middle(
+        pg_out, act_out, box, low, spatial_weight, temporal_weight, order, kept
+    )
     total, far = bits.far_sums(sum_parts(got, own_part))
     section_out, input_grad, done = finish(
-        mine, edge, pg_inner, pg_outer, act, low, own_part, ws, wt, merge, total
+        mine, edge, pg_inner, pg_outer, act, low_in, own_part, ws, wt, merge, begun, total
     )
     totals = spread(total, far, parts, done)
     half = bits.exchange(totals).reshape(kept.shape)

time: 70.2 us -> 78.9 us (1.12)
  Pallas kernels: 25.2 us -> 31.9 us
  waiting for transfers between devices: 6 us -> 1.1 us
  blocking collectives: 13.3 us -> 17.6 us
  local copies, waits for them, and re-layouts: 3.92 us -> 5.6 us
    pallas_call x3, Pallas kernels: 5.25 us -> 10.2 us  [the longest x1 6.18 us: middle(): pl.pallas_call(middle_kernel, in_specs=[HBM] * 7 + [UNREAD], out_specs=[F...]
    all_to_all x1, waiting for transfers between devices: 4.88 us -> 0.01 us  [exchange(): return lax.all_to_all(parts, tuple(self.near), 0, 0, tiled=True)]
    all_to_all x1, blocking collectives: 13.3 us -> 17.6 us  [exchange(): return lax.all_to_all(parts, tuple(self.near), 0, 0, tiled=True)]
    pallas_call x1, Pallas kernels: 3.35 us -> 5.06 us  [backward(): pl.pallas_call(backward_kernel, in_specs=[SCALAR] + [FULL] * 9, out_specs...]
    unnamed x14 -> x18, local copies, waits for them, and re-layouts: 3.92 us -> 5.6 us
    ppermute x5, starting transfers between devices: 8.59 us -> 10.2 us  [swap(): return lax.ppermute(block, axis, [(0, 1), (1, 0)])]
  transfers between devices with their start and end apart: 10 -> 10, of which waited for: 3 -> 2; matrix products, arithmetic and copies ran while one was open for 0% -> 0% of each run, Pallas kernels for 25% -> 28%
where the time goes in v12:
time: 78.9 us; the launch traced here: 78.4 us
  Pallas kernels  31.9 us (40%)
  starting transfers between devices  21 us (27%)
  blocking collectives  17.6 us (22%)
  local copies, waits for them, and re-layouts  5.6 us (7%)
  waiting for transfers between devices  1.1 us (1%)
  between operations  1.02 us (1%)
    all_to_all x1, blocking collectives, exchange(): return lax.all_to_all(parts, tuple(self.near), 0, 0, tiled=True)  17.6 us
    ppermute x5, starting transfers between devices, swap(): return lax.ppermute(block, axis, [(0, 1), (1, 0)])  10.2 us
    all_to_all x1, starting transfers between devices, exchange(): return lax.all_to_all(parts, tuple(self.near), 0, 0, tiled=True)  6.7 us
    pallas_call x1, Pallas kernels, middle(): pl.pallas_call(middle_kernel, in_specs=[HBM] * 7 + [UNREAD], out_specs=[F...  6.18 us
    unnamed x18, local copies, waits for them, and re-layouts  5.6 us
    pallas_call x1, Pallas kernels, finish(): pl.pallas_call(finish_kernel, in_specs=[SCALAR] + [HBM] * 3 + [FULL] * 6...  5.38 us
    pallas_call x1, Pallas kernels, backward(): pl.pallas_call(backward_kernel, in_specs=[SCALAR] + [FULL] * 9, out_specs...  5.06 us
    pallas_call x2, Pallas kernels, put(): pl.pallas_call(put_kernel, in_specs=[SCALAR, FULL] + [HBM] * len(done), o...  3.56 us
  transfers between devices with their start and end apart: 10, of which 2 were waited for; matrix products, arithmetic and copies ran while one was open for 0% of the time, Pallas kernels for 28%

profile of v12, /device:TPU:0, one launch (start us, length us, event | category | flops | bytes accessed | tf_op | source)
XLA Modules:
  0.0 78.4 jit_solution(4661228340209581302)
XLA Ops:
  0.6 0.1 pad_add_fusion.place_ref
  0.7 1.7 %first_messages.1 = (bf16[4,1,32,256]{3,2,1,0:T(8,128)(2,1)S(1)}, bf16[4,1,32,256]{3,2,1,0:T(8,128)(2,1)S(1)}, bf16[2,8,64,256]{3,2,1,0:T(8,128)(2,1)S(1)}) custom-call(s32[2]{0:T(128)S(1)} %pad_add_fusion.place_ref, bf16[4,4,32,256]{3,2,1,0:T(8,128)(2,1)} %bitcast.13, bf16[4,8,64,256]{3,2,1,0:T(8,128)(2,1)} %bitcast.11), custom_call_target="tpu_custom_call" | custom-call | tf_op jit(solution)/shard_map/first_messages/pallas_call | solution.py:231
  2.5 1.3 %collective-permute-start.2 = (bf16[2,8,64,256]{3,2,1,0:T(8,128)(2,1)S(1)}, bf16[2,8,64,256]{3,2,1,0:T(8,128)(2,1)S(1)}, u32[]{:S(2)}, u32[]{:S(2)}) collective-permute-start(bf16[2,8,64,256]{3,2,1,0:T(8,128)(2,1)S(1)} %get-tuple-element.44), channel_id=1, source_target_pairs={{4,0},{8,4},{12,8},{5,1},{9,5},{13,9},{6,2},{10,6},{14,10},{7,3},{... | collective-permute-start | bytes 1572872 | tf_op jit(solution)/shard_map/ppermute | solution.py:40
  3.8 3.1 %collective-permute-start = (bf16[4,1,32,256]{3,2,1,0:T(8,128)(2,1)S(1)}, bf16[4,1,32,256]{3,2,1,0:T(8,128)(2,1)S(1)}, u32[]{:S(2)}, u32[]{:S(2)}) collective-permute-start(bf16[4,1,32,256]{3,2,1,0:T(8,128)(2,1)S(1)} %get-tuple-element.37), channel_id=1, source_target_pairs={{0,1},{1,0},{2,3},{3,2},{4,5},{5,4},{6,7},{7,6},{8,9},{9,8},{10,11... | collective-permute-start | bytes 196616 | tf_op jit(solution)/shard_map/ppermute | solution.py:34
  6.8 0.7 collective-permute-start.1
  7.5 0.1 pad_add_fusion.1.place_ref
  7.6 2.4 %load.1 = (bf16[4,4,32,256]{3,2,1,0:T(8,128)(2,1)S(1)}, bf16[3,3,256,256]{3,2,1,0:T(8,128)(2,1)S(1)}, bf16[256,256]{1,0:T(8,128)(2,1)S(1)}, bf16[768,256]{1,0:T(8,128)(2,1)S(1)}, bf16[4,4,128,256]{3,2,1,0:T(8,128)(2,1)S(1)}) custom-call(bf16[4,4,32,256]{3,2,1,0:T(8,128)(2,1)} %bitcast.14, bf16[4,8,64,256]{3,2,1,0:T(8,128)(2,1)} %bitcast.12, ...), custom_call_target="tpu_custom_call" | custom-call | flops 536870912 | bytes 4194304 | tf_op jit(solution)/shard_map/load/pallas_call | solution.py:268
  10.0 0.0 collective-permute-done.inner_ref
  10.0 0.0 collective-permute-done.1.outer_ref
  10.0 2.4 %forward.1 = (bf16[4,4,128,256]{3,2,1,0:T(8,128)(2,1)S(1)}, f32[4,4,128,256]{3,2,1,0:T(8,128)S(1)}) custom-call(s32[2]{0:T(128)S(1)} %pad_add_fusion.place_ref, bf16[4,4,32,256]{3,2,1,0:T(8,128)(2,1)S(1)} %get-tuple-element.39.low_ref, bf16[4,1,32,256]{3,2,1,0:T(8,128)(2,1)S(1)} %collective-permute-done.inner_ref, ...), custom_call_target="tpu_custom_call" | custom-call | flops 2684354560 | bytes 8388608 | tf_op jit(solution)/shard_map/forward/pallas_call | solution.py:284
  12.4 0.0 collective-permute-done.2.later_ref
  12.4 5.1 %backward.1 = (bf16[4,4,128,256]{3,2,1,0:T(8,128)(2,1)S(1)}, bf16[6,4,128,256]{3,2,1,0:T(8,128)(2,1)S(1)}, f32[12,128,256]{2,1,0:T(8,128)S(1)}, bf16[4,4,128,256...) custom-call(s32[2]{0:T(128)S(1)} %pad_add_fusion.1.place_ref, ...), custom_call_target="tpu_custom_call" | custom-call | flops 4026531840 | bytes 10485760 | tf_op jit(solution)/shard_map/backward/pallas_call | solution.py:335
  17.5 0.0 copy-start
  17.5 0.0 copy-start.1
  17.5 0.0 copy-start.4
  17.5 1.9 %collective-permute-start.3 = (f32[12,128,256]{2,1,0:T(8,128)S(1)}, f32[12,128,256]{2,1,0:T(8,128)S(1)}, u32[]{:S(2)}, u32[]{:S(2)}) collective-permute-start(f32[12,128,256]{2,1,0:T(8,128)S(1)} %get-tuple-element.50), channel_id=1, source_target_pairs={{0,4},{4,0},{1,5},{5,1},{2,6},{6,2},{3,7},{7,3},{8,12},{12,8},{9,1... | collective-permute-start | bytes 4718600 | tf_op jit(solution)/shard_map/ppermute | solution.py:34
  19.4 2.4 %half_grads.1.mine_ref = f32[12,128,256]{2,1,0:T(8,128)S(1)} custom-call(s32[2]{0:T(128)S(1)} %pad_add_fusion.place_ref, bf16[4,4,32,256]{3,2,1,0:T(8,128)(2,1)S(1)} %get-tuple-element.39.low_ref, bf16[4,1,32,256]{3,2,1,0:T(8,128)(2,1)S(1)} %collective-permute-done.inner_ref, bf16[4,1,32,256]{3,2,1,0:T(8,128)(2,1)S(1)} %collective-permute-done.1.outer_ref, ...), custom_call_target="tpu_custom_call" | custom-call | flops 2684354560 | bytes 6291456 | tf_op jit(solution)/shard_map/half_grads/pallas_call | solution.py:350
  21.9 0.0 copy-done
  21.9 0.6 collective-permute-done.3.theirs_ref
  22.5 1.0 %add_halves.1._ = bf16[12,128,256]{2,1,0:T(8,128)(2,1)} custom-call(f32[12,128,256]{2,1,0:T(8,128)S(1)} %half_grads.1.mine_ref, f32[12,128,256]{2,1,0:T(8,128)S(1)} %collective-permute-done.3.theirs_ref), custom_call_target="tpu_custom_call" | custom-call | tf_op jit(solution)/shard_map/add_halves/pallas_call | solution.py:560
  23.5 6.7 %all-to-all-start = ((bf16[8,192,256]{2,1,0:T(8,128)(2,1)}), bf16[8,192,256]{2,1,0:T(8,128)(2,1)S(1)}, u32[]{:S(2)}, u32[]{:S(2)}) async-start(bf16[8,192,256]{2,1,0:T(8,128)(2,1)} %bitcast.5), calls=%async_computation | async-start | bytes 1572864 | tf_op jit(solution)/shard_map/all_to_all | solution.py:43
  30.2 1.6 %edges.1 = (bf16[2,6,32,256]{3,2,1,0:T(8,128)(2,1)S(1)}, bf16[4,2,32,256]{3,2,1,0:T(8,128)(2,1)S(1)}, bf16[4,2,32,256]{3,2,1,0:T(8,128)(2,1)S(1)}) custom-call(s32[2]{0:T(128)S(1)} %pad_add_fusion.place_ref, bf16[4,4,32,256]{3,2,1,0:T(8,128)(2,1)} %bitcast.15, bf16[4,1,32,256]{3,2,1,0:T(8,128)(2,1)S(1)} %collective-permute-done.inner_ref, ...), custom_call_target="tpu_custom_call" | custom-call | tf_op jit(solution)/shard_map/edges/pallas_call | solution.py:319
  31.8 2.1 %collective-permute-start.5 = (bf16[4,2,32,256]{3,2,1,0:T(8,128)(2,1)S(1)}, bf16[4,2,32,256]{3,2,1,0:T(8,128)(2,1)S(1)}, u32[]{:S(2)}, u32[]{:S(2)}) collective-permute-start(bf16[4,2,32,256]{3,2,1,0:T(8,128)(2,1)S(1)} %get-tuple-element.52), channel_id=1, source_target_pairs={{0,1},{1,0},{2,3},{3,2},{4,5},{5,4},{6,7},{7,6},{8,9},{9,8},{10,11... | collective-permute-start | bytes 393224 | tf_op jit(solution)/shard_map/ppermute | solution.py:34
  33.9 0.7 collective-permute-start.6
  34.6 1.5 %collective-permute-start.4 = (bf16[2,6,32,256]{3,2,1,0:T(8,128)(2,1)S(1)}, bf16[2,6,32,256]{3,2,1,0:T(8,128)(2,1)S(1)}, u32[]{:S(2)}, u32[]{:S(2)}) collective-permute-start(bf16[2,6,32,256]{3,2,1,0:T(8,128)(2,1)S(1)} %get-tuple-element.51), channel_id=1, source_target_pairs={{0,4},{4,8},{8,12},{1,5},{5,9},{9,13},{2,6},{6,10},{10,14},{3,7},{... | collective-permute-start | bytes 589832 | tf_op jit(solution)/shard_map/ppermute | solution.py:40
  36.1 6.2 %middle.1 = (f32[4,4,32,256]{3,2,1,0:T(8,128)S(1)}, bf16[4,8,64,256]{3,2,1,0:T(8,128)(2,1)}, bf16[3,3,256,256]{3,2,1,0:T(8,128)(2,1)S(1)}, bf16[3,256,256]{2,1,0...) custom-call(bf16[4,4,128,256]{3,2,1,0:T(8,128)(2,1)} %copy-done, ...), custom_call_target="tpu_custom_call" | custom-call | flops 2147483648 | bytes 5242880 | tf_op jit(solution)/shard_map/middle/pallas_call | solution.py:436
  42.3 0.0 copy-start.2
  42.3 1.0 %copy-done.2 = bf16[4,4,128,256]{3,2,1,0:T(8,128)(2,1)} copy-done((bf16[4,4,128,256]{3,2,1,0:T(8,128)(2,1)}, bf16[4,4,128,256]{3,2,1,0:T(8,128)(2,1)S(1)}, u32[]{:S(2)}) %copy-start.2) | copy-done | bytes 1048600
  43.2 0.8 copy-done.5
  44.0 0.7 copy-done.7
  44.7 0.0 all-to-all-done.got_ref
  44.7 0.1 sum_parts.1.__.own_ref
  44.8 3.1 %collective-permute-start.7 = (bf16[192,256]{1,0:T(8,128)(2,1)S(1)}, bf16[192,256]{1,0:T(8,128)(2,1)S(1)}, u32[]{:S(2)}, u32[]{:S(2)}) collective-permute-start(bf16[192,256]{1,0:T(8,128)(2,1)S(1)} %sum_parts.1.__.own_ref), channel_id=1, source_target_pairs={{0,2},{2,0},{1,3},{3,1},{4,6},{6,4},{5,7},{7,5},{8,10},{10,8},{9,1... | collective-permute-start | bytes 294920 | tf_op jit(solution)/shard_map/ppermute | solution.py:34
  47.9 0.0 collective-permute-done.5.inner_hbm
  47.9 0.0 collective-permute-done.6.outer_hbm
  47.9 0.0 collective-permute-done.4.edge_hbm
  47.9 0.0 copy-start.3
  47.9 1.2 %copy-done.3 = bf16[4,4,128,256]{3,2,1,0:T(8,128)(2,1)S(1)} copy-done((bf16[4,4,128,256]{3,2,1,0:T(8,128)(2,1)S(1)}, bf16[4,4,128,256]{3,2,1,0:T(8,128)(2,1)}, u32[]{:S(2)}) %copy-start.3) | copy-done | bytes 1048600
  49.1 1.0 %copy-done.6 = bf16[3,256,256]{2,1,0:T(8,128)(2,1)S(1)} copy-done((bf16[3,256,256]{2,1,0:T(8,128)(2,1)S(1)}, bf16[3,256,256]{2,1,0:T(8,128)(2,1)}, u32[]{:S(2)}) %copy-start.6) | copy-done | bytes 393240
  50.1 0.9 %copy-done.8 = bf16[4,4,32,256]{3,2,1,0:T(8,128)(2,1)S(1)} copy-done((bf16[4,4,32,256]{3,2,1,0:T(8,128)(2,1)S(1)}, bf16[4,4,32,256]{3,2,1,0:T(8,128)(2,1)}, u32[]{:S(2)}) %copy-start.8) | copy-done | bytes 262168
  51.1 5.4 %finish.1 = (bf16[4,8,64,256]{3,2,1,0:T(8,128)(2,1)}, bf16[4,4,32,256]{3,2,1,0:T(8,128)(2,1)}, f32[8,128]{1,0:T(8,128)S(1)}) custom-call(s32[2]{0:T(128)S(1)} %pad_add_fusion.place_ref, bf16[2,6,32,256]{3,2,1,0:T(8,128)(2,1)S(1)} %collective-permute-done.4.edge_hbm, ...), custom_call_target="tpu_custom_call", output_to_operand_aliasing={{0}: (10, {})} | custom-call | flops 2147483648 | bytes 4194304 | tf_op jit(solution)/shard_map/finish/pallas_call | solution.py:508
  56.4 0.0 collective-permute-done.7.theirs_ref
  56.5 0.1 spread.1
  56.5 17.6 %all_to_all.10 = bf16[8,192,256]{2,1,0:T(8,128)(2,1)S(1)} all-to-all(bf16[8,192,256]{2,1,0:T(8,128)(2,1)S(1)} %spread.1), channel_id=1, replica_groups=mesh['dp0'=2,'tm1'=2,'tm0'=2,'height1'=2,'height0'=2] {'dp0','tm1','heig..., dimensions={0} | all-to-all | bytes 1572864 | tf_op jit(solution)/shard_map/all_to_all | solution.py:43
  74.1 0.0 collective-permute-start.8
  74.2 1.8 %put.2 = (f32[3,3,256,256]{3,2,1,0:T(8,128)}, f32[3,256,256]{2,1,0:T(8,128)}) custom-call(s32[2]{0:T(128)S(1)} %pad_add_fusion.place_ref, bf16[12,128,256]{2,1,0:T(8,128)(2,1)S(1)} %bitcast.10), custom_call_target="tpu_custom_call" | custom-call | tf_op jit(solution)/shard_map/put/pallas_call | solution.py:542
  75.9 0.5 collective-permute-done.8.half_ref
  76.4 1.8 %put.3 = (f32[3,3,256,256]{3,2,1,0:T(8,128)}, f32[3,256,256]{2,1,0:T(8,128)}) custom-call(s32[2]{0:T(128)S(1)} %pad_add_fusion.1.place_ref, bf16[12,128,256]{2,1,0:T(8,128)(2,1)S(1)} %collective-permute-done.8.half_ref, f32[3,3,256,256]{3,2,1,0:T(8,128)} %get-tuple-element.66.refs_0_, ...), custom_call_target="tpu_custom_call", output_to_operand_aliasing={{0}: (2, {}), {1}: (3, {})} | custom-call | tf_op jit(solution)/shard_map/put/pallas_call | solution.py:542
  (6 shorter events, 0.0 us)
Async XLA Ops:
  2.5 9.9 %collective-permute-start.2 = (bf16[2,8,64,256]{3,2,1,0:T(8,128)(2,1)S(1)}, bf16[2,8,64,256]{3,2,1,0:T(8,128)(2,1)S(1)}, u32[]{:S(2)}, u32[]{:S(2)}) collective-permute-start(bf16[2,8,64,256]{3,2,1,0:T(8,128)(2,1)S(1)} %get-tuple-element.44), channel_id=1, source_target_pairs={{4,0},{8,4},{12,8},{5,1},{9,5},{13,9},{6,2},{10,6},{14,10},{7,3},{... | collective-permute-start | bytes 1572872 | tf_op jit(solution)/shard_map/ppermute | solution.py:40
  3.8 6.2 %collective-permute-start = (bf16[4,1,32,256]{3,2,1,0:T(8,128)(2,1)S(1)}, bf16[4,1,32,256]{3,2,1,0:T(8,128)(2,1)S(1)}, u32[]{:S(2)}, u32[]{:S(2)}) collective-permute-start(bf16[4,1,32,256]{3,2,1,0:T(8,128)(2,1)S(1)} %get-tuple-element.37), channel_id=1, source_target_pairs={{0,1},{1,0},{2,3},{3,2},{4,5},{5,4},{6,7},{7,6},{8,9},{9,8},{10,11... | collective-permute-start | bytes 196616 | tf_op jit(solution)/shard_map/ppermute | solution.py:34
  6.8 3.1 %collective-permute-start.1 = (bf16[4,1,32,256]{3,2,1,0:T(8,128)(2,1)S(1)}, bf16[4,1,32,256]{3,2,1,0:T(8,128)(2,1)S(1)}, u32[]{:S(2)}, u32[]{:S(2)}) collective-permute-start(bf16[4,1,32,256]{3,2,1,0:T(8,128)(2,1)S(1)} %get-tuple-element.38), channel_id=1, source_target_pairs={{1,2},{2,1},{5,6},{6,5},{9,10},{10,9},{13,14},{14,13},{17,18},{18,... | collective-permute-start | bytes 196616 | tf_op jit(solution)/shard_map/ppermute | solution.py:49
  17.5 4.4 %copy-start = (bf16[4,4,128,256]{3,2,1,0:T(8,128)(2,1)}, bf16[4,4,128,256]{3,2,1,0:T(8,128)(2,1)S(1)}, u32[]{:S(2)}) copy-start(bf16[4,4,128,256]{3,2,1,0:T(8,128)(2,1)S(1)} %get-tuple-element.47.pg_hbm) | copy-start | bytes 3145732
  17.5 4.4 %copy-start.1 = (bf16[4,4,128,256]{3,2,1,0:T(8,128)(2,1)}, bf16[4,4,128,256]{3,2,1,0:T(8,128)(2,1)S(1)}, u32[]{:S(2)}) copy-start(bf16[4,4,128,256]{3,2,1,0:T(8,128)(2,1)S(1)} %get-tuple-element.54.act_hbm) | copy-start | bytes 3145732
  17.5 4.4 %copy-start.4 = (f32[4,128,256]{2,1,0:T(8,128)}, f32[4,128,256]{2,1,0:T(8,128)S(1)}, u32[]{:S(2)}) copy-start(f32[4,128,256]{2,1,0:T(8,128)S(1)} %get-tuple-element.55.box_hbm) | copy-start | bytes 1572868
  17.5 5.0 %collective-permute-start.3 = (f32[12,128,256]{2,1,0:T(8,128)S(1)}, f32[12,128,256]{2,1,0:T(8,128)S(1)}, u32[]{:S(2)}, u32[]{:S(2)}) collective-permute-start(f32[12,128,256]{2,1,0:T(8,128)S(1)} %get-tuple-element.50), channel_id=1, source_target_pairs={{0,4},{4,0},{1,5},{5,1},{2,6},{6,2},{3,7},{7,3},{8,12},{12,8},{9,1... | collective-permute-start | bytes 4718600 | tf_op jit(solution)/shard_map/ppermute | solution.py:34
  23.5 21.2 %all-to-all-start = ((bf16[8,192,256]{2,1,0:T(8,128)(2,1)}), bf16[8,192,256]{2,1,0:T(8,128)(2,1)S(1)}, u32[]{:S(2)}, u32[]{:S(2)}) async-start(bf16[8,192,256]{2,1,0:T(8,128)(2,1)} %bitcast.5), calls=%async_computation | async-start | bytes 1572864 | tf_op jit(solution)/shard_map/all_to_all | solution.py:43
  31.8 16.0 %collective-permute-start.5 = (bf16[4,2,32,256]{3,2,1,0:T(8,128)(2,1)S(1)}, bf16[4,2,32,256]{3,2,1,0:T(8,128)(2,1)S(1)}, u32[]{:S(2)}, u32[]{:S(2)}) collective-permute-start(bf16[4,2,32,256]{3,2,1,0:T(8,128)(2,1)S(1)} %get-tuple-element.52), channel_id=1, source_target_pairs={{0,1},{1,0},{2,3},{3,2},{4,5},{5,4},{6,7},{7,6},{8,9},{9,8},{10,11... | collective-permute-start | bytes 393224 | tf_op jit(solution)/shard_map/ppermute | solution.py:34
  33.9 14.0 %collective-permute-start.6 = (bf16[4,2,32,256]{3,2,1,0:T(8,128)(2,1)S(1)}, bf16[4,2,32,256]{3,2,1,0:T(8,128)(2,1)S(1)}, u32[]{:S(2)}, u32[]{:S(2)}) collective-permute-start(bf16[4,2,32,256]{3,2,1,0:T(8,128)(2,1)S(1)} %get-tuple-element.53), channel_id=1, source_target_pairs={{1,2},{2,1},{5,6},{6,5},{9,10},{10,9},{13,14},{14,13},{17,18},{18,... | collective-permute-start | bytes 393224 | tf_op jit(solution)/shard_map/ppermute | solution.py:49
  34.6 13.3 %collective-permute-start.4 = (bf16[2,6,32,256]{3,2,1,0:T(8,128)(2,1)S(1)}, bf16[2,6,32,256]{3,2,1,0:T(8,128)(2,1)S(1)}, u32[]{:S(2)}, u32[]{:S(2)}) collective-permute-start(bf16[2,6,32,256]{3,2,1,0:T(8,128)(2,1)S(1)} %get-tuple-element.51), channel_id=1, source_target_pairs={{0,4},{4,8},{8,12},{1,5},{5,9},{9,13},{2,6},{6,10},{10,14},{3,7},{... | collective-permute-start | bytes 589832 | tf_op jit(solution)/shard_map/ppermute | solution.py:40
  42.3 1.0 %copy-start.2 = (bf16[4,4,128,256]{3,2,1,0:T(8,128)(2,1)}, bf16[4,4,128,256]{3,2,1,0:T(8,128)(2,1)S(1)}, u32[]{:S(2)}) copy-start(bf16[4,4,128,256]{3,2,1,0:T(8,128)(2,1)S(1)} %get-tuple-element.56.act_ref) | copy-start | bytes 3145732
  43.2 0.8 copy-start.5
  44.0 0.7 copy-start.7
  44.8 11.6 %collective-permute-start.7 = (bf16[192,256]{1,0:T(8,128)(2,1)S(1)}, bf16[192,256]{1,0:T(8,128)(2,1)S(1)}, u32[]{:S(2)}, u32[]{:S(2)}) collective-permute-start(bf16[192,256]{1,0:T(8,128)(2,1)S(1)} %sum_parts.1.__.own_ref), channel_id=1, source_target_pairs={{0,2},{2,0},{1,3},{3,1},{4,6},{6,4},{5,7},{7,5},{8,10},{10,8},{9,1... | collective-permute-start | bytes 294920 | tf_op jit(solution)/shard_map/ppermute | solution.py:34
  47.9 1.2 %copy-start.3 = (bf16[4,4,128,256]{3,2,1,0:T(8,128)(2,1)S(1)}, bf16[4,4,128,256]{3,2,1,0:T(8,128)(2,1)}, u32[]{:S(2)}) copy-start(bf16[4,4,128,256]{3,2,1,0:T(8,128)(2,1)} %copy-done.2) | copy-start | bytes 3145732
  49.1 1.0 %copy-start.6 = (bf16[3,256,256]{2,1,0:T(8,128)(2,1)S(1)}, bf16[3,256,256]{2,1,0:T(8,128)(2,1)}, u32[]{:S(2)}) copy-start(bf16[3,256,256]{2,1,0:T(8,128)(2,1)} %copy-done.5) | copy-start | bytes 1179652
  50.1 0.9 %copy-start.8 = (bf16[4,4,32,256]{3,2,1,0:T(8,128)(2,1)S(1)}, bf16[4,4,32,256]{3,2,1,0:T(8,128)(2,1)}, u32[]{:S(2)}) copy-start(bf16[4,4,32,256]{3,2,1,0:T(8,128)(2,1)} %copy-done.7) | copy-start | bytes 786436
  74.1 2.3 %collective-permute-start.8 = (bf16[12,128,256]{2,1,0:T(8,128)(2,1)S(1)}, bf16[12,128,256]{2,1,0:T(8,128)(2,1)S(1)}, u32[]{:S(2)}, u32[]{:S(2)}) collective-permute-start(bf16[12,128,256]{2,1,0:T(8,128)(2,1)S(1)} %bitcast.9), channel_id=1, source_target_pairs={{0,4},{4,0},{1,5},{5,1},{2,6},{6,2},{3,7},{7,3},{8,12},{12,8},{9,1... | collective-permute-start | bytes 2359304 | tf_op jit(solution)/shard_map/ppermute | solution.py:34

commit v13 on v11

--- a/solution.py
+++ b/solution.py
@@ -165,7 +165,8 @@
         out_ref[9 + k] = product(act, ext_ref[k : k + frames].reshape(frames * 4 * count, chan))
 
 
-def backward_kernel(place_ref, low_ref, inner_ref, outer_ref, act_ref, slope_ref, cot_ref, later_ref, turned_ref, sort_ref, pg_ref, ext_ref, out_ref):
+def backward_kernel(place_ref, low_ref, inner_ref, outer_ref, act_ref, slope_ref, cot_ref, later_ref, turned_ref, sort_ref,
+                    pg_ref, ext_ref, out_ref, box_ref):
     frames, _, count, chan = cot_ref.shape
     ext_ref[:frames] = cot_ref[...]
     for n in range(2):
@@ -175,6 +176,7 @@
         act_grad = product(jnp.concatenate(cots, axis=1), turned_ref[...])
         slope = slope_ref[frame].reshape(4 * count, chan)
         pg_ref[frame] = (act_grad * slope).astype(jnp.bfloat16).reshape(4, count, chan)
+        box_ref[frame] = sum(cot_ref[frame, side].astype(jnp.float32) for side in range(4))
     half_sums(place_ref, low_ref, inner_ref, outer_ref, act_ref, pg_ref, ext_ref, out_ref)
 
 
@@ -229,7 +231,7 @@
 
 
 def load_kernel(low_hbm, cot_hbm, ws_hbm, wt_hbm, sort_hbm,
-                low_ref, ws_ref, wt_ref, sort_ref, merge_ref, turned_ref, side_ref, cot_ref, wide_ref, sems):
+                low_ref, ws_ref, sort_ref, turned_ref, side_ref, cot_ref, wide_ref, wt_ref, sems):
     frames, cols_low, chan = low_ref.shape[0], low_ref.shape[2], low_ref.shape[3]
     pairs = [(sort_hbm, wide_ref)] + [(cot_hbm.at[n], cot_ref.at[n]) for n in range(frames)]
     pairs += [(wt_hbm.at[k], wt_ref.at[k]) for k in range(3)] + [(low_hbm, low_ref)]
@@ -239,7 +241,6 @@
         copy.start()
     copies[0].wait()
     sort_ref[...] = wide_ref[...].astype(jnp.bfloat16)
-    merge_ref[...] = wide_ref[...].T.astype(jnp.bfloat16)
     for n in range(frames):
         copies[1 + n].wait()
         sort_columns(cot_ref.at[n], side_ref.at[n], cols_low, sort_ref[...])
@@ -250,18 +251,17 @@
         copy.wait()
 
 
-def load(low, cot, ws, wt):
+def load(low, cot, ws, wt, sort):
     frames, rows_low, cols_low, chan = low.shape
-    sort = jnp.asarray(side_order(rows_low, cols_low))
     order = like(sort.shape, jnp.bfloat16)
-    shapes = [low, ws, wt, order, order, like((3 * chan, chan), wt.dtype),
+    shapes = [low, ws, order, like((3 * chan, chan), wt.dtype),
               like((frames, 4, rows_low * cols_low, chan), jnp.bfloat16)]
     return pl.pallas_call(
         load_kernel,
         in_specs=[UNREAD] * 5,
-        out_specs=[FULL] * 7,
+        out_specs=[FULL] * 5,
         out_shape=[like(a.shape, a.dtype) for a in shapes],
-        scratch_shapes=[pltpu.VMEM(cot.shape, cot.dtype), pltpu.VMEM(sort.shape, sort.dtype),
+        scratch_shapes=[pltpu.VMEM(cot.shape, cot.dtype), pltpu.VMEM(sort.shape, sort.dtype), pltpu.VMEM(wt.shape, wt.dtype),
                         pltpu.SemaphoreType.DMA((frames + 14,))],
         compiler_params=grant(14),
         cost_estimate=cost(2, 4),
@@ -309,13 +309,14 @@
 
 
 def backward(place, low, inner, outer, act, slope, cot, later, turned, sort):
-    frames, _, _, chan = act.shape
+    frames, _, count, chan = act.shape
     ext = (frames + 2,) + act.shape[1:]
     return pl.pallas_call(
         backward_kernel,
         in_specs=[SCALAR] + [FULL] * 9,
-        out_specs=[FULL] * 3,
-        out_shape=[like(act.shape, jnp.bfloat16), like(ext, jnp.bfloat16), like((12, chan // 2, chan), jnp.float32)],
+        out_specs=[FULL] * 4,
+        out_shape=[like(act.shape, jnp.bfloat16), like(ext, jnp.bfloat16), like((12, chan // 2, chan), jnp.float32),
+                   like((frames, count, chan), jnp.float32)],
         compiler_params=grant(24),
         cost_estimate=cost(15, 10),
         name="backward",
@@ -351,14 +352,13 @@
     return first + from_left(second, at)
 
 
-def input_kernel(pg_ref, ext_ref, ws_ref, _, out_ref):
+def input_kernel(pg_ref, box_ref, ws_ref, _, out_ref):
     frames, _, count, chan = pg_ref.shape
     cols_low = out_ref.shape[2]
     rows_low = count // cols_low
     at = column(count, cols_low, chan)
     turned = jnp.concatenate([ws_ref[i, j].T for j in range(3) for i in range(3)], axis=0)
     for frame in range(frames):
-        total = sum(ext_ref[frame, side].astype(jnp.float32) for side in range(4))
         own = [pg_ref[frame, side].astype(jnp.float32) for side in range(4)]
         zero = jnp.zeros((1, cols_low, chan), jnp.float32)
         parts = []
@@ -370,11 +370,11 @@
             for value in (odd + below, even + odd, above + even):
                 parts.append(jnp.concatenate(split(value.reshape(count, chan)), axis=0))
         sums = product(jnp.concatenate(parts, axis=1), turned)
-        total = total + (sums[:count] + sums[count:])
+        total = box_ref[frame] + (sums[:count] + sums[count:])
         out_ref[frame] = total.reshape(rows_low, cols_low, chan)
 
 
-def input_own(pg, ext, ws, before, low_shape):
+def input_own(pg, box, ws, before, low_shape):
     return pl.pallas_call(
         input_kernel,
         in_specs=[FULL] * 3 + [UNREAD],
@@ -383,38 +383,25 @@
         compiler_params=grant(16),
         cost_estimate=cost(6, 4),
         name="input_own",
-    )(pg, ext, ws, before)
-
-
-def finish_kernel(place_ref, edge_hbm, inner_hbm, outer_hbm, act_ref, low_ref, own_ref, ws_ref, wt_ref, merge_ref, _,
-                  section_ref, input_ref, token_ref, edge_ref, inner_ref, outer_ref, earlier, held, input_held, sems):
+    )(pg, box, ws, before)
+
+
+def finish_kernel(place_ref, own_ref, inner_hbm, outer_hbm, ws_hbm, edge_hbm, act_hbm, wt_hbm, sort_hbm, low_hbm, _,
+                  section_ref, input_ref, token_ref,
+                  inner_ref, outer_ref, ws_ref, edge_ref, act_ref, wt_ref, wide_ref, low_ref, earlier, held, input_held, sems):
     frames, rows_low, cols_low, chan = low_ref.shape
     group = rows_at_once(rows_low, cols_low)
     span, count = group * cols_low, rows_low * cols_low
-    arrivals = [pltpu.make_async_copy(a, b, sems.at[n]) for n, (a, b) in enumerate(
-        ((edge_hbm, edge_ref), (inner_hbm, inner_ref), (outer_hbm, outer_ref)))]
-    for copy in arrivals:
+    pairs = [(inner_hbm, inner_ref), (outer_hbm, outer_ref)]
+    pairs += [(ws_hbm.at[i, j], ws_ref.at[i, j]) for i in (2, 0, 1) for j in range(3)]
+    pairs += [(edge_hbm, edge_ref), (wt_hbm, wt_ref)]
+    pairs += [(act_hbm.at[n], act_ref.at[n]) for n in range(frames)] + [(sort_hbm, wide_ref), (low_hbm, low_ref)]
+    copies = [pltpu.make_async_copy(a, b, sems.at[n]) for n, (a, b) in enumerate(pairs)]
+    for copy in copies:
         copy.start()
     token_ref[...] = jnp.zeros_like(token_ref)
-    wt = wt_ref[...].reshape(3 * chan, chan)
-    leaving = []
-
-    def section_frame(frame):
-        acts = [act_ref[frame - k] if frame >= k else earlier[frame - k + 2] for k in range(3)]
-        acts = jnp.concatenate([act.reshape(4 * count, chan) for act in acts], axis=1)
-        low = low_ref[frame].reshape(1, count, chan).astype(jnp.float32)
-        mixed = (product(acts, wt).reshape(4, count, chan) + low).astype(jnp.bfloat16)
-        for n in range(rows_low // group):
-            block = mixed[:, n * span : (n + 1) * span].reshape(4 * span, chan)
-            block = product(merge_ref[...], block).astype(jnp.bfloat16)
-            held[frame, 2 * group * n : 2 * group * (n + 1)] = block.reshape(2 * group, 2 * cols_low, chan)
-        leaving.append(pltpu.make_async_copy(held.at[frame], section_ref.at[frame], sems.at[4 + frame]))
-        leaving[-1].start()
-
-    for frame in range(2, frames):
-        section_frame(frame)
-
-    for copy in arrivals[1:]:
+
+    for copy in copies[:8]:
         copy.wait()
     odd_place = place_ref[1] == 1
     flat = (frames * cols_low, chan)
@@ -438,35 +425,49 @@
         if row == rows_low - 1:
             value = value + terms[1]
         input_held[:, row] = value.astype(jnp.bfloat16)
-    leaving.append(pltpu.make_async_copy(input_held, input_ref, sems.at[3]))
-    leaving[-1].start()
-
-    arrivals[0].wait()
+    leaving = [pltpu.make_async_copy(input_held, input_ref, sems.at[len(copies)])]
+    leaving[0].start()
+
+    for copy in copies[8:12]:
+        copy.wait()
     for frame in range(2):
         for side, pre in enumerate(spatial(edge_ref[frame], ws_ref)):
             earlier[frame, side] = (pre * jax.nn.sigmoid(pre)).astype(jnp.bfloat16)
-    for frame in reversed(range(2)):
-        section_frame(frame)
+    for copy in copies[12:]:
+        copy.wait()
+    merge = wide_ref[...].T.astype(jnp.bfloat16)
+    wt = wt_ref[...].reshape(3 * chan, chan)
+    for frame in range(frames):
+        acts = [act_ref[frame - k] if frame >= k else earlier[frame - k + 2] for k in range(3)]
+        acts = jnp.concatenate([act.reshape(4 * count, chan) for act in acts], axis=1)
+        low = low_ref[frame].reshape(1, count, chan).astype(jnp.float32)
+        mixed = (product(acts, wt).reshape(4, count, chan) + low).astype(jnp.bfloat16)
+        for n in range(rows_low // group):
+            block = mixed[:, n * span : (n + 1) * span].reshape(4 * span, chan)
+            block = product(merge, block).astype(jnp.bfloat16)
+            held[frame, 2 * group * n : 2 * group * (n + 1)] = block.reshape(2 * group, 2 * cols_low, chan)
+        leaving.append(pltpu.make_async_copy(held.at[frame], section_ref.at[frame], sems.at[len(copies) + 1 + frame]))
+        leaving[-1].start()
     for copy in leaving:
         copy.wait()
 
 
-def finish(place, edge, inner, outer, act, low, own, ws, wt, merge, before):
+def finish(place, own, inner, outer, ws, edge, act, wt, sort, low, before):
     frames, rows_low, cols_low, chan = low.shape
     out = (frames, 2 * rows_low, 2 * cols_low, chan)
-    arrivals = [edge, inner, outer]
+    fetched = [inner, outer, ws, edge, act, wt, sort, low]
     return pl.pallas_call(
         finish_kernel,
-        in_specs=[SCALAR] + [HBM] * 3 + [FULL] * 6 + [UNREAD],
+        in_specs=[SCALAR, FULL] + [HBM] * 8 + [UNREAD],
         out_specs=[HBM, HBM, FULL],
         out_shape=[like(out, jnp.bfloat16), like(low.shape, jnp.bfloat16), TOKEN],
-        scratch_shapes=[pltpu.VMEM(a.shape, a.dtype) for a in arrivals]
+        scratch_shapes=[pltpu.VMEM(a.shape, a.dtype) for a in fetched]
         + [pltpu.VMEM((2,) + act.shape[1:], act.dtype), pltpu.VMEM(out, jnp.bfloat16),
-           pltpu.VMEM(low.shape, jnp.bfloat16), pltpu.SemaphoreType.DMA((4 + frames,))],
-        compiler_params=grant(14),
+           pltpu.VMEM(low.shape, jnp.bfloat16), pltpu.SemaphoreType.DMA((16 + 2 * frames,))],
+        compiler_params=grant(16),
         cost_estimate=cost(8, 4),
         name="finish",
-    )(place, *arrivals, act, low, own, ws, wt, merge, before)
+    )(place, own, inner, outer, in_hbm(ws), edge, *[in_hbm(a) for a in (act, wt, sort, low)], before)
 
 
 def put_kernel(place_ref, half_ref, *refs):
@@ -562,20 +563,23 @@
     inner, outer, later = first_messages(mine, low, cot)
     later = bits.shift(later, "tm", -1)
     inner, outer = bits.pairs(inner, outer)
-    low, ws, wt, sort, merge, turned, cot_side = load(low, cot, spatial_weight, temporal_weight)
-    act, slope = forward(mine, low, inner, outer, ws)
-    pg, ext, theirs = backward(other, low, inner, outer, act, slope, cot_side, later, turned, sort)
+    order = jnp.asarray(side_order(rows_low, cols_low))
+    low_in, ws, sort, turned, cot_side = load(low, cot, spatial_weight, temporal_weight, order)
+    act, slope = forward(mine, low_in, inner, outer, ws)
+    pg, ext, theirs, box = backward(
+        other, low_in, inner, outer, act, slope, cot_side, later, turned, sort
+    )
     theirs = bits.swap(theirs, bits.core)
-    own = half_grads(mine, low, inner, outer, act, pg, ext)
+    own = half_grads(mine, low_in, inner, outer, act, pg, ext)
     kept = add_halves(own, theirs)
     got = bits.exchange(kept.reshape(parts, -1, chan))
-    edge, pg_inner, pg_outer = edges(mine, low, inner, outer, pg, kept)
+    edge, pg_inner, pg_outer = edges(mine, low_in, inner, outer, pg, kept)
     edge = bits.shift(edge, "tm", 1)
     pg_inner, pg_outer = bits.pairs(pg_inner, pg_outer)
-    own_part = input_own(pg, ext, ws, kept, low.shape)
+    own_part = input_own(pg, box, ws, kept, low.shape)
     total, far = bits.far_sums(sum_parts(got, own_part))
     section_out, input_grad, done = finish(
-        mine, edge, pg_inner, pg_outer, act, low, own_part, ws, wt, merge, total
+        mine, own_part, pg_inner, pg_outer, spatial_weight, edge, act, temporal_weight, order, low, total
     )
     totals = spread(total, far, parts, done)
     half = bits.exchange(totals).reshape(kept.shape)

time: 70.2 us -> 70.1 us (level)
  local copies, waits for them, and re-layouts: 3.92 us -> 0.8 us
  Pallas kernels: 25.2 us -> 26.6 us
  waiting for transfers between devices: 6 us -> 6.76 us
    unnamed x14 -> x6, local copies, waits for them, and re-layouts: 3.92 us -> 0.8 us
    pallas_call x2, Pallas kernels: 7.84 us -> 9.02 us  [the longest x1 6.65 us: finish(): pl.pallas_call(finish_kernel, in_specs=[SCALAR, FULL] + [HBM] * 8 + [UNRE...]
    all_to_all x1, waiting for transfers between devices: 4.88 us -> 5.63 us  [exchange(): return lax.all_to_all(parts, tuple(self.near), 0, 0, tiled=True)]
  transfers between devices with their start and end apart: 10 -> 10, of which waited for: 3 -> 3; matrix products, arithmetic and copies ran while one was open for 0% -> 0% of each run, Pallas kernels for 25% -> 27%
where the time goes in v13:
time: 70.1 us; the launch traced here: 69.7 us
  Pallas kernels  26.6 us (38%)
  starting transfers between devices  20.9 us (30%)
  blocking collectives  13.5 us (19%)
  waiting for transfers between devices  6.76 us (10%)
  between operations  0.95 us (1%)
  local copies, waits for them, and re-layouts  0.8 us (1%)
    all_to_all x1, blocking collectives, exchange(): return lax.all_to_all(parts, tuple(self.near), 0, 0, tiled=True)  13.5 us
    ppermute x5, starting transfers between devices, swap(): return lax.ppermute(block, axis, [(0, 1), (1, 0)])  8.46 us
    all_to_all x1, starting transfers between devices, exchange(): return lax.all_to_all(parts, tuple(self.near), 0, 0, tiled=True)  6.74 us
    pallas_call x1, Pallas kernels, finish(): pl.pallas_call(finish_kernel, in_specs=[SCALAR, FULL] + [HBM] * 8 + [UNRE...  6.65 us
    all_to_all x1, waiting for transfers between devices, exchange(): return lax.all_to_all(parts, tuple(self.near), 0, 0, tiled=True)  5.63 us
    ppermute x2, starting transfers between devices, shift(): return lax.ppermute(block, axes, route)  3.71 us
    pallas_call x2, Pallas kernels, put(): pl.pallas_call(put_kernel, in_specs=[SCALAR, FULL] + [HBM] * len(done), o...  3.56 us
    pallas_call x1, Pallas kernels, backward(): pl.pallas_call(backward_kernel, in_specs=[SCALAR] + [FULL] * 9, out_specs...  3.41 us
  transfers between devices with their start and end apart: 10, of which 3 were waited for; matrix products, arithmetic and copies ran while one was open for 0% of the time, Pallas kernels for 27%

profile of v13, /device:TPU:0, one launch (start us, length us, event | category | flops | bytes accessed | tf_op | source)
XLA Modules:
  0.0 69.7 jit_solution(7964102306354843092)
XLA Ops:
  0.6 0.1 pad_add_fusion.place_ref
  0.7 1.7 %first_messages.1 = (bf16[4,1,32,256]{3,2,1,0:T(8,128)(2,1)S(1)}, bf16[4,1,32,256]{3,2,1,0:T(8,128)(2,1)S(1)}, bf16[2,8,64,256]{3,2,1,0:T(8,128)(2,1)S(1)}) custom-call(s32[2]{0:T(128)S(1)} %pad_add_fusion.place_ref, bf16[4,4,32,256]{3,2,1,0:T(8,128)(2,1)} %bitcast.13, bf16[4,8,64,256]{3,2,1,0:T(8,128)(2,1)} %bitcast.11), custom_call_target="tpu_custom_call" | custom-call | tf_op jit(solution)/shard_map/first_messages/pallas_call | solution.py:222
  2.5 1.3 %collective-permute-start.2 = (bf16[2,8,64,256]{3,2,1,0:T(8,128)(2,1)S(1)}, bf16[2,8,64,256]{3,2,1,0:T(8,128)(2,1)S(1)}, u32[]{:S(2)}, u32[]{:S(2)}) collective-permute-start(bf16[2,8,64,256]{3,2,1,0:T(8,128)(2,1)S(1)} %get-tuple-element.35), channel_id=1, source_target_pairs={{4,0},{8,4},{12,8},{5,1},{9,5},{13,9},{6,2},{10,6},{14,10},{7,3},{... | collective-permute-start | bytes 1572872 | tf_op jit(solution)/shard_map/ppermute | solution.py:40
  3.8 3.1 %collective-permute-start = (bf16[4,1,32,256]{3,2,1,0:T(8,128)(2,1)S(1)}, bf16[4,1,32,256]{3,2,1,0:T(8,128)(2,1)S(1)}, u32[]{:S(2)}, u32[]{:S(2)}) collective-permute-start(bf16[4,1,32,256]{3,2,1,0:T(8,128)(2,1)S(1)} %get-tuple-element.29), channel_id=1, source_target_pairs={{0,1},{1,0},{2,3},{3,2},{4,5},{5,4},{6,7},{7,6},{8,9},{9,8},{10,11... | collective-permute-start | bytes 196616 | tf_op jit(solution)/shard_map/ppermute | solution.py:34
  6.8 0.7 collective-permute-start.1
  7.5 0.1 pad_add_fusion.1.place_ref
  7.6 2.4 %load.1 = (bf16[4,4,32,256]{3,2,1,0:T(8,128)(2,1)S(1)}, bf16[3,3,256,256]{3,2,1,0:T(8,128)(2,1)S(1)}, bf16[256,256]{1,0:T(8,128)(2,1)S(1)}, bf16[768,256]{1,0:T(8,128)(2,1)S(1)}, bf16[4,4,128,256]{3,2,1,0:T(8,128)(2,1)S(1)}) custom-call(bf16[4,4,32,256]{3,2,1,0:T(8,128)(2,1)} %bitcast.14, bf16[4,8,64,256]{3,2,1,0:T(8,128)(2,1)} %bitcast.12, ...), custom_call_target="tpu_custom_call" | custom-call | flops 536870912 | bytes 4194304 | tf_op jit(solution)/shard_map/load/pallas_call | solution.py:259
  10.0 0.0 collective-permute-done.inner_ref
  10.0 0.0 collective-permute-done.1.outer_ref
  10.0 2.4 %forward.1 = (bf16[4,4,128,256]{3,2,1,0:T(8,128)(2,1)S(1)}, f32[4,4,128,256]{3,2,1,0:T(8,128)S(1)}) custom-call(s32[2]{0:T(128)S(1)} %pad_add_fusion.place_ref, bf16[4,4,32,256]{3,2,1,0:T(8,128)(2,1)S(1)} %get-tuple-element.28.low_ref, bf16[4,1,32,256]{3,2,1,0:T(8,128)(2,1)S(1)} %collective-permute-done.inner_ref, ...), custom_call_target="tpu_custom_call" | custom-call | flops 2684354560 | bytes 8388608 | tf_op jit(solution)/shard_map/forward/pallas_call | solution.py:275
  12.4 0.0 copy-start.2
  12.4 0.0 collective-permute-done.2.later_ref
  12.5 3.4 %backward.1 = (bf16[4,4,128,256]{3,2,1,0:T(8,128)(2,1)S(1)}, bf16[6,4,128,256]{3,2,1,0:T(8,128)(2,1)S(1)}, f32[12,128,256]{2,1,0:T(8,128)S(1)}, f32[4,128,256]{2,1,0:T(8,128)S(1)}) custom-call(s32[2]{0:T(128)S(1)} %pad_add_fusion.1.place_ref, bf16[4,4,32,256]{3,2,1,0:T(8,128)(2,1)S(1)} %get-tuple-element.28.low_ref, ...), custom_call_target="tpu_custom_call" | custom-call | flops 4026531840 | bytes 10485760 | tf_op jit(solution)/shard_map/backward/pallas_call | solution.py:314
  15.9 0.0 copy-start
  15.9 0.8 %copy-done = f32[4,128,256]{2,1,0:T(8,128)} copy-done((f32[4,128,256]{2,1,0:T(8,128)}, f32[4,128,256]{2,1,0:T(8,128)S(1)}, u32[]{:S(2)}) %copy-start) | copy-done | bytes 524312
  16.7 1.8 %collective-permute-start.3 = (f32[12,128,256]{2,1,0:T(8,128)S(1)}, f32[12,128,256]{2,1,0:T(8,128)S(1)}, u32[]{:S(2)}, u32[]{:S(2)}) collective-permute-start(f32[12,128,256]{2,1,0:T(8,128)S(1)} %get-tuple-element.41), channel_id=1, source_target_pairs={{0,4},{4,0},{1,5},{5,1},{2,6},{6,2},{3,7},{7,3},{8,12},{12,8},{9,1... | collective-permute-start | bytes 4718600 | tf_op jit(solution)/shard_map/ppermute | solution.py:34
  18.5 0.0 copy-done.2
  18.5 2.4 %half_grads.1.mine_ref = f32[12,128,256]{2,1,0:T(8,128)S(1)} custom-call(s32[2]{0:T(128)S(1)} %pad_add_fusion.place_ref, bf16[4,4,32,256]{3,2,1,0:T(8,128)(2,1)S(1)} %get-tuple-element.28.low_ref, bf16[4,1,32,256]{3,2,1,0:T(8,128)(2,1)S(1)} %collective-permute-done.inner_ref, bf16[4,1,32,256]{3,2,1,0:T(8,128)(2,1)S(1)} %collective-permute-done.1.outer_ref, ...), custom_call_target="tpu_custom_call" | custom-call | flops 2684354560 | bytes 6291456 | tf_op jit(solution)/shard_map/half_grads/pallas_call | solution.py:328
  20.9 0.6 collective-permute-done.3.theirs_ref
  21.5 1.0 %add_halves.1._ = bf16[12,128,256]{2,1,0:T(8,128)(2,1)} custom-call(f32[12,128,256]{2,1,0:T(8,128)S(1)} %half_grads.1.mine_ref, f32[12,128,256]{2,1,0:T(8,128)S(1)} %collective-permute-done.3.theirs_ref), custom_call_target="tpu_custom_call" | custom-call | tf_op jit(solution)/shard_map/add_halves/pallas_call | solution.py:510
  22.5 6.7 %all-to-all-start = ((bf16[8,192,256]{2,1,0:T(8,128)(2,1)}), bf16[8,192,256]{2,1,0:T(8,128)(2,1)S(1)}, u32[]{:S(2)}, u32[]{:S(2)}) async-start(bf16[8,192,256]{2,1,0:T(8,128)(2,1)} %bitcast.5), calls=%async_computation | async-start | bytes 1572864 | tf_op jit(solution)/shard_map/all_to_all | solution.py:43
  29.3 0.0 copy-start.1
  29.3 1.3 %edges.1 = (bf16[2,6,32,256]{3,2,1,0:T(8,128)(2,1)}, bf16[4,2,32,256]{3,2,1,0:T(8,128)(2,1)}, bf16[4,2,32,256]{3,2,1,0:T(8,128)(2,1)}) custom-call(s32[2]{0:T(128)S(1)} %pad_add_fusion.place_ref, bf16[4,4,32,256]{3,2,1,0:T(8,128)(2,1)S(1)} %get-tuple-element.28.low_ref, bf16[4,1,32,256]{3,2,1,0:T(8,128)(2,1)S(1)} %collective-permute-done.inner_ref, ...), custom_call_target="tpu_custom_call" | custom-call | tf_op jit(solution)/shard_map/edges/pallas_call | solution.py:301
  30.6 2.4 %collective-permute-start.6 = (bf16[2,6,32,256]{3,2,1,0:T(8,128)(2,1)}, bf16[2,6,32,256]{3,2,1,0:T(8,128)(2,1)}, u32[]{:S(2)}, u32[]{:S(2)}) collective-permute-start(bf16[2,6,32,256]{3,2,1,0:T(8,128)(2,1)} %get-tuple-element.44), channel_id=1, source_target_pairs={{0,4},{4,8},{8,12},{1,5},{5,9},{9,13},{2,6},{6,10},{10,14},{3,7},{... | collective-permute-start | bytes 589832 | tf_op jit(solution)/shard_map/ppermute | solution.py:40
  33.0 1.7 %collective-permute-start.4 = (bf16[4,2,32,256]{3,2,1,0:T(8,128)(2,1)}, bf16[4,2,32,256]{3,2,1,0:T(8,128)(2,1)}, u32[]{:S(2)}, u32[]{:S(2)}) collective-permute-start(bf16[4,2,32,256]{3,2,1,0:T(8,128)(2,1)} %get-tuple-element.42), channel_id=1, source_target_pairs={{0,1},{1,0},{2,3},{3,2},{4,5},{5,4},{6,7},{7,6},{8,9},{9,8},{10,11... | collective-permute-start | bytes 393224 | tf_op jit(solution)/shard_map/ppermute | solution.py:34
  34.8 1.3 %collective-permute-start.5 = (bf16[4,2,32,256]{3,2,1,0:T(8,128)(2,1)}, bf16[4,2,32,256]{3,2,1,0:T(8,128)(2,1)}, u32[]{:S(2)}, u32[]{:S(2)}) collective-permute-start(bf16[4,2,32,256]{3,2,1,0:T(8,128)(2,1)} %get-tuple-element.43), channel_id=1, source_target_pairs={{1,2},{2,1},{5,6},{6,5},{9,10},{10,9},{13,14},{14,13},{17,18},{18,... | collective-permute-start | bytes 393224 | tf_op jit(solution)/shard_map/ppermute | solution.py:49
  36.1 0.0 copy-done.1
  36.1 1.6 %input_own.1._.own_ref = f32[4,4,32,256]{3,2,1,0:T(8,128)S(1)} custom-call(bf16[4,4,128,256]{3,2,1,0:T(8,128)(2,1)S(1)} %get-tuple-element.38.pg_ref, f32[4,128,256]{2,1,0:T(8,128)S(1)} %copy-done.1, bf16[3,3,256,256]{3,2,1,0:T(8,128)(2,1)S(1)} %get-tuple-element.31.ws_ref, bf16[12,128,256]{2,1,0:T(8,128)(2,1)} %add_halves.1._), custom_call_target="tpu_custom_call" | custom-call | flops 1610612736 | bytes 4194304 | tf_op jit(solution)/shard_map/input_own/pallas_call | solution.py:378
  37.7 5.6 %all-to-all-done.got_ref = bf16[8,192,256]{2,1,0:T(8,128)(2,1)S(1)} async-done(((bf16[8,192,256]{2,1,0:T(8,128)(2,1)}), bf16[8,192,256]{2,1,0:T(8,128)(2,1)S(1)}, u32[]{:S(2)}, u32[]{:S(2)}) %all-to-all-start) | async-done | bytes 786464 | tf_op jit(solution)/shard_map/all_to_all | solution.py:43
  43.3 0.1 sum_parts.1._.own_ref
  43.4 1.8 %collective-permute-start.7 = (bf16[192,256]{1,0:T(8,128)(2,1)S(1)}, bf16[192,256]{1,0:T(8,128)(2,1)S(1)}, u32[]{:S(2)}, u32[]{:S(2)}) collective-permute-start(bf16[192,256]{1,0:T(8,128)(2,1)S(1)} %sum_parts.1._.own_ref), channel_id=1, source_target_pairs={{0,2},{2,0},{1,3},{3,1},{4,6},{6,4},{5,7},{7,5},{8,10},{10,8},{9,1... | collective-permute-start | bytes 294920 | tf_op jit(solution)/shard_map/ppermute | solution.py:34
  45.2 0.0 collective-permute-done.4.inner_hbm
  45.2 0.0 collective-permute-done.5.outer_hbm
  45.2 0.0 collective-permute-done.6.edge_hbm
  45.2 6.6 %finish.1 = (bf16[4,8,64,256]{3,2,1,0:T(8,128)(2,1)}, bf16[4,4,32,256]{3,2,1,0:T(8,128)(2,1)}, f32[8,128]{1,0:T(8,128)S(1)}) custom-call(s32[2]{0:T(128)S(1)} %pad_add_fusion.place_ref, f32[4,4,32,256]{3,2,1,0:T(8,128)S(1)} %input_own.1._.own_ref, bf16[4,2,32,256]{3,2,1,0:T(8,128)(2,1)} %collective-permute-done.4.inner_hbm, ...), custom_call_target="tpu_custom_call" | custom-call | flops 2147483648 | bytes 4194304 | tf_op jit(solution)/shard_map/finish/pallas_call | solution.py:459
  51.9 0.0 collective-permute-done.7.theirs_ref
  51.9 0.1 spread.1
  51.9 13.5 %all_to_all.10 = bf16[8,192,256]{2,1,0:T(8,128)(2,1)S(1)} all-to-all(bf16[8,192,256]{2,1,0:T(8,128)(2,1)S(1)} %spread.1), channel_id=1, replica_groups=mesh['dp0'=2,'tm1'=2,'tm0'=2,'height1'=2,'height0'=2] {'dp0','tm1','heig..., dimensions={0} | all-to-all | bytes 1572864 | tf_op jit(solution)/shard_map/all_to_all | solution.py:43
  65.5 0.0 collective-permute-start.8
  65.5 1.8 %put.2 = (f32[3,3,256,256]{3,2,1,0:T(8,128)}, f32[3,256,256]{2,1,0:T(8,128)}) custom-call(s32[2]{0:T(128)S(1)} %pad_add_fusion.place_ref, bf16[12,128,256]{2,1,0:T(8,128)(2,1)S(1)} %bitcast.10), custom_call_target="tpu_custom_call" | custom-call | tf_op jit(solution)/shard_map/put/pallas_call | solution.py:492
  67.3 0.5 collective-permute-done.8.half_ref
  67.8 1.8 %put.3 = (f32[3,3,256,256]{3,2,1,0:T(8,128)}, f32[3,256,256]{2,1,0:T(8,128)}) custom-call(s32[2]{0:T(128)S(1)} %pad_add_fusion.1.place_ref, bf16[12,128,256]{2,1,0:T(8,128)(2,1)S(1)} %collective-permute-done.8.half_ref, f32[3,3,256,256]{3,2,1,0:T(8,128)} %get-tuple-element.48.refs_0_, ...), custom_call_target="tpu_custom_call", output_to_operand_aliasing={{0}: (2, {}), {1}: (3, {})} | custom-call | tf_op jit(solution)/shard_map/put/pallas_call | solution.py:492
Async XLA Ops:
  2.5 10.0 %collective-permute-start.2 = (bf16[2,8,64,256]{3,2,1,0:T(8,128)(2,1)S(1)}, bf16[2,8,64,256]{3,2,1,0:T(8,128)(2,1)S(1)}, u32[]{:S(2)}, u32[]{:S(2)}) collective-permute-start(bf16[2,8,64,256]{3,2,1,0:T(8,128)(2,1)S(1)} %get-tuple-element.35), channel_id=1, source_target_pairs={{4,0},{8,4},{12,8},{5,1},{9,5},{13,9},{6,2},{10,6},{14,10},{7,3},{... | collective-permute-start | bytes 1572872 | tf_op jit(solution)/shard_map/ppermute | solution.py:40
  3.8 6.2 %collective-permute-start = (bf16[4,1,32,256]{3,2,1,0:T(8,128)(2,1)S(1)}, bf16[4,1,32,256]{3,2,1,0:T(8,128)(2,1)S(1)}, u32[]{:S(2)}, u32[]{:S(2)}) collective-permute-start(bf16[4,1,32,256]{3,2,1,0:T(8,128)(2,1)S(1)} %get-tuple-element.29), channel_id=1, source_target_pairs={{0,1},{1,0},{2,3},{3,2},{4,5},{5,4},{6,7},{7,6},{8,9},{9,8},{10,11... | collective-permute-start | bytes 196616 | tf_op jit(solution)/shard_map/ppermute | solution.py:34
  6.8 3.1 %collective-permute-start.1 = (bf16[4,1,32,256]{3,2,1,0:T(8,128)(2,1)S(1)}, bf16[4,1,32,256]{3,2,1,0:T(8,128)(2,1)S(1)}, u32[]{:S(2)}, u32[]{:S(2)}) collective-permute-start(bf16[4,1,32,256]{3,2,1,0:T(8,128)(2,1)S(1)} %get-tuple-element.30), channel_id=1, source_target_pairs={{1,2},{2,1},{5,6},{6,5},{9,10},{10,9},{13,14},{14,13},{17,18},{18,... | collective-permute-start | bytes 196616 | tf_op jit(solution)/shard_map/ppermute | solution.py:49
  12.4 6.1 %copy-start.2 = (bf16[4,4,128,256]{3,2,1,0:T(8,128)(2,1)}, bf16[4,4,128,256]{3,2,1,0:T(8,128)(2,1)S(1)}, u32[]{:S(2)}) copy-start(bf16[4,4,128,256]{3,2,1,0:T(8,128)(2,1)S(1)} %get-tuple-element.32.act_ref.act_hbm) | copy-start | bytes 3145732
  15.9 0.8 %copy-start = (f32[4,128,256]{2,1,0:T(8,128)}, f32[4,128,256]{2,1,0:T(8,128)S(1)}, u32[]{:S(2)}) copy-start(f32[4,128,256]{2,1,0:T(8,128)S(1)} %get-tuple-element.39.box_ref) | copy-start | bytes 1572868
  16.7 4.9 %collective-permute-start.3 = (f32[12,128,256]{2,1,0:T(8,128)S(1)}, f32[12,128,256]{2,1,0:T(8,128)S(1)}, u32[]{:S(2)}, u32[]{:S(2)}) collective-permute-start(f32[12,128,256]{2,1,0:T(8,128)S(1)} %get-tuple-element.41), channel_id=1, source_target_pairs={{0,4},{4,0},{1,5},{5,1},{2,6},{6,2},{3,7},{7,3},{8,12},{12,8},{9,1... | collective-permute-start | bytes 4718600 | tf_op jit(solution)/shard_map/ppermute | solution.py:34
  22.5 20.7 %all-to-all-start = ((bf16[8,192,256]{2,1,0:T(8,128)(2,1)}), bf16[8,192,256]{2,1,0:T(8,128)(2,1)S(1)}, u32[]{:S(2)}, u32[]{:S(2)}) async-start(bf16[8,192,256]{2,1,0:T(8,128)(2,1)} %bitcast.5), calls=%async_computation | async-start | bytes 1572864 | tf_op jit(solution)/shard_map/all_to_all | solution.py:43
  29.3 6.8 %copy-start.1 = (f32[4,128,256]{2,1,0:T(8,128)S(1)}, f32[4,128,256]{2,1,0:T(8,128)}, u32[]{:S(2)}) copy-start(f32[4,128,256]{2,1,0:T(8,128)} %copy-done) | copy-start | bytes 1572868
  30.6 14.6 %collective-permute-start.6 = (bf16[2,6,32,256]{3,2,1,0:T(8,128)(2,1)}, bf16[2,6,32,256]{3,2,1,0:T(8,128)(2,1)}, u32[]{:S(2)}, u32[]{:S(2)}) collective-permute-start(bf16[2,6,32,256]{3,2,1,0:T(8,128)(2,1)} %get-tuple-element.44), channel_id=1, source_target_pairs={{0,4},{4,8},{8,12},{1,5},{5,9},{9,13},{2,6},{6,10},{10,14},{3,7},{... | collective-permute-start | bytes 589832 | tf_op jit(solution)/shard_map/ppermute | solution.py:40
  33.0 12.2 %collective-permute-start.4 = (bf16[4,2,32,256]{3,2,1,0:T(8,128)(2,1)}, bf16[4,2,32,256]{3,2,1,0:T(8,128)(2,1)}, u32[]{:S(2)}, u32[]{:S(2)}) collective-permute-start(bf16[4,2,32,256]{3,2,1,0:T(8,128)(2,1)} %get-tuple-element.42), channel_id=1, source_target_pairs={{0,1},{1,0},{2,3},{3,2},{4,5},{5,4},{6,7},{7,6},{8,9},{9,8},{10,11... | collective-permute-start | bytes 393224 | tf_op jit(solution)/shard_map/ppermute | solution.py:34
  34.8 10.4 %collective-permute-start.5 = (bf16[4,2,32,256]{3,2,1,0:T(8,128)(2,1)}, bf16[4,2,32,256]{3,2,1,0:T(8,128)(2,1)}, u32[]{:S(2)}, u32[]{:S(2)}) collective-permute-start(bf16[4,2,32,256]{3,2,1,0:T(8,128)(2,1)} %get-tuple-element.43), channel_id=1, source_target_pairs={{1,2},{2,1},{5,6},{6,5},{9,10},{10,9},{13,14},{14,13},{17,18},{18,... | collective-permute-start | bytes 393224 | tf_op jit(solution)/shard_map/ppermute | solution.py:49
  43.4 8.5 %collective-permute-start.7 = (bf16[192,256]{1,0:T(8,128)(2,1)S(1)}, bf16[192,256]{1,0:T(8,128)(2,1)S(1)}, u32[]{:S(2)}, u32[]{:S(2)}) collective-permute-start(bf16[192,256]{1,0:T(8,128)(2,1)S(1)} %sum_parts.1._.own_ref), channel_id=1, source_target_pairs={{0,2},{2,0},{1,3},{3,1},{4,6},{6,4},{5,7},{7,5},{8,10},{10,8},{9,1... | collective-permute-start | bytes 294920 | tf_op jit(solution)/shard_map/ppermute | solution.py:34
  65.5 2.3 %collective-permute-start.8 = (bf16[12,128,256]{2,1,0:T(8,128)(2,1)S(1)}, bf16[12,128,256]{2,1,0:T(8,128)(2,1)S(1)}, u32[]{:S(2)}, u32[]{:S(2)}) collective-permute-start(bf16[12,128,256]{2,1,0:T(8,128)(2,1)S(1)} %bitcast.9), channel_id=1, source_target_pairs={{0,4},{4,0},{1,5},{5,1},{2,6},{6,2},{3,7},{7,3},{8,12},{12,8},{9,1... | collective-permute-start | bytes 2359304 | tf_op jit(solution)/shard_map/ppermute | solution.py:34

commit v14 on v13

--- a/solution.py
+++ b/solution.py
@@ -42,10 +42,13 @@
     def exchange(self, parts):
         return lax.all_to_all(parts, tuple(self.near), 0, 0, tiled=True)
 
-    def pairs(self, inner, outer):
+    def pairs(self, inner, outer, inner_made_first=False):
         axes = self.axes["height"]
         low = range(1, (1 << len(axes)) - 1, 2)
         route = [(i, i + 1) for i in low] + [(i + 1, i) for i in low]
+        if inner_made_first:
+            inner = self.swap(inner, axes[-1])
+            return inner, lax.ppermute(outer, axes, route)
         outer = lax.ppermute(outer, axes, route)
         return self.swap(inner, axes[-1]), outer
 
@@ -165,6 +168,13 @@
         out_ref[9 + k] = product(act, ext_ref[k : k + frames].reshape(frames * 4 * count, chan))
 
 
+def half_kernel(place_ref, low_ref, inner_ref, outer_ref, act_ref, pg_ref, ext_ref, out_ref, act_out, sem):
+    copy = pltpu.make_async_copy(act_ref, act_out, sem)
+    copy.start()
+    half_sums(place_ref, low_ref, inner_ref, outer_ref, act_ref, pg_ref, ext_ref, out_ref)
+    copy.wait()
+
+
 def backward_kernel(place_ref, low_ref, inner_ref, outer_ref, act_ref, slope_ref, cot_ref, later_ref, turned_ref, sort_ref,
                     pg_ref, ext_ref, out_ref, box_ref):
     frames, _, count, chan = cot_ref.shape
@@ -326,10 +336,11 @@
 def half_grads(place, low, inner, outer, act, pg, ext):
     chan = low.shape[-1]
     return pl.pallas_call(
-        half_sums,
+        half_kernel,
         in_specs=[SCALAR] + [FULL] * 6,
-        out_specs=FULL,
-        out_shape=like((12, chan // 2, chan), jnp.float32),
+        out_specs=[FULL, HBM],
+        out_shape=[like((12, chan // 2, chan), jnp.float32), like(act.shape, act.dtype)],
+        scratch_shapes=[pltpu.SemaphoreType.DMA],
         compiler_params=grant(20),
         cost_estimate=cost(10, 6),
         name="half_grads",
@@ -562,7 +573,7 @@
 
     inner, outer, later = first_messages(mine, low, cot)
     later = bits.shift(later, "tm", -1)
-    inner, outer = bits.pairs(inner, outer)
+    inner, outer = bits.pairs(inner, outer, True)
     order = jnp.asarray(side_order(rows_low, cols_low))
     low_in, ws, sort, turned, cot_side = load(low, cot, spatial_weight, temporal_weight, order)
     act, slope = forward(mine, low_in, inner, outer, ws)
@@ -570,7 +581,7 @@
         other, low_in, inner, outer, act, slope, cot_side, later, turned, sort
     )
     theirs = bits.swap(theirs, bits.core)
-    own = half_grads(mine, low_in, inner, outer, act, pg, ext)
+    own, act = half_grads(mine, low_in, inner, outer, act, pg, ext)
     kept = add_halves(own, theirs)
     got = bits.exchange(kept.reshape(parts, -1, chan))
     edge, pg_inner, pg_outer = edges(mine, low_in, inner, outer, pg, kept)

time: 70.1 us -> 70.1 us (level)
    ppermute x2 -> x1, starting transfers between devices: 1.96 us -> 1.32 us  [pairs(): outer = lax.ppermute(outer, axes, route)]
where the time goes in v14:
time: 70.1 us; the launch traced here: 69.7 us
  Pallas kernels  26.7 us (38%)
  starting transfers between devices  20.9 us (30%)
  blocking collectives  13.5 us (19%)
  waiting for transfers between devices  6.63 us (9%)
  between operations  0.95 us (1%)
  local copies, waits for them, and re-layouts  0.8 us (1%)
    all_to_all x1, blocking collectives, exchange(): return lax.all_to_all(parts, tuple(self.near), 0, 0, tiled=True)  13.5 us
    ppermute x5, starting transfers between devices, swap(): return lax.ppermute(block, axis, [(0, 1), (1, 0)])  8.47 us
    all_to_all x1, starting transfers between devices, exchange(): return lax.all_to_all(parts, tuple(self.near), 0, 0, tiled=True)  6.73 us
    pallas_call x1, Pallas kernels, finish(): pl.pallas_call(finish_kernel, in_specs=[SCALAR, FULL] + [HBM] * 8 + [UNRE...  6.65 us
    all_to_all x1, waiting for transfers between devices, exchange(): return lax.all_to_all(parts, tuple(self.near), 0, 0, tiled=True)  5.6 us
    ppermute x2, starting transfers between devices, shift(): return lax.ppermute(block, axes, route)  3.72 us
    pallas_call x2, Pallas kernels, put(): pl.pallas_call(put_kernel, in_specs=[SCALAR, FULL] + [HBM] * len(done), o...  3.56 us
    pallas_call x1, Pallas kernels, backward(): pl.pallas_call(backward_kernel, in_specs=[SCALAR] + [FULL] * 9, out_specs...  3.41 us
  transfers between devices with their start and end apart: 10, of which 3 were waited for; matrix products, arithmetic and copies ran while one was open for 0% of the time, Pallas kernels for 27%

profile of v14, /device:TPU:0, one launch (start us, length us, event | category | flops | bytes accessed | tf_op | source)
XLA Modules:
  0.0 69.7 jit_solution(17004478310194768162)
XLA Ops:
  0.6 0.1 pad_add_fusion.place_ref
  0.7 1.7 %first_messages.1 = (bf16[4,1,32,256]{3,2,1,0:T(8,128)(2,1)S(1)}, bf16[4,1,32,256]{3,2,1,0:T(8,128)(2,1)S(1)}, bf16[2,8,64,256]{3,2,1,0:T(8,128)(2,1)S(1)}) custom-call(s32[2]{0:T(128)S(1)} %pad_add_fusion.place_ref, bf16[4,4,32,256]{3,2,1,0:T(8,128)(2,1)} %bitcast.13, bf16[4,8,64,256]{3,2,1,0:T(8,128)(2,1)} %bitcast.11), custom_call_target="tpu_custom_call" | custom-call | tf_op jit(solution)/shard_map/first_messages/pallas_call | solution.py:232
  2.5 1.3 %collective-permute-start.2 = (bf16[2,8,64,256]{3,2,1,0:T(8,128)(2,1)S(1)}, bf16[2,8,64,256]{3,2,1,0:T(8,128)(2,1)S(1)}, u32[]{:S(2)}, u32[]{:S(2)}) collective-permute-start(bf16[2,8,64,256]{3,2,1,0:T(8,128)(2,1)S(1)} %get-tuple-element.37), channel_id=1, source_target_pairs={{4,0},{8,4},{12,8},{5,1},{9,5},{13,9},{6,2},{10,6},{14,10},{7,3},{... | collective-permute-start | bytes 1572872 | tf_op jit(solution)/shard_map/ppermute | solution.py:40
  3.8 3.1 %collective-permute-start = (bf16[4,1,32,256]{3,2,1,0:T(8,128)(2,1)S(1)}, bf16[4,1,32,256]{3,2,1,0:T(8,128)(2,1)S(1)}, u32[]{:S(2)}, u32[]{:S(2)}) collective-permute-start(bf16[4,1,32,256]{3,2,1,0:T(8,128)(2,1)S(1)} %get-tuple-element.31), channel_id=1, source_target_pairs={{0,1},{1,0},{2,3},{3,2},{4,5},{5,4},{6,7},{7,6},{8,9},{9,8},{10,11... | collective-permute-start | bytes 196616 | tf_op jit(solution)/shard_map/ppermute | solution.py:34
  6.8 0.7 collective-permute-start.1
  7.5 0.1 pad_add_fusion.1.place_ref
  7.6 2.4 %load.1 = (bf16[4,4,32,256]{3,2,1,0:T(8,128)(2,1)S(1)}, bf16[3,3,256,256]{3,2,1,0:T(8,128)(2,1)S(1)}, bf16[256,256]{1,0:T(8,128)(2,1)S(1)}, bf16[768,256]{1,0:T(8,128)(2,1)S(1)}, bf16[4,4,128,256]{3,2,1,0:T(8,128)(2,1)S(1)}) custom-call(bf16[4,4,32,256]{3,2,1,0:T(8,128)(2,1)} %bitcast.14, bf16[4,8,64,256]{3,2,1,0:T(8,128)(2,1)} %bitcast.12, ...), custom_call_target="tpu_custom_call" | custom-call | flops 536870912 | bytes 4194304 | tf_op jit(solution)/shard_map/load/pallas_call | solution.py:269
  10.0 0.0 collective-permute-done.inner_ref
  10.0 0.0 collective-permute-done.1.outer_ref
  10.0 2.4 %forward.1 = (bf16[4,4,128,256]{3,2,1,0:T(8,128)(2,1)S(1)}, f32[4,4,128,256]{3,2,1,0:T(8,128)S(1)}) custom-call(s32[2]{0:T(128)S(1)} %pad_add_fusion.place_ref, bf16[4,4,32,256]{3,2,1,0:T(8,128)(2,1)S(1)} %get-tuple-element.30.low_ref, bf16[4,1,32,256]{3,2,1,0:T(8,128)(2,1)S(1)} %collective-permute-done.inner_ref, ...), custom_call_target="tpu_custom_call" | custom-call | flops 2684354560 | bytes 8388608 | tf_op jit(solution)/shard_map/forward/pallas_call | solution.py:285
  12.4 0.0 collective-permute-done.2.later_ref
  12.4 3.4 %backward.1 = (bf16[4,4,128,256]{3,2,1,0:T(8,128)(2,1)S(1)}, bf16[6,4,128,256]{3,2,1,0:T(8,128)(2,1)S(1)}, f32[12,128,256]{2,1,0:T(8,128)S(1)}, f32[4,128,256]{2,1,0:T(8,128)S(1)}) custom-call(s32[2]{0:T(128)S(1)} %pad_add_fusion.1.place_ref, bf16[4,4,32,256]{3,2,1,0:T(8,128)(2,1)S(1)} %get-tuple-element.30.low_ref, ...), custom_call_target="tpu_custom_call" | custom-call | flops 4026531840 | bytes 10485760 | tf_op jit(solution)/shard_map/backward/pallas_call | solution.py:324
  15.9 0.0 copy-start
  15.9 0.8 %copy-done = f32[4,128,256]{2,1,0:T(8,128)} copy-done((f32[4,128,256]{2,1,0:T(8,128)}, f32[4,128,256]{2,1,0:T(8,128)S(1)}, u32[]{:S(2)}) %copy-start) | copy-done | bytes 524312
  16.7 1.8 %collective-permute-start.3 = (f32[12,128,256]{2,1,0:T(8,128)S(1)}, f32[12,128,256]{2,1,0:T(8,128)S(1)}, u32[]{:S(2)}, u32[]{:S(2)}) collective-permute-start(f32[12,128,256]{2,1,0:T(8,128)S(1)} %get-tuple-element.44), channel_id=1, source_target_pairs={{0,4},{4,0},{1,5},{5,1},{2,6},{6,2},{3,7},{7,3},{8,12},{12,8},{9,1... | collective-permute-start | bytes 4718600 | tf_op jit(solution)/shard_map/ppermute | solution.py:34
  18.5 2.5 %half_grads.1 = (f32[12,128,256]{2,1,0:T(8,128)S(1)}, bf16[4,4,128,256]{3,2,1,0:T(8,128)(2,1)S(1)}) custom-call(s32[2]{0:T(128)S(1)} %pad_add_fusion.place_ref, bf16[4,4,32,256]{3,2,1,0:T(8,128)(2,1)S(1)} %get-tuple-element.30.low_ref, bf16[4,1,32,256]{3,2,1,0:T(8,128)(2,1)S(1)} %collective-permute-done.inner_ref, ...), custom_call_target="tpu_custom_call" | custom-call | flops 2684354560 | bytes 6291456 | tf_op jit(solution)/shard_map/half_grads/pallas_call | solution.py:338
  21.0 0.0 copy-start.2
  21.0 0.5 collective-permute-done.3.theirs_ref
  21.5 1.0 %add_halves.1._ = bf16[12,128,256]{2,1,0:T(8,128)(2,1)} custom-call(f32[12,128,256]{2,1,0:T(8,128)S(1)} %get-tuple-element.43.mine_ref, f32[12,128,256]{2,1,0:T(8,128)S(1)} %collective-permute-done.3.theirs_ref), custom_call_target="tpu_custom_call" | custom-call | tf_op jit(solution)/shard_map/add_halves/pallas_call | solution.py:521
  22.5 0.0 copy-done.2
  22.5 6.7 %all-to-all-start = ((bf16[8,192,256]{2,1,0:T(8,128)(2,1)}), bf16[8,192,256]{2,1,0:T(8,128)(2,1)S(1)}, u32[]{:S(2)}, u32[]{:S(2)}) async-start(bf16[8,192,256]{2,1,0:T(8,128)(2,1)} %bitcast.5), calls=%async_computation | async-start | bytes 1572864 | tf_op jit(solution)/shard_map/all_to_all | solution.py:43
  29.3 0.0 copy-start.1
  29.3 1.3 %edges.1 = (bf16[2,6,32,256]{3,2,1,0:T(8,128)(2,1)}, bf16[4,2,32,256]{3,2,1,0:T(8,128)(2,1)}, bf16[4,2,32,256]{3,2,1,0:T(8,128)(2,1)}) custom-call(s32[2]{0:T(128)S(1)} %pad_add_fusion.place_ref, bf16[4,4,32,256]{3,2,1,0:T(8,128)(2,1)S(1)} %get-tuple-element.30.low_ref, bf16[4,1,32,256]{3,2,1,0:T(8,128)(2,1)S(1)} %collective-permute-done.inner_ref, ...), custom_call_target="tpu_custom_call" | custom-call | tf_op jit(solution)/shard_map/edges/pallas_call | solution.py:311
  30.6 2.4 %collective-permute-start.6 = (bf16[2,6,32,256]{3,2,1,0:T(8,128)(2,1)}, bf16[2,6,32,256]{3,2,1,0:T(8,128)(2,1)}, u32[]{:S(2)}, u32[]{:S(2)}) collective-permute-start(bf16[2,6,32,256]{3,2,1,0:T(8,128)(2,1)} %get-tuple-element.47), channel_id=1, source_target_pairs={{0,4},{4,8},{8,12},{1,5},{5,9},{9,13},{2,6},{6,10},{10,14},{3,7},{... | collective-permute-start | bytes 589832 | tf_op jit(solution)/shard_map/ppermute | solution.py:40
  33.0 1.7 %collective-permute-start.4 = (bf16[4,2,32,256]{3,2,1,0:T(8,128)(2,1)}, bf16[4,2,32,256]{3,2,1,0:T(8,128)(2,1)}, u32[]{:S(2)}, u32[]{:S(2)}) collective-permute-start(bf16[4,2,32,256]{3,2,1,0:T(8,128)(2,1)} %get-tuple-element.45), channel_id=1, source_target_pairs={{0,1},{1,0},{2,3},{3,2},{4,5},{5,4},{6,7},{7,6},{8,9},{9,8},{10,11... | collective-permute-start | bytes 393224 | tf_op jit(solution)/shard_map/ppermute | solution.py:34
  34.8 1.3 %collective-permute-start.5 = (bf16[4,2,32,256]{3,2,1,0:T(8,128)(2,1)}, bf16[4,2,32,256]{3,2,1,0:T(8,128)(2,1)}, u32[]{:S(2)}, u32[]{:S(2)}) collective-permute-start(bf16[4,2,32,256]{3,2,1,0:T(8,128)(2,1)} %get-tuple-element.46), channel_id=1, source_target_pairs={{1,2},{2,1},{5,6},{6,5},{9,10},{10,9},{13,14},{14,13},{17,18},{18,... | collective-permute-start | bytes 393224 | tf_op jit(solution)/shard_map/ppermute | solution.py:52
  36.1 0.0 copy-done.1
  36.1 1.6 %input_own.1._.own_ref = f32[4,4,32,256]{3,2,1,0:T(8,128)S(1)} custom-call(bf16[4,4,128,256]{3,2,1,0:T(8,128)(2,1)S(1)} %get-tuple-element.40.pg_ref, f32[4,128,256]{2,1,0:T(8,128)S(1)} %copy-done.1, bf16[3,3,256,256]{3,2,1,0:T(8,128)(2,1)S(1)} %get-tuple-element.33.ws_ref, bf16[12,128,256]{2,1,0:T(8,128)(2,1)} %add_halves.1._), custom_call_target="tpu_custom_call" | custom-call | flops 1610612736 | bytes 4194304 | tf_op jit(solution)/shard_map/input_own/pallas_call | solution.py:389
  37.7 5.6 %all-to-all-done.got_ref = bf16[8,192,256]{2,1,0:T(8,128)(2,1)S(1)} async-done(((bf16[8,192,256]{2,1,0:T(8,128)(2,1)}), bf16[8,192,256]{2,1,0:T(8,128)(2,1)S(1)}, u32[]{:S(2)}, u32[]{:S(2)}) %all-to-all-start) | async-done | bytes 786464 | tf_op jit(solution)/shard_map/all_to_all | solution.py:43
  43.3 0.1 sum_parts.1._.own_ref
  43.4 1.8 %collective-permute-start.7 = (bf16[192,256]{1,0:T(8,128)(2,1)S(1)}, bf16[192,256]{1,0:T(8,128)(2,1)S(1)}, u32[]{:S(2)}, u32[]{:S(2)}) collective-permute-start(bf16[192,256]{1,0:T(8,128)(2,1)S(1)} %sum_parts.1._.own_ref), channel_id=1, source_target_pairs={{0,2},{2,0},{1,3},{3,1},{4,6},{6,4},{5,7},{7,5},{8,10},{10,8},{9,1... | collective-permute-start | bytes 294920 | tf_op jit(solution)/shard_map/ppermute | solution.py:34
  45.2 0.0 collective-permute-done.4.inner_hbm
  45.2 0.0 collective-permute-done.5.outer_hbm
  45.2 0.0 collective-permute-done.6.edge_hbm
  45.2 6.7 %finish.1 = (bf16[4,8,64,256]{3,2,1,0:T(8,128)(2,1)}, bf16[4,4,32,256]{3,2,1,0:T(8,128)(2,1)}, f32[8,128]{1,0:T(8,128)S(1)}) custom-call(s32[2]{0:T(128)S(1)} %pad_add_fusion.place_ref, f32[4,4,32,256]{3,2,1,0:T(8,128)S(1)} %input_own.1._.own_ref, bf16[4,2,32,256]{3,2,1,0:T(8,128)(2,1)} %collective-permute-done.4.inner_hbm, ...), custom_call_target="tpu_custom_call" | custom-call | flops 2147483648 | bytes 4194304 | tf_op jit(solution)/shard_map/finish/pallas_call | solution.py:470
  51.9 0.0 collective-permute-done.7.theirs_ref
  51.9 0.1 spread.1
  51.9 13.5 %all_to_all.10 = bf16[8,192,256]{2,1,0:T(8,128)(2,1)S(1)} all-to-all(bf16[8,192,256]{2,1,0:T(8,128)(2,1)S(1)} %spread.1), channel_id=1, replica_groups=mesh['dp0'=2,'tm1'=2,'tm0'=2,'height1'=2,'height0'=2] {'dp0','tm1','heig..., dimensions={0} | all-to-all | bytes 1572864 | tf_op jit(solution)/shard_map/all_to_all | solution.py:43
  65.5 0.0 collective-permute-start.8
  65.5 1.8 %put.2 = (f32[3,3,256,256]{3,2,1,0:T(8,128)}, f32[3,256,256]{2,1,0:T(8,128)}) custom-call(s32[2]{0:T(128)S(1)} %pad_add_fusion.place_ref, bf16[12,128,256]{2,1,0:T(8,128)(2,1)S(1)} %bitcast.10), custom_call_target="tpu_custom_call" | custom-call | tf_op jit(solution)/shard_map/put/pallas_call | solution.py:503
  67.3 0.5 collective-permute-done.8.half_ref
  67.8 1.8 %put.3 = (f32[3,3,256,256]{3,2,1,0:T(8,128)}, f32[3,256,256]{2,1,0:T(8,128)}) custom-call(s32[2]{0:T(128)S(1)} %pad_add_fusion.1.place_ref, bf16[12,128,256]{2,1,0:T(8,128)(2,1)S(1)} %collective-permute-done.8.half_ref, f32[3,3,256,256]{3,2,1,0:T(8,128)} %get-tuple-element.52.refs_0_, ...), custom_call_target="tpu_custom_call", output_to_operand_aliasing={{0}: (2, {}), {1}: (3, {})} | custom-call | tf_op jit(solution)/shard_map/put/pallas_call | solution.py:503
Async XLA Ops:
  2.5 10.0 %collective-permute-start.2 = (bf16[2,8,64,256]{3,2,1,0:T(8,128)(2,1)S(1)}, bf16[2,8,64,256]{3,2,1,0:T(8,128)(2,1)S(1)}, u32[]{:S(2)}, u32[]{:S(2)}) collective-permute-start(bf16[2,8,64,256]{3,2,1,0:T(8,128)(2,1)S(1)} %get-tuple-element.37), channel_id=1, source_target_pairs={{4,0},{8,4},{12,8},{5,1},{9,5},{13,9},{6,2},{10,6},{14,10},{7,3},{... | collective-permute-start | bytes 1572872 | tf_op jit(solution)/shard_map/ppermute | solution.py:40
  3.8 6.2 %collective-permute-start = (bf16[4,1,32,256]{3,2,1,0:T(8,128)(2,1)S(1)}, bf16[4,1,32,256]{3,2,1,0:T(8,128)(2,1)S(1)}, u32[]{:S(2)}, u32[]{:S(2)}) collective-permute-start(bf16[4,1,32,256]{3,2,1,0:T(8,128)(2,1)S(1)} %get-tuple-element.31), channel_id=1, source_target_pairs={{0,1},{1,0},{2,3},{3,2},{4,5},{5,4},{6,7},{7,6},{8,9},{9,8},{10,11... | collective-permute-start | bytes 196616 | tf_op jit(solution)/shard_map/ppermute | solution.py:34
  6.8 3.1 %collective-permute-start.1 = (bf16[4,1,32,256]{3,2,1,0:T(8,128)(2,1)S(1)}, bf16[4,1,32,256]{3,2,1,0:T(8,128)(2,1)S(1)}, u32[]{:S(2)}, u32[]{:S(2)}) collective-permute-start(bf16[4,1,32,256]{3,2,1,0:T(8,128)(2,1)S(1)} %get-tuple-element.32), channel_id=1, source_target_pairs={{1,2},{2,1},{5,6},{6,5},{9,10},{10,9},{13,14},{14,13},{17,18},{18,... | collective-permute-start | bytes 196616 | tf_op jit(solution)/shard_map/ppermute | solution.py:51
  15.9 0.8 %copy-start = (f32[4,128,256]{2,1,0:T(8,128)}, f32[4,128,256]{2,1,0:T(8,128)S(1)}, u32[]{:S(2)}) copy-start(f32[4,128,256]{2,1,0:T(8,128)S(1)} %get-tuple-element.41.box_ref) | copy-start | bytes 1572868
  16.7 4.9 %collective-permute-start.3 = (f32[12,128,256]{2,1,0:T(8,128)S(1)}, f32[12,128,256]{2,1,0:T(8,128)S(1)}, u32[]{:S(2)}, u32[]{:S(2)}) collective-permute-start(f32[12,128,256]{2,1,0:T(8,128)S(1)} %get-tuple-element.44), channel_id=1, source_target_pairs={{0,4},{4,0},{1,5},{5,1},{2,6},{6,2},{3,7},{7,3},{8,12},{12,8},{9,1... | collective-permute-start | bytes 4718600 | tf_op jit(solution)/shard_map/ppermute | solution.py:34
  21.0 1.5 %copy-start.2 = (bf16[4,4,128,256]{3,2,1,0:T(8,128)(2,1)}, bf16[4,4,128,256]{3,2,1,0:T(8,128)(2,1)S(1)}, u32[]{:S(2)}) copy-start(bf16[4,4,128,256]{3,2,1,0:T(8,128)(2,1)S(1)} %get-tuple-element.48.act_hbm) | copy-start | bytes 3145732
  22.5 20.7 %all-to-all-start = ((bf16[8,192,256]{2,1,0:T(8,128)(2,1)}), bf16[8,192,256]{2,1,0:T(8,128)(2,1)S(1)}, u32[]{:S(2)}, u32[]{:S(2)}) async-start(bf16[8,192,256]{2,1,0:T(8,128)(2,1)} %bitcast.5), calls=%async_computation | async-start | bytes 1572864 | tf_op jit(solution)/shard_map/all_to_all | solution.py:43
  29.3 6.8 %copy-start.1 = (f32[4,128,256]{2,1,0:T(8,128)S(1)}, f32[4,128,256]{2,1,0:T(8,128)}, u32[]{:S(2)}) copy-start(f32[4,128,256]{2,1,0:T(8,128)} %copy-done) | copy-start | bytes 1572868
  30.6 14.6 %collective-permute-start.6 = (bf16[2,6,32,256]{3,2,1,0:T(8,128)(2,1)}, bf16[2,6,32,256]{3,2,1,0:T(8,128)(2,1)}, u32[]{:S(2)}, u32[]{:S(2)}) collective-permute-start(bf16[2,6,32,256]{3,2,1,0:T(8,128)(2,1)} %get-tuple-element.47), channel_id=1, source_target_pairs={{0,4},{4,8},{8,12},{1,5},{5,9},{9,13},{2,6},{6,10},{10,14},{3,7},{... | collective-permute-start | bytes 589832 | tf_op jit(solution)/shard_map/ppermute | solution.py:40
  33.0 12.2 %collective-permute-start.4 = (bf16[4,2,32,256]{3,2,1,0:T(8,128)(2,1)}, bf16[4,2,32,256]{3,2,1,0:T(8,128)(2,1)}, u32[]{:S(2)}, u32[]{:S(2)}) collective-permute-start(bf16[4,2,32,256]{3,2,1,0:T(8,128)(2,1)} %get-tuple-element.45), channel_id=1, source_target_pairs={{0,1},{1,0},{2,3},{3,2},{4,5},{5,4},{6,7},{7,6},{8,9},{9,8},{10,11... | collective-permute-start | bytes 393224 | tf_op jit(solution)/shard_map/ppermute | solution.py:34
  34.8 10.4 %collective-permute-start.5 = (bf16[4,2,32,256]{3,2,1,0:T(8,128)(2,1)}, bf16[4,2,32,256]{3,2,1,0:T(8,128)(2,1)}, u32[]{:S(2)}, u32[]{:S(2)}) collective-permute-start(bf16[4,2,32,256]{3,2,1,0:T(8,128)(2,1)} %get-tuple-element.46), channel_id=1, source_target_pairs={{1,2},{2,1},{5,6},{6,5},{9,10},{10,9},{13,14},{14,13},{17,18},{18,... | collective-permute-start | bytes 393224 | tf_op jit(solution)/shard_map/ppermute | solution.py:52
  43.4 8.5 %collective-permute-start.7 = (bf16[192,256]{1,0:T(8,128)(2,1)S(1)}, bf16[192,256]{1,0:T(8,128)(2,1)S(1)}, u32[]{:S(2)}, u32[]{:S(2)}) collective-permute-start(bf16[192,256]{1,0:T(8,128)(2,1)S(1)} %sum_parts.1._.own_ref), channel_id=1, source_target_pairs={{0,2},{2,0},{1,3},{3,1},{4,6},{6,4},{5,7},{7,5},{8,10},{10,8},{9,1... | collective-permute-start | bytes 294920 | tf_op jit(solution)/shard_map/ppermute | solution.py:34
  65.5 2.3 %collective-permute-start.8 = (bf16[12,128,256]{2,1,0:T(8,128)(2,1)S(1)}, bf16[12,128,256]{2,1,0:T(8,128)(2,1)S(1)}, u32[]{:S(2)}, u32[]{:S(2)}) collective-permute-start(bf16[12,128,256]{2,1,0:T(8,128)(2,1)S(1)} %bitcast.9), channel_id=1, source_target_pairs={{0,4},{4,0},{1,5},{5,1},{2,6},{6,2},{3,7},{7,3},{8,12},{12,8},{9,1... | collective-permute-start | bytes 2359304 | tf_op jit(solution)/shard_map/ppermute | solution.py:34

commit v15 on v14

--- a/solution.py
+++ b/solution.py
@@ -42,13 +42,10 @@
     def exchange(self, parts):
         return lax.all_to_all(parts, tuple(self.near), 0, 0, tiled=True)
 
-    def pairs(self, inner, outer, inner_made_first=False):
+    def pairs(self, inner, outer):
         axes = self.axes["height"]
         low = range(1, (1 << len(axes)) - 1, 2)
         route = [(i, i + 1) for i in low] + [(i + 1, i) for i in low]
-        if inner_made_first:
-            inner = self.swap(inner, axes[-1])
-            return inner, lax.ppermute(outer, axes, route)
         outer = lax.ppermute(outer, axes, route)
         return self.swap(inner, axes[-1]), outer
 
@@ -339,7 +336,7 @@
         half_kernel,
         in_specs=[SCALAR] + [FULL] * 6,
         out_specs=[FULL, HBM],
-        out_shape=[like((12, chan // 2, chan), jnp.float32), like(act.shape, act.dtype)],
+        out_shape=[like((12, chan // 2, chan), jnp.float32), pltpu.HBM(act.shape, act.dtype)],
         scratch_shapes=[pltpu.SemaphoreType.DMA],
         compiler_params=grant(20),
         cost_estimate=cost(10, 6),
@@ -397,14 +394,13 @@
     )(pg, box, ws, before)
 
 
-def finish_kernel(place_ref, own_ref, inner_hbm, outer_hbm, ws_hbm, edge_hbm, act_hbm, wt_hbm, sort_hbm, low_hbm, _,
+def finish_kernel(place_ref, own_ref, ws_ref, inner_hbm, outer_hbm, edge_hbm, act_hbm, wt_hbm, sort_hbm, low_hbm, _,
                   section_ref, input_ref, token_ref,
-                  inner_ref, outer_ref, ws_ref, edge_ref, act_ref, wt_ref, wide_ref, low_ref, earlier, held, input_held, sems):
+                  inner_ref, outer_ref, edge_ref, act_ref, wt_ref, wide_ref, low_ref, earlier, held, input_held, sems):
     frames, rows_low, cols_low, chan = low_ref.shape
     group = rows_at_once(rows_low, cols_low)
     span, count = group * cols_low, rows_low * cols_low
     pairs = [(inner_hbm, inner_ref), (outer_hbm, outer_ref)]
-    pairs += [(ws_hbm.at[i, j], ws_ref.at[i, j]) for i in (2, 0, 1) for j in range(3)]
     pairs += [(edge_hbm, edge_ref), (wt_hbm, wt_ref)]
     pairs += [(act_hbm.at[n], act_ref.at[n]) for n in range(frames)] + [(sort_hbm, wide_ref), (low_hbm, low_ref)]
     copies = [pltpu.make_async_copy(a, b, sems.at[n]) for n, (a, b) in enumerate(pairs)]
@@ -412,7 +408,7 @@
         copy.start()
     token_ref[...] = jnp.zeros_like(token_ref)
 
-    for copy in copies[:8]:
+    for copy in copies[:2]:
         copy.wait()
     odd_place = place_ref[1] == 1
     flat = (frames * cols_low, chan)
@@ -439,12 +435,12 @@
     leaving = [pltpu.make_async_copy(input_held, input_ref, sems.at[len(copies)])]
     leaving[0].start()
 
-    for copy in copies[8:12]:
+    for copy in copies[2:3]:
         copy.wait()
     for frame in range(2):
         for side, pre in enumerate(spatial(edge_ref[frame], ws_ref)):
             earlier[frame, side] = (pre * jax.nn.sigmoid(pre)).astype(jnp.bfloat16)
-    for copy in copies[12:]:
+    for copy in copies[3:]:
         copy.wait()
     merge = wide_ref[...].T.astype(jnp.bfloat16)
     wt = wt_ref[...].reshape(3 * chan, chan)
@@ -463,22 +459,22 @@
         copy.wait()
 
 
-def finish(place, own, inner, outer, ws, edge, act, wt, sort, low, before):
+def finish(place, own, ws, inner, outer, edge, act, wt, sort, low, before):
     frames, rows_low, cols_low, chan = low.shape
     out = (frames, 2 * rows_low, 2 * cols_low, chan)
-    fetched = [inner, outer, ws, edge, act, wt, sort, low]
+    fetched = [inner, outer, edge, act, wt, sort, low]
     return pl.pallas_call(
         finish_kernel,
-        in_specs=[SCALAR, FULL] + [HBM] * 8 + [UNREAD],
+        in_specs=[SCALAR, FULL, FULL] + [HBM] * 7 + [UNREAD],
         out_specs=[HBM, HBM, FULL],
         out_shape=[like(out, jnp.bfloat16), like(low.shape, jnp.bfloat16), TOKEN],
         scratch_shapes=[pltpu.VMEM(a.shape, a.dtype) for a in fetched]
         + [pltpu.VMEM((2,) + act.shape[1:], act.dtype), pltpu.VMEM(out, jnp.bfloat16),
-           pltpu.VMEM(low.shape, jnp.bfloat16), pltpu.SemaphoreType.DMA((16 + 2 * frames,))],
+           pltpu.VMEM(low.shape, jnp.bfloat16), pltpu.SemaphoreType.DMA((7 + 2 * frames,))],
         compiler_params=grant(16),
         cost_estimate=cost(8, 4),
         name="finish",
-    )(place, own, inner, outer, in_hbm(ws), edge, *[in_hbm(a) for a in (act, wt, sort, low)], before)
+    )(place, own, ws, inner, outer, edge, *[in_hbm(a) for a in (act, wt, sort, low)], before)
 
 
 def put_kernel(place_ref, half_ref, *refs):
@@ -573,7 +569,7 @@
 
     inner, outer, later = first_messages(mine, low, cot)
     later = bits.shift(later, "tm", -1)
-    inner, outer = bits.pairs(inner, outer, True)
+    inner, outer = bits.pairs(inner, outer)
     order = jnp.asarray(side_order(rows_low, cols_low))
     low_in, ws, sort, turned, cot_side = load(low, cot, spatial_weight, temporal_weight, order)
     act, slope = forward(mine, low_in, inner, outer, ws)
@@ -590,7 +586,7 @@
     own_part = input_own(pg, box, ws, kept, low.shape)
     total, far = bits.far_sums(sum_parts(got, own_part))
     section_out, input_grad, done = finish(
-        mine, own_part, pg_inner, pg_outer, spatial_weight, edge, act, temporal_weight, order, low, total
+        mine, own_part, ws, pg_inner, pg_outer, edge, act, temporal_weight, order, low, total
     )
     totals = spread(total, far, parts, done)
     half = bits.exchange(totals).reshape(kept.shape)

time: 70.1 us -> 69.8 us (level)
    ppermute x1 -> x2, starting transfers between devices: 1.32 us -> 1.96 us  [pairs(): outer = lax.ppermute(outer, axes, route)]
  transfers between devices with their start and end apart: 10 -> 10, of which waited for: 3 -> 3; matrix products, arithmetic and copies ran while one was open for 0% -> 0% of each run, Pallas kernels for 27% -> 26%
where the time goes in v15:
time: 69.8 us; the launch traced here: 69.4 us
  Pallas kernels  26.3 us (38%)
  starting transfers between devices  20.9 us (30%)
  blocking collectives  13.5 us (19%)
  waiting for transfers between devices  6.74 us (10%)
  between operations  0.95 us (1%)
  local copies, waits for them, and re-layouts  0.79 us (1%)
    all_to_all x1, blocking collectives, exchange(): return lax.all_to_all(parts, tuple(self.near), 0, 0, tiled=True)  13.5 us
    ppermute x5, starting transfers between devices, swap(): return lax.ppermute(block, axis, [(0, 1), (1, 0)])  8.47 us
    all_to_all x1, starting transfers between devices, exchange(): return lax.all_to_all(parts, tuple(self.near), 0, 0, tiled=True)  6.73 us
    pallas_call x1, Pallas kernels, finish(): pl.pallas_call(finish_kernel, in_specs=[SCALAR, FULL, FULL] + [HBM] * 7 +...  6.33 us
    all_to_all x1, waiting for transfers between devices, exchange(): return lax.all_to_all(parts, tuple(self.near), 0, 0, tiled=True)  5.62 us
    ppermute x2, starting transfers between devices, shift(): return lax.ppermute(block, axes, route)  3.71 us
    pallas_call x2, Pallas kernels, put(): pl.pallas_call(put_kernel, in_specs=[SCALAR, FULL] + [HBM] * len(done), o...  3.56 us
    pallas_call x1, Pallas kernels, backward(): pl.pallas_call(backward_kernel, in_specs=[SCALAR] + [FULL] * 9, out_specs...  3.41 us
  transfers between devices with their start and end apart: 10, of which 3 were waited for; matrix products, arithmetic and copies ran while one was open for 0% of the time, Pallas kernels for 26%

profile of v15, /device:TPU:0, one launch (start us, length us, event | category | flops | bytes accessed | tf_op | source)
XLA Modules:
  0.0 69.4 jit_solution(17141549903367616644)
XLA Ops:
  0.6 0.1 pad_add_fusion.place_ref
  0.7 1.7 %first_messages.1 = (bf16[4,1,32,256]{3,2,1,0:T(8,128)(2,1)S(1)}, bf16[4,1,32,256]{3,2,1,0:T(8,128)(2,1)S(1)}, bf16[2,8,64,256]{3,2,1,0:T(8,128)(2,1)S(1)}) custom-call(s32[2]{0:T(128)S(1)} %pad_add_fusion.place_ref, bf16[4,4,32,256]{3,2,1,0:T(8,128)(2,1)} %bitcast.13, bf16[4,8,64,256]{3,2,1,0:T(8,128)(2,1)} %bitcast.11), custom_call_target="tpu_custom_call" | custom-call | tf_op jit(solution)/shard_map/first_messages/pallas_call | solution.py:229
  2.5 1.3 %collective-permute-start.2 = (bf16[2,8,64,256]{3,2,1,0:T(8,128)(2,1)S(1)}, bf16[2,8,64,256]{3,2,1,0:T(8,128)(2,1)S(1)}, u32[]{:S(2)}, u32[]{:S(2)}) collective-permute-start(bf16[2,8,64,256]{3,2,1,0:T(8,128)(2,1)S(1)} %get-tuple-element.37), channel_id=1, source_target_pairs={{4,0},{8,4},{12,8},{5,1},{9,5},{13,9},{6,2},{10,6},{14,10},{7,3},{... | collective-permute-start | bytes 1572872 | tf_op jit(solution)/shard_map/ppermute | solution.py:40
  3.8 3.1 %collective-permute-start = (bf16[4,1,32,256]{3,2,1,0:T(8,128)(2,1)S(1)}, bf16[4,1,32,256]{3,2,1,0:T(8,128)(2,1)S(1)}, u32[]{:S(2)}, u32[]{:S(2)}) collective-permute-start(bf16[4,1,32,256]{3,2,1,0:T(8,128)(2,1)S(1)} %get-tuple-element.31), channel_id=1, source_target_pairs={{0,1},{1,0},{2,3},{3,2},{4,5},{5,4},{6,7},{7,6},{8,9},{9,8},{10,11... | collective-permute-start | bytes 196616 | tf_op jit(solution)/shard_map/ppermute | solution.py:34
  6.8 0.7 collective-permute-start.1
  7.5 0.1 pad_add_fusion.1.place_ref
  7.6 2.4 %load.1 = (bf16[4,4,32,256]{3,2,1,0:T(8,128)(2,1)S(1)}, bf16[3,3,256,256]{3,2,1,0:T(8,128)(2,1)S(1)}, bf16[256,256]{1,0:T(8,128)(2,1)S(1)}, bf16[768,256]{1,0:T(8,128)(2,1)S(1)}, bf16[4,4,128,256]{3,2,1,0:T(8,128)(2,1)S(1)}) custom-call(bf16[4,4,32,256]{3,2,1,0:T(8,128)(2,1)} %bitcast.14, bf16[4,8,64,256]{3,2,1,0:T(8,128)(2,1)} %bitcast.12, ...), custom_call_target="tpu_custom_call" | custom-call | flops 536870912 | bytes 4194304 | tf_op jit(solution)/shard_map/load/pallas_call | solution.py:266
  10.0 0.0 collective-permute-done.inner_ref
  10.0 0.0 collective-permute-done.1.outer_ref
  10.0 2.4 %forward.1 = (bf16[4,4,128,256]{3,2,1,0:T(8,128)(2,1)S(1)}, f32[4,4,128,256]{3,2,1,0:T(8,128)S(1)}) custom-call(s32[2]{0:T(128)S(1)} %pad_add_fusion.place_ref, bf16[4,4,32,256]{3,2,1,0:T(8,128)(2,1)S(1)} %get-tuple-element.30.low_ref, bf16[4,1,32,256]{3,2,1,0:T(8,128)(2,1)S(1)} %collective-permute-done.inner_ref, ...), custom_call_target="tpu_custom_call" | custom-call | flops 2684354560 | bytes 8388608 | tf_op jit(solution)/shard_map/forward/pallas_call | solution.py:282
  12.4 0.0 collective-permute-done.2.later_ref
  12.4 3.4 %backward.1 = (bf16[4,4,128,256]{3,2,1,0:T(8,128)(2,1)S(1)}, bf16[6,4,128,256]{3,2,1,0:T(8,128)(2,1)S(1)}, f32[12,128,256]{2,1,0:T(8,128)S(1)}, f32[4,128,256]{2,1,0:T(8,128)S(1)}) custom-call(s32[2]{0:T(128)S(1)} %pad_add_fusion.1.place_ref, bf16[4,4,32,256]{3,2,1,0:T(8,128)(2,1)S(1)} %get-tuple-element.30.low_ref, ...), custom_call_target="tpu_custom_call" | custom-call | flops 4026531840 | bytes 10485760 | tf_op jit(solution)/shard_map/backward/pallas_call | solution.py:321
  15.9 0.0 copy-start
  15.9 0.8 %copy-done = f32[4,128,256]{2,1,0:T(8,128)} copy-done((f32[4,128,256]{2,1,0:T(8,128)}, f32[4,128,256]{2,1,0:T(8,128)S(1)}, u32[]{:S(2)}) %copy-start) | copy-done | bytes 524312
  16.7 1.8 %collective-permute-start.3 = (f32[12,128,256]{2,1,0:T(8,128)S(1)}, f32[12,128,256]{2,1,0:T(8,128)S(1)}, u32[]{:S(2)}, u32[]{:S(2)}) collective-permute-start(f32[12,128,256]{2,1,0:T(8,128)S(1)} %get-tuple-element.44), channel_id=1, source_target_pairs={{0,4},{4,0},{1,5},{5,1},{2,6},{6,2},{3,7},{7,3},{8,12},{12,8},{9,1... | collective-permute-start | bytes 4718600 | tf_op jit(solution)/shard_map/ppermute | solution.py:34
  18.5 2.4 %half_grads.1 = (f32[12,128,256]{2,1,0:T(8,128)S(1)}, bf16[4,4,128,256]{3,2,1,0:T(8,128)(2,1)}) custom-call(s32[2]{0:T(128)S(1)} %pad_add_fusion.place_ref, bf16[4,4,32,256]{3,2,1,0:T(8,128)(2,1)S(1)} %get-tuple-element.30.low_ref, bf16[4,1,32,256]{3,2,1,0:T(8,128)(2,1)S(1)} %collective-permute-done.inner_ref, ...), custom_call_target="tpu_custom_call" | custom-call | flops 2684354560 | bytes 6291456 | tf_op jit(solution)/shard_map/half_grads/pallas_call | solution.py:335
  20.9 0.6 collective-permute-done.3.theirs_ref
  21.5 1.0 %add_halves.1._ = bf16[12,128,256]{2,1,0:T(8,128)(2,1)} custom-call(f32[12,128,256]{2,1,0:T(8,128)S(1)} %get-tuple-element.43.mine_ref, f32[12,128,256]{2,1,0:T(8,128)S(1)} %collective-permute-done.3.theirs_ref), custom_call_target="tpu_custom_call" | custom-call | tf_op jit(solution)/shard_map/add_halves/pallas_call | solution.py:517
  22.5 6.7 %all-to-all-start = ((bf16[8,192,256]{2,1,0:T(8,128)(2,1)}), bf16[8,192,256]{2,1,0:T(8,128)(2,1)S(1)}, u32[]{:S(2)}, u32[]{:S(2)}) async-start(bf16[8,192,256]{2,1,0:T(8,128)(2,1)} %bitcast.5), calls=%async_computation | async-start | bytes 1572864 | tf_op jit(solution)/shard_map/all_to_all | solution.py:43
  29.3 0.0 copy-start.1
  29.3 1.3 %edges.1 = (bf16[2,6,32,256]{3,2,1,0:T(8,128)(2,1)}, bf16[4,2,32,256]{3,2,1,0:T(8,128)(2,1)}, bf16[4,2,32,256]{3,2,1,0:T(8,128)(2,1)}) custom-call(s32[2]{0:T(128)S(1)} %pad_add_fusion.place_ref, bf16[4,4,32,256]{3,2,1,0:T(8,128)(2,1)S(1)} %get-tuple-element.30.low_ref, bf16[4,1,32,256]{3,2,1,0:T(8,128)(2,1)S(1)} %collective-permute-done.inner_ref, ...), custom_call_target="tpu_custom_call" | custom-call | tf_op jit(solution)/shard_map/edges/pallas_call | solution.py:308
  30.6 2.4 %collective-permute-start.6 = (bf16[2,6,32,256]{3,2,1,0:T(8,128)(2,1)}, bf16[2,6,32,256]{3,2,1,0:T(8,128)(2,1)}, u32[]{:S(2)}, u32[]{:S(2)}) collective-permute-start(bf16[2,6,32,256]{3,2,1,0:T(8,128)(2,1)} %get-tuple-element.47), channel_id=1, source_target_pairs={{0,4},{4,8},{8,12},{1,5},{5,9},{9,13},{2,6},{6,10},{10,14},{3,7},{... | collective-permute-start | bytes 589832 | tf_op jit(solution)/shard_map/ppermute | solution.py:40
  33.0 1.7 %collective-permute-start.4 = (bf16[4,2,32,256]{3,2,1,0:T(8,128)(2,1)}, bf16[4,2,32,256]{3,2,1,0:T(8,128)(2,1)}, u32[]{:S(2)}, u32[]{:S(2)}) collective-permute-start(bf16[4,2,32,256]{3,2,1,0:T(8,128)(2,1)} %get-tuple-element.45), channel_id=1, source_target_pairs={{0,1},{1,0},{2,3},{3,2},{4,5},{5,4},{6,7},{7,6},{8,9},{9,8},{10,11... | collective-permute-start | bytes 393224 | tf_op jit(solution)/shard_map/ppermute | solution.py:34
  34.8 1.3 %collective-permute-start.5 = (bf16[4,2,32,256]{3,2,1,0:T(8,128)(2,1)}, bf16[4,2,32,256]{3,2,1,0:T(8,128)(2,1)}, u32[]{:S(2)}, u32[]{:S(2)}) collective-permute-start(bf16[4,2,32,256]{3,2,1,0:T(8,128)(2,1)} %get-tuple-element.46), channel_id=1, source_target_pairs={{1,2},{2,1},{5,6},{6,5},{9,10},{10,9},{13,14},{14,13},{17,18},{18,... | collective-permute-start | bytes 393224 | tf_op jit(solution)/shard_map/ppermute | solution.py:49
  36.1 0.0 copy-done.1
  36.1 1.6 %input_own.1._.own_ref = f32[4,4,32,256]{3,2,1,0:T(8,128)S(1)} custom-call(bf16[4,4,128,256]{3,2,1,0:T(8,128)(2,1)S(1)} %get-tuple-element.40.pg_ref, f32[4,128,256]{2,1,0:T(8,128)S(1)} %copy-done.1, bf16[3,3,256,256]{3,2,1,0:T(8,128)(2,1)S(1)} %get-tuple-element.33.ws_ref, bf16[12,128,256]{2,1,0:T(8,128)(2,1)} %add_halves.1._), custom_call_target="tpu_custom_call" | custom-call | flops 1610612736 | bytes 4194304 | tf_op jit(solution)/shard_map/input_own/pallas_call | solution.py:386
  37.6 5.6 %all-to-all-done.got_ref = bf16[8,192,256]{2,1,0:T(8,128)(2,1)S(1)} async-done(((bf16[8,192,256]{2,1,0:T(8,128)(2,1)}), bf16[8,192,256]{2,1,0:T(8,128)(2,1)S(1)}, u32[]{:S(2)}, u32[]{:S(2)}) %all-to-all-start) | async-done | bytes 786464 | tf_op jit(solution)/shard_map/all_to_all | solution.py:43
  43.3 0.1 sum_parts.1._.own_ref
  43.4 1.8 %collective-permute-start.7 = (bf16[192,256]{1,0:T(8,128)(2,1)S(1)}, bf16[192,256]{1,0:T(8,128)(2,1)S(1)}, u32[]{:S(2)}, u32[]{:S(2)}) collective-permute-start(bf16[192,256]{1,0:T(8,128)(2,1)S(1)} %sum_parts.1._.own_ref), channel_id=1, source_target_pairs={{0,2},{2,0},{1,3},{3,1},{4,6},{6,4},{5,7},{7,5},{8,10},{10,8},{9,1... | collective-permute-start | bytes 294920 | tf_op jit(solution)/shard_map/ppermute | solution.py:34
  45.2 0.0 collective-permute-done.4.inner_hbm
  45.2 0.0 collective-permute-done.5.outer_hbm
  45.2 0.0 collective-permute-done.6.edge_hbm
  45.2 6.3 %finish.1 = (bf16[4,8,64,256]{3,2,1,0:T(8,128)(2,1)}, bf16[4,4,32,256]{3,2,1,0:T(8,128)(2,1)}, f32[8,128]{1,0:T(8,128)S(1)}) custom-call(s32[2]{0:T(128)S(1)} %pad_add_fusion.place_ref, f32[4,4,32,256]{3,2,1,0:T(8,128)S(1)} %input_own.1._.own_ref, bf16[3,3,256,256]{3,2,1,0:T(8,128)(2,1)S(1)} %get-tuple-element.33.ws_ref, ...), custom_call_target="tpu_custom_call" | custom-call | flops 2147483648 | bytes 4194304 | tf_op jit(solution)/shard_map/finish/pallas_call | solution.py:466
  51.5 0.0 collective-permute-done.7.theirs_ref
  51.6 0.1 spread.1
  51.6 13.5 %all_to_all.10 = bf16[8,192,256]{2,1,0:T(8,128)(2,1)S(1)} all-to-all(bf16[8,192,256]{2,1,0:T(8,128)(2,1)S(1)} %spread.1), channel_id=1, replica_groups=mesh['dp0'=2,'tm1'=2,'tm0'=2,'height1'=2,'height0'=2] {'dp0','tm1','heig..., dimensions={0} | all-to-all | bytes 1572864 | tf_op jit(solution)/shard_map/all_to_all | solution.py:43
  65.2 0.0 collective-permute-start.8
  65.2 1.8 %put.2 = (f32[3,3,256,256]{3,2,1,0:T(8,128)}, f32[3,256,256]{2,1,0:T(8,128)}) custom-call(s32[2]{0:T(128)S(1)} %pad_add_fusion.place_ref, bf16[12,128,256]{2,1,0:T(8,128)(2,1)S(1)} %bitcast.10), custom_call_target="tpu_custom_call" | custom-call | tf_op jit(solution)/shard_map/put/pallas_call | solution.py:499
  66.9 0.5 collective-permute-done.8.half_ref
  67.4 1.8 %put.3 = (f32[3,3,256,256]{3,2,1,0:T(8,128)}, f32[3,256,256]{2,1,0:T(8,128)}) custom-call(s32[2]{0:T(128)S(1)} %pad_add_fusion.1.place_ref, bf16[12,128,256]{2,1,0:T(8,128)(2,1)S(1)} %collective-permute-done.8.half_ref, f32[3,3,256,256]{3,2,1,0:T(8,128)} %get-tuple-element.52.refs_0_, ...), custom_call_target="tpu_custom_call", output_to_operand_aliasing={{0}: (2, {}), {1}: (3, {})} | custom-call | tf_op jit(solution)/shard_map/put/pallas_call | solution.py:499
Async XLA Ops:
  2.5 10.0 %collective-permute-start.2 = (bf16[2,8,64,256]{3,2,1,0:T(8,128)(2,1)S(1)}, bf16[2,8,64,256]{3,2,1,0:T(8,128)(2,1)S(1)}, u32[]{:S(2)}, u32[]{:S(2)}) collective-permute-start(bf16[2,8,64,256]{3,2,1,0:T(8,128)(2,1)S(1)} %get-tuple-element.37), channel_id=1, source_target_pairs={{4,0},{8,4},{12,8},{5,1},{9,5},{13,9},{6,2},{10,6},{14,10},{7,3},{... | collective-permute-start | bytes 1572872 | tf_op jit(solution)/shard_map/ppermute | solution.py:40
  3.8 6.2 %collective-permute-start = (bf16[4,1,32,256]{3,2,1,0:T(8,128)(2,1)S(1)}, bf16[4,1,32,256]{3,2,1,0:T(8,128)(2,1)S(1)}, u32[]{:S(2)}, u32[]{:S(2)}) collective-permute-start(bf16[4,1,32,256]{3,2,1,0:T(8,128)(2,1)S(1)} %get-tuple-element.31), channel_id=1, source_target_pairs={{0,1},{1,0},{2,3},{3,2},{4,5},{5,4},{6,7},{7,6},{8,9},{9,8},{10,11... | collective-permute-start | bytes 196616 | tf_op jit(solution)/shard_map/ppermute | solution.py:34
  6.8 3.1 %collective-permute-start.1 = (bf16[4,1,32,256]{3,2,1,0:T(8,128)(2,1)S(1)}, bf16[4,1,32,256]{3,2,1,0:T(8,128)(2,1)S(1)}, u32[]{:S(2)}, u32[]{:S(2)}) collective-permute-start(bf16[4,1,32,256]{3,2,1,0:T(8,128)(2,1)S(1)} %get-tuple-element.32), channel_id=1, source_target_pairs={{1,2},{2,1},{5,6},{6,5},{9,10},{10,9},{13,14},{14,13},{17,18},{18,... | collective-permute-start | bytes 196616 | tf_op jit(solution)/shard_map/ppermute | solution.py:49
  15.9 0.8 %copy-start = (f32[4,128,256]{2,1,0:T(8,128)}, f32[4,128,256]{2,1,0:T(8,128)S(1)}, u32[]{:S(2)}) copy-start(f32[4,128,256]{2,1,0:T(8,128)S(1)} %get-tuple-element.41.box_ref) | copy-start | bytes 1572868
  16.7 4.9 %collective-permute-start.3 = (f32[12,128,256]{2,1,0:T(8,128)S(1)}, f32[12,128,256]{2,1,0:T(8,128)S(1)}, u32[]{:S(2)}, u32[]{:S(2)}) collective-permute-start(f32[12,128,256]{2,1,0:T(8,128)S(1)} %get-tuple-element.44), channel_id=1, source_target_pairs={{0,4},{4,0},{1,5},{5,1},{2,6},{6,2},{3,7},{7,3},{8,12},{12,8},{9,1... | collective-permute-start | bytes 4718600 | tf_op jit(solution)/shard_map/ppermute | solution.py:34
  22.5 20.7 %all-to-all-start = ((bf16[8,192,256]{2,1,0:T(8,128)(2,1)}), bf16[8,192,256]{2,1,0:T(8,128)(2,1)S(1)}, u32[]{:S(2)}, u32[]{:S(2)}) async-start(bf16[8,192,256]{2,1,0:T(8,128)(2,1)} %bitcast.5), calls=%async_computation | async-start | bytes 1572864 | tf_op jit(solution)/shard_map/all_to_all | solution.py:43
  29.3 6.8 %copy-start.1 = (f32[4,128,256]{2,1,0:T(8,128)S(1)}, f32[4,128,256]{2,1,0:T(8,128)}, u32[]{:S(2)}) copy-start(f32[4,128,256]{2,1,0:T(8,128)} %copy-done) | copy-start | bytes 1572868
  30.6 14.6 %collective-permute-start.6 = (bf16[2,6,32,256]{3,2,1,0:T(8,128)(2,1)}, bf16[2,6,32,256]{3,2,1,0:T(8,128)(2,1)}, u32[]{:S(2)}, u32[]{:S(2)}) collective-permute-start(bf16[2,6,32,256]{3,2,1,0:T(8,128)(2,1)} %get-tuple-element.47), channel_id=1, source_target_pairs={{0,4},{4,8},{8,12},{1,5},{5,9},{9,13},{2,6},{6,10},{10,14},{3,7},{... | collective-permute-start | bytes 589832 | tf_op jit(solution)/shard_map/ppermute | solution.py:40
  33.0 12.2 %collective-permute-start.4 = (bf16[4,2,32,256]{3,2,1,0:T(8,128)(2,1)}, bf16[4,2,32,256]{3,2,1,0:T(8,128)(2,1)}, u32[]{:S(2)}, u32[]{:S(2)}) collective-permute-start(bf16[4,2,32,256]{3,2,1,0:T(8,128)(2,1)} %get-tuple-element.45), channel_id=1, source_target_pairs={{0,1},{1,0},{2,3},{3,2},{4,5},{5,4},{6,7},{7,6},{8,9},{9,8},{10,11... | collective-permute-start | bytes 393224 | tf_op jit(solution)/shard_map/ppermute | solution.py:34
  34.8 10.4 %collective-permute-start.5 = (bf16[4,2,32,256]{3,2,1,0:T(8,128)(2,1)}, bf16[4,2,32,256]{3,2,1,0:T(8,128)(2,1)}, u32[]{:S(2)}, u32[]{:S(2)}) collective-permute-start(bf16[4,2,32,256]{3,2,1,0:T(8,128)(2,1)} %get-tuple-element.46), channel_id=1, source_target_pairs={{1,2},{2,1},{5,6},{6,5},{9,10},{10,9},{13,14},{14,13},{17,18},{18,... | collective-permute-start | bytes 393224 | tf_op jit(solution)/shard_map/ppermute | solution.py:49
  43.4 8.2 %collective-permute-start.7 = (bf16[192,256]{1,0:T(8,128)(2,1)S(1)}, bf16[192,256]{1,0:T(8,128)(2,1)S(1)}, u32[]{:S(2)}, u32[]{:S(2)}) collective-permute-start(bf16[192,256]{1,0:T(8,128)(2,1)S(1)} %sum_parts.1._.own_ref), channel_id=1, source_target_pairs={{0,2},{2,0},{1,3},{3,1},{4,6},{6,4},{5,7},{7,5},{8,10},{10,8},{9,1... | collective-permute-start | bytes 294920 | tf_op jit(solution)/shard_map/ppermute | solution.py:34
  65.2 2.3 %collective-permute-start.8 = (bf16[12,128,256]{2,1,0:T(8,128)(2,1)S(1)}, bf16[12,128,256]{2,1,0:T(8,128)(2,1)S(1)}, u32[]{:S(2)}, u32[]{:S(2)}) collective-permute-start(bf16[12,128,256]{2,1,0:T(8,128)(2,1)S(1)} %bitcast.9), channel_id=1, source_target_pairs={{0,4},{4,0},{1,5},{5,1},{2,6},{6,2},{3,7},{7,3},{8,12},{12,8},{9,1... | collective-permute-start | bytes 2359304 | tf_op jit(solution)/shard_map/ppermute | solution.py:34

commit v16 on v15

--- a/solution.py
+++ b/solution.py
@@ -165,15 +165,19 @@
         out_ref[9 + k] = product(act, ext_ref[k : k + frames].reshape(frames * 4 * count, chan))
 
 
-def half_kernel(place_ref, low_ref, inner_ref, outer_ref, act_ref, pg_ref, ext_ref, out_ref, act_out, sem):
-    copy = pltpu.make_async_copy(act_ref, act_out, sem)
-    copy.start()
+def half_kernel(place_ref, low_ref, inner_ref, outer_ref, act_ref, pg_ref, ext_ref, out_ref, act_out, box_out, box_ref, sems):
+    copies = [pltpu.make_async_copy(act_ref, act_out, sems.at[0]), pltpu.make_async_copy(box_ref, box_out, sems.at[1])]
+    copies[0].start()
+    for frame in range(box_ref.shape[0]):
+        box_ref[frame] = sum(ext_ref[frame, side].astype(jnp.float32) for side in range(4))
+    copies[1].start()
     half_sums(place_ref, low_ref, inner_ref, outer_ref, act_ref, pg_ref, ext_ref, out_ref)
-    copy.wait()
+    for copy in copies:
+        copy.wait()
 
 
 def backward_kernel(place_ref, low_ref, inner_ref, outer_ref, act_ref, slope_ref, cot_ref, later_ref, turned_ref, sort_ref,
-                    pg_ref, ext_ref, out_ref, box_ref):
+                    pg_ref, ext_ref, out_ref):
     frames, _, count, chan = cot_ref.shape
     ext_ref[:frames] = cot_ref[...]
     for n in range(2):
@@ -183,7 +187,6 @@
         act_grad = product(jnp.concatenate(cots, axis=1), turned_ref[...])
         slope = slope_ref[frame].reshape(4 * count, chan)
         pg_ref[frame] = (act_grad * slope).astype(jnp.bfloat16).reshape(4, count, chan)
-        box_ref[frame] = sum(cot_ref[frame, side].astype(jnp.float32) for side in range(4))
     half_sums(place_ref, low_ref, inner_ref, outer_ref, act_ref, pg_ref, ext_ref, out_ref)
 
 
@@ -238,7 +241,7 @@
 
 
 def load_kernel(low_hbm, cot_hbm, ws_hbm, wt_hbm, sort_hbm,
-                low_ref, ws_ref, sort_ref, turned_ref, side_ref, cot_ref, wide_ref, wt_ref, sems):
+                low_ref, ws_ref, wt_ref, sort_ref, turned_ref, side_ref, cot_ref, wide_ref, sems):
     frames, cols_low, chan = low_ref.shape[0], low_ref.shape[2], low_ref.shape[3]
     pairs = [(sort_hbm, wide_ref)] + [(cot_hbm.at[n], cot_ref.at[n]) for n in range(frames)]
     pairs += [(wt_hbm.at[k], wt_ref.at[k]) for k in range(3)] + [(low_hbm, low_ref)]
@@ -261,14 +264,14 @@
 def load(low, cot, ws, wt, sort):
     frames, rows_low, cols_low, chan = low.shape
     order = like(sort.shape, jnp.bfloat16)
-    shapes = [low, ws, order, like((3 * chan, chan), wt.dtype),
+    shapes = [low, ws, wt, order, like((3 * chan, chan), wt.dtype),
               like((frames, 4, rows_low * cols_low, chan), jnp.bfloat16)]
     return pl.pallas_call(
         load_kernel,
         in_specs=[UNREAD] * 5,
-        out_specs=[FULL] * 5,
+        out_specs=[FULL] * 6,
         out_shape=[like(a.shape, a.dtype) for a in shapes],
-        scratch_shapes=[pltpu.VMEM(cot.shape, cot.dtype), pltpu.VMEM(sort.shape, sort.dtype), pltpu.VMEM(wt.shape, wt.dtype),
+        scratch_shapes=[pltpu.VMEM(cot.shape, cot.dtype), pltpu.VMEM(sort.shape, sort.dtype),
                         pltpu.SemaphoreType.DMA((frames + 14,))],
         compiler_params=grant(14),
         cost_estimate=cost(2, 4),
@@ -321,9 +324,8 @@
     return pl.pallas_call(
         backward_kernel,
         in_specs=[SCALAR] + [FULL] * 9,
-        out_specs=[FULL] * 4,
-        out_shape=[like(act.shape, jnp.bfloat16), like(ext, jnp.bfloat16), like((12, chan // 2, chan), jnp.float32),
-                   like((frames, count, chan), jnp.float32)],
+        out_specs=[FULL] * 3,
+        out_shape=[like(act.shape, jnp.bfloat16), like(ext, jnp.bfloat16), like((12, chan // 2, chan), jnp.float32)],
         compiler_params=grant(24),
         cost_estimate=cost(15, 10),
         name="backward",
@@ -331,13 +333,14 @@
 
 
 def half_grads(place, low, inner, outer, act, pg, ext):
-    chan = low.shape[-1]
+    frames, _, count, chan = act.shape
+    box = (frames, count, chan)
     return pl.pallas_call(
         half_kernel,
         in_specs=[SCALAR] + [FULL] * 6,
-        out_specs=[FULL, HBM],
-        out_shape=[like((12, chan // 2, chan), jnp.float32), pltpu.HBM(act.shape, act.dtype)],
-        scratch_shapes=[pltpu.SemaphoreType.DMA],
+        out_specs=[FULL, HBM, HBM],
+        out_shape=[like((12, chan // 2, chan), jnp.float32), pltpu.HBM(act.shape, act.dtype), pltpu.HBM(box, jnp.float32)],
+        scratch_shapes=[pltpu.VMEM(box, jnp.float32), pltpu.SemaphoreType.DMA((2,))],
         compiler_params=grant(20),
         cost_estimate=cost(10, 6),
         name="half_grads",
@@ -360,11 +363,13 @@
     return first + from_left(second, at)
 
 
-def input_kernel(pg_ref, box_ref, ws_ref, _, out_ref):
+def input_kernel(pg_ref, box_hbm, ws_ref, _, out_ref, box_ref, sem):
     frames, _, count, chan = pg_ref.shape
     cols_low = out_ref.shape[2]
     rows_low = count // cols_low
     at = column(count, cols_low, chan)
+    copy = pltpu.make_async_copy(box_hbm, box_ref, sem)
+    copy.start()
     turned = jnp.concatenate([ws_ref[i, j].T for j in range(3) for i in range(3)], axis=0)
     for frame in range(frames):
         own = [pg_ref[frame, side].astype(jnp.float32) for side in range(4)]
@@ -378,6 +383,8 @@
             for value in (odd + below, even + odd, above + even):
                 parts.append(jnp.concatenate(split(value.reshape(count, chan)), axis=0))
         sums = product(jnp.concatenate(parts, axis=1), turned)
+        if frame == 0:
+            copy.wait()
         total = box_ref[frame] + (sums[:count] + sums[count:])
         out_ref[frame] = total.reshape(rows_low, cols_low, chan)
 
@@ -385,24 +392,25 @@
 def input_own(pg, box, ws, before, low_shape):
     return pl.pallas_call(
         input_kernel,
-        in_specs=[FULL] * 3 + [UNREAD],
+        in_specs=[FULL, HBM, FULL, UNREAD],
         out_specs=FULL,
         out_shape=like(low_shape, jnp.float32),
+        scratch_shapes=[pltpu.VMEM(box.shape, box.dtype), pltpu.SemaphoreType.DMA],
         compiler_params=grant(16),
         cost_estimate=cost(6, 4),
         name="input_own",
-    )(pg, box, ws, before)
-
-
-def finish_kernel(place_ref, own_ref, ws_ref, inner_hbm, outer_hbm, edge_hbm, act_hbm, wt_hbm, sort_hbm, low_hbm, _,
+    )(pg, in_hbm(box), ws, before)
+
+
+def finish_kernel(place_ref, own_ref, ws_ref, wt_ref, sort_ref, low_ref, inner_hbm, outer_hbm, edge_hbm, act_hbm, _,
                   section_ref, input_ref, token_ref,
-                  inner_ref, outer_ref, edge_ref, act_ref, wt_ref, wide_ref, low_ref, earlier, held, input_held, sems):
+                  inner_ref, outer_ref, edge_ref, act_ref, earlier, held, input_held, sems):
     frames, rows_low, cols_low, chan = low_ref.shape
     group = rows_at_once(rows_low, cols_low)
     span, count = group * cols_low, rows_low * cols_low
     pairs = [(inner_hbm, inner_ref), (outer_hbm, outer_ref)]
-    pairs += [(edge_hbm, edge_ref), (wt_hbm, wt_ref)]
-    pairs += [(act_hbm.at[n], act_ref.at[n]) for n in range(frames)] + [(sort_hbm, wide_ref), (low_hbm, low_ref)]
+    pairs += [(edge_hbm, edge_ref)]
+    pairs += [(act_hbm.at[n], act_ref.at[n]) for n in range(frames)]
     copies = [pltpu.make_async_copy(a, b, sems.at[n]) for n, (a, b) in enumerate(pairs)]
     for copy in copies:
         copy.start()
@@ -442,7 +450,7 @@
             earlier[frame, side] = (pre * jax.nn.sigmoid(pre)).astype(jnp.bfloat16)
     for copy in copies[3:]:
         copy.wait()
-    merge = wide_ref[...].T.astype(jnp.bfloat16)
+    merge = sort_ref[...].T
     wt = wt_ref[...].reshape(3 * chan, chan)
     for frame in range(frames):
         acts = [act_ref[frame - k] if frame >= k else earlier[frame - k + 2] for k in range(3)]
@@ -459,13 +467,13 @@
         copy.wait()
 
 
-def finish(place, own, ws, inner, outer, edge, act, wt, sort, low, before):
+def finish(place, own, ws, wt, sort, low, inner, outer, edge, act, before):
     frames, rows_low, cols_low, chan = low.shape
     out = (frames, 2 * rows_low, 2 * cols_low, chan)
-    fetched = [inner, outer, edge, act, wt, sort, low]
+    fetched = [inner, outer, edge, act]
     return pl.pallas_call(
         finish_kernel,
-        in_specs=[SCALAR, FULL, FULL] + [HBM] * 7 + [UNREAD],
+        in_specs=[SCALAR] + [FULL] * 5 + [HBM] * 4 + [UNREAD],
         out_specs=[HBM, HBM, FULL],
         out_shape=[like(out, jnp.bfloat16), like(low.shape, jnp.bfloat16), TOKEN],
         scratch_shapes=[pltpu.VMEM(a.shape, a.dtype) for a in fetched]
@@ -474,7 +482,7 @@
         compiler_params=grant(16),
         cost_estimate=cost(8, 4),
         name="finish",
-    )(place, own, ws, inner, outer, edge, *[in_hbm(a) for a in (act, wt, sort, low)], before)
+    )(place, own, ws, wt, sort, low, inner, outer, edge, in_hbm(act), before)
 
 
 def put_kernel(place_ref, half_ref, *refs):
@@ -571,22 +579,22 @@
     later = bits.shift(later, "tm", -1)
     inner, outer = bits.pairs(inner, outer)
     order = jnp.asarray(side_order(rows_low, cols_low))
-    low_in, ws, sort, turned, cot_side = load(low, cot, spatial_weight, temporal_weight, order)
-    act, slope = forward(mine, low_in, inner, outer, ws)
-    pg, ext, theirs, box = backward(
-        other, low_in, inner, outer, act, slope, cot_side, later, turned, sort
+    low, ws, wt, sort, turned, cot_side = load(low, cot, spatial_weight, temporal_weight, order)
+    act, slope = forward(mine, low, inner, outer, ws)
+    pg, ext, theirs = backward(
+        other, low, inner, outer, act, slope, cot_side, later, turned, sort
     )
     theirs = bits.swap(theirs, bits.core)
-    own, act = half_grads(mine, low_in, inner, outer, act, pg, ext)
+    own, act, box = half_grads(mine, low, inner, outer, act, pg, ext)
     kept = add_halves(own, theirs)
     got = bits.exchange(kept.reshape(parts, -1, chan))
-    edge, pg_inner, pg_outer = edges(mine, low_in, inner, outer, pg, kept)
+    edge, pg_inner, pg_outer = edges(mine, low, inner, outer, pg, kept)
     edge = bits.shift(edge, "tm", 1)
     pg_inner, pg_outer = bits.pairs(pg_inner, pg_outer)
     own_part = input_own(pg, box, ws, kept, low.shape)
     total, far = bits.far_sums(sum_parts(got, own_part))
     section_out, input_grad, done = finish(
-        mine, own_part, ws, pg_inner, pg_outer, edge, act, temporal_weight, order, low, total
+        mine, own_part, ws, wt, sort, low, pg_inner, pg_outer, edge, act, total
     )
     totals = spread(total, far, parts, done)
     half = bits.exchange(totals).reshape(kept.shape)

time: 69.8 us -> 70.5 us (1.010)
  Pallas kernels: 26.3 us -> 28.3 us
  waiting for transfers between devices: 6.74 us -> 5.06 us
    pallas_call x3, Pallas kernels: 10.3 us -> 11.6 us  [the longest x1 6.25 us: finish(): pl.pallas_call(finish_kernel, in_specs=[SCALAR] + [FULL] * 5 + [HBM] * 4...]
    all_to_all x1, waiting for transfers between devices: 5.62 us -> 4.54 us  [exchange(): return lax.all_to_all(parts, tuple(self.near), 0, 0, tiled=True)]
    pallas_call x1, Pallas kernels: 2.43 us -> 3.31 us  [half_grads(): pl.pallas_call(half_kernel, in_specs=[SCALAR] + [FULL] * 6, out_specs=[FU...]
  transfers between devices with their start and end apart: 10 -> 10, of which waited for: 3 -> 2; matrix products, arithmetic and copies ran while one was open for 0% -> 0% of each run, Pallas kernels for 26% -> 29%
where the time goes in v16:
time: 70.5 us; the launch traced here: 70.1 us
  Pallas kernels  28.3 us (40%)
  starting transfers between devices  20.3 us (29%)
  blocking collectives  14 us (20%)
  waiting for transfers between devices  5.06 us (7%)
  local copies, waits for them, and re-layouts  1.28 us (2%)
  between operations  0.97 us (1%)
    all_to_all x1, blocking collectives, exchange(): return lax.all_to_all(parts, tuple(self.near), 0, 0, tiled=True)  14 us
    ppermute x5, starting transfers between devices, swap(): return lax.ppermute(block, axis, [(0, 1), (1, 0)])  8.67 us
    all_to_all x1, starting transfers between devices, exchange(): return lax.all_to_all(parts, tuple(self.near), 0, 0, tiled=True)  6.36 us
    pallas_call x1, Pallas kernels, finish(): pl.pallas_call(finish_kernel, in_specs=[SCALAR] + [FULL] * 5 + [HBM] * 4...  6.25 us
    all_to_all x1, waiting for transfers between devices, exchange(): return lax.all_to_all(parts, tuple(self.near), 0, 0, tiled=True)  4.54 us
    pallas_call x2, Pallas kernels, put(): pl.pallas_call(put_kernel, in_specs=[SCALAR, FULL] + [HBM] * len(done), o...  3.56 us
    ppermute x2, starting transfers between devices, shift(): return lax.ppermute(block, axes, route)  3.36 us
    pallas_call x1, Pallas kernels, backward(): pl.pallas_call(backward_kernel, in_specs=[SCALAR] + [FULL] * 9, out_specs...  3.35 us
  transfers between devices with their start and end apart: 10, of which 2 were waited for; matrix products, arithmetic and copies ran while one was open for 0% of the time, Pallas kernels for 29%

profile of v16, /device:TPU:0, one launch (start us, length us, event | category | flops | bytes accessed | tf_op | source)
XLA Modules:
  0.0 70.1 jit_solution(5738100946601835329)
XLA Ops:
  0.6 0.1 pad_add_fusion.place_ref
  0.7 1.7 %first_messages.1 = (bf16[4,1,32,256]{3,2,1,0:T(8,128)(2,1)S(1)}, bf16[4,1,32,256]{3,2,1,0:T(8,128)(2,1)S(1)}, bf16[2,8,64,256]{3,2,1,0:T(8,128)(2,1)S(1)}) custom-call(s32[2]{0:T(128)S(1)} %pad_add_fusion.place_ref, bf16[4,4,32,256]{3,2,1,0:T(8,128)(2,1)} %bitcast.13, bf16[4,8,64,256]{3,2,1,0:T(8,128)(2,1)} %bitcast.11), custom_call_target="tpu_custom_call" | custom-call | tf_op jit(solution)/shard_map/first_messages/pallas_call | solution.py:232
  2.5 1.3 %collective-permute-start.2 = (bf16[2,8,64,256]{3,2,1,0:T(8,128)(2,1)S(1)}, bf16[2,8,64,256]{3,2,1,0:T(8,128)(2,1)S(1)}, u32[]{:S(2)}, u32[]{:S(2)}) collective-permute-start(bf16[2,8,64,256]{3,2,1,0:T(8,128)(2,1)S(1)} %get-tuple-element.38), channel_id=1, source_target_pairs={{4,0},{8,4},{12,8},{5,1},{9,5},{13,9},{6,2},{10,6},{14,10},{7,3},{... | collective-permute-start | bytes 1572872 | tf_op jit(solution)/shard_map/ppermute | solution.py:40
  3.8 3.1 %collective-permute-start = (bf16[4,1,32,256]{3,2,1,0:T(8,128)(2,1)S(1)}, bf16[4,1,32,256]{3,2,1,0:T(8,128)(2,1)S(1)}, u32[]{:S(2)}, u32[]{:S(2)}) collective-permute-start(bf16[4,1,32,256]{3,2,1,0:T(8,128)(2,1)S(1)} %get-tuple-element.32), channel_id=1, source_target_pairs={{0,1},{1,0},{2,3},{3,2},{4,5},{5,4},{6,7},{7,6},{8,9},{9,8},{10,11... | collective-permute-start | bytes 196616 | tf_op jit(solution)/shard_map/ppermute | solution.py:34
  6.8 0.7 collective-permute-start.1
  7.5 0.1 pad_add_fusion.1.place_ref
  7.6 2.4 %load.1 = (bf16[4,4,32,256]{3,2,1,0:T(8,128)(2,1)S(1)}, bf16[3,3,256,256]{3,2,1,0:T(8,128)(2,1)S(1)}, bf16[3,256,256]{2,1,0:T(8,128)(2,1)S(1)}, bf16[256,256]{1,...) custom-call(bf16[4,4,32,256]{3,2,1,0:T(8,128)(2,1)} %bitcast.14, ...), custom_call_target="tpu_custom_call" | custom-call | flops 536870912 | bytes 4194304 | tf_op jit(solution)/shard_map/load/pallas_call | solution.py:269
  10.0 0.0 copy-start
  10.0 0.0 collective-permute-done.inner_ref
  10.0 0.0 collective-permute-done.1.outer_ref
  10.0 2.3 %forward.1 = (bf16[4,4,128,256]{3,2,1,0:T(8,128)(2,1)S(1)}, f32[4,4,128,256]{3,2,1,0:T(8,128)S(1)}) custom-call(s32[2]{0:T(128)S(1)} %pad_add_fusion.place_ref, bf16[4,4,32,256]{3,2,1,0:T(8,128)(2,1)S(1)} %get-tuple-element.31.low_ref, bf16[4,1,32,256]{3,2,1,0:T(8,128)(2,1)S(1)} %collective-permute-done.inner_ref, ...), custom_call_target="tpu_custom_call" | custom-call | flops 2684354560 | bytes 8388608 | tf_op jit(solution)/shard_map/forward/pallas_call | solution.py:285
  12.3 0.0 copy-done
  12.3 0.0 collective-permute-done.2.later_ref
  12.4 3.3 %backward.1 = (bf16[4,4,128,256]{3,2,1,0:T(8,128)(2,1)S(1)}, bf16[6,4,128,256]{3,2,1,0:T(8,128)(2,1)S(1)}, f32[12,128,256]{2,1,0:T(8,128)S(1)}) custom-call(s32[2]{0:T(128)S(1)} %pad_add_fusion.1.place_ref, bf16[4,4,32,256]{3,2,1,0:T(8,128)(2,1)S(1)} %get-tuple-element.31.low_ref, bf16[4,1,32,256]{3,2,1,0:T(8,128)(2,1)S(1)} %collective-permute-done.inner_ref, ...), custom_call_target="tpu_custom_call" | custom-call | flops 4026531840 | bytes 10485760 | tf_op jit(solution)/shard_map/backward/pallas_call | solution.py:324
  15.7 2.0 %collective-permute-start.3 = (f32[12,128,256]{2,1,0:T(8,128)S(1)}, f32[12,128,256]{2,1,0:T(8,128)S(1)}, u32[]{:S(2)}, u32[]{:S(2)}) collective-permute-start(f32[12,128,256]{2,1,0:T(8,128)S(1)} %get-tuple-element.45), channel_id=1, source_target_pairs={{0,4},{4,0},{1,5},{5,1},{2,6},{6,2},{3,7},{7,3},{8,12},{12,8},{9,1... | collective-permute-start | bytes 4718600 | tf_op jit(solution)/shard_map/ppermute | solution.py:34
  17.7 3.3 %half_grads.1 = (f32[12,128,256]{2,1,0:T(8,128)S(1)}, bf16[4,4,128,256]{3,2,1,0:T(8,128)(2,1)}, f32[4,128,256]{2,1,0:T(8,128)}) custom-call(s32[2]{0:T(128)S(1)} %pad_add_fusion.place_ref, bf16[4,4,32,256]{3,2,1,0:T(8,128)(2,1)S(1)} %get-tuple-element.31.low_ref, bf16[4,1,32,256]{3,2,1,0:T(8,128)(2,1)S(1)} %collective-permute-done.inner_ref, ...), custom_call_target="tpu_custom_call" | custom-call | flops 2684354560 | bytes 6291456 | tf_op jit(solution)/shard_map/half_grads/pallas_call | solution.py:338
  21.0 0.0 collective-permute-done.3.theirs_ref
  21.0 1.0 %add_halves.1._ = bf16[12,128,256]{2,1,0:T(8,128)(2,1)} custom-call(f32[12,128,256]{2,1,0:T(8,128)S(1)} %get-tuple-element.44.mine_ref, f32[12,128,256]{2,1,0:T(8,128)S(1)} %collective-permute-done.3.theirs_ref), custom_call_target="tpu_custom_call" | custom-call | tf_op jit(solution)/shard_map/add_halves/pallas_call | solution.py:525
  22.0 6.4 %all-to-all-start = ((bf16[8,192,256]{2,1,0:T(8,128)(2,1)}), bf16[8,192,256]{2,1,0:T(8,128)(2,1)S(1)}, u32[]{:S(2)}, u32[]{:S(2)}) async-start(bf16[8,192,256]{2,1,0:T(8,128)(2,1)} %bitcast.5), calls=%async_computation | async-start | bytes 1572864 | tf_op jit(solution)/shard_map/all_to_all | solution.py:43
  28.4 0.0 copy-start.1
  28.4 1.3 %edges.1 = (bf16[2,6,32,256]{3,2,1,0:T(8,128)(2,1)S(1)}, bf16[4,2,32,256]{3,2,1,0:T(8,128)(2,1)}, bf16[4,2,32,256]{3,2,1,0:T(8,128)(2,1)}) custom-call(s32[2]{0:T(128)S(1)} %pad_add_fusion.place_ref, bf16[4,4,32,256]{3,2,1,0:T(8,128)(2,1)S(1)} %get-tuple-element.31.low_ref, bf16[4,1,32,256]{3,2,1,0:T(8,128)(2,1)S(1)} %collective-permute-done.inner_ref, ...), custom_call_target="tpu_custom_call" | custom-call | tf_op jit(solution)/shard_map/edges/pallas_call | solution.py:311
  29.7 2.1 %collective-permute-start.6 = (bf16[2,6,32,256]{3,2,1,0:T(8,128)(2,1)S(1)}, bf16[2,6,32,256]{3,2,1,0:T(8,128)(2,1)S(1)}, u32[]{:S(2)}, u32[]{:S(2)}) collective-permute-start(bf16[2,6,32,256]{3,2,1,0:T(8,128)(2,1)S(1)} %get-tuple-element.49), channel_id=1, source_target_pairs={{0,4},{4,8},{8,12},{1,5},{5,9},{9,13},{2,6},{6,10},{10,14},{3,7},{... | collective-permute-start | bytes 589832 | tf_op jit(solution)/shard_map/ppermute | solution.py:40
  31.8 1.8 %collective-permute-start.4 = (bf16[4,2,32,256]{3,2,1,0:T(8,128)(2,1)}, bf16[4,2,32,256]{3,2,1,0:T(8,128)(2,1)}, u32[]{:S(2)}, u32[]{:S(2)}) collective-permute-start(bf16[4,2,32,256]{3,2,1,0:T(8,128)(2,1)} %get-tuple-element.47), channel_id=1, source_target_pairs={{0,1},{1,0},{2,3},{3,2},{4,5},{5,4},{6,7},{7,6},{8,9},{9,8},{10,11... | collective-permute-start | bytes 393224 | tf_op jit(solution)/shard_map/ppermute | solution.py:34
  33.6 1.3 %collective-permute-start.5 = (bf16[4,2,32,256]{3,2,1,0:T(8,128)(2,1)}, bf16[4,2,32,256]{3,2,1,0:T(8,128)(2,1)}, u32[]{:S(2)}, u32[]{:S(2)}) collective-permute-start(bf16[4,2,32,256]{3,2,1,0:T(8,128)(2,1)} %get-tuple-element.48), channel_id=1, source_target_pairs={{1,2},{2,1},{5,6},{6,5},{9,10},{10,9},{13,14},{14,13},{17,18},{18,... | collective-permute-start | bytes 393224 | tf_op jit(solution)/shard_map/ppermute | solution.py:49
  34.9 0.0 copy-done.1
  34.9 2.9 %input_own.1._.own_ref = f32[4,4,32,256]{3,2,1,0:T(8,128)S(1)} custom-call(bf16[4,4,128,256]{3,2,1,0:T(8,128)(2,1)S(1)} %get-tuple-element.41.pg_ref, f32[4,128,256]{2,1,0:T(8,128)} %get-tuple-element.43.box_hbm, bf16[3,3,256,256]{3,2,1,0:T(8,128)(2,1)S(1)} %copy-done.1, bf16[12,128,256]{2,1,0:T(8,128)(2,1)} %add_halves.1._), custom_call_target="tpu_custom_call" | custom-call | flops 1610612736 | bytes 4194304 | tf_op jit(solution)/shard_map/input_own/pallas_call | solution.py:393
  37.8 4.5 %all-to-all-done.got_ref = bf16[8,192,256]{2,1,0:T(8,128)(2,1)S(1)} async-done(((bf16[8,192,256]{2,1,0:T(8,128)(2,1)}), bf16[8,192,256]{2,1,0:T(8,128)(2,1)S(1)}, u32[]{:S(2)}, u32[]{:S(2)}) %all-to-all-start) | async-done | bytes 786464 | tf_op jit(solution)/shard_map/all_to_all | solution.py:43
  42.4 0.1 sum_parts.1._.own_ref
  42.5 1.8 %collective-permute-start.7 = (bf16[192,256]{1,0:T(8,128)(2,1)S(1)}, bf16[192,256]{1,0:T(8,128)(2,1)S(1)}, u32[]{:S(2)}, u32[]{:S(2)}) collective-permute-start(bf16[192,256]{1,0:T(8,128)(2,1)S(1)} %sum_parts.1._.own_ref), channel_id=1, source_target_pairs={{0,2},{2,0},{1,3},{3,1},{4,6},{6,4},{5,7},{7,5},{8,10},{10,8},{9,1... | collective-permute-start | bytes 294920 | tf_op jit(solution)/shard_map/ppermute | solution.py:34
  44.3 0.0 collective-permute-done.4.inner_hbm
  44.3 0.0 collective-permute-done.5.outer_hbm
  44.3 0.0 collective-permute-done.6.edge_hbm
  44.3 0.0 copy-start.2
  44.3 1.3 %copy-done.2 = bf16[3,3,256,256]{3,2,1,0:T(8,128)(2,1)S(1)} copy-done((bf16[3,3,256,256]{3,2,1,0:T(8,128)(2,1)S(1)}, bf16[3,3,256,256]{3,2,1,0:T(8,128)(2,1)}, u32[]{:S(2)}) %copy-start.2) | copy-done | bytes 1179672
  45.6 6.2 %finish.1 = (bf16[4,8,64,256]{3,2,1,0:T(8,128)(2,1)}, bf16[4,4,32,256]{3,2,1,0:T(8,128)(2,1)}, f32[8,128]{1,0:T(8,128)S(1)}) custom-call(s32[2]{0:T(128)S(1)} %pad_add_fusion.place_ref, f32[4,4,32,256]{3,2,1,0:T(8,128)S(1)} %input_own.1._.own_ref, bf16[3,3,256,256]{3,2,1,0:T(8,128)(2,1)S(1)} %copy-done.2, bf16[3,256,256]{2,1,0:T(8,128)(2,1)S(1)} %get-tuple-element.46.wt_ref, ...), custom_call_target="tpu_custom_call" | custom-call | flops 2147483648 | bytes 4194304 | tf_op jit(solution)/shard_map/finish/pallas_call | solution.py:474
  51.8 0.0 collective-permute-done.7.theirs_ref
  51.8 0.1 spread.1
  51.9 14.0 %all_to_all.10 = bf16[8,192,256]{2,1,0:T(8,128)(2,1)S(1)} all-to-all(bf16[8,192,256]{2,1,0:T(8,128)(2,1)S(1)} %spread.1), channel_id=1, replica_groups=mesh['dp0'=2,'tm1'=2,'tm0'=2,'height1'=2,'height0'=2] {'dp0','tm1','heig..., dimensions={0} | all-to-all | bytes 1572864 | tf_op jit(solution)/shard_map/all_to_all | solution.py:43
  65.9 0.0 collective-permute-start.8
  65.9 1.8 %put.2 = (f32[3,3,256,256]{3,2,1,0:T(8,128)}, f32[3,256,256]{2,1,0:T(8,128)}) custom-call(s32[2]{0:T(128)S(1)} %pad_add_fusion.place_ref, bf16[12,128,256]{2,1,0:T(8,128)(2,1)S(1)} %bitcast.10), custom_call_target="tpu_custom_call" | custom-call | tf_op jit(solution)/shard_map/put/pallas_call | solution.py:507
  67.6 0.5 collective-permute-done.8.half_ref
  68.1 1.8 %put.3 = (f32[3,3,256,256]{3,2,1,0:T(8,128)}, f32[3,256,256]{2,1,0:T(8,128)}) custom-call(s32[2]{0:T(128)S(1)} %pad_add_fusion.1.place_ref, bf16[12,128,256]{2,1,0:T(8,128)(2,1)S(1)} %collective-permute-done.8.half_ref, f32[3,3,256,256]{3,2,1,0:T(8,128)} %get-tuple-element.54.refs_0_, ...), custom_call_target="tpu_custom_call", output_to_operand_aliasing={{0}: (2, {}), {1}: (3, {})} | custom-call | tf_op jit(solution)/shard_map/put/pallas_call | solution.py:507
Async XLA Ops:
  2.5 9.9 %collective-permute-start.2 = (bf16[2,8,64,256]{3,2,1,0:T(8,128)(2,1)S(1)}, bf16[2,8,64,256]{3,2,1,0:T(8,128)(2,1)S(1)}, u32[]{:S(2)}, u32[]{:S(2)}) collective-permute-start(bf16[2,8,64,256]{3,2,1,0:T(8,128)(2,1)S(1)} %get-tuple-element.38), channel_id=1, source_target_pairs={{4,0},{8,4},{12,8},{5,1},{9,5},{13,9},{6,2},{10,6},{14,10},{7,3},{... | collective-permute-start | bytes 1572872 | tf_op jit(solution)/shard_map/ppermute | solution.py:40
  3.8 6.2 %collective-permute-start = (bf16[4,1,32,256]{3,2,1,0:T(8,128)(2,1)S(1)}, bf16[4,1,32,256]{3,2,1,0:T(8,128)(2,1)S(1)}, u32[]{:S(2)}, u32[]{:S(2)}) collective-permute-start(bf16[4,1,32,256]{3,2,1,0:T(8,128)(2,1)S(1)} %get-tuple-element.32), channel_id=1, source_target_pairs={{0,1},{1,0},{2,3},{3,2},{4,5},{5,4},{6,7},{7,6},{8,9},{9,8},{10,11... | collective-permute-start | bytes 196616 | tf_op jit(solution)/shard_map/ppermute | solution.py:34
  6.8 3.2 %collective-permute-start.1 = (bf16[4,1,32,256]{3,2,1,0:T(8,128)(2,1)S(1)}, bf16[4,1,32,256]{3,2,1,0:T(8,128)(2,1)S(1)}, u32[]{:S(2)}, u32[]{:S(2)}) collective-permute-start(bf16[4,1,32,256]{3,2,1,0:T(8,128)(2,1)S(1)} %get-tuple-element.33), channel_id=1, source_target_pairs={{1,2},{2,1},{5,6},{6,5},{9,10},{10,9},{13,14},{14,13},{17,18},{18,... | collective-permute-start | bytes 196616 | tf_op jit(solution)/shard_map/ppermute | solution.py:49
  10.0 2.4 %copy-start = (bf16[3,3,256,256]{3,2,1,0:T(8,128)(2,1)}, bf16[3,3,256,256]{3,2,1,0:T(8,128)(2,1)S(1)}, u32[]{:S(2)}) copy-start(bf16[3,3,256,256]{3,2,1,0:T(8,128)(2,1)S(1)} %get-tuple-element.34.ws_ref) | copy-start | bytes 3538948
  15.7 5.3 %collective-permute-start.3 = (f32[12,128,256]{2,1,0:T(8,128)S(1)}, f32[12,128,256]{2,1,0:T(8,128)S(1)}, u32[]{:S(2)}, u32[]{:S(2)}) collective-permute-start(f32[12,128,256]{2,1,0:T(8,128)S(1)} %get-tuple-element.45), channel_id=1, source_target_pairs={{0,4},{4,0},{1,5},{5,1},{2,6},{6,2},{3,7},{7,3},{8,12},{12,8},{9,1... | collective-permute-start | bytes 4718600 | tf_op jit(solution)/shard_map/ppermute | solution.py:34
  22.0 20.3 %all-to-all-start = ((bf16[8,192,256]{2,1,0:T(8,128)(2,1)}), bf16[8,192,256]{2,1,0:T(8,128)(2,1)S(1)}, u32[]{:S(2)}, u32[]{:S(2)}) async-start(bf16[8,192,256]{2,1,0:T(8,128)(2,1)} %bitcast.5), calls=%async_computation | async-start | bytes 1572864 | tf_op jit(solution)/shard_map/all_to_all | solution.py:43
  28.4 6.5 %copy-start.1 = (bf16[3,3,256,256]{3,2,1,0:T(8,128)(2,1)S(1)}, bf16[3,3,256,256]{3,2,1,0:T(8,128)(2,1)}, u32[]{:S(2)}) copy-start(bf16[3,3,256,256]{3,2,1,0:T(8,128)(2,1)} %copy-done) | copy-start | bytes 3538948
  29.7 14.6 %collective-permute-start.6 = (bf16[2,6,32,256]{3,2,1,0:T(8,128)(2,1)S(1)}, bf16[2,6,32,256]{3,2,1,0:T(8,128)(2,1)S(1)}, u32[]{:S(2)}, u32[]{:S(2)}) collective-permute-start(bf16[2,6,32,256]{3,2,1,0:T(8,128)(2,1)S(1)} %get-tuple-element.49), channel_id=1, source_target_pairs={{0,4},{4,8},{8,12},{1,5},{5,9},{9,13},{2,6},{6,10},{10,14},{3,7},{... | collective-permute-start | bytes 589832 | tf_op jit(solution)/shard_map/ppermute | solution.py:40
  31.8 12.5 %collective-permute-start.4 = (bf16[4,2,32,256]{3,2,1,0:T(8,128)(2,1)}, bf16[4,2,32,256]{3,2,1,0:T(8,128)(2,1)}, u32[]{:S(2)}, u32[]{:S(2)}) collective-permute-start(bf16[4,2,32,256]{3,2,1,0:T(8,128)(2,1)} %get-tuple-element.47), channel_id=1, source_target_pairs={{0,1},{1,0},{2,3},{3,2},{4,5},{5,4},{6,7},{7,6},{8,9},{9,8},{10,11... | collective-permute-start | bytes 393224 | tf_op jit(solution)/shard_map/ppermute | solution.py:34
  33.6 10.7 %collective-permute-start.5 = (bf16[4,2,32,256]{3,2,1,0:T(8,128)(2,1)}, bf16[4,2,32,256]{3,2,1,0:T(8,128)(2,1)}, u32[]{:S(2)}, u32[]{:S(2)}) collective-permute-start(bf16[4,2,32,256]{3,2,1,0:T(8,128)(2,1)} %get-tuple-element.48), channel_id=1, source_target_pairs={{1,2},{2,1},{5,6},{6,5},{9,10},{10,9},{13,14},{14,13},{17,18},{18,... | collective-permute-start | bytes 393224 | tf_op jit(solution)/shard_map/ppermute | solution.py:49
  42.5 9.3 %collective-permute-start.7 = (bf16[192,256]{1,0:T(8,128)(2,1)S(1)}, bf16[192,256]{1,0:T(8,128)(2,1)S(1)}, u32[]{:S(2)}, u32[]{:S(2)}) collective-permute-start(bf16[192,256]{1,0:T(8,128)(2,1)S(1)} %sum_parts.1._.own_ref), channel_id=1, source_target_pairs={{0,2},{2,0},{1,3},{3,1},{4,6},{6,4},{5,7},{7,5},{8,10},{10,8},{9,1... | collective-permute-start | bytes 294920 | tf_op jit(solution)/shard_map/ppermute | solution.py:34
  44.3 1.3 %copy-start.2 = (bf16[3,3,256,256]{3,2,1,0:T(8,128)(2,1)S(1)}, bf16[3,3,256,256]{3,2,1,0:T(8,128)(2,1)}, u32[]{:S(2)}) copy-start(bf16[3,3,256,256]{3,2,1,0:T(8,128)(2,1)} %copy-done) | copy-start | bytes 3538948
  65.9 2.3 %collective-permute-start.8 = (bf16[12,128,256]{2,1,0:T(8,128)(2,1)S(1)}, bf16[12,128,256]{2,1,0:T(8,128)(2,1)S(1)}, u32[]{:S(2)}, u32[]{:S(2)}) collective-permute-start(bf16[12,128,256]{2,1,0:T(8,128)(2,1)S(1)} %bitcast.9), channel_id=1, source_target_pairs={{0,4},{4,0},{1,5},{5,1},{2,6},{6,2},{3,7},{7,3},{8,12},{12,8},{9,1... | collective-permute-start | bytes 2359304 | tf_op jit(solution)/shard_map/ppermute | solution.py:34

commit v17 on v15

--- a/solution.py
+++ b/solution.py
@@ -173,7 +173,7 @@
 
 
 def backward_kernel(place_ref, low_ref, inner_ref, outer_ref, act_ref, slope_ref, cot_ref, later_ref, turned_ref, sort_ref,
-                    pg_ref, ext_ref, out_ref, box_ref):
+                    pg_ref, ext_ref, out_ref):
     frames, _, count, chan = cot_ref.shape
     ext_ref[:frames] = cot_ref[...]
     for n in range(2):
@@ -183,7 +183,6 @@
         act_grad = product(jnp.concatenate(cots, axis=1), turned_ref[...])
         slope = slope_ref[frame].reshape(4 * count, chan)
         pg_ref[frame] = (act_grad * slope).astype(jnp.bfloat16).reshape(4, count, chan)
-        box_ref[frame] = sum(cot_ref[frame, side].astype(jnp.float32) for side in range(4))
     half_sums(place_ref, low_ref, inner_ref, outer_ref, act_ref, pg_ref, ext_ref, out_ref)
 
 
@@ -321,9 +320,8 @@
     return pl.pallas_call(
         backward_kernel,
         in_specs=[SCALAR] + [FULL] * 9,
-        out_specs=[FULL] * 4,
-        out_shape=[like(act.shape, jnp.bfloat16), like(ext, jnp.bfloat16), like((12, chan // 2, chan), jnp.float32),
-                   like((frames, count, chan), jnp.float32)],
+        out_specs=[FULL] * 3,
+        out_shape=[like(act.shape, jnp.bfloat16), like(ext, jnp.bfloat16), like((12, chan // 2, chan), jnp.float32)],
         compiler_params=grant(24),
         cost_estimate=cost(15, 10),
         name="backward",
@@ -360,11 +358,14 @@
     return first + from_left(second, at)
 
 
-def input_kernel(pg_ref, box_ref, ws_ref, _, out_ref):
+def input_kernel(pg_ref, ext_hbm, ws_ref, _, out_ref, cot_ref, sems):
     frames, _, count, chan = pg_ref.shape
     cols_low = out_ref.shape[2]
     rows_low = count // cols_low
     at = column(count, cols_low, chan)
+    copies = [pltpu.make_async_copy(ext_hbm.at[n], cot_ref.at[n], sems.at[n]) for n in range(frames)]
+    for copy in copies:
+        copy.start()
     turned = jnp.concatenate([ws_ref[i, j].T for j in range(3) for i in range(3)], axis=0)
     for frame in range(frames):
         own = [pg_ref[frame, side].astype(jnp.float32) for side in range(4)]
@@ -378,20 +379,23 @@
             for value in (odd + below, even + odd, above + even):
                 parts.append(jnp.concatenate(split(value.reshape(count, chan)), axis=0))
         sums = product(jnp.concatenate(parts, axis=1), turned)
-        total = box_ref[frame] + (sums[:count] + sums[count:])
+        copies[frame].wait()
+        total = sum(cot_ref[frame, side].astype(jnp.float32) for side in range(4))
+        total = total + (sums[:count] + sums[count:])
         out_ref[frame] = total.reshape(rows_low, cols_low, chan)
 
 
-def input_own(pg, box, ws, before, low_shape):
+def input_own(pg, ext, ws, before, low_shape):
     return pl.pallas_call(
         input_kernel,
-        in_specs=[FULL] * 3 + [UNREAD],
+        in_specs=[FULL, HBM, FULL, UNREAD],
         out_specs=FULL,
         out_shape=like(low_shape, jnp.float32),
+        scratch_shapes=[pltpu.VMEM(pg.shape, ext.dtype), pltpu.SemaphoreType.DMA((pg.shape[0],))],
         compiler_params=grant(16),
         cost_estimate=cost(6, 4),
         name="input_own",
-    )(pg, box, ws, before)
+    )(pg, in_hbm(ext), ws, before)
 
 
 def finish_kernel(place_ref, own_ref, ws_ref, inner_hbm, outer_hbm, edge_hbm, act_hbm, wt_hbm, sort_hbm, low_hbm, _,
@@ -573,7 +577,7 @@
     order = jnp.asarray(side_order(rows_low, cols_low))
     low_in, ws, sort, turned, cot_side = load(low, cot, spatial_weight, temporal_weight, order)
     act, slope = forward(mine, low_in, inner, outer, ws)
-    pg, ext, theirs, box = backward(
+    pg, ext, theirs = backward(
         other, low_in, inner, outer, act, slope, cot_side, later, turned, sort
     )
     theirs = bits.swap(theirs, bits.core)
@@ -583,7 +587,7 @@
     edge, pg_inner, pg_outer = edges(mine, low_in, inner, outer, pg, kept)
     edge = bits.shift(edge, "tm", 1)
     pg_inner, pg_outer = bits.pairs(pg_inner, pg_outer)
-    own_part = input_own(pg, box, ws, kept, low.shape)
+    own_part = input_own(pg, ext, ws, kept, low.shape)
     total, far = bits.far_sums(sum_parts(got, own_part))
     section_out, input_grad, done = finish(
         mine, own_part, ws, pg_inner, pg_outer, edge, act, temporal_weight, order, low, total

time: 69.8 us -> 69.3 us (level)
  waiting for transfers between devices: 6.74 us -> 4.34 us
  Pallas kernels: 26.3 us -> 28.6 us
  local copies, waits for them, and re-layouts: 0.79 us -> 0.01 us
    all_to_all x1, waiting for transfers between devices: 5.62 us -> 3.23 us  [exchange(): return lax.all_to_all(parts, tuple(self.near), 0, 0, tiled=True)]
    pallas_call x1, Pallas kernels: 1.57 us -> 3.91 us  [input_own(): pl.pallas_call(input_kernel, in_specs=[FULL, HBM, FULL, UNREAD], out_spec...]
    unnamed x4 -> x2, local copies, waits for them, and re-layouts: 0.79 us -> 0.01 us
  transfers between devices with their start and end apart: 10 -> 10, of which waited for: 3 -> 3; matrix products, arithmetic and copies ran while one was open for 0% -> 0% of each run, Pallas kernels for 26% -> 30%
where the time goes in v17:
time: 69.3 us; the launch traced here: 68.9 us
  Pallas kernels  28.6 us (41%)
  starting transfers between devices  21 us (30%)
  blocking collectives  13.9 us (20%)
  waiting for transfers between devices  4.34 us (6%)
  between operations  0.95 us (1%)
    all_to_all x1, blocking collectives, exchange(): return lax.all_to_all(parts, tuple(self.near), 0, 0, tiled=True)  13.9 us
    ppermute x5, starting transfers between devices, swap(): return lax.ppermute(block, axis, [(0, 1), (1, 0)])  8.54 us
    all_to_all x1, starting transfers between devices, exchange(): return lax.all_to_all(parts, tuple(self.near), 0, 0, tiled=True)  6.73 us
    pallas_call x1, Pallas kernels, finish(): pl.pallas_call(finish_kernel, in_specs=[SCALAR, FULL, FULL] + [HBM] * 7 +...  6.33 us
    pallas_call x1, Pallas kernels, input_own(): pl.pallas_call(input_kernel, in_specs=[FULL, HBM, FULL, UNREAD], out_spec...  3.91 us
    ppermute x2, starting transfers between devices, shift(): return lax.ppermute(block, axes, route)  3.75 us
    pallas_call x2, Pallas kernels, put(): pl.pallas_call(put_kernel, in_specs=[SCALAR, FULL] + [HBM] * len(done), o...  3.56 us
    pallas_call x1, Pallas kernels, backward(): pl.pallas_call(backward_kernel, in_specs=[SCALAR] + [FULL] * 9, out_specs...  3.35 us
  transfers between devices with their start and end apart: 10, of which 3 were waited for; matrix products, arithmetic and copies ran while one was open for 0% of the time, Pallas kernels for 30%

profile of v17, /device:TPU:0, one launch (start us, length us, event | category | flops | bytes accessed | tf_op | source)
XLA Modules:
  0.0 68.9 jit_solution(16829517103573424908)
XLA Ops:
  0.6 0.1 pad_add_fusion.place_ref
  0.7 1.7 %first_messages.1 = (bf16[4,1,32,256]{3,2,1,0:T(8,128)(2,1)S(1)}, bf16[4,1,32,256]{3,2,1,0:T(8,128)(2,1)S(1)}, bf16[2,8,64,256]{3,2,1,0:T(8,128)(2,1)S(1)}) custom-call(s32[2]{0:T(128)S(1)} %pad_add_fusion.place_ref, bf16[4,4,32,256]{3,2,1,0:T(8,128)(2,1)} %bitcast.13, bf16[4,8,64,256]{3,2,1,0:T(8,128)(2,1)} %bitcast.11), custom_call_target="tpu_custom_call" | custom-call | tf_op jit(solution)/shard_map/first_messages/pallas_call | solution.py:228
  2.5 1.3 %collective-permute-start.2 = (bf16[2,8,64,256]{3,2,1,0:T(8,128)(2,1)S(1)}, bf16[2,8,64,256]{3,2,1,0:T(8,128)(2,1)S(1)}, u32[]{:S(2)}, u32[]{:S(2)}) collective-permute-start(bf16[2,8,64,256]{3,2,1,0:T(8,128)(2,1)S(1)} %get-tuple-element.36), channel_id=1, source_target_pairs={{4,0},{8,4},{12,8},{5,1},{9,5},{13,9},{6,2},{10,6},{14,10},{7,3},{... | collective-permute-start | bytes 1572872 | tf_op jit(solution)/shard_map/ppermute | solution.py:40
  3.8 3.1 %collective-permute-start = (bf16[4,1,32,256]{3,2,1,0:T(8,128)(2,1)S(1)}, bf16[4,1,32,256]{3,2,1,0:T(8,128)(2,1)S(1)}, u32[]{:S(2)}, u32[]{:S(2)}) collective-permute-start(bf16[4,1,32,256]{3,2,1,0:T(8,128)(2,1)S(1)} %get-tuple-element.30), channel_id=1, source_target_pairs={{0,1},{1,0},{2,3},{3,2},{4,5},{5,4},{6,7},{7,6},{8,9},{9,8},{10,11... | collective-permute-start | bytes 196616 | tf_op jit(solution)/shard_map/ppermute | solution.py:34
  6.8 0.7 collective-permute-start.1
  7.5 0.1 pad_add_fusion.1.place_ref
  7.6 2.4 %load.1 = (bf16[4,4,32,256]{3,2,1,0:T(8,128)(2,1)S(1)}, bf16[3,3,256,256]{3,2,1,0:T(8,128)(2,1)S(1)}, bf16[256,256]{1,0:T(8,128)(2,1)S(1)}, bf16[768,256]{1,0:T(8,128)(2,1)S(1)}, bf16[4,4,128,256]{3,2,1,0:T(8,128)(2,1)S(1)}) custom-call(bf16[4,4,32,256]{3,2,1,0:T(8,128)(2,1)} %bitcast.14, bf16[4,8,64,256]{3,2,1,0:T(8,128)(2,1)} %bitcast.12, ...), custom_call_target="tpu_custom_call" | custom-call | flops 536870912 | bytes 4194304 | tf_op jit(solution)/shard_map/load/pallas_call | solution.py:265
  10.0 0.0 collective-permute-done.inner_ref
  10.0 0.0 collective-permute-done.1.outer_ref
  10.0 2.4 %forward.1 = (bf16[4,4,128,256]{3,2,1,0:T(8,128)(2,1)S(1)}, f32[4,4,128,256]{3,2,1,0:T(8,128)S(1)}) custom-call(s32[2]{0:T(128)S(1)} %pad_add_fusion.place_ref, bf16[4,4,32,256]{3,2,1,0:T(8,128)(2,1)S(1)} %get-tuple-element.29.low_ref, bf16[4,1,32,256]{3,2,1,0:T(8,128)(2,1)S(1)} %collective-permute-done.inner_ref, ...), custom_call_target="tpu_custom_call" | custom-call | flops 2684354560 | bytes 8388608 | tf_op jit(solution)/shard_map/forward/pallas_call | solution.py:281
  12.4 0.0 collective-permute-done.2.later_ref
  12.4 3.3 %backward.1 = (bf16[4,4,128,256]{3,2,1,0:T(8,128)(2,1)S(1)}, bf16[6,4,128,256]{3,2,1,0:T(8,128)(2,1)S(1)}, f32[12,128,256]{2,1,0:T(8,128)S(1)}) custom-call(s32[2]{0:T(128)S(1)} %pad_add_fusion.1.place_ref, bf16[4,4,32,256]{3,2,1,0:T(8,128)(2,1)S(1)} %get-tuple-element.29.low_ref, bf16[4,1,32,256]{3,2,1,0:T(8,128)(2,1)S(1)} %collective-permute-done.inner_ref, ...), custom_call_target="tpu_custom_call" | custom-call | flops 4026531840 | bytes 10485760 | tf_op jit(solution)/shard_map/backward/pallas_call | solution.py:320
  15.8 0.0 copy-start
  15.8 1.9 %collective-permute-start.3 = (f32[12,128,256]{2,1,0:T(8,128)S(1)}, f32[12,128,256]{2,1,0:T(8,128)S(1)}, u32[]{:S(2)}, u32[]{:S(2)}) collective-permute-start(f32[12,128,256]{2,1,0:T(8,128)S(1)} %get-tuple-element.42), channel_id=1, source_target_pairs={{0,4},{4,0},{1,5},{5,1},{2,6},{6,2},{3,7},{7,3},{8,12},{12,8},{9,1... | collective-permute-start | bytes 4718600 | tf_op jit(solution)/shard_map/ppermute | solution.py:34
  17.7 2.4 %half_grads.1 = (f32[12,128,256]{2,1,0:T(8,128)S(1)}, bf16[4,4,128,256]{3,2,1,0:T(8,128)(2,1)}) custom-call(s32[2]{0:T(128)S(1)} %pad_add_fusion.place_ref, bf16[4,4,32,256]{3,2,1,0:T(8,128)(2,1)S(1)} %get-tuple-element.29.low_ref, bf16[4,1,32,256]{3,2,1,0:T(8,128)(2,1)S(1)} %collective-permute-done.inner_ref, ...), custom_call_target="tpu_custom_call" | custom-call | flops 2684354560 | bytes 6291456 | tf_op jit(solution)/shard_map/half_grads/pallas_call | solution.py:333
  20.1 0.0 copy-done
  20.1 0.6 collective-permute-done.3.theirs_ref
  20.7 1.0 %add_halves.1._ = bf16[12,128,256]{2,1,0:T(8,128)(2,1)} custom-call(f32[12,128,256]{2,1,0:T(8,128)S(1)} %get-tuple-element.41.mine_ref, f32[12,128,256]{2,1,0:T(8,128)S(1)} %collective-permute-done.3.theirs_ref), custom_call_target="tpu_custom_call" | custom-call | tf_op jit(solution)/shard_map/add_halves/pallas_call | solution.py:521
  21.8 6.7 %all-to-all-start = ((bf16[8,192,256]{2,1,0:T(8,128)(2,1)}), bf16[8,192,256]{2,1,0:T(8,128)(2,1)S(1)}, u32[]{:S(2)}, u32[]{:S(2)}) async-start(bf16[8,192,256]{2,1,0:T(8,128)(2,1)} %bitcast.5), calls=%async_computation | async-start | bytes 1572864 | tf_op jit(solution)/shard_map/all_to_all | solution.py:43
  28.5 1.3 %edges.1 = (bf16[2,6,32,256]{3,2,1,0:T(8,128)(2,1)}, bf16[4,2,32,256]{3,2,1,0:T(8,128)(2,1)}, bf16[4,2,32,256]{3,2,1,0:T(8,128)(2,1)}) custom-call(s32[2]{0:T(128)S(1)} %pad_add_fusion.place_ref, bf16[4,4,32,256]{3,2,1,0:T(8,128)(2,1)S(1)} %get-tuple-element.29.low_ref, bf16[4,1,32,256]{3,2,1,0:T(8,128)(2,1)S(1)} %collective-permute-done.inner_ref, ...), custom_call_target="tpu_custom_call" | custom-call | tf_op jit(solution)/shard_map/edges/pallas_call | solution.py:307
  29.8 2.5 %collective-permute-start.6 = (bf16[2,6,32,256]{3,2,1,0:T(8,128)(2,1)}, bf16[2,6,32,256]{3,2,1,0:T(8,128)(2,1)}, u32[]{:S(2)}, u32[]{:S(2)}) collective-permute-start(bf16[2,6,32,256]{3,2,1,0:T(8,128)(2,1)} %get-tuple-element.45), channel_id=1, source_target_pairs={{0,4},{4,8},{8,12},{1,5},{5,9},{9,13},{2,6},{6,10},{10,14},{3,7},{... | collective-permute-start | bytes 589832 | tf_op jit(solution)/shard_map/ppermute | solution.py:40
  32.3 1.7 %collective-permute-start.4 = (bf16[4,2,32,256]{3,2,1,0:T(8,128)(2,1)}, bf16[4,2,32,256]{3,2,1,0:T(8,128)(2,1)}, u32[]{:S(2)}, u32[]{:S(2)}) collective-permute-start(bf16[4,2,32,256]{3,2,1,0:T(8,128)(2,1)} %get-tuple-element.43), channel_id=1, source_target_pairs={{0,1},{1,0},{2,3},{3,2},{4,5},{5,4},{6,7},{7,6},{8,9},{9,8},{10,11... | collective-permute-start | bytes 393224 | tf_op jit(solution)/shard_map/ppermute | solution.py:34
  34.0 1.3 %collective-permute-start.5 = (bf16[4,2,32,256]{3,2,1,0:T(8,128)(2,1)}, bf16[4,2,32,256]{3,2,1,0:T(8,128)(2,1)}, u32[]{:S(2)}, u32[]{:S(2)}) collective-permute-start(bf16[4,2,32,256]{3,2,1,0:T(8,128)(2,1)} %get-tuple-element.44), channel_id=1, source_target_pairs={{1,2},{2,1},{5,6},{6,5},{9,10},{10,9},{13,14},{14,13},{17,18},{18,... | collective-permute-start | bytes 393224 | tf_op jit(solution)/shard_map/ppermute | solution.py:49
  35.3 3.9 %input_own.1._.own_ref = f32[4,4,32,256]{3,2,1,0:T(8,128)S(1)} custom-call(bf16[4,4,128,256]{3,2,1,0:T(8,128)(2,1)S(1)} %get-tuple-element.39.pg_ref, bf16[6,4,128,256]{3,2,1,0:T(8,128)(2,1)} %copy-done, bf16[3,3,256,256]{3,2,1,0:T(8,128)(2,1)S(1)} %get-tuple-element.32.ws_ref, bf16[12,128,256]{2,1,0:T(8,128)(2,1)} %add_halves.1._), custom_call_target="tpu_custom_call" | custom-call | flops 1610612736 | bytes 4194304 | tf_op jit(solution)/shard_map/input_own/pallas_call | solution.py:389
  39.3 3.2 %all-to-all-done.got_ref = bf16[8,192,256]{2,1,0:T(8,128)(2,1)S(1)} async-done(((bf16[8,192,256]{2,1,0:T(8,128)(2,1)}), bf16[8,192,256]{2,1,0:T(8,128)(2,1)S(1)}, u32[]{:S(2)}, u32[]{:S(2)}) %all-to-all-start) | async-done | bytes 786464 | tf_op jit(solution)/shard_map/all_to_all | solution.py:43
  42.5 0.1 sum_parts.1._.own_ref
  42.6 1.8 %collective-permute-start.7 = (bf16[192,256]{1,0:T(8,128)(2,1)S(1)}, bf16[192,256]{1,0:T(8,128)(2,1)S(1)}, u32[]{:S(2)}, u32[]{:S(2)}) collective-permute-start(bf16[192,256]{1,0:T(8,128)(2,1)S(1)} %sum_parts.1._.own_ref), channel_id=1, source_target_pairs={{0,2},{2,0},{1,3},{3,1},{4,6},{6,4},{5,7},{7,5},{8,10},{10,8},{9,1... | collective-permute-start | bytes 294920 | tf_op jit(solution)/shard_map/ppermute | solution.py:34
  44.4 0.0 collective-permute-done.4.inner_hbm
  44.4 0.0 collective-permute-done.5.outer_hbm
  44.4 0.0 collective-permute-done.6.edge_hbm
  44.4 6.3 %finish.1 = (bf16[4,8,64,256]{3,2,1,0:T(8,128)(2,1)}, bf16[4,4,32,256]{3,2,1,0:T(8,128)(2,1)}, f32[8,128]{1,0:T(8,128)S(1)}) custom-call(s32[2]{0:T(128)S(1)} %pad_add_fusion.place_ref, f32[4,4,32,256]{3,2,1,0:T(8,128)S(1)} %input_own.1._.own_ref, bf16[3,3,256,256]{3,2,1,0:T(8,128)(2,1)S(1)} %get-tuple-element.32.ws_ref, ...), custom_call_target="tpu_custom_call" | custom-call | flops 2147483648 | bytes 4194304 | tf_op jit(solution)/shard_map/finish/pallas_call | solution.py:470
  50.8 0.0 collective-permute-done.7.theirs_ref
  50.8 0.1 spread.1
  50.8 13.9 %all_to_all.10 = bf16[8,192,256]{2,1,0:T(8,128)(2,1)S(1)} all-to-all(bf16[8,192,256]{2,1,0:T(8,128)(2,1)S(1)} %spread.1), channel_id=1, replica_groups=mesh['dp0'=2,'tm1'=2,'tm0'=2,'height1'=2,'height0'=2] {'dp0','tm1','heig..., dimensions={0} | all-to-all | bytes 1572864 | tf_op jit(solution)/shard_map/all_to_all | solution.py:43
  64.7 0.0 collective-permute-start.8
  64.7 1.8 %put.2 = (f32[3,3,256,256]{3,2,1,0:T(8,128)}, f32[3,256,256]{2,1,0:T(8,128)}) custom-call(s32[2]{0:T(128)S(1)} %pad_add_fusion.place_ref, bf16[12,128,256]{2,1,0:T(8,128)(2,1)S(1)} %bitcast.10), custom_call_target="tpu_custom_call" | custom-call | tf_op jit(solution)/shard_map/put/pallas_call | solution.py:503
  66.5 0.5 collective-permute-done.8.half_ref
  67.0 1.8 %put.3 = (f32[3,3,256,256]{3,2,1,0:T(8,128)}, f32[3,256,256]{2,1,0:T(8,128)}) custom-call(s32[2]{0:T(128)S(1)} %pad_add_fusion.1.place_ref, bf16[12,128,256]{2,1,0:T(8,128)(2,1)S(1)} %collective-permute-done.8.half_ref, f32[3,3,256,256]{3,2,1,0:T(8,128)} %get-tuple-element.50.refs_0_, ...), custom_call_target="tpu_custom_call", output_to_operand_aliasing={{0}: (2, {}), {1}: (3, {})} | custom-call | tf_op jit(solution)/shard_map/put/pallas_call | solution.py:503
Async XLA Ops:
  2.5 10.0 %collective-permute-start.2 = (bf16[2,8,64,256]{3,2,1,0:T(8,128)(2,1)S(1)}, bf16[2,8,64,256]{3,2,1,0:T(8,128)(2,1)S(1)}, u32[]{:S(2)}, u32[]{:S(2)}) collective-permute-start(bf16[2,8,64,256]{3,2,1,0:T(8,128)(2,1)S(1)} %get-tuple-element.36), channel_id=1, source_target_pairs={{4,0},{8,4},{12,8},{5,1},{9,5},{13,9},{6,2},{10,6},{14,10},{7,3},{... | collective-permute-start | bytes 1572872 | tf_op jit(solution)/shard_map/ppermute | solution.py:40
  3.8 6.2 %collective-permute-start = (bf16[4,1,32,256]{3,2,1,0:T(8,128)(2,1)S(1)}, bf16[4,1,32,256]{3,2,1,0:T(8,128)(2,1)S(1)}, u32[]{:S(2)}, u32[]{:S(2)}) collective-permute-start(bf16[4,1,32,256]{3,2,1,0:T(8,128)(2,1)S(1)} %get-tuple-element.30), channel_id=1, source_target_pairs={{0,1},{1,0},{2,3},{3,2},{4,5},{5,4},{6,7},{7,6},{8,9},{9,8},{10,11... | collective-permute-start | bytes 196616 | tf_op jit(solution)/shard_map/ppermute | solution.py:34
  6.8 3.1 %collective-permute-start.1 = (bf16[4,1,32,256]{3,2,1,0:T(8,128)(2,1)S(1)}, bf16[4,1,32,256]{3,2,1,0:T(8,128)(2,1)S(1)}, u32[]{:S(2)}, u32[]{:S(2)}) collective-permute-start(bf16[4,1,32,256]{3,2,1,0:T(8,128)(2,1)S(1)} %get-tuple-element.31), channel_id=1, source_target_pairs={{1,2},{2,1},{5,6},{6,5},{9,10},{10,9},{13,14},{14,13},{17,18},{18,... | collective-permute-start | bytes 196616 | tf_op jit(solution)/shard_map/ppermute | solution.py:49
  15.8 4.3 %copy-start = (bf16[6,4,128,256]{3,2,1,0:T(8,128)(2,1)}, bf16[6,4,128,256]{3,2,1,0:T(8,128)(2,1)S(1)}, u32[]{:S(2)}) copy-start(bf16[6,4,128,256]{3,2,1,0:T(8,128)(2,1)S(1)} %get-tuple-element.40.ext_ref.ext_hbm) | copy-start | bytes 4718596
  15.8 4.9 %collective-permute-start.3 = (f32[12,128,256]{2,1,0:T(8,128)S(1)}, f32[12,128,256]{2,1,0:T(8,128)S(1)}, u32[]{:S(2)}, u32[]{:S(2)}) collective-permute-start(f32[12,128,256]{2,1,0:T(8,128)S(1)} %get-tuple-element.42), channel_id=1, source_target_pairs={{0,4},{4,0},{1,5},{5,1},{2,6},{6,2},{3,7},{7,3},{8,12},{12,8},{9,1... | collective-permute-start | bytes 4718600 | tf_op jit(solution)/shard_map/ppermute | solution.py:34
  21.8 20.7 %all-to-all-start = ((bf16[8,192,256]{2,1,0:T(8,128)(2,1)}), bf16[8,192,256]{2,1,0:T(8,128)(2,1)S(1)}, u32[]{:S(2)}, u32[]{:S(2)}) async-start(bf16[8,192,256]{2,1,0:T(8,128)(2,1)} %bitcast.5), calls=%async_computation | async-start | bytes 1572864 | tf_op jit(solution)/shard_map/all_to_all | solution.py:43
  29.8 14.6 %collective-permute-start.6 = (bf16[2,6,32,256]{3,2,1,0:T(8,128)(2,1)}, bf16[2,6,32,256]{3,2,1,0:T(8,128)(2,1)}, u32[]{:S(2)}, u32[]{:S(2)}) collective-permute-start(bf16[2,6,32,256]{3,2,1,0:T(8,128)(2,1)} %get-tuple-element.45), channel_id=1, source_target_pairs={{0,4},{4,8},{8,12},{1,5},{5,9},{9,13},{2,6},{6,10},{10,14},{3,7},{... | collective-permute-start | bytes 589832 | tf_op jit(solution)/shard_map/ppermute | solution.py:40
  32.3 12.1 %collective-permute-start.4 = (bf16[4,2,32,256]{3,2,1,0:T(8,128)(2,1)}, bf16[4,2,32,256]{3,2,1,0:T(8,128)(2,1)}, u32[]{:S(2)}, u32[]{:S(2)}) collective-permute-start(bf16[4,2,32,256]{3,2,1,0:T(8,128)(2,1)} %get-tuple-element.43), channel_id=1, source_target_pairs={{0,1},{1,0},{2,3},{3,2},{4,5},{5,4},{6,7},{7,6},{8,9},{9,8},{10,11... | collective-permute-start | bytes 393224 | tf_op jit(solution)/shard_map/ppermute | solution.py:34
  34.0 10.4 %collective-permute-start.5 = (bf16[4,2,32,256]{3,2,1,0:T(8,128)(2,1)}, bf16[4,2,32,256]{3,2,1,0:T(8,128)(2,1)}, u32[]{:S(2)}, u32[]{:S(2)}) collective-permute-start(bf16[4,2,32,256]{3,2,1,0:T(8,128)(2,1)} %get-tuple-element.44), channel_id=1, source_target_pairs={{1,2},{2,1},{5,6},{6,5},{9,10},{10,9},{13,14},{14,13},{17,18},{18,... | collective-permute-start | bytes 393224 | tf_op jit(solution)/shard_map/ppermute | solution.py:49
  42.6 8.2 %collective-permute-start.7 = (bf16[192,256]{1,0:T(8,128)(2,1)S(1)}, bf16[192,256]{1,0:T(8,128)(2,1)S(1)}, u32[]{:S(2)}, u32[]{:S(2)}) collective-permute-start(bf16[192,256]{1,0:T(8,128)(2,1)S(1)} %sum_parts.1._.own_ref), channel_id=1, source_target_pairs={{0,2},{2,0},{1,3},{3,1},{4,6},{6,4},{5,7},{7,5},{8,10},{10,8},{9,1... | collective-permute-start | bytes 294920 | tf_op jit(solution)/shard_map/ppermute | solution.py:34
  64.7 2.3 %collective-permute-start.8 = (bf16[12,128,256]{2,1,0:T(8,128)(2,1)S(1)}, bf16[12,128,256]{2,1,0:T(8,128)(2,1)S(1)}, u32[]{:S(2)}, u32[]{:S(2)}) collective-permute-start(bf16[12,128,256]{2,1,0:T(8,128)(2,1)S(1)} %bitcast.9), channel_id=1, source_target_pairs={{0,4},{4,0},{1,5},{5,1},{2,6},{6,2},{3,7},{7,3},{8,12},{12,8},{9,1... | collective-permute-start | bytes 2359304 | tf_op jit(solution)/shard_map/ppermute | solution.py:34

commit v18 on v15

--- a/solution.py
+++ b/solution.py
@@ -165,15 +165,17 @@
         out_ref[9 + k] = product(act, ext_ref[k : k + frames].reshape(frames * 4 * count, chan))
 
 
-def half_kernel(place_ref, low_ref, inner_ref, outer_ref, act_ref, pg_ref, ext_ref, out_ref, act_out, sem):
+def half_kernel(place_ref, low_ref, inner_ref, outer_ref, act_ref, pg_ref, ext_ref, out_ref, act_out, box_ref, sem):
     copy = pltpu.make_async_copy(act_ref, act_out, sem)
     copy.start()
+    for frame in range(box_ref.shape[0]):
+        box_ref[frame] = sum(ext_ref[frame, side].astype(jnp.float32) for side in range(4))
     half_sums(place_ref, low_ref, inner_ref, outer_ref, act_ref, pg_ref, ext_ref, out_ref)
     copy.wait()
 
 
 def backward_kernel(place_ref, low_ref, inner_ref, outer_ref, act_ref, slope_ref, cot_ref, later_ref, turned_ref, sort_ref,
-                    pg_ref, ext_ref, out_ref, box_ref):
+                    pg_ref, ext_ref, out_ref):
     frames, _, count, chan = cot_ref.shape
     ext_ref[:frames] = cot_ref[...]
     for n in range(2):
@@ -183,7 +185,6 @@
         act_grad = product(jnp.concatenate(cots, axis=1), turned_ref[...])
         slope = slope_ref[frame].reshape(4 * count, chan)
         pg_ref[frame] = (act_grad * slope).astype(jnp.bfloat16).reshape(4, count, chan)
-        box_ref[frame] = sum(cot_ref[frame, side].astype(jnp.float32) for side in range(4))
     half_sums(place_ref, low_ref, inner_ref, outer_ref, act_ref, pg_ref, ext_ref, out_ref)
 
 
@@ -321,9 +322,8 @@
     return pl.pallas_call(
         backward_kernel,
         in_specs=[SCALAR] + [FULL] * 9,
-        out_specs=[FULL] * 4,
-        out_shape=[like(act.shape, jnp.bfloat16), like(ext, jnp.bfloat16), like((12, chan // 2, chan), jnp.float32),
-                   like((frames, count, chan), jnp.float32)],
+        out_specs=[FULL] * 3,
+        out_shape=[like(act.shape, jnp.bfloat16), like(ext, jnp.bfloat16), like((12, chan // 2, chan), jnp.float32)],
         compiler_params=grant(24),
         cost_estimate=cost(15, 10),
         name="backward",
@@ -335,8 +335,9 @@
     return pl.pallas_call(
         half_kernel,
         in_specs=[SCALAR] + [FULL] * 6,
-        out_specs=[FULL, HBM],
-        out_shape=[like((12, chan // 2, chan), jnp.float32), pltpu.HBM(act.shape, act.dtype)],
+        out_specs=[FULL, HBM, FULL],
+        out_shape=[like((12, chan // 2, chan), jnp.float32), pltpu.HBM(act.shape, act.dtype),
+                   like((act.shape[0],) + act.shape[2:], jnp.float32)],
         scratch_shapes=[pltpu.SemaphoreType.DMA],
         compiler_params=grant(20),
         cost_estimate=cost(10, 6),
@@ -573,11 +574,11 @@
     order = jnp.asarray(side_order(rows_low, cols_low))
     low_in, ws, sort, turned, cot_side = load(low, cot, spatial_weight, temporal_weight, order)
     act, slope = forward(mine, low_in, inner, outer, ws)
-    pg, ext, theirs, box = backward(
+    pg, ext, theirs = backward(
         other, low_in, inner, outer, act, slope, cot_side, later, turned, sort
     )
     theirs = bits.swap(theirs, bits.core)
-    own, act = half_grads(mine, low_in, inner, outer, act, pg, ext)
+    own, act, box = half_grads(mine, low_in, inner, outer, act, pg, ext)
     kept = add_halves(own, theirs)
     got = bits.exchange(kept.reshape(parts, -1, chan))
     edge, pg_inner, pg_outer = edges(mine, low_in, inner, outer, pg, kept)

time: 69.8 us -> 69 us (0.989)
  local copies, waits for them, and re-layouts: 0.79 us -> 0.01 us
    unnamed x4, local copies, waits for them, and re-layouts: 0.79 us -> 0.01 us
  transfers between devices with their start and end apart: 10 -> 10, of which waited for: 3 -> 3; matrix products, arithmetic and copies ran while one was open for 0% -> 0% of each run, Pallas kernels for 26% -> 27%
where the time goes in v18:
time: 69 us; the launch traced here: 68.6 us
  Pallas kernels  26.5 us (38%)
  starting transfers between devices  20.9 us (30%)
  blocking collectives  13.5 us (20%)
  waiting for transfers between devices  6.47 us (9%)
  between operations  0.94 us (1%)
    all_to_all x1, blocking collectives, exchange(): return lax.all_to_all(parts, tuple(self.near), 0, 0, tiled=True)  13.5 us
    ppermute x5, starting transfers between devices, swap(): return lax.ppermute(block, axis, [(0, 1), (1, 0)])  8.53 us
    all_to_all x1, starting transfers between devices, exchange(): return lax.all_to_all(parts, tuple(self.near), 0, 0, tiled=True)  6.73 us
    pallas_call x1, Pallas kernels, finish(): pl.pallas_call(finish_kernel, in_specs=[SCALAR, FULL, FULL] + [HBM] * 7 +...  6.32 us
    all_to_all x1, waiting for transfers between devices, exchange(): return lax.all_to_all(parts, tuple(self.near), 0, 0, tiled=True)  5.63 us
    ppermute x2, starting transfers between devices, shift(): return lax.ppermute(block, axes, route)  3.71 us
    pallas_call x2, Pallas kernels, put(): pl.pallas_call(put_kernel, in_specs=[SCALAR, FULL] + [HBM] * len(done), o...  3.56 us
    pallas_call x1, Pallas kernels, backward(): pl.pallas_call(backward_kernel, in_specs=[SCALAR] + [FULL] * 9, out_specs...  3.35 us
  transfers between devices with their start and end apart: 10, of which 3 were waited for; matrix products, arithmetic and copies ran while one was open for 0% of the time, Pallas kernels for 27%

profile of v18, /device:TPU:0, one launch (start us, length us, event | category | flops | bytes accessed | tf_op | source)
XLA Modules:
  0.0 68.6 jit_solution(5886593655561464975)
XLA Ops:
  0.6 0.1 pad_add_fusion.place_ref
  0.7 1.7 %first_messages.1 = (bf16[4,1,32,256]{3,2,1,0:T(8,128)(2,1)S(1)}, bf16[4,1,32,256]{3,2,1,0:T(8,128)(2,1)S(1)}, bf16[2,8,64,256]{3,2,1,0:T(8,128)(2,1)S(1)}) custom-call(s32[2]{0:T(128)S(1)} %pad_add_fusion.place_ref, bf16[4,4,32,256]{3,2,1,0:T(8,128)(2,1)} %bitcast.13, bf16[4,8,64,256]{3,2,1,0:T(8,128)(2,1)} %bitcast.11), custom_call_target="tpu_custom_call" | custom-call | tf_op jit(solution)/shard_map/first_messages/pallas_call | solution.py:230
  2.5 1.3 %collective-permute-start.2 = (bf16[2,8,64,256]{3,2,1,0:T(8,128)(2,1)S(1)}, bf16[2,8,64,256]{3,2,1,0:T(8,128)(2,1)S(1)}, u32[]{:S(2)}, u32[]{:S(2)}) collective-permute-start(bf16[2,8,64,256]{3,2,1,0:T(8,128)(2,1)S(1)} %get-tuple-element.37), channel_id=1, source_target_pairs={{4,0},{8,4},{12,8},{5,1},{9,5},{13,9},{6,2},{10,6},{14,10},{7,3},{... | collective-permute-start | bytes 1572872 | tf_op jit(solution)/shard_map/ppermute | solution.py:40
  3.8 3.1 %collective-permute-start = (bf16[4,1,32,256]{3,2,1,0:T(8,128)(2,1)S(1)}, bf16[4,1,32,256]{3,2,1,0:T(8,128)(2,1)S(1)}, u32[]{:S(2)}, u32[]{:S(2)}) collective-permute-start(bf16[4,1,32,256]{3,2,1,0:T(8,128)(2,1)S(1)} %get-tuple-element.31), channel_id=1, source_target_pairs={{0,1},{1,0},{2,3},{3,2},{4,5},{5,4},{6,7},{7,6},{8,9},{9,8},{10,11... | collective-permute-start | bytes 196616 | tf_op jit(solution)/shard_map/ppermute | solution.py:34
  6.8 0.7 collective-permute-start.1
  7.5 0.1 pad_add_fusion.1.place_ref
  7.6 2.4 %load.1 = (bf16[4,4,32,256]{3,2,1,0:T(8,128)(2,1)S(1)}, bf16[3,3,256,256]{3,2,1,0:T(8,128)(2,1)S(1)}, bf16[256,256]{1,0:T(8,128)(2,1)S(1)}, bf16[768,256]{1,0:T(8,128)(2,1)S(1)}, bf16[4,4,128,256]{3,2,1,0:T(8,128)(2,1)S(1)}) custom-call(bf16[4,4,32,256]{3,2,1,0:T(8,128)(2,1)} %bitcast.14, bf16[4,8,64,256]{3,2,1,0:T(8,128)(2,1)} %bitcast.12, ...), custom_call_target="tpu_custom_call" | custom-call | flops 536870912 | bytes 4194304 | tf_op jit(solution)/shard_map/load/pallas_call | solution.py:267
  10.0 0.0 collective-permute-done.inner_ref
  10.0 0.0 collective-permute-done.1.outer_ref
  10.0 2.4 %forward.1 = (bf16[4,4,128,256]{3,2,1,0:T(8,128)(2,1)S(1)}, f32[4,4,128,256]{3,2,1,0:T(8,128)S(1)}) custom-call(s32[2]{0:T(128)S(1)} %pad_add_fusion.place_ref, bf16[4,4,32,256]{3,2,1,0:T(8,128)(2,1)S(1)} %get-tuple-element.30.low_ref, bf16[4,1,32,256]{3,2,1,0:T(8,128)(2,1)S(1)} %collective-permute-done.inner_ref, ...), custom_call_target="tpu_custom_call" | custom-call | flops 2684354560 | bytes 8388608 | tf_op jit(solution)/shard_map/forward/pallas_call | solution.py:283
  12.4 0.0 collective-permute-done.2.later_ref
  12.4 3.3 %backward.1 = (bf16[4,4,128,256]{3,2,1,0:T(8,128)(2,1)S(1)}, bf16[6,4,128,256]{3,2,1,0:T(8,128)(2,1)S(1)}, f32[12,128,256]{2,1,0:T(8,128)S(1)}) custom-call(s32[2]{0:T(128)S(1)} %pad_add_fusion.1.place_ref, bf16[4,4,32,256]{3,2,1,0:T(8,128)(2,1)S(1)} %get-tuple-element.30.low_ref, bf16[4,1,32,256]{3,2,1,0:T(8,128)(2,1)S(1)} %collective-permute-done.inner_ref, ...), custom_call_target="tpu_custom_call" | custom-call | flops 4026531840 | bytes 10485760 | tf_op jit(solution)/shard_map/backward/pallas_call | solution.py:322
  15.8 1.9 %collective-permute-start.3 = (f32[12,128,256]{2,1,0:T(8,128)S(1)}, f32[12,128,256]{2,1,0:T(8,128)S(1)}, u32[]{:S(2)}, u32[]{:S(2)}) collective-permute-start(f32[12,128,256]{2,1,0:T(8,128)S(1)} %get-tuple-element.44), channel_id=1, source_target_pairs={{0,4},{4,0},{1,5},{5,1},{2,6},{6,2},{3,7},{7,3},{8,12},{12,8},{9,1... | collective-permute-start | bytes 4718600 | tf_op jit(solution)/shard_map/ppermute | solution.py:34
  17.7 2.7 %half_grads.1 = (f32[12,128,256]{2,1,0:T(8,128)S(1)}, bf16[4,4,128,256]{3,2,1,0:T(8,128)(2,1)}, f32[4,128,256]{2,1,0:T(8,128)S(1)}) custom-call(s32[2]{0:T(128)S(1)} %pad_add_fusion.place_ref, bf16[4,4,32,256]{3,2,1,0:T(8,128)(2,1)S(1)} %get-tuple-element.30.low_ref, bf16[4,1,32,256]{3,2,1,0:T(8,128)(2,1)S(1)} %collective-permute-done.inner_ref, ...), custom_call_target="tpu_custom_call" | custom-call | flops 2684354560 | bytes 6291456 | tf_op jit(solution)/shard_map/half_grads/pallas_call | solution.py:335
  20.4 0.0 copy-start
  20.4 0.3 collective-permute-done.3.theirs_ref
  20.7 1.0 %add_halves.1._ = bf16[12,128,256]{2,1,0:T(8,128)(2,1)} custom-call(f32[12,128,256]{2,1,0:T(8,128)S(1)} %get-tuple-element.43.mine_ref, f32[12,128,256]{2,1,0:T(8,128)S(1)} %collective-permute-done.3.theirs_ref), custom_call_target="tpu_custom_call" | custom-call | tf_op jit(solution)/shard_map/add_halves/pallas_call | solution.py:518
  21.7 0.0 copy-done
  21.7 6.7 %all-to-all-start = ((bf16[8,192,256]{2,1,0:T(8,128)(2,1)}), bf16[8,192,256]{2,1,0:T(8,128)(2,1)S(1)}, u32[]{:S(2)}, u32[]{:S(2)}) async-start(bf16[8,192,256]{2,1,0:T(8,128)(2,1)} %bitcast.5), calls=%async_computation | async-start | bytes 1572864 | tf_op jit(solution)/shard_map/all_to_all | solution.py:43
  28.5 0.0 copy-start.1
  28.5 1.3 %edges.1 = (bf16[2,6,32,256]{3,2,1,0:T(8,128)(2,1)}, bf16[4,2,32,256]{3,2,1,0:T(8,128)(2,1)}, bf16[4,2,32,256]{3,2,1,0:T(8,128)(2,1)}) custom-call(s32[2]{0:T(128)S(1)} %pad_add_fusion.place_ref, bf16[4,4,32,256]{3,2,1,0:T(8,128)(2,1)S(1)} %get-tuple-element.30.low_ref, bf16[4,1,32,256]{3,2,1,0:T(8,128)(2,1)S(1)} %collective-permute-done.inner_ref, ...), custom_call_target="tpu_custom_call" | custom-call | tf_op jit(solution)/shard_map/edges/pallas_call | solution.py:309
  29.8 2.4 %collective-permute-start.6 = (bf16[2,6,32,256]{3,2,1,0:T(8,128)(2,1)}, bf16[2,6,32,256]{3,2,1,0:T(8,128)(2,1)}, u32[]{:S(2)}, u32[]{:S(2)}) collective-permute-start(bf16[2,6,32,256]{3,2,1,0:T(8,128)(2,1)} %get-tuple-element.47), channel_id=1, source_target_pairs={{0,4},{4,8},{8,12},{1,5},{5,9},{9,13},{2,6},{6,10},{10,14},{3,7},{... | collective-permute-start | bytes 589832 | tf_op jit(solution)/shard_map/ppermute | solution.py:40
  32.2 1.7 %collective-permute-start.4 = (bf16[4,2,32,256]{3,2,1,0:T(8,128)(2,1)}, bf16[4,2,32,256]{3,2,1,0:T(8,128)(2,1)}, u32[]{:S(2)}, u32[]{:S(2)}) collective-permute-start(bf16[4,2,32,256]{3,2,1,0:T(8,128)(2,1)} %get-tuple-element.45), channel_id=1, source_target_pairs={{0,1},{1,0},{2,3},{3,2},{4,5},{5,4},{6,7},{7,6},{8,9},{9,8},{10,11... | collective-permute-start | bytes 393224 | tf_op jit(solution)/shard_map/ppermute | solution.py:34
  34.0 1.3 %collective-permute-start.5 = (bf16[4,2,32,256]{3,2,1,0:T(8,128)(2,1)}, bf16[4,2,32,256]{3,2,1,0:T(8,128)(2,1)}, u32[]{:S(2)}, u32[]{:S(2)}) collective-permute-start(bf16[4,2,32,256]{3,2,1,0:T(8,128)(2,1)} %get-tuple-element.46), channel_id=1, source_target_pairs={{1,2},{2,1},{5,6},{6,5},{9,10},{10,9},{13,14},{14,13},{17,18},{18,... | collective-permute-start | bytes 393224 | tf_op jit(solution)/shard_map/ppermute | solution.py:49
  35.3 0.0 copy-done.1
  35.3 1.6 %input_own.1._.own_ref = f32[4,4,32,256]{3,2,1,0:T(8,128)S(1)} custom-call(bf16[4,4,128,256]{3,2,1,0:T(8,128)(2,1)S(1)} %get-tuple-element.40.pg_ref, f32[4,128,256]{2,1,0:T(8,128)S(1)} %copy-done.1, bf16[3,3,256,256]{3,2,1,0:T(8,128)(2,1)S(1)} %get-tuple-element.33.ws_ref, bf16[12,128,256]{2,1,0:T(8,128)(2,1)} %add_halves.1._), custom_call_target="tpu_custom_call" | custom-call | flops 1610612736 | bytes 4194304 | tf_op jit(solution)/shard_map/input_own/pallas_call | solution.py:387
  36.9 5.6 %all-to-all-done.got_ref = bf16[8,192,256]{2,1,0:T(8,128)(2,1)S(1)} async-done(((bf16[8,192,256]{2,1,0:T(8,128)(2,1)}), bf16[8,192,256]{2,1,0:T(8,128)(2,1)S(1)}, u32[]{:S(2)}, u32[]{:S(2)}) %all-to-all-start) | async-done | bytes 786464 | tf_op jit(solution)/shard_map/all_to_all | solution.py:43
  42.5 0.1 sum_parts.1._.own_ref
  42.6 1.8 %collective-permute-start.7 = (bf16[192,256]{1,0:T(8,128)(2,1)S(1)}, bf16[192,256]{1,0:T(8,128)(2,1)S(1)}, u32[]{:S(2)}, u32[]{:S(2)}) collective-permute-start(bf16[192,256]{1,0:T(8,128)(2,1)S(1)} %sum_parts.1._.own_ref), channel_id=1, source_target_pairs={{0,2},{2,0},{1,3},{3,1},{4,6},{6,4},{5,7},{7,5},{8,10},{10,8},{9,1... | collective-permute-start | bytes 294920 | tf_op jit(solution)/shard_map/ppermute | solution.py:34
  44.4 0.0 collective-permute-done.4.inner_hbm
  44.4 0.0 collective-permute-done.5.outer_hbm
  44.4 0.0 collective-permute-done.6.edge_hbm
  44.4 6.3 %finish.1 = (bf16[4,8,64,256]{3,2,1,0:T(8,128)(2,1)}, bf16[4,4,32,256]{3,2,1,0:T(8,128)(2,1)}, f32[8,128]{1,0:T(8,128)S(1)}) custom-call(s32[2]{0:T(128)S(1)} %pad_add_fusion.place_ref, f32[4,4,32,256]{3,2,1,0:T(8,128)S(1)} %input_own.1._.own_ref, bf16[3,3,256,256]{3,2,1,0:T(8,128)(2,1)S(1)} %get-tuple-element.33.ws_ref, ...), custom_call_target="tpu_custom_call" | custom-call | flops 2147483648 | bytes 4194304 | tf_op jit(solution)/shard_map/finish/pallas_call | solution.py:467
  50.7 0.0 collective-permute-done.7.theirs_ref
  50.8 0.1 spread.1
  50.8 13.5 %all_to_all.10 = bf16[8,192,256]{2,1,0:T(8,128)(2,1)S(1)} all-to-all(bf16[8,192,256]{2,1,0:T(8,128)(2,1)S(1)} %spread.1), channel_id=1, replica_groups=mesh['dp0'=2,'tm1'=2,'tm0'=2,'height1'=2,'height0'=2] {'dp0','tm1','heig..., dimensions={0} | all-to-all | bytes 1572864 | tf_op jit(solution)/shard_map/all_to_all | solution.py:43
  64.4 0.0 collective-permute-start.8
  64.4 1.8 %put.2 = (f32[3,3,256,256]{3,2,1,0:T(8,128)}, f32[3,256,256]{2,1,0:T(8,128)}) custom-call(s32[2]{0:T(128)S(1)} %pad_add_fusion.place_ref, bf16[12,128,256]{2,1,0:T(8,128)(2,1)S(1)} %bitcast.10), custom_call_target="tpu_custom_call" | custom-call | tf_op jit(solution)/shard_map/put/pallas_call | solution.py:500
  66.2 0.5 collective-permute-done.8.half_ref
  66.7 1.8 %put.3 = (f32[3,3,256,256]{3,2,1,0:T(8,128)}, f32[3,256,256]{2,1,0:T(8,128)}) custom-call(s32[2]{0:T(128)S(1)} %pad_add_fusion.1.place_ref, bf16[12,128,256]{2,1,0:T(8,128)(2,1)S(1)} %collective-permute-done.8.half_ref, f32[3,3,256,256]{3,2,1,0:T(8,128)} %get-tuple-element.52.refs_0_, ...), custom_call_target="tpu_custom_call", output_to_operand_aliasing={{0}: (2, {}), {1}: (3, {})} | custom-call | tf_op jit(solution)/shard_map/put/pallas_call | solution.py:500
Async XLA Ops:
  2.5 10.0 %collective-permute-start.2 = (bf16[2,8,64,256]{3,2,1,0:T(8,128)(2,1)S(1)}, bf16[2,8,64,256]{3,2,1,0:T(8,128)(2,1)S(1)}, u32[]{:S(2)}, u32[]{:S(2)}) collective-permute-start(bf16[2,8,64,256]{3,2,1,0:T(8,128)(2,1)S(1)} %get-tuple-element.37), channel_id=1, source_target_pairs={{4,0},{8,4},{12,8},{5,1},{9,5},{13,9},{6,2},{10,6},{14,10},{7,3},{... | collective-permute-start | bytes 1572872 | tf_op jit(solution)/shard_map/ppermute | solution.py:40
  3.8 6.2 %collective-permute-start = (bf16[4,1,32,256]{3,2,1,0:T(8,128)(2,1)S(1)}, bf16[4,1,32,256]{3,2,1,0:T(8,128)(2,1)S(1)}, u32[]{:S(2)}, u32[]{:S(2)}) collective-permute-start(bf16[4,1,32,256]{3,2,1,0:T(8,128)(2,1)S(1)} %get-tuple-element.31), channel_id=1, source_target_pairs={{0,1},{1,0},{2,3},{3,2},{4,5},{5,4},{6,7},{7,6},{8,9},{9,8},{10,11... | collective-permute-start | bytes 196616 | tf_op jit(solution)/shard_map/ppermute | solution.py:34
  6.8 3.1 %collective-permute-start.1 = (bf16[4,1,32,256]{3,2,1,0:T(8,128)(2,1)S(1)}, bf16[4,1,32,256]{3,2,1,0:T(8,128)(2,1)S(1)}, u32[]{:S(2)}, u32[]{:S(2)}) collective-permute-start(bf16[4,1,32,256]{3,2,1,0:T(8,128)(2,1)S(1)} %get-tuple-element.32), channel_id=1, source_target_pairs={{1,2},{2,1},{5,6},{6,5},{9,10},{10,9},{13,14},{14,13},{17,18},{18,... | collective-permute-start | bytes 196616 | tf_op jit(solution)/shard_map/ppermute | solution.py:49
  15.8 4.9 %collective-permute-start.3 = (f32[12,128,256]{2,1,0:T(8,128)S(1)}, f32[12,128,256]{2,1,0:T(8,128)S(1)}, u32[]{:S(2)}, u32[]{:S(2)}) collective-permute-start(f32[12,128,256]{2,1,0:T(8,128)S(1)} %get-tuple-element.44), channel_id=1, source_target_pairs={{0,4},{4,0},{1,5},{5,1},{2,6},{6,2},{3,7},{7,3},{8,12},{12,8},{9,1... | collective-permute-start | bytes 4718600 | tf_op jit(solution)/shard_map/ppermute | solution.py:34
  20.4 1.4 %copy-start = (f32[4,128,256]{2,1,0:T(8,128)}, f32[4,128,256]{2,1,0:T(8,128)S(1)}, u32[]{:S(2)}) copy-start(f32[4,128,256]{2,1,0:T(8,128)S(1)} %get-tuple-element.42.box_ref) | copy-start | bytes 1572868
  21.7 20.7 %all-to-all-start = ((bf16[8,192,256]{2,1,0:T(8,128)(2,1)}), bf16[8,192,256]{2,1,0:T(8,128)(2,1)S(1)}, u32[]{:S(2)}, u32[]{:S(2)}) async-start(bf16[8,192,256]{2,1,0:T(8,128)(2,1)} %bitcast.5), calls=%async_computation | async-start | bytes 1572864 | tf_op jit(solution)/shard_map/all_to_all | solution.py:43
  28.5 6.8 %copy-start.1 = (f32[4,128,256]{2,1,0:T(8,128)S(1)}, f32[4,128,256]{2,1,0:T(8,128)}, u32[]{:S(2)}) copy-start(f32[4,128,256]{2,1,0:T(8,128)} %copy-done) | copy-start | bytes 1572868
  29.8 14.6 %collective-permute-start.6 = (bf16[2,6,32,256]{3,2,1,0:T(8,128)(2,1)}, bf16[2,6,32,256]{3,2,1,0:T(8,128)(2,1)}, u32[]{:S(2)}, u32[]{:S(2)}) collective-permute-start(bf16[2,6,32,256]{3,2,1,0:T(8,128)(2,1)} %get-tuple-element.47), channel_id=1, source_target_pairs={{0,4},{4,8},{8,12},{1,5},{5,9},{9,13},{2,6},{6,10},{10,14},{3,7},{... | collective-permute-start | bytes 589832 | tf_op jit(solution)/shard_map/ppermute | solution.py:40
  32.2 12.2 %collective-permute-start.4 = (bf16[4,2,32,256]{3,2,1,0:T(8,128)(2,1)}, bf16[4,2,32,256]{3,2,1,0:T(8,128)(2,1)}, u32[]{:S(2)}, u32[]{:S(2)}) collective-permute-start(bf16[4,2,32,256]{3,2,1,0:T(8,128)(2,1)} %get-tuple-element.45), channel_id=1, source_target_pairs={{0,1},{1,0},{2,3},{3,2},{4,5},{5,4},{6,7},{7,6},{8,9},{9,8},{10,11... | collective-permute-start | bytes 393224 | tf_op jit(solution)/shard_map/ppermute | solution.py:34
  34.0 10.4 %collective-permute-start.5 = (bf16[4,2,32,256]{3,2,1,0:T(8,128)(2,1)}, bf16[4,2,32,256]{3,2,1,0:T(8,128)(2,1)}, u32[]{:S(2)}, u32[]{:S(2)}) collective-permute-start(bf16[4,2,32,256]{3,2,1,0:T(8,128)(2,1)} %get-tuple-element.46), channel_id=1, source_target_pairs={{1,2},{2,1},{5,6},{6,5},{9,10},{10,9},{13,14},{14,13},{17,18},{18,... | collective-permute-start | bytes 393224 | tf_op jit(solution)/shard_map/ppermute | solution.py:49
  42.6 8.2 %collective-permute-start.7 = (bf16[192,256]{1,0:T(8,128)(2,1)S(1)}, bf16[192,256]{1,0:T(8,128)(2,1)S(1)}, u32[]{:S(2)}, u32[]{:S(2)}) collective-permute-start(bf16[192,256]{1,0:T(8,128)(2,1)S(1)} %sum_parts.1._.own_ref), channel_id=1, source_target_pairs={{0,2},{2,0},{1,3},{3,1},{4,6},{6,4},{5,7},{7,5},{8,10},{10,8},{9,1... | collective-permute-start | bytes 294920 | tf_op jit(solution)/shard_map/ppermute | solution.py:34
  64.4 2.3 %collective-permute-start.8 = (bf16[12,128,256]{2,1,0:T(8,128)(2,1)S(1)}, bf16[12,128,256]{2,1,0:T(8,128)(2,1)S(1)}, u32[]{:S(2)}, u32[]{:S(2)}) collective-permute-start(bf16[12,128,256]{2,1,0:T(8,128)(2,1)S(1)} %bitcast.9), channel_id=1, source_target_pairs={{0,4},{4,0},{1,5},{5,1},{2,6},{6,2},{3,7},{7,3},{8,12},{12,8},{9,1... | collective-permute-start | bytes 2359304 | tf_op jit(solution)/shard_map/ppermute | solution.py:34

commit v19 on v18

--- a/solution.py
+++ b/solution.py
@@ -112,14 +112,15 @@
 
 
 def spatial(low, ws_ref):
-    rows_low, cols_low, chan = low.shape[0] - 2, low.shape[1], low.shape[2]
-    count = rows_low * cols_low
+    frames, rows_tall, cols_low, chan = low.shape
+    rows_low = rows_tall - 2
+    count = frames * rows_low * cols_low
     flat = low.reshape(-1, chan)
     rows = [[], []]
     for j in range(3):
         taps = [product(flat, ws_ref[i, j]).reshape(low.shape) for i in range(3)]
-        even = taps[0][:rows_low] + (taps[1] + taps[2])[1 : rows_low + 1]
-        odd = (taps[0] + taps[1])[1 : rows_low + 1] + taps[2][2:]
+        even = taps[0][:, :rows_low] + (taps[1] + taps[2])[:, 1 : rows_low + 1]
+        odd = (taps[0] + taps[1])[:, 1 : rows_low + 1] + taps[2][:, 2:]
         rows[0].append(even.reshape(count, chan))
         rows[1].append(odd.reshape(count, chan))
     at = column(count, cols_low, chan)
@@ -129,12 +130,13 @@
 
 
 def forward_kernel(place_ref, low_ref, inner_ref, outer_ref, ws_ref, act_ref, slope_ref):
-    for frame in range(low_ref.shape[0]):
-        low = tall(place_ref, low_ref, inner_ref, outer_ref, frame)
-        for side, pre in enumerate(spatial(low, ws_ref)):
-            sig = jax.nn.sigmoid(pre)
-            act_ref[frame, side] = (pre * sig).astype(jnp.bfloat16)
-            slope_ref[frame, side] = sig * (1.0 + pre * (1.0 - sig))
+    frames, rows_low, cols_low, chan = low_ref.shape
+    shape = (frames, rows_low * cols_low, chan)
+    low = jnp.stack([tall(place_ref, low_ref, inner_ref, outer_ref, frame) for frame in range(frames)])
+    for side, pre in enumerate(spatial(low, ws_ref)):
+        sig = jax.nn.sigmoid(pre)
+        act_ref[:, side] = (pre * sig).astype(jnp.bfloat16).reshape(shape)
+        slope_ref[:, side] = (sig * (1.0 + pre * (1.0 - sig))).reshape(shape)
 
 
 def half_sums(place_ref, low_ref, inner_ref, outer_ref, act_ref, pg_ref, ext_ref, out_ref):
@@ -395,15 +397,15 @@
     )(pg, box, ws, before)
 
 
-def finish_kernel(place_ref, own_ref, ws_ref, inner_hbm, outer_hbm, edge_hbm, act_hbm, wt_hbm, sort_hbm, low_hbm, _,
+def finish_kernel(place_ref, own_ref, ws_ref, sort_ref, low_ref, inner_hbm, outer_hbm, edge_hbm, act_hbm, wt_hbm, _,
                   section_ref, input_ref, token_ref,
-                  inner_ref, outer_ref, edge_ref, act_ref, wt_ref, wide_ref, low_ref, earlier, held, input_held, sems):
+                  inner_ref, outer_ref, edge_ref, act_ref, wt_ref, earlier, held, input_held, sems):
     frames, rows_low, cols_low, chan = low_ref.shape
     group = rows_at_once(rows_low, cols_low)
     span, count = group * cols_low, rows_low * cols_low
     pairs = [(inner_hbm, inner_ref), (outer_hbm, outer_ref)]
     pairs += [(edge_hbm, edge_ref), (wt_hbm, wt_ref)]
-    pairs += [(act_hbm.at[n], act_ref.at[n]) for n in range(frames)] + [(sort_hbm, wide_ref), (low_hbm, low_ref)]
+    pairs += [(act_hbm.at[n], act_ref.at[n]) for n in range(frames)]
     copies = [pltpu.make_async_copy(a, b, sems.at[n]) for n, (a, b) in enumerate(pairs)]
     for copy in copies:
         copy.start()
@@ -420,12 +422,10 @@
     below = [jnp.where(odd_place, outer[b], inner[b]) for b in range(2)]
     terms = []
     for (first, second), i in ((above, 2), (below, 0)):
-        total = jnp.zeros(flat, jnp.float32)
-        for j in range(3):
-            parts = jnp.concatenate(split(column_pair(first, second, j, at, cols_low - 1)), axis=0)
-            sums = product_nt(parts, ws_ref[i, j])
-            total = total + (sums[: flat[0]] + sums[flat[0] :])
-        terms.append(total.reshape(frames, cols_low, chan))
+        parts = [split(column_pair(first, second, j, at, cols_low - 1)) for j in range(3)]
+        parts = jnp.concatenate([jnp.concatenate(part, axis=0) for part in parts], axis=1)
+        sums = product(parts, jnp.concatenate([ws_ref[i, j].T for j in range(3)], axis=0))
+        terms.append((sums[: flat[0]] + sums[flat[0] :]).reshape(frames, cols_low, chan))
     for row in range(rows_low):
         value = own_ref[:, row]
         if row == 0:
@@ -438,12 +438,11 @@
 
     for copy in copies[2:3]:
         copy.wait()
-    for frame in range(2):
-        for side, pre in enumerate(spatial(edge_ref[frame], ws_ref)):
-            earlier[frame, side] = (pre * jax.nn.sigmoid(pre)).astype(jnp.bfloat16)
+    for side, pre in enumerate(spatial(edge_ref[...], ws_ref)):
+        earlier[:, side] = (pre * jax.nn.sigmoid(pre)).astype(jnp.bfloat16).reshape(2, count, chan)
     for copy in copies[3:]:
         copy.wait()
-    merge = wide_ref[...].T.astype(jnp.bfloat16)
+    merge = sort_ref[...].T
     wt = wt_ref[...].reshape(3 * chan, chan)
     for frame in range(frames):
         acts = [act_ref[frame - k] if frame >= k else earlier[frame - k + 2] for k in range(3)]
@@ -460,13 +459,13 @@
         copy.wait()
 
 
-def finish(place, own, ws, inner, outer, edge, act, wt, sort, low, before):
+def finish(place, own, ws, sort, low, inner, outer, edge, act, wt, before):
     frames, rows_low, cols_low, chan = low.shape
     out = (frames, 2 * rows_low, 2 * cols_low, chan)
-    fetched = [inner, outer, edge, act, wt, sort, low]
+    fetched = [inner, outer, edge, act, wt]
     return pl.pallas_call(
         finish_kernel,
-        in_specs=[SCALAR, FULL, FULL] + [HBM] * 7 + [UNREAD],
+        in_specs=[SCALAR] + [FULL] * 4 + [HBM] * 5 + [UNREAD],
         out_specs=[HBM, HBM, FULL],
         out_shape=[like(out, jnp.bfloat16), like(low.shape, jnp.bfloat16), TOKEN],
         scratch_shapes=[pltpu.VMEM(a.shape, a.dtype) for a in fetched]
@@ -475,7 +474,7 @@
         compiler_params=grant(16),
         cost_estimate=cost(8, 4),
         name="finish",
-    )(place, own, ws, inner, outer, edge, *[in_hbm(a) for a in (act, wt, sort, low)], before)
+    )(place, own, ws, sort, low, inner, outer, edge, in_hbm(act), in_hbm(wt), before)
 
 
 def put_kernel(place_ref, half_ref, *refs):
@@ -587,7 +586,7 @@
     own_part = input_own(pg, box, ws, kept, low.shape)
     total, far = bits.far_sums(sum_parts(got, own_part))
     section_out, input_grad, done = finish(
-        mine, own_part, ws, pg_inner, pg_outer, edge, act, temporal_weight, order, low, total
+        mine, own_part, ws, sort, low_in, pg_inner, pg_outer, edge, act, temporal_weight, total
     )
     totals = spread(total, far, parts, done)
     half = bits.exchange(totals).reshape(kept.shape)

time: 69 us -> 69.5 us (level)
  local copies, waits for them, and re-layouts: 0.01 us -> 1.29 us
  waiting for transfers between devices: 6.47 us -> 7.62 us
  starting transfers between devices: 20.9 us -> 19.9 us
    unnamed x4 -> x10, local copies, waits for them, and re-layouts: 0.01 us -> 1.29 us
    all_to_all x1, waiting for transfers between devices: 5.63 us -> 6.81 us  [exchange(): return lax.all_to_all(parts, tuple(self.near), 0, 0, tiled=True)]
  transfers between devices with their start and end apart: 10 -> 10, of which waited for: 3 -> 3; matrix products, arithmetic and copies ran while one was open for 0% -> 0% of each run, Pallas kernels for 27% -> 26%
where the time goes in v19:
time: 69.5 us; the launch traced here: 69.1 us
  Pallas kernels  26 us (37%)
  starting transfers between devices  19.9 us (29%)
  blocking collectives  13.2 us (19%)
  waiting for transfers between devices  7.62 us (11%)
  local copies, waits for them, and re-layouts  1.29 us (2%)
  between operations  1.01 us (1%)
    all_to_all x1, blocking collectives, exchange(): return lax.all_to_all(parts, tuple(self.near), 0, 0, tiled=True)  13.2 us
    ppermute x5, starting transfers between devices, swap(): return lax.ppermute(block, axis, [(0, 1), (1, 0)])  8.66 us
    all_to_all x1, waiting for transfers between devices, exchange(): return lax.all_to_all(parts, tuple(self.near), 0, 0, tiled=True)  6.81 us
    all_to_all x1, starting transfers between devices, exchange(): return lax.all_to_all(parts, tuple(self.near), 0, 0, tiled=True)  6.65 us
    pallas_call x1, Pallas kernels, finish(): pl.pallas_call(finish_kernel, in_specs=[SCALAR] + [FULL] * 4 + [HBM] * 5...  5.99 us
    pallas_call x2, Pallas kernels, put(): pl.pallas_call(put_kernel, in_specs=[SCALAR, FULL] + [HBM] * len(done), o...  3.56 us
    pallas_call x1, Pallas kernels, backward(): pl.pallas_call(backward_kernel, in_specs=[SCALAR] + [FULL] * 9, out_specs...  3.35 us
    ppermute x2, starting transfers between devices, shift(): return lax.ppermute(block, axes, route)  3.05 us
  transfers between devices with their start and end apart: 10, of which 3 were waited for; matrix products, arithmetic and copies ran while one was open for 0% of the time, Pallas kernels for 26%

profile of v19, /device:TPU:0, one launch (start us, length us, event | category | flops | bytes accessed | tf_op | source)
XLA Modules:
  0.0 69.1 jit_solution(16178892473260858682)
XLA Ops:
  0.6 0.1 pad_add_fusion.place_ref
  0.7 1.7 %first_messages.1 = (bf16[4,1,32,256]{3,2,1,0:T(8,128)(2,1)S(1)}, bf16[4,1,32,256]{3,2,1,0:T(8,128)(2,1)S(1)}, bf16[2,8,64,256]{3,2,1,0:T(8,128)(2,1)S(1)}) custom-call(s32[2]{0:T(128)S(1)} %pad_add_fusion.place_ref, bf16[4,4,32,256]{3,2,1,0:T(8,128)(2,1)} %bitcast.13, bf16[4,8,64,256]{3,2,1,0:T(8,128)(2,1)} %bitcast.11), custom_call_target="tpu_custom_call" | custom-call | tf_op jit(solution)/shard_map/first_messages/pallas_call | solution.py:232
  2.5 1.3 %collective-permute-start.2 = (bf16[2,8,64,256]{3,2,1,0:T(8,128)(2,1)S(1)}, bf16[2,8,64,256]{3,2,1,0:T(8,128)(2,1)S(1)}, u32[]{:S(2)}, u32[]{:S(2)}) collective-permute-start(bf16[2,8,64,256]{3,2,1,0:T(8,128)(2,1)S(1)} %get-tuple-element.37), channel_id=1, source_target_pairs={{4,0},{8,4},{12,8},{5,1},{9,5},{13,9},{6,2},{10,6},{14,10},{7,3},{... | collective-permute-start | bytes 1572872 | tf_op jit(solution)/shard_map/ppermute | solution.py:40
  3.8 3.1 %collective-permute-start = (bf16[4,1,32,256]{3,2,1,0:T(8,128)(2,1)S(1)}, bf16[4,1,32,256]{3,2,1,0:T(8,128)(2,1)S(1)}, u32[]{:S(2)}, u32[]{:S(2)}) collective-permute-start(bf16[4,1,32,256]{3,2,1,0:T(8,128)(2,1)S(1)} %get-tuple-element.31), channel_id=1, source_target_pairs={{0,1},{1,0},{2,3},{3,2},{4,5},{5,4},{6,7},{7,6},{8,9},{9,8},{10,11... | collective-permute-start | bytes 196616 | tf_op jit(solution)/shard_map/ppermute | solution.py:34
  6.8 0.7 collective-permute-start.1
  7.5 0.1 pad_add_fusion.1.place_ref
  7.6 2.4 %load.1 = (bf16[4,4,32,256]{3,2,1,0:T(8,128)(2,1)S(1)}, bf16[3,3,256,256]{3,2,1,0:T(8,128)(2,1)S(1)}, bf16[256,256]{1,0:T(8,128)(2,1)S(1)}, bf16[768,256]{1,0:T(8,128)(2,1)S(1)}, bf16[4,4,128,256]{3,2,1,0:T(8,128)(2,1)S(1)}) custom-call(bf16[4,4,32,256]{3,2,1,0:T(8,128)(2,1)} %bitcast.14, bf16[4,8,64,256]{3,2,1,0:T(8,128)(2,1)} %bitcast.12, ...), custom_call_target="tpu_custom_call" | custom-call | flops 536870912 | bytes 4194304 | tf_op jit(solution)/shard_map/load/pallas_call | solution.py:269
  10.0 0.0 copy-start
  10.0 0.0 collective-permute-done.inner_ref
  10.0 0.0 collective-permute-done.1.outer_ref
  10.0 2.3 %forward.1 = (bf16[4,4,128,256]{3,2,1,0:T(8,128)(2,1)S(1)}, f32[4,4,128,256]{3,2,1,0:T(8,128)S(1)}) custom-call(s32[2]{0:T(128)S(1)} %pad_add_fusion.place_ref, bf16[4,4,32,256]{3,2,1,0:T(8,128)(2,1)S(1)} %get-tuple-element.30.low_ref, bf16[4,1,32,256]{3,2,1,0:T(8,128)(2,1)S(1)} %collective-permute-done.inner_ref, ...), custom_call_target="tpu_custom_call" | custom-call | flops 2684354560 | bytes 8388608 | tf_op jit(solution)/shard_map/forward/pallas_call | solution.py:285
  12.3 0.0 copy-done
  12.3 0.0 collective-permute-done.2.later_ref
  12.3 3.3 %backward.1 = (bf16[4,4,128,256]{3,2,1,0:T(8,128)(2,1)S(1)}, bf16[6,4,128,256]{3,2,1,0:T(8,128)(2,1)S(1)}, f32[12,128,256]{2,1,0:T(8,128)S(1)}) custom-call(s32[2]{0:T(128)S(1)} %pad_add_fusion.1.place_ref, bf16[4,4,32,256]{3,2,1,0:T(8,128)(2,1)S(1)} %get-tuple-element.30.low_ref, bf16[4,1,32,256]{3,2,1,0:T(8,128)(2,1)S(1)} %collective-permute-done.inner_ref, ...), custom_call_target="tpu_custom_call" | custom-call | flops 4026531840 | bytes 10485760 | tf_op jit(solution)/shard_map/backward/pallas_call | solution.py:324
  15.7 2.0 %collective-permute-start.3 = (f32[12,128,256]{2,1,0:T(8,128)S(1)}, f32[12,128,256]{2,1,0:T(8,128)S(1)}, u32[]{:S(2)}, u32[]{:S(2)}) collective-permute-start(f32[12,128,256]{2,1,0:T(8,128)S(1)} %get-tuple-element.44), channel_id=1, source_target_pairs={{0,4},{4,0},{1,5},{5,1},{2,6},{6,2},{3,7},{7,3},{8,12},{12,8},{9,1... | collective-permute-start | bytes 4718600 | tf_op jit(solution)/shard_map/ppermute | solution.py:34
  17.7 2.7 %half_grads.1 = (f32[12,128,256]{2,1,0:T(8,128)S(1)}, bf16[4,4,128,256]{3,2,1,0:T(8,128)(2,1)}, f32[4,128,256]{2,1,0:T(8,128)S(1)}) custom-call(s32[2]{0:T(128)S(1)} %pad_add_fusion.place_ref, bf16[4,4,32,256]{3,2,1,0:T(8,128)(2,1)S(1)} %get-tuple-element.30.low_ref, bf16[4,1,32,256]{3,2,1,0:T(8,128)(2,1)S(1)} %collective-permute-done.inner_ref, ...), custom_call_target="tpu_custom_call" | custom-call | flops 2684354560 | bytes 6291456 | tf_op jit(solution)/shard_map/half_grads/pallas_call | solution.py:337
  20.4 0.0 copy-start.3
  20.4 0.3 collective-permute-done.3.theirs_ref
  20.7 1.0 %add_halves.1._ = bf16[12,128,256]{2,1,0:T(8,128)(2,1)} custom-call(f32[12,128,256]{2,1,0:T(8,128)S(1)} %get-tuple-element.43.mine_ref, f32[12,128,256]{2,1,0:T(8,128)S(1)} %collective-permute-done.3.theirs_ref), custom_call_target="tpu_custom_call" | custom-call | tf_op jit(solution)/shard_map/add_halves/pallas_call | solution.py:517
  21.7 0.0 copy-done.3
  21.7 6.7 %all-to-all-start = ((bf16[8,192,256]{2,1,0:T(8,128)(2,1)}), bf16[8,192,256]{2,1,0:T(8,128)(2,1)S(1)}, u32[]{:S(2)}, u32[]{:S(2)}) async-start(bf16[8,192,256]{2,1,0:T(8,128)(2,1)} %bitcast.5), calls=%async_computation | async-start | bytes 1572864 | tf_op jit(solution)/shard_map/all_to_all | solution.py:43
  28.4 0.0 copy-start.1
  28.4 0.0 copy-start.4
  28.4 1.2 %edges.1 = (bf16[2,6,32,256]{3,2,1,0:T(8,128)(2,1)S(1)}, bf16[4,2,32,256]{3,2,1,0:T(8,128)(2,1)}, bf16[4,2,32,256]{3,2,1,0:T(8,128)(2,1)S(1)}) custom-call(s32[2]{0:T(128)S(1)} %pad_add_fusion.place_ref, bf16[4,4,32,256]{3,2,1,0:T(8,128)(2,1)S(1)} %get-tuple-element.30.low_ref, bf16[4,1,32,256]{3,2,1,0:T(8,128)(2,1)S(1)} %collective-permute-done.inner_ref, ...), custom_call_target="tpu_custom_call" | custom-call | tf_op jit(solution)/shard_map/edges/pallas_call | solution.py:311
  29.7 1.8 %collective-permute-start.6 = (bf16[2,6,32,256]{3,2,1,0:T(8,128)(2,1)S(1)}, bf16[2,6,32,256]{3,2,1,0:T(8,128)(2,1)S(1)}, u32[]{:S(2)}, u32[]{:S(2)}) collective-permute-start(bf16[2,6,32,256]{3,2,1,0:T(8,128)(2,1)S(1)} %get-tuple-element.47), channel_id=1, source_target_pairs={{0,4},{4,8},{8,12},{1,5},{5,9},{9,13},{2,6},{6,10},{10,14},{3,7},{... | collective-permute-start | bytes 589832 | tf_op jit(solution)/shard_map/ppermute | solution.py:40
  31.4 1.8 %collective-permute-start.4 = (bf16[4,2,32,256]{3,2,1,0:T(8,128)(2,1)}, bf16[4,2,32,256]{3,2,1,0:T(8,128)(2,1)S(1)}, u32[]{:S(2)}, u32[]{:S(2)}) collective-permute-start(bf16[4,2,32,256]{3,2,1,0:T(8,128)(2,1)} %get-tuple-element.45), channel_id=1, source_target_pairs={{0,1},{1,0},{2,3},{3,2},{4,5},{5,4},{6,7},{7,6},{8,9},{9,8},{10,11... | collective-permute-start | bytes 393224 | tf_op jit(solution)/shard_map/ppermute | solution.py:34
  33.2 0.8 %collective-permute-start.5 = (bf16[4,2,32,256]{3,2,1,0:T(8,128)(2,1)S(1)}, bf16[4,2,32,256]{3,2,1,0:T(8,128)(2,1)S(1)}, u32[]{:S(2)}, u32[]{:S(2)}) collective-permute-start(bf16[4,2,32,256]{3,2,1,0:T(8,128)(2,1)S(1)} %get-tuple-element.46), channel_id=1, source_target_pairs={{1,2},{2,1},{5,6},{6,5},{9,10},{10,9},{13,14},{14,13},{17,18},{18,... | collective-permute-start | bytes 393224 | tf_op jit(solution)/shard_map/ppermute | solution.py:49
  34.1 0.0 copy-done.1
  34.1 0.0 copy-done.4
  34.1 1.5 %input_own.1._.own_ref = f32[4,4,32,256]{3,2,1,0:T(8,128)S(1)} custom-call(bf16[4,4,128,256]{3,2,1,0:T(8,128)(2,1)S(1)} %get-tuple-element.40.pg_ref, f32[4,128,256]{2,1,0:T(8,128)S(1)} %copy-done.4, bf16[3,3,256,256]{3,2,1,0:T(8,128)(2,1)S(1)} %copy-done.1, bf16[12,128,256]{2,1,0:T(8,128)(2,1)} %add_halves.1._), custom_call_target="tpu_custom_call" | custom-call | flops 1610612736 | bytes 4194304 | tf_op jit(solution)/shard_map/input_own/pallas_call | solution.py:389
  35.6 6.8 %all-to-all-done.got_ref = bf16[8,192,256]{2,1,0:T(8,128)(2,1)S(1)} async-done(((bf16[8,192,256]{2,1,0:T(8,128)(2,1)}), bf16[8,192,256]{2,1,0:T(8,128)(2,1)S(1)}, u32[]{:S(2)}, u32[]{:S(2)}) %all-to-all-start) | async-done | bytes 786464 | tf_op jit(solution)/shard_map/all_to_all | solution.py:43
  42.4 0.1 sum_parts.1._.own_ref
  42.5 1.8 %collective-permute-start.7 = (bf16[192,256]{1,0:T(8,128)(2,1)S(1)}, bf16[192,256]{1,0:T(8,128)(2,1)S(1)}, u32[]{:S(2)}, u32[]{:S(2)}) collective-permute-start(bf16[192,256]{1,0:T(8,128)(2,1)S(1)} %sum_parts.1._.own_ref), channel_id=1, source_target_pairs={{0,2},{2,0},{1,3},{3,1},{4,6},{6,4},{5,7},{7,5},{8,10},{10,8},{9,1... | collective-permute-start | bytes 294920 | tf_op jit(solution)/shard_map/ppermute | solution.py:34
  44.3 0.0 collective-permute-done.4.inner_hbm
  44.3 0.0 collective-permute-done.5.outer_hbm
  44.3 0.0 collective-permute-done.6.edge_hbm
  44.3 0.0 copy-start.2
  44.3 1.3 %copy-done.2 = bf16[3,3,256,256]{3,2,1,0:T(8,128)(2,1)S(1)} copy-done((bf16[3,3,256,256]{3,2,1,0:T(8,128)(2,1)S(1)}, bf16[3,3,256,256]{3,2,1,0:T(8,128)(2,1)}, u32[]{:S(2)}) %copy-start.2) | copy-done | bytes 1179672
  45.6 6.0 %finish.1 = (bf16[4,8,64,256]{3,2,1,0:T(8,128)(2,1)}, bf16[4,4,32,256]{3,2,1,0:T(8,128)(2,1)}, f32[8,128]{1,0:T(8,128)S(1)}) custom-call(s32[2]{0:T(128)S(1)} %pad_add_fusion.place_ref, f32[4,4,32,256]{3,2,1,0:T(8,128)S(1)} %input_own.1._.own_ref, bf16[3,3,256,256]{3,2,1,0:T(8,128)(2,1)S(1)} %copy-done.2, bf16[256,256]{1,0:T(8,128)(2,1)S(1)} %get-tuple-element.39.sort_ref, ...), custom_call_target="tpu_custom_call" | custom-call | flops 2147483648 | bytes 4194304 | tf_op jit(solution)/shard_map/finish/pallas_call | solution.py:466
  51.6 0.0 collective-permute-done.7.theirs_ref
  51.6 0.1 spread.1
  51.7 13.2 %all_to_all.10 = bf16[8,192,256]{2,1,0:T(8,128)(2,1)S(1)} all-to-all(bf16[8,192,256]{2,1,0:T(8,128)(2,1)S(1)} %spread.1), channel_id=1, replica_groups=mesh['dp0'=2,'tm1'=2,'tm0'=2,'height1'=2,'height0'=2] {'dp0','tm1','heig..., dimensions={0} | all-to-all | bytes 1572864 | tf_op jit(solution)/shard_map/all_to_all | solution.py:43
  64.9 0.0 collective-permute-start.8
  64.9 1.8 %put.2 = (f32[3,3,256,256]{3,2,1,0:T(8,128)}, f32[3,256,256]{2,1,0:T(8,128)}) custom-call(s32[2]{0:T(128)S(1)} %pad_add_fusion.place_ref, bf16[12,128,256]{2,1,0:T(8,128)(2,1)S(1)} %bitcast.10), custom_call_target="tpu_custom_call" | custom-call | tf_op jit(solution)/shard_map/put/pallas_call | solution.py:499
  66.6 0.5 collective-permute-done.8.half_ref
  67.1 1.8 %put.3 = (f32[3,3,256,256]{3,2,1,0:T(8,128)}, f32[3,256,256]{2,1,0:T(8,128)}) custom-call(s32[2]{0:T(128)S(1)} %pad_add_fusion.1.place_ref, bf16[12,128,256]{2,1,0:T(8,128)(2,1)S(1)} %collective-permute-done.8.half_ref, f32[3,3,256,256]{3,2,1,0:T(8,128)} %get-tuple-element.52.refs_0_, ...), custom_call_target="tpu_custom_call", output_to_operand_aliasing={{0}: (2, {}), {1}: (3, {})} | custom-call | tf_op jit(solution)/shard_map/put/pallas_call | solution.py:499
Async XLA Ops:
  2.5 9.9 %collective-permute-start.2 = (bf16[2,8,64,256]{3,2,1,0:T(8,128)(2,1)S(1)}, bf16[2,8,64,256]{3,2,1,0:T(8,128)(2,1)S(1)}, u32[]{:S(2)}, u32[]{:S(2)}) collective-permute-start(bf16[2,8,64,256]{3,2,1,0:T(8,128)(2,1)S(1)} %get-tuple-element.37), channel_id=1, source_target_pairs={{4,0},{8,4},{12,8},{5,1},{9,5},{13,9},{6,2},{10,6},{14,10},{7,3},{... | collective-permute-start | bytes 1572872 | tf_op jit(solution)/shard_map/ppermute | solution.py:40
  3.8 6.2 %collective-permute-start = (bf16[4,1,32,256]{3,2,1,0:T(8,128)(2,1)S(1)}, bf16[4,1,32,256]{3,2,1,0:T(8,128)(2,1)S(1)}, u32[]{:S(2)}, u32[]{:S(2)}) collective-permute-start(bf16[4,1,32,256]{3,2,1,0:T(8,128)(2,1)S(1)} %get-tuple-element.31), channel_id=1, source_target_pairs={{0,1},{1,0},{2,3},{3,2},{4,5},{5,4},{6,7},{7,6},{8,9},{9,8},{10,11... | collective-permute-start | bytes 196616 | tf_op jit(solution)/shard_map/ppermute | solution.py:34
  6.8 3.2 %collective-permute-start.1 = (bf16[4,1,32,256]{3,2,1,0:T(8,128)(2,1)S(1)}, bf16[4,1,32,256]{3,2,1,0:T(8,128)(2,1)S(1)}, u32[]{:S(2)}, u32[]{:S(2)}) collective-permute-start(bf16[4,1,32,256]{3,2,1,0:T(8,128)(2,1)S(1)} %get-tuple-element.32), channel_id=1, source_target_pairs={{1,2},{2,1},{5,6},{6,5},{9,10},{10,9},{13,14},{14,13},{17,18},{18,... | collective-permute-start | bytes 196616 | tf_op jit(solution)/shard_map/ppermute | solution.py:49
  10.0 2.4 %copy-start = (bf16[3,3,256,256]{3,2,1,0:T(8,128)(2,1)}, bf16[3,3,256,256]{3,2,1,0:T(8,128)(2,1)S(1)}, u32[]{:S(2)}) copy-start(bf16[3,3,256,256]{3,2,1,0:T(8,128)(2,1)S(1)} %get-tuple-element.33.ws_ref) | copy-start | bytes 3538948
  15.7 5.0 %collective-permute-start.3 = (f32[12,128,256]{2,1,0:T(8,128)S(1)}, f32[12,128,256]{2,1,0:T(8,128)S(1)}, u32[]{:S(2)}, u32[]{:S(2)}) collective-permute-start(f32[12,128,256]{2,1,0:T(8,128)S(1)} %get-tuple-element.44), channel_id=1, source_target_pairs={{0,4},{4,0},{1,5},{5,1},{2,6},{6,2},{3,7},{7,3},{8,12},{12,8},{9,1... | collective-permute-start | bytes 4718600 | tf_op jit(solution)/shard_map/ppermute | solution.py:34
  20.4 1.3 %copy-start.3 = (f32[4,128,256]{2,1,0:T(8,128)}, f32[4,128,256]{2,1,0:T(8,128)S(1)}, u32[]{:S(2)}) copy-start(f32[4,128,256]{2,1,0:T(8,128)S(1)} %get-tuple-element.42.box_ref) | copy-start | bytes 1572868
  21.7 20.7 %all-to-all-start = ((bf16[8,192,256]{2,1,0:T(8,128)(2,1)}), bf16[8,192,256]{2,1,0:T(8,128)(2,1)S(1)}, u32[]{:S(2)}, u32[]{:S(2)}) async-start(bf16[8,192,256]{2,1,0:T(8,128)(2,1)} %bitcast.5), calls=%async_computation | async-start | bytes 1572864 | tf_op jit(solution)/shard_map/all_to_all | solution.py:43
  28.4 5.7 %copy-start.1 = (bf16[3,3,256,256]{3,2,1,0:T(8,128)(2,1)S(1)}, bf16[3,3,256,256]{3,2,1,0:T(8,128)(2,1)}, u32[]{:S(2)}) copy-start(bf16[3,3,256,256]{3,2,1,0:T(8,128)(2,1)} %copy-done) | copy-start | bytes 3538948
  28.4 5.7 %copy-start.4 = (f32[4,128,256]{2,1,0:T(8,128)S(1)}, f32[4,128,256]{2,1,0:T(8,128)}, u32[]{:S(2)}) copy-start(f32[4,128,256]{2,1,0:T(8,128)} %copy-done.3) | copy-start | bytes 1572868
  29.7 14.7 %collective-permute-start.6 = (bf16[2,6,32,256]{3,2,1,0:T(8,128)(2,1)S(1)}, bf16[2,6,32,256]{3,2,1,0:T(8,128)(2,1)S(1)}, u32[]{:S(2)}, u32[]{:S(2)}) collective-permute-start(bf16[2,6,32,256]{3,2,1,0:T(8,128)(2,1)S(1)} %get-tuple-element.47), channel_id=1, source_target_pairs={{0,4},{4,8},{8,12},{1,5},{5,9},{9,13},{2,6},{6,10},{10,14},{3,7},{... | collective-permute-start | bytes 589832 | tf_op jit(solution)/shard_map/ppermute | solution.py:40
  31.4 12.9 %collective-permute-start.4 = (bf16[4,2,32,256]{3,2,1,0:T(8,128)(2,1)}, bf16[4,2,32,256]{3,2,1,0:T(8,128)(2,1)S(1)}, u32[]{:S(2)}, u32[]{:S(2)}) collective-permute-start(bf16[4,2,32,256]{3,2,1,0:T(8,128)(2,1)} %get-tuple-element.45), channel_id=1, source_target_pairs={{0,1},{1,0},{2,3},{3,2},{4,5},{5,4},{6,7},{7,6},{8,9},{9,8},{10,11... | collective-permute-start | bytes 393224 | tf_op jit(solution)/shard_map/ppermute | solution.py:34
  33.2 11.1 %collective-permute-start.5 = (bf16[4,2,32,256]{3,2,1,0:T(8,128)(2,1)S(1)}, bf16[4,2,32,256]{3,2,1,0:T(8,128)(2,1)S(1)}, u32[]{:S(2)}, u32[]{:S(2)}) collective-permute-start(bf16[4,2,32,256]{3,2,1,0:T(8,128)(2,1)S(1)} %get-tuple-element.46), channel_id=1, source_target_pairs={{1,2},{2,1},{5,6},{6,5},{9,10},{10,9},{13,14},{14,13},{17,18},{18,... | collective-permute-start | bytes 393224 | tf_op jit(solution)/shard_map/ppermute | solution.py:49
  42.5 9.1 %collective-permute-start.7 = (bf16[192,256]{1,0:T(8,128)(2,1)S(1)}, bf16[192,256]{1,0:T(8,128)(2,1)S(1)}, u32[]{:S(2)}, u32[]{:S(2)}) collective-permute-start(bf16[192,256]{1,0:T(8,128)(2,1)S(1)} %sum_parts.1._.own_ref), channel_id=1, source_target_pairs={{0,2},{2,0},{1,3},{3,1},{4,6},{6,4},{5,7},{7,5},{8,10},{10,8},{9,1... | collective-permute-start | bytes 294920 | tf_op jit(solution)/shard_map/ppermute | solution.py:34
  44.3 1.3 %copy-start.2 = (bf16[3,3,256,256]{3,2,1,0:T(8,128)(2,1)S(1)}, bf16[3,3,256,256]{3,2,1,0:T(8,128)(2,1)}, u32[]{:S(2)}) copy-start(bf16[3,3,256,256]{3,2,1,0:T(8,128)(2,1)} %copy-done) | copy-start | bytes 3538948
  64.9 2.3 %collective-permute-start.8 = (bf16[12,128,256]{2,1,0:T(8,128)(2,1)S(1)}, bf16[12,128,256]{2,1,0:T(8,128)(2,1)S(1)}, u32[]{:S(2)}, u32[]{:S(2)}) collective-permute-start(bf16[12,128,256]{2,1,0:T(8,128)(2,1)S(1)} %bitcast.9), channel_id=1, source_target_pairs={{0,4},{4,0},{1,5},{5,1},{2,6},{6,2},{3,7},{7,3},{8,12},{12,8},{9,1... | collective-permute-start | bytes 2359304 | tf_op jit(solution)/shard_map/ppermute | solution.py:34

commit v20 on v19

--- a/solution.py
+++ b/solution.py
@@ -219,7 +219,7 @@
         (low_ref.at[:, pl.ds(last * (1 - odd), 1)], inner_ref),
         (low_ref.at[:, pl.ds(last * odd, 1)], outer_ref),
     ]
-    copies += [(cot_ref.at[n, r], later_ref.at[n, r]) for n in range(2) for r in range(cot_ref.shape[1])]
+    copies += [(cot_ref.at[0:2], later_ref)]
     copies = [pltpu.make_async_copy(a, b, sems.at[n]) for n, (a, b) in enumerate(copies)]
     for copy in copies:
         copy.start()
@@ -234,7 +234,7 @@
         in_specs=[SCALAR, UNREAD, UNREAD],
         out_specs=[FULL] * 3,
         out_shape=[row, row, like(cot[:2].shape, cot.dtype)],
-        scratch_shapes=[pltpu.SemaphoreType.DMA((2 + 2 * cot.shape[1],))],
+        scratch_shapes=[pltpu.SemaphoreType.DMA((3,))],
         compiler_params=grant(4),
         name="first_messages",
     )(place, in_hbm(low), in_hbm(cot))
@@ -397,15 +397,15 @@
     )(pg, box, ws, before)
 
 
-def finish_kernel(place_ref, own_ref, ws_ref, sort_ref, low_ref, inner_hbm, outer_hbm, edge_hbm, act_hbm, wt_hbm, _,
+def finish_kernel(place_ref, own_ref, ws_ref, inner_hbm, outer_hbm, edge_hbm, act_hbm, wt_hbm, sort_hbm, low_hbm, _,
                   section_ref, input_ref, token_ref,
-                  inner_ref, outer_ref, edge_ref, act_ref, wt_ref, earlier, held, input_held, sems):
+                  inner_ref, outer_ref, edge_ref, act_ref, wt_ref, wide_ref, low_ref, earlier, held, input_held, sems):
     frames, rows_low, cols_low, chan = low_ref.shape
     group = rows_at_once(rows_low, cols_low)
     span, count = group * cols_low, rows_low * cols_low
     pairs = [(inner_hbm, inner_ref), (outer_hbm, outer_ref)]
     pairs += [(edge_hbm, edge_ref), (wt_hbm, wt_ref)]
-    pairs += [(act_hbm.at[n], act_ref.at[n]) for n in range(frames)]
+    pairs += [(act_hbm.at[n], act_ref.at[n]) for n in range(frames)] + [(sort_hbm, wide_ref), (low_hbm, low_ref)]
     copies = [pltpu.make_async_copy(a, b, sems.at[n]) for n, (a, b) in enumerate(pairs)]
     for copy in copies:
         copy.start()
@@ -442,7 +442,7 @@
         earlier[:, side] = (pre * jax.nn.sigmoid(pre)).astype(jnp.bfloat16).reshape(2, count, chan)
     for copy in copies[3:]:
         copy.wait()
-    merge = sort_ref[...].T
+    merge = wide_ref[...].T.astype(jnp.bfloat16)
     wt = wt_ref[...].reshape(3 * chan, chan)
     for frame in range(frames):
         acts = [act_ref[frame - k] if frame >= k else earlier[frame - k + 2] for k in range(3)]
@@ -459,13 +459,13 @@
         copy.wait()
 
 
-def finish(place, own, ws, sort, low, inner, outer, edge, act, wt, before):
+def finish(place, own, ws, inner, outer, edge, act, wt, sort, low, before):
     frames, rows_low, cols_low, chan = low.shape
     out = (frames, 2 * rows_low, 2 * cols_low, chan)
-    fetched = [inner, outer, edge, act, wt]
+    fetched = [inner, outer, edge, act, wt, sort, low]
     return pl.pallas_call(
         finish_kernel,
-        in_specs=[SCALAR] + [FULL] * 4 + [HBM] * 5 + [UNREAD],
+        in_specs=[SCALAR, FULL, FULL] + [HBM] * 7 + [UNREAD],
         out_specs=[HBM, HBM, FULL],
         out_shape=[like(out, jnp.bfloat16), like(low.shape, jnp.bfloat16), TOKEN],
         scratch_shapes=[pltpu.VMEM(a.shape, a.dtype) for a in fetched]
@@ -474,7 +474,7 @@
         compiler_params=grant(16),
         cost_estimate=cost(8, 4),
         name="finish",
-    )(place, own, ws, sort, low, inner, outer, edge, in_hbm(act), in_hbm(wt), before)
+    )(place, own, ws, inner, outer, edge, *[in_hbm(a) for a in (act, wt, sort, low)], before)
 
 
 def put_kernel(place_ref, half_ref, *refs):
@@ -586,7 +586,7 @@
     own_part = input_own(pg, box, ws, kept, low.shape)
     total, far = bits.far_sums(sum_parts(got, own_part))
     section_out, input_grad, done = finish(
-        mine, own_part, ws, sort, low_in, pg_inner, pg_outer, edge, act, temporal_weight, total
+        mine, own_part, ws, pg_inner, pg_outer, edge, act, temporal_weight, order, low, total
     )
     totals = spread(total, far, parts, done)
     half = bits.exchange(totals).reshape(kept.shape)

time: 69.5 us -> 68.8 us (0.990)
  local copies, waits for them, and re-layouts: 1.29 us -> 0.01 us
  waiting for transfers between devices: 7.62 us -> 6.47 us
  starting transfers between devices: 19.9 us -> 20.9 us
    unnamed x10 -> x4, local copies, waits for them, and re-layouts: 1.29 us -> 0.01 us
    all_to_all x1, waiting for transfers between devices: 6.81 us -> 5.63 us  [exchange(): return lax.all_to_all(parts, tuple(self.near), 0, 0, tiled=True)]
  transfers between devices with their start and end apart: 10 -> 10, of which waited for: 3 -> 3; matrix products, arithmetic and copies ran while one was open for 0% -> 0% of each run, Pallas kernels for 26% -> 27%
where the time goes in v20:
time: 68.8 us; the launch traced here: 68.5 us
  Pallas kernels  26.4 us (38%)
  starting transfers between devices  20.9 us (30%)
  blocking collectives  13.6 us (20%)
  waiting for transfers between devices  6.47 us (9%)
  between operations  0.94 us (1%)
    all_to_all x1, blocking collectives, exchange(): return lax.all_to_all(parts, tuple(self.near), 0, 0, tiled=True)  13.6 us
    ppermute x5, starting transfers between devices, swap(): return lax.ppermute(block, axis, [(0, 1), (1, 0)])  8.63 us
    all_to_all x1, starting transfers between devices, exchange(): return lax.all_to_all(parts, tuple(self.near), 0, 0, tiled=True)  6.63 us
    pallas_call x1, Pallas kernels, finish(): pl.pallas_call(finish_kernel, in_specs=[SCALAR, FULL, FULL] + [HBM] * 7 +...  6.36 us
    all_to_all x1, waiting for transfers between devices, exchange(): return lax.all_to_all(parts, tuple(self.near), 0, 0, tiled=True)  5.63 us
    ppermute x2, starting transfers between devices, shift(): return lax.ppermute(block, axes, route)  3.71 us
    pallas_call x2, Pallas kernels, put(): pl.pallas_call(put_kernel, in_specs=[SCALAR, FULL] + [HBM] * len(done), o...  3.56 us
    pallas_call x1, Pallas kernels, backward(): pl.pallas_call(backward_kernel, in_specs=[SCALAR] + [FULL] * 9, out_specs...  3.35 us
  transfers between devices with their start and end apart: 10, of which 3 were waited for; matrix products, arithmetic and copies ran while one was open for 0% of the time, Pallas kernels for 27%

profile of v20, /device:TPU:0, one launch (start us, length us, event | category | flops | bytes accessed | tf_op | source)
XLA Modules:
  0.0 68.5 jit_solution(17947091644966940374)
XLA Ops:
  0.6 0.1 pad_add_fusion.place_ref
  0.7 1.7 %first_messages.1 = (bf16[4,1,32,256]{3,2,1,0:T(8,128)(2,1)S(1)}, bf16[4,1,32,256]{3,2,1,0:T(8,128)(2,1)S(1)}, bf16[2,8,64,256]{3,2,1,0:T(8,128)(2,1)S(1)}) custom-call(s32[2]{0:T(128)S(1)} %pad_add_fusion.place_ref, bf16[4,4,32,256]{3,2,1,0:T(8,128)(2,1)} %bitcast.13, bf16[4,8,64,256]{3,2,1,0:T(8,128)(2,1)} %bitcast.11), custom_call_target="tpu_custom_call" | custom-call | tf_op jit(solution)/shard_map/first_messages/pallas_call | solution.py:232
  2.4 1.3 %collective-permute-start.2 = (bf16[2,8,64,256]{3,2,1,0:T(8,128)(2,1)S(1)}, bf16[2,8,64,256]{3,2,1,0:T(8,128)(2,1)S(1)}, u32[]{:S(2)}, u32[]{:S(2)}) collective-permute-start(bf16[2,8,64,256]{3,2,1,0:T(8,128)(2,1)S(1)} %get-tuple-element.37), channel_id=1, source_target_pairs={{4,0},{8,4},{12,8},{5,1},{9,5},{13,9},{6,2},{10,6},{14,10},{7,3},{... | collective-permute-start | bytes 1572872 | tf_op jit(solution)/shard_map/ppermute | solution.py:40
  3.7 3.1 %collective-permute-start = (bf16[4,1,32,256]{3,2,1,0:T(8,128)(2,1)S(1)}, bf16[4,1,32,256]{3,2,1,0:T(8,128)(2,1)S(1)}, u32[]{:S(2)}, u32[]{:S(2)}) collective-permute-start(bf16[4,1,32,256]{3,2,1,0:T(8,128)(2,1)S(1)} %get-tuple-element.31), channel_id=1, source_target_pairs={{0,1},{1,0},{2,3},{3,2},{4,5},{5,4},{6,7},{7,6},{8,9},{9,8},{10,11... | collective-permute-start | bytes 196616 | tf_op jit(solution)/shard_map/ppermute | solution.py:34
  6.8 0.7 collective-permute-start.1
  7.5 0.1 pad_add_fusion.1.place_ref
  7.5 2.4 %load.1 = (bf16[4,4,32,256]{3,2,1,0:T(8,128)(2,1)S(1)}, bf16[3,3,256,256]{3,2,1,0:T(8,128)(2,1)S(1)}, bf16[256,256]{1,0:T(8,128)(2,1)S(1)}, bf16[768,256]{1,0:T(8,128)(2,1)S(1)}, bf16[4,4,128,256]{3,2,1,0:T(8,128)(2,1)S(1)}) custom-call(bf16[4,4,32,256]{3,2,1,0:T(8,128)(2,1)} %bitcast.14, bf16[4,8,64,256]{3,2,1,0:T(8,128)(2,1)} %bitcast.12, ...), custom_call_target="tpu_custom_call" | custom-call | flops 536870912 | bytes 4194304 | tf_op jit(solution)/shard_map/load/pallas_call | solution.py:269
  9.9 0.0 collective-permute-done.inner_ref
  9.9 0.0 collective-permute-done.1.outer_ref
  9.9 2.3 %forward.1 = (bf16[4,4,128,256]{3,2,1,0:T(8,128)(2,1)S(1)}, f32[4,4,128,256]{3,2,1,0:T(8,128)S(1)}) custom-call(s32[2]{0:T(128)S(1)} %pad_add_fusion.place_ref, bf16[4,4,32,256]{3,2,1,0:T(8,128)(2,1)S(1)} %get-tuple-element.30.low_ref, bf16[4,1,32,256]{3,2,1,0:T(8,128)(2,1)S(1)} %collective-permute-done.inner_ref, ...), custom_call_target="tpu_custom_call" | custom-call | flops 2684354560 | bytes 8388608 | tf_op jit(solution)/shard_map/forward/pallas_call | solution.py:285
  12.3 0.0 collective-permute-done.2.later_ref
  12.3 3.3 %backward.1 = (bf16[4,4,128,256]{3,2,1,0:T(8,128)(2,1)S(1)}, bf16[6,4,128,256]{3,2,1,0:T(8,128)(2,1)S(1)}, f32[12,128,256]{2,1,0:T(8,128)S(1)}) custom-call(s32[2]{0:T(128)S(1)} %pad_add_fusion.1.place_ref, bf16[4,4,32,256]{3,2,1,0:T(8,128)(2,1)S(1)} %get-tuple-element.30.low_ref, bf16[4,1,32,256]{3,2,1,0:T(8,128)(2,1)S(1)} %collective-permute-done.inner_ref, ...), custom_call_target="tpu_custom_call" | custom-call | flops 4026531840 | bytes 10485760 | tf_op jit(solution)/shard_map/backward/pallas_call | solution.py:324
  15.6 2.0 %collective-permute-start.3 = (f32[12,128,256]{2,1,0:T(8,128)S(1)}, f32[12,128,256]{2,1,0:T(8,128)S(1)}, u32[]{:S(2)}, u32[]{:S(2)}) collective-permute-start(f32[12,128,256]{2,1,0:T(8,128)S(1)} %get-tuple-element.44), channel_id=1, source_target_pairs={{0,4},{4,0},{1,5},{5,1},{2,6},{6,2},{3,7},{7,3},{8,12},{12,8},{9,1... | collective-permute-start | bytes 4718600 | tf_op jit(solution)/shard_map/ppermute | solution.py:34
  17.6 2.7 %half_grads.1 = (f32[12,128,256]{2,1,0:T(8,128)S(1)}, bf16[4,4,128,256]{3,2,1,0:T(8,128)(2,1)}, f32[4,128,256]{2,1,0:T(8,128)S(1)}) custom-call(s32[2]{0:T(128)S(1)} %pad_add_fusion.place_ref, bf16[4,4,32,256]{3,2,1,0:T(8,128)(2,1)S(1)} %get-tuple-element.30.low_ref, bf16[4,1,32,256]{3,2,1,0:T(8,128)(2,1)S(1)} %collective-permute-done.inner_ref, ...), custom_call_target="tpu_custom_call" | custom-call | flops 2684354560 | bytes 6291456 | tf_op jit(solution)/shard_map/half_grads/pallas_call | solution.py:337
  20.3 0.0 copy-start
  20.3 0.3 collective-permute-done.3.theirs_ref
  20.7 1.0 %add_halves.1._ = bf16[12,128,256]{2,1,0:T(8,128)(2,1)} custom-call(f32[12,128,256]{2,1,0:T(8,128)S(1)} %get-tuple-element.43.mine_ref, f32[12,128,256]{2,1,0:T(8,128)S(1)} %collective-permute-done.3.theirs_ref), custom_call_target="tpu_custom_call" | custom-call | tf_op jit(solution)/shard_map/add_halves/pallas_call | solution.py:517
  21.7 0.0 copy-done
  21.7 6.6 %all-to-all-start = ((bf16[8,192,256]{2,1,0:T(8,128)(2,1)}), bf16[8,192,256]{2,1,0:T(8,128)(2,1)S(1)}, u32[]{:S(2)}, u32[]{:S(2)}) async-start(bf16[8,192,256]{2,1,0:T(8,128)(2,1)} %bitcast.5), calls=%async_computation | async-start | bytes 1572864 | tf_op jit(solution)/shard_map/all_to_all | solution.py:43
  28.3 0.0 copy-start.1
  28.3 1.3 %edges.1 = (bf16[2,6,32,256]{3,2,1,0:T(8,128)(2,1)}, bf16[4,2,32,256]{3,2,1,0:T(8,128)(2,1)}, bf16[4,2,32,256]{3,2,1,0:T(8,128)(2,1)}) custom-call(s32[2]{0:T(128)S(1)} %pad_add_fusion.place_ref, bf16[4,4,32,256]{3,2,1,0:T(8,128)(2,1)S(1)} %get-tuple-element.30.low_ref, bf16[4,1,32,256]{3,2,1,0:T(8,128)(2,1)S(1)} %collective-permute-done.inner_ref, ...), custom_call_target="tpu_custom_call" | custom-call | tf_op jit(solution)/shard_map/edges/pallas_call | solution.py:311
  29.7 2.4 %collective-permute-start.6 = (bf16[2,6,32,256]{3,2,1,0:T(8,128)(2,1)}, bf16[2,6,32,256]{3,2,1,0:T(8,128)(2,1)}, u32[]{:S(2)}, u32[]{:S(2)}) collective-permute-start(bf16[2,6,32,256]{3,2,1,0:T(8,128)(2,1)} %get-tuple-element.47), channel_id=1, source_target_pairs={{0,4},{4,8},{8,12},{1,5},{5,9},{9,13},{2,6},{6,10},{10,14},{3,7},{... | collective-permute-start | bytes 589832 | tf_op jit(solution)/shard_map/ppermute | solution.py:40
  32.1 1.7 %collective-permute-start.4 = (bf16[4,2,32,256]{3,2,1,0:T(8,128)(2,1)}, bf16[4,2,32,256]{3,2,1,0:T(8,128)(2,1)}, u32[]{:S(2)}, u32[]{:S(2)}) collective-permute-start(bf16[4,2,32,256]{3,2,1,0:T(8,128)(2,1)} %get-tuple-element.45), channel_id=1, source_target_pairs={{0,1},{1,0},{2,3},{3,2},{4,5},{5,4},{6,7},{7,6},{8,9},{9,8},{10,11... | collective-permute-start | bytes 393224 | tf_op jit(solution)/shard_map/ppermute | solution.py:34
  33.8 1.3 %collective-permute-start.5 = (bf16[4,2,32,256]{3,2,1,0:T(8,128)(2,1)}, bf16[4,2,32,256]{3,2,1,0:T(8,128)(2,1)}, u32[]{:S(2)}, u32[]{:S(2)}) collective-permute-start(bf16[4,2,32,256]{3,2,1,0:T(8,128)(2,1)} %get-tuple-element.46), channel_id=1, source_target_pairs={{1,2},{2,1},{5,6},{6,5},{9,10},{10,9},{13,14},{14,13},{17,18},{18,... | collective-permute-start | bytes 393224 | tf_op jit(solution)/shard_map/ppermute | solution.py:49
  35.1 0.0 copy-done.1
  35.1 1.6 %input_own.1._.own_ref = f32[4,4,32,256]{3,2,1,0:T(8,128)S(1)} custom-call(bf16[4,4,128,256]{3,2,1,0:T(8,128)(2,1)S(1)} %get-tuple-element.40.pg_ref, f32[4,128,256]{2,1,0:T(8,128)S(1)} %copy-done.1, bf16[3,3,256,256]{3,2,1,0:T(8,128)(2,1)S(1)} %get-tuple-element.33.ws_ref, bf16[12,128,256]{2,1,0:T(8,128)(2,1)} %add_halves.1._), custom_call_target="tpu_custom_call" | custom-call | flops 1610612736 | bytes 4194304 | tf_op jit(solution)/shard_map/input_own/pallas_call | solution.py:389
  36.7 5.6 %all-to-all-done.got_ref = bf16[8,192,256]{2,1,0:T(8,128)(2,1)S(1)} async-done(((bf16[8,192,256]{2,1,0:T(8,128)(2,1)}), bf16[8,192,256]{2,1,0:T(8,128)(2,1)S(1)}, u32[]{:S(2)}, u32[]{:S(2)}) %all-to-all-start) | async-done | bytes 786464 | tf_op jit(solution)/shard_map/all_to_all | solution.py:43
  42.3 0.1 sum_parts.1._.own_ref
  42.4 1.8 %collective-permute-start.7 = (bf16[192,256]{1,0:T(8,128)(2,1)S(1)}, bf16[192,256]{1,0:T(8,128)(2,1)S(1)}, u32[]{:S(2)}, u32[]{:S(2)}) collective-permute-start(bf16[192,256]{1,0:T(8,128)(2,1)S(1)} %sum_parts.1._.own_ref), channel_id=1, source_target_pairs={{0,2},{2,0},{1,3},{3,1},{4,6},{6,4},{5,7},{7,5},{8,10},{10,8},{9,1... | collective-permute-start | bytes 294920 | tf_op jit(solution)/shard_map/ppermute | solution.py:34
  44.2 0.0 collective-permute-done.4.inner_hbm
  44.2 0.0 collective-permute-done.5.outer_hbm
  44.2 0.0 collective-permute-done.6.edge_hbm
  44.3 6.4 %finish.1 = (bf16[4,8,64,256]{3,2,1,0:T(8,128)(2,1)}, bf16[4,4,32,256]{3,2,1,0:T(8,128)(2,1)}, f32[8,128]{1,0:T(8,128)S(1)}) custom-call(s32[2]{0:T(128)S(1)} %pad_add_fusion.place_ref, f32[4,4,32,256]{3,2,1,0:T(8,128)S(1)} %input_own.1._.own_ref, bf16[3,3,256,256]{3,2,1,0:T(8,128)(2,1)S(1)} %get-tuple-element.33.ws_ref, ...), custom_call_target="tpu_custom_call" | custom-call | flops 2147483648 | bytes 4194304 | tf_op jit(solution)/shard_map/finish/pallas_call | solution.py:466
  50.6 0.0 collective-permute-done.7.theirs_ref
  50.6 0.1 spread.1
  50.7 13.6 %all_to_all.10 = bf16[8,192,256]{2,1,0:T(8,128)(2,1)S(1)} all-to-all(bf16[8,192,256]{2,1,0:T(8,128)(2,1)S(1)} %spread.1), channel_id=1, replica_groups=mesh['dp0'=2,'tm1'=2,'tm0'=2,'height1'=2,'height0'=2] {'dp0','tm1','heig..., dimensions={0} | all-to-all | bytes 1572864 | tf_op jit(solution)/shard_map/all_to_all | solution.py:43
  64.3 0.0 collective-permute-start.8
  64.3 1.8 %put.2 = (f32[3,3,256,256]{3,2,1,0:T(8,128)}, f32[3,256,256]{2,1,0:T(8,128)}) custom-call(s32[2]{0:T(128)S(1)} %pad_add_fusion.place_ref, bf16[12,128,256]{2,1,0:T(8,128)(2,1)S(1)} %bitcast.10), custom_call_target="tpu_custom_call" | custom-call | tf_op jit(solution)/shard_map/put/pallas_call | solution.py:499
  66.0 0.5 collective-permute-done.8.half_ref
  66.5 1.8 %put.3 = (f32[3,3,256,256]{3,2,1,0:T(8,128)}, f32[3,256,256]{2,1,0:T(8,128)}) custom-call(s32[2]{0:T(128)S(1)} %pad_add_fusion.1.place_ref, bf16[12,128,256]{2,1,0:T(8,128)(2,1)S(1)} %collective-permute-done.8.half_ref, f32[3,3,256,256]{3,2,1,0:T(8,128)} %get-tuple-element.52.refs_0_, ...), custom_call_target="tpu_custom_call", output_to_operand_aliasing={{0}: (2, {}), {1}: (3, {})} | custom-call | tf_op jit(solution)/shard_map/put/pallas_call | solution.py:499
Async XLA Ops:
  2.4 9.9 %collective-permute-start.2 = (bf16[2,8,64,256]{3,2,1,0:T(8,128)(2,1)S(1)}, bf16[2,8,64,256]{3,2,1,0:T(8,128)(2,1)S(1)}, u32[]{:S(2)}, u32[]{:S(2)}) collective-permute-start(bf16[2,8,64,256]{3,2,1,0:T(8,128)(2,1)S(1)} %get-tuple-element.37), channel_id=1, source_target_pairs={{4,0},{8,4},{12,8},{5,1},{9,5},{13,9},{6,2},{10,6},{14,10},{7,3},{... | collective-permute-start | bytes 1572872 | tf_op jit(solution)/shard_map/ppermute | solution.py:40
  3.7 6.2 %collective-permute-start = (bf16[4,1,32,256]{3,2,1,0:T(8,128)(2,1)S(1)}, bf16[4,1,32,256]{3,2,1,0:T(8,128)(2,1)S(1)}, u32[]{:S(2)}, u32[]{:S(2)}) collective-permute-start(bf16[4,1,32,256]{3,2,1,0:T(8,128)(2,1)S(1)} %get-tuple-element.31), channel_id=1, source_target_pairs={{0,1},{1,0},{2,3},{3,2},{4,5},{5,4},{6,7},{7,6},{8,9},{9,8},{10,11... | collective-permute-start | bytes 196616 | tf_op jit(solution)/shard_map/ppermute | solution.py:34
  6.8 3.1 %collective-permute-start.1 = (bf16[4,1,32,256]{3,2,1,0:T(8,128)(2,1)S(1)}, bf16[4,1,32,256]{3,2,1,0:T(8,128)(2,1)S(1)}, u32[]{:S(2)}, u32[]{:S(2)}) collective-permute-start(bf16[4,1,32,256]{3,2,1,0:T(8,128)(2,1)S(1)} %get-tuple-element.32), channel_id=1, source_target_pairs={{1,2},{2,1},{5,6},{6,5},{9,10},{10,9},{13,14},{14,13},{17,18},{18,... | collective-permute-start | bytes 196616 | tf_op jit(solution)/shard_map/ppermute | solution.py:49
  15.6 5.0 %collective-permute-start.3 = (f32[12,128,256]{2,1,0:T(8,128)S(1)}, f32[12,128,256]{2,1,0:T(8,128)S(1)}, u32[]{:S(2)}, u32[]{:S(2)}) collective-permute-start(f32[12,128,256]{2,1,0:T(8,128)S(1)} %get-tuple-element.44), channel_id=1, source_target_pairs={{0,4},{4,0},{1,5},{5,1},{2,6},{6,2},{3,7},{7,3},{8,12},{12,8},{9,1... | collective-permute-start | bytes 4718600 | tf_op jit(solution)/shard_map/ppermute | solution.py:34
  20.3 1.4 %copy-start = (f32[4,128,256]{2,1,0:T(8,128)}, f32[4,128,256]{2,1,0:T(8,128)S(1)}, u32[]{:S(2)}) copy-start(f32[4,128,256]{2,1,0:T(8,128)S(1)} %get-tuple-element.42.box_ref) | copy-start | bytes 1572868
  21.7 20.6 %all-to-all-start = ((bf16[8,192,256]{2,1,0:T(8,128)(2,1)}), bf16[8,192,256]{2,1,0:T(8,128)(2,1)S(1)}, u32[]{:S(2)}, u32[]{:S(2)}) async-start(bf16[8,192,256]{2,1,0:T(8,128)(2,1)} %bitcast.5), calls=%async_computation | async-start | bytes 1572864 | tf_op jit(solution)/shard_map/all_to_all | solution.py:43
  28.3 6.8 %copy-start.1 = (f32[4,128,256]{2,1,0:T(8,128)S(1)}, f32[4,128,256]{2,1,0:T(8,128)}, u32[]{:S(2)}) copy-start(f32[4,128,256]{2,1,0:T(8,128)} %copy-done) | copy-start | bytes 1572868
  29.7 14.6 %collective-permute-start.6 = (bf16[2,6,32,256]{3,2,1,0:T(8,128)(2,1)}, bf16[2,6,32,256]{3,2,1,0:T(8,128)(2,1)}, u32[]{:S(2)}, u32[]{:S(2)}) collective-permute-start(bf16[2,6,32,256]{3,2,1,0:T(8,128)(2,1)} %get-tuple-element.47), channel_id=1, source_target_pairs={{0,4},{4,8},{8,12},{1,5},{5,9},{9,13},{2,6},{6,10},{10,14},{3,7},{... | collective-permute-start | bytes 589832 | tf_op jit(solution)/shard_map/ppermute | solution.py:40
  32.1 12.2 %collective-permute-start.4 = (bf16[4,2,32,256]{3,2,1,0:T(8,128)(2,1)}, bf16[4,2,32,256]{3,2,1,0:T(8,128)(2,1)}, u32[]{:S(2)}, u32[]{:S(2)}) collective-permute-start(bf16[4,2,32,256]{3,2,1,0:T(8,128)(2,1)} %get-tuple-element.45), channel_id=1, source_target_pairs={{0,1},{1,0},{2,3},{3,2},{4,5},{5,4},{6,7},{7,6},{8,9},{9,8},{10,11... | collective-permute-start | bytes 393224 | tf_op jit(solution)/shard_map/ppermute | solution.py:34
  33.8 10.4 %collective-permute-start.5 = (bf16[4,2,32,256]{3,2,1,0:T(8,128)(2,1)}, bf16[4,2,32,256]{3,2,1,0:T(8,128)(2,1)}, u32[]{:S(2)}, u32[]{:S(2)}) collective-permute-start(bf16[4,2,32,256]{3,2,1,0:T(8,128)(2,1)} %get-tuple-element.46), channel_id=1, source_target_pairs={{1,2},{2,1},{5,6},{6,5},{9,10},{10,9},{13,14},{14,13},{17,18},{18,... | collective-permute-start | bytes 393224 | tf_op jit(solution)/shard_map/ppermute | solution.py:49
  42.4 8.2 %collective-permute-start.7 = (bf16[192,256]{1,0:T(8,128)(2,1)S(1)}, bf16[192,256]{1,0:T(8,128)(2,1)S(1)}, u32[]{:S(2)}, u32[]{:S(2)}) collective-permute-start(bf16[192,256]{1,0:T(8,128)(2,1)S(1)} %sum_parts.1._.own_ref), channel_id=1, source_target_pairs={{0,2},{2,0},{1,3},{3,1},{4,6},{6,4},{5,7},{7,5},{8,10},{10,8},{9,1... | collective-permute-start | bytes 294920 | tf_op jit(solution)/shard_map/ppermute | solution.py:34
  64.3 2.3 %collective-permute-start.8 = (bf16[12,128,256]{2,1,0:T(8,128)(2,1)S(1)}, bf16[12,128,256]{2,1,0:T(8,128)(2,1)S(1)}, u32[]{:S(2)}, u32[]{:S(2)}) collective-permute-start(bf16[12,128,256]{2,1,0:T(8,128)(2,1)S(1)} %bitcast.9), channel_id=1, source_target_pairs={{0,4},{4,0},{1,5},{5,1},{2,6},{6,2},{3,7},{7,3},{8,12},{12,8},{9,1... | collective-permute-start | bytes 2359304 | tf_op jit(solution)/shard_map/ppermute | solution.py:34

commit v21 on v20

--- a/solution.py
+++ b/solution.py
@@ -404,8 +404,8 @@
     group = rows_at_once(rows_low, cols_low)
     span, count = group * cols_low, rows_low * cols_low
     pairs = [(inner_hbm, inner_ref), (outer_hbm, outer_ref)]
-    pairs += [(edge_hbm, edge_ref), (wt_hbm, wt_ref)]
-    pairs += [(act_hbm.at[n], act_ref.at[n]) for n in range(frames)] + [(sort_hbm, wide_ref), (low_hbm, low_ref)]
+    pairs += [(edge_hbm, edge_ref), (wt_hbm, wt_ref), (sort_hbm, wide_ref), (low_hbm, low_ref)]
+    pairs += [(act_hbm.at[n], act_ref.at[n]) for n in range(frames)]
     copies = [pltpu.make_async_copy(a, b, sems.at[n]) for n, (a, b) in enumerate(pairs)]
     for copy in copies:
         copy.start()
@@ -440,11 +440,12 @@
         copy.wait()
     for side, pre in enumerate(spatial(edge_ref[...], ws_ref)):
         earlier[:, side] = (pre * jax.nn.sigmoid(pre)).astype(jnp.bfloat16).reshape(2, count, chan)
-    for copy in copies[3:]:
+    for copy in copies[3:6]:
         copy.wait()
     merge = wide_ref[...].T.astype(jnp.bfloat16)
     wt = wt_ref[...].reshape(3 * chan, chan)
     for frame in range(frames):
+        copies[6 + frame].wait()
         acts = [act_ref[frame - k] if frame >= k else earlier[frame - k + 2] for k in range(3)]
         acts = jnp.concatenate([act.reshape(4 * count, chan) for act in acts], axis=1)
         low = low_ref[frame].reshape(1, count, chan).astype(jnp.float32)
@@ -508,18 +509,26 @@
     )(place, half, *done)
 
 
-def add_kernel(mine_ref, theirs_ref, out_ref):
-    out_ref[...] = (mine_ref[...] + theirs_ref[...]).astype(jnp.bfloat16)
+def add_kernel(mine_ref, theirs_ref, out_ref, held, sems):
+    size = held.shape[0] // 4
+    copies = []
+    for n in range(4):
+        at = pl.ds(n * size, size)
+        held[at] = (mine_ref[at] + theirs_ref[at]).astype(jnp.bfloat16)
+        copies.append(pltpu.make_async_copy(held.at[at], out_ref.at[at], sems.at[n]))
+        copies[-1].start()
+    for copy in copies:
+        copy.wait()
 
 
 def add_halves(mine, theirs):
-    full = pl.BlockSpec(memory_space=pltpu.VMEM)
     return pl.pallas_call(
         add_kernel,
-        in_specs=[full, full],
-        out_specs=full,
-        out_shape=like(mine.shape, jnp.bfloat16),
-        compiler_params=grant(8),
+        in_specs=[FULL, FULL],
+        out_specs=HBM,
+        out_shape=pltpu.HBM(mine.shape, jnp.bfloat16),
+        scratch_shapes=[pltpu.VMEM(mine.shape, jnp.bfloat16), pltpu.SemaphoreType.DMA((4,))],
+        compiler_params=grant(6),
         name="add_halves",
     )(mine, theirs)
 
@@ -580,10 +589,10 @@
     own, act, box = half_grads(mine, low_in, inner, outer, act, pg, ext)
     kept = add_halves(own, theirs)
     got = bits.exchange(kept.reshape(parts, -1, chan))
-    edge, pg_inner, pg_outer = edges(mine, low_in, inner, outer, pg, kept)
+    edge, pg_inner, pg_outer = edges(mine, low_in, inner, outer, pg, in_hbm(kept))
     edge = bits.shift(edge, "tm", 1)
     pg_inner, pg_outer = bits.pairs(pg_inner, pg_outer)
-    own_part = input_own(pg, box, ws, kept, low.shape)
+    own_part = input_own(pg, box, ws, in_hbm(kept), low.shape)
     total, far = bits.far_sums(sum_parts(got, own_part))
     section_out, input_grad, done = finish(
         mine, own_part, ws, pg_inner, pg_outer, edge, act, temporal_weight, order, low, total

time: 68.8 us -> 69.4 us (level)
  transfers between devices with their start and end apart: 10 -> 10, of which waited for: 3 -> 3; matrix products, arithmetic and copies ran while one was open for 0% -> 0% of each run, Pallas kernels for 27% -> 28%
where the time goes in v21:
time: 69.4 us; the launch traced here: 69 us
  Pallas kernels  26.9 us (39%)
  starting transfers between devices  21 us (30%)
  blocking collectives  13.6 us (20%)
  waiting for transfers between devices  6.43 us (9%)
  between operations  0.96 us (1%)
    all_to_all x1, blocking collectives, exchange(): return lax.all_to_all(parts, tuple(self.near), 0, 0, tiled=True)  13.6 us
    ppermute x5, starting transfers between devices, swap(): return lax.ppermute(block, axis, [(0, 1), (1, 0)])  8.64 us
    pallas_call x1, Pallas kernels, finish(): pl.pallas_call(finish_kernel, in_specs=[SCALAR, FULL, FULL] + [HBM] * 7 +...  6.94 us
    all_to_all x1, starting transfers between devices, exchange(): return lax.all_to_all(parts, tuple(self.near), 0, 0, tiled=True)  6.61 us
    all_to_all x1, waiting for transfers between devices, exchange(): return lax.all_to_all(parts, tuple(self.near), 0, 0, tiled=True)  5.59 us
    ppermute x2, starting transfers between devices, shift(): return lax.ppermute(block, axes, route)  3.74 us
    pallas_call x2, Pallas kernels, put(): pl.pallas_call(put_kernel, in_specs=[SCALAR, FULL] + [HBM] * len(done), o...  3.56 us
    pallas_call x1, Pallas kernels, backward(): pl.pallas_call(backward_kernel, in_specs=[SCALAR] + [FULL] * 9, out_specs...  3.35 us
  transfers between devices with their start and end apart: 10, of which 3 were waited for; matrix products, arithmetic and copies ran while one was open for 0% of the time, Pallas kernels for 28%

profile of v21, /device:TPU:0, one launch (start us, length us, event | category | flops | bytes accessed | tf_op | source)
XLA Modules:
  0.0 69.0 jit_solution(1244338109708429167)
XLA Ops:
  0.6 0.1 pad_add_fusion.place_ref
  0.7 1.7 %first_messages.1 = (bf16[4,1,32,256]{3,2,1,0:T(8,128)(2,1)S(1)}, bf16[4,1,32,256]{3,2,1,0:T(8,128)(2,1)S(1)}, bf16[2,8,64,256]{3,2,1,0:T(8,128)(2,1)S(1)}) custom-call(s32[2]{0:T(128)S(1)} %pad_add_fusion.place_ref, bf16[4,4,32,256]{3,2,1,0:T(8,128)(2,1)} %bitcast.14, bf16[4,8,64,256]{3,2,1,0:T(8,128)(2,1)} %bitcast.12), custom_call_target="tpu_custom_call" | custom-call | tf_op jit(solution)/shard_map/first_messages/pallas_call | solution.py:232
  2.4 1.3 %collective-permute-start.2 = (bf16[2,8,64,256]{3,2,1,0:T(8,128)(2,1)S(1)}, bf16[2,8,64,256]{3,2,1,0:T(8,128)(2,1)S(1)}, u32[]{:S(2)}, u32[]{:S(2)}) collective-permute-start(bf16[2,8,64,256]{3,2,1,0:T(8,128)(2,1)S(1)} %get-tuple-element.37), channel_id=1, source_target_pairs={{4,0},{8,4},{12,8},{5,1},{9,5},{13,9},{6,2},{10,6},{14,10},{7,3},{... | collective-permute-start | bytes 1572872 | tf_op jit(solution)/shard_map/ppermute | solution.py:40
  3.7 3.1 %collective-permute-start = (bf16[4,1,32,256]{3,2,1,0:T(8,128)(2,1)S(1)}, bf16[4,1,32,256]{3,2,1,0:T(8,128)(2,1)S(1)}, u32[]{:S(2)}, u32[]{:S(2)}) collective-permute-start(bf16[4,1,32,256]{3,2,1,0:T(8,128)(2,1)S(1)} %get-tuple-element.31), channel_id=1, source_target_pairs={{0,1},{1,0},{2,3},{3,2},{4,5},{5,4},{6,7},{7,6},{8,9},{9,8},{10,11... | collective-permute-start | bytes 196616 | tf_op jit(solution)/shard_map/ppermute | solution.py:34
  6.8 0.7 collective-permute-start.1
  7.5 0.1 pad_add_fusion.1.place_ref
  7.5 2.4 %load.1 = (bf16[4,4,32,256]{3,2,1,0:T(8,128)(2,1)S(1)}, bf16[3,3,256,256]{3,2,1,0:T(8,128)(2,1)S(1)}, bf16[256,256]{1,0:T(8,128)(2,1)S(1)}, bf16[768,256]{1,0:T(8,128)(2,1)S(1)}, bf16[4,4,128,256]{3,2,1,0:T(8,128)(2,1)S(1)}) custom-call(bf16[4,4,32,256]{3,2,1,0:T(8,128)(2,1)} %bitcast.15, bf16[4,8,64,256]{3,2,1,0:T(8,128)(2,1)} %bitcast.13, ...), custom_call_target="tpu_custom_call" | custom-call | flops 536870912 | bytes 4194304 | tf_op jit(solution)/shard_map/load/pallas_call | solution.py:269
  9.9 0.0 collective-permute-done.inner_ref
  9.9 0.0 collective-permute-done.1.outer_ref
  9.9 2.3 %forward.1 = (bf16[4,4,128,256]{3,2,1,0:T(8,128)(2,1)S(1)}, f32[4,4,128,256]{3,2,1,0:T(8,128)S(1)}) custom-call(s32[2]{0:T(128)S(1)} %pad_add_fusion.place_ref, bf16[4,4,32,256]{3,2,1,0:T(8,128)(2,1)S(1)} %get-tuple-element.30.low_ref, bf16[4,1,32,256]{3,2,1,0:T(8,128)(2,1)S(1)} %collective-permute-done.inner_ref, ...), custom_call_target="tpu_custom_call" | custom-call | flops 2684354560 | bytes 8388608 | tf_op jit(solution)/shard_map/forward/pallas_call | solution.py:285
  12.3 0.0 collective-permute-done.2.later_ref
  12.3 3.3 %backward.1 = (bf16[4,4,128,256]{3,2,1,0:T(8,128)(2,1)S(1)}, bf16[6,4,128,256]{3,2,1,0:T(8,128)(2,1)S(1)}, f32[12,128,256]{2,1,0:T(8,128)S(1)}) custom-call(s32[2]{0:T(128)S(1)} %pad_add_fusion.1.place_ref, bf16[4,4,32,256]{3,2,1,0:T(8,128)(2,1)S(1)} %get-tuple-element.30.low_ref, bf16[4,1,32,256]{3,2,1,0:T(8,128)(2,1)S(1)} %collective-permute-done.inner_ref, ...), custom_call_target="tpu_custom_call" | custom-call | flops 4026531840 | bytes 10485760 | tf_op jit(solution)/shard_map/backward/pallas_call | solution.py:324
  15.6 2.0 %collective-permute-start.3 = (f32[12,128,256]{2,1,0:T(8,128)S(1)}, f32[12,128,256]{2,1,0:T(8,128)S(1)}, u32[]{:S(2)}, u32[]{:S(2)}) collective-permute-start(f32[12,128,256]{2,1,0:T(8,128)S(1)} %get-tuple-element.44), channel_id=1, source_target_pairs={{0,4},{4,0},{1,5},{5,1},{2,6},{6,2},{3,7},{7,3},{8,12},{12,8},{9,1... | collective-permute-start | bytes 4718600 | tf_op jit(solution)/shard_map/ppermute | solution.py:34
  17.6 2.7 %half_grads.1 = (f32[12,128,256]{2,1,0:T(8,128)S(1)}, bf16[4,4,128,256]{3,2,1,0:T(8,128)(2,1)}, f32[4,128,256]{2,1,0:T(8,128)S(1)}) custom-call(s32[2]{0:T(128)S(1)} %pad_add_fusion.place_ref, bf16[4,4,32,256]{3,2,1,0:T(8,128)(2,1)S(1)} %get-tuple-element.30.low_ref, bf16[4,1,32,256]{3,2,1,0:T(8,128)(2,1)S(1)} %collective-permute-done.inner_ref, ...), custom_call_target="tpu_custom_call" | custom-call | flops 2684354560 | bytes 6291456 | tf_op jit(solution)/shard_map/half_grads/pallas_call | solution.py:337
  20.3 0.0 copy-start
  20.3 0.3 collective-permute-done.3.theirs_ref
  20.7 1.0 %add_halves.1._ = bf16[12,128,256]{2,1,0:T(8,128)(2,1)} custom-call(f32[12,128,256]{2,1,0:T(8,128)S(1)} %get-tuple-element.43.mine_ref, f32[12,128,256]{2,1,0:T(8,128)S(1)} %collective-permute-done.3.theirs_ref), custom_call_target="tpu_custom_call" | custom-call | tf_op jit(solution)/shard_map/add_halves/pallas_call | solution.py:525
  21.7 0.0 copy-done
  21.7 6.6 %all-to-all-start = ((bf16[8,192,256]{2,1,0:T(8,128)(2,1)}), bf16[8,192,256]{2,1,0:T(8,128)(2,1)S(1)}, u32[]{:S(2)}, u32[]{:S(2)}) async-start(bf16[8,192,256]{2,1,0:T(8,128)(2,1)} %bitcast.11), calls=%async_computation | async-start | bytes 1572864 | tf_op jit(solution)/shard_map/all_to_all | solution.py:43
  28.3 0.0 copy-start.1
  28.3 1.3 %edges.1 = (bf16[2,6,32,256]{3,2,1,0:T(8,128)(2,1)}, bf16[4,2,32,256]{3,2,1,0:T(8,128)(2,1)}, bf16[4,2,32,256]{3,2,1,0:T(8,128)(2,1)}) custom-call(s32[2]{0:T(128)S(1)} %pad_add_fusion.place_ref, bf16[4,4,32,256]{3,2,1,0:T(8,128)(2,1)S(1)} %get-tuple-element.30.low_ref, bf16[4,1,32,256]{3,2,1,0:T(8,128)(2,1)S(1)} %collective-permute-done.inner_ref, ...), custom_call_target="tpu_custom_call" | custom-call | tf_op jit(solution)/shard_map/edges/pallas_call | solution.py:311
  29.6 2.4 %collective-permute-start.6 = (bf16[2,6,32,256]{3,2,1,0:T(8,128)(2,1)}, bf16[2,6,32,256]{3,2,1,0:T(8,128)(2,1)}, u32[]{:S(2)}, u32[]{:S(2)}) collective-permute-start(bf16[2,6,32,256]{3,2,1,0:T(8,128)(2,1)} %get-tuple-element.47), channel_id=1, source_target_pairs={{0,4},{4,8},{8,12},{1,5},{5,9},{9,13},{2,6},{6,10},{10,14},{3,7},{... | collective-permute-start | bytes 589832 | tf_op jit(solution)/shard_map/ppermute | solution.py:40
  32.1 1.7 %collective-permute-start.4 = (bf16[4,2,32,256]{3,2,1,0:T(8,128)(2,1)}, bf16[4,2,32,256]{3,2,1,0:T(8,128)(2,1)}, u32[]{:S(2)}, u32[]{:S(2)}) collective-permute-start(bf16[4,2,32,256]{3,2,1,0:T(8,128)(2,1)} %get-tuple-element.45), channel_id=1, source_target_pairs={{0,1},{1,0},{2,3},{3,2},{4,5},{5,4},{6,7},{7,6},{8,9},{9,8},{10,11... | collective-permute-start | bytes 393224 | tf_op jit(solution)/shard_map/ppermute | solution.py:34
  33.8 1.3 %collective-permute-start.5 = (bf16[4,2,32,256]{3,2,1,0:T(8,128)(2,1)}, bf16[4,2,32,256]{3,2,1,0:T(8,128)(2,1)}, u32[]{:S(2)}, u32[]{:S(2)}) collective-permute-start(bf16[4,2,32,256]{3,2,1,0:T(8,128)(2,1)} %get-tuple-element.46), channel_id=1, source_target_pairs={{1,2},{2,1},{5,6},{6,5},{9,10},{10,9},{13,14},{14,13},{17,18},{18,... | collective-permute-start | bytes 393224 | tf_op jit(solution)/shard_map/ppermute | solution.py:49
  35.1 0.0 copy-done.1
  35.1 1.6 %input_own.1._.own_ref = f32[4,4,32,256]{3,2,1,0:T(8,128)S(1)} custom-call(bf16[4,4,128,256]{3,2,1,0:T(8,128)(2,1)S(1)} %get-tuple-element.40.pg_ref, f32[4,128,256]{2,1,0:T(8,128)S(1)} %copy-done.1, bf16[3,3,256,256]{3,2,1,0:T(8,128)(2,1)S(1)} %get-tuple-element.33.ws_ref, bf16[12,128,256]{2,1,0:T(8,128)(2,1)} %add_halves.1._), custom_call_target="tpu_custom_call" | custom-call | flops 1610612736 | bytes 4194304 | tf_op jit(solution)/shard_map/input_own/pallas_call | solution.py:389
  36.7 5.6 %all-to-all-done.got_ref = bf16[8,192,256]{2,1,0:T(8,128)(2,1)S(1)} async-done(((bf16[8,192,256]{2,1,0:T(8,128)(2,1)}), bf16[8,192,256]{2,1,0:T(8,128)(2,1)S(1)}, u32[]{:S(2)}, u32[]{:S(2)}) %all-to-all-start) | async-done | bytes 786464 | tf_op jit(solution)/shard_map/all_to_all | solution.py:43
  42.3 0.1 sum_parts.1._.own_ref
  42.4 1.8 %collective-permute-start.7 = (bf16[192,256]{1,0:T(8,128)(2,1)S(1)}, bf16[192,256]{1,0:T(8,128)(2,1)S(1)}, u32[]{:S(2)}, u32[]{:S(2)}) collective-permute-start(bf16[192,256]{1,0:T(8,128)(2,1)S(1)} %sum_parts.1._.own_ref), channel_id=1, source_target_pairs={{0,2},{2,0},{1,3},{3,1},{4,6},{6,4},{5,7},{7,5},{8,10},{10,8},{9,1... | collective-permute-start | bytes 294920 | tf_op jit(solution)/shard_map/ppermute | solution.py:34
  44.2 0.0 collective-permute-done.4.inner_hbm
  44.2 0.0 collective-permute-done.5.outer_hbm
  44.2 0.0 collective-permute-done.6.edge_hbm
  44.2 6.9 %finish.1 = (bf16[4,8,64,256]{3,2,1,0:T(8,128)(2,1)}, bf16[4,4,32,256]{3,2,1,0:T(8,128)(2,1)}, f32[8,128]{1,0:T(8,128)S(1)}) custom-call(s32[2]{0:T(128)S(1)} %pad_add_fusion.place_ref, f32[4,4,32,256]{3,2,1,0:T(8,128)S(1)} %input_own.1._.own_ref, bf16[3,3,256,256]{3,2,1,0:T(8,128)(2,1)S(1)} %get-tuple-element.33.ws_ref, ...), custom_call_target="tpu_custom_call" | custom-call | flops 2147483648 | bytes 4194304 | tf_op jit(solution)/shard_map/finish/pallas_call | solution.py:467
  51.2 0.0 collective-permute-done.7.theirs_ref
  51.2 0.1 spread.1
  51.2 13.6 %all_to_all.10 = bf16[8,192,256]{2,1,0:T(8,128)(2,1)S(1)} all-to-all(bf16[8,192,256]{2,1,0:T(8,128)(2,1)S(1)} %spread.1), channel_id=1, replica_groups=mesh['dp0'=2,'tm1'=2,'tm0'=2,'height1'=2,'height0'=2] {'dp0','tm1','heig..., dimensions={0} | all-to-all | bytes 1572864 | tf_op jit(solution)/shard_map/all_to_all | solution.py:43
  64.8 0.0 collective-permute-start.8
  64.8 1.8 %put.2 = (f32[3,3,256,256]{3,2,1,0:T(8,128)}, f32[3,256,256]{2,1,0:T(8,128)}) custom-call(s32[2]{0:T(128)S(1)} %pad_add_fusion.place_ref, bf16[12,128,256]{2,1,0:T(8,128)(2,1)S(1)} %bitcast.10), custom_call_target="tpu_custom_call" | custom-call | tf_op jit(solution)/shard_map/put/pallas_call | solution.py:500
  66.6 0.5 collective-permute-done.8.half_ref
  67.1 1.8 %put.3 = (f32[3,3,256,256]{3,2,1,0:T(8,128)}, f32[3,256,256]{2,1,0:T(8,128)}) custom-call(s32[2]{0:T(128)S(1)} %pad_add_fusion.1.place_ref, bf16[12,128,256]{2,1,0:T(8,128)(2,1)S(1)} %collective-permute-done.8.half_ref, f32[3,3,256,256]{3,2,1,0:T(8,128)} %get-tuple-element.52.refs_0_, ...), custom_call_target="tpu_custom_call", output_to_operand_aliasing={{0}: (2, {}), {1}: (3, {})} | custom-call | tf_op jit(solution)/shard_map/put/pallas_call | solution.py:500
Async XLA Ops:
  2.4 9.9 %collective-permute-start.2 = (bf16[2,8,64,256]{3,2,1,0:T(8,128)(2,1)S(1)}, bf16[2,8,64,256]{3,2,1,0:T(8,128)(2,1)S(1)}, u32[]{:S(2)}, u32[]{:S(2)}) collective-permute-start(bf16[2,8,64,256]{3,2,1,0:T(8,128)(2,1)S(1)} %get-tuple-element.37), channel_id=1, source_target_pairs={{4,0},{8,4},{12,8},{5,1},{9,5},{13,9},{6,2},{10,6},{14,10},{7,3},{... | collective-permute-start | bytes 1572872 | tf_op jit(solution)/shard_map/ppermute | solution.py:40
  3.7 6.2 %collective-permute-start = (bf16[4,1,32,256]{3,2,1,0:T(8,128)(2,1)S(1)}, bf16[4,1,32,256]{3,2,1,0:T(8,128)(2,1)S(1)}, u32[]{:S(2)}, u32[]{:S(2)}) collective-permute-start(bf16[4,1,32,256]{3,2,1,0:T(8,128)(2,1)S(1)} %get-tuple-element.31), channel_id=1, source_target_pairs={{0,1},{1,0},{2,3},{3,2},{4,5},{5,4},{6,7},{7,6},{8,9},{9,8},{10,11... | collective-permute-start | bytes 196616 | tf_op jit(solution)/shard_map/ppermute | solution.py:34
  6.8 3.1 %collective-permute-start.1 = (bf16[4,1,32,256]{3,2,1,0:T(8,128)(2,1)S(1)}, bf16[4,1,32,256]{3,2,1,0:T(8,128)(2,1)S(1)}, u32[]{:S(2)}, u32[]{:S(2)}) collective-permute-start(bf16[4,1,32,256]{3,2,1,0:T(8,128)(2,1)S(1)} %get-tuple-element.32), channel_id=1, source_target_pairs={{1,2},{2,1},{5,6},{6,5},{9,10},{10,9},{13,14},{14,13},{17,18},{18,... | collective-permute-start | bytes 196616 | tf_op jit(solution)/shard_map/ppermute | solution.py:49
  15.6 5.0 %collective-permute-start.3 = (f32[12,128,256]{2,1,0:T(8,128)S(1)}, f32[12,128,256]{2,1,0:T(8,128)S(1)}, u32[]{:S(2)}, u32[]{:S(2)}) collective-permute-start(f32[12,128,256]{2,1,0:T(8,128)S(1)} %get-tuple-element.44), channel_id=1, source_target_pairs={{0,4},{4,0},{1,5},{5,1},{2,6},{6,2},{3,7},{7,3},{8,12},{12,8},{9,1... | collective-permute-start | bytes 4718600 | tf_op jit(solution)/shard_map/ppermute | solution.py:34
  20.3 1.3 %copy-start = (f32[4,128,256]{2,1,0:T(8,128)}, f32[4,128,256]{2,1,0:T(8,128)S(1)}, u32[]{:S(2)}) copy-start(f32[4,128,256]{2,1,0:T(8,128)S(1)} %get-tuple-element.42.box_ref) | copy-start | bytes 1572868
  21.7 20.6 %all-to-all-start = ((bf16[8,192,256]{2,1,0:T(8,128)(2,1)}), bf16[8,192,256]{2,1,0:T(8,128)(2,1)S(1)}, u32[]{:S(2)}, u32[]{:S(2)}) async-start(bf16[8,192,256]{2,1,0:T(8,128)(2,1)} %bitcast.11), calls=%async_computation | async-start | bytes 1572864 | tf_op jit(solution)/shard_map/all_to_all | solution.py:43
  28.3 6.8 %copy-start.1 = (f32[4,128,256]{2,1,0:T(8,128)S(1)}, f32[4,128,256]{2,1,0:T(8,128)}, u32[]{:S(2)}) copy-start(f32[4,128,256]{2,1,0:T(8,128)} %copy-done) | copy-start | bytes 1572868
  29.6 14.6 %collective-permute-start.6 = (bf16[2,6,32,256]{3,2,1,0:T(8,128)(2,1)}, bf16[2,6,32,256]{3,2,1,0:T(8,128)(2,1)}, u32[]{:S(2)}, u32[]{:S(2)}) collective-permute-start(bf16[2,6,32,256]{3,2,1,0:T(8,128)(2,1)} %get-tuple-element.47), channel_id=1, source_target_pairs={{0,4},{4,8},{8,12},{1,5},{5,9},{9,13},{2,6},{6,10},{10,14},{3,7},{... | collective-permute-start | bytes 589832 | tf_op jit(solution)/shard_map/ppermute | solution.py:40
  32.1 12.1 %collective-permute-start.4 = (bf16[4,2,32,256]{3,2,1,0:T(8,128)(2,1)}, bf16[4,2,32,256]{3,2,1,0:T(8,128)(2,1)}, u32[]{:S(2)}, u32[]{:S(2)}) collective-permute-start(bf16[4,2,32,256]{3,2,1,0:T(8,128)(2,1)} %get-tuple-element.45), channel_id=1, source_target_pairs={{0,1},{1,0},{2,3},{3,2},{4,5},{5,4},{6,7},{7,6},{8,9},{9,8},{10,11... | collective-permute-start | bytes 393224 | tf_op jit(solution)/shard_map/ppermute | solution.py:34
  33.8 10.4 %collective-permute-start.5 = (bf16[4,2,32,256]{3,2,1,0:T(8,128)(2,1)}, bf16[4,2,32,256]{3,2,1,0:T(8,128)(2,1)}, u32[]{:S(2)}, u32[]{:S(2)}) collective-permute-start(bf16[4,2,32,256]{3,2,1,0:T(8,128)(2,1)} %get-tuple-element.46), channel_id=1, source_target_pairs={{1,2},{2,1},{5,6},{6,5},{9,10},{10,9},{13,14},{14,13},{17,18},{18,... | collective-permute-start | bytes 393224 | tf_op jit(solution)/shard_map/ppermute | solution.py:49
  42.4 8.8 %collective-permute-start.7 = (bf16[192,256]{1,0:T(8,128)(2,1)S(1)}, bf16[192,256]{1,0:T(8,128)(2,1)S(1)}, u32[]{:S(2)}, u32[]{:S(2)}) collective-permute-start(bf16[192,256]{1,0:T(8,128)(2,1)S(1)} %sum_parts.1._.own_ref), channel_id=1, source_target_pairs={{0,2},{2,0},{1,3},{3,1},{4,6},{6,4},{5,7},{7,5},{8,10},{10,8},{9,1... | collective-permute-start | bytes 294920 | tf_op jit(solution)/shard_map/ppermute | solution.py:34
  64.8 2.3 %collective-permute-start.8 = (bf16[12,128,256]{2,1,0:T(8,128)(2,1)S(1)}, bf16[12,128,256]{2,1,0:T(8,128)(2,1)S(1)}, u32[]{:S(2)}, u32[]{:S(2)}) collective-permute-start(bf16[12,128,256]{2,1,0:T(8,128)(2,1)S(1)} %bitcast.9), channel_id=1, source_target_pairs={{0,4},{4,0},{1,5},{5,1},{2,6},{6,2},{3,7},{7,3},{8,12},{12,8},{9,1... | collective-permute-start | bytes 2359304 | tf_op jit(solution)/shard_map/ppermute | solution.py:34

commit v22 on v20

--- a/solution.py
+++ b/solution.py
@@ -411,7 +411,7 @@
         copy.start()
     token_ref[...] = jnp.zeros_like(token_ref)
 
-    for copy in copies[:2]:
+    for copy in copies[:3]:
         copy.wait()
     odd_place = place_ref[1] == 1
     flat = (frames * cols_low, chan)
@@ -436,8 +436,6 @@
     leaving = [pltpu.make_async_copy(input_held, input_ref, sems.at[len(copies)])]
     leaving[0].start()
 
-    for copy in copies[2:3]:
-        copy.wait()
     for side, pre in enumerate(spatial(edge_ref[...], ws_ref)):
         earlier[:, side] = (pre * jax.nn.sigmoid(pre)).astype(jnp.bfloat16).reshape(2, count, chan)
     for copy in copies[3:]:

time: 68.8 us -> 68.7 us (level)
  no operation moved by 1% of the time
where the time goes in v22:
time: 68.7 us; the launch traced here: 68.4 us
  Pallas kernels  26.3 us (38%)
  starting transfers between devices  20.9 us (30%)
  blocking collectives  13.5 us (20%)
  waiting for transfers between devices  6.47 us (9%)
  between operations  0.94 us (1%)
    all_to_all x1, blocking collectives, exchange(): return lax.all_to_all(parts, tuple(self.near), 0, 0, tiled=True)  13.5 us
    ppermute x5, starting transfers between devices, swap(): return lax.ppermute(block, axis, [(0, 1), (1, 0)])  8.63 us
    all_to_all x1, starting transfers between devices, exchange(): return lax.all_to_all(parts, tuple(self.near), 0, 0, tiled=True)  6.63 us
    pallas_call x1, Pallas kernels, finish(): pl.pallas_call(finish_kernel, in_specs=[SCALAR, FULL, FULL] + [HBM] * 7 +...  6.29 us
    all_to_all x1, waiting for transfers between devices, exchange(): return lax.all_to_all(parts, tuple(self.near), 0, 0, tiled=True)  5.63 us
    ppermute x2, starting transfers between devices, shift(): return lax.ppermute(block, axes, route)  3.71 us
    pallas_call x2, Pallas kernels, put(): pl.pallas_call(put_kernel, in_specs=[SCALAR, FULL] + [HBM] * len(done), o...  3.56 us
    pallas_call x1, Pallas kernels, backward(): pl.pallas_call(backward_kernel, in_specs=[SCALAR] + [FULL] * 9, out_specs...  3.35 us
  transfers between devices with their start and end apart: 10, of which 3 were waited for; matrix products, arithmetic and copies ran while one was open for 0% of the time, Pallas kernels for 27%

profile of v22, /device:TPU:0, one launch (start us, length us, event | category | flops | bytes accessed | tf_op | source)
XLA Modules:
  0.0 68.4 jit_solution(8672718817858106807)
XLA Ops:
  0.6 0.1 pad_add_fusion.place_ref
  0.7 1.7 %first_messages.1 = (bf16[4,1,32,256]{3,2,1,0:T(8,128)(2,1)S(1)}, bf16[4,1,32,256]{3,2,1,0:T(8,128)(2,1)S(1)}, bf16[2,8,64,256]{3,2,1,0:T(8,128)(2,1)S(1)}) custom-call(s32[2]{0:T(128)S(1)} %pad_add_fusion.place_ref, bf16[4,4,32,256]{3,2,1,0:T(8,128)(2,1)} %bitcast.13, bf16[4,8,64,256]{3,2,1,0:T(8,128)(2,1)} %bitcast.11), custom_call_target="tpu_custom_call" | custom-call | tf_op jit(solution)/shard_map/first_messages/pallas_call | solution.py:232
  2.4 1.3 %collective-permute-start.2 = (bf16[2,8,64,256]{3,2,1,0:T(8,128)(2,1)S(1)}, bf16[2,8,64,256]{3,2,1,0:T(8,128)(2,1)S(1)}, u32[]{:S(2)}, u32[]{:S(2)}) collective-permute-start(bf16[2,8,64,256]{3,2,1,0:T(8,128)(2,1)S(1)} %get-tuple-element.37), channel_id=1, source_target_pairs={{4,0},{8,4},{12,8},{5,1},{9,5},{13,9},{6,2},{10,6},{14,10},{7,3},{... | collective-permute-start | bytes 1572872 | tf_op jit(solution)/shard_map/ppermute | solution.py:40
  3.7 3.1 %collective-permute-start = (bf16[4,1,32,256]{3,2,1,0:T(8,128)(2,1)S(1)}, bf16[4,1,32,256]{3,2,1,0:T(8,128)(2,1)S(1)}, u32[]{:S(2)}, u32[]{:S(2)}) collective-permute-start(bf16[4,1,32,256]{3,2,1,0:T(8,128)(2,1)S(1)} %get-tuple-element.31), channel_id=1, source_target_pairs={{0,1},{1,0},{2,3},{3,2},{4,5},{5,4},{6,7},{7,6},{8,9},{9,8},{10,11... | collective-permute-start | bytes 196616 | tf_op jit(solution)/shard_map/ppermute | solution.py:34
  6.8 0.7 collective-permute-start.1
  7.5 0.1 pad_add_fusion.1.place_ref
  7.5 2.4 %load.1 = (bf16[4,4,32,256]{3,2,1,0:T(8,128)(2,1)S(1)}, bf16[3,3,256,256]{3,2,1,0:T(8,128)(2,1)S(1)}, bf16[256,256]{1,0:T(8,128)(2,1)S(1)}, bf16[768,256]{1,0:T(8,128)(2,1)S(1)}, bf16[4,4,128,256]{3,2,1,0:T(8,128)(2,1)S(1)}) custom-call(bf16[4,4,32,256]{3,2,1,0:T(8,128)(2,1)} %bitcast.14, bf16[4,8,64,256]{3,2,1,0:T(8,128)(2,1)} %bitcast.12, ...), custom_call_target="tpu_custom_call" | custom-call | flops 536870912 | bytes 4194304 | tf_op jit(solution)/shard_map/load/pallas_call | solution.py:269
  9.9 0.0 collective-permute-done.inner_ref
  9.9 0.0 collective-permute-done.1.outer_ref
  9.9 2.3 %forward.1 = (bf16[4,4,128,256]{3,2,1,0:T(8,128)(2,1)S(1)}, f32[4,4,128,256]{3,2,1,0:T(8,128)S(1)}) custom-call(s32[2]{0:T(128)S(1)} %pad_add_fusion.place_ref, bf16[4,4,32,256]{3,2,1,0:T(8,128)(2,1)S(1)} %get-tuple-element.30.low_ref, bf16[4,1,32,256]{3,2,1,0:T(8,128)(2,1)S(1)} %collective-permute-done.inner_ref, ...), custom_call_target="tpu_custom_call" | custom-call | flops 2684354560 | bytes 8388608 | tf_op jit(solution)/shard_map/forward/pallas_call | solution.py:285
  12.3 0.0 collective-permute-done.2.later_ref
  12.3 3.3 %backward.1 = (bf16[4,4,128,256]{3,2,1,0:T(8,128)(2,1)S(1)}, bf16[6,4,128,256]{3,2,1,0:T(8,128)(2,1)S(1)}, f32[12,128,256]{2,1,0:T(8,128)S(1)}) custom-call(s32[2]{0:T(128)S(1)} %pad_add_fusion.1.place_ref, bf16[4,4,32,256]{3,2,1,0:T(8,128)(2,1)S(1)} %get-tuple-element.30.low_ref, bf16[4,1,32,256]{3,2,1,0:T(8,128)(2,1)S(1)} %collective-permute-done.inner_ref, ...), custom_call_target="tpu_custom_call" | custom-call | flops 4026531840 | bytes 10485760 | tf_op jit(solution)/shard_map/backward/pallas_call | solution.py:324
  15.6 2.0 %collective-permute-start.3 = (f32[12,128,256]{2,1,0:T(8,128)S(1)}, f32[12,128,256]{2,1,0:T(8,128)S(1)}, u32[]{:S(2)}, u32[]{:S(2)}) collective-permute-start(f32[12,128,256]{2,1,0:T(8,128)S(1)} %get-tuple-element.44), channel_id=1, source_target_pairs={{0,4},{4,0},{1,5},{5,1},{2,6},{6,2},{3,7},{7,3},{8,12},{12,8},{9,1... | collective-permute-start | bytes 4718600 | tf_op jit(solution)/shard_map/ppermute | solution.py:34
  17.6 2.7 %half_grads.1 = (f32[12,128,256]{2,1,0:T(8,128)S(1)}, bf16[4,4,128,256]{3,2,1,0:T(8,128)(2,1)}, f32[4,128,256]{2,1,0:T(8,128)S(1)}) custom-call(s32[2]{0:T(128)S(1)} %pad_add_fusion.place_ref, bf16[4,4,32,256]{3,2,1,0:T(8,128)(2,1)S(1)} %get-tuple-element.30.low_ref, bf16[4,1,32,256]{3,2,1,0:T(8,128)(2,1)S(1)} %collective-permute-done.inner_ref, ...), custom_call_target="tpu_custom_call" | custom-call | flops 2684354560 | bytes 6291456 | tf_op jit(solution)/shard_map/half_grads/pallas_call | solution.py:337
  20.3 0.0 copy-start
  20.3 0.3 collective-permute-done.3.theirs_ref
  20.7 1.0 %add_halves.1._ = bf16[12,128,256]{2,1,0:T(8,128)(2,1)} custom-call(f32[12,128,256]{2,1,0:T(8,128)S(1)} %get-tuple-element.43.mine_ref, f32[12,128,256]{2,1,0:T(8,128)S(1)} %collective-permute-done.3.theirs_ref), custom_call_target="tpu_custom_call" | custom-call | tf_op jit(solution)/shard_map/add_halves/pallas_call | solution.py:515
  21.7 0.0 copy-done
  21.7 6.6 %all-to-all-start = ((bf16[8,192,256]{2,1,0:T(8,128)(2,1)}), bf16[8,192,256]{2,1,0:T(8,128)(2,1)S(1)}, u32[]{:S(2)}, u32[]{:S(2)}) async-start(bf16[8,192,256]{2,1,0:T(8,128)(2,1)} %bitcast.5), calls=%async_computation | async-start | bytes 1572864 | tf_op jit(solution)/shard_map/all_to_all | solution.py:43
  28.3 0.0 copy-start.1
  28.3 1.3 %edges.1 = (bf16[2,6,32,256]{3,2,1,0:T(8,128)(2,1)}, bf16[4,2,32,256]{3,2,1,0:T(8,128)(2,1)}, bf16[4,2,32,256]{3,2,1,0:T(8,128)(2,1)}) custom-call(s32[2]{0:T(128)S(1)} %pad_add_fusion.place_ref, bf16[4,4,32,256]{3,2,1,0:T(8,128)(2,1)S(1)} %get-tuple-element.30.low_ref, bf16[4,1,32,256]{3,2,1,0:T(8,128)(2,1)S(1)} %collective-permute-done.inner_ref, ...), custom_call_target="tpu_custom_call" | custom-call | tf_op jit(solution)/shard_map/edges/pallas_call | solution.py:311
  29.7 2.4 %collective-permute-start.6 = (bf16[2,6,32,256]{3,2,1,0:T(8,128)(2,1)}, bf16[2,6,32,256]{3,2,1,0:T(8,128)(2,1)}, u32[]{:S(2)}, u32[]{:S(2)}) collective-permute-start(bf16[2,6,32,256]{3,2,1,0:T(8,128)(2,1)} %get-tuple-element.47), channel_id=1, source_target_pairs={{0,4},{4,8},{8,12},{1,5},{5,9},{9,13},{2,6},{6,10},{10,14},{3,7},{... | collective-permute-start | bytes 589832 | tf_op jit(solution)/shard_map/ppermute | solution.py:40
  32.1 1.7 %collective-permute-start.4 = (bf16[4,2,32,256]{3,2,1,0:T(8,128)(2,1)}, bf16[4,2,32,256]{3,2,1,0:T(8,128)(2,1)}, u32[]{:S(2)}, u32[]{:S(2)}) collective-permute-start(bf16[4,2,32,256]{3,2,1,0:T(8,128)(2,1)} %get-tuple-element.45), channel_id=1, source_target_pairs={{0,1},{1,0},{2,3},{3,2},{4,5},{5,4},{6,7},{7,6},{8,9},{9,8},{10,11... | collective-permute-start | bytes 393224 | tf_op jit(solution)/shard_map/ppermute | solution.py:34
  33.8 1.3 %collective-permute-start.5 = (bf16[4,2,32,256]{3,2,1,0:T(8,128)(2,1)}, bf16[4,2,32,256]{3,2,1,0:T(8,128)(2,1)}, u32[]{:S(2)}, u32[]{:S(2)}) collective-permute-start(bf16[4,2,32,256]{3,2,1,0:T(8,128)(2,1)} %get-tuple-element.46), channel_id=1, source_target_pairs={{1,2},{2,1},{5,6},{6,5},{9,10},{10,9},{13,14},{14,13},{17,18},{18,... | collective-permute-start | bytes 393224 | tf_op jit(solution)/shard_map/ppermute | solution.py:49
  35.1 0.0 copy-done.1
  35.1 1.6 %input_own.1._.own_ref = f32[4,4,32,256]{3,2,1,0:T(8,128)S(1)} custom-call(bf16[4,4,128,256]{3,2,1,0:T(8,128)(2,1)S(1)} %get-tuple-element.40.pg_ref, f32[4,128,256]{2,1,0:T(8,128)S(1)} %copy-done.1, bf16[3,3,256,256]{3,2,1,0:T(8,128)(2,1)S(1)} %get-tuple-element.33.ws_ref, bf16[12,128,256]{2,1,0:T(8,128)(2,1)} %add_halves.1._), custom_call_target="tpu_custom_call" | custom-call | flops 1610612736 | bytes 4194304 | tf_op jit(solution)/shard_map/input_own/pallas_call | solution.py:389
  36.7 5.6 %all-to-all-done.got_ref = bf16[8,192,256]{2,1,0:T(8,128)(2,1)S(1)} async-done(((bf16[8,192,256]{2,1,0:T(8,128)(2,1)}), bf16[8,192,256]{2,1,0:T(8,128)(2,1)S(1)}, u32[]{:S(2)}, u32[]{:S(2)}) %all-to-all-start) | async-done | bytes 786464 | tf_op jit(solution)/shard_map/all_to_all | solution.py:43
  42.3 0.1 sum_parts.1._.own_ref
  42.4 1.8 %collective-permute-start.7 = (bf16[192,256]{1,0:T(8,128)(2,1)S(1)}, bf16[192,256]{1,0:T(8,128)(2,1)S(1)}, u32[]{:S(2)}, u32[]{:S(2)}) collective-permute-start(bf16[192,256]{1,0:T(8,128)(2,1)S(1)} %sum_parts.1._.own_ref), channel_id=1, source_target_pairs={{0,2},{2,0},{1,3},{3,1},{4,6},{6,4},{5,7},{7,5},{8,10},{10,8},{9,1... | collective-permute-start | bytes 294920 | tf_op jit(solution)/shard_map/ppermute | solution.py:34
  44.2 0.0 collective-permute-done.4.inner_hbm
  44.2 0.0 collective-permute-done.5.outer_hbm
  44.2 0.0 collective-permute-done.6.edge_hbm
  44.3 6.3 %finish.1 = (bf16[4,8,64,256]{3,2,1,0:T(8,128)(2,1)}, bf16[4,4,32,256]{3,2,1,0:T(8,128)(2,1)}, f32[8,128]{1,0:T(8,128)S(1)}) custom-call(s32[2]{0:T(128)S(1)} %pad_add_fusion.place_ref, f32[4,4,32,256]{3,2,1,0:T(8,128)S(1)} %input_own.1._.own_ref, bf16[3,3,256,256]{3,2,1,0:T(8,128)(2,1)S(1)} %get-tuple-element.33.ws_ref, ...), custom_call_target="tpu_custom_call" | custom-call | flops 2147483648 | bytes 4194304 | tf_op jit(solution)/shard_map/finish/pallas_call | solution.py:464
  50.5 0.0 collective-permute-done.7.theirs_ref
  50.6 0.1 spread.1
  50.6 13.5 %all_to_all.10 = bf16[8,192,256]{2,1,0:T(8,128)(2,1)S(1)} all-to-all(bf16[8,192,256]{2,1,0:T(8,128)(2,1)S(1)} %spread.1), channel_id=1, replica_groups=mesh['dp0'=2,'tm1'=2,'tm0'=2,'height1'=2,'height0'=2] {'dp0','tm1','heig..., dimensions={0} | all-to-all | bytes 1572864 | tf_op jit(solution)/shard_map/all_to_all | solution.py:43
  64.2 0.0 collective-permute-start.8
  64.2 1.8 %put.2 = (f32[3,3,256,256]{3,2,1,0:T(8,128)}, f32[3,256,256]{2,1,0:T(8,128)}) custom-call(s32[2]{0:T(128)S(1)} %pad_add_fusion.place_ref, bf16[12,128,256]{2,1,0:T(8,128)(2,1)S(1)} %bitcast.10), custom_call_target="tpu_custom_call" | custom-call | tf_op jit(solution)/shard_map/put/pallas_call | solution.py:497
  66.0 0.5 collective-permute-done.8.half_ref
  66.5 1.8 %put.3 = (f32[3,3,256,256]{3,2,1,0:T(8,128)}, f32[3,256,256]{2,1,0:T(8,128)}) custom-call(s32[2]{0:T(128)S(1)} %pad_add_fusion.1.place_ref, bf16[12,128,256]{2,1,0:T(8,128)(2,1)S(1)} %collective-permute-done.8.half_ref, f32[3,3,256,256]{3,2,1,0:T(8,128)} %get-tuple-element.52.refs_0_, ...), custom_call_target="tpu_custom_call", output_to_operand_aliasing={{0}: (2, {}), {1}: (3, {})} | custom-call | tf_op jit(solution)/shard_map/put/pallas_call | solution.py:497
Async XLA Ops:
  2.4 9.9 %collective-permute-start.2 = (bf16[2,8,64,256]{3,2,1,0:T(8,128)(2,1)S(1)}, bf16[2,8,64,256]{3,2,1,0:T(8,128)(2,1)S(1)}, u32[]{:S(2)}, u32[]{:S(2)}) collective-permute-start(bf16[2,8,64,256]{3,2,1,0:T(8,128)(2,1)S(1)} %get-tuple-element.37), channel_id=1, source_target_pairs={{4,0},{8,4},{12,8},{5,1},{9,5},{13,9},{6,2},{10,6},{14,10},{7,3},{... | collective-permute-start | bytes 1572872 | tf_op jit(solution)/shard_map/ppermute | solution.py:40
  3.7 6.2 %collective-permute-start = (bf16[4,1,32,256]{3,2,1,0:T(8,128)(2,1)S(1)}, bf16[4,1,32,256]{3,2,1,0:T(8,128)(2,1)S(1)}, u32[]{:S(2)}, u32[]{:S(2)}) collective-permute-start(bf16[4,1,32,256]{3,2,1,0:T(8,128)(2,1)S(1)} %get-tuple-element.31), channel_id=1, source_target_pairs={{0,1},{1,0},{2,3},{3,2},{4,5},{5,4},{6,7},{7,6},{8,9},{9,8},{10,11... | collective-permute-start | bytes 196616 | tf_op jit(solution)/shard_map/ppermute | solution.py:34
  6.8 3.1 %collective-permute-start.1 = (bf16[4,1,32,256]{3,2,1,0:T(8,128)(2,1)S(1)}, bf16[4,1,32,256]{3,2,1,0:T(8,128)(2,1)S(1)}, u32[]{:S(2)}, u32[]{:S(2)}) collective-permute-start(bf16[4,1,32,256]{3,2,1,0:T(8,128)(2,1)S(1)} %get-tuple-element.32), channel_id=1, source_target_pairs={{1,2},{2,1},{5,6},{6,5},{9,10},{10,9},{13,14},{14,13},{17,18},{18,... | collective-permute-start | bytes 196616 | tf_op jit(solution)/shard_map/ppermute | solution.py:49
  15.6 5.0 %collective-permute-start.3 = (f32[12,128,256]{2,1,0:T(8,128)S(1)}, f32[12,128,256]{2,1,0:T(8,128)S(1)}, u32[]{:S(2)}, u32[]{:S(2)}) collective-permute-start(f32[12,128,256]{2,1,0:T(8,128)S(1)} %get-tuple-element.44), channel_id=1, source_target_pairs={{0,4},{4,0},{1,5},{5,1},{2,6},{6,2},{3,7},{7,3},{8,12},{12,8},{9,1... | collective-permute-start | bytes 4718600 | tf_op jit(solution)/shard_map/ppermute | solution.py:34
  20.3 1.4 %copy-start = (f32[4,128,256]{2,1,0:T(8,128)}, f32[4,128,256]{2,1,0:T(8,128)S(1)}, u32[]{:S(2)}) copy-start(f32[4,128,256]{2,1,0:T(8,128)S(1)} %get-tuple-element.42.box_ref) | copy-start | bytes 1572868
  21.7 20.6 %all-to-all-start = ((bf16[8,192,256]{2,1,0:T(8,128)(2,1)}), bf16[8,192,256]{2,1,0:T(8,128)(2,1)S(1)}, u32[]{:S(2)}, u32[]{:S(2)}) async-start(bf16[8,192,256]{2,1,0:T(8,128)(2,1)} %bitcast.5), calls=%async_computation | async-start | bytes 1572864 | tf_op jit(solution)/shard_map/all_to_all | solution.py:43
  28.3 6.8 %copy-start.1 = (f32[4,128,256]{2,1,0:T(8,128)S(1)}, f32[4,128,256]{2,1,0:T(8,128)}, u32[]{:S(2)}) copy-start(f32[4,128,256]{2,1,0:T(8,128)} %copy-done) | copy-start | bytes 1572868
  29.7 14.6 %collective-permute-start.6 = (bf16[2,6,32,256]{3,2,1,0:T(8,128)(2,1)}, bf16[2,6,32,256]{3,2,1,0:T(8,128)(2,1)}, u32[]{:S(2)}, u32[]{:S(2)}) collective-permute-start(bf16[2,6,32,256]{3,2,1,0:T(8,128)(2,1)} %get-tuple-element.47), channel_id=1, source_target_pairs={{0,4},{4,8},{8,12},{1,5},{5,9},{9,13},{2,6},{6,10},{10,14},{3,7},{... | collective-permute-start | bytes 589832 | tf_op jit(solution)/shard_map/ppermute | solution.py:40
  32.1 12.2 %collective-permute-start.4 = (bf16[4,2,32,256]{3,2,1,0:T(8,128)(2,1)}, bf16[4,2,32,256]{3,2,1,0:T(8,128)(2,1)}, u32[]{:S(2)}, u32[]{:S(2)}) collective-permute-start(bf16[4,2,32,256]{3,2,1,0:T(8,128)(2,1)} %get-tuple-element.45), channel_id=1, source_target_pairs={{0,1},{1,0},{2,3},{3,2},{4,5},{5,4},{6,7},{7,6},{8,9},{9,8},{10,11... | collective-permute-start | bytes 393224 | tf_op jit(solution)/shard_map/ppermute | solution.py:34
  33.8 10.4 %collective-permute-start.5 = (bf16[4,2,32,256]{3,2,1,0:T(8,128)(2,1)}, bf16[4,2,32,256]{3,2,1,0:T(8,128)(2,1)}, u32[]{:S(2)}, u32[]{:S(2)}) collective-permute-start(bf16[4,2,32,256]{3,2,1,0:T(8,128)(2,1)} %get-tuple-element.46), channel_id=1, source_target_pairs={{1,2},{2,1},{5,6},{6,5},{9,10},{10,9},{13,14},{14,13},{17,18},{18,... | collective-permute-start | bytes 393224 | tf_op jit(solution)/shard_map/ppermute | solution.py:49
  42.4 8.1 %collective-permute-start.7 = (bf16[192,256]{1,0:T(8,128)(2,1)S(1)}, bf16[192,256]{1,0:T(8,128)(2,1)S(1)}, u32[]{:S(2)}, u32[]{:S(2)}) collective-permute-start(bf16[192,256]{1,0:T(8,128)(2,1)S(1)} %sum_parts.1._.own_ref), channel_id=1, source_target_pairs={{0,2},{2,0},{1,3},{3,1},{4,6},{6,4},{5,7},{7,5},{8,10},{10,8},{9,1... | collective-permute-start | bytes 294920 | tf_op jit(solution)/shard_map/ppermute | solution.py:34
  64.2 2.3 %collective-permute-start.8 = (bf16[12,128,256]{2,1,0:T(8,128)(2,1)S(1)}, bf16[12,128,256]{2,1,0:T(8,128)(2,1)S(1)}, u32[]{:S(2)}, u32[]{:S(2)}) collective-permute-start(bf16[12,128,256]{2,1,0:T(8,128)(2,1)S(1)} %bitcast.9), channel_id=1, source_target_pairs={{0,4},{4,0},{1,5},{5,1},{2,6},{6,2},{3,7},{7,3},{8,12},{12,8},{9,1... | collective-permute-start | bytes 2359304 | tf_op jit(solution)/shard_map/ppermute | solution.py:34

commit v23 on v22

--- a/solution.py
+++ b/solution.py
@@ -433,11 +433,10 @@
         if row == rows_low - 1:
             value = value + terms[1]
         input_held[:, row] = value.astype(jnp.bfloat16)
+    for side, pre in enumerate(spatial(edge_ref[...], ws_ref)):
+        earlier[:, side] = (pre * jax.nn.sigmoid(pre)).astype(jnp.bfloat16).reshape(2, count, chan)
     leaving = [pltpu.make_async_copy(input_held, input_ref, sems.at[len(copies)])]
     leaving[0].start()
-
-    for side, pre in enumerate(spatial(edge_ref[...], ws_ref)):
-        earlier[:, side] = (pre * jax.nn.sigmoid(pre)).astype(jnp.bfloat16).reshape(2, count, chan)
     for copy in copies[3:]:
         copy.wait()
     merge = wide_ref[...].T.astype(jnp.bfloat16)

time: 68.7 us -> 68.7 us (level)
  no operation moved by 1% of the time
where the time goes in v23:
time: 68.7 us; the launch traced here: 68.4 us
  Pallas kernels  26.3 us (38%)
  starting transfers between devices  20.9 us (30%)
  blocking collectives  13.5 us (20%)
  waiting for transfers between devices  6.47 us (9%)
  between operations  0.94 us (1%)
    all_to_all x1, blocking collectives, exchange(): return lax.all_to_all(parts, tuple(self.near), 0, 0, tiled=True)  13.5 us
    ppermute x5, starting transfers between devices, swap(): return lax.ppermute(block, axis, [(0, 1), (1, 0)])  8.63 us
    all_to_all x1, starting transfers between devices, exchange(): return lax.all_to_all(parts, tuple(self.near), 0, 0, tiled=True)  6.63 us
    pallas_call x1, Pallas kernels, finish(): pl.pallas_call(finish_kernel, in_specs=[SCALAR, FULL, FULL] + [HBM] * 7 +...  6.29 us
    all_to_all x1, waiting for transfers between devices, exchange(): return lax.all_to_all(parts, tuple(self.near), 0, 0, tiled=True)  5.63 us
    ppermute x2, starting transfers between devices, shift(): return lax.ppermute(block, axes, route)  3.71 us
    pallas_call x2, Pallas kernels, put(): pl.pallas_call(put_kernel, in_specs=[SCALAR, FULL] + [HBM] * len(done), o...  3.56 us
    pallas_call x1, Pallas kernels, backward(): pl.pallas_call(backward_kernel, in_specs=[SCALAR] + [FULL] * 9, out_specs...  3.35 us
  transfers between devices with their start and end apart: 10, of which 3 were waited for; matrix products, arithmetic and copies ran while one was open for 0% of the time, Pallas kernels for 27%

profile of v23, /device:TPU:0, one launch (start us, length us, event | category | flops | bytes accessed | tf_op | source)
XLA Modules:
  0.0 68.4 jit_solution(8672718817858106807)
XLA Ops:
  0.6 0.1 pad_add_fusion.place_ref
  0.7 1.7 %first_messages.1 = (bf16[4,1,32,256]{3,2,1,0:T(8,128)(2,1)S(1)}, bf16[4,1,32,256]{3,2,1,0:T(8,128)(2,1)S(1)}, bf16[2,8,64,256]{3,2,1,0:T(8,128)(2,1)S(1)}) custom-call(s32[2]{0:T(128)S(1)} %pad_add_fusion.place_ref, bf16[4,4,32,256]{3,2,1,0:T(8,128)(2,1)} %bitcast.13, bf16[4,8,64,256]{3,2,1,0:T(8,128)(2,1)} %bitcast.11), custom_call_target="tpu_custom_call" | custom-call | tf_op jit(solution)/shard_map/first_messages/pallas_call | solution.py:232
  2.4 1.3 %collective-permute-start.2 = (bf16[2,8,64,256]{3,2,1,0:T(8,128)(2,1)S(1)}, bf16[2,8,64,256]{3,2,1,0:T(8,128)(2,1)S(1)}, u32[]{:S(2)}, u32[]{:S(2)}) collective-permute-start(bf16[2,8,64,256]{3,2,1,0:T(8,128)(2,1)S(1)} %get-tuple-element.37), channel_id=1, source_target_pairs={{4,0},{8,4},{12,8},{5,1},{9,5},{13,9},{6,2},{10,6},{14,10},{7,3},{... | collective-permute-start | bytes 1572872 | tf_op jit(solution)/shard_map/ppermute | solution.py:40
  3.7 3.1 %collective-permute-start = (bf16[4,1,32,256]{3,2,1,0:T(8,128)(2,1)S(1)}, bf16[4,1,32,256]{3,2,1,0:T(8,128)(2,1)S(1)}, u32[]{:S(2)}, u32[]{:S(2)}) collective-permute-start(bf16[4,1,32,256]{3,2,1,0:T(8,128)(2,1)S(1)} %get-tuple-element.31), channel_id=1, source_target_pairs={{0,1},{1,0},{2,3},{3,2},{4,5},{5,4},{6,7},{7,6},{8,9},{9,8},{10,11... | collective-permute-start | bytes 196616 | tf_op jit(solution)/shard_map/ppermute | solution.py:34
  6.8 0.7 collective-permute-start.1
  7.5 0.1 pad_add_fusion.1.place_ref
  7.5 2.4 %load.1 = (bf16[4,4,32,256]{3,2,1,0:T(8,128)(2,1)S(1)}, bf16[3,3,256,256]{3,2,1,0:T(8,128)(2,1)S(1)}, bf16[256,256]{1,0:T(8,128)(2,1)S(1)}, bf16[768,256]{1,0:T(8,128)(2,1)S(1)}, bf16[4,4,128,256]{3,2,1,0:T(8,128)(2,1)S(1)}) custom-call(bf16[4,4,32,256]{3,2,1,0:T(8,128)(2,1)} %bitcast.14, bf16[4,8,64,256]{3,2,1,0:T(8,128)(2,1)} %bitcast.12, ...), custom_call_target="tpu_custom_call" | custom-call | flops 536870912 | bytes 4194304 | tf_op jit(solution)/shard_map/load/pallas_call | solution.py:269
  9.9 0.0 collective-permute-done.inner_ref
  9.9 0.0 collective-permute-done.1.outer_ref
  9.9 2.3 %forward.1 = (bf16[4,4,128,256]{3,2,1,0:T(8,128)(2,1)S(1)}, f32[4,4,128,256]{3,2,1,0:T(8,128)S(1)}) custom-call(s32[2]{0:T(128)S(1)} %pad_add_fusion.place_ref, bf16[4,4,32,256]{3,2,1,0:T(8,128)(2,1)S(1)} %get-tuple-element.30.low_ref, bf16[4,1,32,256]{3,2,1,0:T(8,128)(2,1)S(1)} %collective-permute-done.inner_ref, ...), custom_call_target="tpu_custom_call" | custom-call | flops 2684354560 | bytes 8388608 | tf_op jit(solution)/shard_map/forward/pallas_call | solution.py:285
  12.3 0.0 collective-permute-done.2.later_ref
  12.3 3.3 %backward.1 = (bf16[4,4,128,256]{3,2,1,0:T(8,128)(2,1)S(1)}, bf16[6,4,128,256]{3,2,1,0:T(8,128)(2,1)S(1)}, f32[12,128,256]{2,1,0:T(8,128)S(1)}) custom-call(s32[2]{0:T(128)S(1)} %pad_add_fusion.1.place_ref, bf16[4,4,32,256]{3,2,1,0:T(8,128)(2,1)S(1)} %get-tuple-element.30.low_ref, bf16[4,1,32,256]{3,2,1,0:T(8,128)(2,1)S(1)} %collective-permute-done.inner_ref, ...), custom_call_target="tpu_custom_call" | custom-call | flops 4026531840 | bytes 10485760 | tf_op jit(solution)/shard_map/backward/pallas_call | solution.py:324
  15.6 2.0 %collective-permute-start.3 = (f32[12,128,256]{2,1,0:T(8,128)S(1)}, f32[12,128,256]{2,1,0:T(8,128)S(1)}, u32[]{:S(2)}, u32[]{:S(2)}) collective-permute-start(f32[12,128,256]{2,1,0:T(8,128)S(1)} %get-tuple-element.44), channel_id=1, source_target_pairs={{0,4},{4,0},{1,5},{5,1},{2,6},{6,2},{3,7},{7,3},{8,12},{12,8},{9,1... | collective-permute-start | bytes 4718600 | tf_op jit(solution)/shard_map/ppermute | solution.py:34
  17.6 2.7 %half_grads.1 = (f32[12,128,256]{2,1,0:T(8,128)S(1)}, bf16[4,4,128,256]{3,2,1,0:T(8,128)(2,1)}, f32[4,128,256]{2,1,0:T(8,128)S(1)}) custom-call(s32[2]{0:T(128)S(1)} %pad_add_fusion.place_ref, bf16[4,4,32,256]{3,2,1,0:T(8,128)(2,1)S(1)} %get-tuple-element.30.low_ref, bf16[4,1,32,256]{3,2,1,0:T(8,128)(2,1)S(1)} %collective-permute-done.inner_ref, ...), custom_call_target="tpu_custom_call" | custom-call | flops 2684354560 | bytes 6291456 | tf_op jit(solution)/shard_map/half_grads/pallas_call | solution.py:337
  20.3 0.0 copy-start
  20.3 0.3 collective-permute-done.3.theirs_ref
  20.7 1.0 %add_halves.1._ = bf16[12,128,256]{2,1,0:T(8,128)(2,1)} custom-call(f32[12,128,256]{2,1,0:T(8,128)S(1)} %get-tuple-element.43.mine_ref, f32[12,128,256]{2,1,0:T(8,128)S(1)} %collective-permute-done.3.theirs_ref), custom_call_target="tpu_custom_call" | custom-call | tf_op jit(solution)/shard_map/add_halves/pallas_call | solution.py:514
  21.7 0.0 copy-done
  21.7 6.6 %all-to-all-start = ((bf16[8,192,256]{2,1,0:T(8,128)(2,1)}), bf16[8,192,256]{2,1,0:T(8,128)(2,1)S(1)}, u32[]{:S(2)}, u32[]{:S(2)}) async-start(bf16[8,192,256]{2,1,0:T(8,128)(2,1)} %bitcast.5), calls=%async_computation | async-start | bytes 1572864 | tf_op jit(solution)/shard_map/all_to_all | solution.py:43
  28.3 0.0 copy-start.1
  28.3 1.3 %edges.1 = (bf16[2,6,32,256]{3,2,1,0:T(8,128)(2,1)}, bf16[4,2,32,256]{3,2,1,0:T(8,128)(2,1)}, bf16[4,2,32,256]{3,2,1,0:T(8,128)(2,1)}) custom-call(s32[2]{0:T(128)S(1)} %pad_add_fusion.place_ref, bf16[4,4,32,256]{3,2,1,0:T(8,128)(2,1)S(1)} %get-tuple-element.30.low_ref, bf16[4,1,32,256]{3,2,1,0:T(8,128)(2,1)S(1)} %collective-permute-done.inner_ref, ...), custom_call_target="tpu_custom_call" | custom-call | tf_op jit(solution)/shard_map/edges/pallas_call | solution.py:311
  29.7 2.4 %collective-permute-start.6 = (bf16[2,6,32,256]{3,2,1,0:T(8,128)(2,1)}, bf16[2,6,32,256]{3,2,1,0:T(8,128)(2,1)}, u32[]{:S(2)}, u32[]{:S(2)}) collective-permute-start(bf16[2,6,32,256]{3,2,1,0:T(8,128)(2,1)} %get-tuple-element.47), channel_id=1, source_target_pairs={{0,4},{4,8},{8,12},{1,5},{5,9},{9,13},{2,6},{6,10},{10,14},{3,7},{... | collective-permute-start | bytes 589832 | tf_op jit(solution)/shard_map/ppermute | solution.py:40
  32.1 1.7 %collective-permute-start.4 = (bf16[4,2,32,256]{3,2,1,0:T(8,128)(2,1)}, bf16[4,2,32,256]{3,2,1,0:T(8,128)(2,1)}, u32[]{:S(2)}, u32[]{:S(2)}) collective-permute-start(bf16[4,2,32,256]{3,2,1,0:T(8,128)(2,1)} %get-tuple-element.45), channel_id=1, source_target_pairs={{0,1},{1,0},{2,3},{3,2},{4,5},{5,4},{6,7},{7,6},{8,9},{9,8},{10,11... | collective-permute-start | bytes 393224 | tf_op jit(solution)/shard_map/ppermute | solution.py:34
  33.8 1.3 %collective-permute-start.5 = (bf16[4,2,32,256]{3,2,1,0:T(8,128)(2,1)}, bf16[4,2,32,256]{3,2,1,0:T(8,128)(2,1)}, u32[]{:S(2)}, u32[]{:S(2)}) collective-permute-start(bf16[4,2,32,256]{3,2,1,0:T(8,128)(2,1)} %get-tuple-element.46), channel_id=1, source_target_pairs={{1,2},{2,1},{5,6},{6,5},{9,10},{10,9},{13,14},{14,13},{17,18},{18,... | collective-permute-start | bytes 393224 | tf_op jit(solution)/shard_map/ppermute | solution.py:49
  35.1 0.0 copy-done.1
  35.1 1.6 %input_own.1._.own_ref = f32[4,4,32,256]{3,2,1,0:T(8,128)S(1)} custom-call(bf16[4,4,128,256]{3,2,1,0:T(8,128)(2,1)S(1)} %get-tuple-element.40.pg_ref, f32[4,128,256]{2,1,0:T(8,128)S(1)} %copy-done.1, bf16[3,3,256,256]{3,2,1,0:T(8,128)(2,1)S(1)} %get-tuple-element.33.ws_ref, bf16[12,128,256]{2,1,0:T(8,128)(2,1)} %add_halves.1._), custom_call_target="tpu_custom_call" | custom-call | flops 1610612736 | bytes 4194304 | tf_op jit(solution)/shard_map/input_own/pallas_call | solution.py:389
  36.7 5.6 %all-to-all-done.got_ref = bf16[8,192,256]{2,1,0:T(8,128)(2,1)S(1)} async-done(((bf16[8,192,256]{2,1,0:T(8,128)(2,1)}), bf16[8,192,256]{2,1,0:T(8,128)(2,1)S(1)}, u32[]{:S(2)}, u32[]{:S(2)}) %all-to-all-start) | async-done | bytes 786464 | tf_op jit(solution)/shard_map/all_to_all | solution.py:43
  42.3 0.1 sum_parts.1._.own_ref
  42.4 1.8 %collective-permute-start.7 = (bf16[192,256]{1,0:T(8,128)(2,1)S(1)}, bf16[192,256]{1,0:T(8,128)(2,1)S(1)}, u32[]{:S(2)}, u32[]{:S(2)}) collective-permute-start(bf16[192,256]{1,0:T(8,128)(2,1)S(1)} %sum_parts.1._.own_ref), channel_id=1, source_target_pairs={{0,2},{2,0},{1,3},{3,1},{4,6},{6,4},{5,7},{7,5},{8,10},{10,8},{9,1... | collective-permute-start | bytes 294920 | tf_op jit(solution)/shard_map/ppermute | solution.py:34
  44.2 0.0 collective-permute-done.4.inner_hbm
  44.2 0.0 collective-permute-done.5.outer_hbm
  44.2 0.0 collective-permute-done.6.edge_hbm
  44.3 6.3 %finish.1 = (bf16[4,8,64,256]{3,2,1,0:T(8,128)(2,1)}, bf16[4,4,32,256]{3,2,1,0:T(8,128)(2,1)}, f32[8,128]{1,0:T(8,128)S(1)}) custom-call(s32[2]{0:T(128)S(1)} %pad_add_fusion.place_ref, f32[4,4,32,256]{3,2,1,0:T(8,128)S(1)} %input_own.1._.own_ref, bf16[3,3,256,256]{3,2,1,0:T(8,128)(2,1)S(1)} %get-tuple-element.33.ws_ref, ...), custom_call_target="tpu_custom_call" | custom-call | flops 2147483648 | bytes 4194304 | tf_op jit(solution)/shard_map/finish/pallas_call | solution.py:463
  50.5 0.0 collective-permute-done.7.theirs_ref
  50.6 0.1 spread.1
  50.6 13.5 %all_to_all.10 = bf16[8,192,256]{2,1,0:T(8,128)(2,1)S(1)} all-to-all(bf16[8,192,256]{2,1,0:T(8,128)(2,1)S(1)} %spread.1), channel_id=1, replica_groups=mesh['dp0'=2,'tm1'=2,'tm0'=2,'height1'=2,'height0'=2] {'dp0','tm1','heig..., dimensions={0} | all-to-all | bytes 1572864 | tf_op jit(solution)/shard_map/all_to_all | solution.py:43
  64.2 0.0 collective-permute-start.8
  64.2 1.8 %put.2 = (f32[3,3,256,256]{3,2,1,0:T(8,128)}, f32[3,256,256]{2,1,0:T(8,128)}) custom-call(s32[2]{0:T(128)S(1)} %pad_add_fusion.place_ref, bf16[12,128,256]{2,1,0:T(8,128)(2,1)S(1)} %bitcast.10), custom_call_target="tpu_custom_call" | custom-call | tf_op jit(solution)/shard_map/put/pallas_call | solution.py:496
  66.0 0.5 collective-permute-done.8.half_ref
  66.5 1.8 %put.3 = (f32[3,3,256,256]{3,2,1,0:T(8,128)}, f32[3,256,256]{2,1,0:T(8,128)}) custom-call(s32[2]{0:T(128)S(1)} %pad_add_fusion.1.place_ref, bf16[12,128,256]{2,1,0:T(8,128)(2,1)S(1)} %collective-permute-done.8.half_ref, f32[3,3,256,256]{3,2,1,0:T(8,128)} %get-tuple-element.52.refs_0_, ...), custom_call_target="tpu_custom_call", output_to_operand_aliasing={{0}: (2, {}), {1}: (3, {})} | custom-call | tf_op jit(solution)/shard_map/put/pallas_call | solution.py:496
Async XLA Ops:
  2.4 9.9 %collective-permute-start.2 = (bf16[2,8,64,256]{3,2,1,0:T(8,128)(2,1)S(1)}, bf16[2,8,64,256]{3,2,1,0:T(8,128)(2,1)S(1)}, u32[]{:S(2)}, u32[]{:S(2)}) collective-permute-start(bf16[2,8,64,256]{3,2,1,0:T(8,128)(2,1)S(1)} %get-tuple-element.37), channel_id=1, source_target_pairs={{4,0},{8,4},{12,8},{5,1},{9,5},{13,9},{6,2},{10,6},{14,10},{7,3},{... | collective-permute-start | bytes 1572872 | tf_op jit(solution)/shard_map/ppermute | solution.py:40
  3.7 6.2 %collective-permute-start = (bf16[4,1,32,256]{3,2,1,0:T(8,128)(2,1)S(1)}, bf16[4,1,32,256]{3,2,1,0:T(8,128)(2,1)S(1)}, u32[]{:S(2)}, u32[]{:S(2)}) collective-permute-start(bf16[4,1,32,256]{3,2,1,0:T(8,128)(2,1)S(1)} %get-tuple-element.31), channel_id=1, source_target_pairs={{0,1},{1,0},{2,3},{3,2},{4,5},{5,4},{6,7},{7,6},{8,9},{9,8},{10,11... | collective-permute-start | bytes 196616 | tf_op jit(solution)/shard_map/ppermute | solution.py:34
  6.8 3.1 %collective-permute-start.1 = (bf16[4,1,32,256]{3,2,1,0:T(8,128)(2,1)S(1)}, bf16[4,1,32,256]{3,2,1,0:T(8,128)(2,1)S(1)}, u32[]{:S(2)}, u32[]{:S(2)}) collective-permute-start(bf16[4,1,32,256]{3,2,1,0:T(8,128)(2,1)S(1)} %get-tuple-element.32), channel_id=1, source_target_pairs={{1,2},{2,1},{5,6},{6,5},{9,10},{10,9},{13,14},{14,13},{17,18},{18,... | collective-permute-start | bytes 196616 | tf_op jit(solution)/shard_map/ppermute | solution.py:49
  15.6 5.0 %collective-permute-start.3 = (f32[12,128,256]{2,1,0:T(8,128)S(1)}, f32[12,128,256]{2,1,0:T(8,128)S(1)}, u32[]{:S(2)}, u32[]{:S(2)}) collective-permute-start(f32[12,128,256]{2,1,0:T(8,128)S(1)} %get-tuple-element.44), channel_id=1, source_target_pairs={{0,4},{4,0},{1,5},{5,1},{2,6},{6,2},{3,7},{7,3},{8,12},{12,8},{9,1... | collective-permute-start | bytes 4718600 | tf_op jit(solution)/shard_map/ppermute | solution.py:34
  20.3 1.4 %copy-start = (f32[4,128,256]{2,1,0:T(8,128)}, f32[4,128,256]{2,1,0:T(8,128)S(1)}, u32[]{:S(2)}) copy-start(f32[4,128,256]{2,1,0:T(8,128)S(1)} %get-tuple-element.42.box_ref) | copy-start | bytes 1572868
  21.7 20.6 %all-to-all-start = ((bf16[8,192,256]{2,1,0:T(8,128)(2,1)}), bf16[8,192,256]{2,1,0:T(8,128)(2,1)S(1)}, u32[]{:S(2)}, u32[]{:S(2)}) async-start(bf16[8,192,256]{2,1,0:T(8,128)(2,1)} %bitcast.5), calls=%async_computation | async-start | bytes 1572864 | tf_op jit(solution)/shard_map/all_to_all | solution.py:43
  28.3 6.8 %copy-start.1 = (f32[4,128,256]{2,1,0:T(8,128)S(1)}, f32[4,128,256]{2,1,0:T(8,128)}, u32[]{:S(2)}) copy-start(f32[4,128,256]{2,1,0:T(8,128)} %copy-done) | copy-start | bytes 1572868
  29.7 14.6 %collective-permute-start.6 = (bf16[2,6,32,256]{3,2,1,0:T(8,128)(2,1)}, bf16[2,6,32,256]{3,2,1,0:T(8,128)(2,1)}, u32[]{:S(2)}, u32[]{:S(2)}) collective-permute-start(bf16[2,6,32,256]{3,2,1,0:T(8,128)(2,1)} %get-tuple-element.47), channel_id=1, source_target_pairs={{0,4},{4,8},{8,12},{1,5},{5,9},{9,13},{2,6},{6,10},{10,14},{3,7},{... | collective-permute-start | bytes 589832 | tf_op jit(solution)/shard_map/ppermute | solution.py:40
  32.1 12.2 %collective-permute-start.4 = (bf16[4,2,32,256]{3,2,1,0:T(8,128)(2,1)}, bf16[4,2,32,256]{3,2,1,0:T(8,128)(2,1)}, u32[]{:S(2)}, u32[]{:S(2)}) collective-permute-start(bf16[4,2,32,256]{3,2,1,0:T(8,128)(2,1)} %get-tuple-element.45), channel_id=1, source_target_pairs={{0,1},{1,0},{2,3},{3,2},{4,5},{5,4},{6,7},{7,6},{8,9},{9,8},{10,11... | collective-permute-start | bytes 393224 | tf_op jit(solution)/shard_map/ppermute | solution.py:34
  33.8 10.4 %collective-permute-start.5 = (bf16[4,2,32,256]{3,2,1,0:T(8,128)(2,1)}, bf16[4,2,32,256]{3,2,1,0:T(8,128)(2,1)}, u32[]{:S(2)}, u32[]{:S(2)}) collective-permute-start(bf16[4,2,32,256]{3,2,1,0:T(8,128)(2,1)} %get-tuple-element.46), channel_id=1, source_target_pairs={{1,2},{2,1},{5,6},{6,5},{9,10},{10,9},{13,14},{14,13},{17,18},{18,... | collective-permute-start | bytes 393224 | tf_op jit(solution)/shard_map/ppermute | solution.py:49
  42.4 8.1 %collective-permute-start.7 = (bf16[192,256]{1,0:T(8,128)(2,1)S(1)}, bf16[192,256]{1,0:T(8,128)(2,1)S(1)}, u32[]{:S(2)}, u32[]{:S(2)}) collective-permute-start(bf16[192,256]{1,0:T(8,128)(2,1)S(1)} %sum_parts.1._.own_ref), channel_id=1, source_target_pairs={{0,2},{2,0},{1,3},{3,1},{4,6},{6,4},{5,7},{7,5},{8,10},{10,8},{9,1... | collective-permute-start | bytes 294920 | tf_op jit(solution)/shard_map/ppermute | solution.py:34
  64.2 2.3 %collective-permute-start.8 = (bf16[12,128,256]{2,1,0:T(8,128)(2,1)S(1)}, bf16[12,128,256]{2,1,0:T(8,128)(2,1)S(1)}, u32[]{:S(2)}, u32[]{:S(2)}) collective-permute-start(bf16[12,128,256]{2,1,0:T(8,128)(2,1)S(1)} %bitcast.9), channel_id=1, source_target_pairs={{0,4},{4,0},{1,5},{5,1},{2,6},{6,2},{3,7},{7,3},{8,12},{12,8},{9,1... | collective-permute-start | bytes 2359304 | tf_op jit(solution)/shard_map/ppermute | solution.py:34
